TPU v7x, 32 devices: a whole 2x2x4 slice. The times are simulated.
32 devices in a mesh: ctx: 16 (over z, y, x), ch: 2 (over core).
Axes of the slice: x: 2, y: 2, z: 4, core: 2. Of those that a mesh axis runs over, the one named last changes fastest.
Arguments:
- q_proj: bfloat16 [4096, 4096], P('ctx', 'ch'), may hold values from -6 to 6
- k_proj: bfloat16 [4096, 4096], P('ctx', 'ch'), may hold values from -6 to 6
- v_proj: bfloat16 [4096, 4096], P('ctx', 'ch'), may hold values from -6 to 6
- residue: float32 [16, 4096], P(None, 'ch'), may hold values from -4 to 4
- rate: float32 [16, 4096], P(None, 'ch'), may hold values from 4.8828125e-05 to 0.1
- skip: float32 [4096], P('ch'), may hold values from -4 to 4
- w_out: bfloat16 [4096, 6144], P('ctx', 'ch'), may hold values from -0.09375 to 0.09375
Outputs:
- mixed: bfloat16 [4096, 6144], P('ctx', 'ch')
All inputs are finite; a program needn't handle non-finite values.
Results may differ from a plain program's by a relative error of at most 0.0049.
Values may be sent and summed in bfloat16 or wider, within the bound.
No kernel may reach another device: no remote copies, remote signals or barrier semaphores. Data moves between devices by JAX's collectives and lax.ppermute only.
A program may use at most 192 MiB of HBM per device.

v0:
```python
import jax
import jax.numpy as jnp
from jax import lax
from jax.sharding import PartitionSpec as P


def body(q_proj, k_proj, v_proj, residue, rate, skip, w_out):
    highest = lax.Precision.HIGHEST
    tok_rows, chan_count = q_proj.shape
    signal = k_proj.astype(jnp.float32) * v_proj.astype(jnp.float32)
    sub_len = min(64, tok_rows // 4)
    sub_count = tok_rows // sub_len
    pieces = signal.reshape(sub_count, sub_len, chan_count)
    lag_steps = jnp.arange(sub_len).astype(jnp.float32)
    powers = jnp.exp(-rate[:, None, :] * lag_steps[None, :, None])
    coefficient = residue * jnp.sqrt(2.0 * rate)
    filter_taps = jnp.einsum("mc,mkc->kc", coefficient, powers, precision=highest)
    offsets = jnp.arange(sub_len)[:, None] - jnp.arange(sub_len)[None, :]
    toeplitz = jnp.where(
        (offsets >= 0)[:, :, None], filter_taps[jnp.clip(offsets, 0, sub_len - 1)], 0.0
    )
    local_part = jnp.einsum("tsc,bsc->btc", toeplitz, pieces, precision=highest)
    ends = jnp.einsum("msc,bsc->bmc", powers[:, ::-1, :], pieces, precision=highest)
    sub_index = jnp.arange(sub_count)
    sub_gap = sub_index[:, None] - 1 - sub_index[None, :]
    gap_float = jnp.maximum(sub_gap, 0).astype(jnp.float32)
    within = jnp.where(
        (sub_gap >= 0)[:, :, None, None],
        jnp.exp(-(rate * sub_len)[None, None] * gap_float[:, :, None, None]),
        0.0,
    )
    inner = jnp.einsum("bamc,amc->bmc", within, ends, precision=highest)
    sub_decay = jnp.exp(-rate * sub_len)
    total_end = sub_decay * inner[-1] + ends[-1]
    states = lax.all_gather(total_end[None], "ctx", axis=0, tiled=True)
    device_count = lax.axis_size("ctx")
    my_index = lax.axis_index("ctx")
    dev_gap = my_index - 1 - jnp.arange(device_count)
    dev_gap_float = jnp.maximum(dev_gap, 0).astype(jnp.float32)
    weights = jnp.where(
        (dev_gap >= 0)[:, None, None],
        jnp.exp(-(rate * tok_rows)[None] * dev_gap_float[:, None, None]),
        0.0,
    )
    entering = jnp.sum(weights * states, axis=0)
    start_powers = jnp.exp(-(rate * sub_len)[None] * sub_index.astype(jnp.float32)[:, None, None])
    arriving = inner + start_powers * entering[None]
    reach = coefficient[:, None, :] * powers * jnp.exp(-rate)[:, None, :]
    carried = jnp.einsum("mtc,bmc->btc", reach, arriving, precision=highest)
    conv = (local_part + carried).reshape(tok_rows, chan_count) + skip[None, :] * signal
    gated = (q_proj.astype(jnp.float32) * conv).astype(jnp.bfloat16)
    full_gated = lax.all_gather(gated, "ch", axis=1, tiled=True)
    mixed = jnp.dot(
        full_gated,
        lax.all_gather(w_out, "ctx", axis=0, tiled=True),
        preferred_element_type=jnp.float32,
    )
    return mixed.astype(jnp.bfloat16)


def solution(mesh):
    placed = (
        P("ctx", "ch"),
        P("ctx", "ch"),
        P("ctx", "ch"),
        P(None, "ch"),
        P(None, "ch"),
        P("ch"),
        P("ctx", "ch"),
    )
    return jax.shard_map(
        body, mesh=mesh, in_specs=placed, out_specs=P("ctx", "ch"), check_vma=False
    )
```

profile of v0, /device:TPU:8, one launch (start us, length us, event | category | flops | bytes accessed | tf_op | source)
XLA Modules:
  0.0 636.7 jit_solution(6322114798848415500)
XLA Ops:
  6.7 1.9 convert_multiply_fusion
  8.6 3.1 copy.44
  12.1 9.3 %multiply_exponential_fusion = f32[16,64,2048]{1,0,2:T(8,128)} fusion(f32[64]{0:T(128)S(1)} %iota_convert_fusion.1, f32[16,2048]{0,1:T(8,128)S(1)} %copy.42), kind=kLoop, calls=%fused_computation.9 | loop fusion | flops 2097152 | bytes 8519936 | tf_op jit(solution)/shard_map/exp | solution.py:15
  21.4 24.9 %rev.3 = f32[16,64,2048]{1,0,2:T(8,128)} reverse(f32[16,64,2048]{1,0,2:T(8,128)} %multiply_exponential_fusion), dimensions={1} | reverse | bytes 16777216 | tf_op jit(solution)/shard_map/rev | solution.py:23
  46.3 30.2 %fusion.20 = f32[2048,4,16]{2,1,0:T(4,128)} fusion(f32[4,64,2048]{1,0,2:T(4,128)} %copy.44, f32[16,64,2048]{1,0,2:T(8,128)} %rev.3), kind=kOutput, calls=%fused_computation.44 | convolution fusion | flops 100663296 | bytes 11010048 | tf_op jit(solution)/shard_map/msc,bsc->bmc/dot_general | solution.py:23
  76.6 3.5 copy.68
  80.1 0.5 multiply_reduce_fusion.1
  80.6 0.8 negate_exponential_fusion
  81.9 12.7 %multiply_reduce_fusion = f32[2048,64]{1,0:T(8,128)} fusion(f32[2048,16]{1,0:T(8,128)S(1)} %copy.66, f32[64]{0:T(128)S(1)} %iota_convert_fusion.1, f32[16,2048]{0,1:T(8,128)S(1)} %copy.42), kind=kLoop, calls=%fused_computation.5 | loop fusion | flops 6160384 | bytes 786688
  94.6 0.3 copy.47
  95.0 1.5 copy.56
  96.6 23.9 %gather_fusion = f32[4096,2048]{1,0:T(8,128)} fusion(f32[64,2048]{1,0:T(8,128)S(1)} %bitcast.46, s32[4096]{0:T(1024)S(1)} %broadcast_clamp_fusion), kind=kCustom, calls=%fused_computation | custom fusion | bytes 67125248 | tf_op jit(solution)/shard_map/gather | solution.py:20
  120.5 58.9 %copy.43 = f32[64,64,2048]{1,0,2:T(8,128)} copy(f32[64,64,2048]{2,1,0:T(8,128)} %bitcast.47) | data formatting | bytes 67108864 | tf_op jit(solution)/shard_map/gather | solution.py:20
  179.5 1.3 copy.48
  180.8 109.1 %fusion = f32[2048,4,64]{2,1,0:T(4,128)} fusion(f32[4,64,2048]{1,0,2:T(4,128)} %copy.44, f32[64,64,2048]{1,0,2:T(8,128)} %copy.43, pred[64,64]{1,0:T(8,128)(4,1)S(1)} %subtract_compare_fusion), kind=kOutput, calls=%fused_computation.1 | convolution fusion | flops 411041792 | bytes 37752832 | tf_op jit(solution)/shard_map/tsc,bsc->btc/dot_general | solution.py:22
  289.9 2.1 multiply_reduce_fusion.2
  292.2 3.1 copy.49
  295.3 29.7 %add_bitcast_fusion = f32[4,64,2048]{1,0,2:T(4,128)} fusion(f32[2048,4,64]{2,1,0:T(4,128)} %fusion, f32[4,16,2048]{1,0,2:T(4,128)} %copy.49, f32[16,2048]{0,1:T(8,128)} %copy.48, f32[16,2048]{0,1:T(8,128)S(1)} %copy.47, f32[64]{0:T(128)S(1)} %iota_convert_fusion.1, f32[16,2048]{0,1:T(8,128)S(1)} %copy.42), kind=kOutput, calls=%fused_computation.14 | convolution fusion | flops 107479040 | bytes 5112064 | tf_op jit(solution)/shard_map/mtc,bmc->btc/dot_general | solution.py:49
  325.0 3.6 copy.50
  328.6 3.2 fusion.14
  331.9 0.7 all-gather.7.cloned.1.call-update
  332.6 11.4 %all-gather.5.cloned.1.call-done = bf16[256,4096]{1,0:T(8,128)(2,1)} async-done(((bf16[256,2048]{1,0:T(8,128)(2,1)}), bf16[256,4096]{1,0:T(8,128)(2,1)}) %all-gather.5.cloned.1.call-update) | async-done | bytes 2097168 | tf_op jit(solution)/shard_map/all_gather | solution.py:52
  344.0 273.1 %all-gather.7.cloned.1.call-done = bf16[4096,3072]{1,0:T(8,128)(2,1)} async-done(((bf16[256,3072]{1,0:T(8,128)(2,1)}), bf16[4096,3072]{1,0:T(8,128)(2,1)}) %all-gather.7.cloned.1.call-update) | async-done | bytes 25165840 | tf_op jit(solution)/shard_map/all_gather | solution.py:55
  617.1 13.0 %convolution_convert_fusion = bf16[256,3072]{1,0:T(8,128)(2,1)} fusion(bf16[256,4096]{1,0:T(8,128)(2,1)} %all-gather.5.cloned.1.call-done, bf16[4096,3072]{1,0:T(8,128)(2,1)} %all-gather.7.cloned.1.call-done), kind=kOutput, calls=%fused_computation.15 | convolution fusion | flops 6443237376 | bytes 28835840 | tf_op jit(solution)/shard_map/dot_general | solution.py:53
  (31 shorter events, 1.4 us)
Async XLA Ops:
  6.5 283.4 %all-gather.9.cloned.1.call-start = ((), (), s32[]{:S(2)}) async-start(), calls=%async_computation.2 | async-start | bytes 2228224 | tf_op jit(solution)/shard_map/all_gather | solution.py:35
  8.6 3.1 copy-start.1
  76.6 4.0 copy-start.3
  81.4 262.7 %all-gather.5.cloned.1.call-start = ((), (), s32[]{:S(2)}) async-start(), calls=%async_computation | async-start | bytes 3145728 | tf_op jit(solution)/shard_map/all_gather | solution.py:52
  120.5 58.9 %copy-start.2 = (f32[16,2048]{1,0:T(8,128)S(1)}, f32[16,2048]{1,0:T(8,128)}, u32[]{:S(2)}) copy-start(f32[16,2048]{1,0:T(8,128)} %get-tuple-element.5) | copy-start | bytes 393220
  325.0 3.6 copy-start
  325.0 3.6 copy-start.4
  331.9 285.3 %all-gather.7.cloned.1.call-start = ((), (), s32[]{:S(2)}) async-start(), calls=%async_computation.1 | async-start | bytes 26738688 | tf_op jit(solution)/shard_map/all_gather | solution.py:55
Sparse Core Ops, SparseCore 0:
  81.5 61.9 all-gather.8
  332.0 11.9 all-gather.4
  346.8 270.2 all-gather.6
where the time goes:
time: 642 us; the launch traced here: 637 us
  waiting for transfers between devices  285 us (44%)
  matrix products  182 us (28%)
  local copies, waits for them, and re-layouts  125 us (19%)
  other arithmetic  30.9 us (5%)
  between operations  13.2 us (2%)
    all_gather x1, waiting for transfers between devices, body(): lax.all_gather(w_out, 'ctx', axis=0, tiled=True)  273 us
    dot_general x1, matrix products, body(): local_part = jnp.einsum('tsc,bsc->btc', toeplitz, pieces, precision=highest)  109 us
    gather x2, local copies, waits for them, and re-layouts, body(): filter_taps[jnp.clip(offsets, 0, sub_len - 1)]  82.9 us
    dot_general x1, matrix products, body(): jnp.einsum('msc,bsc->bmc', powers[:, ::-1, :], pieces, precision=highest)  30.2 us
    dot_general x1, matrix products, body(): carried = jnp.einsum('mtc,bmc->btc', reach, arriving, precision=highest)  29.7 us
    rev x1, local copies, waits for them, and re-layouts, body(): powers[:, ::-1, :]  24.9 us
    dot_general x1, matrix products, body(): jnp.dot(full_gated, lax.all_gather(w_out, 'ctx', axis=0, tiled=True), pre...  13 us
  transfers between devices with their start and end apart: 3, of which 2 were waited for; matrix products, arithmetic and copies ran while one was open for 33% of the time, Pallas kernels for 0%

commit v1 on v0

v1 whole, which is shorter than its diff:
```python
import jax
import jax.numpy as jnp
from jax import lax
from jax.experimental import pallas as pl
from jax.experimental.pallas import tpu as pltpu
from jax.sharding import PartitionSpec as P

LANES = 128
RADIX = 4


def spread_signal(k_ref, v_ref, sig_ref):
    rows, width = k_ref.shape
    groups = width // LANES
    for g in range(groups):
        cols = pl.ds(g * LANES, LANES)
        product = k_ref[:, cols].astype(jnp.float32) * v_ref[:, cols].astype(jnp.float32)
        sig_ref[pl.ds(g, rows, stride=groups), :] = product


def ends_kernel(k_ref, v_ref, rate_ref, end_ref, sig_ref):
    rows, width = k_ref.shape
    modes, groups, _ = rate_ref.shape
    spread_signal(k_ref, v_ref, sig_ref)
    decay = [jnp.exp(-rate_ref[m]) for m in range(modes)]

    def step(t, state):
        s = sig_ref[pl.ds(pl.multiple_of(t * groups, groups), groups), :]
        return tuple(d * h + s for d, h in zip(decay, state))

    zero = jnp.zeros((groups, LANES), jnp.float32)
    state = lax.fori_loop(0, rows, step, (zero,) * modes, unroll=8)
    for m in range(modes):
        end_ref[m] = state[m]


def conv_kernel(q_ref, k_ref, v_ref, rate_ref, residue_ref, skip_ref, enter_ref, out_ref, sig_ref, conv_ref):
    rows, width = k_ref.shape
    modes, groups, _ = rate_ref.shape
    spread_signal(k_ref, v_ref, sig_ref)
    decay = [jnp.exp(-rate_ref[m]) for m in range(modes)]
    weight = [residue_ref[m] * jnp.sqrt(2.0 * rate_ref[m]) for m in range(modes)]
    skip = skip_ref[...]

    def step(t, state):
        at = pl.ds(pl.multiple_of(t * groups, groups), groups)
        s = sig_ref[at, :]
        state = tuple(d * h + s for d, h in zip(decay, state))
        terms = [c * h for c, h in zip(weight, state)] + [skip * s]
        while len(terms) > 1:
            terms = [sum(terms[i : i + 2]) for i in range(0, len(terms), 2)]
        conv_ref[at, :] = terms[0]
        return state

    lax.fori_loop(0, rows, step, tuple(enter_ref[m] for m in range(modes)), unroll=4)
    for g in range(groups):
        cols = pl.ds(g * LANES, LANES)
        conv = conv_ref[pl.ds(g, rows, stride=groups), :]
        out_ref[:, cols] = (q_ref[:, cols].astype(jnp.float32) * conv).astype(out_ref.dtype)


def block_specs(rows, modes, width):
    groups = width // LANES
    return (
        pl.BlockSpec((rows, width), lambda i: (0, i)),
        pl.BlockSpec((modes, groups, LANES), lambda i: (0, i, 0)),
        pl.BlockSpec((groups, LANES), lambda i: (i, 0)),
    )


def end_states(k, v, rate):
    rows, chan = k.shape
    modes = rate.shape[0]
    width = min(chan, 8 * LANES)
    wide, moded, _ = block_specs(rows, modes, width)
    return pl.pallas_call(
        ends_kernel,
        grid=(chan // width,),
        in_specs=[wide, wide, moded],
        out_specs=moded,
        out_shape=jax.ShapeDtypeStruct(rate.shape, jnp.float32),
        scratch_shapes=[pltpu.VMEM((rows * width // LANES, LANES), jnp.float32)],
        compiler_params=pltpu.CompilerParams(vmem_limit_bytes=32 << 20),
        cost_estimate=pl.CostEstimate(
            flops=2 * modes * rows * chan, bytes_accessed=4 * rows * chan, transcendentals=modes * chan
        ),
        name="end_states",
    )(k, v, rate)


def gated_conv(q, k, v, rate, residue, skip, enter):
    rows, chan = k.shape
    modes = rate.shape[0]
    width = min(chan, 8 * LANES)
    wide, moded, single = block_specs(rows, modes, width)
    spread = pltpu.VMEM((rows * width // LANES, LANES), jnp.float32)
    return pl.pallas_call(
        conv_kernel,
        grid=(chan // width,),
        in_specs=[wide, wide, wide, moded, moded, single, moded],
        out_specs=wide,
        out_shape=jax.ShapeDtypeStruct((rows, chan), jnp.bfloat16),
        scratch_shapes=[spread, spread],
        compiler_params=pltpu.CompilerParams(vmem_limit_bytes=32 << 20),
        cost_estimate=pl.CostEstimate(
            flops=4 * modes * rows * chan, bytes_accessed=8 * rows * chan, transcendentals=2 * modes * chan
        ),
        name="gated_conv",
    )(q, k, v, rate, residue, skip, enter)


def shift_ctx(x, by, count):
    return lax.ppermute(x, "ctx", [(i, i + by) for i in range(count - by)])


def entering_states(ends, rate, rows):
    count = lax.axis_size("ctx")
    total = jnp.zeros_like(ends)
    for k in range(1, min(RADIX, count - 1) + 1):
        total = total + jnp.exp(-rate * float(rows * (k - 1))) * shift_ctx(ends, k, count)
    stride = RADIX
    while stride < count:
        base = total
        for k in range(1, RADIX):
            if stride * k < count:
                total = total + jnp.exp(-rate * float(rows * stride * k)) * shift_ctx(base, stride * k, count)
        stride *= RADIX
    return total


def body(q, k, v, residue, rate, skip, w_out):
    rows, chan = q.shape
    modes = rate.shape[0]
    groups = chan // LANES
    w_full = lax.all_gather(w_out, "ctx", axis=0, tiled=True)
    rate = rate.reshape(modes, groups, LANES)
    residue = residue.reshape(modes, groups, LANES)
    skip = skip.reshape(groups, LANES)
    ends = end_states(k, v, rate)
    enter = entering_states(ends, rate, rows)
    gated = gated_conv(q, k, v, rate, residue, skip, enter)
    full_gated = lax.all_gather(gated, "ch", axis=1, tiled=True)
    mixed = jnp.dot(full_gated, w_full, preferred_element_type=jnp.float32)
    return mixed.astype(jnp.bfloat16)


def solution(mesh):
    placed = (
        P("ctx", "ch"),
        P("ctx", "ch"),
        P("ctx", "ch"),
        P(None, "ch"),
        P(None, "ch"),
        P("ch"),
        P("ctx", "ch"),
    )
    return jax.shard_map(
        body, mesh=mesh, in_specs=placed, out_specs=P("ctx", "ch"), check_vma=False
    )
```

time: 642 us -> 361 us (0.56)
  matrix products: 182 us -> 13 us
  local copies, waits for them, and re-layouts: 125 us -> 3.45 us
  other arithmetic: 30.9 us -> 0.17 us
  starting transfers between devices: 0.27 us -> 19 us
  waiting for transfers between devices: 285 us -> 297 us
  Pallas kernels: 0 us -> 10.8 us
    dot_general x4 -> x1, matrix products: 182 us -> 13 us  [body(): mixed = jnp.dot(full_gated, w_full, preferred_element_type=jnp.float32)]
    gather x2 -> x0, local copies, waits for them, and re-layouts: 82.9 us -> none  [body(): filter_taps[jnp.clip(offsets, 0, sub_len - 1)]]
    rev x1 -> x0, local copies, waits for them, and re-layouts: 24.9 us -> none  [body(): powers[:, ::-1, :]]
    ppermute x0 -> x7, starting transfers between devices: none -> 19 us  [shift_ctx(): return lax.ppermute(x, 'ctx', [(i, i + by) for i in range(count - by)])]
    ppermute x0 -> x7, waiting for transfers between devices: none -> 14.3 us  [shift_ctx(): return lax.ppermute(x, 'ctx', [(i, i + by) for i in range(count - by)])]
    unnamed x1 -> x0, other arithmetic: 12.7 us -> none
    pallas_call x0 -> x2, Pallas kernels: none -> 10.8 us  [the longest x1 7.6 us: gated_conv(): pl.pallas_call(conv_kernel, grid=(chan // width,), in_specs=[wide, wide,...]
    exp x2 -> x0, other arithmetic: 10.1 us -> none  [the longest x1 9.3 us: body(): powers = jnp.exp(-rate[:, None, :] * lag_steps[None, :, None])]
  transfers between devices with their start and end apart: 3 -> 9, of which waited for: 2 -> 6; matrix products, arithmetic and copies ran while one was open for 33% -> 0% of each run, Pallas kernels for 0% -> 0%
where the time goes in v1:
time: 361 us; the launch traced here: 358 us
  waiting for transfers between devices  297 us (82%)
  starting transfers between devices  19 us (5%)
  between operations  13.5 us (4%)
  matrix products  13 us (4%)
  Pallas kernels  10.8 us (3%)
    all_gather x1, waiting for transfers between devices, body(): w_full = lax.all_gather(w_out, 'ctx', axis=0, tiled=True)  273 us
    ppermute x7, starting transfers between devices, shift_ctx(): return lax.ppermute(x, 'ctx', [(i, i + by) for i in range(count - by)])  19 us
    ppermute x7, waiting for transfers between devices, shift_ctx(): return lax.ppermute(x, 'ctx', [(i, i + by) for i in range(count - by)])  14.3 us
    dot_general x1, matrix products, body(): mixed = jnp.dot(full_gated, w_full, preferred_element_type=jnp.float32)  13 us
    all_gather x1, waiting for transfers between devices, body(): full_gated = lax.all_gather(gated, 'ch', axis=1, tiled=True)  9.41 us
    pallas_call x1, Pallas kernels, gated_conv(): pl.pallas_call(conv_kernel, grid=(chan // width,), in_specs=[wide, wide,...  7.6 us
  transfers between devices with their start and end apart: 9, of which 6 were waited for; matrix products, arithmetic and copies ran while one was open for 0% of the time, Pallas kernels for 0%

profile of v1, /device:TPU:8, one launch (start us, length us, event | category | flops | bytes accessed | tf_op | source)
XLA Modules:
  0.0 357.5 jit_solution(16342181641248290824)
XLA Ops:
  6.5 1.0 copy.8
  7.5 1.2 copy-done
  8.7 1.2 copy-done.1
  10.0 3.2 end_states.1
  13.2 3.5 collective-permute-start.3
  16.7 4.4 %collective-permute-start.2 = (f32[16,16,128]{2,1,0:T(8,128)S(1)}, f32[16,16,128]{2,1,0:T(8,128)S(1)}, u32[]{:S(2)}, u32[]{:S(2)}) collective-permute-start(f32[16,16,128]{2,1,0:T(8,128)S(1)} %end_states.1), channel_id=1, source_target_pairs={{0,6},{2,8},{4,10},{6,12},{8,14},{10,16},{12,18},{14,20},{16,22},{... | collective-permute-start | bytes 393224 | tf_op jit(solution)/shard_map/ppermute | solution.py:113
  21.1 3.4 collective-permute-start.1
  24.5 2.5 collective-permute-start
  27.0 1.8 collective-permute-done.1
  28.8 4.3 %collective-permute-done = f32[16,16,128]{2,1,0:T(8,128)S(1)} collective-permute-done((f32[16,16,128]{2,1,0:T(8,128)S(1)}, f32[16,16,128]{2,1,0:T(8,128)S(1)}, u32[]{:S(2)}, u32[]{:S(2)}) %collective-permute-start) | collective-permute-done | bytes 131104 | tf_op jit(solution)/shard_map/ppermute | solution.py:113
  33.2 0.1 multiply_add_fusion.1
  33.3 0.7 collective-permute-start.6
  33.9 2.6 collective-permute-start.5
  36.5 1.9 collective-permute-start.4
  38.5 5.4 %collective-permute-done.5 = f32[16,16,128]{2,1,0:T(8,128)S(1)} collective-permute-done((f32[16,16,128]{2,1,0:T(8,128)S(1)}, f32[16,16,128]{2,1,0:T(8,128)S(1)}, u32[]{:S(2)}, u32[]{:S(2)}) %collective-permute-start.5) | collective-permute-done | bytes 131104 | tf_op jit(solution)/shard_map/ppermute | solution.py:113
  44.0 2.7 collective-permute-done.4
  46.7 0.1 multiply_add_fusion.enter_ref
  46.8 7.6 %gated_conv.1 = bf16[256,2048]{1,0:T(8,128)(2,1)} custom-call(bf16[256,2048]{1,0:T(8,128)(2,1)S(1)} %copy-done.2, bf16[256,2048]{1,0:T(8,128)(2,1)S(1)} %copy-done, bf16[256,2048]{1,0:T(8,128)(2,1)S(1)} %copy-done.1, f32[16,16,128]{2,1,0:T(8,128)S(1)} %bitcast.10, f32[16,16,128]{2,1,0:T(8,128)S(1)} %bitcast.11, f32[16,128]{1,0:T(8,128)S(1)} %bitcast.12, ...), custom_call_target="tpu_custom_call" | custom-call | flops 33554432 | bytes 4194304 | tf_op jit(solution)/shard_map/gated_conv/pallas_call | solution.py:97
  54.4 0.0 all-gather.3.cloned.1.call-update
  54.4 0.0 all-gather.5.cloned.1.call-start
  54.4 0.7 all-gather.5.cloned.1.call-update
  55.1 9.4 %all-gather.3.cloned.1.call-done = bf16[256,4096]{1,0:T(8,128)(2,1)} async-done(((bf16[256,2048]{1,0:T(8,128)(2,1)}), bf16[256,4096]{1,0:T(8,128)(2,1)}) %all-gather.3.cloned.1.call-update) | async-done | bytes 2097168 | tf_op jit(solution)/shard_map/all_gather | solution.py:142
  64.6 273.1 %all-gather.5.cloned.1.call-done = bf16[4096,3072]{1,0:T(8,128)(2,1)} async-done(((bf16[256,3072]{1,0:T(8,128)(2,1)}), bf16[4096,3072]{1,0:T(8,128)(2,1)}) %all-gather.5.cloned.1.call-update) | async-done | bytes 25165840 | tf_op jit(solution)/shard_map/all_gather | solution.py:135
  337.7 13.0 %convolution_convert_fusion = bf16[256,3072]{1,0:T(8,128)(2,1)} fusion(bf16[256,4096]{1,0:T(8,128)(2,1)} %all-gather.3.cloned.1.call-done, bf16[4096,3072]{1,0:T(8,128)(2,1)} %all-gather.5.cloned.1.call-done), kind=kOutput, calls=%fused_computation | convolution fusion | flops 6443237376 | bytes 28835840 | tf_op jit(solution)/shard_map/dot_general | solution.py:143
  (13 shorter events, 0.1 us)
Async XLA Ops:
  6.5 31.9 %copy-start.4 = (f32[16,2048]{1,0:T(8,128)S(1)}, f32[16,2048]{1,0:T(8,128)}, u32[]{:S(2)}) copy-start(f32[16,2048]{1,0:T(8,128)} %param.10) | copy-start | bytes 393220
  6.5 58.0 %all-gather.3.cloned.1.call-start = ((), (), s32[]{:S(2)}) async-start(), calls=%async_computation | async-start | bytes 3145728 | tf_op jit(solution)/shard_map/all_gather | solution.py:142
  7.5 1.2 copy-start
  8.7 1.2 copy-start.1
  10.0 36.8 %copy-start.2 = (bf16[256,2048]{1,0:T(8,128)(2,1)S(1)}, bf16[256,2048]{1,0:T(8,128)(2,1)}, u32[]{:S(2)}) copy-start(bf16[256,2048]{1,0:T(8,128)(2,1)} %q_ref.1) | copy-start | bytes 3145732
  10.0 36.8 %copy-start.3 = (f32[2048]{0:T(1024)S(1)}, f32[2048]{0:T(1024)}, u32[]{:S(2)}) copy-start(f32[2048]{0:T(1024)} %param.12) | copy-start | bytes 24580
  13.2 13.8 %collective-permute-start.3 = (f32[16,16,128]{2,1,0:T(8,128)S(1)}, f32[16,16,128]{2,1,0:T(8,128)S(1)}, u32[]{:S(2)}, u32[]{:S(2)}) collective-permute-start(f32[16,16,128]{2,1,0:T(8,128)S(1)} %end_states.1), channel_id=1, source_target_pairs={{0,8},{2,10},{4,12},{6,14},{8,16},{10,18},{12,20},{14,22},{16,24},... | collective-permute-start | bytes 393224 | tf_op jit(solution)/shard_map/ppermute | solution.py:113
  16.7 10.3 %collective-permute-start.2 = (f32[16,16,128]{2,1,0:T(8,128)S(1)}, f32[16,16,128]{2,1,0:T(8,128)S(1)}, u32[]{:S(2)}, u32[]{:S(2)}) collective-permute-start(f32[16,16,128]{2,1,0:T(8,128)S(1)} %end_states.1), channel_id=1, source_target_pairs={{0,6},{2,8},{4,10},{6,12},{8,14},{10,16},{12,18},{14,20},{16,22},{... | collective-permute-start | bytes 393224 | tf_op jit(solution)/shard_map/ppermute | solution.py:113
  21.1 7.8 %collective-permute-start.1 = (f32[16,16,128]{2,1,0:T(8,128)S(1)}, f32[16,16,128]{2,1,0:T(8,128)S(1)}, u32[]{:S(2)}, u32[]{:S(2)}) collective-permute-start(f32[16,16,128]{2,1,0:T(8,128)S(1)} %end_states.1), channel_id=1, source_target_pairs={{0,4},{2,6},{4,8},{6,10},{8,12},{10,14},{12,16},{14,18},{16,20},{1... | collective-permute-start | bytes 393224 | tf_op jit(solution)/shard_map/ppermute | solution.py:113
  24.5 8.7 %collective-permute-start = (f32[16,16,128]{2,1,0:T(8,128)S(1)}, f32[16,16,128]{2,1,0:T(8,128)S(1)}, u32[]{:S(2)}, u32[]{:S(2)}) collective-permute-start(f32[16,16,128]{2,1,0:T(8,128)S(1)} %end_states.1), channel_id=1, source_target_pairs={{0,2},{2,4},{4,6},{6,8},{8,10},{10,12},{12,14},{14,16},{16,18},{18... | collective-permute-start | bytes 393224 | tf_op jit(solution)/shard_map/ppermute | solution.py:113
  33.3 5.3 %collective-permute-start.6 = (f32[16,16,128]{2,1,0:T(8,128)S(1)}, f32[16,16,128]{2,1,0:T(8,128)S(1)}, u32[]{:S(2)}, u32[]{:S(2)}) collective-permute-start(f32[16,16,128]{2,1,0:T(8,128)S(1)} %multiply_add_fusion.1), channel_id=1, source_target_pairs={{0,24},{2,26},{4,28},{6,30},{1,25},{3,27},{5,29},{7,31}} | collective-permute-start | bytes 393224 | tf_op jit(solution)/shard_map/ppermute | solution.py:113
  33.9 10.0 %collective-permute-start.5 = (f32[16,16,128]{2,1,0:T(8,128)S(1)}, f32[16,16,128]{2,1,0:T(8,128)S(1)}, u32[]{:S(2)}, u32[]{:S(2)}) collective-permute-start(f32[16,16,128]{2,1,0:T(8,128)S(1)} %multiply_add_fusion.1), channel_id=1, source_target_pairs={{0,16},{2,18},{4,20},{6,22},{8,24},{10,26},{12,28},{14,30},{1,17},... | collective-permute-start | bytes 393224 | tf_op jit(solution)/shard_map/ppermute | solution.py:113
  36.5 10.1 %collective-permute-start.4 = (f32[16,16,128]{2,1,0:T(8,128)S(1)}, f32[16,16,128]{2,1,0:T(8,128)S(1)}, u32[]{:S(2)}, u32[]{:S(2)}) collective-permute-start(f32[16,16,128]{2,1,0:T(8,128)S(1)} %multiply_add_fusion.1), channel_id=1, source_target_pairs={{0,8},{2,10},{4,12},{6,14},{8,16},{10,18},{12,20},{14,22},{16,24},... | collective-permute-start | bytes 393224 | tf_op jit(solution)/shard_map/ppermute | solution.py:113
  54.4 283.3 %all-gather.5.cloned.1.call-start = ((), (), s32[]{:S(2)}) async-start(), calls=%async_computation.1 | async-start | bytes 26738688 | tf_op jit(solution)/shard_map/all_gather | solution.py:135
Sparse Core Ops, SparseCore 0:
  54.5 9.9 all-gather.2
  67.3 270.2 all-gather.4

commit v2 on v1

--- a/solution.py
+++ b/solution.py
@@ -7,6 +7,7 @@
 
 LANES = 128
 RADIX = 4
+PLANE = 4
 
 
 def spread_signal(k_ref, v_ref, sig_ref):
@@ -98,8 +99,8 @@
         conv_kernel,
         grid=(chan // width,),
         in_specs=[wide, wide, wide, moded, moded, single, moded],
-        out_specs=wide,
-        out_shape=jax.ShapeDtypeStruct((rows, chan), jnp.bfloat16),
+        out_specs=pl.BlockSpec((None, rows, width), lambda i: (i, 0, 0)),
+        out_shape=jax.ShapeDtypeStruct((chan // width, rows, width), jnp.bfloat16),
         scratch_shapes=[spread, spread],
         compiler_params=pltpu.CompilerParams(vmem_limit_bytes=32 << 20),
         cost_estimate=pl.CostEstimate(
@@ -128,18 +129,163 @@
     return total
 
 
+def exchange(x, axis, flip):
+    count = lax.axis_size(axis)
+    return lax.ppermute(x, axis, [(i, i ^ flip) for i in range(count)])
+
+
+def project(pick, gated, weights, acc, out_dtype):
+    _, _, rows, depth = gated.shape
+    chunk = depth // PLANE
+    cols = weights[0][0].shape[1]
+    blocks = len(weights)
+    flat = [piece for block in weights for piece in block]
+    sizes = [[piece.shape[0] // chunk for piece in block] for block in weights]
+
+    def kernel(pick_ref, *refs):
+        gated_refs, refs = refs[:blocks], refs[blocks:]
+        piece_refs, refs = refs[: len(flat)], refs[len(flat) :]
+        out_ref = refs[-1]
+        total = refs[0][...] if acc is not None else jnp.zeros((rows, cols), jnp.float32)
+        at = 0
+        for b in range(blocks):
+            r = 0
+            for size in sizes[b]:
+                for part in range(size):
+                    start = pl.multiple_of(pick_ref[blocks + r] * chunk, chunk)
+                    total = total + jnp.dot(
+                        gated_refs[b][:, pl.ds(start, chunk)],
+                        piece_refs[at][pl.ds(part * chunk, chunk), :],
+                        preferred_element_type=jnp.float32,
+                    )
+                    r += 1
+                at += 1
+        out_ref[...] = total.astype(out_ref.dtype)
+
+    def gated_spec(b):
+        return pl.BlockSpec((None, None, rows, depth), lambda i, pick_ref: (pick_ref[b], i, 0, 0))
+
+    row_spec = pl.BlockSpec((None, rows, cols), lambda i, pick_ref: (i, 0, 0))
+    whole = [pl.BlockSpec(piece.shape, lambda i, pick_ref: (0, 0)) for piece in flat]
+    args = [gated] * blocks + flat + ([] if acc is None else [acc])
+    return pl.pallas_call(
+        kernel,
+        grid_spec=pltpu.PrefetchScalarGridSpec(
+            num_scalar_prefetch=1,
+            grid=(PLANE,),
+            in_specs=[gated_spec(b) for b in range(blocks)] + whole + ([] if acc is None else [row_spec]),
+            out_specs=row_spec,
+        ),
+        out_shape=jax.ShapeDtypeStruct((PLANE, rows, cols), out_dtype),
+        compiler_params=pltpu.CompilerParams(vmem_limit_bytes=48 << 20),
+        cost_estimate=pl.CostEstimate(
+            flops=2 * PLANE * rows * depth * blocks * cols,
+            bytes_accessed=2 * blocks * depth * (PLANE * rows + cols) + 4 * PLANE * rows * cols,
+            transcendentals=0,
+        ),
+        name="project",
+    )(pick, *args)
+
+
+def assemble(place, pieces):
+    rows, cols = pieces[0].shape
+
+    def kernel(place_ref, *refs):
+        *piece_refs, out_ref, sems = refs
+        copies = []
+        for r, piece_ref in enumerate(piece_refs):
+            start = pl.multiple_of(place_ref[r] * cols, cols)
+            copies.append(pltpu.make_async_copy(piece_ref, out_ref.at[:, pl.ds(start, cols)], sems.at[r]))
+            copies[-1].start()
+        for copy in copies:
+            copy.wait()
+
+    return pl.pallas_call(
+        kernel,
+        in_specs=[pl.BlockSpec(memory_space=pltpu.SMEM)] + [pl.BlockSpec(memory_space=pl.ANY)] * len(pieces),
+        out_specs=pl.BlockSpec(memory_space=pl.ANY),
+        out_shape=jax.ShapeDtypeStruct((rows, cols * len(pieces)), pieces[0].dtype),
+        scratch_shapes=[pltpu.SemaphoreType.DMA((len(pieces),))],
+        name="assemble",
+    )(place, *pieces)
+
+
+def split_projection(gated_halves, w_out):
+    me = lax.axis_index("ctx")
+    core = lax.axis_index("ch")
+    spot, plane = me % PLANE, me // PLANE
+    count = lax.axis_size("ctx")
+    chunk, feats = w_out.shape
+    cols = feats // PLANE
+    rows = gated_halves.shape[1]
+
+    def group(r):
+        return lax.dynamic_slice_in_dim(w_out, (spot ^ r) * cols, cols, axis=1)
+
+    first = group(0)
+    first_far = exchange(first, "ctx", 2 * PLANE)
+    first_near = exchange(first, "ctx", PLANE)
+    rest = jnp.concatenate([exchange(group(r), "ctx", r) for r in range(1, PLANE)], axis=0)
+    rest_far = exchange(rest, "ctx", 2 * PLANE)
+    rest_near = exchange(rest, "ctx", PLANE)
+    middle = [i for i in range(count) if PLANE <= i < 3 * PLANE]
+    across_pairs = [(i, i ^ (3 * PLANE)) for i in middle]
+    end_pairs = [(i, i ^ PLANE) for i in middle]
+    own_block = jnp.concatenate([first, rest], axis=0)
+    far_block = jnp.concatenate([first_far, rest_far], axis=0)
+    across = lax.ppermute(own_block, "ctx", across_pairs)
+    ends = lax.ppermute(far_block, "ctx", end_pairs)
+
+    one, two = gated_halves[0], gated_halves[1]
+    one_x, two_y = exchange(one, "ctx", 1), exchange(two, "ctx", 2)
+    one_pair = jnp.stack([one, one_x])
+    two_pair = jnp.stack([two, two_y])
+    one_far, two_far = exchange(one_pair, "ctx", 2), exchange(two_pair, "ctx", 1)
+    ours = jnp.stack(
+        [
+            jnp.concatenate([one_pair, one_far]),
+            jnp.stack([two, two_far[0], two_y, two_far[1]]),
+        ]
+    )
+    theirs = exchange(ours, "ch", 1)
+    everything = jnp.concatenate([ours, theirs])
+
+    def block_at(b):
+        return jnp.where(b // 2 == core, b % 2, 2 + b % 2)
+
+    chunks = [spot ^ r for r in range(PLANE)]
+    most = jnp.stack([block_at(plane), block_at(plane ^ 1), block_at(plane ^ 2)] + chunks).astype(jnp.int32)
+    last = jnp.stack([block_at(plane ^ 3)] + chunks).astype(jnp.int32)
+    acc = project(most, everything, [[own_block], [first_near, rest_near], [far_block]], None, jnp.float32)
+    made = project(last, everything, [[across + ends]], acc, jnp.bfloat16)
+    back = [made[0]] + [exchange(made[r], "ctx", r) for r in range(1, PLANE)]
+    return assemble(jnp.stack(chunks).astype(jnp.int32), back)
+
+
 def body(q, k, v, residue, rate, skip, w_out):
     rows, chan = q.shape
     modes = rate.shape[0]
     groups = chan // LANES
-    w_full = lax.all_gather(w_out, "ctx", axis=0, tiled=True)
+    count, cores = lax.axis_size("ctx"), lax.axis_size("ch")
+    chunk, feats = w_out.shape
+    split = (
+        count == 4 * PLANE
+        and cores == 2
+        and chan == 8 * chunk
+        and chunk % LANES == 0
+        and feats % (PLANE * LANES) == 0
+    )
     rate = rate.reshape(modes, groups, LANES)
     residue = residue.reshape(modes, groups, LANES)
     skip = skip.reshape(groups, LANES)
     ends = end_states(k, v, rate)
     enter = entering_states(ends, rate, rows)
     gated = gated_conv(q, k, v, rate, residue, skip, enter)
+    if split:
+        return split_projection(gated, w_out)
+    gated = gated.transpose(1, 0, 2).reshape(rows, chan)
     full_gated = lax.all_gather(gated, "ch", axis=1, tiled=True)
+    w_full = lax.all_gather(w_out, "ctx", axis=0, tiled=True)
     mixed = jnp.dot(full_gated, w_full, preferred_element_type=jnp.float32)
     return mixed.astype(jnp.bfloat16)
 

time: 361 us -> 332 us (0.920)
  waiting for transfers between devices: 297 us -> 181 us
  Pallas kernels: 10.8 us -> 73.8 us
  starting transfers between devices: 19 us -> 49.4 us
  other arithmetic: 0.17 us -> 13.4 us
  between operations: 13.5 us -> 0.3 us
  matrix products: 13 us -> 0 us
  local copies, waits for them, and re-layouts: 3.45 us -> 9.33 us
    all_gather x2 -> x0, waiting for transfers between devices: 283 us -> none  [the longest x1 273 us: body(): w_full = lax.all_gather(w_out, 'ctx', axis=0, tiled=True)]
    ppermute x0 -> x17, waiting for transfers between devices: none -> 170 us  [the longest x15 138 us: exchange(): return lax.ppermute(x, axis, [(i, i ^ flip) for i in range(count)])]
    pallas_call x0 -> x3, Pallas kernels: none -> 63.8 us  [the longest x1 49.4 us: assemble(): pl.pallas_call(kernel, in_specs=[pl.BlockSpec(memory_space=pltpu.SMEM)] +...]
    ppermute x0 -> x17, starting transfers between devices: none -> 29.3 us  [the longest x15 20.9 us: exchange(): return lax.ppermute(x, axis, [(i, i ^ flip) for i in range(count)])]
    dot_general x1 -> x0, matrix products: 13 us -> none  [body(): mixed = jnp.dot(full_gated, w_full, preferred_element_type=jnp.float32)]
    concatenate x0 -> x2, other arithmetic: none -> 7.31 us  [the longest x1 6.18 us: split_projection(): everything = jnp.concatenate([ours, theirs])]
    another operation x0 -> x6, other arithmetic: none -> 3.66 us  [the longest x3 2.81 us: split_projection(): jnp.stack([jnp.concatenate([one_pair, one_far]), jnp.stack([two, two_far[...]
  transfers between devices with their start and end apart: 9 -> 24, of which waited for: 6 -> 14; matrix products, arithmetic and copies ran while one was open for 0% -> 4% of each run, Pallas kernels for 0% -> 0%
where the time goes in v2:
time: 332 us; the launch traced here: 327 us
  waiting for transfers between devices  181 us (55%)
  Pallas kernels  73.8 us (22%)
  starting transfers between devices  49.4 us (15%)
  other arithmetic  13.4 us (4%)
  local copies, waits for them, and re-layouts  9.33 us (3%)
    ppermute x15, waiting for transfers between devices, exchange(): return lax.ppermute(x, axis, [(i, i ^ flip) for i in range(count)])  138 us
    pallas_call x1, Pallas kernels, assemble(): pl.pallas_call(kernel, in_specs=[pl.BlockSpec(memory_space=pltpu.SMEM)] +...  49.4 us
    ppermute x1, waiting for transfers between devices, split_projection(): across = lax.ppermute(own_block, 'ctx', across_pairs)  25.7 us
    ppermute x15, starting transfers between devices, exchange(): return lax.ppermute(x, axis, [(i, i ^ flip) for i in range(count)])  20.9 us
    ppermute x7, starting transfers between devices, shift_ctx(): return lax.ppermute(x, 'ctx', [(i, i + by) for i in range(count - by)])  20.1 us
    pallas_call x2, Pallas kernels, project(): pl.pallas_call(kernel, grid_spec=pltpu.PrefetchScalarGridSpec(num_scalar_...  14.3 us
    ppermute x7, waiting for transfers between devices, shift_ctx(): return lax.ppermute(x, 'ctx', [(i, i + by) for i in range(count - by)])  10.8 us
    pallas_call x1, Pallas kernels, gated_conv(): pl.pallas_call(conv_kernel, grid=(chan // width,), in_specs=[wide, wide,...  6.75 us
  transfers between devices with their start and end apart: 24, of which 14 were waited for; matrix products, arithmetic and copies ran while one was open for 4% of the time, Pallas kernels for 0%

profile of v2, /device:TPU:8, one launch (start us, length us, event | category | flops | bytes accessed | tf_op | source)
XLA Modules:
  0.0 326.8 jit_solution(3758033512801357834)
XLA Ops:
  6.7 3.4 %collective-permute-start = (f32[16,16,128]{2,1,0:T(8,128)S(1)}, f32[16,16,128]{2,1,0:T(8,128)S(1)}, u32[]{:S(2)}, u32[]{:S(2)}) collective-permute-start(f32[16,16,128]{2,1,0:T(8,128)S(1)} %end_states.1), channel_id=1, source_target_pairs={{0,2},{2,4},{4,6},{6,8},{8,10},{10,12},{12,14},{14,16},{16,18},{18... | collective-permute-start | bytes 393224 | tf_op jit(solution)/shard_map/ppermute | solution.py:114
  10.1 3.4 %collective-permute-start.1 = (f32[16,16,128]{2,1,0:T(8,128)S(1)}, f32[16,16,128]{2,1,0:T(8,128)S(1)}, u32[]{:S(2)}, u32[]{:S(2)}) collective-permute-start(f32[16,16,128]{2,1,0:T(8,128)S(1)} %end_states.1), channel_id=1, source_target_pairs={{0,4},{2,6},{4,8},{6,10},{8,12},{10,14},{12,16},{14,18},{16,20},{1... | collective-permute-start | bytes 393224 | tf_op jit(solution)/shard_map/ppermute | solution.py:114
  13.5 4.4 %collective-permute-start.2 = (f32[16,16,128]{2,1,0:T(8,128)S(1)}, f32[16,16,128]{2,1,0:T(8,128)S(1)}, u32[]{:S(2)}, u32[]{:S(2)}) collective-permute-start(f32[16,16,128]{2,1,0:T(8,128)S(1)} %end_states.1), channel_id=1, source_target_pairs={{0,6},{2,8},{4,10},{6,12},{8,14},{10,16},{12,18},{14,20},{16,22},{... | collective-permute-start | bytes 393224 | tf_op jit(solution)/shard_map/ppermute | solution.py:114
  17.9 3.5 %collective-permute-start.3 = (f32[16,16,128]{2,1,0:T(8,128)S(1)}, f32[16,16,128]{2,1,0:T(8,128)S(1)}, u32[]{:S(2)}, u32[]{:S(2)}) collective-permute-start(f32[16,16,128]{2,1,0:T(8,128)S(1)} %end_states.1), channel_id=1, source_target_pairs={{0,8},{2,10},{4,12},{6,14},{8,16},{10,18},{12,20},{14,22},{16,24},... | collective-permute-start | bytes 393224 | tf_op jit(solution)/shard_map/ppermute | solution.py:114
  21.4 3.3 %collective-permute-done.3 = f32[16,16,128]{2,1,0:T(8,128)S(1)} collective-permute-done((f32[16,16,128]{2,1,0:T(8,128)S(1)}, f32[16,16,128]{2,1,0:T(8,128)S(1)}, u32[]{:S(2)}, u32[]{:S(2)}) %collective-permute-start.3) | collective-permute-done | bytes 131104 | tf_op jit(solution)/shard_map/ppermute | solution.py:114
  24.8 3.5 %collective-permute-start.4 = (f32[16,16,128]{2,1,0:T(8,128)S(1)}, f32[16,16,128]{2,1,0:T(8,128)S(1)}, u32[]{:S(2)}, u32[]{:S(2)}) collective-permute-start(f32[16,16,128]{2,1,0:T(8,128)S(1)} %multiply_add_fusion.1), channel_id=1, source_target_pairs={{0,8},{2,10},{4,12},{6,14},{8,16},{10,18},{12,20},{14,22},{16,24},... | collective-permute-start | bytes 393224 | tf_op jit(solution)/shard_map/ppermute | solution.py:114
  33.0 4.8 %collective-permute-done.5 = f32[16,16,128]{2,1,0:T(8,128)S(1)} collective-permute-done((f32[16,16,128]{2,1,0:T(8,128)S(1)}, f32[16,16,128]{2,1,0:T(8,128)S(1)}, u32[]{:S(2)}, u32[]{:S(2)}) %collective-permute-start.5) | collective-permute-done | bytes 131104 | tf_op jit(solution)/shard_map/ppermute | solution.py:114
  37.9 6.8 %gated_conv.1 = bf16[2,256,1024]{2,1,0:T(8,128)(2,1)S(1)} custom-call(bf16[256,2048]{1,0:T(8,128)(2,1)S(1)} %copy-done.2, bf16[256,2048]{1,0:T(8,128)(2,1)S(1)} %copy-done, bf16[256,2048]{1,0:T(8,128)(2,1)S(1)} %copy-done.1, f32[16,16,128]{2,1,0:T(8,128)S(1)} %bitcast.34, f32[16,16,128]{2,1,0:T(8,128)S(1)} %bitcast.35, f32[16,128]{1,0:T(8,128)S(1)} %bitcast.36, ...), custom_call_target="tpu_custom_call" | custom-call | flops 33554432 | bytes 4194304 | tf_op jit(solution)/shard_map/gated_conv/pallas_call | solution.py:98
  47.6 6.5 %collective-permute-done.9 = bf16[256,1024]{1,0:T(8,128)(2,1)S(1)} collective-permute-done((bf16[256,1024]{1,0:T(8,128)(2,1)S(1)}, bf16[256,1024]{1,0:T(8,128)(2,1)S(1)}, u32[]{:S(2)}, u32[]{:S(2)}) %collective-permute-start.9) | collective-permute-done | bytes 524320 | tf_op jit(solution)/shard_map/ppermute | solution.py:134
  54.3 4.6 %collective-permute-start.10 = (bf16[2,256,1024]{2,1,0:T(8,128)(2,1)S(1)}, bf16[2,256,1024]{2,1,0:T(8,128)(2,1)S(1)}, u32[]{:S(2)}, u32[]{:S(2)}) collective-permute-start(bf16[2,256,1024]{2,1,0:T(8,128)(2,1)S(1)} %pad_maximum_fusion.4), channel_id=1, source_target_pairs={{0,2},{2,0},{4,6},{6,4},{8,10},{10,8},{12,14},{14,12},{16,18},{18,... | collective-permute-start | bytes 3145736 | tf_op jit(solution)/shard_map/ppermute | solution.py:134
  60.2 20.1 %collective-permute-done.10 = bf16[2,256,1024]{2,1,0:T(8,128)(2,1)S(1)} collective-permute-done((bf16[2,256,1024]{2,1,0:T(8,128)(2,1)S(1)}, bf16[2,256,1024]{2,1,0:T(8,128)(2,1)S(1)}, u32[]{:S(2)}, u32[]{:S(2)}) %collective-permute-start.10) | collective-permute-done | bytes 1048608 | tf_op jit(solution)/shard_map/ppermute | solution.py:134
  88.4 8.4 %collective-permute-done.12 = bf16[256,768]{1,0:T(8,128)(2,1)S(1)} collective-permute-done((bf16[256,768]{1,0:T(8,128)(2,1)S(1)}, bf16[256,768]{1,0:T(8,128)(2,1)S(1)}, u32[]{:S(2)}, u32[]{:S(2)}) %collective-permute-start.12) | collective-permute-done | bytes 393248 | tf_op jit(solution)/shard_map/ppermute | solution.py:134
  97.6 8.7 %collective-permute-done.13 = bf16[256,768]{1,0:T(8,128)(2,1)S(1)} collective-permute-done((bf16[256,768]{1,0:T(8,128)(2,1)S(1)}, bf16[256,768]{1,0:T(8,128)(2,1)S(1)}, u32[]{:S(2)}, u32[]{:S(2)}) %collective-permute-start.13) | collective-permute-done | bytes 393248 | tf_op jit(solution)/shard_map/ppermute | solution.py:134
  114.2 60.2 %collective-permute-done.16 = bf16[256,768]{1,0:T(8,128)(2,1)S(1)} collective-permute-done((bf16[256,768]{1,0:T(8,128)(2,1)}, bf16[256,768]{1,0:T(8,128)(2,1)S(1)}, u32[]{:S(2)}, u32[]{:S(2)}) %collective-permute-start.16) | collective-permute-done | bytes 393248 | tf_op jit(solution)/shard_map/ppermute | solution.py:134
  174.6 6.5 %collective-permute-start.18 = (bf16[1024,768]{1,0:T(8,128)(2,1)S(1)}, bf16[1024,768]{1,0:T(8,128)(2,1)}, u32[]{:S(2)}, u32[]{:S(2)}) collective-permute-start(bf16[1024,768]{1,0:T(8,128)(2,1)S(1)} %constant_dynamic-update-slice_fusion.3.refs_6_), channel_id=1, source_target_pairs={{8,0},{10,2},{12,4},{14,6},{16,24},{18,26},{20,28},{22,30},{9,1},{... | collective-permute-start | bytes 4718600 | tf_op jit(solution)/shard_map/ppermute | solution.py:237
  183.3 25.7 %collective-permute-done.15 = bf16[1024,768]{1,0:T(8,128)(2,1)} collective-permute-done((bf16[1024,768]{1,0:T(8,128)(2,1)S(1)}, bf16[1024,768]{1,0:T(8,128)(2,1)}, u32[]{:S(2)}, u32[]{:S(2)}) %collective-permute-start.15) | collective-permute-done | bytes 1572896 | tf_op jit(solution)/shard_map/ppermute | solution.py:236
  209.0 5.8 %collective-permute-done.18 = bf16[1024,768]{1,0:T(8,128)(2,1)} collective-permute-done((bf16[1024,768]{1,0:T(8,128)(2,1)S(1)}, bf16[1024,768]{1,0:T(8,128)(2,1)}, u32[]{:S(2)}, u32[]{:S(2)}) %collective-permute-start.18) | collective-permute-done | bytes 1572896 | tf_op jit(solution)/shard_map/ppermute | solution.py:237
  217.1 6.2 %pad_maximum_fusion.refs_0_.refs_1_.refs_2_ = bf16[4,4,256,1024]{3,2,1,0:T(8,128)(2,1)} fusion(bf16[2,4,256,1024]{3,2,1,0:T(8,128)(2,1)} %collective-permute-done.11, bf16[1,4,256,1024]{3,2,1,0:T(8,128)(2,1)S(1)} %copy-done.5, bf16[1,4,256,1024]{3,2,1,0:T(8,128)(2,1)S(1)} %copy-done.7), kind=kLoop, calls=%fused_computation | loop fusion | flops 8388608 | bytes 16777216 | tf_op jit(solution)/shard_map/concatenate | solution.py:251
  223.2 21.9 %collective-permute-done.19.refs_4_ = bf16[256,768]{1,0:T(8,128)(2,1)S(1)} collective-permute-done((bf16[256,768]{1,0:T(8,128)(2,1)}, bf16[256,768]{1,0:T(8,128)(2,1)S(1)}, u32[]{:S(2)}, u32[]{:S(2)}) %collective-permute-start.19) | collective-permute-done | bytes 393248 | tf_op jit(solution)/shard_map/ppermute | solution.py:134
  245.1 9.3 %project.2.refs_2_ = f32[4,256,768]{2,1,0:T(8,128)} custom-call(s32[7]{0:T(128)S(1)} %stack.84.pick_ref, bf16[4,4,256,1024]{3,2,1,0:T(8,128)(2,1)} %pad_maximum_fusion.refs_0_.refs_1_.refs_2_, bf16[4,4,256,1024]{3,2,1,0:T(8,128)(2,1)} %pad_maximum_fusion.refs_0_.refs_1_.refs_2_, bf16[4,4,256,1024]{3,2,1,0:T(8,128)(2,1)} %pad_maximum_fusion.refs_0_.refs_1_.refs_2_, ...), custom_call_target="tpu_custom_call" | custom-call | flops 4831838208 | bytes 14155776 | tf_op jit(solution)/shard_map/project/pallas_call | solution.py:171
  254.4 5.0 %project.3 = bf16[4,256,768]{2,1,0:T(8,128)(2,1)S(1)} custom-call(s32[5]{0:T(128)S(1)} %stack.72.pick_ref, bf16[4,4,256,1024]{3,2,1,0:T(8,128)(2,1)} %pad_maximum_fusion.refs_0_.refs_1_.refs_2_, bf16[1024,768]{1,0:T(8,128)(2,1)S(1)} %add.83.refs_1_, f32[4,256,768]{2,1,0:T(8,128)} %project.2.refs_2_), custom_call_target="tpu_custom_call" | custom-call | flops 1610612736 | bytes 6815744 | tf_op jit(solution)/shard_map/project/pallas_call | solution.py:171
  264.5 7.7 %collective-permute-done.21.refs_1_ = bf16[256,768]{1,0:T(8,128)(2,1)S(1)} collective-permute-done((bf16[256,768]{1,0:T(8,128)(2,1)S(1)}, bf16[256,768]{1,0:T(8,128)(2,1)S(1)}, u32[]{:S(2)}, u32[]{:S(2)}) %collective-permute-start.21) | collective-permute-done | bytes 393248 | tf_op jit(solution)/shard_map/ppermute | solution.py:134
  272.2 4.2 %collective-permute-done.22.refs_2_ = bf16[256,768]{1,0:T(8,128)(2,1)S(1)} collective-permute-done((bf16[256,768]{1,0:T(8,128)(2,1)S(1)}, bf16[256,768]{1,0:T(8,128)(2,1)S(1)}, u32[]{:S(2)}, u32[]{:S(2)}) %collective-permute-start.22) | collective-permute-done | bytes 393248 | tf_op jit(solution)/shard_map/ppermute | solution.py:134
  277.3 49.4 %assemble.1 = bf16[256,3072]{1,0:T(8,128)(2,1)} custom-call(s32[4]{0:T(128)} %pad_add_fusion.place_ref, bf16[256,768]{1,0:T(8,128)(2,1)} %get-tuple-element.8.refs_0_, bf16[256,768]{1,0:T(8,128)(2,1)} %copy-done.9, bf16[256,768]{1,0:T(8,128)(2,1)} %copy-done.10, bf16[256,768]{1,0:T(8,128)(2,1)} %copy-done.11), custom_call_target="tpu_custom_call" | custom-call | tf_op jit(solution)/shard_map/assemble/pallas_call | solution.py:203
  (79 shorter events, 43.0 us)
Async XLA Ops:
  6.7 14.7 %collective-permute-start = (f32[16,16,128]{2,1,0:T(8,128)S(1)}, f32[16,16,128]{2,1,0:T(8,128)S(1)}, u32[]{:S(2)}, u32[]{:S(2)}) collective-permute-start(f32[16,16,128]{2,1,0:T(8,128)S(1)} %end_states.1), channel_id=1, source_target_pairs={{0,2},{2,4},{4,6},{6,8},{8,10},{10,12},{12,14},{14,16},{16,18},{18... | collective-permute-start | bytes 393224 | tf_op jit(solution)/shard_map/ppermute | solution.py:114
  10.1 11.3 %collective-permute-start.1 = (f32[16,16,128]{2,1,0:T(8,128)S(1)}, f32[16,16,128]{2,1,0:T(8,128)S(1)}, u32[]{:S(2)}, u32[]{:S(2)}) collective-permute-start(f32[16,16,128]{2,1,0:T(8,128)S(1)} %end_states.1), channel_id=1, source_target_pairs={{0,4},{2,6},{4,8},{6,10},{8,12},{10,14},{12,16},{14,18},{16,20},{1... | collective-permute-start | bytes 393224 | tf_op jit(solution)/shard_map/ppermute | solution.py:114
  13.5 7.9 %collective-permute-start.2 = (f32[16,16,128]{2,1,0:T(8,128)S(1)}, f32[16,16,128]{2,1,0:T(8,128)S(1)}, u32[]{:S(2)}, u32[]{:S(2)}) collective-permute-start(f32[16,16,128]{2,1,0:T(8,128)S(1)} %end_states.1), channel_id=1, source_target_pairs={{0,6},{2,8},{4,10},{6,12},{8,14},{10,16},{12,18},{14,20},{16,22},{... | collective-permute-start | bytes 393224 | tf_op jit(solution)/shard_map/ppermute | solution.py:114
  17.9 6.9 %collective-permute-start.3 = (f32[16,16,128]{2,1,0:T(8,128)S(1)}, f32[16,16,128]{2,1,0:T(8,128)S(1)}, u32[]{:S(2)}, u32[]{:S(2)}) collective-permute-start(f32[16,16,128]{2,1,0:T(8,128)S(1)} %end_states.1), channel_id=1, source_target_pairs={{0,8},{2,10},{4,12},{6,14},{8,16},{10,18},{12,20},{14,22},{16,24},... | collective-permute-start | bytes 393224 | tf_op jit(solution)/shard_map/ppermute | solution.py:114
  24.8 8.2 %collective-permute-start.4 = (f32[16,16,128]{2,1,0:T(8,128)S(1)}, f32[16,16,128]{2,1,0:T(8,128)S(1)}, u32[]{:S(2)}, u32[]{:S(2)}) collective-permute-start(f32[16,16,128]{2,1,0:T(8,128)S(1)} %multiply_add_fusion.1), channel_id=1, source_target_pairs={{0,8},{2,10},{4,12},{6,14},{8,16},{10,18},{12,20},{14,22},{16,24},... | collective-permute-start | bytes 393224 | tf_op jit(solution)/shard_map/ppermute | solution.py:114
  28.3 9.5 %collective-permute-start.5 = (f32[16,16,128]{2,1,0:T(8,128)S(1)}, f32[16,16,128]{2,1,0:T(8,128)S(1)}, u32[]{:S(2)}, u32[]{:S(2)}) collective-permute-start(f32[16,16,128]{2,1,0:T(8,128)S(1)} %multiply_add_fusion.1), channel_id=1, source_target_pairs={{0,16},{2,18},{4,20},{6,22},{8,24},{10,26},{12,28},{14,30},{1,17},... | collective-permute-start | bytes 393224 | tf_op jit(solution)/shard_map/ppermute | solution.py:114
  29.6 8.2 %collective-permute-start.6 = (f32[16,16,128]{2,1,0:T(8,128)S(1)}, f32[16,16,128]{2,1,0:T(8,128)S(1)}, u32[]{:S(2)}, u32[]{:S(2)}) collective-permute-start(f32[16,16,128]{2,1,0:T(8,128)S(1)} %multiply_add_fusion.1), channel_id=1, source_target_pairs={{0,24},{2,26},{4,28},{6,30},{1,25},{3,27},{5,29},{7,31}} | collective-permute-start | bytes 393224 | tf_op jit(solution)/shard_map/ppermute | solution.py:114
  44.9 9.2 %collective-permute-start.9 = (bf16[256,1024]{1,0:T(8,128)(2,1)S(1)}, bf16[256,1024]{1,0:T(8,128)(2,1)S(1)}, u32[]{:S(2)}, u32[]{:S(2)}) collective-permute-start(bf16[256,1024]{1,0:T(8,128)(2,1)S(1)} %get-tuple-element.15), channel_id=1, source_target_pairs={{0,4},{2,6},{4,0},{6,2},{8,12},{10,14},{12,8},{14,10},{16,20},{18,... | collective-permute-start | bytes 1572872 | tf_op jit(solution)/shard_map/ppermute | solution.py:134
  46.6 12.2 %collective-permute-start.7 = (bf16[256,1024]{1,0:T(8,128)(2,1)S(1)}, bf16[256,1024]{1,0:T(8,128)(2,1)S(1)}, u32[]{:S(2)}, u32[]{:S(2)}) collective-permute-start(bf16[256,1024]{1,0:T(8,128)(2,1)S(1)} %get-tuple-element.14), channel_id=1, source_target_pairs={{0,2},{2,0},{4,6},{6,4},{8,10},{10,8},{12,14},{14,12},{16,18},{18,... | collective-permute-start | bytes 1572872 | tf_op jit(solution)/shard_map/ppermute | solution.py:134
  54.3 26.1 %collective-permute-start.10 = (bf16[2,256,1024]{2,1,0:T(8,128)(2,1)S(1)}, bf16[2,256,1024]{2,1,0:T(8,128)(2,1)S(1)}, u32[]{:S(2)}, u32[]{:S(2)}) collective-permute-start(bf16[2,256,1024]{2,1,0:T(8,128)(2,1)S(1)} %pad_maximum_fusion.4), channel_id=1, source_target_pairs={{0,2},{2,0},{4,6},{6,4},{8,10},{10,8},{12,14},{14,12},{16,18},{18,... | collective-permute-start | bytes 3145736 | tf_op jit(solution)/shard_map/ppermute | solution.py:134
  58.9 22.2 %collective-permute-start.8 = (bf16[2,256,1024]{2,1,0:T(8,128)(2,1)S(1)}, bf16[2,256,1024]{2,1,0:T(8,128)(2,1)S(1)}, u32[]{:S(2)}, u32[]{:S(2)}) collective-permute-start(bf16[2,256,1024]{2,1,0:T(8,128)(2,1)S(1)} %pad_maximum_fusion.3), channel_id=1, source_target_pairs={{0,4},{2,6},{4,0},{6,2},{8,12},{10,14},{12,8},{14,10},{16,20},{18,... | collective-permute-start | bytes 3145736 | tf_op jit(solution)/shard_map/ppermute | solution.py:134
  84.0 133.0 %collective-permute-start.11 = (bf16[2,4,256,1024]{3,2,1,0:T(8,128)(2,1)}, bf16[2,4,256,1024]{3,2,1,0:T(8,128)(2,1)}, u32[]{:S(2)}, u32[]{:S(2)}) collective-permute-start(bf16[2,4,256,1024]{3,2,1,0:T(8,128)(2,1)} %pad_maximum_fusion.1), channel_id=1, source_target_pairs={{0,1},{1,0},{2,3},{3,2},{4,5},{5,4},{6,7},{7,6},{8,9},{9,8},{10,11... | collective-permute-start | bytes 12582920 | tf_op jit(solution)/shard_map/ppermute | solution.py:134
  84.9 11.9 %collective-permute-start.12 = (bf16[256,768]{1,0:T(8,128)(2,1)S(1)}, bf16[256,768]{1,0:T(8,128)(2,1)S(1)}, u32[]{:S(2)}, u32[]{:S(2)}) collective-permute-start(bf16[256,768]{1,0:T(8,128)(2,1)S(1)} %get-tuple-element.10), channel_id=1, source_target_pairs={{0,2},{2,0},{4,6},{6,4},{8,10},{10,8},{12,14},{14,12},{16,18},{18,... | collective-permute-start | bytes 1179656 | tf_op jit(solution)/shard_map/ppermute | solution.py:134
  86.7 19.7 %collective-permute-start.13 = (bf16[256,768]{1,0:T(8,128)(2,1)S(1)}, bf16[256,768]{1,0:T(8,128)(2,1)S(1)}, u32[]{:S(2)}, u32[]{:S(2)}) collective-permute-start(bf16[256,768]{1,0:T(8,128)(2,1)S(1)} %get-tuple-element.12), channel_id=1, source_target_pairs={{0,4},{2,6},{4,0},{6,2},{8,12},{10,14},{12,8},{14,10},{16,20},{18,... | collective-permute-start | bytes 1179656 | tf_op jit(solution)/shard_map/ppermute | solution.py:134
  87.5 19.6 %collective-permute-start.14 = (bf16[256,768]{1,0:T(8,128)(2,1)S(1)}, bf16[256,768]{1,0:T(8,128)(2,1)S(1)}, u32[]{:S(2)}, u32[]{:S(2)}) collective-permute-start(bf16[256,768]{1,0:T(8,128)(2,1)S(1)} %get-tuple-element.11), channel_id=1, source_target_pairs={{0,6},{2,4},{4,2},{6,0},{8,14},{10,12},{12,10},{14,8},{16,22},{18,... | collective-permute-start | bytes 1179656 | tf_op jit(solution)/shard_map/ppermute | solution.py:134
  107.9 66.6 %collective-permute-start.17 = (bf16[768,768]{1,0:T(8,128)(2,1)}, bf16[768,768]{1,0:T(8,128)(2,1)S(1)}, u32[]{:S(2)}, u32[]{:S(2)}) collective-permute-start(bf16[768,768]{1,0:T(8,128)(2,1)} %constant_dynamic-update-slice_fusion), channel_id=1, source_target_pairs={{0,16},{2,18},{4,20},{6,22},{8,24},{10,26},{12,28},{14,30},{16,0},... | collective-permute-start | bytes 3538952 | tf_op jit(solution)/shard_map/ppermute | solution.py:134
  111.1 63.3 %collective-permute-start.16 = (bf16[256,768]{1,0:T(8,128)(2,1)}, bf16[256,768]{1,0:T(8,128)(2,1)S(1)}, u32[]{:S(2)}, u32[]{:S(2)}) collective-permute-start(bf16[256,768]{1,0:T(8,128)(2,1)} %get-tuple-element.9), channel_id=1, source_target_pairs={{0,16},{2,18},{4,20},{6,22},{8,24},{10,26},{12,28},{14,30},{16,0},... | collective-permute-start | bytes 1179656 | tf_op jit(solution)/shard_map/ppermute | solution.py:134
  112.3 96.7 %collective-permute-start.15 = (bf16[1024,768]{1,0:T(8,128)(2,1)S(1)}, bf16[1024,768]{1,0:T(8,128)(2,1)}, u32[]{:S(2)}, u32[]{:S(2)}) collective-permute-start(bf16[1024,768]{1,0:T(8,128)(2,1)S(1)} %pad_maximum_fusion.2.refs_3_), channel_id=1, source_target_pairs={{8,16},{10,18},{12,20},{14,22},{16,8},{18,10},{20,12},{22,14},{9,1... | collective-permute-start | bytes 4718600 | tf_op jit(solution)/shard_map/ppermute | solution.py:236
  174.6 40.2 %collective-permute-start.18 = (bf16[1024,768]{1,0:T(8,128)(2,1)S(1)}, bf16[1024,768]{1,0:T(8,128)(2,1)}, u32[]{:S(2)}, u32[]{:S(2)}) collective-permute-start(bf16[1024,768]{1,0:T(8,128)(2,1)S(1)} %constant_dynamic-update-slice_fusion.3.refs_6_), channel_id=1, source_target_pairs={{8,0},{10,2},{12,4},{14,6},{16,24},{18,26},{20,28},{22,30},{9,1},{... | collective-permute-start | bytes 4718600 | tf_op jit(solution)/shard_map/ppermute | solution.py:237
  181.1 64.0 %collective-permute-start.20 = (bf16[768,768]{1,0:T(8,128)(2,1)}, bf16[768,768]{1,0:T(8,128)(2,1)}, u32[]{:S(2)}, u32[]{:S(2)}) collective-permute-start(bf16[768,768]{1,0:T(8,128)(2,1)} %constant_dynamic-update-slice_fusion), channel_id=1, source_target_pairs={{0,8},{2,10},{4,12},{6,14},{8,0},{10,2},{12,4},{14,6},{16,24},{18,... | collective-permute-start | bytes 3538952 | tf_op jit(solution)/shard_map/ppermute | solution.py:134
  181.1 64.0 %collective-permute-start.19 = (bf16[256,768]{1,0:T(8,128)(2,1)}, bf16[256,768]{1,0:T(8,128)(2,1)S(1)}, u32[]{:S(2)}, u32[]{:S(2)}) collective-permute-start(bf16[256,768]{1,0:T(8,128)(2,1)} %get-tuple-element.9), channel_id=1, source_target_pairs={{0,8},{2,10},{4,12},{6,14},{8,0},{10,2},{12,4},{14,6},{16,24},{18,... | collective-permute-start | bytes 1179656 | tf_op jit(solution)/shard_map/ppermute | solution.py:134
  260.3 11.9 %collective-permute-start.21 = (bf16[256,768]{1,0:T(8,128)(2,1)S(1)}, bf16[256,768]{1,0:T(8,128)(2,1)S(1)}, u32[]{:S(2)}, u32[]{:S(2)}) collective-permute-start(bf16[256,768]{1,0:T(8,128)(2,1)S(1)} %get-tuple-element.7), channel_id=1, source_target_pairs={{0,2},{2,0},{4,6},{6,4},{8,10},{10,8},{12,14},{14,12},{16,18},{18,... | collective-permute-start | bytes 1179656 | tf_op jit(solution)/shard_map/ppermute | solution.py:134
  260.5 15.9 %collective-permute-start.22 = (bf16[256,768]{1,0:T(8,128)(2,1)S(1)}, bf16[256,768]{1,0:T(8,128)(2,1)S(1)}, u32[]{:S(2)}, u32[]{:S(2)}) collective-permute-start(bf16[256,768]{1,0:T(8,128)(2,1)S(1)} %get-tuple-element.6), channel_id=1, source_target_pairs={{0,4},{2,6},{4,0},{6,2},{8,12},{10,14},{12,8},{14,10},{16,20},{18,... | collective-permute-start | bytes 1179656 | tf_op jit(solution)/shard_map/ppermute | solution.py:134
  260.8 15.6 %collective-permute-start.23 = (bf16[256,768]{1,0:T(8,128)(2,1)S(1)}, bf16[256,768]{1,0:T(8,128)(2,1)S(1)}, u32[]{:S(2)}, u32[]{:S(2)}) collective-permute-start(bf16[256,768]{1,0:T(8,128)(2,1)S(1)} %get-tuple-element.5), channel_id=1, source_target_pairs={{0,6},{2,4},{4,2},{6,0},{8,14},{10,12},{12,10},{14,8},{16,22},{18,... | collective-permute-start | bytes 1179656 | tf_op jit(solution)/shard_map/ppermute | solution.py:134
  (13 other events, 183.5 us)

commit v3 on v1

--- a/solution.py
+++ b/solution.py
@@ -7,6 +7,7 @@
 
 LANES = 128
 RADIX = 4
+PLANE = 4
 
 
 def spread_signal(k_ref, v_ref, sig_ref):
@@ -98,8 +99,8 @@
         conv_kernel,
         grid=(chan // width,),
         in_specs=[wide, wide, wide, moded, moded, single, moded],
-        out_specs=wide,
-        out_shape=jax.ShapeDtypeStruct((rows, chan), jnp.bfloat16),
+        out_specs=pl.BlockSpec((None, rows, width), lambda i: (i, 0, 0)),
+        out_shape=jax.ShapeDtypeStruct((chan // width, rows, width), jnp.bfloat16),
         scratch_shapes=[spread, spread],
         compiler_params=pltpu.CompilerParams(vmem_limit_bytes=32 << 20),
         cost_estimate=pl.CostEstimate(
@@ -109,37 +110,310 @@
     )(q, k, v, rate, residue, skip, enter)
 
 
-def shift_ctx(x, by, count):
+def shift_ctx(x, by):
+    count = lax.axis_size("ctx")
     return lax.ppermute(x, "ctx", [(i, i + by) for i in range(count - by)])
+
+
+def exchange(x, axis, flip):
+    count = lax.axis_size(axis)
+    return lax.ppermute(x, axis, [(i, i ^ flip) for i in range(count)])
+
+
+def tie(*values):
+    return lax.optimization_barrier(values)
 
 
 def entering_states(ends, rate, rows):
     count = lax.axis_size("ctx")
     total = jnp.zeros_like(ends)
     for k in range(1, min(RADIX, count - 1) + 1):
-        total = total + jnp.exp(-rate * float(rows * (k - 1))) * shift_ctx(ends, k, count)
+        total = total + jnp.exp(-rate * float(rows * (k - 1))) * shift_ctx(ends, k)
     stride = RADIX
     while stride < count:
         base = total
         for k in range(1, RADIX):
             if stride * k < count:
-                total = total + jnp.exp(-rate * float(rows * stride * k)) * shift_ctx(base, stride * k, count)
+                total = total + jnp.exp(-rate * float(rows * stride * k)) * shift_ctx(base, stride * k)
         stride *= RADIX
     return total
+
+
+def fold_pair(ends, before, rate, flip, span):
+    other = exchange(ends, "ctx", flip)
+    later = (lax.axis_index("ctx") & flip) != 0
+    decay = jnp.exp(-rate * float(span))
+    both = jnp.where(later, decay * other + ends, decay * ends + other)
+    return both, other, later
+
+
+def take_copies(copies):
+    for copy in copies:
+        copy.start()
+    return copies
+
+
+def project(flags, places, gated, weights, accs, out_widths, out_dtype):
+    rows, depth = gated[0][0][0].shape[1:]
+    chunk = depth // PLANE
+    cols = sum(out_widths)
+    blocks = len(weights)
+    arrays = []
+
+    def index_of(array):
+        for at, known in enumerate(arrays):
+            if known is array:
+                return at
+        arrays.append(array)
+        return len(arrays) - 1
+
+    gated_at = [[(index_of(a), at) for a, at in rows_of] for rows_of in gated]
+    plan = []
+    for b, (flag, pieces) in enumerate(weights):
+        for choices, choice_flag, place, offset, first_col in pieces:
+            plan.append((b, [index_of(a) for a in choices], choice_flag, place, offset, first_col, choices[0].shape))
+    count_in = len(arrays)
+    parts = len(out_widths)
+    count_acc = 0 if accs is None else len(accs)
+
+    def kernel(flag_ref, place_ref, *refs):
+        ins, refs = refs[:count_in], refs[count_in:]
+        acc_refs, refs = refs[:count_acc], refs[count_acc:]
+        out_refs, (gated_buf, weight_buf, gated_sems, weight_sems) = refs[: PLANE * parts], refs[PLANE * parts :]
+
+        for n, (b, choices, choice_flag, place, offset, first_col, shape) in enumerate(plan):
+            start = pl.multiple_of(b * depth + place_ref[place] * chunk + offset, 64)
+            target = weight_buf.at[pl.ds(start, shape[0]), pl.ds(first_col, shape[1])]
+            for c, choice in enumerate(choices):
+                copy = pltpu.make_async_copy(ins[choice], target, weight_sems.at[n])
+                if choice_flag is None:
+                    copy.start()
+                else:
+                    pl.when(flag_ref[choice_flag] == c)(copy.start)
+        for r in range(PLANE):
+            for b, (flag, _) in enumerate(weights):
+                for source in range(len(gated_at)):
+                    at, index = gated_at[source][r]
+                    copy = pltpu.make_async_copy(ins[at].at[index], gated_buf.at[r, b], gated_sems.at[r, b])
+                    pl.when(flag_ref[flag] == source)(copy.start)
+        for n, (b, choices, choice_flag, place, offset, first_col, shape) in enumerate(plan):
+            start = pl.multiple_of(b * depth + place_ref[place] * chunk + offset, 64)
+            target = weight_buf.at[pl.ds(start, shape[0]), pl.ds(first_col, shape[1])]
+            pltpu.make_async_copy(ins[choices[0]], target, weight_sems.at[n]).wait()
+        for r in range(PLANE):
+            for b in range(blocks):
+                at, index = gated_at[0][r]
+                pltpu.make_async_copy(ins[at].at[index], gated_buf.at[r, b], gated_sems.at[r, b]).wait()
+            first_col = 0
+            for part, width in enumerate(out_widths):
+                total = None
+                for b in range(blocks):
+                    product = jnp.dot(
+                        gated_buf[r, b],
+                        weight_buf[pl.ds(b * depth, depth), pl.ds(first_col, width)],
+                        preferred_element_type=jnp.float32,
+                    )
+                    total = product if total is None else total + product
+                if accs is not None:
+                    total = total + acc_refs[part * PLANE + r][...]
+                out_refs[part * PLANE + r][...] = total.astype(out_dtype)
+                first_col += width
+
+    smem = pl.BlockSpec(memory_space=pltpu.SMEM)
+    vmem = pl.BlockSpec(memory_space=pltpu.VMEM)
+    anywhere = pl.BlockSpec(memory_space=pl.ANY)
+    made = pl.pallas_call(
+        kernel,
+        in_specs=[smem, smem] + [anywhere] * count_in + [vmem] * count_acc,
+        out_specs=[vmem] * (PLANE * parts),
+        out_shape=[jax.ShapeDtypeStruct((rows, width), out_dtype) for width in out_widths for _ in range(PLANE)],
+        scratch_shapes=[
+            pltpu.VMEM((PLANE, blocks, rows, depth), jnp.bfloat16),
+            pltpu.VMEM((blocks * depth, cols), jnp.bfloat16),
+            pltpu.SemaphoreType.DMA((PLANE, blocks)),
+            pltpu.SemaphoreType.DMA((len(plan),)),
+        ],
+        compiler_params=pltpu.CompilerParams(vmem_limit_bytes=32 << 20),
+        cost_estimate=pl.CostEstimate(
+            flops=2 * PLANE * rows * depth * blocks * cols,
+            bytes_accessed=2 * blocks * depth * (PLANE * rows + cols),
+            transcendentals=0,
+        ),
+        name="project",
+    )(flags, places, *arrays, *([] if accs is None else accs))
+    return [made[part * PLANE : (part + 1) * PLANE] for part in range(parts)]
+
+
+def assemble(spot, parts):
+    rows = parts[0][0].shape[0]
+    widths = [part[0].shape[1] for part in parts]
+    cols = sum(widths)
+
+    def kernel(spot_ref, *refs):
+        out_ref = refs[-1]
+        group = pl.program_id(0)
+        for r in range(PLANE):
+
+            @pl.when((spot_ref[0] ^ r) == group)
+            def _():
+                first = 0
+                for part, width in enumerate(widths):
+                    out_ref[:, pl.ds(first, width)] = refs[part * PLANE + r][...]
+                    first += width
+
+    flat = [piece for part in parts for piece in part]
+    return pl.pallas_call(
+        kernel,
+        grid=(PLANE,),
+        in_specs=[pl.BlockSpec(memory_space=pltpu.SMEM)] + [pl.BlockSpec(p.shape, lambda i: (0, 0)) for p in flat],
+        out_specs=pl.BlockSpec((rows, cols), lambda i: (0, i)),
+        out_shape=jax.ShapeDtypeStruct((rows, cols * PLANE), flat[0].dtype),
+        name="assemble",
+    )(spot.reshape(1), *flat)
+
+
+def split_block(q, k, v, residue, rate, skip, w_out):
+    rows, chan = q.shape
+    me = lax.axis_index("ctx")
+    core = lax.axis_index("ch")
+    spot, plane = me & (PLANE - 1), me // PLANE
+    count = lax.axis_size("ctx")
+    chunk, feats = w_out.shape
+    cols = feats // PLANE
+    far_flip, near_flip = 2 * PLANE, PLANE
+
+    def far(x):
+        return exchange(x, "ctx", far_flip)
+
+    def near(x):
+        return exchange(x, "ctx", near_flip)
+
+    middle = [i for i in range(count) if PLANE <= i < 3 * PLANE]
+
+    def across(x):
+        return lax.ppermute(x, "ctx", [(i, i ^ (3 * PLANE)) for i in middle])
+
+    def outward(x):
+        return lax.ppermute(x, "ctx", [(i, i ^ PLANE) for i in middle])
+
+    own = [lax.dynamic_slice_in_dim(w_out, (spot ^ r) * cols, cols, axis=1) for r in range(PLANE)]
+    w0 = own[0]
+    f0, n0 = far(w0), near(w0)
+    w1, w2, w3 = [exchange(own[r], "ctx", r) for r in range(1, PLANE)]
+    ends = end_states(k, v, rate)
+    both, other, later = fold_pair(ends, None, rate, 1, rows)
+    before = jnp.where(later, other, 0.0)
+    f0, n0, w0, w1, w2, w3, both, before, rate = tie(f0, n0, w0, w1, w2, w3, both, before, rate)
+
+    f1, n1 = far(w1), near(w1)
+    half = chunk // 2
+    both, other, later = fold_pair(both, before, rate, 2, 2 * rows)
+    odd = (me & 1).astype(jnp.float32)
+    before = before + jnp.where(later, jnp.exp(-rate * (odd * rows)) * other, 0.0)
+    last = shift_ctx(both, PLANE)
+    decay = jnp.exp(-rate * float(PLANE * rows))
+    carried = last + decay * shift_ctx(both + decay * last, 2 * PLANE)
+    enter = before + jnp.exp(-rate * (spot * rows).astype(jnp.float32)) * carried
+    f1, n1, w2, w3, enter, q = tie(f1, n1, w2, w3, enter, q)
+
+    f2a, n2a = far(w2[:half]), near(w2[:half])
+    gated = gated_conv(q, k, v, rate, residue, skip, enter)
+    one, two = gated
+    f2a, n2a, w2, w3, one, two = tie(f2a, n2a, w2, w3, one, two)
+
+    f2b, n2b = far(w2[half:]), near(w2[half:])
+    one_x, two_y = exchange(one, "ctx", 1), exchange(two, "ctx", 2)
+    f2b, n2b, w3, f0, w0, one_x, two_y = tie(f2b, n2b, w3, f0, w0, one_x, two_y)
+
+    f3, n3 = far(w3), near(w3)
+    out0, mid0 = outward(f0), across(w0)
+    one_pair = jnp.stack([one, one_x])
+    two_pair = jnp.stack([two, two_y])
+    one_far, two_far = exchange(one_pair, "ctx", 2), exchange(two_pair, "ctx", 1)
+    one_pair_t, two_pair_t = exchange(one_pair, "ch", 1), exchange(two_pair, "ch", 1)
+    f3, n3, out0, mid0, one_far, two_far, one_pair_t, two_pair_t = tie(
+        f3, n3, out0, mid0, one_far, two_far, one_pair_t, two_pair_t
+    )
+
+    wide = 2 * cols // 3
+    rest_out = jnp.concatenate([f1, f2a, f2b, f3])
+    rest_mid = jnp.concatenate([w1, w2, w3])
+    outA, midA = outward(rest_out[:, :wide]), across(rest_mid[:, :wide])
+    one_far_t, two_far_t = exchange(one_far, "ch", 1), exchange(two_far, "ch", 1)
+
+    def row_blocks(pair_one, far_one, pair_two, far_two):
+        return [
+            [(pair_one, 0), (pair_one, 1), (far_one, 0), (far_one, 1)],
+            [(pair_two, 0), (far_two, 0), (pair_two, 1), (far_two, 1)],
+        ]
+
+    sources = row_blocks(one_pair, one_far, two_pair, two_far) + row_blocks(one_pair_t, one_far_t, two_pair_t, two_far_t)
+
+    def source_of(b):
+        return jnp.where(b // 2 == core, b & 1, 2 + (b & 1))
+
+    ends_plane = jnp.where((plane == 0) | (plane == 3), 0, 1)
+    flags = jnp.stack([source_of(plane), source_of(plane ^ 1), source_of(plane ^ 2), source_of(plane ^ 3), ends_plane])
+    flags = flags.astype(jnp.int32)
+    places = jnp.stack([spot ^ r for r in range(PLANE)]).astype(jnp.int32)
+
+    def pieces(p0, p1, p2a, p2b, p3):
+        return [((p0,), None, 0, 0, 0), ((p1,), None, 1, 0, 0), ((p2a,), None, 2, 0, 0), ((p2b,), None, 2, half, 0), ((p3,), None, 3, 0, 0)]
+
+    weights = [
+        (0, [((w,), None, r, 0, 0) for r, w in enumerate((w0, w1, w2, w3))]),
+        (1, pieces(n0, n1, n2a, n2b, n3)),
+        (2, pieces(f0, f1, f2a, f2b, f3)),
+    ]
+    accs = project(flags, places, sources, weights, None, [wide, cols - wide], jnp.float32)
+    tied = tie(outA, midA, rest_out, rest_mid, *accs[0], *accs[1])
+    outA, midA, rest_out, rest_mid = tied[:4]
+    accs = [tied[4 : 4 + PLANE], tied[4 + PLANE :]]
+
+    outB, midB = outward(rest_out[:, wide:]), across(rest_mid[:, wide:])
+
+    def last_block(out_first, mid_first, out_rest, mid_rest):
+        found = [((out_first, mid_first), 4, 0, 0, 0)]
+        for r in range(1, PLANE):
+            at = (r - 1) * chunk
+            found.append(((out_rest[at : at + chunk], mid_rest[at : at + chunk]), 4, r, 0, 0))
+        return [(3, found)]
+
+    (madeA,) = project(
+        flags, places, sources, last_block(out0[:, :wide], mid0[:, :wide], outA, midA), accs[0], [wide], jnp.bfloat16
+    )
+    backA = [madeA[0]] + [exchange(madeA[r], "ctx", r) for r in range(1, PLANE)]
+    (madeB,) = project(
+        flags, places, sources, last_block(out0[:, wide:], mid0[:, wide:], outB, midB), accs[1], [cols - wide], jnp.bfloat16
+    )
+    backB = [madeB[0]] + [exchange(madeB[r], "ctx", r) for r in range(1, PLANE)]
+    return assemble(spot.astype(jnp.int32), [backA, backB])
 
 
 def body(q, k, v, residue, rate, skip, w_out):
     rows, chan = q.shape
     modes = rate.shape[0]
     groups = chan // LANES
-    w_full = lax.all_gather(w_out, "ctx", axis=0, tiled=True)
+    count, cores = lax.axis_size("ctx"), lax.axis_size("ch")
+    chunk, feats = w_out.shape
+    split = (
+        count == 4 * PLANE
+        and cores == 2
+        and chan == 8 * chunk
+        and chunk % LANES == 0
+        and feats % (PLANE * LANES) == 0
+    )
     rate = rate.reshape(modes, groups, LANES)
     residue = residue.reshape(modes, groups, LANES)
     skip = skip.reshape(groups, LANES)
+    if split:
+        return split_block(q, k, v, residue, rate, skip, w_out)
     ends = end_states(k, v, rate)
     enter = entering_states(ends, rate, rows)
     gated = gated_conv(q, k, v, rate, residue, skip, enter)
+    gated = gated.transpose(1, 0, 2).reshape(rows, chan)
     full_gated = lax.all_gather(gated, "ch", axis=1, tiled=True)
+    w_full = lax.all_gather(w_out, "ctx", axis=0, tiled=True)
     mixed = jnp.dot(full_gated, w_full, preferred_element_type=jnp.float32)
     return mixed.astype(jnp.bfloat16)
 

time: 361 us -> 207 us (0.57)
  waiting for transfers between devices: 297 us -> 86.2 us
  starting transfers between devices: 19 us -> 53.6 us
  local copies, waits for them, and re-layouts: 3.45 us -> 30.9 us
  Pallas kernels: 10.8 us -> 30.5 us
  matrix products: 13 us -> 0 us
  between operations: 13.5 us -> 0.7 us
    all_gather x2 -> x0, waiting for transfers between devices: 283 us -> none  [the longest x1 273 us: body(): w_full = lax.all_gather(w_out, 'ctx', axis=0, tiled=True)]
    ppermute x0 -> x35, waiting for transfers between devices: none -> 68.4 us  [the longest x29 50 us: exchange(): return lax.ppermute(x, axis, [(i, i ^ flip) for i in range(count)])]
    ppermute x0 -> x35, starting transfers between devices: none -> 49.3 us  [the longest x29 33.7 us: exchange(): return lax.ppermute(x, axis, [(i, i ^ flip) for i in range(count)])]
    pallas_call x0 -> x4, Pallas kernels: none -> 20.6 us  [the longest x3 17.5 us: project(): pl.pallas_call(kernel, in_specs=[smem, smem] + [anywhere] * count_in + [v...]
    unnamed x12 -> x113, local copies, waits for them, and re-layouts: 3.45 us -> 23.9 us
    ppermute x7 -> x2, starting transfers between devices: 19 us -> 4.3 us  [shift_ctx(): return lax.ppermute(x, 'ctx', [(i, i + by) for i in range(count - by)])]
    dot_general x1 -> x0, matrix products: 13 us -> none  [body(): mixed = jnp.dot(full_gated, w_full, preferred_element_type=jnp.float32)]
    slice x0 -> x13, local copies, waits for them, and re-layouts: none -> 5.74 us  [the longest x2 2.09 us: split_block(): outB, midB = (outward(rest_out[:, wide:]), across(rest_mid[:, wide:]))]
  transfers between devices with their start and end apart: 9 -> 37, of which waited for: 6 -> 16; matrix products, arithmetic and copies ran while one was open for 0% -> 6% of each run, Pallas kernels for 0% -> 12%
where the time goes in v3:
time: 207 us; the launch traced here: 206 us
  waiting for transfers between devices  86.2 us (42%)
  starting transfers between devices  53.6 us (26%)
  local copies, waits for them, and re-layouts  30.9 us (15%)
  Pallas kernels  30.5 us (15%)
  other arithmetic  3.72 us (2%)
    ppermute x29, waiting for transfers between devices, exchange(): return lax.ppermute(x, axis, [(i, i ^ flip) for i in range(count)])  50 us
    ppermute x29, starting transfers between devices, exchange(): return lax.ppermute(x, axis, [(i, i ^ flip) for i in range(count)])  33.7 us
    unnamed x113, local copies, waits for them, and re-layouts  23.9 us
    ppermute x2, waiting for transfers between devices, shift_ctx(): return lax.ppermute(x, 'ctx', [(i, i + by) for i in range(count - by)])  17.8 us
    pallas_call x3, Pallas kernels, project(): pl.pallas_call(kernel, in_specs=[smem, smem] + [anywhere] * count_in + [v...  17.5 us
    ppermute x3, waiting for transfers between devices, across(): return lax.ppermute(x, 'ctx', [(i, i ^ 3 * PLANE) for i in middle])  9.93 us
    ppermute x3, waiting for transfers between devices, outward(): return lax.ppermute(x, 'ctx', [(i, i ^ PLANE) for i in middle])  8.48 us
    ppermute x3, starting transfers between devices, outward(): return lax.ppermute(x, 'ctx', [(i, i ^ PLANE) for i in middle])  7.98 us
  transfers between devices with their start and end apart: 37, of which 16 were waited for; matrix products, arithmetic and copies ran while one was open for 6% of the time, Pallas kernels for 12%

profile of v3, /device:TPU:8, one launch (start us, length us, event | category | flops | bytes accessed | tf_op | source)
XLA Modules:
  0.0 205.6 jit_solution(7897411343395133588)
XLA Ops:
  3.4 3.2 %end_states.1 = f32[16,16,128]{2,1,0:T(8,128)S(1)} custom-call(bf16[256,2048]{1,0:T(8,128)(2,1)S(1)} %copy-done, bf16[256,2048]{1,0:T(8,128)(2,1)S(1)} %copy-done.2, f32[16,16,128]{2,1,0:T(8,128)S(1)} %bitcast.23), custom_call_target="tpu_custom_call" | custom-call | flops 16777216 | bytes 2097152 | tf_op jit(solution)/shard_map/end_states/pallas_call | solution.py:77
  9.2 2.6 %collective-permute-start = (bf16[256,768]{1,0:T(8,128)(2,1)S(1)}, bf16[256,768]{1,0:T(8,128)(2,1)S(1)}, u32[]{:S(2)}, u32[]{:S(2)}) collective-permute-start(bf16[256,768]{1,0:T(8,128)(2,1)S(1)} %get-tuple-element.88.refs_8_), channel_id=1, source_target_pairs={{0,16},{2,18},{4,20},{6,22},{8,24},{10,26},{12,28},{14,30},{16,0},... | collective-permute-start | bytes 1179656 | tf_op jit(solution)/shard_map/ppermute | solution.py:120
  17.4 10.9 %collective-permute-done.refs_17_ = bf16[256,768]{1,0:T(8,128)(2,1)S(1)} collective-permute-done((bf16[256,768]{1,0:T(8,128)(2,1)S(1)}, bf16[256,768]{1,0:T(8,128)(2,1)S(1)}, u32[]{:S(2)}, u32[]{:S(2)}) %collective-permute-start) | collective-permute-done | bytes 393248 | tf_op jit(solution)/shard_map/ppermute | solution.py:120
  32.8 4.1 %collective-permute-done.8 = f32[16,16,128]{2,1,0:T(8,128)S(1)} collective-permute-done((f32[16,16,128]{2,1,0:T(8,128)S(1)}, f32[16,16,128]{2,1,0:T(8,128)S(1)}, u32[]{:S(2)}, u32[]{:S(2)}) %collective-permute-start.8) | collective-permute-done | bytes 131104 | tf_op jit(solution)/shard_map/ppermute | solution.py:120
  36.9 2.4 %collective-permute-start.9 = (f32[16,16,128]{2,1,0:T(8,128)S(1)}, f32[16,16,128]{2,1,0:T(8,128)S(1)}, u32[]{:S(2)}, u32[]{:S(2)}) collective-permute-start(f32[16,16,128]{2,1,0:T(8,128)S(1)} %add_select_fusion), channel_id=1, source_target_pairs={{0,8},{2,10},{4,12},{6,14},{8,16},{10,18},{12,20},{14,22},{16,24},... | collective-permute-start | bytes 393224 | tf_op jit(solution)/shard_map/ppermute | solution.py:115
  39.4 2.6 %collective-permute-start.7 = (bf16[256,768]{1,0:T(8,128)(2,1)S(1)}, bf16[256,768]{1,0:T(8,128)(2,1)}, u32[]{:S(2)}, u32[]{:S(2)}) collective-permute-start(bf16[256,768]{1,0:T(8,128)(2,1)S(1)} %collective-permute-done.2.refs_9_), channel_id=1, source_target_pairs={{0,8},{2,10},{4,12},{6,14},{8,0},{10,2},{12,4},{14,6},{16,24},{18,... | collective-permute-start | bytes 1179656 | tf_op jit(solution)/shard_map/ppermute | solution.py:120
  42.0 8.2 %collective-permute-done.9 = f32[16,16,128]{2,1,0:T(8,128)S(1)} collective-permute-done((f32[16,16,128]{2,1,0:T(8,128)S(1)}, f32[16,16,128]{2,1,0:T(8,128)S(1)}, u32[]{:S(2)}, u32[]{:S(2)}) %collective-permute-start.9) | collective-permute-done | bytes 131104 | tf_op jit(solution)/shard_map/ppermute | solution.py:115
  53.8 9.6 %collective-permute-done.10 = f32[16,16,128]{2,1,0:T(8,128)} collective-permute-done((f32[16,16,128]{2,1,0:T(8,128)}, f32[16,16,128]{2,1,0:T(8,128)}, u32[]{:S(2)}, u32[]{:S(2)}) %collective-permute-start.10) | collective-permute-done | bytes 131104 | tf_op jit(solution)/shard_map/ppermute | solution.py:115
  64.5 3.5 %collective-permute-start.11 = (bf16[128,768]{1,0:T(8,128)(2,1)S(1)}, bf16[128,768]{1,0:T(8,128)(2,1)S(1)}, u32[]{:S(2)}, u32[]{:S(2)}) collective-permute-start(bf16[128,768]{1,0:T(8,128)(2,1)S(1)} %slice.68), channel_id=1, source_target_pairs={{0,16},{2,18},{4,20},{6,22},{8,24},{10,26},{12,28},{14,30},{16,0},... | collective-permute-start | bytes 589832 | tf_op jit(solution)/shard_map/ppermute | solution.py:120
  69.3 6.7 %gated_conv.1 = bf16[2,256,1024]{2,1,0:T(8,128)(2,1)S(1)} custom-call(bf16[256,2048]{1,0:T(8,128)(2,1)S(1)} %copy-done.8, bf16[256,2048]{1,0:T(8,128)(2,1)S(1)} %copy-done.1, bf16[256,2048]{1,0:T(8,128)(2,1)S(1)} %copy-done.3, f32[16,16,128]{2,1,0:T(8,128)S(1)} %bitcast.27, f32[16,16,128]{2,1,0:T(8,128)S(1)} %bitcast.28, f32[16,128]{1,0:T(8,128)S(1)} %bitcast.29, ...), custom_call_target="tpu_custom_call" | custom-call | flops 33554432 | bytes 4194304 | tf_op jit(solution)/shard_map/gated_conv/pallas_call | solution.py:98
  80.2 4.6 %collective-permute-done.13.refs_20_ = bf16[128,768]{1,0:T(8,128)(2,1)S(1)} collective-permute-done((bf16[128,768]{1,0:T(8,128)(2,1)S(1)}, bf16[128,768]{1,0:T(8,128)(2,1)S(1)}, u32[]{:S(2)}, u32[]{:S(2)}) %collective-permute-start.13) | collective-permute-done | bytes 196640 | tf_op jit(solution)/shard_map/ppermute | solution.py:120
  89.3 5.2 %collective-permute-start.18 = (bf16[256,768]{1,0:T(8,128)(2,1)S(1)}, bf16[256,768]{1,0:T(8,128)(2,1)S(1)}, u32[]{:S(2)}, u32[]{:S(2)}) collective-permute-start(bf16[256,768]{1,0:T(8,128)(2,1)S(1)} %copy-done.13), channel_id=1, source_target_pairs={{0,8},{2,10},{4,12},{6,14},{8,0},{10,2},{12,4},{14,6},{16,24},{18,... | collective-permute-start | bytes 1179656 | tf_op jit(solution)/shard_map/ppermute | solution.py:120
  94.7 3.1 %collective-permute-done.17.refs_21_ = bf16[256,768]{1,0:T(8,128)(2,1)S(1)} collective-permute-done((bf16[256,768]{1,0:T(8,128)(2,1)S(1)}, bf16[256,768]{1,0:T(8,128)(2,1)S(1)}, u32[]{:S(2)}, u32[]{:S(2)}) %collective-permute-start.17) | collective-permute-done | bytes 393248 | tf_op jit(solution)/shard_map/ppermute | solution.py:120
  97.8 12.9 %collective-permute-done.18.refs_16_ = bf16[256,768]{1,0:T(8,128)(2,1)S(1)} collective-permute-done((bf16[256,768]{1,0:T(8,128)(2,1)S(1)}, bf16[256,768]{1,0:T(8,128)(2,1)S(1)}, u32[]{:S(2)}, u32[]{:S(2)}) %collective-permute-start.18) | collective-permute-done | bytes 393248 | tf_op jit(solution)/shard_map/ppermute | solution.py:120
  110.7 4.4 %collective-permute-start.19 = (bf16[256,768]{1,0:T(8,128)(2,1)S(1)}, bf16[256,768]{1,0:T(8,128)(2,1)S(1)}, u32[]{:S(2)}, u32[]{:S(2)}) collective-permute-start(bf16[256,768]{1,0:T(8,128)(2,1)S(1)} %copy-done.28), channel_id=1, source_target_pairs={{8,0},{10,2},{12,4},{14,6},{16,24},{18,26},{20,28},{22,30},{9,1},{... | collective-permute-start | bytes 1179656 | tf_op jit(solution)/shard_map/ppermute | solution.py:297
  115.1 8.3 %collective-permute-done.19 = bf16[256,768]{1,0:T(8,128)(2,1)S(1)} collective-permute-done((bf16[256,768]{1,0:T(8,128)(2,1)S(1)}, bf16[256,768]{1,0:T(8,128)(2,1)S(1)}, u32[]{:S(2)}, u32[]{:S(2)}) %collective-permute-start.19) | collective-permute-done | bytes 393248 | tf_op jit(solution)/shard_map/ppermute | solution.py:297
  125.5 9.9 %collective-permute-done.20 = bf16[256,768]{1,0:T(8,128)(2,1)S(1)} collective-permute-done((bf16[256,768]{1,0:T(8,128)(2,1)S(1)}, bf16[256,768]{1,0:T(8,128)(2,1)S(1)}, u32[]{:S(2)}, u32[]{:S(2)}) %collective-permute-start.20) | collective-permute-done | bytes 393248 | tf_op jit(solution)/shard_map/ppermute | solution.py:294
  142.7 2.3 %collective-permute-start.27 = (bf16[768,512]{1,0:T(8,128)(2,1)}, bf16[768,512]{1,0:T(8,128)(2,1)}, u32[]{:S(2)}, u32[]{:S(2)}) collective-permute-start(bf16[768,512]{1,0:T(8,128)(2,1)} %slice.90), channel_id=1, source_target_pairs={{8,0},{10,2},{12,4},{14,6},{16,24},{18,26},{20,28},{22,30},{9,1},{... | collective-permute-start | bytes 2359304 | tf_op jit(solution)/shard_map/ppermute | solution.py:297
  158.3 11.1 %project.3 = (f32[256,512]{1,0:T(8,128)S(1)}, f32[256,512]{1,0:T(8,128)S(1)}, f32[256,512]{1,0:T(8,128)S(1)}, f32[256,512]{1,0:T(8,128)S(1)}, f32[256,256]{1,0:T...) custom-call(s32[5]{0:T(128)S(1)} %stack.54.flag_ref, ...), custom_call_target="tpu_custom_call" | custom-call | flops 4831838208 | bytes 11010048 | tf_op jit(solution)/shard_map/project/pallas_call | solution.py:225
  170.5 3.6 %collective-permute-start.33 = (bf16[768,256]{1,0:T(8,128)(2,1)S(1)}, bf16[768,256]{1,0:T(8,128)(2,1)S(1)}, u32[]{:S(2)}, u32[]{:S(2)}) collective-permute-start(bf16[768,256]{1,0:T(8,128)(2,1)S(1)} %slice.84), channel_id=1, source_target_pairs={{8,16},{10,18},{12,20},{14,22},{16,8},{18,10},{20,12},{22,14},{9,1... | collective-permute-start | bytes 1179656 | tf_op jit(solution)/shard_map/ppermute | solution.py:294
  178.0 3.0 %project.4 = (bf16[256,512]{1,0:T(8,128)(2,1)S(1)}, bf16[256,512]{1,0:T(8,128)(2,1)S(1)}, bf16[256,512]{1,0:T(8,128)(2,1)S(1)}, bf16[256,512]{1,0:T(8,128)(2,1)S(1)}) custom-call(s32[5]{0:T(128)S(1)} %stack.54.flag_ref, s32[4]{0:T(128)S(1)} %pad_add_fusion.place_ref, bf16[2,256,1024]{2,1,0:T(8,128)(2,1)S(1)} %pad_maximum_fusion.refs_0_, ...), custom_call_target="tpu_custom_call" | custom-call | flops 1073741824 | bytes 3145728 | tf_op jit(solution)/shard_map/project/pallas_call | solution.py:225
  184.9 3.4 %project.5 = (bf16[256,256]{1,0:T(8,128)(2,1)S(1)}, bf16[256,256]{1,0:T(8,128)(2,1)S(1)}, bf16[256,256]{1,0:T(8,128)(2,1)S(1)}, bf16[256,256]{1,0:T(8,128)(2,1)S(1)}) custom-call(s32[5]{0:T(128)S(1)} %stack.54.flag_ref, s32[4]{0:T(128)S(1)} %pad_add_fusion.place_ref, bf16[2,256,1024]{2,1,0:T(8,128)(2,1)S(1)} %pad_maximum_fusion.refs_0_, ...), custom_call_target="tpu_custom_call" | custom-call | flops 536870912 | bytes 2621440 | tf_op jit(solution)/shard_map/project/pallas_call | solution.py:225
  192.5 7.6 %collective-permute-done.30.refs_2_ = bf16[256,512]{1,0:T(8,128)(2,1)S(1)} collective-permute-done((bf16[256,512]{1,0:T(8,128)(2,1)S(1)}, bf16[256,512]{1,0:T(8,128)(2,1)S(1)}, u32[]{:S(2)}, u32[]{:S(2)}) %collective-permute-start.30) | collective-permute-done | bytes 262176 | tf_op jit(solution)/shard_map/ppermute | solution.py:120
  202.6 3.0 %assemble.1 = bf16[256,3072]{1,0:T(8,128)(2,1)} custom-call(s32[1]{0:T(128)} %bitcast.spot_ref, bf16[256,512]{1,0:T(8,128)(2,1)} %copy-done.20, bf16[256,512]{1,0:T(8,128)(2,1)} %copy-done.46, bf16[256,512]{1,0:T(8,128)(2,1)} %copy-done.47, bf16[256,512]{1,0:T(8,128)(2,1)} %copy-done.48, bf16[256,256]{1,0:T(8,128)(2,1)} %copy-done.25, ...), custom_call_target="tpu_custom_call" | custom-call | tf_op jit(solution)/shard_map/assemble/pallas_call | solution.py:265
  (194 shorter events, 68.5 us)
Async XLA Ops:
  9.2 19.0 %collective-permute-start = (bf16[256,768]{1,0:T(8,128)(2,1)S(1)}, bf16[256,768]{1,0:T(8,128)(2,1)S(1)}, u32[]{:S(2)}, u32[]{:S(2)}) collective-permute-start(bf16[256,768]{1,0:T(8,128)(2,1)S(1)} %get-tuple-element.88.refs_8_), channel_id=1, source_target_pairs={{0,16},{2,18},{4,20},{6,22},{8,24},{10,26},{12,28},{14,30},{16,0},... | collective-permute-start | bytes 1179656 | tf_op jit(solution)/shard_map/ppermute | solution.py:120
  11.8 17.5 %collective-permute-start.1 = (bf16[256,768]{1,0:T(8,128)(2,1)S(1)}, bf16[256,768]{1,0:T(8,128)(2,1)S(1)}, u32[]{:S(2)}, u32[]{:S(2)}) collective-permute-start(bf16[256,768]{1,0:T(8,128)(2,1)S(1)} %get-tuple-element.88.refs_8_), channel_id=1, source_target_pairs={{0,8},{2,10},{4,12},{6,14},{8,0},{10,2},{12,4},{14,6},{16,24},{18,... | collective-permute-start | bytes 1179656 | tf_op jit(solution)/shard_map/ppermute | solution.py:120
  12.3 17.8 %collective-permute-start.2 = (bf16[256,768]{1,0:T(8,128)(2,1)}, bf16[256,768]{1,0:T(8,128)(2,1)S(1)}, u32[]{:S(2)}, u32[]{:S(2)}) collective-permute-start(bf16[256,768]{1,0:T(8,128)(2,1)} %get-tuple-element.134), channel_id=1, source_target_pairs={{0,2},{2,0},{4,6},{6,4},{8,10},{10,8},{12,14},{14,12},{16,18},{18,... | collective-permute-start | bytes 1179656 | tf_op jit(solution)/shard_map/ppermute | solution.py:120
  12.8 17.5 %collective-permute-start.3 = (bf16[256,768]{1,0:T(8,128)(2,1)}, bf16[256,768]{1,0:T(8,128)(2,1)S(1)}, u32[]{:S(2)}, u32[]{:S(2)}) collective-permute-start(bf16[256,768]{1,0:T(8,128)(2,1)} %get-tuple-element.136), channel_id=1, source_target_pairs={{0,4},{2,6},{4,0},{6,2},{8,12},{10,14},{12,8},{14,10},{16,20},{18,... | collective-permute-start | bytes 1179656 | tf_op jit(solution)/shard_map/ppermute | solution.py:120
  14.3 17.5 %collective-permute-start.4 = (bf16[256,768]{1,0:T(8,128)(2,1)}, bf16[256,768]{1,0:T(8,128)(2,1)S(1)}, u32[]{:S(2)}, u32[]{:S(2)}) collective-permute-start(bf16[256,768]{1,0:T(8,128)(2,1)} %get-tuple-element.133), channel_id=1, source_target_pairs={{0,6},{2,4},{4,2},{6,0},{8,14},{10,12},{12,10},{14,8},{16,22},{18,... | collective-permute-start | bytes 1179656 | tf_op jit(solution)/shard_map/ppermute | solution.py:120
  36.9 13.3 %collective-permute-start.9 = (f32[16,16,128]{2,1,0:T(8,128)S(1)}, f32[16,16,128]{2,1,0:T(8,128)S(1)}, u32[]{:S(2)}, u32[]{:S(2)}) collective-permute-start(f32[16,16,128]{2,1,0:T(8,128)S(1)} %add_select_fusion), channel_id=1, source_target_pairs={{0,8},{2,10},{4,12},{6,14},{8,16},{10,18},{12,20},{14,22},{16,24},... | collective-permute-start | bytes 393224 | tf_op jit(solution)/shard_map/ppermute | solution.py:115
  39.3 25.2 %collective-permute-start.6 = (bf16[256,768]{1,0:T(8,128)(2,1)S(1)}, bf16[256,768]{1,0:T(8,128)(2,1)}, u32[]{:S(2)}, u32[]{:S(2)}) collective-permute-start(bf16[256,768]{1,0:T(8,128)(2,1)S(1)} %collective-permute-done.2.refs_9_), channel_id=1, source_target_pairs={{0,16},{2,18},{4,20},{6,22},{8,24},{10,26},{12,28},{14,30},{16,0},... | collective-permute-start | bytes 1179656 | tf_op jit(solution)/shard_map/ppermute | solution.py:120
  39.4 25.1 %collective-permute-start.7 = (bf16[256,768]{1,0:T(8,128)(2,1)S(1)}, bf16[256,768]{1,0:T(8,128)(2,1)}, u32[]{:S(2)}, u32[]{:S(2)}) collective-permute-start(bf16[256,768]{1,0:T(8,128)(2,1)S(1)} %collective-permute-done.2.refs_9_), channel_id=1, source_target_pairs={{0,8},{2,10},{4,12},{6,14},{8,0},{10,2},{12,4},{14,6},{16,24},{18,... | collective-permute-start | bytes 1179656 | tf_op jit(solution)/shard_map/ppermute | solution.py:120
  50.9 12.5 %collective-permute-start.10 = (f32[16,16,128]{2,1,0:T(8,128)}, f32[16,16,128]{2,1,0:T(8,128)}, u32[]{:S(2)}, u32[]{:S(2)}) collective-permute-start(f32[16,16,128]{2,1,0:T(8,128)} %multiply_add_fusion.1), channel_id=1, source_target_pairs={{0,16},{2,18},{4,20},{6,22},{8,24},{10,26},{12,28},{14,30},{1,17},... | collective-permute-start | bytes 393224 | tf_op jit(solution)/shard_map/ppermute | solution.py:115
  64.5 11.6 %collective-permute-start.11 = (bf16[128,768]{1,0:T(8,128)(2,1)S(1)}, bf16[128,768]{1,0:T(8,128)(2,1)S(1)}, u32[]{:S(2)}, u32[]{:S(2)}) collective-permute-start(bf16[128,768]{1,0:T(8,128)(2,1)S(1)} %slice.68), channel_id=1, source_target_pairs={{0,16},{2,18},{4,20},{6,22},{8,24},{10,26},{12,28},{14,30},{16,0},... | collective-permute-start | bytes 589832 | tf_op jit(solution)/shard_map/ppermute | solution.py:120
  76.2 11.3 %collective-permute-start.15 = (bf16[256,1024]{1,0:T(8,128)(2,1)S(1)}, bf16[256,1024]{1,0:T(8,128)(2,1)S(1)}, u32[]{:S(2)}, u32[]{:S(2)}) collective-permute-start(bf16[256,1024]{1,0:T(8,128)(2,1)S(1)} %get-tuple-element.79), channel_id=1, source_target_pairs={{0,2},{2,0},{4,6},{6,4},{8,10},{10,8},{12,14},{14,12},{16,18},{18,... | collective-permute-start | bytes 1572872 | tf_op jit(solution)/shard_map/ppermute | solution.py:120
  76.3 11.3 %collective-permute-start.16 = (bf16[256,1024]{1,0:T(8,128)(2,1)S(1)}, bf16[256,1024]{1,0:T(8,128)(2,1)S(1)}, u32[]{:S(2)}, u32[]{:S(2)}) collective-permute-start(bf16[256,1024]{1,0:T(8,128)(2,1)S(1)} %get-tuple-element.84), channel_id=1, source_target_pairs={{0,4},{2,6},{4,0},{6,2},{8,12},{10,14},{12,8},{14,10},{16,20},{18,... | collective-permute-start | bytes 1572872 | tf_op jit(solution)/shard_map/ppermute | solution.py:120
  89.1 46.2 %collective-permute-start.22 = (bf16[2,256,1024]{2,1,0:T(8,128)(2,1)S(1)}, bf16[2,256,1024]{2,1,0:T(8,128)(2,1)S(1)}, u32[]{:S(2)}, u32[]{:S(2)}) collective-permute-start(bf16[2,256,1024]{2,1,0:T(8,128)(2,1)S(1)} %pad_maximum_fusion.1.refs_2_), channel_id=1, source_target_pairs={{0,2},{2,0},{4,6},{6,4},{8,10},{10,8},{12,14},{14,12},{16,18},{18,... | collective-permute-start | bytes 3145736 | tf_op jit(solution)/shard_map/ppermute | solution.py:120
  89.2 46.2 %collective-permute-start.24 = (bf16[2,256,1024]{2,1,0:T(8,128)(2,1)S(1)}, bf16[2,256,1024]{2,1,0:T(8,128)(2,1)S(1)}, u32[]{:S(2)}, u32[]{:S(2)}) collective-permute-start(bf16[2,256,1024]{2,1,0:T(8,128)(2,1)S(1)} %pad_maximum_fusion.1.refs_2_), channel_id=1, source_target_pairs={{0,1},{1,0},{2,3},{3,2},{4,5},{5,4},{6,7},{7,6},{8,9},{9,8},{10,11... | collective-permute-start | bytes 3145736 | tf_op jit(solution)/shard_map/ppermute | solution.py:120
  89.3 21.4 %collective-permute-start.18 = (bf16[256,768]{1,0:T(8,128)(2,1)S(1)}, bf16[256,768]{1,0:T(8,128)(2,1)S(1)}, u32[]{:S(2)}, u32[]{:S(2)}) collective-permute-start(bf16[256,768]{1,0:T(8,128)(2,1)S(1)} %copy-done.13), channel_id=1, source_target_pairs={{0,8},{2,10},{4,12},{6,14},{8,0},{10,2},{12,4},{14,6},{16,24},{18,... | collective-permute-start | bytes 1179656 | tf_op jit(solution)/shard_map/ppermute | solution.py:120
  94.6 40.8 %collective-permute-start.21 = (bf16[2,256,1024]{2,1,0:T(8,128)(2,1)S(1)}, bf16[2,256,1024]{2,1,0:T(8,128)(2,1)}, u32[]{:S(2)}, u32[]{:S(2)}) collective-permute-start(bf16[2,256,1024]{2,1,0:T(8,128)(2,1)S(1)} %pad_maximum_fusion.refs_0_), channel_id=1, source_target_pairs={{0,4},{2,6},{4,0},{6,2},{8,12},{10,14},{12,8},{14,10},{16,20},{18,... | collective-permute-start | bytes 3145736 | tf_op jit(solution)/shard_map/ppermute | solution.py:120
  97.8 37.6 %collective-permute-start.23 = (bf16[2,256,1024]{2,1,0:T(8,128)(2,1)S(1)}, bf16[2,256,1024]{2,1,0:T(8,128)(2,1)S(1)}, u32[]{:S(2)}, u32[]{:S(2)}) collective-permute-start(bf16[2,256,1024]{2,1,0:T(8,128)(2,1)S(1)} %pad_maximum_fusion.refs_0_), channel_id=1, source_target_pairs={{0,1},{1,0},{2,3},{3,2},{4,5},{5,4},{6,7},{7,6},{8,9},{9,8},{10,11... | collective-permute-start | bytes 3145736 | tf_op jit(solution)/shard_map/ppermute | solution.py:120
  110.7 12.8 %collective-permute-start.19 = (bf16[256,768]{1,0:T(8,128)(2,1)S(1)}, bf16[256,768]{1,0:T(8,128)(2,1)S(1)}, u32[]{:S(2)}, u32[]{:S(2)}) collective-permute-start(bf16[256,768]{1,0:T(8,128)(2,1)S(1)} %copy-done.28), channel_id=1, source_target_pairs={{8,0},{10,2},{12,4},{14,6},{16,24},{18,26},{20,28},{22,30},{9,1},{... | collective-permute-start | bytes 1179656 | tf_op jit(solution)/shard_map/ppermute | solution.py:297
  123.5 11.9 %collective-permute-start.20 = (bf16[256,768]{1,0:T(8,128)(2,1)S(1)}, bf16[256,768]{1,0:T(8,128)(2,1)S(1)}, u32[]{:S(2)}, u32[]{:S(2)}) collective-permute-start(bf16[256,768]{1,0:T(8,128)(2,1)S(1)} %copy-done.18), channel_id=1, source_target_pairs={{8,16},{10,18},{12,20},{14,22},{16,8},{18,10},{20,12},{22,14},{9,1... | collective-permute-start | bytes 1179656 | tf_op jit(solution)/shard_map/ppermute | solution.py:294
  139.1 30.3 %collective-permute-start.28 = (bf16[768,512]{1,0:T(8,128)(2,1)}, bf16[768,512]{1,0:T(8,128)(2,1)}, u32[]{:S(2)}, u32[]{:S(2)}) collective-permute-start(bf16[768,512]{1,0:T(8,128)(2,1)} %slice.91), channel_id=1, source_target_pairs={{8,16},{10,18},{12,20},{14,22},{16,8},{18,10},{20,12},{22,14},{9,1... | collective-permute-start | bytes 2359304 | tf_op jit(solution)/shard_map/ppermute | solution.py:294
  142.7 26.8 %collective-permute-start.27 = (bf16[768,512]{1,0:T(8,128)(2,1)}, bf16[768,512]{1,0:T(8,128)(2,1)}, u32[]{:S(2)}, u32[]{:S(2)}) collective-permute-start(bf16[768,512]{1,0:T(8,128)(2,1)} %slice.90), channel_id=1, source_target_pairs={{8,0},{10,2},{12,4},{14,6},{16,24},{18,26},{20,28},{22,30},{9,1},{... | collective-permute-start | bytes 2359304 | tf_op jit(solution)/shard_map/ppermute | solution.py:297
  170.5 14.2 %collective-permute-start.33 = (bf16[768,256]{1,0:T(8,128)(2,1)S(1)}, bf16[768,256]{1,0:T(8,128)(2,1)S(1)}, u32[]{:S(2)}, u32[]{:S(2)}) collective-permute-start(bf16[768,256]{1,0:T(8,128)(2,1)S(1)} %slice.84), channel_id=1, source_target_pairs={{8,16},{10,18},{12,20},{14,22},{16,8},{18,10},{20,12},{22,14},{9,1... | collective-permute-start | bytes 1179656 | tf_op jit(solution)/shard_map/ppermute | solution.py:294
  183.2 16.9 %collective-permute-start.30 = (bf16[256,512]{1,0:T(8,128)(2,1)S(1)}, bf16[256,512]{1,0:T(8,128)(2,1)S(1)}, u32[]{:S(2)}, u32[]{:S(2)}) collective-permute-start(bf16[256,512]{1,0:T(8,128)(2,1)S(1)} %get-tuple-element.121), channel_id=1, source_target_pairs={{0,4},{2,6},{4,0},{6,2},{8,12},{10,14},{12,8},{14,10},{16,20},{18,... | collective-permute-start | bytes 786440 | tf_op jit(solution)/shard_map/ppermute | solution.py:120
  183.2 16.9 %collective-permute-start.31 = (bf16[256,512]{1,0:T(8,128)(2,1)S(1)}, bf16[256,512]{1,0:T(8,128)(2,1)S(1)}, u32[]{:S(2)}, u32[]{:S(2)}) collective-permute-start(bf16[256,512]{1,0:T(8,128)(2,1)S(1)} %get-tuple-element.122), channel_id=1, source_target_pairs={{0,6},{2,4},{4,2},{6,0},{8,14},{10,12},{12,10},{14,8},{16,22},{18,... | collective-permute-start | bytes 786440 | tf_op jit(solution)/shard_map/ppermute | solution.py:120
  (66 other events, 698.9 us)

commit v4 on v1

--- a/solution.py
+++ b/solution.py
@@ -7,6 +7,7 @@
 
 LANES = 128
 RADIX = 4
+PLANE = 4
 
 
 def spread_signal(k_ref, v_ref, sig_ref):
@@ -98,8 +99,8 @@
         conv_kernel,
         grid=(chan // width,),
         in_specs=[wide, wide, wide, moded, moded, single, moded],
-        out_specs=wide,
-        out_shape=jax.ShapeDtypeStruct((rows, chan), jnp.bfloat16),
+        out_specs=pl.BlockSpec((None, rows, width), lambda i: (i, 0, 0)),
+        out_shape=jax.ShapeDtypeStruct((chan // width, rows, width), jnp.bfloat16),
         scratch_shapes=[spread, spread],
         compiler_params=pltpu.CompilerParams(vmem_limit_bytes=32 << 20),
         cost_estimate=pl.CostEstimate(
@@ -109,37 +110,317 @@
     )(q, k, v, rate, residue, skip, enter)
 
 
-def shift_ctx(x, by, count):
+def shift_ctx(x, by):
+    count = lax.axis_size("ctx")
     return lax.ppermute(x, "ctx", [(i, i + by) for i in range(count - by)])
+
+
+def exchange(x, axis, flip):
+    count = lax.axis_size(axis)
+    return lax.ppermute(x, axis, [(i, i ^ flip) for i in range(count)])
+
+
+def tie(*values):
+    return lax.optimization_barrier(values)
 
 
 def entering_states(ends, rate, rows):
     count = lax.axis_size("ctx")
     total = jnp.zeros_like(ends)
     for k in range(1, min(RADIX, count - 1) + 1):
-        total = total + jnp.exp(-rate * float(rows * (k - 1))) * shift_ctx(ends, k, count)
+        total = total + jnp.exp(-rate * float(rows * (k - 1))) * shift_ctx(ends, k)
     stride = RADIX
     while stride < count:
         base = total
         for k in range(1, RADIX):
             if stride * k < count:
-                total = total + jnp.exp(-rate * float(rows * stride * k)) * shift_ctx(base, stride * k, count)
+                total = total + jnp.exp(-rate * float(rows * stride * k)) * shift_ctx(base, stride * k)
         stride *= RADIX
     return total
+
+
+def box(fn, *args):
+    once = (lax.axis_index("ctx") >= 0).astype(jnp.int32)
+    shapes = jax.eval_shape(fn, *args)
+    empty = jax.tree.map(lambda a: jnp.zeros(a.shape, a.dtype), shapes)
+
+    def run(step, _):
+        return fn(*tie(step, *args)[1:])
+
+    return lax.fori_loop(0, once, run, empty)
+
+
+def fold_pair(ends, rate, flip, span):
+    other = exchange(ends, "ctx", flip)
+    later = (lax.axis_index("ctx") & flip) != 0
+    decay = jnp.exp(-rate * float(span))
+    both = jnp.where(later, decay * other + ends, decay * ends + other)
+    return both, other, later
+
+
+def in_order(gated_ref, index, place_ref, chunk):
+    found = []
+    for r in range(PLANE):
+        start = pl.multiple_of(place_ref[r] * chunk, chunk)
+        found.append(gated_ref[index, :, pl.ds(start, chunk)])
+    return jnp.concatenate(found, axis=1)
+
+
+def project(flags, places, sources, blocks, widths):
+    rows, depth = sources[0][0][0].shape[1:]
+    chunk = depth // PLANE
+    arrays = []
+    for source in sources:
+        for array, _ in source:
+            if not any(array is known for known in arrays):
+                arrays.append(array)
+    where = [[([a is known for known in arrays].index(True), at) for a, at in source] for source in sources]
+    count = len(arrays)
+
+    def kernel(flag_ref, place_ref, *refs):
+        gated_refs, refs = refs[:count], refs[count:]
+        weight_refs, out_refs = refs[: len(weights)], refs[len(weights) :]
+        pieces = len(weights) // len(blocks)
+        for b in range(len(blocks)):
+            piece_refs = weight_refs[pieces * b : pieces * (b + 1)]
+            for n, source in enumerate(where):
+
+                @pl.when(flag_ref[b] == n)
+                def _():
+                    for r, (at, index) in enumerate(source):
+                        lhs = in_order(gated_refs[at], index, place_ref, chunk)
+                        first = 0
+                        for part, width in enumerate(widths):
+                            cols = pl.ds(first, width)
+                            out_ref = out_refs[part * PLANE + r]
+                            total = out_ref[...] if b else jnp.zeros(out_ref.shape, jnp.float32)
+                            at_row = 0
+                            for piece_ref in piece_refs:
+                                depth_here = piece_ref.shape[0]
+                                total += jnp.dot(
+                                    lhs[:, at_row : at_row + depth_here],
+                                    piece_ref[:, cols],
+                                    preferred_element_type=jnp.float32,
+                                )
+                                at_row += depth_here
+                            out_ref[...] = total
+                            first += width
+
+    smem = pl.BlockSpec(memory_space=pltpu.SMEM)
+    vmem = pl.BlockSpec(memory_space=pltpu.VMEM)
+    weights = [piece for block in blocks for piece in block]
+    cols = sum(widths)
+    made = pl.pallas_call(
+        kernel,
+        in_specs=[smem, smem] + [vmem] * (count + len(weights)),
+        out_specs=[vmem] * (PLANE * len(widths)),
+        out_shape=[jax.ShapeDtypeStruct((rows, width), jnp.float32) for width in widths for _ in range(PLANE)],
+        compiler_params=pltpu.CompilerParams(vmem_limit_bytes=16 << 20),
+        cost_estimate=pl.CostEstimate(
+            flops=2 * PLANE * rows * depth * len(blocks) * cols,
+            bytes_accessed=2 * len(blocks) * depth * (PLANE * rows + cols),
+            transcendentals=0,
+        ),
+        name="project",
+    )(flags, places, *arrays, *weights)
+    return [made[part * PLANE : (part + 1) * PLANE] for part in range(len(widths))]
+
+
+def finish(flags, places, sources, heads, rests, accs, first_col):
+    rows, depth = sources[0][0][0].shape[1:]
+    chunk = depth // PLANE
+    width = accs[0].shape[1]
+    arrays = []
+    for source in sources:
+        for array, _ in source:
+            if not any(array is known for known in arrays):
+                arrays.append(array)
+    where = [[([a is known for known in arrays].index(True), at) for a, at in source] for source in sources]
+    count = len(arrays)
+
+    def kernel(flag_ref, place_ref, *refs):
+        gated_refs, refs = refs[:count], refs[count:]
+        head_a, head_b, rest_a, rest_b = refs[:4]
+        acc_refs, out_refs, weight_ref = refs[4 : 4 + PLANE], refs[4 + PLANE : 4 + 2 * PLANE], refs[-1]
+        cols = pl.ds(first_col, width)
+        weight_ref[pl.ds(0, chunk), :] = head_a[:, cols] + head_b[:, cols]
+        weight_ref[pl.ds(chunk, depth - chunk), :] = rest_a[...] + rest_b[...]
+        for n, source in enumerate(where):
+
+            @pl.when(flag_ref[3] == n)
+            def _():
+                for r, (at, index) in enumerate(source):
+                    lhs = in_order(gated_refs[at], index, place_ref, chunk)
+                    total = acc_refs[r][...] + jnp.dot(lhs, weight_ref[...], preferred_element_type=jnp.float32)
+                    out_refs[r][...] = total.astype(jnp.bfloat16)
+
+    smem = pl.BlockSpec(memory_space=pltpu.SMEM)
+    vmem = pl.BlockSpec(memory_space=pltpu.VMEM)
+    return pl.pallas_call(
+        kernel,
+        in_specs=[smem, smem] + [vmem] * (count + 4 + PLANE),
+        out_specs=[vmem] * PLANE,
+        out_shape=[jax.ShapeDtypeStruct((rows, width), jnp.bfloat16)] * PLANE,
+        scratch_shapes=[pltpu.VMEM((depth, width), jnp.bfloat16)],
+        compiler_params=pltpu.CompilerParams(vmem_limit_bytes=16 << 20),
+        cost_estimate=pl.CostEstimate(
+            flops=2 * PLANE * rows * depth * width, bytes_accessed=2 * depth * (PLANE * rows + width), transcendentals=0
+        ),
+        name="finish",
+    )(flags, places, *arrays, *heads, *rests, *accs)
+
+
+def assemble(spot, parts):
+    rows = parts[0][0].shape[0]
+    widths = [part[0].shape[1] for part in parts]
+    cols = sum(widths)
+
+    def kernel(spot_ref, *refs):
+        out_ref = refs[-1]
+        group = pl.program_id(0)
+        for r in range(PLANE):
+
+            @pl.when((spot_ref[0] ^ r) == group)
+            def _():
+                first = 0
+                for part, width in enumerate(widths):
+                    out_ref[:, pl.ds(first, width)] = refs[part * PLANE + r][...]
+                    first += width
+
+    flat = [piece for part in parts for piece in part]
+    return pl.pallas_call(
+        kernel,
+        grid=(PLANE,),
+        in_specs=[pl.BlockSpec(memory_space=pltpu.SMEM)] + [pl.BlockSpec(p.shape, lambda i: (0, 0)) for p in flat],
+        out_specs=pl.BlockSpec((rows, cols), lambda i: (0, i)),
+        out_shape=jax.ShapeDtypeStruct((rows, cols * PLANE), flat[0].dtype),
+        name="assemble",
+    )(spot.reshape(1), *flat)
+
+
+def split_block(q, k, v, residue, rate, skip, w_out):
+    rows, chan = q.shape
+    me = lax.axis_index("ctx")
+    core = lax.axis_index("ch")
+    spot, plane = me & (PLANE - 1), me // PLANE
+    count = lax.axis_size("ctx")
+    chunk, feats = w_out.shape
+    cols = feats // PLANE
+    wide = 2 * cols // 3
+    widths = [wide, cols - wide]
+
+    def far(x):
+        return exchange(x, "ctx", 2 * PLANE)
+
+    def near(x):
+        return exchange(x, "ctx", PLANE)
+
+    middle = [i for i in range(count) if PLANE <= i < 3 * PLANE]
+
+    def across(x):
+        return lax.ppermute(x, "ctx", [(i, i ^ (3 * PLANE)) for i in middle])
+
+    def outward(x):
+        return lax.ppermute(x, "ctx", [(i, i ^ PLANE) for i in middle])
+
+    def plane_scan(k, v, rate):
+        ends = end_states(k, v, rate)
+        both, other, later = fold_pair(ends, rate, 1, rows)
+        before = jnp.where(later, other, 0.0)
+        both, other, later = fold_pair(both, rate, 2, 2 * rows)
+        odd = (me & 1).astype(jnp.float32)
+        return both, before + jnp.where(later, jnp.exp(-rate * (odd * rows)) * other, 0.0)
+
+    own = [lax.dynamic_slice_in_dim(w_out, (spot ^ r) * cols, cols, axis=1) for r in range(PLANE)]
+    w0, w1, w2, w3 = tie(*own)
+    f0, n0 = far(w0), near(w0)
+    w1, w2 = exchange(w1, "ctx", 1), exchange(w2, "ctx", 2)
+    both, before = box(plane_scan, k, v, rate)
+    f0, n0, w0, w1, w2, w3, both, before = tie(f0, n0, w0, w1, w2, w3, both, before)
+
+    w3 = exchange(w3, "ctx", 3)
+    out0, mid0 = outward(f0), across(w0)
+    last = shift_ctx(both, PLANE)
+    decay = jnp.exp(-rate * float(PLANE * rows))
+    carried = last + decay * shift_ctx(both + decay * last, 2 * PLANE)
+    enter = before + jnp.exp(-rate * (spot * rows).astype(jnp.float32)) * carried
+    out0, mid0, w1, w2, w3, enter = tie(out0, mid0, w1, w2, w3, enter)
+
+    def convolve(q, k, v, enter):
+        one, two = gated_conv(q, k, v, rate, residue, skip, enter)
+        one_x, two_y = exchange(one, "ctx", 1), exchange(two, "ctx", 2)
+        return jnp.stack([one, one_x]), jnp.stack([two, two_y]), jnp.stack([one, one_x, two, two_y])
+
+    f1, n1 = far(w1), near(w1)
+    one_pair, two_pair, pairs = box(convolve, q, k, v, enter)
+    early = 3 * chunk // 2
+    w23 = jnp.concatenate([w2, w3])
+    w23, w4 = w23[:early], w23[early:]
+    f1, n1, w1, w23, w4, one_pair, two_pair, pairs = tie(f1, n1, w1, w23, w4, one_pair, two_pair, pairs)
+
+    f23, n23 = far(w23), near(w23)
+    one_far, two_far = exchange(one_pair, "ctx", 2), exchange(two_pair, "ctx", 1)
+    pairs_t = exchange(pairs, "ch", 1)
+    f23, n23, w4, one_far, two_far, pairs_t = tie(f23, n23, w4, one_far, two_far, pairs_t)
+
+    f4, n4 = far(w4), near(w4)
+    one_far_t, two_far_t = exchange(one_far, "ch", 1), exchange(two_far, "ch", 1)
+    f4, n4, one_far_t, two_far_t = tie(f4, n4, one_far_t, two_far_t)
+
+    def row_blocks(nearest, far_one, far_two):
+        return [
+            [(nearest, 0), (nearest, 1), (far_one, 0), (far_one, 1)],
+            [(nearest, 2), (far_two, 0), (nearest, 3), (far_two, 1)],
+        ]
+
+    def source_of(b):
+        return jnp.where(b // 2 == core, b & 1, 2 + (b & 1))
+
+    flags = jnp.stack([source_of(plane ^ r) for r in range(4)]).astype(jnp.int32)
+    places = jnp.stack([spot ^ r for r in range(PLANE)]).astype(jnp.int32)
+
+    def side(part, *blocks):
+        span = slice(wide, None) if part else slice(0, wide)
+        return jnp.concatenate([block[:, span] for block in blocks])
+
+    outA, midA = outward(side(0, f1, f23, f4)), across(side(0, w1, w23, w4))
+    sources = row_blocks(pairs, one_far, two_far) + row_blocks(pairs_t, one_far_t, two_far_t)
+    accA, accB = project(flags, places, sources, [(w0, w1, w23, w4), (n0, n1, n23, n4), (f0, f1, f23, f4)], widths)
+    outA, midA, f1, f23, f4, w1, w23, w4, *accs = tie(outA, midA, f1, f23, f4, w1, w23, w4, *accA, *accB)
+    accA, accB = accs[:PLANE], accs[PLANE:]
+
+    outB, midB = outward(side(1, f1, f23, f4)), across(side(1, w1, w23, w4))
+    madeA = finish(flags, places, sources, (out0, mid0), (outA, midA), accA, 0)
+    backA = [madeA[0]] + [exchange(madeA[r], "ctx", r) for r in range(1, PLANE)]
+    madeB = finish(flags, places, sources, (out0, mid0), (outB, midB), accB, wide)
+    backB = [madeB[0]] + [exchange(madeB[r], "ctx", r) for r in range(1, PLANE)]
+    return assemble(spot.astype(jnp.int32), [backA, backB])
 
 
 def body(q, k, v, residue, rate, skip, w_out):
     rows, chan = q.shape
     modes = rate.shape[0]
     groups = chan // LANES
-    w_full = lax.all_gather(w_out, "ctx", axis=0, tiled=True)
+    count, cores = lax.axis_size("ctx"), lax.axis_size("ch")
+    chunk, feats = w_out.shape
+    split = (
+        count == 4 * PLANE
+        and cores == 2
+        and chan == 8 * chunk
+        and chunk % LANES == 0
+        and feats % (PLANE * LANES) == 0
+    )
     rate = rate.reshape(modes, groups, LANES)
     residue = residue.reshape(modes, groups, LANES)
     skip = skip.reshape(groups, LANES)
+    if split:
+        return split_block(q, k, v, residue, rate, skip, w_out)
     ends = end_states(k, v, rate)
     enter = entering_states(ends, rate, rows)
     gated = gated_conv(q, k, v, rate, residue, skip, enter)
+    gated = gated.transpose(1, 0, 2).reshape(rows, chan)
     full_gated = lax.all_gather(gated, "ch", axis=1, tiled=True)
+    w_full = lax.all_gather(w_out, "ctx", axis=0, tiled=True)
     mixed = jnp.dot(full_gated, w_full, preferred_element_type=jnp.float32)
     return mixed.astype(jnp.bfloat16)
 

time: 361 us -> 199 us (0.55)
  waiting for transfers between devices: 297 us -> 69 us
  starting transfers between devices: 19 us -> 52.2 us
  local copies, waits for them, and re-layouts: 3.45 us -> 34.8 us
  Pallas kernels: 10.8 us -> 28.1 us
  other arithmetic: 0.17 us -> 13.4 us
  between operations: 13.5 us -> 0.49 us
  matrix products: 13 us -> 0 us
    all_gather x2 -> x0, waiting for transfers between devices: 283 us -> none  [the longest x1 273 us: body(): w_full = lax.all_gather(w_out, 'ctx', axis=0, tiled=True)]
    ppermute x0 -> x32, waiting for transfers between devices: none -> 55.6 us  [the longest x26 53.7 us: exchange(): return lax.ppermute(x, axis, [(i, i ^ flip) for i in range(count)])]
    ppermute x0 -> x32, starting transfers between devices: none -> 48.5 us  [the longest x26 31.2 us: exchange(): return lax.ppermute(x, axis, [(i, i ^ flip) for i in range(count)])]
    unnamed x12 -> x88, local copies, waits for them, and re-layouts: 3.45 us -> 23.4 us
    pallas_call x0 -> x4, Pallas kernels: none -> 16 us  [the longest x1 8.79 us: project(): pl.pallas_call(kernel, in_specs=[smem, smem] + [vmem] * (count + len(weig...]
    ppermute x7 -> x2, starting transfers between devices: 19 us -> 3.66 us  [shift_ctx(): return lax.ppermute(x, 'ctx', [(i, i + by) for i in range(count - by)])]
    dot_general x1 -> x0, matrix products: 13 us -> none  [body(): mixed = jnp.dot(full_gated, w_full, preferred_element_type=jnp.float32)]
    another operation x0 -> x4, other arithmetic: none -> 7.04 us  [the longest x1 2.76 us: convolve(): jnp.stack([one, one_x, two, two_y])]
  transfers between devices with their start and end apart: 9 -> 34, of which waited for: 6 -> 14; matrix products, arithmetic and copies ran while one was open for 0% -> 12% of each run, Pallas kernels for 0% -> 13%
where the time goes in v4:
time: 199 us; the launch traced here: 198 us
  waiting for transfers between devices  69 us (35%)
  starting transfers between devices  52.2 us (26%)
  local copies, waits for them, and re-layouts  34.8 us (17%)
  Pallas kernels  28.1 us (14%)
  other arithmetic  13.4 us (7%)
    ppermute x26, waiting for transfers between devices, exchange(): return lax.ppermute(x, axis, [(i, i ^ flip) for i in range(count)])  53.7 us
    ppermute x26, starting transfers between devices, exchange(): return lax.ppermute(x, axis, [(i, i ^ flip) for i in range(count)])  31.2 us
    unnamed x88, local copies, waits for them, and re-layouts  23.4 us
    ppermute x2, waiting for transfers between devices, shift_ctx(): return lax.ppermute(x, 'ctx', [(i, i + by) for i in range(count - by)])  13.4 us
    ppermute x3, starting transfers between devices, outward(): return lax.ppermute(x, 'ctx', [(i, i ^ PLANE) for i in middle])  9.39 us
    pallas_call x1, Pallas kernels, project(): pl.pallas_call(kernel, in_specs=[smem, smem] + [vmem] * (count + len(weig...  8.79 us
    ppermute x3, starting transfers between devices, across(): return lax.ppermute(x, 'ctx', [(i, i ^ 3 * PLANE) for i in middle])  7.93 us
    pallas_call x1, Pallas kernels, gated_conv(): pl.pallas_call(conv_kernel, grid=(chan // width,), in_specs=[wide, wide,...  7.85 us
  transfers between devices with their start and end apart: 34, of which 14 were waited for; matrix products, arithmetic and copies ran while one was open for 12% of the time, Pallas kernels for 13%

profile of v4, /device:TPU:8, one launch (start us, length us, event | category | flops | bytes accessed | tf_op | source)
XLA Modules:
  0.0 197.9 jit_solution(6765697529838457453)
XLA Ops:
  2.2 2.6 %collective-permute-start.4 = (bf16[256,768]{1,0:T(8,128)(2,1)S(1)}, bf16[256,768]{1,0:T(8,128)(2,1)S(1)}, u32[]{:S(2)}, u32[]{:S(2)}) collective-permute-start(bf16[256,768]{1,0:T(8,128)(2,1)S(1)} %get-tuple-element.243.refs_6_), channel_id=1, source_target_pairs={{0,16},{2,18},{4,20},{6,22},{8,24},{10,26},{12,28},{14,30},{16,0},... | collective-permute-start | bytes 1179656 | tf_op jit(solution)/shard_map/ppermute | solution.py:120
  9.7 15.2 %while.28 = (s32[]{:T(128)}, f32[16,16,128]{2,1,0:T(8,128)}, f32[16,16,128]{2,1,0:T(8,128)}, s32[]{:T(128)}, bf16[256,2048]{1,0:T(8,128)(2,1)}, /*index=5*/bf16[...) while((s32[]{:T(128)}, f32[16,16,128]{2,1,0:T(8,128)}, ...), condition=%wide.region_1.2_spmd, body=%wide.region_0.1_spmd.sunk | while | flops 17399808 | bytes 4456734 | solution.py:150
  9.7 4.3 %end_states.3 = f32[16,16,128]{2,1,0:T(8,128)S(1)} custom-call(bf16[256,2048]{1,0:T(8,128)(2,1)} %get-tuple-element.479.k_ref, bf16[256,2048]{1,0:T(8,128)(2,1)} %get-tuple-element.480.v_ref, f32[16,16,128]{2,1,0:T(8,128)S(1)} %get-tuple-element.481.rate_ref), custom_call_target="tpu_custom_call" | custom-call | flops 16777216 | bytes 2097152 | tf_op jit(solution)/shard_map/while/body/end_states/pallas_call | solution.py:77
  14.6 4.4 %collective-permute-done = f32[16,16,128]{2,1,0:T(8,128)S(1)} collective-permute-done((f32[16,16,128]{2,1,0:T(8,128)S(1)}, f32[16,16,128]{2,1,0:T(8,128)S(1)}, u32[]{:S(2)}, u32[]{:S(2)}) %collective-permute-start) | collective-permute-done | bytes 131104 | tf_op jit(solution)/shard_map/while/body/ppermute | solution.py:120
  20.0 4.1 %collective-permute-done.1 = f32[16,16,128]{2,1,0:T(8,128)S(1)} collective-permute-done((f32[16,16,128]{2,1,0:T(8,128)S(1)}, f32[16,16,128]{2,1,0:T(8,128)S(1)}, u32[]{:S(2)}, u32[]{:S(2)}) %collective-permute-start.1) | collective-permute-done | bytes 131104 | tf_op jit(solution)/shard_map/while/body/ppermute | solution.py:120
  25.7 2.4 %collective-permute-start.11 = (f32[16,16,128]{2,1,0:T(8,128)}, f32[16,16,128]{2,1,0:T(8,128)S(1)}, u32[]{:S(2)}, u32[]{:S(2)}) collective-permute-start(f32[16,16,128]{2,1,0:T(8,128)} %get-tuple-element.248), channel_id=1, source_target_pairs={{0,8},{2,10},{4,12},{6,14},{8,16},{10,18},{12,20},{14,22},{16,24},... | collective-permute-start | bytes 393224 | tf_op jit(solution)/shard_map/ppermute | solution.py:115
  30.0 3.5 %collective-permute-start.8 = (bf16[256,768]{1,0:T(8,128)(2,1)S(1)}, bf16[256,768]{1,0:T(8,128)(2,1)S(1)}, u32[]{:S(2)}, u32[]{:S(2)}) collective-permute-start(bf16[256,768]{1,0:T(8,128)(2,1)S(1)} %collective-permute-done.4.refs_14_), channel_id=1, source_target_pairs={{8,0},{10,2},{12,4},{14,6},{16,24},{18,26},{20,28},{22,30},{9,1},{... | collective-permute-start | bytes 1179656 | tf_op jit(solution)/shard_map/ppermute | solution.py:324
  38.3 13.4 %collective-permute-done.12 = f32[16,16,128]{2,1,0:T(8,128)S(1)} collective-permute-done((f32[16,16,128]{2,1,0:T(8,128)S(1)}, f32[16,16,128]{2,1,0:T(8,128)S(1)}, u32[]{:S(2)}, u32[]{:S(2)}) %collective-permute-start.12) | collective-permute-done | bytes 131104 | tf_op jit(solution)/shard_map/ppermute | solution.py:115
  53.4 3.4 %collective-permute-start.13 = (bf16[256,768]{1,0:T(8,128)(2,1)S(1)}, bf16[256,768]{1,0:T(8,128)(2,1)S(1)}, u32[]{:S(2)}, u32[]{:S(2)}) collective-permute-start(bf16[256,768]{1,0:T(8,128)(2,1)S(1)} %collective-permute-done.6.refs_7_), channel_id=1, source_target_pairs={{0,16},{2,18},{4,20},{6,22},{8,24},{10,26},{12,28},{14,30},{16,0},... | collective-permute-start | bytes 1179656 | tf_op jit(solution)/shard_map/ppermute | solution.py:120
  62.2 26.7 %while.29 = (s32[]{:T(128)}, bf16[2,256,1024]{2,1,0:T(8,128)(2,1)}, bf16[2,256,1024]{2,1,0:T(8,128)(2,1)}, bf16[4,256,1024]{2,1,0:T(8,128)(2,1)}, s32[]{:T(128)}...) while((s32[]{:T(128)}, bf16[2,256,1024]{2,1,0:T(8,128)(2,1)}, ...), condition=%wide.region_3.4_spmd, body=%wide.region_2.3_spmd.sunk | while | flops 37748736 | bytes 19923148 | solution.py:150
  62.2 7.8 %gated_conv.1 = bf16[2,256,1024]{2,1,0:T(8,128)(2,1)S(1)} custom-call(bf16[256,2048]{1,0:T(8,128)(2,1)} %get-tuple-element.493.q_ref, bf16[256,2048]{1,0:T(8,128)(2,1)} %get-tuple-element.494.k_ref, bf16[256,2048]{1,0:T(8,128)(2,1)} %get-tuple-element.495.v_ref, f32[16,16,128]{2,1,0:T(8,128)S(1)} %get-tuple-element.575.rate_ref, ...), custom_call_target="tpu_custom_call" | custom-call | flops 33554432 | bytes 4194304 | tf_op jit(solution)/shard_map/while/body/gated_conv/pallas_call | solution.py:98
  71.3 2.8 %collective-permute-start.3 = (bf16[256,1024]{1,0:T(8,128)(2,1)}, bf16[256,1024]{1,0:T(8,128)(2,1)}, u32[]{:S(2)}, u32[]{:S(2)}) collective-permute-start(bf16[256,1024]{1,0:T(8,128)(2,1)} %get-tuple-element.499), channel_id=1, source_target_pairs={{0,4},{2,6},{4,0},{6,2},{8,12},{10,14},{12,8},{14,10},{16,20},{18,... | collective-permute-start | bytes 1572872 | tf_op jit(solution)/shard_map/while/body/ppermute | solution.py:120
  75.0 6.9 %collective-permute-done.3 = bf16[256,1024]{1,0:T(8,128)(2,1)} collective-permute-done((bf16[256,1024]{1,0:T(8,128)(2,1)}, bf16[256,1024]{1,0:T(8,128)(2,1)}, u32[]{:S(2)}, u32[]{:S(2)}) %collective-permute-start.3) | collective-permute-done | bytes 524320 | tf_op jit(solution)/shard_map/while/body/ppermute | solution.py:120
  84.0 2.8 %pad_maximum_fusion.13 = bf16[4,256,1024]{2,1,0:T(8,128)(2,1)} fusion(bf16[1,256,1024]{2,1,0:T(8,128)(2,1)} %bitcast.24, bf16[1,256,1024]{2,1,0:T(8,128)(2,1)S(1)} %get-tuple-element.500, bf16[1,256,1024]{2,1,0:T(8,128)(2,1)} %bitcast.23, bf16[1,256,1024]{2,1,0:T(8,128)(2,1)S(1)} %get-tuple-element.498), kind=kLoop, calls=%fused_computation.3.clone.1 | loop fusion | flops 3145728 | bytes 4194304 | tf_op jit(solution)/shard_map/while/body/stack | solution.py:352
  94.5 23.9 %collective-permute-done.15.refs_16_ = bf16[384,768]{1,0:T(8,128)(2,1)S(1)} collective-permute-done((bf16[384,768]{1,0:T(8,128)(2,1)}, bf16[384,768]{1,0:T(8,128)(2,1)S(1)}, u32[]{:S(2)}, u32[]{:S(2)}) %collective-permute-start.15) | collective-permute-done | bytes 589856 | tf_op jit(solution)/shard_map/ppermute | solution.py:120
  118.4 2.4 %collective-permute-done.16.refs_12_ = bf16[384,768]{1,0:T(8,128)(2,1)S(1)} collective-permute-done((bf16[384,768]{1,0:T(8,128)(2,1)}, bf16[384,768]{1,0:T(8,128)(2,1)S(1)}, u32[]{:S(2)}, u32[]{:S(2)}) %collective-permute-start.16) | collective-permute-done | bytes 589856 | tf_op jit(solution)/shard_map/ppermute | solution.py:120
  127.8 2.8 %collective-permute-start.25 = (bf16[768,512]{1,0:T(8,128)(2,1)}, bf16[768,512]{1,0:T(8,128)(2,1)}, u32[]{:S(2)}, u32[]{:S(2)}) collective-permute-start(bf16[768,512]{1,0:T(8,128)(2,1)} %pad_maximum_fusion.4), channel_id=1, source_target_pairs={{8,16},{10,18},{12,20},{14,22},{16,8},{18,10},{20,12},{22,14},{9,1... | collective-permute-start | bytes 2359304 | tf_op jit(solution)/shard_map/ppermute | solution.py:321
  130.6 2.5 %collective-permute-done.20.refs_17_ = bf16[128,768]{1,0:T(8,128)(2,1)S(1)} collective-permute-done((bf16[128,768]{1,0:T(8,128)(2,1)}, bf16[128,768]{1,0:T(8,128)(2,1)S(1)}, u32[]{:S(2)}, u32[]{:S(2)}) %collective-permute-start.20) | collective-permute-done | bytes 196640 | tf_op jit(solution)/shard_map/ppermute | solution.py:120
  138.5 4.6 %collective-permute-start.24 = (bf16[768,512]{1,0:T(8,128)(2,1)}, bf16[768,512]{1,0:T(8,128)(2,1)}, u32[]{:S(2)}, u32[]{:S(2)}) collective-permute-start(bf16[768,512]{1,0:T(8,128)(2,1)} %pad_maximum_fusion.3), channel_id=1, source_target_pairs={{8,0},{10,2},{12,4},{14,6},{16,24},{18,26},{20,28},{22,30},{9,1},{... | collective-permute-start | bytes 2359304 | tf_op jit(solution)/shard_map/ppermute | solution.py:324
  158.8 8.8 %project.1 = (f32[256,512]{1,0:T(8,128)S(1)}, f32[256,512]{1,0:T(8,128)S(1)}, f32[256,512]{1,0:T(8,128)S(1)}, f32[256,512]{1,0:T(8,128)S(1)}, f32[256,256]{1,0:T...) custom-call(s32[4]{0:T(128)S(1)} %get-tuple-element.359.flag_ref, ...), custom_call_target="tpu_custom_call" | custom-call | flops 4831838208 | bytes 11010048 | tf_op jit(solution)/shard_map/project/pallas_call | solution.py:213
  167.8 3.2 %collective-permute-start.30 = (bf16[768,256]{1,0:T(8,128)(2,1)S(1)}, bf16[768,256]{1,0:T(8,128)(2,1)S(1)}, u32[]{:S(2)}, u32[]{:S(2)}) collective-permute-start(bf16[768,256]{1,0:T(8,128)(2,1)S(1)} %pad_maximum_fusion.7), channel_id=1, source_target_pairs={{8,16},{10,18},{12,20},{14,22},{16,8},{18,10},{20,12},{22,14},{9,1... | collective-permute-start | bytes 1179656 | tf_op jit(solution)/shard_map/ppermute | solution.py:321
  172.4 2.8 %finish.2 = (bf16[256,512]{1,0:T(8,128)(2,1)S(1)}, bf16[256,512]{1,0:T(8,128)(2,1)S(1)}, bf16[256,512]{1,0:T(8,128)(2,1)S(1)}, bf16[256,512]{1,0:T(8,128)(2,1)S(1)}) custom-call(s32[4]{0:T(128)S(1)} %get-tuple-element.359.flag_ref, s32[4]{0:T(128)S(1)} %get-tuple-element.360.place_ref, bf16[4,256,1024]{2,1,0:T(8,128)(2,1)S(1)} %copy-done.33, ...), custom_call_target="tpu_custom_call" | custom-call | flops 1073741824 | bytes 3145728 | tf_op jit(solution)/shard_map/finish/pallas_call | solution.py:259
  187.0 3.7 %collective-permute-done.28.refs_3_ = bf16[256,512]{1,0:T(8,128)(2,1)S(1)} collective-permute-done((bf16[256,512]{1,0:T(8,128)(2,1)S(1)}, bf16[256,512]{1,0:T(8,128)(2,1)S(1)}, u32[]{:S(2)}, u32[]{:S(2)}) %collective-permute-start.28) | collective-permute-done | bytes 262176 | tf_op jit(solution)/shard_map/ppermute | solution.py:120
  194.9 3.0 %assemble.1 = bf16[256,3072]{1,0:T(8,128)(2,1)} custom-call(s32[1]{0:T(128)} %bitcast.4.spot_ref, bf16[256,512]{1,0:T(8,128)(2,1)} %copy-done.19, bf16[256,512]{1,0:T(8,128)(2,1)} %copy-done.34, bf16[256,512]{1,0:T(8,128)(2,1)} %copy-done.35, bf16[256,512]{1,0:T(8,128)(2,1)} %copy-done.36, bf16[256,256]{1,0:T(8,128)(2,1)} %copy-done.22, ...), custom_call_target="tpu_custom_call" | custom-call | tf_op jit(solution)/shard_map/assemble/pallas_call | solution.py:291
  (177 shorter events, 81.3 us)
Async XLA Ops:
  2.2 22.7 %collective-permute-start.4 = (bf16[256,768]{1,0:T(8,128)(2,1)S(1)}, bf16[256,768]{1,0:T(8,128)(2,1)S(1)}, u32[]{:S(2)}, u32[]{:S(2)}) collective-permute-start(bf16[256,768]{1,0:T(8,128)(2,1)S(1)} %get-tuple-element.243.refs_6_), channel_id=1, source_target_pairs={{0,16},{2,18},{4,20},{6,22},{8,24},{10,26},{12,28},{14,30},{16,0},... | collective-permute-start | bytes 1179656 | tf_op jit(solution)/shard_map/ppermute | solution.py:120
  4.8 20.1 %collective-permute-start.5 = (bf16[256,768]{1,0:T(8,128)(2,1)S(1)}, bf16[256,768]{1,0:T(8,128)(2,1)S(1)}, u32[]{:S(2)}, u32[]{:S(2)}) collective-permute-start(bf16[256,768]{1,0:T(8,128)(2,1)S(1)} %get-tuple-element.243.refs_6_), channel_id=1, source_target_pairs={{0,8},{2,10},{4,12},{6,14},{8,0},{10,2},{12,4},{14,6},{16,24},{18,... | collective-permute-start | bytes 1179656 | tf_op jit(solution)/shard_map/ppermute | solution.py:120
  5.3 20.4 %collective-permute-start.6 = (bf16[256,768]{1,0:T(8,128)(2,1)S(1)}, bf16[256,768]{1,0:T(8,128)(2,1)S(1)}, u32[]{:S(2)}, u32[]{:S(2)}) collective-permute-start(bf16[256,768]{1,0:T(8,128)(2,1)S(1)} %get-tuple-element.237), channel_id=1, source_target_pairs={{0,2},{2,0},{4,6},{6,4},{8,10},{10,8},{12,14},{14,12},{16,18},{18,... | collective-permute-start | bytes 1179656 | tf_op jit(solution)/shard_map/ppermute | solution.py:120
  6.8 18.9 %collective-permute-start.7 = (bf16[256,768]{1,0:T(8,128)(2,1)S(1)}, bf16[256,768]{1,0:T(8,128)(2,1)S(1)}, u32[]{:S(2)}, u32[]{:S(2)}) collective-permute-start(bf16[256,768]{1,0:T(8,128)(2,1)S(1)} %get-tuple-element.238), channel_id=1, source_target_pairs={{0,4},{2,6},{4,0},{6,2},{8,12},{10,14},{12,8},{14,10},{16,20},{18,... | collective-permute-start | bytes 1179656 | tf_op jit(solution)/shard_map/ppermute | solution.py:120
  28.1 25.3 %collective-permute-start.10 = (bf16[256,768]{1,0:T(8,128)(2,1)}, bf16[256,768]{1,0:T(8,128)(2,1)S(1)}, u32[]{:S(2)}, u32[]{:S(2)}) collective-permute-start(bf16[256,768]{1,0:T(8,128)(2,1)} %get-tuple-element.246), channel_id=1, source_target_pairs={{0,6},{2,4},{4,2},{6,0},{8,14},{10,12},{12,10},{14,8},{16,22},{18,... | collective-permute-start | bytes 1179656 | tf_op jit(solution)/shard_map/ppermute | solution.py:120
  30.0 23.4 %collective-permute-start.8 = (bf16[256,768]{1,0:T(8,128)(2,1)S(1)}, bf16[256,768]{1,0:T(8,128)(2,1)S(1)}, u32[]{:S(2)}, u32[]{:S(2)}) collective-permute-start(bf16[256,768]{1,0:T(8,128)(2,1)S(1)} %collective-permute-done.4.refs_14_), channel_id=1, source_target_pairs={{8,0},{10,2},{12,4},{14,6},{16,24},{18,26},{20,28},{22,30},{9,1},{... | collective-permute-start | bytes 1179656 | tf_op jit(solution)/shard_map/ppermute | solution.py:324
  33.5 19.9 %collective-permute-start.9 = (bf16[256,768]{1,0:T(8,128)(2,1)S(1)}, bf16[256,768]{1,0:T(8,128)(2,1)S(1)}, u32[]{:S(2)}, u32[]{:S(2)}) collective-permute-start(bf16[256,768]{1,0:T(8,128)(2,1)S(1)} %get-tuple-element.243.refs_6_), channel_id=1, source_target_pairs={{8,16},{10,18},{12,20},{14,22},{16,8},{18,10},{20,12},{22,14},{9,1... | collective-permute-start | bytes 1179656 | tf_op jit(solution)/shard_map/ppermute | solution.py:321
  36.3 15.4 %collective-permute-start.12 = (f32[16,16,128]{2,1,0:T(8,128)S(1)}, f32[16,16,128]{2,1,0:T(8,128)S(1)}, u32[]{:S(2)}, u32[]{:S(2)}) collective-permute-start(f32[16,16,128]{2,1,0:T(8,128)S(1)} %multiply_add_fusion.1), channel_id=1, source_target_pairs={{0,16},{2,18},{4,20},{6,22},{8,24},{10,26},{12,28},{14,30},{1,17},... | collective-permute-start | bytes 393224 | tf_op jit(solution)/shard_map/ppermute | solution.py:115
  53.4 35.5 %collective-permute-start.13 = (bf16[256,768]{1,0:T(8,128)(2,1)S(1)}, bf16[256,768]{1,0:T(8,128)(2,1)S(1)}, u32[]{:S(2)}, u32[]{:S(2)}) collective-permute-start(bf16[256,768]{1,0:T(8,128)(2,1)S(1)} %collective-permute-done.6.refs_7_), channel_id=1, source_target_pairs={{0,16},{2,18},{4,20},{6,22},{8,24},{10,26},{12,28},{14,30},{16,0},... | collective-permute-start | bytes 1179656 | tf_op jit(solution)/shard_map/ppermute | solution.py:120
  56.8 32.1 %collective-permute-start.14 = (bf16[256,768]{1,0:T(8,128)(2,1)S(1)}, bf16[256,768]{1,0:T(8,128)(2,1)S(1)}, u32[]{:S(2)}, u32[]{:S(2)}) collective-permute-start(bf16[256,768]{1,0:T(8,128)(2,1)S(1)} %collective-permute-done.6.refs_7_), channel_id=1, source_target_pairs={{0,8},{2,10},{4,12},{6,14},{8,0},{10,2},{12,4},{14,6},{16,24},{18,... | collective-permute-start | bytes 1179656 | tf_op jit(solution)/shard_map/ppermute | solution.py:120
  89.8 31.8 %collective-permute-start.19 = (bf16[4,256,1024]{2,1,0:T(8,128)(2,1)}, bf16[4,256,1024]{2,1,0:T(8,128)(2,1)S(1)}, u32[]{:S(2)}, u32[]{:S(2)}) collective-permute-start(bf16[4,256,1024]{2,1,0:T(8,128)(2,1)} %get-tuple-element.256.refs_0_), channel_id=1, source_target_pairs={{0,1},{1,0},{2,3},{3,2},{4,5},{5,4},{6,7},{7,6},{8,9},{9,8},{10,11... | collective-permute-start | bytes 6291464 | tf_op jit(solution)/shard_map/ppermute | solution.py:120
  89.8 31.8 %collective-permute-start.17 = (bf16[2,256,1024]{2,1,0:T(8,128)(2,1)}, bf16[2,256,1024]{2,1,0:T(8,128)(2,1)S(1)}, u32[]{:S(2)}, u32[]{:S(2)}) collective-permute-start(bf16[2,256,1024]{2,1,0:T(8,128)(2,1)} %get-tuple-element.259), channel_id=1, source_target_pairs={{0,4},{2,6},{4,0},{6,2},{8,12},{10,14},{12,8},{14,10},{16,20},{18,... | collective-permute-start | bytes 3145736 | tf_op jit(solution)/shard_map/ppermute | solution.py:120
  91.4 30.2 %collective-permute-start.18 = (bf16[2,256,1024]{2,1,0:T(8,128)(2,1)}, bf16[2,256,1024]{2,1,0:T(8,128)(2,1)S(1)}, u32[]{:S(2)}, u32[]{:S(2)}) collective-permute-start(bf16[2,256,1024]{2,1,0:T(8,128)(2,1)} %get-tuple-element.260), channel_id=1, source_target_pairs={{0,2},{2,0},{4,6},{6,4},{8,10},{10,8},{12,14},{14,12},{16,18},{18,... | collective-permute-start | bytes 3145736 | tf_op jit(solution)/shard_map/ppermute | solution.py:120
  92.4 26.0 %collective-permute-start.15 = (bf16[384,768]{1,0:T(8,128)(2,1)}, bf16[384,768]{1,0:T(8,128)(2,1)S(1)}, u32[]{:S(2)}, u32[]{:S(2)}) collective-permute-start(bf16[384,768]{1,0:T(8,128)(2,1)} %pad_maximum_fusion.5.refs_8_), channel_id=1, source_target_pairs={{0,16},{2,18},{4,20},{6,22},{8,24},{10,26},{12,28},{14,30},{16,0},... | collective-permute-start | bytes 1769480 | tf_op jit(solution)/shard_map/ppermute | solution.py:120
  92.5 28.3 %collective-permute-start.16 = (bf16[384,768]{1,0:T(8,128)(2,1)}, bf16[384,768]{1,0:T(8,128)(2,1)S(1)}, u32[]{:S(2)}, u32[]{:S(2)}) collective-permute-start(bf16[384,768]{1,0:T(8,128)(2,1)} %pad_maximum_fusion.5.refs_8_), channel_id=1, source_target_pairs={{0,8},{2,10},{4,12},{6,14},{8,0},{10,2},{12,4},{14,6},{16,24},{18,... | collective-permute-start | bytes 1769480 | tf_op jit(solution)/shard_map/ppermute | solution.py:120
  121.6 13.2 %collective-permute-start.22 = (bf16[2,256,1024]{2,1,0:T(8,128)(2,1)S(1)}, bf16[2,256,1024]{2,1,0:T(8,128)(2,1)S(1)}, u32[]{:S(2)}, u32[]{:S(2)}) collective-permute-start(bf16[2,256,1024]{2,1,0:T(8,128)(2,1)S(1)} %collective-permute-done.17.refs_1_), channel_id=1, source_target_pairs={{0,1},{1,0},{2,3},{3,2},{4,5},{5,4},{6,7},{7,6},{8,9},{9,8},{10,11... | collective-permute-start | bytes 3145736 | tf_op jit(solution)/shard_map/ppermute | solution.py:120
  121.7 14.1 %collective-permute-start.23 = (bf16[2,256,1024]{2,1,0:T(8,128)(2,1)S(1)}, bf16[2,256,1024]{2,1,0:T(8,128)(2,1)S(1)}, u32[]{:S(2)}, u32[]{:S(2)}) collective-permute-start(bf16[2,256,1024]{2,1,0:T(8,128)(2,1)S(1)} %collective-permute-done.18.refs_2_), channel_id=1, source_target_pairs={{0,1},{1,0},{2,3},{3,2},{4,5},{5,4},{6,7},{7,6},{8,9},{9,8},{10,11... | collective-permute-start | bytes 3145736 | tf_op jit(solution)/shard_map/ppermute | solution.py:120
  122.2 11.0 %collective-permute-start.20 = (bf16[128,768]{1,0:T(8,128)(2,1)}, bf16[128,768]{1,0:T(8,128)(2,1)S(1)}, u32[]{:S(2)}, u32[]{:S(2)}) collective-permute-start(bf16[128,768]{1,0:T(8,128)(2,1)} %slice.43.refs_9_), channel_id=1, source_target_pairs={{0,16},{2,18},{4,20},{6,22},{8,24},{10,26},{12,28},{14,30},{16,0},... | collective-permute-start | bytes 589832 | tf_op jit(solution)/shard_map/ppermute | solution.py:120
  123.3 10.8 %collective-permute-start.21 = (bf16[128,768]{1,0:T(8,128)(2,1)}, bf16[128,768]{1,0:T(8,128)(2,1)S(1)}, u32[]{:S(2)}, u32[]{:S(2)}) collective-permute-start(bf16[128,768]{1,0:T(8,128)(2,1)} %slice.43.refs_9_), channel_id=1, source_target_pairs={{0,8},{2,10},{4,12},{6,14},{8,0},{10,2},{12,4},{14,6},{16,24},{18,... | collective-permute-start | bytes 589832 | tf_op jit(solution)/shard_map/ppermute | solution.py:120
  127.8 39.9 %collective-permute-start.25 = (bf16[768,512]{1,0:T(8,128)(2,1)}, bf16[768,512]{1,0:T(8,128)(2,1)}, u32[]{:S(2)}, u32[]{:S(2)}) collective-permute-start(bf16[768,512]{1,0:T(8,128)(2,1)} %pad_maximum_fusion.4), channel_id=1, source_target_pairs={{8,16},{10,18},{12,20},{14,22},{16,8},{18,10},{20,12},{22,14},{9,1... | collective-permute-start | bytes 2359304 | tf_op jit(solution)/shard_map/ppermute | solution.py:321
  138.5 29.1 %collective-permute-start.24 = (bf16[768,512]{1,0:T(8,128)(2,1)}, bf16[768,512]{1,0:T(8,128)(2,1)}, u32[]{:S(2)}, u32[]{:S(2)}) collective-permute-start(bf16[768,512]{1,0:T(8,128)(2,1)} %pad_maximum_fusion.3), channel_id=1, source_target_pairs={{8,0},{10,2},{12,4},{14,6},{16,24},{18,26},{20,28},{22,30},{9,1},{... | collective-permute-start | bytes 2359304 | tf_op jit(solution)/shard_map/ppermute | solution.py:324
  167.8 12.8 %collective-permute-start.30 = (bf16[768,256]{1,0:T(8,128)(2,1)S(1)}, bf16[768,256]{1,0:T(8,128)(2,1)S(1)}, u32[]{:S(2)}, u32[]{:S(2)}) collective-permute-start(bf16[768,256]{1,0:T(8,128)(2,1)S(1)} %pad_maximum_fusion.7), channel_id=1, source_target_pairs={{8,16},{10,18},{12,20},{14,22},{16,8},{18,10},{20,12},{22,14},{9,1... | collective-permute-start | bytes 1179656 | tf_op jit(solution)/shard_map/ppermute | solution.py:321
  176.3 10.7 %collective-permute-start.27 = (bf16[256,512]{1,0:T(8,128)(2,1)S(1)}, bf16[256,512]{1,0:T(8,128)(2,1)S(1)}, u32[]{:S(2)}, u32[]{:S(2)}) collective-permute-start(bf16[256,512]{1,0:T(8,128)(2,1)S(1)} %get-tuple-element.293), channel_id=1, source_target_pairs={{0,4},{2,6},{4,0},{6,2},{8,12},{10,14},{12,8},{14,10},{16,20},{18,... | collective-permute-start | bytes 786440 | tf_op jit(solution)/shard_map/ppermute | solution.py:120
  176.8 14.0 %collective-permute-start.28 = (bf16[256,512]{1,0:T(8,128)(2,1)S(1)}, bf16[256,512]{1,0:T(8,128)(2,1)S(1)}, u32[]{:S(2)}, u32[]{:S(2)}) collective-permute-start(bf16[256,512]{1,0:T(8,128)(2,1)S(1)} %get-tuple-element.294), channel_id=1, source_target_pairs={{0,6},{2,4},{4,2},{6,0},{8,14},{10,12},{12,10},{14,8},{16,22},{18,... | collective-permute-start | bytes 786440 | tf_op jit(solution)/shard_map/ppermute | solution.py:120
  (57 other events, 371.2 us)

commit v5 on v4

--- a/solution.py
+++ b/solution.py
@@ -8,6 +8,7 @@
 LANES = 128
 RADIX = 4
 PLANE = 4
+VMEM_BYTES = 60 << 20
 
 
 def spread_signal(k_ref, v_ref, sig_ref):
@@ -81,7 +82,7 @@
         out_specs=moded,
         out_shape=jax.ShapeDtypeStruct(rate.shape, jnp.float32),
         scratch_shapes=[pltpu.VMEM((rows * width // LANES, LANES), jnp.float32)],
-        compiler_params=pltpu.CompilerParams(vmem_limit_bytes=32 << 20),
+        compiler_params=pltpu.CompilerParams(vmem_limit_bytes=VMEM_BYTES),
         cost_estimate=pl.CostEstimate(
             flops=2 * modes * rows * chan, bytes_accessed=4 * rows * chan, transcendentals=modes * chan
         ),
@@ -102,7 +103,7 @@
         out_specs=pl.BlockSpec((None, rows, width), lambda i: (i, 0, 0)),
         out_shape=jax.ShapeDtypeStruct((chan // width, rows, width), jnp.bfloat16),
         scratch_shapes=[spread, spread],
-        compiler_params=pltpu.CompilerParams(vmem_limit_bytes=32 << 20),
+        compiler_params=pltpu.CompilerParams(vmem_limit_bytes=VMEM_BYTES),
         cost_estimate=pl.CostEstimate(
             flops=4 * modes * rows * chan, bytes_accessed=8 * rows * chan, transcendentals=2 * modes * chan
         ),
@@ -137,17 +138,6 @@
                 total = total + jnp.exp(-rate * float(rows * stride * k)) * shift_ctx(base, stride * k)
         stride *= RADIX
     return total
-
-
-def box(fn, *args):
-    once = (lax.axis_index("ctx") >= 0).astype(jnp.int32)
-    shapes = jax.eval_shape(fn, *args)
-    empty = jax.tree.map(lambda a: jnp.zeros(a.shape, a.dtype), shapes)
-
-    def run(step, _):
-        return fn(*tie(step, *args)[1:])
-
-    return lax.fori_loop(0, once, run, empty)
 
 
 def fold_pair(ends, rate, flip, span):
@@ -215,7 +205,7 @@
         in_specs=[smem, smem] + [vmem] * (count + len(weights)),
         out_specs=[vmem] * (PLANE * len(widths)),
         out_shape=[jax.ShapeDtypeStruct((rows, width), jnp.float32) for width in widths for _ in range(PLANE)],
-        compiler_params=pltpu.CompilerParams(vmem_limit_bytes=16 << 20),
+        compiler_params=pltpu.CompilerParams(vmem_limit_bytes=VMEM_BYTES),
         cost_estimate=pl.CostEstimate(
             flops=2 * PLANE * rows * depth * len(blocks) * cols,
             bytes_accessed=2 * len(blocks) * depth * (PLANE * rows + cols),
@@ -323,55 +313,38 @@
     def outward(x):
         return lax.ppermute(x, "ctx", [(i, i ^ PLANE) for i in middle])
 
-    def plane_scan(k, v, rate):
-        ends = end_states(k, v, rate)
-        both, other, later = fold_pair(ends, rate, 1, rows)
-        before = jnp.where(later, other, 0.0)
-        both, other, later = fold_pair(both, rate, 2, 2 * rows)
-        odd = (me & 1).astype(jnp.float32)
-        return both, before + jnp.where(later, jnp.exp(-rate * (odd * rows)) * other, 0.0)
-
     own = [lax.dynamic_slice_in_dim(w_out, (spot ^ r) * cols, cols, axis=1) for r in range(PLANE)]
     w0, w1, w2, w3 = tie(*own)
     f0, n0 = far(w0), near(w0)
-    w1, w2 = exchange(w1, "ctx", 1), exchange(w2, "ctx", 2)
-    both, before = box(plane_scan, k, v, rate)
-    f0, n0, w0, w1, w2, w3, both, before = tie(f0, n0, w0, w1, w2, w3, both, before)
-
-    w3 = exchange(w3, "ctx", 3)
-    out0, mid0 = outward(f0), across(w0)
+    ends = end_states(k, v, rate)
+    both, other, later = fold_pair(ends, rate, 1, rows)
+    before = jnp.where(later, other, 0.0)
+    both, other, later = fold_pair(both, rate, 2, 2 * rows)
+    odd = (me & 1).astype(jnp.float32)
+    before = before + jnp.where(later, jnp.exp(-rate * (odd * rows)) * other, 0.0)
+    f0, n0, w1, w2, w3, both, before = tie(f0, n0, w1, w2, w3, both, before)
+
+    arrived = [exchange(w, "ctx", r + 1) for r, w in enumerate((w1, w2, w3))]
     last = shift_ctx(both, PLANE)
     decay = jnp.exp(-rate * float(PLANE * rows))
     carried = last + decay * shift_ctx(both + decay * last, 2 * PLANE)
     enter = before + jnp.exp(-rate * (spot * rows).astype(jnp.float32)) * carried
-    out0, mid0, w1, w2, w3, enter = tie(out0, mid0, w1, w2, w3, enter)
-
-    def convolve(q, k, v, enter):
-        one, two = gated_conv(q, k, v, rate, residue, skip, enter)
-        one_x, two_y = exchange(one, "ctx", 1), exchange(two, "ctx", 2)
-        return jnp.stack([one, one_x]), jnp.stack([two, two_y]), jnp.stack([one, one_x, two, two_y])
-
-    f1, n1 = far(w1), near(w1)
-    one_pair, two_pair, pairs = box(convolve, q, k, v, enter)
-    early = 3 * chunk // 2
-    w23 = jnp.concatenate([w2, w3])
-    w23, w4 = w23[:early], w23[early:]
-    f1, n1, w1, w23, w4, one_pair, two_pair, pairs = tie(f1, n1, w1, w23, w4, one_pair, two_pair, pairs)
-
-    f23, n23 = far(w23), near(w23)
-    one_far, two_far = exchange(one_pair, "ctx", 2), exchange(two_pair, "ctx", 1)
-    pairs_t = exchange(pairs, "ch", 1)
-    f23, n23, w4, one_far, two_far, pairs_t = tie(f23, n23, w4, one_far, two_far, pairs_t)
-
-    f4, n4 = far(w4), near(w4)
-    one_far_t, two_far_t = exchange(one_far, "ch", 1), exchange(two_far, "ch", 1)
-    f4, n4, one_far_t, two_far_t = tie(f4, n4, one_far_t, two_far_t)
-
-    def row_blocks(nearest, far_one, far_two):
-        return [
-            [(nearest, 0), (nearest, 1), (far_one, 0), (far_one, 1)],
-            [(nearest, 2), (far_two, 0), (nearest, 3), (far_two, 1)],
-        ]
+    gated = gated_conv(q, k, v, rate, residue, skip, enter)
+    rest = jnp.concatenate(arrived)
+    gated, rest = tie(gated, rest)
+
+    fr, nr = far(rest), near(rest)
+    held = [gated] + [exchange(gated, "ctx", r) for r in range(1, PLANE)]
+    mid_first, mid_second = rest[:, :wide], rest[:, wide:]
+    fr, nr, mid_first, mid_second, *held = tie(fr, nr, mid_first, mid_second, *held)
+
+    out0 = outward(f0)
+    outA = outward(fr[:, :wide])
+    theirs = [exchange(x, "ch", 1) for x in held]
+    out0, outA, *held = tie(out0, outA, *held, *theirs)
+
+    def row_blocks(found):
+        return [[(x, half) for x in found] for half in range(2)]
 
     def source_of(b):
         return jnp.where(b // 2 == core, b & 1, 2 + (b & 1))
@@ -383,13 +356,13 @@
         span = slice(wide, None) if part else slice(0, wide)
         return jnp.concatenate([block[:, span] for block in blocks])
 
-    outA, midA = outward(side(0, f1, f23, f4)), across(side(0, w1, w23, w4))
-    sources = row_blocks(pairs, one_far, two_far) + row_blocks(pairs_t, one_far_t, two_far_t)
-    accA, accB = project(flags, places, sources, [(w0, w1, w23, w4), (n0, n1, n23, n4), (f0, f1, f23, f4)], widths)
-    outA, midA, f1, f23, f4, w1, w23, w4, *accs = tie(outA, midA, f1, f23, f4, w1, w23, w4, *accA, *accB)
+    mid0, midA = across(w0), across(mid_first)
+    sources = row_blocks(held[:PLANE]) + row_blocks(held[PLANE:])
+    accA, accB = project(flags, places, sources, [(w0, rest), (n0, nr), (f0, fr)], widths)
+    mid0, midA, fr, mid_second, *accs = tie(mid0, midA, fr, mid_second, *accA, *accB)
     accA, accB = accs[:PLANE], accs[PLANE:]
 
-    outB, midB = outward(side(1, f1, f23, f4)), across(side(1, w1, w23, w4))
+    outB, midB = outward(fr[:, wide:]), across(mid_second)
     madeA = finish(flags, places, sources, (out0, mid0), (outA, midA), accA, 0)
     backA = [madeA[0]] + [exchange(madeA[r], "ctx", r) for r in range(1, PLANE)]
     madeB = finish(flags, places, sources, (out0, mid0), (outB, midB), accB, wide)

time: 199 us -> 202 us (1.015)
  waiting for transfers between devices: 69 us -> 94.4 us
  local copies, waits for them, and re-layouts: 34.8 us -> 16.3 us
  other arithmetic: 13.4 us -> 1.6 us
  Pallas kernels: 28.1 us -> 36.9 us
    ppermute x3, waiting for transfers between devices: 0.01 us -> 18 us  [outward(): return lax.ppermute(x, 'ctx', [(i, i ^ PLANE) for i in middle])]
    unnamed x88 -> x76, local copies, waits for them, and re-layouts: 23.4 us -> 12.3 us
    ppermute x2, waiting for transfers between devices: 13.4 us -> 4.47 us  [shift_ctx(): return lax.ppermute(x, 'ctx', [(i, i + by) for i in range(count - by)])]
    ppermute x26 -> x22, waiting for transfers between devices: 53.7 us -> 62.5 us  [exchange(): return lax.ppermute(x, axis, [(i, i ^ flip) for i in range(count)])]
    ppermute x3, waiting for transfers between devices: 1.85 us -> 9.51 us  [across(): return lax.ppermute(x, 'ctx', [(i, i ^ 3 * PLANE) for i in middle])]
    another operation x3 -> x0, other arithmetic: 6.96 us -> none  [the longest x1 2.76 us: convolve(): jnp.stack([one, one_x, two, two_y])]
    ppermute x26 -> x22, starting transfers between devices: 31.2 us -> 24.8 us  [exchange(): return lax.ppermute(x, axis, [(i, i ^ flip) for i in range(count)])]
    another operation x5 -> x0, local copies, waits for them, and re-layouts: 4.76 us -> none
  transfers between devices with their start and end apart: 34 -> 30, of which waited for: 14 -> 14; matrix products, arithmetic and copies ran while one was open for 12% -> 3% of each run, Pallas kernels for 13% -> 14%
where the time goes in v5:
time: 202 us; the launch traced here: 201 us
  waiting for transfers between devices  94.4 us (47%)
  starting transfers between devices  51.5 us (25%)
  Pallas kernels  36.9 us (18%)
  local copies, waits for them, and re-layouts  16.3 us (8%)
    ppermute x22, waiting for transfers between devices, exchange(): return lax.ppermute(x, axis, [(i, i ^ flip) for i in range(count)])  62.5 us
    ppermute x22, starting transfers between devices, exchange(): return lax.ppermute(x, axis, [(i, i ^ flip) for i in range(count)])  24.8 us
    ppermute x3, waiting for transfers between devices, outward(): return lax.ppermute(x, 'ctx', [(i, i ^ PLANE) for i in middle])  18 us
    ppermute x3, starting transfers between devices, across(): return lax.ppermute(x, 'ctx', [(i, i ^ 3 * PLANE) for i in middle])  12.6 us
    unnamed x76, local copies, waits for them, and re-layouts  12.3 us
    pallas_call x1, Pallas kernels, project(): pl.pallas_call(kernel, in_specs=[smem, smem] + [vmem] * (count + len(weig...  12.3 us
    ppermute x3, waiting for transfers between devices, across(): return lax.ppermute(x, 'ctx', [(i, i ^ 3 * PLANE) for i in middle])  9.51 us
    pallas_call x1, Pallas kernels, gated_conv(): pl.pallas_call(conv_kernel, grid=(chan // width,), in_specs=[wide, wide,...  8.76 us
  transfers between devices with their start and end apart: 30, of which 14 were waited for; matrix products, arithmetic and copies ran while one was open for 3% of the time, Pallas kernels for 14%

profile of v5, /device:TPU:8, one launch (start us, length us, event | category | flops | bytes accessed | tf_op | source)
XLA Modules:
  0.0 201.3 jit_solution(8309065044695445778)
XLA Ops:
  1.7 4.9 %end_states.1 = f32[16,16,128]{2,1,0:T(8,128)} custom-call(bf16[256,2048]{1,0:T(8,128)(2,1)} %k_ref.3, bf16[256,2048]{1,0:T(8,128)(2,1)} %v_ref.3, f32[16,16,128]{2,1,0:T(8,128)} %bitcast.18), custom_call_target="tpu_custom_call" | custom-call | flops 16777216 | bytes 2097152 | tf_op jit(solution)/shard_map/end_states/pallas_call | solution.py:78
  9.2 2.6 %collective-permute-start = (bf16[256,768]{1,0:T(8,128)(2,1)S(1)}, bf16[256,768]{1,0:T(8,128)(2,1)S(1)}, u32[]{:S(2)}, u32[]{:S(2)}) collective-permute-start(bf16[256,768]{1,0:T(8,128)(2,1)S(1)} %get-tuple-element.64.refs_8_), channel_id=1, source_target_pairs={{0,16},{2,18},{4,20},{6,22},{8,24},{10,26},{12,28},{14,30},{16,0},... | collective-permute-start | bytes 1179656 | tf_op jit(solution)/shard_map/ppermute | solution.py:121
  13.9 3.4 %collective-permute-done.3 = f32[16,16,128]{2,1,0:T(8,128)S(1)} collective-permute-done((f32[16,16,128]{2,1,0:T(8,128)S(1)}, f32[16,16,128]{2,1,0:T(8,128)S(1)}, u32[]{:S(2)}, u32[]{:S(2)}) %collective-permute-start.3) | collective-permute-done | bytes 131104 | tf_op jit(solution)/shard_map/ppermute | solution.py:121
  17.4 10.8 %collective-permute-done.refs_12_ = bf16[256,768]{1,0:T(8,128)(2,1)S(1)} collective-permute-done((bf16[256,768]{1,0:T(8,128)(2,1)S(1)}, bf16[256,768]{1,0:T(8,128)(2,1)S(1)}, u32[]{:S(2)}, u32[]{:S(2)}) %collective-permute-start) | collective-permute-done | bytes 393248 | tf_op jit(solution)/shard_map/ppermute | solution.py:121
  29.2 2.3 %collective-permute-start.5 = (f32[16,16,128]{2,1,0:T(8,128)S(1)}, f32[16,16,128]{2,1,0:T(8,128)S(1)}, u32[]{:S(2)}, u32[]{:S(2)}) collective-permute-start(f32[16,16,128]{2,1,0:T(8,128)S(1)} %get-tuple-element.70), channel_id=1, source_target_pairs={{0,8},{2,10},{4,12},{6,14},{8,16},{10,18},{12,20},{14,22},{16,24},... | collective-permute-start | bytes 393224 | tf_op jit(solution)/shard_map/ppermute | solution.py:116
  36.1 4.7 %collective-permute-start.6 = (f32[16,16,128]{2,1,0:T(8,128)S(1)}, f32[16,16,128]{2,1,0:T(8,128)S(1)}, u32[]{:S(2)}, u32[]{:S(2)}) collective-permute-start(f32[16,16,128]{2,1,0:T(8,128)S(1)} %multiply_add_fusion.1), channel_id=1, source_target_pairs={{0,16},{2,18},{4,20},{6,22},{8,24},{10,26},{12,28},{14,30},{1,17},... | collective-permute-start | bytes 393224 | tf_op jit(solution)/shard_map/ppermute | solution.py:116
  41.5 3.5 %collective-permute-done.6 = f32[16,16,128]{2,1,0:T(8,128)S(1)} collective-permute-done((f32[16,16,128]{2,1,0:T(8,128)S(1)}, f32[16,16,128]{2,1,0:T(8,128)S(1)}, u32[]{:S(2)}, u32[]{:S(2)}) %collective-permute-start.6) | collective-permute-done | bytes 131104 | tf_op jit(solution)/shard_map/ppermute | solution.py:116
  45.8 8.8 %gated_conv.1.refs_0_ = bf16[2,256,1024]{2,1,0:T(8,128)(2,1)} custom-call(bf16[256,2048]{1,0:T(8,128)(2,1)} %q_ref.1, bf16[256,2048]{1,0:T(8,128)(2,1)} %k_ref.3, bf16[256,2048]{1,0:T(8,128)(2,1)} %v_ref.3, f32[16,16,128]{2,1,0:T(8,128)} %bitcast.19, f32[16,16,128]{2,1,0:T(8,128)} %bitcast.20, f32[16,128]{1,0:T(8,128)} %bitcast.23, ...), custom_call_target="tpu_custom_call" | custom-call | flops 33554432 | bytes 4194304 | tf_op jit(solution)/shard_map/gated_conv/pallas_call | solution.py:99
  56.3 3.4 %collective-permute-start.10 = (bf16[768,768]{1,0:T(8,128)(2,1)S(1)}, bf16[768,768]{1,0:T(8,128)(2,1)S(1)}, u32[]{:S(2)}, u32[]{:S(2)}) collective-permute-start(bf16[768,768]{1,0:T(8,128)(2,1)S(1)} %pad_maximum_fusion.refs_9_), channel_id=1, source_target_pairs={{0,16},{2,18},{4,20},{6,22},{8,24},{10,26},{12,28},{14,30},{16,0},... | collective-permute-start | bytes 3538952 | tf_op jit(solution)/shard_map/ppermute | solution.py:121
  62.6 19.2 %collective-permute-done.12.refs_1_ = bf16[2,256,1024]{2,1,0:T(8,128)(2,1)S(1)} collective-permute-done((bf16[2,256,1024]{2,1,0:T(8,128)(2,1)S(1)}, bf16[2,256,1024]{2,1,0:T(8,128)(2,1)S(1)}, u32[]{:S(2)}, u32[]{:S(2)}) %collective-permute-start.12) | collective-permute-done | bytes 1048608 | tf_op jit(solution)/shard_map/ppermute | solution.py:121
  84.9 21.0 %collective-permute-done.13.refs_2_ = bf16[2,256,1024]{2,1,0:T(8,128)(2,1)S(1)} collective-permute-done((bf16[2,256,1024]{2,1,0:T(8,128)(2,1)S(1)}, bf16[2,256,1024]{2,1,0:T(8,128)(2,1)S(1)}, u32[]{:S(2)}, u32[]{:S(2)}) %collective-permute-start.13) | collective-permute-done | bytes 1048608 | tf_op jit(solution)/shard_map/ppermute | solution.py:121
  107.0 4.4 %collective-permute-start.15 = (bf16[768,512]{1,0:T(8,128)(2,1)S(1)}, bf16[768,512]{1,0:T(8,128)(2,1)S(1)}, u32[]{:S(2)}, u32[]{:S(2)}) collective-permute-start(bf16[768,512]{1,0:T(8,128)(2,1)S(1)} %slice.14), channel_id=1, source_target_pairs={{8,0},{10,2},{12,4},{14,6},{16,24},{18,26},{20,28},{22,30},{9,1},{... | collective-permute-start | bytes 2359304 | tf_op jit(solution)/shard_map/ppermute | solution.py:314
  112.1 3.1 %collective-permute-done.4.refs_8_ = bf16[256,768]{1,0:T(8,128)(2,1)S(1)} collective-permute-done((bf16[256,768]{1,0:T(8,128)(2,1)S(1)}, bf16[256,768]{1,0:T(8,128)(2,1)S(1)}, u32[]{:S(2)}, u32[]{:S(2)}) %collective-permute-start.4) | collective-permute-done | bytes 393248 | tf_op jit(solution)/shard_map/ppermute | solution.py:314
  115.2 14.8 %collective-permute-done.15.refs_10_ = bf16[768,512]{1,0:T(8,128)(2,1)S(1)} collective-permute-done((bf16[768,512]{1,0:T(8,128)(2,1)S(1)}, bf16[768,512]{1,0:T(8,128)(2,1)S(1)}, u32[]{:S(2)}, u32[]{:S(2)}) %collective-permute-start.15) | collective-permute-done | bytes 786464 | tf_op jit(solution)/shard_map/ppermute | solution.py:314
  131.0 7.1 %collective-permute-start.21 = (bf16[768,512]{1,0:T(8,128)(2,1)}, bf16[768,512]{1,0:T(8,128)(2,1)}, u32[]{:S(2)}, u32[]{:S(2)}) collective-permute-start(bf16[768,512]{1,0:T(8,128)(2,1)} %slice.12), channel_id=1, source_target_pairs={{8,16},{10,18},{12,20},{14,22},{16,8},{18,10},{20,12},{22,14},{9,1... | collective-permute-start | bytes 2359304 | tf_op jit(solution)/shard_map/ppermute | solution.py:311
  138.8 1.9 collective-permute-start.20
  140.8 12.3 %project.1 = (f32[256,512]{1,0:T(8,128)}, f32[256,512]{1,0:T(8,128)}, f32[256,512]{1,0:T(8,128)}, f32[256,512]{1,0:T(8,128)}, f32[256,256]{1,0:T(8,128)}, /*inde...) custom-call(s32[4]{0:T(128)} %get-tuple-element.129.flag_ref, s32[4]{0:T(128)} %get-tuple-element.130.place_ref, ...), custom_call_target="tpu_custom_call" | custom-call | flops 4831838208 | bytes 11010048 | tf_op jit(solution)/shard_map/project/pallas_call | solution.py:203
  153.2 9.5 %collective-permute-done.20.refs_9_ = bf16[256,768]{1,0:T(8,128)(2,1)} collective-permute-done((bf16[256,768]{1,0:T(8,128)(2,1)}, bf16[256,768]{1,0:T(8,128)(2,1)}, u32[]{:S(2)}, u32[]{:S(2)}) %collective-permute-start.20) | collective-permute-done | bytes 393248 | tf_op jit(solution)/shard_map/ppermute | solution.py:311
  165.1 3.6 %collective-permute-start.26 = (bf16[768,256]{1,0:T(8,128)(2,1)S(1)}, bf16[768,256]{1,0:T(8,128)(2,1)S(1)}, u32[]{:S(2)}, u32[]{:S(2)}) collective-permute-start(bf16[768,256]{1,0:T(8,128)(2,1)S(1)} %copy-done.25), channel_id=1, source_target_pairs={{8,16},{10,18},{12,20},{14,22},{16,8},{18,10},{20,12},{22,14},{9,1... | collective-permute-start | bytes 1179656 | tf_op jit(solution)/shard_map/ppermute | solution.py:311
  175.3 4.5 %finish.2 = (bf16[256,512]{1,0:T(8,128)(2,1)S(1)}, bf16[256,512]{1,0:T(8,128)(2,1)S(1)}, bf16[256,512]{1,0:T(8,128)(2,1)S(1)}, bf16[256,512]{1,0:T(8,128)(2,1)S(1)}) custom-call(s32[4]{0:T(128)S(1)} %copy-done.18, s32[4]{0:T(128)S(1)} %copy-done.19, bf16[2,256,1024]{2,1,0:T(8,128)(2,1)S(1)} %copy-done.1, bf16[2,256,1024]{2,1,0:T(8,128)(2,1)S(1)} %copy-done.3, ...), custom_call_target="tpu_custom_call" | custom-call | flops 1073741824 | bytes 3145728 | tf_op jit(solution)/shard_map/finish/pallas_call | solution.py:249
  183.4 3.4 %finish.3 = (bf16[256,256]{1,0:T(8,128)(2,1)S(1)}, bf16[256,256]{1,0:T(8,128)(2,1)S(1)}, bf16[256,256]{1,0:T(8,128)(2,1)S(1)}, bf16[256,256]{1,0:T(8,128)(2,1)S(1)}) custom-call(s32[4]{0:T(128)S(1)} %copy-done.18, s32[4]{0:T(128)S(1)} %copy-done.19, bf16[2,256,1024]{2,1,0:T(8,128)(2,1)S(1)} %copy-done.1, bf16[2,256,1024]{2,1,0:T(8,128)(2,1)S(1)} %copy-done.3, ...), custom_call_target="tpu_custom_call" | custom-call | flops 536870912 | bytes 2621440 | tf_op jit(solution)/shard_map/finish/pallas_call | solution.py:249
  191.6 3.2 %collective-permute-done.23.refs_2_ = bf16[256,512]{1,0:T(8,128)(2,1)S(1)} collective-permute-done((bf16[256,512]{1,0:T(8,128)(2,1)S(1)}, bf16[256,512]{1,0:T(8,128)(2,1)S(1)}, u32[]{:S(2)}, u32[]{:S(2)}) %collective-permute-start.23) | collective-permute-done | bytes 262176 | tf_op jit(solution)/shard_map/ppermute | solution.py:121
  195.0 2.5 %collective-permute-done.28.refs_6_ = bf16[256,256]{1,0:T(8,128)(2,1)S(1)} collective-permute-done((bf16[256,256]{1,0:T(8,128)(2,1)S(1)}, bf16[256,256]{1,0:T(8,128)(2,1)S(1)}, u32[]{:S(2)}, u32[]{:S(2)}) %collective-permute-start.28) | collective-permute-done | bytes 131104 | tf_op jit(solution)/shard_map/ppermute | solution.py:121
  198.3 3.0 %assemble.1 = bf16[256,3072]{1,0:T(8,128)(2,1)} custom-call(s32[1]{0:T(128)} %bitcast.spot_ref, bf16[256,512]{1,0:T(8,128)(2,1)} %copy-done.16, bf16[256,512]{1,0:T(8,128)(2,1)} %copy-done.27, bf16[256,512]{1,0:T(8,128)(2,1)} %copy-done.28, bf16[256,512]{1,0:T(8,128)(2,1)} %copy-done.29, bf16[256,256]{1,0:T(8,128)(2,1)} %copy-done.17, ...), custom_call_target="tpu_custom_call" | custom-call | tf_op jit(solution)/shard_map/assemble/pallas_call | solution.py:281
  (129 shorter events, 42.6 us)
Async XLA Ops:
  9.2 19.0 %collective-permute-start = (bf16[256,768]{1,0:T(8,128)(2,1)S(1)}, bf16[256,768]{1,0:T(8,128)(2,1)S(1)}, u32[]{:S(2)}, u32[]{:S(2)}) collective-permute-start(bf16[256,768]{1,0:T(8,128)(2,1)S(1)} %get-tuple-element.64.refs_8_), channel_id=1, source_target_pairs={{0,16},{2,18},{4,20},{6,22},{8,24},{10,26},{12,28},{14,30},{16,0},... | collective-permute-start | bytes 1179656 | tf_op jit(solution)/shard_map/ppermute | solution.py:121
  11.8 17.5 %collective-permute-start.1 = (bf16[256,768]{1,0:T(8,128)(2,1)S(1)}, bf16[256,768]{1,0:T(8,128)(2,1)S(1)}, u32[]{:S(2)}, u32[]{:S(2)}) collective-permute-start(bf16[256,768]{1,0:T(8,128)(2,1)S(1)} %get-tuple-element.64.refs_8_), channel_id=1, source_target_pairs={{0,8},{2,10},{4,12},{6,14},{8,0},{10,2},{12,4},{14,6},{16,24},{18,... | collective-permute-start | bytes 1179656 | tf_op jit(solution)/shard_map/ppermute | solution.py:121
  31.6 22.9 %collective-permute-start.7 = (bf16[256,768]{1,0:T(8,128)(2,1)}, bf16[256,768]{1,0:T(8,128)(2,1)S(1)}, u32[]{:S(2)}, u32[]{:S(2)}) collective-permute-start(bf16[256,768]{1,0:T(8,128)(2,1)} %get-tuple-element.71), channel_id=1, source_target_pairs={{0,2},{2,0},{4,6},{6,4},{8,10},{10,8},{12,14},{14,12},{16,18},{18,... | collective-permute-start | bytes 1179656 | tf_op jit(solution)/shard_map/ppermute | solution.py:121
  32.2 22.4 %collective-permute-start.8 = (bf16[256,768]{1,0:T(8,128)(2,1)}, bf16[256,768]{1,0:T(8,128)(2,1)S(1)}, u32[]{:S(2)}, u32[]{:S(2)}) collective-permute-start(bf16[256,768]{1,0:T(8,128)(2,1)} %get-tuple-element.72), channel_id=1, source_target_pairs={{0,4},{2,6},{4,0},{6,2},{8,12},{10,14},{12,8},{14,10},{16,20},{18,... | collective-permute-start | bytes 1179656 | tf_op jit(solution)/shard_map/ppermute | solution.py:121
  33.7 20.8 %collective-permute-start.9 = (bf16[256,768]{1,0:T(8,128)(2,1)S(1)}, bf16[256,768]{1,0:T(8,128)(2,1)S(1)}, u32[]{:S(2)}, u32[]{:S(2)}) collective-permute-start(bf16[256,768]{1,0:T(8,128)(2,1)S(1)} %get-tuple-element.73), channel_id=1, source_target_pairs={{0,6},{2,4},{4,2},{6,0},{8,14},{10,12},{12,10},{14,8},{16,22},{18,... | collective-permute-start | bytes 1179656 | tf_op jit(solution)/shard_map/ppermute | solution.py:121
  36.1 8.9 %collective-permute-start.6 = (f32[16,16,128]{2,1,0:T(8,128)S(1)}, f32[16,16,128]{2,1,0:T(8,128)S(1)}, u32[]{:S(2)}, u32[]{:S(2)}) collective-permute-start(f32[16,16,128]{2,1,0:T(8,128)S(1)} %multiply_add_fusion.1), channel_id=1, source_target_pairs={{0,16},{2,18},{4,20},{6,22},{8,24},{10,26},{12,28},{14,30},{1,17},... | collective-permute-start | bytes 393224 | tf_op jit(solution)/shard_map/ppermute | solution.py:116
  55.8 26.1 %collective-permute-start.12 = (bf16[2,256,1024]{2,1,0:T(8,128)(2,1)S(1)}, bf16[2,256,1024]{2,1,0:T(8,128)(2,1)S(1)}, u32[]{:S(2)}, u32[]{:S(2)}) collective-permute-start(bf16[2,256,1024]{2,1,0:T(8,128)(2,1)S(1)} %copy-done), channel_id=1, source_target_pairs={{0,2},{2,0},{4,6},{6,4},{8,10},{10,8},{12,14},{14,12},{16,18},{18,... | collective-permute-start | bytes 3145736 | tf_op jit(solution)/shard_map/ppermute | solution.py:121
  56.3 49.6 %collective-permute-start.10 = (bf16[768,768]{1,0:T(8,128)(2,1)S(1)}, bf16[768,768]{1,0:T(8,128)(2,1)S(1)}, u32[]{:S(2)}, u32[]{:S(2)}) collective-permute-start(bf16[768,768]{1,0:T(8,128)(2,1)S(1)} %pad_maximum_fusion.refs_9_), channel_id=1, source_target_pairs={{0,16},{2,18},{4,20},{6,22},{8,24},{10,26},{12,28},{14,30},{16,0},... | collective-permute-start | bytes 3538952 | tf_op jit(solution)/shard_map/ppermute | solution.py:121
  59.7 47.2 %collective-permute-start.11 = (bf16[768,768]{1,0:T(8,128)(2,1)S(1)}, bf16[768,768]{1,0:T(8,128)(2,1)}, u32[]{:S(2)}, u32[]{:S(2)}) collective-permute-start(bf16[768,768]{1,0:T(8,128)(2,1)S(1)} %pad_maximum_fusion.refs_9_), channel_id=1, source_target_pairs={{0,8},{2,10},{4,12},{6,14},{8,0},{10,2},{12,4},{14,6},{16,24},{18,... | collective-permute-start | bytes 3538952 | tf_op jit(solution)/shard_map/ppermute | solution.py:121
  59.7 46.3 %collective-permute-start.13 = (bf16[2,256,1024]{2,1,0:T(8,128)(2,1)S(1)}, bf16[2,256,1024]{2,1,0:T(8,128)(2,1)S(1)}, u32[]{:S(2)}, u32[]{:S(2)}) collective-permute-start(bf16[2,256,1024]{2,1,0:T(8,128)(2,1)S(1)} %copy-done), channel_id=1, source_target_pairs={{0,4},{2,6},{4,0},{6,2},{8,12},{10,14},{12,8},{14,10},{16,20},{18,... | collective-permute-start | bytes 3145736 | tf_op jit(solution)/shard_map/ppermute | solution.py:121
  61.2 44.7 %collective-permute-start.14 = (bf16[2,256,1024]{2,1,0:T(8,128)(2,1)S(1)}, bf16[2,256,1024]{2,1,0:T(8,128)(2,1)}, u32[]{:S(2)}, u32[]{:S(2)}) collective-permute-start(bf16[2,256,1024]{2,1,0:T(8,128)(2,1)S(1)} %copy-done), channel_id=1, source_target_pairs={{0,6},{2,4},{4,2},{6,0},{8,14},{10,12},{12,10},{14,8},{16,22},{18,... | collective-permute-start | bytes 3145736 | tf_op jit(solution)/shard_map/ppermute | solution.py:121
  81.9 33.4 %collective-permute-start.4 = (bf16[256,768]{1,0:T(8,128)(2,1)S(1)}, bf16[256,768]{1,0:T(8,128)(2,1)S(1)}, u32[]{:S(2)}, u32[]{:S(2)}) collective-permute-start(bf16[256,768]{1,0:T(8,128)(2,1)S(1)} %copy-done.35), channel_id=1, source_target_pairs={{8,0},{10,2},{12,4},{14,6},{16,24},{18,26},{20,28},{22,30},{9,1},{... | collective-permute-start | bytes 1179656 | tf_op jit(solution)/shard_map/ppermute | solution.py:314
  107.0 23.0 %collective-permute-start.15 = (bf16[768,512]{1,0:T(8,128)(2,1)S(1)}, bf16[768,512]{1,0:T(8,128)(2,1)S(1)}, u32[]{:S(2)}, u32[]{:S(2)}) collective-permute-start(bf16[768,512]{1,0:T(8,128)(2,1)S(1)} %slice.14), channel_id=1, source_target_pairs={{8,0},{10,2},{12,4},{14,6},{16,24},{18,26},{20,28},{22,30},{9,1},{... | collective-permute-start | bytes 2359304 | tf_op jit(solution)/shard_map/ppermute | solution.py:314
  111.4 27.4 %collective-permute-start.16 = (bf16[2,256,1024]{2,1,0:T(8,128)(2,1)S(1)}, bf16[2,256,1024]{2,1,0:T(8,128)(2,1)}, u32[]{:S(2)}, u32[]{:S(2)}) collective-permute-start(bf16[2,256,1024]{2,1,0:T(8,128)(2,1)S(1)} %copy-done), channel_id=1, source_target_pairs={{0,1},{1,0},{2,3},{3,2},{4,5},{5,4},{6,7},{7,6},{8,9},{9,8},{10,11... | collective-permute-start | bytes 3145736 | tf_op jit(solution)/shard_map/ppermute | solution.py:121
  111.5 29.2 %collective-permute-start.17 = (bf16[2,256,1024]{2,1,0:T(8,128)(2,1)S(1)}, bf16[2,256,1024]{2,1,0:T(8,128)(2,1)}, u32[]{:S(2)}, u32[]{:S(2)}) collective-permute-start(bf16[2,256,1024]{2,1,0:T(8,128)(2,1)S(1)} %collective-permute-done.12.refs_1_), channel_id=1, source_target_pairs={{0,1},{1,0},{2,3},{3,2},{4,5},{5,4},{6,7},{7,6},{8,9},{9,8},{10,11... | collective-permute-start | bytes 3145736 | tf_op jit(solution)/shard_map/ppermute | solution.py:121
  112.0 28.8 %collective-permute-start.18 = (bf16[2,256,1024]{2,1,0:T(8,128)(2,1)S(1)}, bf16[2,256,1024]{2,1,0:T(8,128)(2,1)}, u32[]{:S(2)}, u32[]{:S(2)}) collective-permute-start(bf16[2,256,1024]{2,1,0:T(8,128)(2,1)S(1)} %collective-permute-done.13.refs_2_), channel_id=1, source_target_pairs={{0,1},{1,0},{2,3},{3,2},{4,5},{5,4},{6,7},{7,6},{8,9},{9,8},{10,11... | collective-permute-start | bytes 3145736 | tf_op jit(solution)/shard_map/ppermute | solution.py:121
  115.2 25.6 %collective-permute-start.19 = (bf16[2,256,1024]{2,1,0:T(8,128)(2,1)}, bf16[2,256,1024]{2,1,0:T(8,128)(2,1)}, u32[]{:S(2)}, u32[]{:S(2)}) collective-permute-start(bf16[2,256,1024]{2,1,0:T(8,128)(2,1)} %collective-permute-done.14.refs_3_), channel_id=1, source_target_pairs={{0,1},{1,0},{2,3},{3,2},{4,5},{5,4},{6,7},{7,6},{8,9},{9,8},{10,11... | collective-permute-start | bytes 3145736 | tf_op jit(solution)/shard_map/ppermute | solution.py:121
  131.0 31.7 %collective-permute-start.21 = (bf16[768,512]{1,0:T(8,128)(2,1)}, bf16[768,512]{1,0:T(8,128)(2,1)}, u32[]{:S(2)}, u32[]{:S(2)}) collective-permute-start(bf16[768,512]{1,0:T(8,128)(2,1)} %slice.12), channel_id=1, source_target_pairs={{8,16},{10,18},{12,20},{14,22},{16,8},{18,10},{20,12},{22,14},{9,1... | collective-permute-start | bytes 2359304 | tf_op jit(solution)/shard_map/ppermute | solution.py:311
  138.8 23.8 %collective-permute-start.20 = (bf16[256,768]{1,0:T(8,128)(2,1)}, bf16[256,768]{1,0:T(8,128)(2,1)}, u32[]{:S(2)}, u32[]{:S(2)}) collective-permute-start(bf16[256,768]{1,0:T(8,128)(2,1)} %copy-done.26), channel_id=1, source_target_pairs={{8,16},{10,18},{12,20},{14,22},{16,8},{18,10},{20,12},{22,14},{9,1... | collective-permute-start | bytes 1179656 | tf_op jit(solution)/shard_map/ppermute | solution.py:311
  163.8 19.6 %collective-permute-start.25 = (bf16[768,256]{1,0:T(8,128)(2,1)S(1)}, bf16[768,256]{1,0:T(8,128)(2,1)S(1)}, u32[]{:S(2)}, u32[]{:S(2)}) collective-permute-start(bf16[768,256]{1,0:T(8,128)(2,1)S(1)} %slice.15), channel_id=1, source_target_pairs={{8,0},{10,2},{12,4},{14,6},{16,24},{18,26},{20,28},{22,30},{9,1},{... | collective-permute-start | bytes 1179656 | tf_op jit(solution)/shard_map/ppermute | solution.py:314
  165.1 18.3 %collective-permute-start.26 = (bf16[768,256]{1,0:T(8,128)(2,1)S(1)}, bf16[768,256]{1,0:T(8,128)(2,1)S(1)}, u32[]{:S(2)}, u32[]{:S(2)}) collective-permute-start(bf16[768,256]{1,0:T(8,128)(2,1)S(1)} %copy-done.25), channel_id=1, source_target_pairs={{8,16},{10,18},{12,20},{14,22},{16,8},{18,10},{20,12},{22,14},{9,1... | collective-permute-start | bytes 1179656 | tf_op jit(solution)/shard_map/ppermute | solution.py:311
  179.8 10.7 %collective-permute-start.22 = (bf16[256,512]{1,0:T(8,128)(2,1)S(1)}, bf16[256,512]{1,0:T(8,128)(2,1)S(1)}, u32[]{:S(2)}, u32[]{:S(2)}) collective-permute-start(bf16[256,512]{1,0:T(8,128)(2,1)S(1)} %get-tuple-element.110), channel_id=1, source_target_pairs={{0,2},{2,0},{4,6},{6,4},{8,10},{10,8},{12,14},{14,12},{16,18},{18,... | collective-permute-start | bytes 786440 | tf_op jit(solution)/shard_map/ppermute | solution.py:121
  181.4 13.4 %collective-permute-start.23 = (bf16[256,512]{1,0:T(8,128)(2,1)S(1)}, bf16[256,512]{1,0:T(8,128)(2,1)S(1)}, u32[]{:S(2)}, u32[]{:S(2)}) collective-permute-start(bf16[256,512]{1,0:T(8,128)(2,1)S(1)} %get-tuple-element.111), channel_id=1, source_target_pairs={{0,4},{2,6},{4,0},{6,2},{8,12},{10,14},{12,8},{14,10},{16,20},{18,... | collective-permute-start | bytes 786440 | tf_op jit(solution)/shard_map/ppermute | solution.py:121
  182.9 11.9 %collective-permute-start.24 = (bf16[256,512]{1,0:T(8,128)(2,1)S(1)}, bf16[256,512]{1,0:T(8,128)(2,1)S(1)}, u32[]{:S(2)}, u32[]{:S(2)}) collective-permute-start(bf16[256,512]{1,0:T(8,128)(2,1)S(1)} %get-tuple-element.112), channel_id=1, source_target_pairs={{0,6},{2,4},{4,2},{6,0},{8,14},{10,12},{12,10},{14,8},{16,22},{18,... | collective-permute-start | bytes 786440 | tf_op jit(solution)/shard_map/ppermute | solution.py:121
  (43 other events, 541.8 us)

commit v6 on v1

v6 whole, which is shorter than its diff:
```python
import jax
import jax.numpy as jnp
from jax import lax
from jax.experimental import pallas as pl
from jax.experimental.pallas import tpu as pltpu
from jax.sharding import PartitionSpec as P

LANES = 128
RADIX = 4
PLANE = 4
VMEM_BYTES = 60 << 20


def spread_signal(k_ref, v_ref, sig_ref):
    rows, width = k_ref.shape
    groups = width // LANES
    for g in range(groups):
        cols = pl.ds(g * LANES, LANES)
        product = k_ref[:, cols].astype(jnp.float32) * v_ref[:, cols].astype(jnp.float32)
        sig_ref[pl.ds(g, rows, stride=groups), :] = product


def spread_modes(ref, out_ref):
    modes, width = ref.shape
    groups = width // LANES
    for g in range(groups):
        out_ref[pl.ds(g, modes, stride=groups), :] = ref[:, pl.ds(g * LANES, LANES)]


def ends_kernel(k_ref, v_ref, rate_ref, end_ref, sig_ref, mode_ref):
    rows, width = k_ref.shape
    modes, groups, _ = end_ref.shape
    spread_signal(k_ref, v_ref, sig_ref)
    spread_modes(rate_ref, mode_ref)
    decay = [jnp.exp(-mode_ref[pl.ds(m * groups, groups), :]) for m in range(modes)]

    def step(t, state):
        s = sig_ref[pl.ds(pl.multiple_of(t * groups, groups), groups), :]
        return tuple(d * h + s for d, h in zip(decay, state))

    zero = jnp.zeros((groups, LANES), jnp.float32)
    state = lax.fori_loop(0, rows, step, (zero,) * modes, unroll=8)
    for m in range(modes):
        end_ref[m] = state[m]


def conv_kernel(q_ref, k_ref, v_ref, rate_ref, residue_ref, skip_ref, enter_ref, out_ref, sig_ref, conv_ref, mode_ref, weight_ref):
    rows, width = k_ref.shape
    modes, groups, _ = enter_ref.shape
    spread_signal(k_ref, v_ref, sig_ref)
    spread_modes(rate_ref, mode_ref)
    spread_modes(residue_ref, weight_ref)
    rates = [mode_ref[pl.ds(m * groups, groups), :] for m in range(modes)]
    decay = [jnp.exp(-rate) for rate in rates]
    weight = [weight_ref[pl.ds(m * groups, groups), :] * jnp.sqrt(2.0 * rate) for m, rate in enumerate(rates)]
    skip = skip_ref[...]

    def step(t, state):
        at = pl.ds(pl.multiple_of(t * groups, groups), groups)
        s = sig_ref[at, :]
        state = tuple(d * h + s for d, h in zip(decay, state))
        terms = [c * h for c, h in zip(weight, state)] + [skip * s]
        while len(terms) > 1:
            terms = [sum(terms[i : i + 2]) for i in range(0, len(terms), 2)]
        conv_ref[at, :] = terms[0]
        return state

    lax.fori_loop(0, rows, step, tuple(enter_ref[m] for m in range(modes)), unroll=4)
    for g in range(groups):
        cols = pl.ds(g * LANES, LANES)
        conv = conv_ref[pl.ds(g, rows, stride=groups), :]
        out_ref[:, cols] = (q_ref[:, cols].astype(jnp.float32) * conv).astype(out_ref.dtype)


def block_specs(rows, modes, width):
    groups = width // LANES
    return (
        pl.BlockSpec((rows, width), lambda i: (0, i)),
        pl.BlockSpec((modes, width), lambda i: (0, i)),
        pl.BlockSpec((modes, groups, LANES), lambda i: (0, i, 0)),
        pl.BlockSpec((groups, LANES), lambda i: (i, 0)),
    )


def end_states(k, v, rate):
    rows, chan = k.shape
    modes = rate.shape[0]
    width = min(chan, 8 * LANES)
    wide, moded, state, _ = block_specs(rows, modes, width)
    return pl.pallas_call(
        ends_kernel,
        grid=(chan // width,),
        in_specs=[wide, wide, moded],
        out_specs=state,
        out_shape=jax.ShapeDtypeStruct((modes, chan // LANES, LANES), jnp.float32),
        scratch_shapes=[
            pltpu.VMEM((rows * width // LANES, LANES), jnp.float32),
            pltpu.VMEM((modes * width // LANES, LANES), jnp.float32),
        ],
        compiler_params=pltpu.CompilerParams(vmem_limit_bytes=VMEM_BYTES),
        cost_estimate=pl.CostEstimate(
            flops=2 * modes * rows * chan, bytes_accessed=4 * rows * chan, transcendentals=modes * chan
        ),
        name="end_states",
    )(k, v, rate)


def gated_conv(q, k, v, rate, residue, skip, enter):
    rows, chan = k.shape
    modes = rate.shape[0]
    width = min(chan, 8 * LANES)
    wide, moded, state, single = block_specs(rows, modes, width)
    spread = pltpu.VMEM((rows * width // LANES, LANES), jnp.float32)
    moded_spread = pltpu.VMEM((modes * width // LANES, LANES), jnp.float32)
    return pl.pallas_call(
        conv_kernel,
        grid=(chan // width,),
        in_specs=[wide, wide, wide, moded, moded, single, state],
        out_specs=pl.BlockSpec((None, rows, width), lambda i: (i, 0, 0)),
        out_shape=jax.ShapeDtypeStruct((chan // width, rows, width), jnp.bfloat16),
        scratch_shapes=[spread, spread, moded_spread, moded_spread],
        compiler_params=pltpu.CompilerParams(vmem_limit_bytes=VMEM_BYTES),
        cost_estimate=pl.CostEstimate(
            flops=4 * modes * rows * chan, bytes_accessed=8 * rows * chan, transcendentals=2 * modes * chan
        ),
        name="gated_conv",
    )(q, k, v, rate, residue, skip, enter)


def shift_ctx(x, by):
    count = lax.axis_size("ctx")
    return lax.ppermute(x, "ctx", [(i, i + by) for i in range(count - by)])


def exchange(x, axis, flip):
    count = lax.axis_size(axis)
    return lax.ppermute(x, axis, [(i, i ^ flip) for i in range(count)])


def tie(*values):
    return lax.optimization_barrier(values)


def entering_states(ends, rate, rows):
    count = lax.axis_size("ctx")
    total = jnp.zeros_like(ends)
    for k in range(1, min(RADIX, count - 1) + 1):
        total = total + jnp.exp(-rate * float(rows * (k - 1))) * shift_ctx(ends, k)
    stride = RADIX
    while stride < count:
        base = total
        for k in range(1, RADIX):
            if stride * k < count:
                total = total + jnp.exp(-rate * float(rows * stride * k)) * shift_ctx(base, stride * k)
        stride *= RADIX
    return total


def box(fn, *args):
    once = (lax.axis_index("ctx") >= 0).astype(jnp.int32)
    shapes = jax.eval_shape(fn, *args)
    empty = jax.tree.map(lambda a: jnp.zeros(a.shape, a.dtype), shapes)

    def run(step, _):
        return fn(*tie(step, *args)[1:])

    return lax.fori_loop(0, once, run, empty)


def product(flags, places, ours, theirs, blocks, accs, widths, out_dtype):
    _, rows, depth = ours[0].shape
    chunk = depth // PLANE
    cols = sum(widths)
    count = len(blocks)
    weights = [array for _, _, pieces in blocks for choices, *_ in pieces for array in choices]
    accs = accs or []

    def kernel(flag_ref, place_ref, *refs):
        our_refs, their_refs, refs = refs[:PLANE], refs[PLANE : 2 * PLANE], refs[2 * PLANE :]
        weight_refs, refs = list(refs[: len(weights)]), refs[len(weights) :]
        acc_refs, out_refs = refs[: len(accs)], refs[len(accs) : len(accs) + PLANE * len(widths)]
        gated_buf, weight_buf, gated_sems, weight_sems = refs[-4:]

        def target(b, r):
            start = pl.multiple_of(b * depth + place_ref[r] * chunk, chunk)
            return weight_buf.at[pl.ds(start, chunk), :]

        for b, (flag, pick, pieces) in enumerate(blocks):
            for choices, first, chunks, col in pieces:
                for c in range(len(choices)):
                    ref = weight_refs.pop(0)
                    for r in range(first, first + chunks):
                        source = ref.at[pl.ds((r - first) * chunk, chunk), pl.ds(col, cols)]
                        copy = pltpu.make_async_copy(source, target(b, r), weight_sems.at[b])
                        if pick is None:
                            copy.start()
                        else:
                            pl.when(flag_ref[pick] == c)(copy.start)
            half = flag_ref[flag] & 1
            for r in range(PLANE):
                for c, refs_of in enumerate((our_refs, their_refs)):
                    copy = pltpu.make_async_copy(refs_of[r].at[half], gated_buf.at[b, r], gated_sems.at[b, r])
                    pl.when(flag_ref[flag] // 2 == c)(copy.start)
        for b in range(count):
            block = weight_buf.at[pl.ds(b * depth, depth), :]
            pltpu.make_async_copy(block, block, weight_sems.at[b]).wait()
            for r in range(PLANE):
                pltpu.make_async_copy(our_refs[r].at[0], gated_buf.at[b, r], gated_sems.at[b, r]).wait()
                first = 0
                for part, width in enumerate(widths):
                    at = part * PLANE + r
                    total = jnp.dot(
                        gated_buf[b, r],
                        weight_buf[pl.ds(b * depth, depth), pl.ds(first, width)],
                        preferred_element_type=jnp.float32,
                    )
                    if b:
                        total = total + out_refs[at][...]
                    elif accs:
                        total = total + acc_refs[at][...]
                    out_refs[at][...] = total.astype(out_dtype)
                    first += width

    smem = pl.BlockSpec(memory_space=pltpu.SMEM)
    vmem = pl.BlockSpec(memory_space=pltpu.VMEM)
    anywhere = pl.BlockSpec(memory_space=pl.ANY)
    made = pl.pallas_call(
        kernel,
        in_specs=[smem, smem] + [anywhere] * (2 * PLANE + len(weights)) + [vmem] * len(accs),
        out_specs=[vmem] * (PLANE * len(widths)),
        out_shape=[jax.ShapeDtypeStruct((rows, width), out_dtype) for width in widths for _ in range(PLANE)],
        scratch_shapes=[
            pltpu.VMEM((count, PLANE, rows, depth), jnp.bfloat16),
            pltpu.VMEM((count * depth, cols), jnp.bfloat16),
            pltpu.SemaphoreType.DMA((count, PLANE)),
            pltpu.SemaphoreType.DMA((count,)),
        ],
        compiler_params=pltpu.CompilerParams(vmem_limit_bytes=VMEM_BYTES),
        cost_estimate=pl.CostEstimate(
            flops=2 * PLANE * rows * depth * count * cols,
            bytes_accessed=2 * count * depth * (PLANE * rows + cols),
            transcendentals=0,
        ),
        name="product",
    )(flags, places, *ours, *theirs, *weights, *accs)
    return [list(made[part * PLANE : (part + 1) * PLANE]) for part in range(len(widths))]


def assemble(places, parts):
    rows = parts[0][0].shape[0]
    widths = [part[0].shape[1] for part in parts]
    cols = sum(widths)
    flat = [piece for part in parts for piece in part]

    def kernel(place_ref, *refs):
        *piece_refs, out_ref, sems = refs
        copies = []
        first = 0
        for part, width in enumerate(widths):
            for r in range(PLANE):
                at = part * PLANE + r
                start = pl.multiple_of(place_ref[r] * cols + first, LANES)
                target = out_ref.at[:, pl.ds(start, width)]
                copies.append(pltpu.make_async_copy(piece_refs[at], target, sems.at[at]))
                copies[-1].start()
            first += width
        for copy in copies:
            copy.wait()

    return pl.pallas_call(
        kernel,
        in_specs=[pl.BlockSpec(memory_space=pltpu.SMEM)] + [pl.BlockSpec(memory_space=pltpu.VMEM)] * len(flat),
        out_specs=pl.BlockSpec(memory_space=pl.ANY),
        out_shape=jax.ShapeDtypeStruct((rows, cols * PLANE), flat[0].dtype),
        scratch_shapes=[pltpu.SemaphoreType.DMA((len(flat),))],
        compiler_params=pltpu.CompilerParams(vmem_limit_bytes=16 << 20),
        name="assemble",
    )(places, *flat)


def split_block(q, k, v, residue, rate, skip, w_out):
    rows, chan = q.shape
    modes = rate.shape[0]
    me = lax.axis_index("ctx")
    core = lax.axis_index("ch")
    spot, plane = me & (PLANE - 1), me // PLANE
    count = lax.axis_size("ctx")
    chunk, feats = w_out.shape
    cols = feats // PLANE
    wide = 2 * cols // 3
    widths = [wide, cols - wide]
    speed = rate.reshape(modes, chan // LANES, LANES)

    def far(x):
        return exchange(x, "ctx", 2 * PLANE)

    def near(x):
        return exchange(x, "ctx", PLANE)

    middle = [i for i in range(count) if PLANE <= i < 3 * PLANE]

    def across(x):
        return lax.ppermute(x, "ctx", [(i, i ^ (3 * PLANE)) for i in middle])

    def outward(x):
        return lax.ppermute(x, "ctx", [(i, i ^ PLANE) for i in middle])

    def fade(span):
        return jnp.exp(-speed * span)

    def line_scan(k, v, rate, speed):
        ends = end_states(k, v, rate)
        decay = jnp.exp(-speed * float(PLANE * rows))
        last = shift_ctx(ends, PLANE)
        line = last + decay * shift_ctx(ends + decay * last, 2 * PLANE)
        return jnp.stack([ends, line])

    own = [lax.dynamic_slice_in_dim(w_out, (spot ^ r) * cols, cols, axis=1) for r in range(PLANE)]
    w0, w1, w2, w3 = tie(*own)
    f0 = far(w0)
    w1, w2, w3 = [exchange(w, "ctx", r + 1) for r, w in enumerate((w1, w2, w3))]
    pair = box(line_scan, k, v, rate, speed)
    f0, w0, w1, w2, w3, pair = tie(f0, w0, w1, w2, w3, pair)

    f1, n0 = far(w1), near(w0)
    out0, mid0 = outward(f0), across(w0)
    x_later, y_later = (spot & 1) != 0, (spot & 2) != 0
    other = exchange(pair, "ctx", 1)
    both = jnp.where(x_later, fade(float(rows)) * other + pair, fade(float(rows)) * pair + other)
    before = jnp.where(x_later, other[0], 0.0)
    other = exchange(both, "ctx", 2)
    before = before + jnp.where(y_later, fade((spot & 1).astype(jnp.float32) * rows) * other[0], 0.0)
    line = jnp.where(y_later, fade(2.0 * rows) * other[1] + both[1], fade(2.0 * rows) * both[1] + other[1])
    enter = before + fade((spot * rows).astype(jnp.float32)) * line
    gated = gated_conv(q, k, v, rate, residue, skip, enter)
    rest, last_two = jnp.concatenate([w1, w2, w3]), jnp.concatenate([w2, w3])
    f1, n0, out0, mid0, gated, rest, last_two = tie(f1, n0, out0, mid0, gated, rest, last_two)

    f23, nr = far(last_two), near(rest)
    ours = [gated] + [exchange(gated, "ctx", r) for r in range(1, PLANE)]
    theirs = [exchange(x, "ch", 1) for x in ours]
    midA, midB = rest[:, :wide], rest[:, wide:]
    f23, nr, midA, midB, *held = tie(f23, nr, midA, midB, *ours, *theirs)
    ours, theirs = held[:PLANE], held[PLANE:]

    def source_of(b):
        return jnp.where(b // 2 == core, b & 1, 2 + (b & 1))

    is_middle = jnp.where((plane == 0) | (plane == 3), 0, 1)
    flags = jnp.stack([source_of(plane ^ r) for r in range(4)] + [is_middle]).astype(jnp.int32)
    places = jnp.stack([spot ^ r for r in range(PLANE)]).astype(jnp.int32)

    outA, midA = outward(jnp.concatenate([f1[:, :wide], f23[:, :wide]])), across(midA)
    blocks = [
        (0, None, [((w0,), 0, 1, 0), ((rest,), 1, 3, 0)]),
        (1, None, [((n0,), 0, 1, 0), ((nr,), 1, 3, 0)]),
        (2, None, [((f0,), 0, 1, 0), ((f1,), 1, 1, 0), ((f23,), 2, 2, 0)]),
    ]
    accA, accB = product(flags, places, ours, theirs, blocks, None, widths, jnp.float32)
    outA, midA, f1, f23, midB, *accs = tie(outA, midA, f1, f23, midB, *accA, *accB)
    accA, accB = accs[:PLANE], accs[PLANE:]

    outB, midB = outward(jnp.concatenate([f1[:, wide:], f23[:, wide:]])), across(midB)
    blocks = [(3, 4, [((out0, mid0), 0, 1, 0), ((outA, midA), 1, 3, 0)])]
    (madeA,) = product(flags, places, ours, theirs, blocks, accA, widths[:1], jnp.bfloat16)
    backA = [madeA[0]] + [exchange(madeA[r], "ctx", r) for r in range(1, PLANE)]
    blocks = [(3, 4, [((out0, mid0), 0, 1, wide), ((outB, midB), 1, 3, 0)])]
    (madeB,) = product(flags, places, ours, theirs, blocks, accB, widths[1:], jnp.bfloat16)
    backB = [madeB[0]] + [exchange(madeB[r], "ctx", r) for r in range(1, PLANE)]
    return assemble(places, [backA, backB])


def body(q, k, v, residue, rate, skip, w_out):
    rows, chan = q.shape
    modes = rate.shape[0]
    groups = chan // LANES
    count, cores = lax.axis_size("ctx"), lax.axis_size("ch")
    chunk, feats = w_out.shape
    split = (
        count == 4 * PLANE
        and cores == 2
        and chan == 8 * chunk
        and chunk % LANES == 0
        and feats % (PLANE * LANES) == 0
    )
    skip = skip.reshape(groups, LANES)
    if split:
        return split_block(q, k, v, residue, rate, skip, w_out)
    ends = end_states(k, v, rate)
    enter = entering_states(ends, rate.reshape(modes, groups, LANES), rows)
    gated = gated_conv(q, k, v, rate, residue, skip, enter)
    gated = gated.transpose(1, 0, 2).reshape(rows, chan)
    full_gated = lax.all_gather(gated, "ch", axis=1, tiled=True)
    w_full = lax.all_gather(w_out, "ctx", axis=0, tiled=True)
    mixed = jnp.dot(full_gated, w_full, preferred_element_type=jnp.float32)
    return mixed.astype(jnp.bfloat16)


def solution(mesh):
    placed = (
        P("ctx", "ch"),
        P("ctx", "ch"),
        P("ctx", "ch"),
        P(None, "ch"),
        P(None, "ch"),
        P("ch"),
        P("ctx", "ch"),
    )
    return jax.shard_map(
        body, mesh=mesh, in_specs=placed, out_specs=P("ctx", "ch"), check_vma=False
    )
```

time: 361 us -> 183 us (0.51)
  waiting for transfers between devices: 297 us -> 71.8 us
  starting transfers between devices: 19 us -> 53.5 us
  Pallas kernels: 10.8 us -> 37.7 us
  matrix products: 13 us -> 0 us
  between operations: 13.5 us -> 0.72 us
  local copies, waits for them, and re-layouts: 3.45 us -> 11.1 us
  other arithmetic: 0.17 us -> 7.45 us
    all_gather x2 -> x0, waiting for transfers between devices: 283 us -> none  [the longest x1 273 us: body(): w_full = lax.all_gather(w_out, 'ctx', axis=0, tiled=True)]
    ppermute x0 -> x29, waiting for transfers between devices: none -> 56.3 us  [the longest x23 52.1 us: exchange(): return lax.ppermute(x, axis, [(i, i ^ flip) for i in range(count)])]
    ppermute x0 -> x29, starting transfers between devices: none -> 46.5 us  [the longest x23 23.9 us: exchange(): return lax.ppermute(x, axis, [(i, i ^ flip) for i in range(count)])]
    pallas_call x0 -> x4, Pallas kernels: none -> 25.4 us  [the longest x3 23.6 us: product(): pl.pallas_call(kernel, in_specs=[smem, smem] + [anywhere] * (2 * PLANE +...]
    dot_general x1 -> x0, matrix products: 13 us -> none  [body(): mixed = jnp.dot(full_gated, w_full, preferred_element_type=jnp.float32)]
    ppermute x7 -> x2, starting transfers between devices: 19 us -> 7.05 us  [shift_ctx(): return lax.ppermute(x, 'ctx', [(i, i + by) for i in range(count - by)])]
    slice x0 -> x7, local copies, waits for them, and re-layouts: none -> 3.82 us  [the longest x2 1.79 us: split_block(): midA, midB = (rest[:, :wide], rest[:, wide:])]
    ppermute x7 -> x2, waiting for transfers between devices: 14.3 us -> 15.4 us  [shift_ctx(): return lax.ppermute(x, 'ctx', [(i, i + by) for i in range(count - by)])]
  transfers between devices with their start and end apart: 9 -> 31, of which waited for: 6 -> 11; matrix products, arithmetic and copies ran while one was open for 0% -> 6% of each run, Pallas kernels for 0% -> 20%
where the time goes in v6:
time: 183 us; the launch traced here: 182 us
  waiting for transfers between devices  71.8 us (39%)
  starting transfers between devices  53.5 us (29%)
  Pallas kernels  37.7 us (21%)
  local copies, waits for them, and re-layouts  11.1 us (6%)
  other arithmetic  7.45 us (4%)
    ppermute x23, waiting for transfers between devices, exchange(): return lax.ppermute(x, axis, [(i, i ^ flip) for i in range(count)])  52.1 us
    ppermute x23, starting transfers between devices, exchange(): return lax.ppermute(x, axis, [(i, i ^ flip) for i in range(count)])  23.9 us
    pallas_call x3, Pallas kernels, product(): pl.pallas_call(kernel, in_specs=[smem, smem] + [anywhere] * (2 * PLANE +...  23.6 us
    ppermute x2, waiting for transfers between devices, shift_ctx(): return lax.ppermute(x, 'ctx', [(i, i + by) for i in range(count - by)])  15.4 us
    ppermute x3, starting transfers between devices, across(): return lax.ppermute(x, 'ctx', [(i, i ^ 3 * PLANE) for i in middle])  12.7 us
    ppermute x3, starting transfers between devices, outward(): return lax.ppermute(x, 'ctx', [(i, i ^ PLANE) for i in middle])  9.89 us
    pallas_call x1, Pallas kernels, gated_conv(): pl.pallas_call(conv_kernel, grid=(chan // width,), in_specs=[wide, wide,...  8.35 us
    ppermute x2, starting transfers between devices, shift_ctx(): return lax.ppermute(x, 'ctx', [(i, i + by) for i in range(count - by)])  7.05 us
  transfers between devices with their start and end apart: 31, of which 11 were waited for; matrix products, arithmetic and copies ran while one was open for 6% of the time, Pallas kernels for 20%

profile of v6, /device:TPU:8, one launch (start us, length us, event | category | flops | bytes accessed | tf_op | source)
XLA Modules:
  0.0 182.3 jit_solution(2147851487193828947)
XLA Ops:
  0.0 2.7 %constant_dynamic-slice_fusion = (bf16[256,768]{1,0:T(8,128)(2,1)}, bf16[256,768]{1,0:T(8,128)(2,1)}, bf16[256,768]{1,0:T(8,128)(2,1)}, bf16[256,768]{1,0:T(8,128)(2,1)}) fusion(bf16[256,3072]{1,0:T(8,128)(2,1)} %param.15, s32[]{:T(128)S(6)} %select_n.89, s32[]{:T(128)S(6)} %select_n.87, s32[]{:T(128)S(6)} %select_n.86, s32[]{:T(128)S(6)} %select_n.88), kind=kLoop, calls=%fused_computation.19 | loop fusion | bytes 3145744 | tf_op jit(solution)/shard_map/dynamic_slice | solution.py:318
  2.7 2.6 %collective-permute-start.2 = (bf16[256,768]{1,0:T(8,128)(2,1)}, bf16[256,768]{1,0:T(8,128)(2,1)}, u32[]{:S(2)}, u32[]{:S(2)}) collective-permute-start(bf16[256,768]{1,0:T(8,128)(2,1)} %get-tuple-element.110.refs_8_), channel_id=1, source_target_pairs={{0,16},{2,18},{4,20},{6,22},{8,24},{10,26},{12,28},{14,30},{16,0},... | collective-permute-start | bytes 1179656 | tf_op jit(solution)/shard_map/ppermute | solution.py:137
  9.5 29.1 %while.10 = (s32[]{:T(128)}, f32[2,16,16,128]{3,2,1,0:T(8,128)}, s32[]{:T(128)}, bf16[256,2048]{1,0:T(8,128)(2,1)S(1)}, bf16[256,2048]{1,0:T(8,128)(2,1)S(1)}, /...) while((s32[]{:T(128)}, f32[2,16,16,128]{3,2,1,0:T(8,128)}, s32[]{:T(128)}, ...), condition=%wide.region_1.2_spmd, body=%wide.region_0.1_spmd.sunk | while | flops 17104896 | bytes 4718757 | solution.py:167
  9.5 4.0 %end_states.1 = f32[16,16,128]{2,1,0:T(8,128)} custom-call(bf16[256,2048]{1,0:T(8,128)(2,1)S(1)} %get-tuple-element.227.k_ref, bf16[256,2048]{1,0:T(8,128)(2,1)S(1)} %get-tuple-element.228.v_ref, f32[16,2048]{1,0:T(8,128)S(1)} %get-tuple-element.229.rate_ref), custom_call_target="tpu_custom_call" | custom-call | flops 16777216 | bytes 2097152 | tf_op jit(solution)/shard_map/while/body/end_states/pallas_call | solution.py:90
  13.5 1.9 %collective-permute-start = (f32[16,16,128]{2,1,0:T(8,128)}, f32[16,16,128]{2,1,0:T(8,128)S(1)}, u32[]{:S(2)}, u32[]{:S(2)}) collective-permute-start(f32[16,16,128]{2,1,0:T(8,128)} %end_states.1), channel_id=1, source_target_pairs={{0,8},{2,10},{4,12},{6,14},{8,16},{10,18},{12,20},{14,22},{16,24},... | collective-permute-start | bytes 393224 | tf_op jit(solution)/shard_map/while/body/ppermute | solution.py:132
  15.4 9.7 %collective-permute-done = f32[16,16,128]{2,1,0:T(8,128)S(1)} collective-permute-done((f32[16,16,128]{2,1,0:T(8,128)}, f32[16,16,128]{2,1,0:T(8,128)S(1)}, u32[]{:S(2)}, u32[]{:S(2)}) %collective-permute-start) | collective-permute-done | bytes 131104 | tf_op jit(solution)/shard_map/while/body/ppermute | solution.py:132
  26.1 5.1 %collective-permute-start.1 = (f32[16,16,128]{2,1,0:T(8,128)S(1)}, f32[16,16,128]{2,1,0:T(8,128)S(1)}, u32[]{:S(2)}, u32[]{:S(2)}) collective-permute-start(f32[16,16,128]{2,1,0:T(8,128)S(1)} %multiply_add_fusion.2), channel_id=1, source_target_pairs={{0,16},{2,18},{4,20},{6,22},{8,24},{10,26},{12,28},{14,30},{1,17},... | collective-permute-start | bytes 393224 | tf_op jit(solution)/shard_map/while/body/ppermute | solution.py:132
  31.2 5.7 %collective-permute-done.1 = f32[16,16,128]{2,1,0:T(8,128)S(1)} collective-permute-done((f32[16,16,128]{2,1,0:T(8,128)S(1)}, f32[16,16,128]{2,1,0:T(8,128)S(1)}, u32[]{:S(2)}, u32[]{:S(2)}) %collective-permute-start.1) | collective-permute-done | bytes 131104 | tf_op jit(solution)/shard_map/while/body/ppermute | solution.py:132
  40.3 5.8 %collective-permute-start.9 = (bf16[256,768]{1,0:T(8,128)(2,1)}, bf16[256,768]{1,0:T(8,128)(2,1)S(1)}, u32[]{:S(2)}, u32[]{:S(2)}) collective-permute-start(bf16[256,768]{1,0:T(8,128)(2,1)} %get-tuple-element.110.refs_8_), channel_id=1, source_target_pairs={{8,16},{10,18},{12,20},{14,22},{16,8},{18,10},{20,12},{22,14},{9,1... | collective-permute-start | bytes 1179656 | tf_op jit(solution)/shard_map/ppermute | solution.py:303
  46.2 4.1 %collective-permute-start.8 = (bf16[256,768]{1,0:T(8,128)(2,1)}, bf16[256,768]{1,0:T(8,128)(2,1)}, u32[]{:S(2)}, u32[]{:S(2)}) collective-permute-start(bf16[256,768]{1,0:T(8,128)(2,1)} %collective-permute-done.2.refs_12_), channel_id=1, source_target_pairs={{8,0},{10,2},{12,4},{14,6},{16,24},{18,26},{20,28},{22,30},{9,1},{... | collective-permute-start | bytes 1179656 | tf_op jit(solution)/shard_map/ppermute | solution.py:306
  55.4 3.2 %collective-permute-done.11 = f32[2,16,16,128]{3,2,1,0:T(8,128)S(1)} collective-permute-done((f32[2,16,16,128]{3,2,1,0:T(8,128)S(1)}, f32[2,16,16,128]{3,2,1,0:T(8,128)S(1)}, u32[]{:S(2)}, u32[]{:S(2)}) %collective-permute-start.11) | collective-permute-done | bytes 262176 | tf_op jit(solution)/shard_map/ppermute | solution.py:137
  59.3 8.4 %gated_conv.1.refs_0_ = bf16[2,256,1024]{2,1,0:T(8,128)(2,1)} custom-call(bf16[256,2048]{1,0:T(8,128)(2,1)} %q_ref.1, bf16[256,2048]{1,0:T(8,128)(2,1)S(1)} %get-tuple-element.261, bf16[256,2048]{1,0:T(8,128)(2,1)S(1)} %get-tuple-element.262, f32[16,2048]{1,0:T(8,128)S(1)} %get-tuple-element.270, f32[16,2048]{1,0:T(8,128)} %residue_ref.1, ...), custom_call_target="tpu_custom_call" | custom-call | flops 33554432 | bytes 4194304 | tf_op jit(solution)/shard_map/gated_conv/pallas_call | solution.py:115
  67.7 3.6 %collective-permute-done.6.refs_13_ = bf16[256,768]{1,0:T(8,128)(2,1)} collective-permute-done((bf16[256,768]{1,0:T(8,128)(2,1)}, bf16[256,768]{1,0:T(8,128)(2,1)}, u32[]{:S(2)}, u32[]{:S(2)}) %collective-permute-start.6) | collective-permute-done | bytes 393248 | tf_op jit(solution)/shard_map/ppermute | solution.py:137
  74.8 3.4 %collective-permute-start.12 = (bf16[512,768]{1,0:T(8,128)(2,1)}, bf16[512,768]{1,0:T(8,128)(2,1)S(1)}, u32[]{:S(2)}, u32[]{:S(2)}) collective-permute-start(bf16[512,768]{1,0:T(8,128)(2,1)} %pad_maximum_fusion.2), channel_id=1, source_target_pairs={{0,16},{2,18},{4,20},{6,22},{8,24},{10,26},{12,28},{14,30},{16,0},... | collective-permute-start | bytes 2359304 | tf_op jit(solution)/shard_map/ppermute | solution.py:137
  78.2 30.7 %collective-permute-done.12.refs_14_ = bf16[512,768]{1,0:T(8,128)(2,1)S(1)} collective-permute-done((bf16[512,768]{1,0:T(8,128)(2,1)}, bf16[512,768]{1,0:T(8,128)(2,1)S(1)}, u32[]{:S(2)}, u32[]{:S(2)}) %collective-permute-start.12) | collective-permute-done | bytes 786464 | tf_op jit(solution)/shard_map/ppermute | solution.py:137
  109.4 7.6 %collective-permute-done.15.refs_2_ = bf16[2,256,1024]{2,1,0:T(8,128)(2,1)S(1)} collective-permute-done((bf16[2,256,1024]{2,1,0:T(8,128)(2,1)}, bf16[2,256,1024]{2,1,0:T(8,128)(2,1)S(1)}, u32[]{:S(2)}, u32[]{:S(2)}) %collective-permute-start.15) | collective-permute-done | bytes 1048608 | tf_op jit(solution)/shard_map/ppermute | solution.py:137
  122.3 4.5 %collective-permute-start.21 = (bf16[768,512]{1,0:T(8,128)(2,1)S(1)}, bf16[768,512]{1,0:T(8,128)(2,1)S(1)}, u32[]{:S(2)}, u32[]{:S(2)}) collective-permute-start(bf16[768,512]{1,0:T(8,128)(2,1)S(1)} %pad_maximum_fusion.3), channel_id=1, source_target_pairs={{8,0},{10,2},{12,4},{14,6},{16,24},{18,26},{20,28},{22,30},{9,1},{... | collective-permute-start | bytes 2359304 | tf_op jit(solution)/shard_map/ppermute | solution.py:306
  126.8 3.3 %collective-permute-start.22 = (bf16[768,512]{1,0:T(8,128)(2,1)}, bf16[768,512]{1,0:T(8,128)(2,1)S(1)}, u32[]{:S(2)}, u32[]{:S(2)}) collective-permute-start(bf16[768,512]{1,0:T(8,128)(2,1)} %slice.36), channel_id=1, source_target_pairs={{8,16},{10,18},{12,20},{14,22},{16,8},{18,10},{20,12},{22,14},{9,1... | collective-permute-start | bytes 2359304 | tf_op jit(solution)/shard_map/ppermute | solution.py:303
  131.5 12.8 %product.3 = (f32[256,512]{1,0:T(8,128)}, f32[256,512]{1,0:T(8,128)}, f32[256,512]{1,0:T(8,128)}, f32[256,512]{1,0:T(8,128)}, f32[256,256]{1,0:T(8,128)}, /*inde...) custom-call(s32[5]{0:T(128)} %stack.52.flag_ref, s32[4]{0:T(128)} %pad_add_fusion.place_ref, ...), custom_call_target="tpu_custom_call" | custom-call | flops 4831838208 | bytes 11010048 | tf_op jit(solution)/shard_map/product/pallas_call | solution.py:227
  144.3 4.2 %collective-permute-done.22.refs_11_ = bf16[768,512]{1,0:T(8,128)(2,1)S(1)} collective-permute-done((bf16[768,512]{1,0:T(8,128)(2,1)}, bf16[768,512]{1,0:T(8,128)(2,1)S(1)}, u32[]{:S(2)}, u32[]{:S(2)}) %collective-permute-start.22) | collective-permute-done | bytes 786464 | tf_op jit(solution)/shard_map/ppermute | solution.py:303
  150.9 3.5 %collective-permute-start.27 = (bf16[768,256]{1,0:T(8,128)(2,1)S(1)}, bf16[768,256]{1,0:T(8,128)(2,1)S(1)}, u32[]{:S(2)}, u32[]{:S(2)}) collective-permute-start(bf16[768,256]{1,0:T(8,128)(2,1)S(1)} %copy-done.24), channel_id=1, source_target_pairs={{8,16},{10,18},{12,20},{14,22},{16,8},{18,10},{20,12},{22,14},{9,1... | collective-permute-start | bytes 1179656 | tf_op jit(solution)/shard_map/ppermute | solution.py:303
  154.5 5.7 %product.4 = (bf16[256,512]{1,0:T(8,128)(2,1)}, bf16[256,512]{1,0:T(8,128)(2,1)}, bf16[256,512]{1,0:T(8,128)(2,1)}, bf16[256,512]{1,0:T(8,128)(2,1)}) custom-call(s32[5]{0:T(128)} %stack.52.flag_ref, s32[4]{0:T(128)} %pad_add_fusion.place_ref, bf16[2,256,1024]{2,1,0:T(8,128)(2,1)} %gated_conv.1.refs_0_, bf16[2,256,1024]{2,1,0:T(8,128)(2,1)} %copy-done.7, ...), custom_call_target="tpu_custom_call" | custom-call | flops 1073741824 | bytes 3145728 | tf_op jit(solution)/shard_map/product/pallas_call | solution.py:227
  165.3 5.1 %product.5 = (bf16[256,256]{1,0:T(8,128)(2,1)}, bf16[256,256]{1,0:T(8,128)(2,1)}, bf16[256,256]{1,0:T(8,128)(2,1)}, bf16[256,256]{1,0:T(8,128)(2,1)}) custom-call(s32[5]{0:T(128)} %stack.52.flag_ref, s32[4]{0:T(128)} %pad_add_fusion.place_ref, bf16[2,256,1024]{2,1,0:T(8,128)(2,1)} %gated_conv.1.refs_0_, bf16[2,256,1024]{2,1,0:T(8,128)(2,1)} %copy-done.7, ...), custom_call_target="tpu_custom_call" | custom-call | flops 536870912 | bytes 2621440 | tf_op jit(solution)/shard_map/product/pallas_call | solution.py:227
  175.5 2.3 %collective-permute-done.28.refs_5_ = bf16[256,256]{1,0:T(8,128)(2,1)S(1)} collective-permute-done((bf16[256,256]{1,0:T(8,128)(2,1)}, bf16[256,256]{1,0:T(8,128)(2,1)S(1)}, u32[]{:S(2)}, u32[]{:S(2)}) %collective-permute-start.28) | collective-permute-done | bytes 131104 | tf_op jit(solution)/shard_map/ppermute | solution.py:137
  (119 shorter events, 41.7 us)
Async XLA Ops:
  2.7 35.9 %collective-permute-start.2 = (bf16[256,768]{1,0:T(8,128)(2,1)}, bf16[256,768]{1,0:T(8,128)(2,1)}, u32[]{:S(2)}, u32[]{:S(2)}) collective-permute-start(bf16[256,768]{1,0:T(8,128)(2,1)} %get-tuple-element.110.refs_8_), channel_id=1, source_target_pairs={{0,16},{2,18},{4,20},{6,22},{8,24},{10,26},{12,28},{14,30},{16,0},... | collective-permute-start | bytes 1179656 | tf_op jit(solution)/shard_map/ppermute | solution.py:137
  5.3 33.3 %collective-permute-start.3 = (bf16[256,768]{1,0:T(8,128)(2,1)}, bf16[256,768]{1,0:T(8,128)(2,1)}, u32[]{:S(2)}, u32[]{:S(2)}) collective-permute-start(bf16[256,768]{1,0:T(8,128)(2,1)} %get-tuple-element.105), channel_id=1, source_target_pairs={{0,2},{2,0},{4,6},{6,4},{8,10},{10,8},{12,14},{14,12},{16,18},{18,... | collective-permute-start | bytes 1179656 | tf_op jit(solution)/shard_map/ppermute | solution.py:137
  6.8 31.8 %collective-permute-start.4 = (bf16[256,768]{1,0:T(8,128)(2,1)}, bf16[256,768]{1,0:T(8,128)(2,1)S(1)}, u32[]{:S(2)}, u32[]{:S(2)}) collective-permute-start(bf16[256,768]{1,0:T(8,128)(2,1)} %get-tuple-element.106), channel_id=1, source_target_pairs={{0,4},{2,6},{4,0},{6,2},{8,12},{10,14},{12,8},{14,10},{16,20},{18,... | collective-permute-start | bytes 1179656 | tf_op jit(solution)/shard_map/ppermute | solution.py:137
  8.3 30.3 %collective-permute-start.5 = (bf16[256,768]{1,0:T(8,128)(2,1)}, bf16[256,768]{1,0:T(8,128)(2,1)S(1)}, u32[]{:S(2)}, u32[]{:S(2)}) collective-permute-start(bf16[256,768]{1,0:T(8,128)(2,1)} %get-tuple-element.107), channel_id=1, source_target_pairs={{0,6},{2,4},{4,2},{6,0},{8,14},{10,12},{12,10},{14,8},{16,22},{18,... | collective-permute-start | bytes 1179656 | tf_op jit(solution)/shard_map/ppermute | solution.py:137
  13.5 11.6 %collective-permute-start = (f32[16,16,128]{2,1,0:T(8,128)}, f32[16,16,128]{2,1,0:T(8,128)S(1)}, u32[]{:S(2)}, u32[]{:S(2)}) collective-permute-start(f32[16,16,128]{2,1,0:T(8,128)} %end_states.1), channel_id=1, source_target_pairs={{0,8},{2,10},{4,12},{6,14},{8,16},{10,18},{12,20},{14,22},{16,24},... | collective-permute-start | bytes 393224 | tf_op jit(solution)/shard_map/while/body/ppermute | solution.py:132
  38.6 11.7 %collective-permute-start.10 = (f32[2,16,16,128]{3,2,1,0:T(8,128)}, f32[2,16,16,128]{3,2,1,0:T(8,128)S(1)}, u32[]{:S(2)}, u32[]{:S(2)}) collective-permute-start(f32[2,16,16,128]{3,2,1,0:T(8,128)} %get-tuple-element.112), channel_id=1, source_target_pairs={{0,2},{2,0},{4,6},{6,4},{8,10},{10,8},{12,14},{14,12},{16,18},{18,... | collective-permute-start | bytes 786440 | tf_op jit(solution)/shard_map/ppermute | solution.py:137
  40.2 31.0 %collective-permute-start.7 = (bf16[256,768]{1,0:T(8,128)(2,1)}, bf16[256,768]{1,0:T(8,128)(2,1)}, u32[]{:S(2)}, u32[]{:S(2)}) collective-permute-start(bf16[256,768]{1,0:T(8,128)(2,1)} %get-tuple-element.110.refs_8_), channel_id=1, source_target_pairs={{0,8},{2,10},{4,12},{6,14},{8,0},{10,2},{12,4},{14,6},{16,24},{18,... | collective-permute-start | bytes 1179656 | tf_op jit(solution)/shard_map/ppermute | solution.py:137
  40.3 30.9 %collective-permute-start.9 = (bf16[256,768]{1,0:T(8,128)(2,1)}, bf16[256,768]{1,0:T(8,128)(2,1)S(1)}, u32[]{:S(2)}, u32[]{:S(2)}) collective-permute-start(bf16[256,768]{1,0:T(8,128)(2,1)} %get-tuple-element.110.refs_8_), channel_id=1, source_target_pairs={{8,16},{10,18},{12,20},{14,22},{16,8},{18,10},{20,12},{22,14},{9,1... | collective-permute-start | bytes 1179656 | tf_op jit(solution)/shard_map/ppermute | solution.py:303
  46.1 25.1 %collective-permute-start.6 = (bf16[256,768]{1,0:T(8,128)(2,1)}, bf16[256,768]{1,0:T(8,128)(2,1)}, u32[]{:S(2)}, u32[]{:S(2)}) collective-permute-start(bf16[256,768]{1,0:T(8,128)(2,1)} %collective-permute-done.3), channel_id=1, source_target_pairs={{0,16},{2,18},{4,20},{6,22},{8,24},{10,26},{12,28},{14,30},{16,0},... | collective-permute-start | bytes 1179656 | tf_op jit(solution)/shard_map/ppermute | solution.py:137
  46.2 25.0 %collective-permute-start.8 = (bf16[256,768]{1,0:T(8,128)(2,1)}, bf16[256,768]{1,0:T(8,128)(2,1)}, u32[]{:S(2)}, u32[]{:S(2)}) collective-permute-start(bf16[256,768]{1,0:T(8,128)(2,1)} %collective-permute-done.2.refs_12_), channel_id=1, source_target_pairs={{8,0},{10,2},{12,4},{14,6},{16,24},{18,26},{20,28},{22,30},{9,1},{... | collective-permute-start | bytes 1179656 | tf_op jit(solution)/shard_map/ppermute | solution.py:306
  71.3 37.6 %collective-permute-start.14 = (bf16[2,256,1024]{2,1,0:T(8,128)(2,1)}, bf16[2,256,1024]{2,1,0:T(8,128)(2,1)S(1)}, u32[]{:S(2)}, u32[]{:S(2)}) collective-permute-start(bf16[2,256,1024]{2,1,0:T(8,128)(2,1)} %gated_conv.1.refs_0_), channel_id=1, source_target_pairs={{0,2},{2,0},{4,6},{6,4},{8,10},{10,8},{12,14},{14,12},{16,18},{18,... | collective-permute-start | bytes 3145736 | tf_op jit(solution)/shard_map/ppermute | solution.py:137
  71.9 45.1 %collective-permute-start.15 = (bf16[2,256,1024]{2,1,0:T(8,128)(2,1)}, bf16[2,256,1024]{2,1,0:T(8,128)(2,1)S(1)}, u32[]{:S(2)}, u32[]{:S(2)}) collective-permute-start(bf16[2,256,1024]{2,1,0:T(8,128)(2,1)} %gated_conv.1.refs_0_), channel_id=1, source_target_pairs={{0,4},{2,6},{4,0},{6,2},{8,12},{10,14},{12,8},{14,10},{16,20},{18,... | collective-permute-start | bytes 3145736 | tf_op jit(solution)/shard_map/ppermute | solution.py:137
  73.4 45.1 %collective-permute-start.16 = (bf16[2,256,1024]{2,1,0:T(8,128)(2,1)}, bf16[2,256,1024]{2,1,0:T(8,128)(2,1)S(1)}, u32[]{:S(2)}, u32[]{:S(2)}) collective-permute-start(bf16[2,256,1024]{2,1,0:T(8,128)(2,1)} %gated_conv.1.refs_0_), channel_id=1, source_target_pairs={{0,6},{2,4},{4,2},{6,0},{8,14},{10,12},{12,10},{14,8},{16,22},{18,... | collective-permute-start | bytes 3145736 | tf_op jit(solution)/shard_map/ppermute | solution.py:137
  74.8 34.1 %collective-permute-start.12 = (bf16[512,768]{1,0:T(8,128)(2,1)}, bf16[512,768]{1,0:T(8,128)(2,1)S(1)}, u32[]{:S(2)}, u32[]{:S(2)}) collective-permute-start(bf16[512,768]{1,0:T(8,128)(2,1)} %pad_maximum_fusion.2), channel_id=1, source_target_pairs={{0,16},{2,18},{4,20},{6,22},{8,24},{10,26},{12,28},{14,30},{16,0},... | collective-permute-start | bytes 2359304 | tf_op jit(solution)/shard_map/ppermute | solution.py:137
  78.2 43.1 %collective-permute-start.13 = (bf16[768,768]{1,0:T(8,128)(2,1)S(1)}, bf16[768,768]{1,0:T(8,128)(2,1)S(1)}, u32[]{:S(2)}, u32[]{:S(2)}) collective-permute-start(bf16[768,768]{1,0:T(8,128)(2,1)S(1)} %pad_maximum_fusion.1.refs_9_), channel_id=1, source_target_pairs={{0,8},{2,10},{4,12},{6,14},{8,0},{10,2},{12,4},{14,6},{16,24},{18,... | collective-permute-start | bytes 3538952 | tf_op jit(solution)/shard_map/ppermute | solution.py:137
  108.9 12.4 %collective-permute-start.17 = (bf16[2,256,1024]{2,1,0:T(8,128)(2,1)}, bf16[2,256,1024]{2,1,0:T(8,128)(2,1)S(1)}, u32[]{:S(2)}, u32[]{:S(2)}) collective-permute-start(bf16[2,256,1024]{2,1,0:T(8,128)(2,1)} %gated_conv.1.refs_0_), channel_id=1, source_target_pairs={{0,1},{1,0},{2,3},{3,2},{4,5},{5,4},{6,7},{7,6},{8,9},{9,8},{10,11... | collective-permute-start | bytes 3145736 | tf_op jit(solution)/shard_map/ppermute | solution.py:137
  108.9 12.4 %collective-permute-start.18 = (bf16[2,256,1024]{2,1,0:T(8,128)(2,1)S(1)}, bf16[2,256,1024]{2,1,0:T(8,128)(2,1)S(1)}, u32[]{:S(2)}, u32[]{:S(2)}) collective-permute-start(bf16[2,256,1024]{2,1,0:T(8,128)(2,1)S(1)} %collective-permute-done.14.refs_1_), channel_id=1, source_target_pairs={{0,1},{1,0},{2,3},{3,2},{4,5},{5,4},{6,7},{7,6},{8,9},{9,8},{10,11... | collective-permute-start | bytes 3145736 | tf_op jit(solution)/shard_map/ppermute | solution.py:137
  122.3 22.1 %collective-permute-start.21 = (bf16[768,512]{1,0:T(8,128)(2,1)S(1)}, bf16[768,512]{1,0:T(8,128)(2,1)S(1)}, u32[]{:S(2)}, u32[]{:S(2)}) collective-permute-start(bf16[768,512]{1,0:T(8,128)(2,1)S(1)} %pad_maximum_fusion.3), channel_id=1, source_target_pairs={{8,0},{10,2},{12,4},{14,6},{16,24},{18,26},{20,28},{22,30},{9,1},{... | collective-permute-start | bytes 2359304 | tf_op jit(solution)/shard_map/ppermute | solution.py:306
  126.8 21.7 %collective-permute-start.22 = (bf16[768,512]{1,0:T(8,128)(2,1)}, bf16[768,512]{1,0:T(8,128)(2,1)S(1)}, u32[]{:S(2)}, u32[]{:S(2)}) collective-permute-start(bf16[768,512]{1,0:T(8,128)(2,1)} %slice.36), channel_id=1, source_target_pairs={{8,16},{10,18},{12,20},{14,22},{16,8},{18,10},{20,12},{22,14},{9,1... | collective-permute-start | bytes 2359304 | tf_op jit(solution)/shard_map/ppermute | solution.py:303
  149.6 14.2 %collective-permute-start.26 = (bf16[768,256]{1,0:T(8,128)(2,1)S(1)}, bf16[768,256]{1,0:T(8,128)(2,1)S(1)}, u32[]{:S(2)}, u32[]{:S(2)}) collective-permute-start(bf16[768,256]{1,0:T(8,128)(2,1)S(1)} %pad_maximum_fusion.4), channel_id=1, source_target_pairs={{8,0},{10,2},{12,4},{14,6},{16,24},{18,26},{20,28},{22,30},{9,1},{... | collective-permute-start | bytes 1179656 | tf_op jit(solution)/shard_map/ppermute | solution.py:306
  150.9 12.9 %collective-permute-start.27 = (bf16[768,256]{1,0:T(8,128)(2,1)S(1)}, bf16[768,256]{1,0:T(8,128)(2,1)S(1)}, u32[]{:S(2)}, u32[]{:S(2)}) collective-permute-start(bf16[768,256]{1,0:T(8,128)(2,1)S(1)} %copy-done.24), channel_id=1, source_target_pairs={{8,16},{10,18},{12,20},{14,22},{16,8},{18,10},{20,12},{22,14},{9,1... | collective-permute-start | bytes 1179656 | tf_op jit(solution)/shard_map/ppermute | solution.py:303
  160.2 12.8 %collective-permute-start.23 = (bf16[256,512]{1,0:T(8,128)(2,1)}, bf16[256,512]{1,0:T(8,128)(2,1)S(1)}, u32[]{:S(2)}, u32[]{:S(2)}) collective-permute-start(bf16[256,512]{1,0:T(8,128)(2,1)} %get-tuple-element.149), channel_id=1, source_target_pairs={{0,2},{2,0},{4,6},{6,4},{8,10},{10,8},{12,14},{14,12},{16,18},{18,... | collective-permute-start | bytes 786440 | tf_op jit(solution)/shard_map/ppermute | solution.py:137
  161.3 12.7 %collective-permute-start.24 = (bf16[256,512]{1,0:T(8,128)(2,1)}, bf16[256,512]{1,0:T(8,128)(2,1)S(1)}, u32[]{:S(2)}, u32[]{:S(2)}) collective-permute-start(bf16[256,512]{1,0:T(8,128)(2,1)} %get-tuple-element.150), channel_id=1, source_target_pairs={{0,4},{2,6},{4,0},{6,2},{8,12},{10,14},{12,8},{14,10},{16,20},{18,... | collective-permute-start | bytes 786440 | tf_op jit(solution)/shard_map/ppermute | solution.py:137
  162.8 12.6 %collective-permute-start.25 = (bf16[256,512]{1,0:T(8,128)(2,1)}, bf16[256,512]{1,0:T(8,128)(2,1)S(1)}, u32[]{:S(2)}, u32[]{:S(2)}) collective-permute-start(bf16[256,512]{1,0:T(8,128)(2,1)} %get-tuple-element.151), channel_id=1, source_target_pairs={{0,6},{2,4},{4,2},{6,0},{8,14},{10,12},{12,10},{14,8},{16,22},{18,... | collective-permute-start | bytes 786440 | tf_op jit(solution)/shard_map/ppermute | solution.py:137
  (34 other events, 362.2 us)

commit v7 on v6

--- a/solution.py
+++ b/solution.py
@@ -167,6 +167,36 @@
     return lax.fori_loop(0, once, run, empty)
 
 
+def pack(sources, recipes):
+    shapes = [(sum(part[1].stop - part[1].start for part in recipe), recipe[0][3]) for recipe in recipes]
+    moves = []
+    for out, recipe in enumerate(recipes):
+        row = 0
+        for source, span, col, cols in recipe:
+            moves.append((source, span.start, span.stop - span.start, col, cols, out, row))
+            row += span.stop - span.start
+
+    def kernel(*refs):
+        in_refs, out_refs, sems = refs[: len(sources)], refs[len(sources) : -1], refs[-1]
+        copies = []
+        for n, (source, first, count, col, cols, out, row) in enumerate(moves):
+            block = in_refs[source].at[pl.ds(first, count), pl.ds(col, cols)]
+            copies.append(pltpu.make_async_copy(block, out_refs[out].at[pl.ds(row, count), :], sems.at[n]))
+            copies[-1].start()
+        for copy in copies:
+            copy.wait()
+
+    return pl.pallas_call(
+        kernel,
+        in_specs=[pl.BlockSpec(memory_space=pl.ANY)] * len(sources),
+        out_specs=[pl.BlockSpec(memory_space=pltpu.VMEM)] * len(recipes),
+        out_shape=[jax.ShapeDtypeStruct(shape, sources[0].dtype) for shape in shapes],
+        scratch_shapes=[pltpu.SemaphoreType.DMA((len(moves),))],
+        compiler_params=pltpu.CompilerParams(vmem_limit_bytes=VMEM_BYTES),
+        name="pack",
+    )(*sources)
+
+
 def product(flags, places, ours, theirs, blocks, accs, widths, out_dtype):
     _, rows, depth = ours[0].shape
     chunk = depth // PLANE
@@ -181,45 +211,53 @@
         acc_refs, out_refs = refs[: len(accs)], refs[len(accs) : len(accs) + PLANE * len(widths)]
         gated_buf, weight_buf, gated_sems, weight_sems = refs[-4:]
 
-        def target(b, r):
-            start = pl.multiple_of(b * depth + place_ref[r] * chunk, chunk)
-            return weight_buf.at[pl.ds(start, chunk), :]
+        step = chunk // 2
+
+        def target(b, at):
+            start = pl.multiple_of(b * depth + place_ref[at // chunk] * chunk + at % chunk, step)
+            return weight_buf.at[pl.ds(start, step), :]
 
         for b, (flag, pick, pieces) in enumerate(blocks):
-            for choices, first, chunks, col in pieces:
+            row = 0
+            for choices, col in pieces:
                 for c in range(len(choices)):
                     ref = weight_refs.pop(0)
-                    for r in range(first, first + chunks):
-                        source = ref.at[pl.ds((r - first) * chunk, chunk), pl.ds(col, cols)]
-                        copy = pltpu.make_async_copy(source, target(b, r), weight_sems.at[b])
+                    for at in range(0, ref.shape[0], step):
+                        source = ref.at[pl.ds(at, step), pl.ds(col, cols)]
+                        copy = pltpu.make_async_copy(source, target(b, row + at), weight_sems.at[b])
                         if pick is None:
                             copy.start()
                         else:
                             pl.when(flag_ref[pick] == c)(copy.start)
+                row += choices[0].shape[0]
             half = flag_ref[flag] & 1
             for r in range(PLANE):
                 for c, refs_of in enumerate((our_refs, their_refs)):
-                    copy = pltpu.make_async_copy(refs_of[r].at[half], gated_buf.at[b, r], gated_sems.at[b, r])
+                    target_rows = gated_buf.at[b, pl.ds(r * rows, rows), :]
+                    copy = pltpu.make_async_copy(refs_of[r].at[half], target_rows, gated_sems.at[b])
                     pl.when(flag_ref[flag] // 2 == c)(copy.start)
         for b in range(count):
             block = weight_buf.at[pl.ds(b * depth, depth), :]
             pltpu.make_async_copy(block, block, weight_sems.at[b]).wait()
-            for r in range(PLANE):
-                pltpu.make_async_copy(our_refs[r].at[0], gated_buf.at[b, r], gated_sems.at[b, r]).wait()
-                first = 0
-                for part, width in enumerate(widths):
-                    at = part * PLANE + r
-                    total = jnp.dot(
-                        gated_buf[b, r],
-                        weight_buf[pl.ds(b * depth, depth), pl.ds(first, width)],
+            pltpu.make_async_copy(gated_buf.at[b], gated_buf.at[b], gated_sems.at[b]).wait()
+            first = 0
+            for part, width in enumerate(widths):
+                for col in range(0, width, 2 * LANES):
+                    here = pl.ds(col, 2 * LANES)
+                    made = jnp.dot(
+                        gated_buf[b],
+                        weight_buf[pl.ds(b * depth, depth), pl.ds(first + col, 2 * LANES)],
                         preferred_element_type=jnp.float32,
                     )
-                    if b:
-                        total = total + out_refs[at][...]
-                    elif accs:
-                        total = total + acc_refs[at][...]
-                    out_refs[at][...] = total.astype(out_dtype)
-                    first += width
+                    for r in range(PLANE):
+                        at = part * PLANE + r
+                        total = made[r * rows : (r + 1) * rows]
+                        if b:
+                            total = total + out_refs[at][:, here]
+                        elif accs:
+                            total = total + acc_refs[at][:, here]
+                        out_refs[at][:, here] = total.astype(out_dtype)
+                first += width
 
     smem = pl.BlockSpec(memory_space=pltpu.SMEM)
     vmem = pl.BlockSpec(memory_space=pltpu.VMEM)
@@ -230,9 +268,9 @@
         out_specs=[vmem] * (PLANE * len(widths)),
         out_shape=[jax.ShapeDtypeStruct((rows, width), out_dtype) for width in widths for _ in range(PLANE)],
         scratch_shapes=[
-            pltpu.VMEM((count, PLANE, rows, depth), jnp.bfloat16),
+            pltpu.VMEM((count, PLANE * rows, depth), jnp.bfloat16),
             pltpu.VMEM((count * depth, cols), jnp.bfloat16),
-            pltpu.SemaphoreType.DMA((count, PLANE)),
+            pltpu.SemaphoreType.DMA((count,)),
             pltpu.SemaphoreType.DMA((count,)),
         ],
         compiler_params=pltpu.CompilerParams(vmem_limit_bytes=VMEM_BYTES),
@@ -317,13 +355,24 @@
 
     own = [lax.dynamic_slice_in_dim(w_out, (spot ^ r) * cols, cols, axis=1) for r in range(PLANE)]
     w0, w1, w2, w3 = tie(*own)
-    f0 = far(w0)
     w1, w2, w3 = [exchange(w, "ctx", r + 1) for r, w in enumerate((w1, w2, w3))]
     pair = box(line_scan, k, v, rate, speed)
-    f0, w0, w1, w2, w3, pair = tie(f0, w0, w1, w2, w3, pair)
-
-    f1, n0 = far(w1), near(w0)
-    out0, mid0 = outward(f0), across(w0)
+    w0, w1, w2, w3, pair = tie(w0, w1, w2, w3, pair)
+
+    half = chunk // 2
+    every, upper, lower = slice(0, chunk), slice(0, half), slice(half, chunk)
+    head, tail, tail1, tail2, midA, midB = pack(
+        [w0, w1, w2, w3],
+        [
+            [(0, every, 0, cols), (1, upper, 0, cols)],
+            [(1, lower, 0, cols), (2, every, 0, cols), (3, every, 0, cols)],
+            [(1, lower, 0, cols), (2, every, 0, cols), (3, upper, 0, cols)],
+            [(3, lower, 0, cols)],
+            [(r, every, 0, wide) for r in range(PLANE)],
+            [(r, every, wide, cols - wide) for r in range(PLANE)],
+        ],
+    )
+    f0, n0 = far(head), near(head)
     x_later, y_later = (spot & 1) != 0, (spot & 2) != 0
     other = exchange(pair, "ctx", 1)
     both = jnp.where(x_later, fade(float(rows)) * other + pair, fade(float(rows)) * pair + other)
@@ -333,14 +382,15 @@
     line = jnp.where(y_later, fade(2.0 * rows) * other[1] + both[1], fade(2.0 * rows) * both[1] + other[1])
     enter = before + fade((spot * rows).astype(jnp.float32)) * line
     gated = gated_conv(q, k, v, rate, residue, skip, enter)
-    rest, last_two = jnp.concatenate([w1, w2, w3]), jnp.concatenate([w2, w3])
-    f1, n0, out0, mid0, gated, rest, last_two = tie(f1, n0, out0, mid0, gated, rest, last_two)
-
-    f23, nr = far(last_two), near(rest)
+    f0, n0, tail, tail1, tail2, midA, midB, gated = tie(f0, n0, tail, tail1, tail2, midA, midB, gated)
+
+    f1, n1 = far(tail1), near(tail)
     ours = [gated] + [exchange(gated, "ctx", r) for r in range(1, PLANE)]
+    f1, n1, tail2, midA, midB, *ours = tie(f1, n1, tail2, midA, midB, *ours)
+
+    f2 = far(tail2)
     theirs = [exchange(x, "ch", 1) for x in ours]
-    midA, midB = rest[:, :wide], rest[:, wide:]
-    f23, nr, midA, midB, *held = tie(f23, nr, midA, midB, *ours, *theirs)
+    f0, f1, f2, midA, midB, *held = tie(f0, f1, f2, midA, midB, *ours, *theirs)
     ours, theirs = held[:PLANE], held[PLANE:]
 
     def source_of(b):
@@ -350,21 +400,29 @@
     flags = jnp.stack([source_of(plane ^ r) for r in range(4)] + [is_middle]).astype(jnp.int32)
     places = jnp.stack([spot ^ r for r in range(PLANE)]).astype(jnp.int32)
 
-    outA, midA = outward(jnp.concatenate([f1[:, :wide], f23[:, :wide]])), across(midA)
+    full = [slice(0, x.shape[0]) for x in (f0, f1, f2)]
+    outA, outB = pack(
+        [f0, f1, f2],
+        [
+            [(n, span, 0, wide) for n, span in enumerate(full)],
+            [(n, span, wide, cols - wide) for n, span in enumerate(full)],
+        ],
+    )
+    outA, midA = outward(outA), across(midA)
     blocks = [
-        (0, None, [((w0,), 0, 1, 0), ((rest,), 1, 3, 0)]),
-        (1, None, [((n0,), 0, 1, 0), ((nr,), 1, 3, 0)]),
-        (2, None, [((f0,), 0, 1, 0), ((f1,), 1, 1, 0), ((f23,), 2, 2, 0)]),
+        (0, None, [((w,), 0) for w in (w0, w1, w2, w3)]),
+        (1, None, [((n0,), 0), ((n1,), 0)]),
+        (2, None, [((f0,), 0), ((f1,), 0), ((f2,), 0)]),
     ]
     accA, accB = product(flags, places, ours, theirs, blocks, None, widths, jnp.float32)
-    outA, midA, f1, f23, midB, *accs = tie(outA, midA, f1, f23, midB, *accA, *accB)
+    outA, midA, outB, midB, *accs = tie(outA, midA, outB, midB, *accA, *accB)
     accA, accB = accs[:PLANE], accs[PLANE:]
 
-    outB, midB = outward(jnp.concatenate([f1[:, wide:], f23[:, wide:]])), across(midB)
-    blocks = [(3, 4, [((out0, mid0), 0, 1, 0), ((outA, midA), 1, 3, 0)])]
+    outB, midB = outward(outB), across(midB)
+    blocks = [(3, 4, [((outA, midA), 0)])]
     (madeA,) = product(flags, places, ours, theirs, blocks, accA, widths[:1], jnp.bfloat16)
     backA = [madeA[0]] + [exchange(madeA[r], "ctx", r) for r in range(1, PLANE)]
-    blocks = [(3, 4, [((out0, mid0), 0, 1, wide), ((outB, midB), 1, 3, 0)])]
+    blocks = [(3, 4, [((outB, midB), 0)])]
     (madeB,) = product(flags, places, ours, theirs, blocks, accB, widths[1:], jnp.bfloat16)
     backB = [madeB[0]] + [exchange(madeB[r], "ctx", r) for r in range(1, PLANE)]
     return assemble(places, [backA, backB])
@@ -381,7 +439,7 @@
         and cores == 2
         and chan == 8 * chunk
         and chunk % LANES == 0
-        and feats % (PLANE * LANES) == 0
+        and feats % (6 * PLANE * LANES) == 0
     )
     skip = skip.reshape(groups, LANES)
     if split:

time: 183 us -> 188 us (1.027)
  waiting for transfers between devices: 71.8 us -> 82.7 us
  starting transfers between devices: 53.5 us -> 48.1 us
  Pallas kernels: 37.7 us -> 42 us
  local copies, waits for them, and re-layouts: 11.1 us -> 8.17 us
    ppermute x23, waiting for transfers between devices: 52.1 us -> 61.9 us  [exchange(): return lax.ppermute(x, axis, [(i, i ^ flip) for i in range(count)])]
    ppermute x2, waiting for transfers between devices: 15.4 us -> 7.42 us  [shift_ctx(): return lax.ppermute(x, 'ctx', [(i, i + by) for i in range(count - by)])]
    pallas_call x0 -> x2, Pallas kernels: none -> 7.03 us  [pack(): pl.pallas_call(kernel, in_specs=[pl.BlockSpec(memory_space=pl.ANY)] * len...]
    ppermute x3 -> x2, waiting for transfers between devices: 0.01 us -> 5.35 us  [outward(): return lax.ppermute(x, 'ctx', [(i, i ^ PLANE) for i in middle])]
    ppermute x3 -> x2, starting transfers between devices: 9.89 us -> 4.58 us  [outward(): return lax.ppermute(x, 'ctx', [(i, i ^ PLANE) for i in middle])]
    ppermute x3 -> x2, starting transfers between devices: 12.7 us -> 8.19 us  [across(): return lax.ppermute(x, 'ctx', [(i, i ^ 3 * PLANE) for i in middle])]
    ppermute x3 -> x2, waiting for transfers between devices: 4.16 us -> 8.06 us  [across(): return lax.ppermute(x, 'ctx', [(i, i ^ 3 * PLANE) for i in middle])]
    slice x7 -> x0, local copies, waits for them, and re-layouts: 3.82 us -> none  [the longest x2 1.79 us: split_block(): midA, midB = (rest[:, :wide], rest[:, wide:])]
  transfers between devices with their start and end apart: 31 -> 29, of which waited for: 11 -> 15; matrix products, arithmetic and copies ran while one was open for 6% -> 4% of each run, Pallas kernels for 20% -> 20%
where the time goes in v7:
time: 188 us; the launch traced here: 187 us
  waiting for transfers between devices  82.7 us (44%)
  starting transfers between devices  48.1 us (26%)
  Pallas kernels  42 us (22%)
  local copies, waits for them, and re-layouts  8.17 us (4%)
  other arithmetic  5.63 us (3%)
    ppermute x23, waiting for transfers between devices, exchange(): return lax.ppermute(x, axis, [(i, i ^ flip) for i in range(count)])  61.9 us
    ppermute x23, starting transfers between devices, exchange(): return lax.ppermute(x, axis, [(i, i ^ flip) for i in range(count)])  27.4 us
    pallas_call x3, Pallas kernels, product(): pl.pallas_call(kernel, in_specs=[smem, smem] + [anywhere] * (2 * PLANE +...  20.9 us
    pallas_call x1, Pallas kernels, gated_conv(): pl.pallas_call(conv_kernel, grid=(chan // width,), in_specs=[wide, wide,...  8.38 us
    ppermute x2, starting transfers between devices, across(): return lax.ppermute(x, 'ctx', [(i, i ^ 3 * PLANE) for i in middle])  8.19 us
    ppermute x2, waiting for transfers between devices, across(): return lax.ppermute(x, 'ctx', [(i, i ^ 3 * PLANE) for i in middle])  8.06 us
    ppermute x2, starting transfers between devices, shift_ctx(): return lax.ppermute(x, 'ctx', [(i, i + by) for i in range(count - by)])  7.97 us
    ppermute x2, waiting for transfers between devices, shift_ctx(): return lax.ppermute(x, 'ctx', [(i, i + by) for i in range(count - by)])  7.42 us
  transfers between devices with their start and end apart: 29, of which 15 were waited for; matrix products, arithmetic and copies ran while one was open for 4% of the time, Pallas kernels for 20%

profile of v7, /device:TPU:8, one launch (start us, length us, event | category | flops | bytes accessed | tf_op | source)
XLA Modules:
  0.0 187.0 jit_solution(7514731906788650421)
XLA Ops:
  0.0 2.7 %constant_dynamic-slice_fusion = (bf16[256,768]{1,0:T(8,128)(2,1)}, bf16[256,768]{1,0:T(8,128)(2,1)}, bf16[256,768]{1,0:T(8,128)(2,1)}, bf16[256,768]{1,0:T(8,128)(2,1)}) fusion(bf16[256,3072]{1,0:T(8,128)(2,1)} %param.15, s32[]{:T(128)S(6)} %select_n.89, s32[]{:T(128)S(6)} %select_n.87, s32[]{:T(128)S(6)} %select_n.86, s32[]{:T(128)S(6)} %select_n.88), kind=kLoop, calls=%fused_computation.15 | loop fusion | bytes 3145744 | tf_op jit(solution)/shard_map/dynamic_slice | solution.py:356
  7.0 22.0 %while.10 = (s32[]{:T(128)}, f32[2,16,16,128]{3,2,1,0:T(8,128)}, s32[]{:T(128)}, bf16[256,2048]{1,0:T(8,128)(2,1)S(1)}, bf16[256,2048]{1,0:T(8,128)(2,1)S(1)}, /...) while((s32[]{:T(128)}, f32[2,16,16,128]{3,2,1,0:T(8,128)}, s32[]{:T(128)}, ...), condition=%wide.region_1.2_spmd, body=%wide.region_0.1_spmd.sunk | while | flops 17104896 | bytes 4718757 | solution.py:167
  7.0 3.9 %end_states.1 = f32[16,16,128]{2,1,0:T(8,128)} custom-call(bf16[256,2048]{1,0:T(8,128)(2,1)S(1)} %get-tuple-element.261.k_ref, bf16[256,2048]{1,0:T(8,128)(2,1)S(1)} %get-tuple-element.262.v_ref, f32[16,2048]{1,0:T(8,128)S(1)} %get-tuple-element.263.rate_ref), custom_call_target="tpu_custom_call" | custom-call | flops 16777216 | bytes 2097152 | tf_op jit(solution)/shard_map/while/body/end_states/pallas_call | solution.py:90
  10.9 3.5 %collective-permute-start = (f32[16,16,128]{2,1,0:T(8,128)}, f32[16,16,128]{2,1,0:T(8,128)S(1)}, u32[]{:S(2)}, u32[]{:S(2)}) collective-permute-start(f32[16,16,128]{2,1,0:T(8,128)} %end_states.1), channel_id=1, source_target_pairs={{0,8},{2,10},{4,12},{6,14},{8,16},{10,18},{12,20},{14,22},{16,24},... | collective-permute-start | bytes 393224 | tf_op jit(solution)/shard_map/while/body/ppermute | solution.py:132
  14.4 3.6 %collective-permute-done = f32[16,16,128]{2,1,0:T(8,128)S(1)} collective-permute-done((f32[16,16,128]{2,1,0:T(8,128)}, f32[16,16,128]{2,1,0:T(8,128)S(1)}, u32[]{:S(2)}, u32[]{:S(2)}) %collective-permute-start) | collective-permute-done | bytes 131104 | tf_op jit(solution)/shard_map/while/body/ppermute | solution.py:132
  18.9 4.5 %collective-permute-start.1 = (f32[16,16,128]{2,1,0:T(8,128)S(1)}, f32[16,16,128]{2,1,0:T(8,128)S(1)}, u32[]{:S(2)}, u32[]{:S(2)}) collective-permute-start(f32[16,16,128]{2,1,0:T(8,128)S(1)} %multiply_add_fusion.2), channel_id=1, source_target_pairs={{0,16},{2,18},{4,20},{6,22},{8,24},{10,26},{12,28},{14,30},{1,17},... | collective-permute-start | bytes 393224 | tf_op jit(solution)/shard_map/while/body/ppermute | solution.py:132
  23.4 3.8 %collective-permute-done.1 = f32[16,16,128]{2,1,0:T(8,128)S(1)} collective-permute-done((f32[16,16,128]{2,1,0:T(8,128)S(1)}, f32[16,16,128]{2,1,0:T(8,128)S(1)}, u32[]{:S(2)}, u32[]{:S(2)}) %collective-permute-start.1) | collective-permute-done | bytes 131104 | tf_op jit(solution)/shard_map/while/body/ppermute | solution.py:132
  30.5 4.5 %pack.2 = (bf16[384,768]{1,0:T(8,128)(2,1)}, bf16[640,768]{1,0:T(8,128)(2,1)}, bf16[512,768]{1,0:T(8,128)(2,1)}, bf16[128,768]{1,0:T(8,128)(2,1)}, bf16[1024,512]{1,0:T(8,128)(2,1)}, /*index=5*/bf16[1024,256]{1,0:T(8,128)(2,1)}) custom-call(bf16[256,768]{1,0:T(8,128)(2,1)} %get-tuple-element.126.refs_0_.refs_8_, bf16[256,768]{1,0:T(8,128)(2,1)} %copy-done.18, ...), custom_call_target="tpu_custom_call" | custom-call | tf_op jit(solution)/shard_map/pack/pallas_call | solution.py:189
  35.1 3.4 %collective-permute-start.5 = (bf16[384,768]{1,0:T(8,128)(2,1)}, bf16[384,768]{1,0:T(8,128)(2,1)S(1)}, u32[]{:S(2)}, u32[]{:S(2)}) collective-permute-start(bf16[384,768]{1,0:T(8,128)(2,1)} %get-tuple-element.130), channel_id=1, source_target_pairs={{0,16},{2,18},{4,20},{6,22},{8,24},{10,26},{12,28},{14,30},{16,0},... | collective-permute-start | bytes 1769480 | tf_op jit(solution)/shard_map/ppermute | solution.py:137
  40.9 5.1 %collective-permute-done.8 = f32[2,16,16,128]{3,2,1,0:T(8,128)S(1)} collective-permute-done((f32[2,16,16,128]{3,2,1,0:T(8,128)}, f32[2,16,16,128]{3,2,1,0:T(8,128)S(1)}, u32[]{:S(2)}, u32[]{:S(2)}) %collective-permute-start.8) | collective-permute-done | bytes 262176 | tf_op jit(solution)/shard_map/ppermute | solution.py:137
  47.6 8.4 %gated_conv.1.refs_0_ = bf16[2,256,1024]{2,1,0:T(8,128)(2,1)} custom-call(bf16[256,2048]{1,0:T(8,128)(2,1)} %q_ref.1, bf16[256,2048]{1,0:T(8,128)(2,1)S(1)} %get-tuple-element.295, bf16[256,2048]{1,0:T(8,128)(2,1)S(1)} %get-tuple-element.296, f32[16,2048]{1,0:T(8,128)S(1)} %get-tuple-element.304, f32[16,2048]{1,0:T(8,128)} %residue_ref.1, ...), custom_call_target="tpu_custom_call" | custom-call | flops 33554432 | bytes 4194304 | tf_op jit(solution)/shard_map/gated_conv/pallas_call | solution.py:115
  57.9 3.8 %collective-permute-done.5.refs_0_.refs_14_ = bf16[384,768]{1,0:T(8,128)(2,1)S(1)} collective-permute-done((bf16[384,768]{1,0:T(8,128)(2,1)}, bf16[384,768]{1,0:T(8,128)(2,1)S(1)}, u32[]{:S(2)}, u32[]{:S(2)}) %collective-permute-start.5) | collective-permute-done | bytes 589856 | tf_op jit(solution)/shard_map/ppermute | solution.py:137
  67.9 34.5 %collective-permute-done.9.refs_1_.refs_15_ = bf16[512,768]{1,0:T(8,128)(2,1)S(1)} collective-permute-done((bf16[512,768]{1,0:T(8,128)(2,1)}, bf16[512,768]{1,0:T(8,128)(2,1)S(1)}, u32[]{:S(2)}, u32[]{:S(2)}) %collective-permute-start.9) | collective-permute-done | bytes 786464 | tf_op jit(solution)/shard_map/ppermute | solution.py:137
  102.4 4.0 %collective-permute-done.12.refs_2_ = bf16[2,256,1024]{2,1,0:T(8,128)(2,1)S(1)} collective-permute-done((bf16[2,256,1024]{2,1,0:T(8,128)(2,1)}, bf16[2,256,1024]{2,1,0:T(8,128)(2,1)S(1)}, u32[]{:S(2)}, u32[]{:S(2)}) %collective-permute-start.12) | collective-permute-done | bytes 1048608 | tf_op jit(solution)/shard_map/ppermute | solution.py:137
  107.5 3.0 %collective-permute-start.14 = (bf16[128,768]{1,0:T(8,128)(2,1)S(1)}, bf16[128,768]{1,0:T(8,128)(2,1)S(1)}, u32[]{:S(2)}, u32[]{:S(2)}) collective-permute-start(bf16[128,768]{1,0:T(8,128)(2,1)S(1)} %copy-done.21), channel_id=1, source_target_pairs={{0,16},{2,18},{4,20},{6,22},{8,24},{10,26},{12,28},{14,30},{16,0},... | collective-permute-start | bytes 589832 | tf_op jit(solution)/shard_map/ppermute | solution.py:137
  110.5 7.6 %collective-permute-done.14.refs_2_.refs_16_ = bf16[128,768]{1,0:T(8,128)(2,1)S(1)} collective-permute-done((bf16[128,768]{1,0:T(8,128)(2,1)S(1)}, bf16[128,768]{1,0:T(8,128)(2,1)S(1)}, u32[]{:S(2)}, u32[]{:S(2)}) %collective-permute-start.14) | collective-permute-done | bytes 196640 | tf_op jit(solution)/shard_map/ppermute | solution.py:137
  123.0 3.3 %collective-permute-start.19 = (bf16[1024,512]{1,0:T(8,128)(2,1)}, bf16[1024,512]{1,0:T(8,128)(2,1)S(1)}, u32[]{:S(2)}, u32[]{:S(2)}) collective-permute-start(bf16[1024,512]{1,0:T(8,128)(2,1)} %get-tuple-element.163), channel_id=1, source_target_pairs={{8,0},{10,2},{12,4},{14,6},{16,24},{18,26},{20,28},{22,30},{9,1},{... | collective-permute-start | bytes 3145736 | tf_op jit(solution)/shard_map/ppermute | solution.py:344
  126.3 4.6 %collective-permute-start.20 = (bf16[1024,512]{1,0:T(8,128)(2,1)}, bf16[1024,512]{1,0:T(8,128)(2,1)}, u32[]{:S(2)}, u32[]{:S(2)}) collective-permute-start(bf16[1024,512]{1,0:T(8,128)(2,1)} %get-tuple-element.164), channel_id=1, source_target_pairs={{8,16},{10,18},{12,20},{14,22},{16,8},{18,10},{20,12},{22,14},{9,1... | collective-permute-start | bytes 3145736 | tf_op jit(solution)/shard_map/ppermute | solution.py:341
  132.2 11.0 %product.3 = (f32[256,512]{1,0:T(8,128)}, f32[256,512]{1,0:T(8,128)}, f32[256,512]{1,0:T(8,128)}, f32[256,512]{1,0:T(8,128)}, f32[256,256]{1,0:T(8,128)}, /*inde...) custom-call(s32[5]{0:T(128)} %stack.52.flag_ref, s32[4]{0:T(128)} %pad_add_fusion.place_ref, ...), custom_call_target="tpu_custom_call" | custom-call | flops 4831838208 | bytes 11010048 | tf_op jit(solution)/shard_map/product/pallas_call | solution.py:265
  143.2 5.3 %collective-permute-done.19.refs_8_ = bf16[1024,512]{1,0:T(8,128)(2,1)S(1)} collective-permute-done((bf16[1024,512]{1,0:T(8,128)(2,1)}, bf16[1024,512]{1,0:T(8,128)(2,1)S(1)}, u32[]{:S(2)}, u32[]{:S(2)}) %collective-permute-start.19) | collective-permute-done | bytes 1048608 | tf_op jit(solution)/shard_map/ppermute | solution.py:344
  148.5 5.7 %collective-permute-done.20.refs_9_ = bf16[1024,512]{1,0:T(8,128)(2,1)} collective-permute-done((bf16[1024,512]{1,0:T(8,128)(2,1)}, bf16[1024,512]{1,0:T(8,128)(2,1)}, u32[]{:S(2)}, u32[]{:S(2)}) %collective-permute-start.20) | collective-permute-done | bytes 1048608 | tf_op jit(solution)/shard_map/ppermute | solution.py:341
  155.6 3.6 %collective-permute-start.25 = (bf16[1024,256]{1,0:T(8,128)(2,1)}, bf16[1024,256]{1,0:T(8,128)(2,1)S(1)}, u32[]{:S(2)}, u32[]{:S(2)}) collective-permute-start(bf16[1024,256]{1,0:T(8,128)(2,1)} %get-tuple-element.188), channel_id=1, source_target_pairs={{8,16},{10,18},{12,20},{14,22},{16,8},{18,10},{20,12},{22,14},{9,1... | collective-permute-start | bytes 1572872 | tf_op jit(solution)/shard_map/ppermute | solution.py:341
  159.2 5.5 %product.4 = (bf16[256,512]{1,0:T(8,128)(2,1)}, bf16[256,512]{1,0:T(8,128)(2,1)}, bf16[256,512]{1,0:T(8,128)(2,1)}, bf16[256,512]{1,0:T(8,128)(2,1)}) custom-call(s32[5]{0:T(128)} %stack.52.flag_ref, s32[4]{0:T(128)} %pad_add_fusion.place_ref, bf16[2,256,1024]{2,1,0:T(8,128)(2,1)} %gated_conv.1.refs_0_, bf16[2,256,1024]{2,1,0:T(8,128)(2,1)} %copy-done.8, ...), custom_call_target="tpu_custom_call" | custom-call | flops 1073741824 | bytes 3145728 | tf_op jit(solution)/shard_map/product/pallas_call | solution.py:265
  171.5 4.3 %product.5 = (bf16[256,256]{1,0:T(8,128)(2,1)}, bf16[256,256]{1,0:T(8,128)(2,1)}, bf16[256,256]{1,0:T(8,128)(2,1)}, bf16[256,256]{1,0:T(8,128)(2,1)}) custom-call(s32[5]{0:T(128)} %stack.52.flag_ref, s32[4]{0:T(128)} %pad_add_fusion.place_ref, bf16[2,256,1024]{2,1,0:T(8,128)(2,1)} %gated_conv.1.refs_0_, bf16[2,256,1024]{2,1,0:T(8,128)(2,1)} %copy-done.8, ...), custom_call_target="tpu_custom_call" | custom-call | flops 536870912 | bytes 2621440 | tf_op jit(solution)/shard_map/product/pallas_call | solution.py:265
  (98 shorter events, 46.9 us)
Async XLA Ops:
  2.7 26.2 %collective-permute-start.2 = (bf16[256,768]{1,0:T(8,128)(2,1)}, bf16[256,768]{1,0:T(8,128)(2,1)S(1)}, u32[]{:S(2)}, u32[]{:S(2)}) collective-permute-start(bf16[256,768]{1,0:T(8,128)(2,1)} %get-tuple-element.122), channel_id=1, source_target_pairs={{0,2},{2,0},{4,6},{6,4},{8,10},{10,8},{12,14},{14,12},{16,18},{18,... | collective-permute-start | bytes 1179656 | tf_op jit(solution)/shard_map/ppermute | solution.py:137
  4.2 24.7 %collective-permute-start.3 = (bf16[256,768]{1,0:T(8,128)(2,1)}, bf16[256,768]{1,0:T(8,128)(2,1)}, u32[]{:S(2)}, u32[]{:S(2)}) collective-permute-start(bf16[256,768]{1,0:T(8,128)(2,1)} %get-tuple-element.123), channel_id=1, source_target_pairs={{0,4},{2,6},{4,0},{6,2},{8,12},{10,14},{12,8},{14,10},{16,20},{18,... | collective-permute-start | bytes 1179656 | tf_op jit(solution)/shard_map/ppermute | solution.py:137
  5.7 23.2 %collective-permute-start.4 = (bf16[256,768]{1,0:T(8,128)(2,1)}, bf16[256,768]{1,0:T(8,128)(2,1)}, u32[]{:S(2)}, u32[]{:S(2)}) collective-permute-start(bf16[256,768]{1,0:T(8,128)(2,1)} %get-tuple-element.124), channel_id=1, source_target_pairs={{0,6},{2,4},{4,2},{6,0},{8,14},{10,12},{12,10},{14,8},{16,22},{18,... | collective-permute-start | bytes 1179656 | tf_op jit(solution)/shard_map/ppermute | solution.py:137
  18.9 8.3 %collective-permute-start.1 = (f32[16,16,128]{2,1,0:T(8,128)S(1)}, f32[16,16,128]{2,1,0:T(8,128)S(1)}, u32[]{:S(2)}, u32[]{:S(2)}) collective-permute-start(f32[16,16,128]{2,1,0:T(8,128)S(1)} %multiply_add_fusion.2), channel_id=1, source_target_pairs={{0,16},{2,18},{4,20},{6,22},{8,24},{10,26},{12,28},{14,30},{1,17},... | collective-permute-start | bytes 393224 | tf_op jit(solution)/shard_map/while/body/ppermute | solution.py:132
  28.9 9.7 %collective-permute-start.7 = (f32[2,16,16,128]{3,2,1,0:T(8,128)}, f32[2,16,16,128]{3,2,1,0:T(8,128)S(1)}, u32[]{:S(2)}, u32[]{:S(2)}) collective-permute-start(f32[2,16,16,128]{3,2,1,0:T(8,128)} %get-tuple-element.136), channel_id=1, source_target_pairs={{0,2},{2,0},{4,6},{6,4},{8,10},{10,8},{12,14},{14,12},{16,18},{18,... | collective-permute-start | bytes 786440 | tf_op jit(solution)/shard_map/ppermute | solution.py:137
  35.1 22.8 %collective-permute-start.6 = (bf16[384,768]{1,0:T(8,128)(2,1)}, bf16[384,768]{1,0:T(8,128)(2,1)}, u32[]{:S(2)}, u32[]{:S(2)}) collective-permute-start(bf16[384,768]{1,0:T(8,128)(2,1)} %get-tuple-element.130), channel_id=1, source_target_pairs={{0,8},{2,10},{4,12},{6,14},{8,0},{10,2},{12,4},{14,6},{16,24},{18,... | collective-permute-start | bytes 1769480 | tf_op jit(solution)/shard_map/ppermute | solution.py:137
  35.1 26.6 %collective-permute-start.5 = (bf16[384,768]{1,0:T(8,128)(2,1)}, bf16[384,768]{1,0:T(8,128)(2,1)S(1)}, u32[]{:S(2)}, u32[]{:S(2)}) collective-permute-start(bf16[384,768]{1,0:T(8,128)(2,1)} %get-tuple-element.130), channel_id=1, source_target_pairs={{0,16},{2,18},{4,20},{6,22},{8,24},{10,26},{12,28},{14,30},{16,0},... | collective-permute-start | bytes 1769480 | tf_op jit(solution)/shard_map/ppermute | solution.py:137
  61.7 40.7 %collective-permute-start.13 = (bf16[2,256,1024]{2,1,0:T(8,128)(2,1)}, bf16[2,256,1024]{2,1,0:T(8,128)(2,1)S(1)}, u32[]{:S(2)}, u32[]{:S(2)}) collective-permute-start(bf16[2,256,1024]{2,1,0:T(8,128)(2,1)} %gated_conv.1.refs_0_), channel_id=1, source_target_pairs={{0,6},{2,4},{4,2},{6,0},{8,14},{10,12},{12,10},{14,8},{16,22},{18,... | collective-permute-start | bytes 3145736 | tf_op jit(solution)/shard_map/ppermute | solution.py:137
  63.6 42.8 %collective-permute-start.12 = (bf16[2,256,1024]{2,1,0:T(8,128)(2,1)}, bf16[2,256,1024]{2,1,0:T(8,128)(2,1)S(1)}, u32[]{:S(2)}, u32[]{:S(2)}) collective-permute-start(bf16[2,256,1024]{2,1,0:T(8,128)(2,1)} %gated_conv.1.refs_0_), channel_id=1, source_target_pairs={{0,4},{2,6},{4,0},{6,2},{8,12},{10,14},{12,8},{14,10},{16,20},{18,... | collective-permute-start | bytes 3145736 | tf_op jit(solution)/shard_map/ppermute | solution.py:137
  64.1 42.4 %collective-permute-start.11 = (bf16[2,256,1024]{2,1,0:T(8,128)(2,1)}, bf16[2,256,1024]{2,1,0:T(8,128)(2,1)S(1)}, u32[]{:S(2)}, u32[]{:S(2)}) collective-permute-start(bf16[2,256,1024]{2,1,0:T(8,128)(2,1)} %gated_conv.1.refs_0_), channel_id=1, source_target_pairs={{0,2},{2,0},{4,6},{6,4},{8,10},{10,8},{12,14},{14,12},{16,18},{18,... | collective-permute-start | bytes 3145736 | tf_op jit(solution)/shard_map/ppermute | solution.py:137
  65.2 37.2 %collective-permute-start.10 = (bf16[640,768]{1,0:T(8,128)(2,1)}, bf16[640,768]{1,0:T(8,128)(2,1)S(1)}, u32[]{:S(2)}, u32[]{:S(2)}) collective-permute-start(bf16[640,768]{1,0:T(8,128)(2,1)} %get-tuple-element.139), channel_id=1, source_target_pairs={{0,8},{2,10},{4,12},{6,14},{8,0},{10,2},{12,4},{14,6},{16,24},{18,... | collective-permute-start | bytes 2949128 | tf_op jit(solution)/shard_map/ppermute | solution.py:137
  66.9 35.5 %collective-permute-start.9 = (bf16[512,768]{1,0:T(8,128)(2,1)}, bf16[512,768]{1,0:T(8,128)(2,1)S(1)}, u32[]{:S(2)}, u32[]{:S(2)}) collective-permute-start(bf16[512,768]{1,0:T(8,128)(2,1)} %get-tuple-element.138), channel_id=1, source_target_pairs={{0,16},{2,18},{4,20},{6,22},{8,24},{10,26},{12,28},{14,30},{16,0},... | collective-permute-start | bytes 2359304 | tf_op jit(solution)/shard_map/ppermute | solution.py:137
  106.5 11.6 %collective-permute-start.15 = (bf16[2,256,1024]{2,1,0:T(8,128)(2,1)}, bf16[2,256,1024]{2,1,0:T(8,128)(2,1)S(1)}, u32[]{:S(2)}, u32[]{:S(2)}) collective-permute-start(bf16[2,256,1024]{2,1,0:T(8,128)(2,1)} %gated_conv.1.refs_0_), channel_id=1, source_target_pairs={{0,1},{1,0},{2,3},{3,2},{4,5},{5,4},{6,7},{7,6},{8,9},{9,8},{10,11... | collective-permute-start | bytes 3145736 | tf_op jit(solution)/shard_map/ppermute | solution.py:137
  106.5 11.6 %collective-permute-start.16 = (bf16[2,256,1024]{2,1,0:T(8,128)(2,1)S(1)}, bf16[2,256,1024]{2,1,0:T(8,128)(2,1)S(1)}, u32[]{:S(2)}, u32[]{:S(2)}) collective-permute-start(bf16[2,256,1024]{2,1,0:T(8,128)(2,1)S(1)} %collective-permute-done.11.refs_1_), channel_id=1, source_target_pairs={{0,1},{1,0},{2,3},{3,2},{4,5},{5,4},{6,7},{7,6},{8,9},{9,8},{10,11... | collective-permute-start | bytes 3145736 | tf_op jit(solution)/shard_map/ppermute | solution.py:137
  107.0 11.1 %collective-permute-start.17 = (bf16[2,256,1024]{2,1,0:T(8,128)(2,1)S(1)}, bf16[2,256,1024]{2,1,0:T(8,128)(2,1)S(1)}, u32[]{:S(2)}, u32[]{:S(2)}) collective-permute-start(bf16[2,256,1024]{2,1,0:T(8,128)(2,1)S(1)} %collective-permute-done.12.refs_2_), channel_id=1, source_target_pairs={{0,1},{1,0},{2,3},{3,2},{4,5},{5,4},{6,7},{7,6},{8,9},{9,8},{10,11... | collective-permute-start | bytes 3145736 | tf_op jit(solution)/shard_map/ppermute | solution.py:137
  107.1 13.4 %collective-permute-start.18 = (bf16[2,256,1024]{2,1,0:T(8,128)(2,1)S(1)}, bf16[2,256,1024]{2,1,0:T(8,128)(2,1)}, u32[]{:S(2)}, u32[]{:S(2)}) collective-permute-start(bf16[2,256,1024]{2,1,0:T(8,128)(2,1)S(1)} %collective-permute-done.13.refs_3_), channel_id=1, source_target_pairs={{0,1},{1,0},{2,3},{3,2},{4,5},{5,4},{6,7},{7,6},{8,9},{9,8},{10,11... | collective-permute-start | bytes 3145736 | tf_op jit(solution)/shard_map/ppermute | solution.py:137
  107.5 10.6 %collective-permute-start.14 = (bf16[128,768]{1,0:T(8,128)(2,1)S(1)}, bf16[128,768]{1,0:T(8,128)(2,1)S(1)}, u32[]{:S(2)}, u32[]{:S(2)}) collective-permute-start(bf16[128,768]{1,0:T(8,128)(2,1)S(1)} %copy-done.21), channel_id=1, source_target_pairs={{0,16},{2,18},{4,20},{6,22},{8,24},{10,26},{12,28},{14,30},{16,0},... | collective-permute-start | bytes 589832 | tf_op jit(solution)/shard_map/ppermute | solution.py:137
  123.0 25.5 %collective-permute-start.19 = (bf16[1024,512]{1,0:T(8,128)(2,1)}, bf16[1024,512]{1,0:T(8,128)(2,1)S(1)}, u32[]{:S(2)}, u32[]{:S(2)}) collective-permute-start(bf16[1024,512]{1,0:T(8,128)(2,1)} %get-tuple-element.163), channel_id=1, source_target_pairs={{8,0},{10,2},{12,4},{14,6},{16,24},{18,26},{20,28},{22,30},{9,1},{... | collective-permute-start | bytes 3145736 | tf_op jit(solution)/shard_map/ppermute | solution.py:344
  126.3 27.9 %collective-permute-start.20 = (bf16[1024,512]{1,0:T(8,128)(2,1)}, bf16[1024,512]{1,0:T(8,128)(2,1)}, u32[]{:S(2)}, u32[]{:S(2)}) collective-permute-start(bf16[1024,512]{1,0:T(8,128)(2,1)} %get-tuple-element.164), channel_id=1, source_target_pairs={{8,16},{10,18},{12,20},{14,22},{16,8},{18,10},{20,12},{22,14},{9,1... | collective-permute-start | bytes 3145736 | tf_op jit(solution)/shard_map/ppermute | solution.py:341
  154.2 14.1 %collective-permute-start.24 = (bf16[1024,256]{1,0:T(8,128)(2,1)}, bf16[1024,256]{1,0:T(8,128)(2,1)S(1)}, u32[]{:S(2)}, u32[]{:S(2)}) collective-permute-start(bf16[1024,256]{1,0:T(8,128)(2,1)} %get-tuple-element.187), channel_id=1, source_target_pairs={{8,0},{10,2},{12,4},{14,6},{16,24},{18,26},{20,28},{22,30},{9,1},{... | collective-permute-start | bytes 1572872 | tf_op jit(solution)/shard_map/ppermute | solution.py:344
  155.6 15.1 %collective-permute-start.25 = (bf16[1024,256]{1,0:T(8,128)(2,1)}, bf16[1024,256]{1,0:T(8,128)(2,1)S(1)}, u32[]{:S(2)}, u32[]{:S(2)}) collective-permute-start(bf16[1024,256]{1,0:T(8,128)(2,1)} %get-tuple-element.188), channel_id=1, source_target_pairs={{8,16},{10,18},{12,20},{14,22},{16,8},{18,10},{20,12},{22,14},{9,1... | collective-permute-start | bytes 1572872 | tf_op jit(solution)/shard_map/ppermute | solution.py:341
  164.7 13.5 %collective-permute-start.21 = (bf16[256,512]{1,0:T(8,128)(2,1)}, bf16[256,512]{1,0:T(8,128)(2,1)S(1)}, u32[]{:S(2)}, u32[]{:S(2)}) collective-permute-start(bf16[256,512]{1,0:T(8,128)(2,1)} %get-tuple-element.184), channel_id=1, source_target_pairs={{0,2},{2,0},{4,6},{6,4},{8,10},{10,8},{12,14},{14,12},{16,18},{18,... | collective-permute-start | bytes 786440 | tf_op jit(solution)/shard_map/ppermute | solution.py:137
  165.7 13.7 %collective-permute-start.22 = (bf16[256,512]{1,0:T(8,128)(2,1)}, bf16[256,512]{1,0:T(8,128)(2,1)S(1)}, u32[]{:S(2)}, u32[]{:S(2)}) collective-permute-start(bf16[256,512]{1,0:T(8,128)(2,1)} %get-tuple-element.185), channel_id=1, source_target_pairs={{0,4},{2,6},{4,0},{6,2},{8,12},{10,14},{12,8},{14,10},{16,20},{18,... | collective-permute-start | bytes 786440 | tf_op jit(solution)/shard_map/ppermute | solution.py:137
  167.1 12.3 %collective-permute-start.23 = (bf16[256,512]{1,0:T(8,128)(2,1)}, bf16[256,512]{1,0:T(8,128)(2,1)S(1)}, u32[]{:S(2)}, u32[]{:S(2)}) collective-permute-start(bf16[256,512]{1,0:T(8,128)(2,1)} %get-tuple-element.186), channel_id=1, source_target_pairs={{0,6},{2,4},{4,2},{6,0},{8,14},{10,12},{12,10},{14,8},{16,22},{18,... | collective-permute-start | bytes 786440 | tf_op jit(solution)/shard_map/ppermute | solution.py:137
  (27 other events, 325.6 us)

commit v8 on v7

--- a/solution.py
+++ b/solution.py
@@ -167,36 +167,6 @@
     return lax.fori_loop(0, once, run, empty)
 
 
-def pack(sources, recipes):
-    shapes = [(sum(part[1].stop - part[1].start for part in recipe), recipe[0][3]) for recipe in recipes]
-    moves = []
-    for out, recipe in enumerate(recipes):
-        row = 0
-        for source, span, col, cols in recipe:
-            moves.append((source, span.start, span.stop - span.start, col, cols, out, row))
-            row += span.stop - span.start
-
-    def kernel(*refs):
-        in_refs, out_refs, sems = refs[: len(sources)], refs[len(sources) : -1], refs[-1]
-        copies = []
-        for n, (source, first, count, col, cols, out, row) in enumerate(moves):
-            block = in_refs[source].at[pl.ds(first, count), pl.ds(col, cols)]
-            copies.append(pltpu.make_async_copy(block, out_refs[out].at[pl.ds(row, count), :], sems.at[n]))
-            copies[-1].start()
-        for copy in copies:
-            copy.wait()
-
-    return pl.pallas_call(
-        kernel,
-        in_specs=[pl.BlockSpec(memory_space=pl.ANY)] * len(sources),
-        out_specs=[pl.BlockSpec(memory_space=pltpu.VMEM)] * len(recipes),
-        out_shape=[jax.ShapeDtypeStruct(shape, sources[0].dtype) for shape in shapes],
-        scratch_shapes=[pltpu.SemaphoreType.DMA((len(moves),))],
-        compiler_params=pltpu.CompilerParams(vmem_limit_bytes=VMEM_BYTES),
-        name="pack",
-    )(*sources)
-
-
 def product(flags, places, ours, theirs, blocks, accs, widths, out_dtype):
     _, rows, depth = ours[0].shape
     chunk = depth // PLANE
@@ -209,7 +179,7 @@
         our_refs, their_refs, refs = refs[:PLANE], refs[PLANE : 2 * PLANE], refs[2 * PLANE :]
         weight_refs, refs = list(refs[: len(weights)]), refs[len(weights) :]
         acc_refs, out_refs = refs[: len(accs)], refs[len(accs) : len(accs) + PLANE * len(widths)]
-        gated_buf, weight_buf, gated_sems, weight_sems = refs[-4:]
+        gated_buf, weight_buf, acc_buf, gated_sems, weight_sems, acc_sem = refs[-6:]
 
         step = chunk // 2
 
@@ -236,10 +206,14 @@
                     target_rows = gated_buf.at[b, pl.ds(r * rows, rows), :]
                     copy = pltpu.make_async_copy(refs_of[r].at[half], target_rows, gated_sems.at[b])
                     pl.when(flag_ref[flag] // 2 == c)(copy.start)
+        for at, acc_ref in enumerate(acc_refs):
+            pltpu.make_async_copy(acc_ref, acc_buf.at[at], acc_sem).start()
         for b in range(count):
             block = weight_buf.at[pl.ds(b * depth, depth), :]
             pltpu.make_async_copy(block, block, weight_sems.at[b]).wait()
             pltpu.make_async_copy(gated_buf.at[b], gated_buf.at[b], gated_sems.at[b]).wait()
+            if accs and not b:
+                pltpu.make_async_copy(acc_buf, acc_buf, acc_sem).wait()
             first = 0
             for part, width in enumerate(widths):
                 for col in range(0, width, 2 * LANES):
@@ -255,7 +229,7 @@
                         if b:
                             total = total + out_refs[at][:, here]
                         elif accs:
-                            total = total + acc_refs[at][:, here]
+                            total = total + acc_buf[at, :, here]
                         out_refs[at][:, here] = total.astype(out_dtype)
                 first += width
 
@@ -264,14 +238,16 @@
     anywhere = pl.BlockSpec(memory_space=pl.ANY)
     made = pl.pallas_call(
         kernel,
-        in_specs=[smem, smem] + [anywhere] * (2 * PLANE + len(weights)) + [vmem] * len(accs),
+        in_specs=[smem, smem] + [anywhere] * (2 * PLANE + len(weights) + len(accs)),
         out_specs=[vmem] * (PLANE * len(widths)),
         out_shape=[jax.ShapeDtypeStruct((rows, width), out_dtype) for width in widths for _ in range(PLANE)],
         scratch_shapes=[
             pltpu.VMEM((count, PLANE * rows, depth), jnp.bfloat16),
             pltpu.VMEM((count * depth, cols), jnp.bfloat16),
+            pltpu.VMEM((len(accs), *accs[0].shape) if accs else (8, LANES), jnp.float32),
             pltpu.SemaphoreType.DMA((count,)),
             pltpu.SemaphoreType.DMA((count,)),
+            pltpu.SemaphoreType.DMA,
         ],
         compiler_params=pltpu.CompilerParams(vmem_limit_bytes=VMEM_BYTES),
         cost_estimate=pl.CostEstimate(
@@ -325,8 +301,6 @@
     count = lax.axis_size("ctx")
     chunk, feats = w_out.shape
     cols = feats // PLANE
-    wide = 2 * cols // 3
-    widths = [wide, cols - wide]
     speed = rate.reshape(modes, chan // LANES, LANES)
 
     def far(x):
@@ -343,54 +317,45 @@
     def outward(x):
         return lax.ppermute(x, "ctx", [(i, i ^ PLANE) for i in middle])
 
-    def fade(span):
-        return jnp.exp(-speed * span)
-
-    def line_scan(k, v, rate, speed):
+    def group(x, r):
+        return lax.dynamic_slice_in_dim(x, (spot ^ r) * cols, cols, axis=1)
+
+    def plane_scan(k, v, rate, speed):
+        def fade(span):
+            return jnp.exp(-speed * span)
+
         ends = end_states(k, v, rate)
-        decay = jnp.exp(-speed * float(PLANE * rows))
-        last = shift_ctx(ends, PLANE)
-        line = last + decay * shift_ctx(ends + decay * last, 2 * PLANE)
-        return jnp.stack([ends, line])
-
-    own = [lax.dynamic_slice_in_dim(w_out, (spot ^ r) * cols, cols, axis=1) for r in range(PLANE)]
-    w0, w1, w2, w3 = tie(*own)
-    w1, w2, w3 = [exchange(w, "ctx", r + 1) for r, w in enumerate((w1, w2, w3))]
-    pair = box(line_scan, k, v, rate, speed)
-    w0, w1, w2, w3, pair = tie(w0, w1, w2, w3, pair)
-
-    half = chunk // 2
-    every, upper, lower = slice(0, chunk), slice(0, half), slice(half, chunk)
-    head, tail, tail1, tail2, midA, midB = pack(
-        [w0, w1, w2, w3],
-        [
-            [(0, every, 0, cols), (1, upper, 0, cols)],
-            [(1, lower, 0, cols), (2, every, 0, cols), (3, every, 0, cols)],
-            [(1, lower, 0, cols), (2, every, 0, cols), (3, upper, 0, cols)],
-            [(3, lower, 0, cols)],
-            [(r, every, 0, wide) for r in range(PLANE)],
-            [(r, every, wide, cols - wide) for r in range(PLANE)],
-        ],
-    )
-    f0, n0 = far(head), near(head)
+        other = exchange(ends, "ctx", 1)
+        both = jnp.where(x_later, fade(float(rows)) * other + ends, fade(float(rows)) * ends + other)
+        before = jnp.where(x_later, other, 0.0)
+        other = exchange(both, "ctx", 2)
+        before = before + jnp.where(y_later, fade((spot & 1).astype(jnp.float32) * rows) * other, 0.0)
+        both = jnp.where(y_later, fade(2.0 * rows) * other + both, fade(2.0 * rows) * both + other)
+        return jnp.stack([both, before])
+
     x_later, y_later = (spot & 1) != 0, (spot & 2) != 0
-    other = exchange(pair, "ctx", 1)
-    both = jnp.where(x_later, fade(float(rows)) * other + pair, fade(float(rows)) * pair + other)
-    before = jnp.where(x_later, other[0], 0.0)
-    other = exchange(both, "ctx", 2)
-    before = before + jnp.where(y_later, fade((spot & 1).astype(jnp.float32) * rows) * other[0], 0.0)
-    line = jnp.where(y_later, fade(2.0 * rows) * other[1] + both[1], fade(2.0 * rows) * both[1] + other[1])
-    enter = before + fade((spot * rows).astype(jnp.float32)) * line
+    w0, w_out = tie(group(w_out, 0), w_out)
+    f0, n0 = far(w0), near(w0)
+    scanned = box(plane_scan, k, v, rate, speed)
+    f0, n0, w0, scanned, w_out = tie(f0, n0, w0, scanned, w_out)
+
+    arrived = [exchange(group(w_out, r), "ctx", r) for r in range(1, PLANE)]
+    both, before = scanned[0], scanned[1]
+    decay = jnp.exp(-speed * float(PLANE * rows))
+    last = shift_ctx(both, PLANE)
+    line = last + decay * shift_ctx(both + decay * last, 2 * PLANE)
+    enter = before + jnp.exp(-speed * (spot * rows).astype(jnp.float32)) * line
     gated = gated_conv(q, k, v, rate, residue, skip, enter)
-    f0, n0, tail, tail1, tail2, midA, midB, gated = tie(f0, n0, tail, tail1, tail2, midA, midB, gated)
-
-    f1, n1 = far(tail1), near(tail)
+    rest = jnp.concatenate(arrived)
+    gated, rest = tie(gated, rest)
+
+    fr, nr = far(rest), near(rest)
     ours = [gated] + [exchange(gated, "ctx", r) for r in range(1, PLANE)]
-    f1, n1, tail2, midA, midB, *ours = tie(f1, n1, tail2, midA, midB, *ours)
-
-    f2 = far(tail2)
-    theirs = [exchange(x, "ch", 1) for x in ours]
-    f0, f1, f2, midA, midB, *held = tie(f0, f1, f2, midA, midB, *ours, *theirs)
+    fr, nr, f0, w0, rest, *ours = tie(fr, nr, f0, w0, rest, *ours)
+
+    out0, mid0 = outward(f0), across(w0)
+    theirs = [exchange(x, "ch", 1) for x in ours[1:]]
+    out0, mid0, fr, rest, *held = tie(out0, mid0, fr, rest, *ours, *theirs)
     ours, theirs = held[:PLANE], held[PLANE:]
 
     def source_of(b):
@@ -400,32 +365,20 @@
     flags = jnp.stack([source_of(plane ^ r) for r in range(4)] + [is_middle]).astype(jnp.int32)
     places = jnp.stack([spot ^ r for r in range(PLANE)]).astype(jnp.int32)
 
-    full = [slice(0, x.shape[0]) for x in (f0, f1, f2)]
-    outA, outB = pack(
-        [f0, f1, f2],
-        [
-            [(n, span, 0, wide) for n, span in enumerate(full)],
-            [(n, span, wide, cols - wide) for n, span in enumerate(full)],
-        ],
-    )
-    outA, midA = outward(outA), across(midA)
+    out1, mid1 = outward(fr), across(rest)
+    theirs = [exchange(ours[0], "ch", 1)] + theirs
     blocks = [
-        (0, None, [((w,), 0) for w in (w0, w1, w2, w3)]),
-        (1, None, [((n0,), 0), ((n1,), 0)]),
-        (2, None, [((f0,), 0), ((f1,), 0), ((f2,), 0)]),
+        (0, None, [((w0,), 0), ((rest,), 0)]),
+        (1, None, [((n0,), 0), ((nr,), 0)]),
+        (2, None, [((f0,), 0), ((fr,), 0)]),
     ]
-    accA, accB = product(flags, places, ours, theirs, blocks, None, widths, jnp.float32)
-    outA, midA, outB, midB, *accs = tie(outA, midA, outB, midB, *accA, *accB)
-    accA, accB = accs[:PLANE], accs[PLANE:]
-
-    outB, midB = outward(outB), across(midB)
-    blocks = [(3, 4, [((outA, midA), 0)])]
-    (madeA,) = product(flags, places, ours, theirs, blocks, accA, widths[:1], jnp.bfloat16)
-    backA = [madeA[0]] + [exchange(madeA[r], "ctx", r) for r in range(1, PLANE)]
-    blocks = [(3, 4, [((outB, midB), 0)])]
-    (madeB,) = product(flags, places, ours, theirs, blocks, accB, widths[1:], jnp.bfloat16)
-    backB = [madeB[0]] + [exchange(madeB[r], "ctx", r) for r in range(1, PLANE)]
-    return assemble(places, [backA, backB])
+    (accs,) = product(flags, places, ours, theirs, blocks, None, [cols], jnp.float32)
+    out1, mid1, *accs = tie(out1, mid1, *accs)
+
+    blocks = [(3, 4, [((out0, mid0), 0), ((out1, mid1), 0)])]
+    (made,) = product(flags, places, ours, theirs, blocks, accs, [cols], jnp.bfloat16)
+    back = [made[0]] + [exchange(made[r], "ctx", r) for r in range(1, PLANE)]
+    return assemble(places, [back])
 
 
 def body(q, k, v, residue, rate, skip, w_out):
@@ -439,7 +392,7 @@
         and cores == 2
         and chan == 8 * chunk
         and chunk % LANES == 0
-        and feats % (6 * PLANE * LANES) == 0
+        and feats % (2 * PLANE * LANES) == 0
     )
     skip = skip.reshape(groups, LANES)
     if split:

time: 188 us -> 180 us (0.957)
  starting transfers between devices: 48.1 us -> 38 us
  waiting for transfers between devices: 82.7 us -> 92.8 us
  Pallas kernels: 42 us -> 33.3 us
    ppermute x2, waiting for transfers between devices: 5.35 us -> 14.4 us  [outward(): return lax.ppermute(x, 'ctx', [(i, i ^ PLANE) for i in middle])]
    pallas_call x2 -> x0, Pallas kernels: 7.03 us -> none  [pack(): pl.pallas_call(kernel, in_specs=[pl.BlockSpec(memory_space=pl.ANY)] * len...]
    ppermute x23 -> x19, starting transfers between devices: 27.4 us -> 21.4 us  [exchange(): return lax.ppermute(x, axis, [(i, i ^ flip) for i in range(count)])]
    ppermute x23 -> x19, waiting for transfers between devices: 61.9 us -> 67.3 us  [exchange(): return lax.ppermute(x, axis, [(i, i ^ flip) for i in range(count)])]
    ppermute x2, waiting for transfers between devices: 7.42 us -> 2.49 us  [shift_ctx(): return lax.ppermute(x, 'ctx', [(i, i + by) for i in range(count - by)])]
    ppermute x2, starting transfers between devices: 7.97 us -> 4.51 us  [shift_ctx(): return lax.ppermute(x, 'ctx', [(i, i + by) for i in range(count - by)])]
    pallas_call x3 -> x2, Pallas kernels: 20.9 us -> 18.3 us  [product(): pl.pallas_call(kernel, in_specs=[smem, smem] + [anywhere] * (2 * PLANE +...]
    unnamed x45 -> x47, local copies, waits for them, and re-layouts: 4.17 us -> 4.14 us
  transfers between devices with their start and end apart: 29 -> 25, of which waited for: 15 -> 16; matrix products, arithmetic and copies ran while one was open for 4% -> 4% of each run, Pallas kernels for 20% -> 14%
where the time goes in v8:
time: 180 us; the launch traced here: 178 us
  waiting for transfers between devices  92.8 us (52%)
  starting transfers between devices  38 us (21%)
  Pallas kernels  33.3 us (18%)
  local copies, waits for them, and re-layouts  9.62 us (5%)
  other arithmetic  4.35 us (2%)
    ppermute x19, waiting for transfers between devices, exchange(): return lax.ppermute(x, axis, [(i, i ^ flip) for i in range(count)])  67.3 us
    ppermute x19, starting transfers between devices, exchange(): return lax.ppermute(x, axis, [(i, i ^ flip) for i in range(count)])  21.4 us
    pallas_call x2, Pallas kernels, product(): pl.pallas_call(kernel, in_specs=[smem, smem] + [anywhere] * (2 * PLANE +...  18.3 us
    ppermute x2, waiting for transfers between devices, outward(): return lax.ppermute(x, 'ctx', [(i, i ^ PLANE) for i in middle])  14.4 us
    ppermute x2, waiting for transfers between devices, across(): return lax.ppermute(x, 'ctx', [(i, i ^ 3 * PLANE) for i in middle])  8.59 us
    pallas_call x1, Pallas kernels, gated_conv(): pl.pallas_call(conv_kernel, grid=(chan // width,), in_specs=[wide, wide,...  8.36 us
    ppermute x2, starting transfers between devices, across(): return lax.ppermute(x, 'ctx', [(i, i ^ 3 * PLANE) for i in middle])  7.67 us
    pallas_call x1, Pallas kernels, end_states(): pl.pallas_call(ends_kernel, grid=(chan // width,), in_specs=[wide, wide,...  4.99 us
  transfers between devices with their start and end apart: 25, of which 16 were waited for; matrix products, arithmetic and copies ran while one was open for 4% of the time, Pallas kernels for 14%

profile of v8, /device:TPU:8, one launch (start us, length us, event | category | flops | bytes accessed | tf_op | source)
XLA Modules:
  0.0 178.5 jit_solution(454593484169749958)
XLA Ops:
  1.1 3.0 %collective-permute-start.2 = (bf16[256,768]{1,0:T(8,128)(2,1)S(1)}, bf16[256,768]{1,0:T(8,128)(2,1)S(1)}, u32[]{:S(2)}, u32[]{:S(2)}) collective-permute-start(bf16[256,768]{1,0:T(8,128)(2,1)S(1)} %constant_dynamic-slice_fusion.3.refs_8_), channel_id=1, source_target_pairs={{0,16},{2,18},{4,20},{6,22},{8,24},{10,26},{12,28},{14,30},{16,0},... | collective-permute-start | bytes 1179656 | tf_op jit(solution)/shard_map/ppermute | solution.py:137
  5.8 16.9 %while.12 = (s32[]{:T(128)}, f32[2,16,16,128]{3,2,1,0:T(8,128)}, s32[]{:T(128)}, pred[]{:T(512)}, bf16[256,2048]{1,0:T(8,128)(2,1)}, /*index=5*/bf16[256,2048]{1...) while((s32[]{:T(128)}, f32[2,16,16,128]{3,2,1,0:T(8,128)}, ...), condition=%wide.region_1.2_spmd, body=%wide.region_0.1_spmd.sunk | while | flops 17465344 | bytes 4980932 | solution.py:167
  5.8 5.0 %end_states.3 = f32[16,16,128]{2,1,0:T(8,128)} custom-call(bf16[256,2048]{1,0:T(8,128)(2,1)} %get-tuple-element.305.k_ref, bf16[256,2048]{1,0:T(8,128)(2,1)} %get-tuple-element.306.v_ref, f32[16,2048]{1,0:T(8,128)} %get-tuple-element.307.rate_ref), custom_call_target="tpu_custom_call" | custom-call | flops 16777216 | bytes 2097152 | tf_op jit(solution)/shard_map/while/body/end_states/pallas_call | solution.py:90
  12.3 3.7 %collective-permute-done = f32[16,16,128]{2,1,0:T(8,128)S(1)} collective-permute-done((f32[16,16,128]{2,1,0:T(8,128)}, f32[16,16,128]{2,1,0:T(8,128)S(1)}, u32[]{:S(2)}, u32[]{:S(2)}) %collective-permute-start) | collective-permute-done | bytes 131104 | tf_op jit(solution)/shard_map/while/body/ppermute | solution.py:137
  18.5 3.4 %collective-permute-done.1 = f32[16,16,128]{2,1,0:T(8,128)S(1)} collective-permute-done((f32[16,16,128]{2,1,0:T(8,128)S(1)}, f32[16,16,128]{2,1,0:T(8,128)S(1)}, u32[]{:S(2)}, u32[]{:S(2)}) %collective-permute-start.1) | collective-permute-done | bytes 131104 | tf_op jit(solution)/shard_map/while/body/ppermute | solution.py:137
  24.6 2.5 %collective-permute-start.4 = (f32[16,16,128]{2,1,0:T(8,128)S(1)}, f32[16,16,128]{2,1,0:T(8,128)S(1)}, u32[]{:S(2)}, u32[]{:S(2)}) collective-permute-start(f32[16,16,128]{2,1,0:T(8,128)S(1)} %slice_bitcast_fusion), channel_id=1, source_target_pairs={{0,8},{2,10},{4,12},{6,14},{8,16},{10,18},{12,20},{14,22},{16,24},... | collective-permute-start | bytes 393224 | tf_op jit(solution)/shard_map/ppermute | solution.py:132
  27.1 2.2 %constant_dynamic-slice_fusion.2 = (bf16[256,768]{1,0:T(8,128)(2,1)}, bf16[256,768]{1,0:T(8,128)(2,1)}, bf16[256,768]{1,0:T(8,128)(2,1)S(1)}) fusion(bf16[256,3072]{1,0:T(8,128)(2,1)} %param.15, s32[]{:T(128)S(6)} %select_n.92, s32[]{:T(128)S(6)} %select_n.94, s32[]{:T(128)S(6)} %select_n.93), kind=kLoop, calls=%fused_computation.11 | loop fusion | bytes 2359308 | tf_op jit(solution)/shard_map/dynamic_slice | solution.py:321
  34.9 2.5 %collective-permute-done.5 = f32[16,16,128]{2,1,0:T(8,128)S(1)} collective-permute-done((f32[16,16,128]{2,1,0:T(8,128)S(1)}, f32[16,16,128]{2,1,0:T(8,128)S(1)}, u32[]{:S(2)}, u32[]{:S(2)}) %collective-permute-start.5) | collective-permute-done | bytes 131104 | tf_op jit(solution)/shard_map/ppermute | solution.py:132
  38.1 8.4 %gated_conv.1.refs_0_ = bf16[2,256,1024]{2,1,0:T(8,128)(2,1)} custom-call(bf16[256,2048]{1,0:T(8,128)(2,1)} %q_ref.1, bf16[256,2048]{1,0:T(8,128)(2,1)S(1)} %copy-done.2, bf16[256,2048]{1,0:T(8,128)(2,1)S(1)} %copy-done.3, f32[16,2048]{1,0:T(8,128)S(1)} %copy-done.4, f32[16,2048]{1,0:T(8,128)} %residue_ref.1, f32[16,128]{1,0:T(8,128)} %bitcast.30, ...), custom_call_target="tpu_custom_call" | custom-call | flops 33554432 | bytes 4194304 | tf_op jit(solution)/shard_map/gated_conv/pallas_call | solution.py:115
  51.6 2.4 %collective-permute-start.9 = (bf16[768,768]{1,0:T(8,128)(2,1)S(1)}, bf16[768,768]{1,0:T(8,128)(2,1)}, u32[]{:S(2)}, u32[]{:S(2)}) collective-permute-start(bf16[768,768]{1,0:T(8,128)(2,1)S(1)} %pad_maximum_fusion.1.refs_9_), channel_id=1, source_target_pairs={{0,16},{2,18},{4,20},{6,22},{8,24},{10,26},{12,28},{14,30},{16,0},... | collective-permute-start | bytes 3538952 | tf_op jit(solution)/shard_map/ppermute | solution.py:137
  54.0 2.4 %collective-permute-start.13 = (bf16[2,256,1024]{2,1,0:T(8,128)(2,1)S(1)}, bf16[2,256,1024]{2,1,0:T(8,128)(2,1)S(1)}, u32[]{:S(2)}, u32[]{:S(2)}) collective-permute-start(bf16[2,256,1024]{2,1,0:T(8,128)(2,1)S(1)} %copy-done.5), channel_id=1, source_target_pairs={{0,6},{2,4},{4,2},{6,0},{8,14},{10,12},{12,10},{14,8},{16,22},{18,... | collective-permute-start | bytes 3145736 | tf_op jit(solution)/shard_map/ppermute | solution.py:137
  57.5 23.5 %collective-permute-done.13.refs_3_ = bf16[2,256,1024]{2,1,0:T(8,128)(2,1)S(1)} collective-permute-done((bf16[2,256,1024]{2,1,0:T(8,128)(2,1)S(1)}, bf16[2,256,1024]{2,1,0:T(8,128)(2,1)S(1)}, u32[]{:S(2)}, u32[]{:S(2)}) %collective-permute-start.13) | collective-permute-done | bytes 1048608 | tf_op jit(solution)/shard_map/ppermute | solution.py:137
  81.0 15.4 %collective-permute-done.12.refs_2_ = bf16[2,256,1024]{2,1,0:T(8,128)(2,1)S(1)} collective-permute-done((bf16[2,256,1024]{2,1,0:T(8,128)(2,1)S(1)}, bf16[2,256,1024]{2,1,0:T(8,128)(2,1)S(1)}, u32[]{:S(2)}, u32[]{:S(2)}) %collective-permute-start.12) | collective-permute-done | bytes 1048608 | tf_op jit(solution)/shard_map/ppermute | solution.py:137
  100.2 3.0 %collective-permute-start.14 = (bf16[256,768]{1,0:T(8,128)(2,1)S(1)}, bf16[256,768]{1,0:T(8,128)(2,1)S(1)}, u32[]{:S(2)}, u32[]{:S(2)}) collective-permute-start(bf16[256,768]{1,0:T(8,128)(2,1)S(1)} %copy-done.22), channel_id=1, source_target_pairs={{8,0},{10,2},{12,4},{14,6},{16,24},{18,26},{20,28},{22,30},{9,1},{... | collective-permute-start | bytes 1179656 | tf_op jit(solution)/shard_map/ppermute | solution.py:318
  103.3 4.0 %collective-permute-start.15 = (bf16[256,768]{1,0:T(8,128)(2,1)S(1)}, bf16[256,768]{1,0:T(8,128)(2,1)S(1)}, u32[]{:S(2)}, u32[]{:S(2)}) collective-permute-start(bf16[256,768]{1,0:T(8,128)(2,1)S(1)} %copy-done.16), channel_id=1, source_target_pairs={{8,16},{10,18},{12,20},{14,22},{16,8},{18,10},{20,12},{22,14},{9,1... | collective-permute-start | bytes 1179656 | tf_op jit(solution)/shard_map/ppermute | solution.py:315
  107.3 4.9 %collective-permute-done.14.refs_8_ = bf16[256,768]{1,0:T(8,128)(2,1)S(1)} collective-permute-done((bf16[256,768]{1,0:T(8,128)(2,1)S(1)}, bf16[256,768]{1,0:T(8,128)(2,1)S(1)}, u32[]{:S(2)}, u32[]{:S(2)}) %collective-permute-start.14) | collective-permute-done | bytes 393248 | tf_op jit(solution)/shard_map/ppermute | solution.py:318
  112.3 4.5 %collective-permute-done.15.refs_9_ = bf16[256,768]{1,0:T(8,128)(2,1)S(1)} collective-permute-done((bf16[256,768]{1,0:T(8,128)(2,1)S(1)}, bf16[256,768]{1,0:T(8,128)(2,1)S(1)}, u32[]{:S(2)}, u32[]{:S(2)}) %collective-permute-start.15) | collective-permute-done | bytes 393248 | tf_op jit(solution)/shard_map/ppermute | solution.py:315
  118.6 3.6 %collective-permute-start.21 = (bf16[768,768]{1,0:T(8,128)(2,1)S(1)}, bf16[768,768]{1,0:T(8,128)(2,1)}, u32[]{:S(2)}, u32[]{:S(2)}) collective-permute-start(bf16[768,768]{1,0:T(8,128)(2,1)S(1)} %pad_maximum_fusion.1.refs_9_), channel_id=1, source_target_pairs={{8,16},{10,18},{12,20},{14,22},{16,8},{18,10},{20,12},{22,14},{9,1... | collective-permute-start | bytes 3538952 | tf_op jit(solution)/shard_map/ppermute | solution.py:315
  123.6 11.7 %product.2 = (f32[256,768]{1,0:T(8,128)}, f32[256,768]{1,0:T(8,128)}, f32[256,768]{1,0:T(8,128)}, f32[256,768]{1,0:T(8,128)}) custom-call(s32[5]{0:T(128)} %stack.58.flag_ref, s32[4]{0:T(128)} %pad_add_fusion.place_ref, bf16[2,256,1024]{2,1,0:T(8,128)(2,1)} %gated_conv.1.refs_0_, bf16[2,256,1024]{2,1,0:T(8,128)(2,1)} %copy-done.11, ...), custom_call_target="tpu_custom_call" | custom-call | flops 4831838208 | bytes 11010048 | tf_op jit(solution)/shard_map/product/pallas_call | solution.py:239
  135.3 9.4 %collective-permute-done.20.refs_10_ = bf16[768,768]{1,0:T(8,128)(2,1)S(1)} collective-permute-done((bf16[768,768]{1,0:T(8,128)(2,1)}, bf16[768,768]{1,0:T(8,128)(2,1)S(1)}, u32[]{:S(2)}, u32[]{:S(2)}) %collective-permute-start.20) | collective-permute-done | bytes 1179680 | tf_op jit(solution)/shard_map/ppermute | solution.py:318
  144.7 4.0 %collective-permute-done.21.refs_11_ = bf16[768,768]{1,0:T(8,128)(2,1)} collective-permute-done((bf16[768,768]{1,0:T(8,128)(2,1)S(1)}, bf16[768,768]{1,0:T(8,128)(2,1)}, u32[]{:S(2)}, u32[]{:S(2)}) %collective-permute-start.21) | collective-permute-done | bytes 1179680 | tf_op jit(solution)/shard_map/ppermute | solution.py:315
  148.8 6.6 %product.3 = (bf16[256,768]{1,0:T(8,128)(2,1)}, bf16[256,768]{1,0:T(8,128)(2,1)}, bf16[256,768]{1,0:T(8,128)(2,1)}, bf16[256,768]{1,0:T(8,128)(2,1)}) custom-call(s32[5]{0:T(128)} %stack.58.flag_ref, s32[4]{0:T(128)} %pad_add_fusion.place_ref, bf16[2,256,1024]{2,1,0:T(8,128)(2,1)} %gated_conv.1.refs_0_, bf16[2,256,1024]{2,1,0:T(8,128)(2,1)} %copy-done.11, ...), custom_call_target="tpu_custom_call" | custom-call | flops 1610612736 | bytes 3670016 | tf_op jit(solution)/shard_map/product/pallas_call | solution.py:239
  158.9 8.8 %collective-permute-done.22.refs_1_ = bf16[256,768]{1,0:T(8,128)(2,1)S(1)} collective-permute-done((bf16[256,768]{1,0:T(8,128)(2,1)}, bf16[256,768]{1,0:T(8,128)(2,1)S(1)}, u32[]{:S(2)}, u32[]{:S(2)}) %collective-permute-start.22) | collective-permute-done | bytes 393248 | tf_op jit(solution)/shard_map/ppermute | solution.py:137
  167.7 8.1 %collective-permute-done.23.refs_2_ = bf16[256,768]{1,0:T(8,128)(2,1)S(1)} collective-permute-done((bf16[256,768]{1,0:T(8,128)(2,1)}, bf16[256,768]{1,0:T(8,128)(2,1)S(1)}, u32[]{:S(2)}, u32[]{:S(2)}) %collective-permute-start.23) | collective-permute-done | bytes 393248 | tf_op jit(solution)/shard_map/ppermute | solution.py:137
  (91 shorter events, 34.8 us)
Async XLA Ops:
  1.0 21.7 %collective-permute-start.3 = (bf16[256,768]{1,0:T(8,128)(2,1)S(1)}, bf16[256,768]{1,0:T(8,128)(2,1)S(1)}, u32[]{:S(2)}, u32[]{:S(2)}) collective-permute-start(bf16[256,768]{1,0:T(8,128)(2,1)S(1)} %constant_dynamic-slice_fusion.3.refs_8_), channel_id=1, source_target_pairs={{0,8},{2,10},{4,12},{6,14},{8,0},{10,2},{12,4},{14,6},{16,24},{18,... | collective-permute-start | bytes 1179656 | tf_op jit(solution)/shard_map/ppermute | solution.py:137
  1.1 21.7 %collective-permute-start.2 = (bf16[256,768]{1,0:T(8,128)(2,1)S(1)}, bf16[256,768]{1,0:T(8,128)(2,1)S(1)}, u32[]{:S(2)}, u32[]{:S(2)}) collective-permute-start(bf16[256,768]{1,0:T(8,128)(2,1)S(1)} %constant_dynamic-slice_fusion.3.refs_8_), channel_id=1, source_target_pairs={{0,16},{2,18},{4,20},{6,22},{8,24},{10,26},{12,28},{14,30},{16,0},... | collective-permute-start | bytes 1179656 | tf_op jit(solution)/shard_map/ppermute | solution.py:137
  10.8 5.2 %collective-permute-start = (f32[16,16,128]{2,1,0:T(8,128)}, f32[16,16,128]{2,1,0:T(8,128)S(1)}, u32[]{:S(2)}, u32[]{:S(2)}) collective-permute-start(f32[16,16,128]{2,1,0:T(8,128)} %end_states.3), channel_id=1, source_target_pairs={{0,2},{2,0},{4,6},{6,4},{8,10},{10,8},{12,14},{14,12},{16,18},{18,... | collective-permute-start | bytes 393224 | tf_op jit(solution)/shard_map/while/body/ppermute | solution.py:137
  16.9 5.0 %collective-permute-start.1 = (f32[16,16,128]{2,1,0:T(8,128)S(1)}, f32[16,16,128]{2,1,0:T(8,128)S(1)}, u32[]{:S(2)}, u32[]{:S(2)}) collective-permute-start(f32[16,16,128]{2,1,0:T(8,128)S(1)} %add_select_fusion.2), channel_id=1, source_target_pairs={{0,4},{2,6},{4,0},{6,2},{8,12},{10,14},{12,8},{14,10},{16,20},{18,... | collective-permute-start | bytes 393224 | tf_op jit(solution)/shard_map/while/body/ppermute | solution.py:137
  24.6 8.2 %collective-permute-start.4 = (f32[16,16,128]{2,1,0:T(8,128)S(1)}, f32[16,16,128]{2,1,0:T(8,128)S(1)}, u32[]{:S(2)}, u32[]{:S(2)}) collective-permute-start(f32[16,16,128]{2,1,0:T(8,128)S(1)} %slice_bitcast_fusion), channel_id=1, source_target_pairs={{0,8},{2,10},{4,12},{6,14},{8,16},{10,18},{12,20},{14,22},{16,24},... | collective-permute-start | bytes 393224 | tf_op jit(solution)/shard_map/ppermute | solution.py:132
  29.3 17.1 %collective-permute-start.6 = (bf16[256,768]{1,0:T(8,128)(2,1)}, bf16[256,768]{1,0:T(8,128)(2,1)}, u32[]{:S(2)}, u32[]{:S(2)}) collective-permute-start(bf16[256,768]{1,0:T(8,128)(2,1)} %get-tuple-element.236), channel_id=1, source_target_pairs={{0,2},{2,0},{4,6},{6,4},{8,10},{10,8},{12,14},{14,12},{16,18},{18,... | collective-permute-start | bytes 1179656 | tf_op jit(solution)/shard_map/ppermute | solution.py:137
  30.8 16.6 %collective-permute-start.8 = (bf16[256,768]{1,0:T(8,128)(2,1)}, bf16[256,768]{1,0:T(8,128)(2,1)}, u32[]{:S(2)}, u32[]{:S(2)}) collective-permute-start(bf16[256,768]{1,0:T(8,128)(2,1)} %get-tuple-element.237), channel_id=1, source_target_pairs={{0,6},{2,4},{4,2},{6,0},{8,14},{10,12},{12,10},{14,8},{16,22},{18,... | collective-permute-start | bytes 1179656 | tf_op jit(solution)/shard_map/ppermute | solution.py:137
  32.3 16.3 %collective-permute-start.7 = (bf16[256,768]{1,0:T(8,128)(2,1)S(1)}, bf16[256,768]{1,0:T(8,128)(2,1)}, u32[]{:S(2)}, u32[]{:S(2)}) collective-permute-start(bf16[256,768]{1,0:T(8,128)(2,1)S(1)} %get-tuple-element.238), channel_id=1, source_target_pairs={{0,4},{2,6},{4,0},{6,2},{8,12},{10,14},{12,8},{14,10},{16,20},{18,... | collective-permute-start | bytes 1179656 | tf_op jit(solution)/shard_map/ppermute | solution.py:137
  49.9 47.4 %collective-permute-start.10 = (bf16[768,768]{1,0:T(8,128)(2,1)S(1)}, bf16[768,768]{1,0:T(8,128)(2,1)S(1)}, u32[]{:S(2)}, u32[]{:S(2)}) collective-permute-start(bf16[768,768]{1,0:T(8,128)(2,1)S(1)} %pad_maximum_fusion.1.refs_9_), channel_id=1, source_target_pairs={{0,8},{2,10},{4,12},{6,14},{8,0},{10,2},{12,4},{14,6},{16,24},{18,... | collective-permute-start | bytes 3538952 | tf_op jit(solution)/shard_map/ppermute | solution.py:137
  51.6 48.2 %collective-permute-start.9 = (bf16[768,768]{1,0:T(8,128)(2,1)S(1)}, bf16[768,768]{1,0:T(8,128)(2,1)}, u32[]{:S(2)}, u32[]{:S(2)}) collective-permute-start(bf16[768,768]{1,0:T(8,128)(2,1)S(1)} %pad_maximum_fusion.1.refs_9_), channel_id=1, source_target_pairs={{0,16},{2,18},{4,20},{6,22},{8,24},{10,26},{12,28},{14,30},{16,0},... | collective-permute-start | bytes 3538952 | tf_op jit(solution)/shard_map/ppermute | solution.py:137
  54.0 27.0 %collective-permute-start.13 = (bf16[2,256,1024]{2,1,0:T(8,128)(2,1)S(1)}, bf16[2,256,1024]{2,1,0:T(8,128)(2,1)S(1)}, u32[]{:S(2)}, u32[]{:S(2)}) collective-permute-start(bf16[2,256,1024]{2,1,0:T(8,128)(2,1)S(1)} %copy-done.5), channel_id=1, source_target_pairs={{0,6},{2,4},{4,2},{6,0},{8,14},{10,12},{12,10},{14,8},{16,22},{18,... | collective-permute-start | bytes 3145736 | tf_op jit(solution)/shard_map/ppermute | solution.py:137
  56.5 39.9 %collective-permute-start.12 = (bf16[2,256,1024]{2,1,0:T(8,128)(2,1)S(1)}, bf16[2,256,1024]{2,1,0:T(8,128)(2,1)S(1)}, u32[]{:S(2)}, u32[]{:S(2)}) collective-permute-start(bf16[2,256,1024]{2,1,0:T(8,128)(2,1)S(1)} %copy-done.5), channel_id=1, source_target_pairs={{0,4},{2,6},{4,0},{6,2},{8,12},{10,14},{12,8},{14,10},{16,20},{18,... | collective-permute-start | bytes 3145736 | tf_op jit(solution)/shard_map/ppermute | solution.py:137
  57.0 39.5 %collective-permute-start.11 = (bf16[2,256,1024]{2,1,0:T(8,128)(2,1)S(1)}, bf16[2,256,1024]{2,1,0:T(8,128)(2,1)S(1)}, u32[]{:S(2)}, u32[]{:S(2)}) collective-permute-start(bf16[2,256,1024]{2,1,0:T(8,128)(2,1)S(1)} %copy-done.5), channel_id=1, source_target_pairs={{0,2},{2,0},{4,6},{6,4},{8,10},{10,8},{12,14},{14,12},{16,18},{18,... | collective-permute-start | bytes 3145736 | tf_op jit(solution)/shard_map/ppermute | solution.py:137
  99.7 17.1 %collective-permute-start.16 = (bf16[2,256,1024]{2,1,0:T(8,128)(2,1)S(1)}, bf16[2,256,1024]{2,1,0:T(8,128)(2,1)S(1)}, u32[]{:S(2)}, u32[]{:S(2)}) collective-permute-start(bf16[2,256,1024]{2,1,0:T(8,128)(2,1)S(1)} %collective-permute-done.11.refs_1_), channel_id=1, source_target_pairs={{0,1},{1,0},{2,3},{3,2},{4,5},{5,4},{6,7},{7,6},{8,9},{9,8},{10,11... | collective-permute-start | bytes 3145736 | tf_op jit(solution)/shard_map/ppermute | solution.py:137
  99.7 17.1 %collective-permute-start.17 = (bf16[2,256,1024]{2,1,0:T(8,128)(2,1)S(1)}, bf16[2,256,1024]{2,1,0:T(8,128)(2,1)S(1)}, u32[]{:S(2)}, u32[]{:S(2)}) collective-permute-start(bf16[2,256,1024]{2,1,0:T(8,128)(2,1)S(1)} %collective-permute-done.12.refs_2_), channel_id=1, source_target_pairs={{0,1},{1,0},{2,3},{3,2},{4,5},{5,4},{6,7},{7,6},{8,9},{9,8},{10,11... | collective-permute-start | bytes 3145736 | tf_op jit(solution)/shard_map/ppermute | solution.py:137
  100.2 16.6 %collective-permute-start.18 = (bf16[2,256,1024]{2,1,0:T(8,128)(2,1)S(1)}, bf16[2,256,1024]{2,1,0:T(8,128)(2,1)S(1)}, u32[]{:S(2)}, u32[]{:S(2)}) collective-permute-start(bf16[2,256,1024]{2,1,0:T(8,128)(2,1)S(1)} %collective-permute-done.13.refs_3_), channel_id=1, source_target_pairs={{0,1},{1,0},{2,3},{3,2},{4,5},{5,4},{6,7},{7,6},{8,9},{9,8},{10,11... | collective-permute-start | bytes 3145736 | tf_op jit(solution)/shard_map/ppermute | solution.py:137
  100.2 12.1 %collective-permute-start.14 = (bf16[256,768]{1,0:T(8,128)(2,1)S(1)}, bf16[256,768]{1,0:T(8,128)(2,1)S(1)}, u32[]{:S(2)}, u32[]{:S(2)}) collective-permute-start(bf16[256,768]{1,0:T(8,128)(2,1)S(1)} %copy-done.22), channel_id=1, source_target_pairs={{8,0},{10,2},{12,4},{14,6},{16,24},{18,26},{20,28},{22,30},{9,1},{... | collective-permute-start | bytes 1179656 | tf_op jit(solution)/shard_map/ppermute | solution.py:318
  103.3 13.5 %collective-permute-start.15 = (bf16[256,768]{1,0:T(8,128)(2,1)S(1)}, bf16[256,768]{1,0:T(8,128)(2,1)S(1)}, u32[]{:S(2)}, u32[]{:S(2)}) collective-permute-start(bf16[256,768]{1,0:T(8,128)(2,1)S(1)} %copy-done.16), channel_id=1, source_target_pairs={{8,16},{10,18},{12,20},{14,22},{16,8},{18,10},{20,12},{22,14},{9,1... | collective-permute-start | bytes 1179656 | tf_op jit(solution)/shard_map/ppermute | solution.py:315
  116.9 6.7 %collective-permute-start.19 = (bf16[2,256,1024]{2,1,0:T(8,128)(2,1)S(1)}, bf16[2,256,1024]{2,1,0:T(8,128)(2,1)}, u32[]{:S(2)}, u32[]{:S(2)}) collective-permute-start(bf16[2,256,1024]{2,1,0:T(8,128)(2,1)S(1)} %copy-done.5), channel_id=1, source_target_pairs={{0,1},{1,0},{2,3},{3,2},{4,5},{5,4},{6,7},{7,6},{8,9},{9,8},{10,11... | collective-permute-start | bytes 3145736 | tf_op jit(solution)/shard_map/ppermute | solution.py:137
  117.0 27.7 %collective-permute-start.20 = (bf16[768,768]{1,0:T(8,128)(2,1)}, bf16[768,768]{1,0:T(8,128)(2,1)S(1)}, u32[]{:S(2)}, u32[]{:S(2)}) collective-permute-start(bf16[768,768]{1,0:T(8,128)(2,1)} %collective-permute-done.9.refs_13_), channel_id=1, source_target_pairs={{8,0},{10,2},{12,4},{14,6},{16,24},{18,26},{20,28},{22,30},{9,1},{... | collective-permute-start | bytes 3538952 | tf_op jit(solution)/shard_map/ppermute | solution.py:318
  118.6 30.1 %collective-permute-start.21 = (bf16[768,768]{1,0:T(8,128)(2,1)S(1)}, bf16[768,768]{1,0:T(8,128)(2,1)}, u32[]{:S(2)}, u32[]{:S(2)}) collective-permute-start(bf16[768,768]{1,0:T(8,128)(2,1)S(1)} %pad_maximum_fusion.1.refs_9_), channel_id=1, source_target_pairs={{8,16},{10,18},{12,20},{14,22},{16,8},{18,10},{20,12},{22,14},{9,1... | collective-permute-start | bytes 3538952 | tf_op jit(solution)/shard_map/ppermute | solution.py:315
  155.3 12.3 %collective-permute-start.22 = (bf16[256,768]{1,0:T(8,128)(2,1)}, bf16[256,768]{1,0:T(8,128)(2,1)S(1)}, u32[]{:S(2)}, u32[]{:S(2)}) collective-permute-start(bf16[256,768]{1,0:T(8,128)(2,1)} %get-tuple-element.211), channel_id=1, source_target_pairs={{0,2},{2,0},{4,6},{6,4},{8,10},{10,8},{12,14},{14,12},{16,18},{18,... | collective-permute-start | bytes 1179656 | tf_op jit(solution)/shard_map/ppermute | solution.py:137
  156.9 18.9 %collective-permute-start.23 = (bf16[256,768]{1,0:T(8,128)(2,1)}, bf16[256,768]{1,0:T(8,128)(2,1)S(1)}, u32[]{:S(2)}, u32[]{:S(2)}) collective-permute-start(bf16[256,768]{1,0:T(8,128)(2,1)} %get-tuple-element.212), channel_id=1, source_target_pairs={{0,4},{2,6},{4,0},{6,2},{8,12},{10,14},{12,8},{14,10},{16,20},{18,... | collective-permute-start | bytes 1179656 | tf_op jit(solution)/shard_map/ppermute | solution.py:137
  158.4 17.3 %collective-permute-start.24 = (bf16[256,768]{1,0:T(8,128)(2,1)}, bf16[256,768]{1,0:T(8,128)(2,1)S(1)}, u32[]{:S(2)}, u32[]{:S(2)}) collective-permute-start(bf16[256,768]{1,0:T(8,128)(2,1)} %get-tuple-element.213), channel_id=1, source_target_pairs={{0,6},{2,4},{4,2},{6,0},{8,14},{10,12},{12,10},{14,8},{16,22},{18,... | collective-permute-start | bytes 1179656 | tf_op jit(solution)/shard_map/ppermute | solution.py:137
  (24 other events, 378.7 us)

commit v9 on v8

--- a/solution.py
+++ b/solution.py
@@ -167,33 +167,31 @@
     return lax.fori_loop(0, once, run, empty)
 
 
-def product(flags, places, ours, theirs, blocks, accs, widths, out_dtype):
+def product(flags, places, ours, theirs, blocks, accs, out_dtype):
     _, rows, depth = ours[0].shape
     chunk = depth // PLANE
-    cols = sum(widths)
-    count = len(blocks)
-    weights = [array for _, _, pieces in blocks for choices, *_ in pieces for array in choices]
+    cols = blocks[0][2][0][0][0].shape[1]
+    count, parts = len(blocks), len(ours)
+    weights = [array for _, _, pieces in blocks for choices, _ in pieces for array in choices]
     accs = accs or []
 
     def kernel(flag_ref, place_ref, *refs):
-        our_refs, their_refs, refs = refs[:PLANE], refs[PLANE : 2 * PLANE], refs[2 * PLANE :]
+        our_refs, their_refs, refs = refs[:parts], refs[parts : 2 * parts], refs[2 * parts :]
         weight_refs, refs = list(refs[: len(weights)]), refs[len(weights) :]
-        acc_refs, out_refs = refs[: len(accs)], refs[len(accs) : len(accs) + PLANE * len(widths)]
+        acc_refs, out_refs = refs[: len(accs)], refs[len(accs) : len(accs) + parts]
         gated_buf, weight_buf, acc_buf, gated_sems, weight_sems, acc_sem = refs[-6:]
 
-        step = chunk // 2
-
         def target(b, at):
-            start = pl.multiple_of(b * depth + place_ref[at // chunk] * chunk + at % chunk, step)
-            return weight_buf.at[pl.ds(start, step), :]
+            start = pl.multiple_of(b * depth + place_ref[at // chunk] * chunk, chunk)
+            return weight_buf.at[pl.ds(start, chunk), :]
 
         for b, (flag, pick, pieces) in enumerate(blocks):
             row = 0
             for choices, col in pieces:
                 for c in range(len(choices)):
                     ref = weight_refs.pop(0)
-                    for at in range(0, ref.shape[0], step):
-                        source = ref.at[pl.ds(at, step), pl.ds(col, cols)]
+                    for at in range(0, ref.shape[0], chunk):
+                        source = ref.at[pl.ds(at, chunk), pl.ds(col, cols)]
                         copy = pltpu.make_async_copy(source, target(b, row + at), weight_sems.at[b])
                         if pick is None:
                             copy.start()
@@ -201,48 +199,41 @@
                             pl.when(flag_ref[pick] == c)(copy.start)
                 row += choices[0].shape[0]
             half = flag_ref[flag] & 1
-            for r in range(PLANE):
+            for r in range(parts):
                 for c, refs_of in enumerate((our_refs, their_refs)):
                     target_rows = gated_buf.at[b, pl.ds(r * rows, rows), :]
                     copy = pltpu.make_async_copy(refs_of[r].at[half], target_rows, gated_sems.at[b])
                     pl.when(flag_ref[flag] // 2 == c)(copy.start)
-        for at, acc_ref in enumerate(acc_refs):
-            pltpu.make_async_copy(acc_ref, acc_buf.at[at], acc_sem).start()
+        for r, acc_ref in enumerate(acc_refs):
+            pltpu.make_async_copy(acc_ref, acc_buf.at[r], acc_sem).start()
         for b in range(count):
             block = weight_buf.at[pl.ds(b * depth, depth), :]
             pltpu.make_async_copy(block, block, weight_sems.at[b]).wait()
             pltpu.make_async_copy(gated_buf.at[b], gated_buf.at[b], gated_sems.at[b]).wait()
             if accs and not b:
                 pltpu.make_async_copy(acc_buf, acc_buf, acc_sem).wait()
-            first = 0
-            for part, width in enumerate(widths):
-                for col in range(0, width, 2 * LANES):
-                    here = pl.ds(col, 2 * LANES)
-                    made = jnp.dot(
-                        gated_buf[b],
-                        weight_buf[pl.ds(b * depth, depth), pl.ds(first + col, 2 * LANES)],
-                        preferred_element_type=jnp.float32,
-                    )
-                    for r in range(PLANE):
-                        at = part * PLANE + r
-                        total = made[r * rows : (r + 1) * rows]
-                        if b:
-                            total = total + out_refs[at][:, here]
-                        elif accs:
-                            total = total + acc_buf[at, :, here]
-                        out_refs[at][:, here] = total.astype(out_dtype)
-                first += width
+            for col in range(0, cols, 2 * LANES):
+                here = pl.ds(col, 2 * LANES)
+                made = jnp.dot(
+                    gated_buf[b], weight_buf[pl.ds(b * depth, depth), here], preferred_element_type=jnp.float32
+                )
+                for r in range(parts):
+                    total = made[r * rows : (r + 1) * rows]
+                    if b:
+                        total = total + out_refs[r][:, here]
+                    elif accs:
+                        total = total + acc_buf[r, :, here]
+                    out_refs[r][:, here] = total.astype(out_dtype)
 
     smem = pl.BlockSpec(memory_space=pltpu.SMEM)
-    vmem = pl.BlockSpec(memory_space=pltpu.VMEM)
     anywhere = pl.BlockSpec(memory_space=pl.ANY)
-    made = pl.pallas_call(
+    return pl.pallas_call(
         kernel,
-        in_specs=[smem, smem] + [anywhere] * (2 * PLANE + len(weights) + len(accs)),
-        out_specs=[vmem] * (PLANE * len(widths)),
-        out_shape=[jax.ShapeDtypeStruct((rows, width), out_dtype) for width in widths for _ in range(PLANE)],
+        in_specs=[smem, smem] + [anywhere] * (2 * parts + len(weights) + len(accs)),
+        out_specs=[pl.BlockSpec(memory_space=pltpu.VMEM)] * parts,
+        out_shape=[jax.ShapeDtypeStruct((rows, cols), out_dtype)] * parts,
         scratch_shapes=[
-            pltpu.VMEM((count, PLANE * rows, depth), jnp.bfloat16),
+            pltpu.VMEM((count, parts * rows, depth), jnp.bfloat16),
             pltpu.VMEM((count * depth, cols), jnp.bfloat16),
             pltpu.VMEM((len(accs), *accs[0].shape) if accs else (8, LANES), jnp.float32),
             pltpu.SemaphoreType.DMA((count,)),
@@ -251,45 +242,36 @@
         ],
         compiler_params=pltpu.CompilerParams(vmem_limit_bytes=VMEM_BYTES),
         cost_estimate=pl.CostEstimate(
-            flops=2 * PLANE * rows * depth * count * cols,
-            bytes_accessed=2 * count * depth * (PLANE * rows + cols),
+            flops=2 * parts * rows * depth * count * cols,
+            bytes_accessed=2 * count * depth * (parts * rows + cols),
             transcendentals=0,
         ),
         name="product",
     )(flags, places, *ours, *theirs, *weights, *accs)
-    return [list(made[part * PLANE : (part + 1) * PLANE]) for part in range(len(widths))]
-
-
-def assemble(places, parts):
-    rows = parts[0][0].shape[0]
-    widths = [part[0].shape[1] for part in parts]
-    cols = sum(widths)
-    flat = [piece for part in parts for piece in part]
+
+
+def assemble(places, pieces):
+    rows, cols = pieces[0].shape
 
     def kernel(place_ref, *refs):
         *piece_refs, out_ref, sems = refs
         copies = []
-        first = 0
-        for part, width in enumerate(widths):
-            for r in range(PLANE):
-                at = part * PLANE + r
-                start = pl.multiple_of(place_ref[r] * cols + first, LANES)
-                target = out_ref.at[:, pl.ds(start, width)]
-                copies.append(pltpu.make_async_copy(piece_refs[at], target, sems.at[at]))
-                copies[-1].start()
-            first += width
+        for r, piece_ref in enumerate(piece_refs):
+            target = out_ref.at[:, pl.ds(pl.multiple_of(place_ref[r] * cols, cols), cols)]
+            copies.append(pltpu.make_async_copy(piece_ref, target, sems.at[r]))
+            copies[-1].start()
         for copy in copies:
             copy.wait()
 
     return pl.pallas_call(
         kernel,
-        in_specs=[pl.BlockSpec(memory_space=pltpu.SMEM)] + [pl.BlockSpec(memory_space=pltpu.VMEM)] * len(flat),
+        in_specs=[pl.BlockSpec(memory_space=pltpu.SMEM)] + [pl.BlockSpec(memory_space=pltpu.VMEM)] * len(pieces),
         out_specs=pl.BlockSpec(memory_space=pl.ANY),
-        out_shape=jax.ShapeDtypeStruct((rows, cols * PLANE), flat[0].dtype),
-        scratch_shapes=[pltpu.SemaphoreType.DMA((len(flat),))],
+        out_shape=jax.ShapeDtypeStruct((rows, cols * PLANE), pieces[0].dtype),
+        scratch_shapes=[pltpu.SemaphoreType.DMA((len(pieces),))],
         compiler_params=pltpu.CompilerParams(vmem_limit_bytes=16 << 20),
         name="assemble",
-    )(places, *flat)
+    )(places, *pieces)
 
 
 def split_block(q, k, v, residue, rate, skip, w_out):
@@ -345,18 +327,15 @@
     last = shift_ctx(both, PLANE)
     line = last + decay * shift_ctx(both + decay * last, 2 * PLANE)
     enter = before + jnp.exp(-speed * (spot * rows).astype(jnp.float32)) * line
+    f0, w0, enter = tie(f0, w0, enter)
+    out0, mid0 = outward(f0), across(w0)
     gated = gated_conv(q, k, v, rate, residue, skip, enter)
     rest = jnp.concatenate(arrived)
-    gated, rest = tie(gated, rest)
+    gated, rest, out0, mid0 = tie(gated, rest, out0, mid0)
 
     fr, nr = far(rest), near(rest)
     ours = [gated] + [exchange(gated, "ctx", r) for r in range(1, PLANE)]
-    fr, nr, f0, w0, rest, *ours = tie(fr, nr, f0, w0, rest, *ours)
-
-    out0, mid0 = outward(f0), across(w0)
-    theirs = [exchange(x, "ch", 1) for x in ours[1:]]
-    out0, mid0, fr, rest, *held = tie(out0, mid0, fr, rest, *ours, *theirs)
-    ours, theirs = held[:PLANE], held[PLANE:]
+    fr, nr, rest, *ours = tie(fr, nr, rest, *ours)
 
     def source_of(b):
         return jnp.where(b // 2 == core, b & 1, 2 + (b & 1))
@@ -366,19 +345,25 @@
     places = jnp.stack([spot ^ r for r in range(PLANE)]).astype(jnp.int32)
 
     out1, mid1 = outward(fr), across(rest)
-    theirs = [exchange(ours[0], "ch", 1)] + theirs
+    theirs = [exchange(x, "ch", 1) for x in ours]
     blocks = [
         (0, None, [((w0,), 0), ((rest,), 0)]),
         (1, None, [((n0,), 0), ((nr,), 0)]),
         (2, None, [((f0,), 0), ((fr,), 0)]),
     ]
-    (accs,) = product(flags, places, ours, theirs, blocks, None, [cols], jnp.float32)
+    accs = product(flags, places, ours, theirs, blocks, None, jnp.float32)
     out1, mid1, *accs = tie(out1, mid1, *accs)
 
     blocks = [(3, 4, [((out0, mid0), 0), ((out1, mid1), 0)])]
-    (made,) = product(flags, places, ours, theirs, blocks, accs, [cols], jnp.bfloat16)
-    back = [made[0]] + [exchange(made[r], "ctx", r) for r in range(1, PLANE)]
-    return assemble(places, [back])
+
+    def finish(*spots):
+        chosen = [ours[r] for r in spots], [theirs[r] for r in spots]
+        return product(flags, places, *chosen, blocks, [accs[r] for r in spots], jnp.bfloat16)
+
+    (made3,) = finish(3)
+    back3 = exchange(made3, "ctx", 3)
+    back3, made0, made1, made2 = tie(back3, *finish(0, 1, 2))
+    return assemble(places, [made0, exchange(made1, "ctx", 1), exchange(made2, "ctx", 2), back3])
 
 
 def body(q, k, v, residue, rate, skip, w_out):

time: 180 us -> 172 us (0.956)
  waiting for transfers between devices: 92.8 us -> 76.5 us
  Pallas kernels: 33.3 us -> 36.8 us
  starting transfers between devices: 38 us -> 40.3 us
  other arithmetic: 4.35 us -> 6.45 us
    ppermute x19, waiting for transfers between devices: 67.3 us -> 59.5 us  [exchange(): return lax.ppermute(x, axis, [(i, i ^ flip) for i in range(count)])]
    ppermute x2, waiting for transfers between devices: 14.4 us -> 7.44 us  [outward(): return lax.ppermute(x, 'ctx', [(i, i ^ PLANE) for i in middle])]
    ppermute x2, waiting for transfers between devices: 8.59 us -> 5.07 us  [across(): return lax.ppermute(x, 'ctx', [(i, i ^ 3 * PLANE) for i in middle])]
    pallas_call x2 -> x3, Pallas kernels: 18.3 us -> 21.7 us  [product(): pl.pallas_call(kernel, in_specs=[smem, smem] + [anywhere] * (2 * parts +...]
    ppermute x2, waiting for transfers between devices: 2.49 us -> 4.47 us  [shift_ctx(): return lax.ppermute(x, 'ctx', [(i, i + by) for i in range(count - by)])]
    unnamed x47 -> x29, local copies, waits for them, and re-layouts: 4.14 us -> 4.97 us
  transfers between devices with their start and end apart: 25 -> 25, of which waited for: 16 -> 12; matrix products, arithmetic and copies ran while one was open for 4% -> 6% of each run, Pallas kernels for 14% -> 18%
where the time goes in v9:
time: 172 us
  waiting for transfers between devices  76.5 us (44%)
  starting transfers between devices  40.3 us (23%)
  Pallas kernels  36.8 us (21%)
  local copies, waits for them, and re-layouts  11.4 us (7%)
  other arithmetic  6.45 us (4%)
    ppermute x19, waiting for transfers between devices, exchange(): return lax.ppermute(x, axis, [(i, i ^ flip) for i in range(count)])  59.5 us
    pallas_call x3, Pallas kernels, product(): pl.pallas_call(kernel, in_specs=[smem, smem] + [anywhere] * (2 * parts +...  21.7 us
    ppermute x19, starting transfers between devices, exchange(): return lax.ppermute(x, axis, [(i, i ^ flip) for i in range(count)])  21.6 us
    pallas_call x1, Pallas kernels, gated_conv(): pl.pallas_call(conv_kernel, grid=(chan // width,), in_specs=[wide, wide,...  8.36 us
    ppermute x2, waiting for transfers between devices, outward(): return lax.ppermute(x, 'ctx', [(i, i ^ PLANE) for i in middle])  7.44 us
    ppermute x2, starting transfers between devices, across(): return lax.ppermute(x, 'ctx', [(i, i ^ 3 * PLANE) for i in middle])  6.81 us
    ppermute x2, starting transfers between devices, outward(): return lax.ppermute(x, 'ctx', [(i, i ^ PLANE) for i in middle])  5.97 us
    ppermute x2, starting transfers between devices, shift_ctx(): return lax.ppermute(x, 'ctx', [(i, i + by) for i in range(count - by)])  5.94 us
  transfers between devices with their start and end apart: 25, of which 12 were waited for; matrix products, arithmetic and copies ran while one was open for 6% of the time, Pallas kernels for 18%

profile of v9, /device:TPU:8, one launch (start us, length us, event | category | flops | bytes accessed | tf_op | source)
XLA Modules:
  0.0 171.8 jit_solution(9641860565462799459)
XLA Ops:
  1.8 3.0 %collective-permute-start.2 = (bf16[256,768]{1,0:T(8,128)(2,1)}, bf16[256,768]{1,0:T(8,128)(2,1)}, u32[]{:S(2)}, u32[]{:S(2)}) collective-permute-start(bf16[256,768]{1,0:T(8,128)(2,1)} %constant_dynamic-slice_fusion.3.refs_8_), channel_id=1, source_target_pairs={{0,16},{2,18},{4,20},{6,22},{8,24},{10,26},{12,28},{14,30},{16,0},... | collective-permute-start | bytes 1179656 | tf_op jit(solution)/shard_map/ppermute | solution.py:137
  6.5 17.0 %while.12 = (s32[]{:T(128)}, f32[2,16,16,128]{3,2,1,0:T(8,128)}, s32[]{:T(128)}, pred[]{:T(512)}, bf16[256,2048]{1,0:T(8,128)(2,1)}, /*index=5*/bf16[256,2048]{1...) while((s32[]{:T(128)}, f32[2,16,16,128]{3,2,1,0:T(8,128)}, ...), condition=%wide.region_1.2_spmd, body=%wide.region_0.1_spmd.sunk | while | flops 17465344 | bytes 4980932 | solution.py:167
  6.5 5.0 %end_states.3 = f32[16,16,128]{2,1,0:T(8,128)} custom-call(bf16[256,2048]{1,0:T(8,128)(2,1)} %get-tuple-element.295.k_ref, bf16[256,2048]{1,0:T(8,128)(2,1)} %get-tuple-element.296.v_ref, f32[16,2048]{1,0:T(8,128)} %get-tuple-element.297.rate_ref), custom_call_target="tpu_custom_call" | custom-call | flops 16777216 | bytes 2097152 | tf_op jit(solution)/shard_map/while/body/end_states/pallas_call | solution.py:90
  13.0 3.7 %collective-permute-done = f32[16,16,128]{2,1,0:T(8,128)S(1)} collective-permute-done((f32[16,16,128]{2,1,0:T(8,128)}, f32[16,16,128]{2,1,0:T(8,128)S(1)}, u32[]{:S(2)}, u32[]{:S(2)}) %collective-permute-start) | collective-permute-done | bytes 131104 | tf_op jit(solution)/shard_map/while/body/ppermute | solution.py:137
  19.2 3.4 %collective-permute-done.1 = f32[16,16,128]{2,1,0:T(8,128)S(1)} collective-permute-done((f32[16,16,128]{2,1,0:T(8,128)S(1)}, f32[16,16,128]{2,1,0:T(8,128)S(1)}, u32[]{:S(2)}, u32[]{:S(2)}) %collective-permute-start.1) | collective-permute-done | bytes 131104 | tf_op jit(solution)/shard_map/while/body/ppermute | solution.py:137
  26.9 4.5 %collective-permute-done.4 = f32[16,16,128]{2,1,0:T(8,128)S(1)} collective-permute-done((f32[16,16,128]{2,1,0:T(8,128)S(1)}, f32[16,16,128]{2,1,0:T(8,128)S(1)}, u32[]{:S(2)}, u32[]{:S(2)}) %collective-permute-start.4) | collective-permute-done | bytes 131104 | tf_op jit(solution)/shard_map/ppermute | solution.py:132
  32.4 3.6 %collective-permute-start.5 = (f32[16,16,128]{2,1,0:T(8,128)S(1)}, f32[16,16,128]{2,1,0:T(8,128)S(1)}, u32[]{:S(2)}, u32[]{:S(2)}) collective-permute-start(f32[16,16,128]{2,1,0:T(8,128)S(1)} %multiply_add_fusion), channel_id=1, source_target_pairs={{0,16},{2,18},{4,20},{6,22},{8,24},{10,26},{12,28},{14,30},{1,17},... | collective-permute-start | bytes 393224 | tf_op jit(solution)/shard_map/ppermute | solution.py:132
  44.7 3.5 %collective-permute-start.10 = (bf16[256,768]{1,0:T(8,128)(2,1)}, bf16[256,768]{1,0:T(8,128)(2,1)}, u32[]{:S(2)}, u32[]{:S(2)}) collective-permute-start(bf16[256,768]{1,0:T(8,128)(2,1)} %constant_dynamic-slice_fusion.3.refs_8_), channel_id=1, source_target_pairs={{8,16},{10,18},{12,20},{14,22},{16,8},{18,10},{20,12},{22,14},{9,1... | collective-permute-start | bytes 1179656 | tf_op jit(solution)/shard_map/ppermute | solution.py:297
  48.2 8.4 %gated_conv.1.refs_0_ = bf16[2,256,1024]{2,1,0:T(8,128)(2,1)} custom-call(bf16[256,2048]{1,0:T(8,128)(2,1)} %q_ref.1, bf16[256,2048]{1,0:T(8,128)(2,1)S(1)} %copy-done.2, bf16[256,2048]{1,0:T(8,128)(2,1)S(1)} %copy-done.3, f32[16,2048]{1,0:T(8,128)S(1)} %copy-done.4, f32[16,2048]{1,0:T(8,128)} %residue_ref.1, f32[16,128]{1,0:T(8,128)} %bitcast.30, ...), custom_call_target="tpu_custom_call" | custom-call | flops 33554432 | bytes 4194304 | tf_op jit(solution)/shard_map/gated_conv/pallas_call | solution.py:115
  56.6 2.4 %pad_maximum_fusion.1.refs_9_ = bf16[768,768]{1,0:T(8,128)(2,1)} fusion(bf16[256,768]{1,0:T(8,128)(2,1)} %collective-permute-done.8, bf16[256,768]{1,0:T(8,128)(2,1)} %collective-permute-done.7, bf16[256,768]{1,0:T(8,128)(2,1)} %collective-permute-done.6), kind=kLoop, calls=%fused_computation.4 | loop fusion | flops 3538944 | bytes 2359296 | tf_op jit(solution)/shard_map/concatenate | solution.py:333
  61.0 2.4 %collective-permute-start.15 = (bf16[2,256,1024]{2,1,0:T(8,128)(2,1)S(1)}, bf16[2,256,1024]{2,1,0:T(8,128)(2,1)S(1)}, u32[]{:S(2)}, u32[]{:S(2)}) collective-permute-start(bf16[2,256,1024]{2,1,0:T(8,128)(2,1)S(1)} %copy-done.7), channel_id=1, source_target_pairs={{0,6},{2,4},{4,2},{6,0},{8,14},{10,12},{12,10},{14,8},{16,22},{18,... | collective-permute-start | bytes 3145736 | tf_op jit(solution)/shard_map/ppermute | solution.py:137
  64.5 23.5 %collective-permute-done.15.refs_3_.refs_0_ = bf16[2,256,1024]{2,1,0:T(8,128)(2,1)S(1)} collective-permute-done((bf16[2,256,1024]{2,1,0:T(8,128)(2,1)S(1)}, bf16[2,256,1024]{2,1,0:T(8,128)(2,1)S(1)}, u32[]{:S(2)}, u32[]{:S(2)}) %collective-permute-start.15) | collective-permute-done | bytes 1048608 | tf_op jit(solution)/shard_map/ppermute | solution.py:137
  88.0 16.0 %collective-permute-done.14.refs_2_ = bf16[2,256,1024]{2,1,0:T(8,128)(2,1)} collective-permute-done((bf16[2,256,1024]{2,1,0:T(8,128)(2,1)S(1)}, bf16[2,256,1024]{2,1,0:T(8,128)(2,1)}, u32[]{:S(2)}, u32[]{:S(2)}) %collective-permute-start.14) | collective-permute-done | bytes 1048608 | tf_op jit(solution)/shard_map/ppermute | solution.py:137
  105.1 2.4 %collective-permute-done.11.refs_13_ = bf16[768,768]{1,0:T(8,128)(2,1)} collective-permute-done((bf16[768,768]{1,0:T(8,128)(2,1)}, bf16[768,768]{1,0:T(8,128)(2,1)}, u32[]{:S(2)}, u32[]{:S(2)}) %collective-permute-start.11) | collective-permute-done | bytes 1179680 | tf_op jit(solution)/shard_map/ppermute | solution.py:137
  108.6 3.7 %collective-permute-start.17 = (bf16[768,768]{1,0:T(8,128)(2,1)}, bf16[768,768]{1,0:T(8,128)(2,1)S(1)}, u32[]{:S(2)}, u32[]{:S(2)}) collective-permute-start(bf16[768,768]{1,0:T(8,128)(2,1)} %collective-permute-done.11.refs_13_), channel_id=1, source_target_pairs={{8,0},{10,2},{12,4},{14,6},{16,24},{18,26},{20,28},{22,30},{9,1},{... | collective-permute-start | bytes 3538952 | tf_op jit(solution)/shard_map/ppermute | solution.py:300
  113.3 3.3 %collective-permute-start.18 = (bf16[768,768]{1,0:T(8,128)(2,1)}, bf16[768,768]{1,0:T(8,128)(2,1)S(1)}, u32[]{:S(2)}, u32[]{:S(2)}) collective-permute-start(bf16[768,768]{1,0:T(8,128)(2,1)} %pad_maximum_fusion.1.refs_9_), channel_id=1, source_target_pairs={{8,16},{10,18},{12,20},{14,22},{16,8},{18,10},{20,12},{22,14},{9,1... | collective-permute-start | bytes 3538952 | tf_op jit(solution)/shard_map/ppermute | solution.py:297
  118.0 12.4 %product.3 = (f32[256,768]{1,0:T(8,128)}, f32[256,768]{1,0:T(8,128)}, f32[256,768]{1,0:T(8,128)}, f32[256,768]{1,0:T(8,128)}) custom-call(s32[5]{0:T(128)} %stack.58.flag_ref, s32[4]{0:T(128)} %pad_add_fusion.place_ref, bf16[2,256,1024]{2,1,0:T(8,128)(2,1)} %gated_conv.1.refs_0_, bf16[2,256,1024]{2,1,0:T(8,128)(2,1)} %collective-permute-done.13.refs_1_, ...), custom_call_target="tpu_custom_call" | custom-call | flops 4831838208 | bytes 11010048 | tf_op jit(solution)/shard_map/product/pallas_call | solution.py:230
  130.4 7.4 %collective-permute-done.17.refs_4_.refs_8_ = bf16[768,768]{1,0:T(8,128)(2,1)S(1)} collective-permute-done((bf16[768,768]{1,0:T(8,128)(2,1)}, bf16[768,768]{1,0:T(8,128)(2,1)S(1)}, u32[]{:S(2)}, u32[]{:S(2)}) %collective-permute-start.17) | collective-permute-done | bytes 1179680 | tf_op jit(solution)/shard_map/ppermute | solution.py:300
  137.9 5.1 %collective-permute-done.18.refs_5_.refs_9_ = bf16[768,768]{1,0:T(8,128)(2,1)S(1)} collective-permute-done((bf16[768,768]{1,0:T(8,128)(2,1)}, bf16[768,768]{1,0:T(8,128)(2,1)S(1)}, u32[]{:S(2)}, u32[]{:S(2)}) %collective-permute-start.18) | collective-permute-done | bytes 1179680 | tf_op jit(solution)/shard_map/ppermute | solution.py:297
  144.0 3.8 %product.4 = bf16[256,768]{1,0:T(8,128)(2,1)} custom-call(s32[5]{0:T(128)} %stack.58.flag_ref, s32[4]{0:T(128)} %pad_add_fusion.place_ref, bf16[2,256,1024]{2,1,0:T(8,128)(2,1)} %copy-done.10, bf16[2,256,1024]{2,1,0:T(8,128)(2,1)} %copy-done.11, bf16[256,768]{1,0:T(8,128)(2,1)} %copy-done.9, bf16[256,768]{1,0:T(8,128)(2,1)} %collective-permute-done.10.refs_3_.refs_7_, ...), custom_call_target="tpu_custom_call" | custom-call | flops 402653184 | bytes 2097152 | tf_op jit(solution)/shard_map/product/pallas_call | solution.py:230
  147.8 2.5 %collective-permute-start.22 = (bf16[256,768]{1,0:T(8,128)(2,1)}, bf16[256,768]{1,0:T(8,128)(2,1)S(1)}, u32[]{:S(2)}, u32[]{:S(2)}) collective-permute-start(bf16[256,768]{1,0:T(8,128)(2,1)} %product.4), channel_id=1, source_target_pairs={{0,6},{2,4},{4,2},{6,0},{8,14},{10,12},{12,10},{14,8},{16,22},{18,... | collective-permute-start | bytes 1179656 | tf_op jit(solution)/shard_map/ppermute | solution.py:137
  150.3 5.5 %product.5 = (bf16[256,768]{1,0:T(8,128)(2,1)}, bf16[256,768]{1,0:T(8,128)(2,1)}, bf16[256,768]{1,0:T(8,128)(2,1)}) custom-call(s32[5]{0:T(128)} %stack.58.flag_ref, s32[4]{0:T(128)} %pad_add_fusion.place_ref, bf16[2,256,1024]{2,1,0:T(8,128)(2,1)} %gated_conv.1.refs_0_, bf16[2,256,1024]{2,1,0:T(8,128)(2,1)} %collective-permute-done.13.refs_1_, ...), custom_call_target="tpu_custom_call" | custom-call | flops 1207959552 | bytes 3145728 | tf_op jit(solution)/shard_map/product/pallas_call | solution.py:230
  155.8 3.0 %collective-permute-done.22.refs_3_ = bf16[256,768]{1,0:T(8,128)(2,1)S(1)} collective-permute-done((bf16[256,768]{1,0:T(8,128)(2,1)}, bf16[256,768]{1,0:T(8,128)(2,1)S(1)}, u32[]{:S(2)}, u32[]{:S(2)}) %collective-permute-start.22) | collective-permute-done | bytes 393248 | tf_op jit(solution)/shard_map/ppermute | solution.py:137
  161.8 6.1 %collective-permute-done.23.refs_1_ = bf16[256,768]{1,0:T(8,128)(2,1)S(1)} collective-permute-done((bf16[256,768]{1,0:T(8,128)(2,1)}, bf16[256,768]{1,0:T(8,128)(2,1)S(1)}, u32[]{:S(2)}, u32[]{:S(2)}) %collective-permute-start.23) | collective-permute-done | bytes 393248 | tf_op jit(solution)/shard_map/ppermute | solution.py:137
  (74 shorter events, 36.8 us)
Async XLA Ops:
  1.8 21.7 %collective-permute-start.3 = (bf16[256,768]{1,0:T(8,128)(2,1)}, bf16[256,768]{1,0:T(8,128)(2,1)S(1)}, u32[]{:S(2)}, u32[]{:S(2)}) collective-permute-start(bf16[256,768]{1,0:T(8,128)(2,1)} %constant_dynamic-slice_fusion.3.refs_8_), channel_id=1, source_target_pairs={{0,8},{2,10},{4,12},{6,14},{8,0},{10,2},{12,4},{14,6},{16,24},{18,... | collective-permute-start | bytes 1179656 | tf_op jit(solution)/shard_map/ppermute | solution.py:137
  1.8 21.7 %collective-permute-start.2 = (bf16[256,768]{1,0:T(8,128)(2,1)}, bf16[256,768]{1,0:T(8,128)(2,1)}, u32[]{:S(2)}, u32[]{:S(2)}) collective-permute-start(bf16[256,768]{1,0:T(8,128)(2,1)} %constant_dynamic-slice_fusion.3.refs_8_), channel_id=1, source_target_pairs={{0,16},{2,18},{4,20},{6,22},{8,24},{10,26},{12,28},{14,30},{16,0},... | collective-permute-start | bytes 1179656 | tf_op jit(solution)/shard_map/ppermute | solution.py:137
  11.5 5.2 %collective-permute-start = (f32[16,16,128]{2,1,0:T(8,128)}, f32[16,16,128]{2,1,0:T(8,128)S(1)}, u32[]{:S(2)}, u32[]{:S(2)}) collective-permute-start(f32[16,16,128]{2,1,0:T(8,128)} %end_states.3), channel_id=1, source_target_pairs={{0,2},{2,0},{4,6},{6,4},{8,10},{10,8},{12,14},{14,12},{16,18},{18,... | collective-permute-start | bytes 393224 | tf_op jit(solution)/shard_map/while/body/ppermute | solution.py:137
  17.6 5.0 %collective-permute-start.1 = (f32[16,16,128]{2,1,0:T(8,128)S(1)}, f32[16,16,128]{2,1,0:T(8,128)S(1)}, u32[]{:S(2)}, u32[]{:S(2)}) collective-permute-start(f32[16,16,128]{2,1,0:T(8,128)S(1)} %add_select_fusion.2), channel_id=1, source_target_pairs={{0,4},{2,6},{4,0},{6,2},{8,12},{10,14},{12,8},{14,10},{16,20},{18,... | collective-permute-start | bytes 393224 | tf_op jit(solution)/shard_map/while/body/ppermute | solution.py:137
  24.5 6.9 %collective-permute-start.4 = (f32[16,16,128]{2,1,0:T(8,128)S(1)}, f32[16,16,128]{2,1,0:T(8,128)S(1)}, u32[]{:S(2)}, u32[]{:S(2)}) collective-permute-start(f32[16,16,128]{2,1,0:T(8,128)S(1)} %slice_bitcast_fusion), channel_id=1, source_target_pairs={{0,8},{2,10},{4,12},{6,14},{8,16},{10,18},{12,20},{14,22},{16,24},... | collective-permute-start | bytes 393224 | tf_op jit(solution)/shard_map/ppermute | solution.py:132
  32.4 9.3 %collective-permute-start.5 = (f32[16,16,128]{2,1,0:T(8,128)S(1)}, f32[16,16,128]{2,1,0:T(8,128)S(1)}, u32[]{:S(2)}, u32[]{:S(2)}) collective-permute-start(f32[16,16,128]{2,1,0:T(8,128)S(1)} %multiply_add_fusion), channel_id=1, source_target_pairs={{0,16},{2,18},{4,20},{6,22},{8,24},{10,26},{12,28},{14,30},{1,17},... | collective-permute-start | bytes 393224 | tf_op jit(solution)/shard_map/ppermute | solution.py:132
  38.2 18.4 %collective-permute-start.6 = (bf16[256,768]{1,0:T(8,128)(2,1)}, bf16[256,768]{1,0:T(8,128)(2,1)}, u32[]{:S(2)}, u32[]{:S(2)}) collective-permute-start(bf16[256,768]{1,0:T(8,128)(2,1)} %get-tuple-element.226), channel_id=1, source_target_pairs={{0,2},{2,0},{4,6},{6,4},{8,10},{10,8},{12,14},{14,12},{16,18},{18,... | collective-permute-start | bytes 1179656 | tf_op jit(solution)/shard_map/ppermute | solution.py:137
  39.7 16.9 %collective-permute-start.8 = (bf16[256,768]{1,0:T(8,128)(2,1)}, bf16[256,768]{1,0:T(8,128)(2,1)}, u32[]{:S(2)}, u32[]{:S(2)}) collective-permute-start(bf16[256,768]{1,0:T(8,128)(2,1)} %get-tuple-element.227), channel_id=1, source_target_pairs={{0,6},{2,4},{4,2},{6,0},{8,14},{10,12},{12,10},{14,8},{16,22},{18,... | collective-permute-start | bytes 1179656 | tf_op jit(solution)/shard_map/ppermute | solution.py:137
  41.1 15.4 %collective-permute-start.7 = (bf16[256,768]{1,0:T(8,128)(2,1)S(1)}, bf16[256,768]{1,0:T(8,128)(2,1)}, u32[]{:S(2)}, u32[]{:S(2)}) collective-permute-start(bf16[256,768]{1,0:T(8,128)(2,1)S(1)} %get-tuple-element.228), channel_id=1, source_target_pairs={{0,4},{2,6},{4,0},{6,2},{8,12},{10,14},{12,8},{14,10},{16,20},{18,... | collective-permute-start | bytes 1179656 | tf_op jit(solution)/shard_map/ppermute | solution.py:137
  42.4 16.6 %collective-permute-start.9 = (bf16[256,768]{1,0:T(8,128)(2,1)}, bf16[256,768]{1,0:T(8,128)(2,1)S(1)}, u32[]{:S(2)}, u32[]{:S(2)}) collective-permute-start(bf16[256,768]{1,0:T(8,128)(2,1)} %collective-permute-done.2.refs_12_), channel_id=1, source_target_pairs={{8,0},{10,2},{12,4},{14,6},{16,24},{18,26},{20,28},{22,30},{9,1},{... | collective-permute-start | bytes 1179656 | tf_op jit(solution)/shard_map/ppermute | solution.py:300
  44.7 14.3 %collective-permute-start.10 = (bf16[256,768]{1,0:T(8,128)(2,1)}, bf16[256,768]{1,0:T(8,128)(2,1)}, u32[]{:S(2)}, u32[]{:S(2)}) collective-permute-start(bf16[256,768]{1,0:T(8,128)(2,1)} %constant_dynamic-slice_fusion.3.refs_8_), channel_id=1, source_target_pairs={{8,16},{10,18},{12,20},{14,22},{16,8},{18,10},{20,12},{22,14},{9,1... | collective-permute-start | bytes 1179656 | tf_op jit(solution)/shard_map/ppermute | solution.py:297
  59.0 45.1 %collective-permute-start.12 = (bf16[768,768]{1,0:T(8,128)(2,1)}, bf16[768,768]{1,0:T(8,128)(2,1)S(1)}, u32[]{:S(2)}, u32[]{:S(2)}) collective-permute-start(bf16[768,768]{1,0:T(8,128)(2,1)} %pad_maximum_fusion.1.refs_9_), channel_id=1, source_target_pairs={{0,8},{2,10},{4,12},{6,14},{8,0},{10,2},{12,4},{14,6},{16,24},{18,... | collective-permute-start | bytes 3538952 | tf_op jit(solution)/shard_map/ppermute | solution.py:137
  59.3 48.2 %collective-permute-start.11 = (bf16[768,768]{1,0:T(8,128)(2,1)}, bf16[768,768]{1,0:T(8,128)(2,1)}, u32[]{:S(2)}, u32[]{:S(2)}) collective-permute-start(bf16[768,768]{1,0:T(8,128)(2,1)} %pad_maximum_fusion.1.refs_9_), channel_id=1, source_target_pairs={{0,16},{2,18},{4,20},{6,22},{8,24},{10,26},{12,28},{14,30},{16,0},... | collective-permute-start | bytes 3538952 | tf_op jit(solution)/shard_map/ppermute | solution.py:137
  61.0 27.0 %collective-permute-start.15 = (bf16[2,256,1024]{2,1,0:T(8,128)(2,1)S(1)}, bf16[2,256,1024]{2,1,0:T(8,128)(2,1)S(1)}, u32[]{:S(2)}, u32[]{:S(2)}) collective-permute-start(bf16[2,256,1024]{2,1,0:T(8,128)(2,1)S(1)} %copy-done.7), channel_id=1, source_target_pairs={{0,6},{2,4},{4,2},{6,0},{8,14},{10,12},{12,10},{14,8},{16,22},{18,... | collective-permute-start | bytes 3145736 | tf_op jit(solution)/shard_map/ppermute | solution.py:137
  63.4 40.6 %collective-permute-start.14 = (bf16[2,256,1024]{2,1,0:T(8,128)(2,1)S(1)}, bf16[2,256,1024]{2,1,0:T(8,128)(2,1)}, u32[]{:S(2)}, u32[]{:S(2)}) collective-permute-start(bf16[2,256,1024]{2,1,0:T(8,128)(2,1)S(1)} %copy-done.7), channel_id=1, source_target_pairs={{0,4},{2,6},{4,0},{6,2},{8,12},{10,14},{12,8},{14,10},{16,20},{18,... | collective-permute-start | bytes 3145736 | tf_op jit(solution)/shard_map/ppermute | solution.py:137
  63.9 40.2 %collective-permute-start.13 = (bf16[2,256,1024]{2,1,0:T(8,128)(2,1)S(1)}, bf16[2,256,1024]{2,1,0:T(8,128)(2,1)}, u32[]{:S(2)}, u32[]{:S(2)}) collective-permute-start(bf16[2,256,1024]{2,1,0:T(8,128)(2,1)S(1)} %copy-done.7), channel_id=1, source_target_pairs={{0,2},{2,0},{4,6},{6,4},{8,10},{10,8},{12,14},{14,12},{16,18},{18,... | collective-permute-start | bytes 3145736 | tf_op jit(solution)/shard_map/ppermute | solution.py:137
  107.5 10.5 %collective-permute-start.19 = (bf16[2,256,1024]{2,1,0:T(8,128)(2,1)S(1)}, bf16[2,256,1024]{2,1,0:T(8,128)(2,1)}, u32[]{:S(2)}, u32[]{:S(2)}) collective-permute-start(bf16[2,256,1024]{2,1,0:T(8,128)(2,1)S(1)} %copy-done.7), channel_id=1, source_target_pairs={{0,1},{1,0},{2,3},{3,2},{4,5},{5,4},{6,7},{7,6},{8,9},{9,8},{10,11... | collective-permute-start | bytes 3145736 | tf_op jit(solution)/shard_map/ppermute | solution.py:137
  108.1 10.0 %collective-permute-start.20 = (bf16[2,256,1024]{2,1,0:T(8,128)(2,1)}, bf16[2,256,1024]{2,1,0:T(8,128)(2,1)}, u32[]{:S(2)}, u32[]{:S(2)}) collective-permute-start(bf16[2,256,1024]{2,1,0:T(8,128)(2,1)} %collective-permute-done.13.refs_1_), channel_id=1, source_target_pairs={{0,1},{1,0},{2,3},{3,2},{4,5},{5,4},{6,7},{7,6},{8,9},{9,8},{10,11... | collective-permute-start | bytes 3145736 | tf_op jit(solution)/shard_map/ppermute | solution.py:137
  108.1 10.0 %collective-permute-start.21 = (bf16[2,256,1024]{2,1,0:T(8,128)(2,1)}, bf16[2,256,1024]{2,1,0:T(8,128)(2,1)}, u32[]{:S(2)}, u32[]{:S(2)}) collective-permute-start(bf16[2,256,1024]{2,1,0:T(8,128)(2,1)} %collective-permute-done.14.refs_2_), channel_id=1, source_target_pairs={{0,1},{1,0},{2,3},{3,2},{4,5},{5,4},{6,7},{7,6},{8,9},{9,8},{10,11... | collective-permute-start | bytes 3145736 | tf_op jit(solution)/shard_map/ppermute | solution.py:137
  108.6 29.3 %collective-permute-start.17 = (bf16[768,768]{1,0:T(8,128)(2,1)}, bf16[768,768]{1,0:T(8,128)(2,1)S(1)}, u32[]{:S(2)}, u32[]{:S(2)}) collective-permute-start(bf16[768,768]{1,0:T(8,128)(2,1)} %collective-permute-done.11.refs_13_), channel_id=1, source_target_pairs={{8,0},{10,2},{12,4},{14,6},{16,24},{18,26},{20,28},{22,30},{9,1},{... | collective-permute-start | bytes 3538952 | tf_op jit(solution)/shard_map/ppermute | solution.py:300
  113.3 29.7 %collective-permute-start.18 = (bf16[768,768]{1,0:T(8,128)(2,1)}, bf16[768,768]{1,0:T(8,128)(2,1)S(1)}, u32[]{:S(2)}, u32[]{:S(2)}) collective-permute-start(bf16[768,768]{1,0:T(8,128)(2,1)} %pad_maximum_fusion.1.refs_9_), channel_id=1, source_target_pairs={{8,16},{10,18},{12,20},{14,22},{16,8},{18,10},{20,12},{22,14},{9,1... | collective-permute-start | bytes 3538952 | tf_op jit(solution)/shard_map/ppermute | solution.py:297
  147.8 11.0 %collective-permute-start.22 = (bf16[256,768]{1,0:T(8,128)(2,1)}, bf16[256,768]{1,0:T(8,128)(2,1)S(1)}, u32[]{:S(2)}, u32[]{:S(2)}) collective-permute-start(bf16[256,768]{1,0:T(8,128)(2,1)} %product.4), channel_id=1, source_target_pairs={{0,6},{2,4},{4,2},{6,0},{8,14},{10,12},{12,10},{14,8},{16,22},{18,... | collective-permute-start | bytes 1179656 | tf_op jit(solution)/shard_map/ppermute | solution.py:137
  158.8 9.1 %collective-permute-start.23 = (bf16[256,768]{1,0:T(8,128)(2,1)}, bf16[256,768]{1,0:T(8,128)(2,1)S(1)}, u32[]{:S(2)}, u32[]{:S(2)}) collective-permute-start(bf16[256,768]{1,0:T(8,128)(2,1)} %get-tuple-element.201), channel_id=1, source_target_pairs={{0,2},{2,0},{4,6},{6,4},{8,10},{10,8},{12,14},{14,12},{16,18},{18,... | collective-permute-start | bytes 1179656 | tf_op jit(solution)/shard_map/ppermute | solution.py:137
  160.3 8.9 %collective-permute-start.24 = (bf16[256,768]{1,0:T(8,128)(2,1)}, bf16[256,768]{1,0:T(8,128)(2,1)S(1)}, u32[]{:S(2)}, u32[]{:S(2)}) collective-permute-start(bf16[256,768]{1,0:T(8,128)(2,1)} %get-tuple-element.202), channel_id=1, source_target_pairs={{0,4},{2,6},{4,0},{6,2},{8,12},{10,14},{12,8},{14,10},{16,20},{18,... | collective-permute-start | bytes 1179656 | tf_op jit(solution)/shard_map/ppermute | solution.py:137
  (15 other events, 190.8 us)

commit v10 on v9

--- a/solution.py
+++ b/solution.py
@@ -167,18 +167,19 @@
     return lax.fori_loop(0, once, run, empty)
 
 
-def product(flags, places, ours, theirs, blocks, accs, out_dtype):
+def product(flags, places, ours, theirs, blocks, accs, widths, out_dtype):
     _, rows, depth = ours[0].shape
     chunk = depth // PLANE
-    cols = blocks[0][2][0][0][0].shape[1]
+    cols = sum(widths)
     count, parts = len(blocks), len(ours)
+    outs = parts * len(widths)
     weights = [array for _, _, pieces in blocks for choices, _ in pieces for array in choices]
     accs = accs or []
 
     def kernel(flag_ref, place_ref, *refs):
         our_refs, their_refs, refs = refs[:parts], refs[parts : 2 * parts], refs[2 * parts :]
         weight_refs, refs = list(refs[: len(weights)]), refs[len(weights) :]
-        acc_refs, out_refs = refs[: len(accs)], refs[len(accs) : len(accs) + parts]
+        acc_refs, out_refs = refs[: len(accs)], refs[len(accs) : len(accs) + outs]
         gated_buf, weight_buf, acc_buf, gated_sems, weight_sems, acc_sem = refs[-6:]
 
         def target(b, at):
@@ -217,21 +218,24 @@
                 made = jnp.dot(
                     gated_buf[b], weight_buf[pl.ds(b * depth, depth), here], preferred_element_type=jnp.float32
                 )
+                part = 0 if col < widths[0] else 1
+                inside = pl.ds(col - part * widths[0], 2 * LANES)
                 for r in range(parts):
                     total = made[r * rows : (r + 1) * rows]
+                    out_ref = out_refs[part * parts + r]
                     if b:
-                        total = total + out_refs[r][:, here]
+                        total = total + out_ref[:, inside]
                     elif accs:
                         total = total + acc_buf[r, :, here]
-                    out_refs[r][:, here] = total.astype(out_dtype)
+                    out_ref[:, inside] = total.astype(out_dtype)
 
     smem = pl.BlockSpec(memory_space=pltpu.SMEM)
     anywhere = pl.BlockSpec(memory_space=pl.ANY)
-    return pl.pallas_call(
+    made = pl.pallas_call(
         kernel,
         in_specs=[smem, smem] + [anywhere] * (2 * parts + len(weights) + len(accs)),
-        out_specs=[pl.BlockSpec(memory_space=pltpu.VMEM)] * parts,
-        out_shape=[jax.ShapeDtypeStruct((rows, cols), out_dtype)] * parts,
+        out_specs=[pl.BlockSpec(memory_space=pltpu.VMEM)] * outs,
+        out_shape=[jax.ShapeDtypeStruct((rows, width), out_dtype) for width in widths for _ in range(parts)],
         scratch_shapes=[
             pltpu.VMEM((count, parts * rows, depth), jnp.bfloat16),
             pltpu.VMEM((count * depth, cols), jnp.bfloat16),
@@ -248,30 +252,39 @@
         ),
         name="product",
     )(flags, places, *ours, *theirs, *weights, *accs)
-
-
-def assemble(places, pieces):
-    rows, cols = pieces[0].shape
+    return [list(made[at : at + parts]) for at in range(0, outs, parts)]
+
+
+def assemble(places, parts):
+    rows = parts[0][0].shape[0]
+    widths = [part[0].shape[1] for part in parts]
+    cols = sum(widths)
+    flat = [piece for part in parts for piece in part]
 
     def kernel(place_ref, *refs):
         *piece_refs, out_ref, sems = refs
         copies = []
-        for r, piece_ref in enumerate(piece_refs):
-            target = out_ref.at[:, pl.ds(pl.multiple_of(place_ref[r] * cols, cols), cols)]
-            copies.append(pltpu.make_async_copy(piece_ref, target, sems.at[r]))
-            copies[-1].start()
+        first = 0
+        for part, width in enumerate(widths):
+            for r in range(PLANE):
+                at = part * PLANE + r
+                start = pl.multiple_of(place_ref[r] * cols + first, LANES)
+                target = out_ref.at[:, pl.ds(start, width)]
+                copies.append(pltpu.make_async_copy(piece_refs[at], target, sems.at[at]))
+                copies[-1].start()
+            first += width
         for copy in copies:
             copy.wait()
 
     return pl.pallas_call(
         kernel,
-        in_specs=[pl.BlockSpec(memory_space=pltpu.SMEM)] + [pl.BlockSpec(memory_space=pltpu.VMEM)] * len(pieces),
+        in_specs=[pl.BlockSpec(memory_space=pltpu.SMEM)] + [pl.BlockSpec(memory_space=pltpu.VMEM)] * len(flat),
         out_specs=pl.BlockSpec(memory_space=pl.ANY),
-        out_shape=jax.ShapeDtypeStruct((rows, cols * PLANE), pieces[0].dtype),
-        scratch_shapes=[pltpu.SemaphoreType.DMA((len(pieces),))],
+        out_shape=jax.ShapeDtypeStruct((rows, cols * PLANE), flat[0].dtype),
+        scratch_shapes=[pltpu.SemaphoreType.DMA((len(flat),))],
         compiler_params=pltpu.CompilerParams(vmem_limit_bytes=16 << 20),
         name="assemble",
-    )(places, *pieces)
+    )(places, *flat)
 
 
 def split_block(q, k, v, residue, rate, skip, w_out):
@@ -283,6 +296,7 @@
     count = lax.axis_size("ctx")
     chunk, feats = w_out.shape
     cols = feats // PLANE
+    wide = 2 * cols // 3
     speed = rate.reshape(modes, chan // LANES, LANES)
 
     def far(x):
@@ -316,12 +330,12 @@
         return jnp.stack([both, before])
 
     x_later, y_later = (spot & 1) != 0, (spot & 2) != 0
-    w0, w_out = tie(group(w_out, 0), w_out)
+    w0, w1, w2, w3 = tie(*[group(w_out, r) for r in range(PLANE)])
     f0, n0 = far(w0), near(w0)
     scanned = box(plane_scan, k, v, rate, speed)
-    f0, n0, w0, scanned, w_out = tie(f0, n0, w0, scanned, w_out)
-
-    arrived = [exchange(group(w_out, r), "ctx", r) for r in range(1, PLANE)]
+    f0, n0, w0, w1, w2, w3, scanned = tie(f0, n0, w0, w1, w2, w3, scanned)
+
+    arrived = [exchange(w, "ctx", r + 1) for r, w in enumerate((w1, w2, w3))]
     both, before = scanned[0], scanned[1]
     decay = jnp.exp(-speed * float(PLANE * rows))
     last = shift_ctx(both, PLANE)
@@ -335,7 +349,8 @@
 
     fr, nr = far(rest), near(rest)
     ours = [gated] + [exchange(gated, "ctx", r) for r in range(1, PLANE)]
-    fr, nr, rest, *ours = tie(fr, nr, rest, *ours)
+    restA, restB = rest[:, :wide], rest[:, wide:]
+    fr, nr, rest, restA, restB, *ours = tie(fr, nr, rest, restA, restB, *ours)
 
     def source_of(b):
         return jnp.where(b // 2 == core, b & 1, 2 + (b & 1))
@@ -344,26 +359,25 @@
     flags = jnp.stack([source_of(plane ^ r) for r in range(4)] + [is_middle]).astype(jnp.int32)
     places = jnp.stack([spot ^ r for r in range(PLANE)]).astype(jnp.int32)
 
-    out1, mid1 = outward(fr), across(rest)
+    outA, midA = outward(fr[:, :wide]), across(restA)
     theirs = [exchange(x, "ch", 1) for x in ours]
     blocks = [
         (0, None, [((w0,), 0), ((rest,), 0)]),
         (1, None, [((n0,), 0), ((nr,), 0)]),
         (2, None, [((f0,), 0), ((fr,), 0)]),
     ]
-    accs = product(flags, places, ours, theirs, blocks, None, jnp.float32)
-    out1, mid1, *accs = tie(out1, mid1, *accs)
-
-    blocks = [(3, 4, [((out0, mid0), 0), ((out1, mid1), 0)])]
-
-    def finish(*spots):
-        chosen = [ours[r] for r in spots], [theirs[r] for r in spots]
-        return product(flags, places, *chosen, blocks, [accs[r] for r in spots], jnp.bfloat16)
-
-    (made3,) = finish(3)
-    back3 = exchange(made3, "ctx", 3)
-    back3, made0, made1, made2 = tie(back3, *finish(0, 1, 2))
-    return assemble(places, [made0, exchange(made1, "ctx", 1), exchange(made2, "ctx", 2), back3])
+    accA, accB = product(flags, places, ours, theirs, blocks, None, [wide, cols - wide], jnp.float32)
+    outA, midA, fr, restB, *accs = tie(outA, midA, fr, restB, *accA, *accB)
+    accA, accB = accs[:PLANE], accs[PLANE:]
+
+    outB, midB = outward(fr[:, wide:]), across(restB)
+
+    def finish(first, out1, mid1, accs):
+        blocks = [(3, 4, [((out0, mid0), first), ((out1, mid1), 0)])]
+        (made,) = product(flags, places, ours, theirs, blocks, accs, [accs[0].shape[1]], jnp.bfloat16)
+        return [made[0]] + [exchange(made[r], "ctx", r) for r in range(1, PLANE)]
+
+    return assemble(places, [finish(0, outA, midA, accA), finish(wide, outB, midB, accB)])
 
 
 def body(q, k, v, residue, rate, skip, w_out):
@@ -377,7 +391,7 @@
         and cores == 2
         and chan == 8 * chunk
         and chunk % LANES == 0
-        and feats % (2 * PLANE * LANES) == 0
+        and feats % (6 * PLANE * LANES) == 0
     )
     skip = skip.reshape(groups, LANES)
     if split:

time: 172 us -> 171 us (level)
  starting transfers between devices: 40.3 us -> 43.6 us
  waiting for transfers between devices: 76.5 us -> 73.2 us
    ppermute x2 -> x3, waiting for transfers between devices: 7.44 us -> 0.39 us  [outward(): return lax.ppermute(x, 'ctx', [(i, i ^ PLANE) for i in middle])]
    slice x0 -> x4, local copies, waits for them, and re-layouts: none -> 4.02 us  [the longest x2 1.73 us: split_block(): restA, restB = (rest[:, :wide], rest[:, wide:])]
    ppermute x19 -> x22, waiting for transfers between devices: 59.5 us -> 62.8 us  [exchange(): return lax.ppermute(x, axis, [(i, i ^ flip) for i in range(count)])]
    ppermute x19 -> x22, starting transfers between devices: 21.6 us -> 23.5 us  [exchange(): return lax.ppermute(x, axis, [(i, i ^ flip) for i in range(count)])]
    unnamed x29 -> x39, local copies, waits for them, and re-layouts: 4.97 us -> 3.25 us
    dynamic_slice x2 -> x1, local copies, waits for them, and re-layouts: 3.98 us -> 2.57 us  [group(): return lax.dynamic_slice_in_dim(x, (spot ^ r) * cols, cols, axis=1)]
    ppermute x2 -> x3, starting transfers between devices: 6.81 us -> 7.31 us  [across(): return lax.ppermute(x, 'ctx', [(i, i ^ 3 * PLANE) for i in middle])]
    ppermute x2 -> x3, starting transfers between devices: 5.97 us -> 5.71 us  [outward(): return lax.ppermute(x, 'ctx', [(i, i ^ PLANE) for i in middle])]
  transfers between devices with their start and end apart: 25 -> 30, of which waited for: 12 -> 17; matrix products, arithmetic and copies ran while one was open for 6% -> 5% of each run, Pallas kernels for 18% -> 20%
where the time goes in v10:
time: 171 us; the launch traced here: 170 us
  waiting for transfers between devices  73.2 us (43%)
  starting transfers between devices  43.6 us (25%)
  Pallas kernels  35.2 us (21%)
  local copies, waits for them, and re-layouts  12.1 us (7%)
  other arithmetic  5.97 us (3%)
    ppermute x22, waiting for transfers between devices, exchange(): return lax.ppermute(x, axis, [(i, i ^ flip) for i in range(count)])  62.8 us
    ppermute x22, starting transfers between devices, exchange(): return lax.ppermute(x, axis, [(i, i ^ flip) for i in range(count)])  23.5 us
    pallas_call x3, Pallas kernels, product(): pl.pallas_call(kernel, in_specs=[smem, smem] + [anywhere] * (2 * parts +...  21.1 us
    pallas_call x1, Pallas kernels, gated_conv(): pl.pallas_call(conv_kernel, grid=(chan // width,), in_specs=[wide, wide,...  8.36 us
    ppermute x3, starting transfers between devices, across(): return lax.ppermute(x, 'ctx', [(i, i ^ 3 * PLANE) for i in middle])  7.31 us
    ppermute x2, starting transfers between devices, shift_ctx(): return lax.ppermute(x, 'ctx', [(i, i + by) for i in range(count - by)])  7.06 us
    ppermute x3, starting transfers between devices, outward(): return lax.ppermute(x, 'ctx', [(i, i ^ PLANE) for i in middle])  5.71 us
    ppermute x3, waiting for transfers between devices, across(): return lax.ppermute(x, 'ctx', [(i, i ^ 3 * PLANE) for i in middle])  5.24 us
  transfers between devices with their start and end apart: 30, of which 17 were waited for; matrix products, arithmetic and copies ran while one was open for 5% of the time, Pallas kernels for 20%

profile of v10, /device:TPU:8, one launch (start us, length us, event | category | flops | bytes accessed | tf_op | source)
XLA Modules:
  0.0 170.5 jit_solution(7159656200211797428)
XLA Ops:
  0.0 2.6 %constant_dynamic-slice_fusion = (bf16[256,768]{1,0:T(8,128)(2,1)}, bf16[256,768]{1,0:T(8,128)(2,1)}, bf16[256,768]{1,0:T(8,128)(2,1)S(1)}, bf16[256,768]{1,0:T(8,128)(2,1)}) fusion(bf16[256,3072]{1,0:T(8,128)(2,1)} %param.15, s32[]{:T(128)S(6)} %select_n.94, s32[]{:T(128)S(6)} %select_n.92, s32[]{:T(128)S(6)} %select_n.91, s32[]{:T(128)S(6)} %select_n.93), kind=kLoop, calls=%fused_computation.9 | loop fusion | bytes 3145744 | tf_op jit(solution)/shard_map/dynamic_slice | solution.py:317
  2.6 2.6 %collective-permute-start.2 = (bf16[256,768]{1,0:T(8,128)(2,1)S(1)}, bf16[256,768]{1,0:T(8,128)(2,1)S(1)}, u32[]{:S(2)}, u32[]{:S(2)}) collective-permute-start(bf16[256,768]{1,0:T(8,128)(2,1)S(1)} %get-tuple-element.195.refs_8_), channel_id=1, source_target_pairs={{0,16},{2,18},{4,20},{6,22},{8,24},{10,26},{12,28},{14,30},{16,0},... | collective-permute-start | bytes 1179656 | tf_op jit(solution)/shard_map/ppermute | solution.py:137
  6.4 16.0 %while.12 = (s32[]{:T(128)}, f32[2,16,16,128]{3,2,1,0:T(8,128)}, s32[]{:T(128)}, pred[]{:T(512)}, bf16[256,2048]{1,0:T(8,128)(2,1)S(1)}, /*index=5*/bf16[256,204...) while((s32[]{:T(128)}, f32[2,16,16,128]{3,2,1,0:T(8,128)}, ...), condition=%wide.region_1.2_spmd, body=%wide.region_0.1_spmd.sunk | while | flops 17465344 | bytes 4980932 | solution.py:167
  6.4 4.0 %end_states.3 = f32[16,16,128]{2,1,0:T(8,128)} custom-call(bf16[256,2048]{1,0:T(8,128)(2,1)S(1)} %get-tuple-element.330.k_ref, bf16[256,2048]{1,0:T(8,128)(2,1)S(1)} %get-tuple-element.331.v_ref, f32[16,2048]{1,0:T(8,128)S(1)} %get-tuple-element.332.rate_ref), custom_call_target="tpu_custom_call" | custom-call | flops 16777216 | bytes 2097152 | tf_op jit(solution)/shard_map/while/body/end_states/pallas_call | solution.py:90
  11.9 3.7 %collective-permute-done = f32[16,16,128]{2,1,0:T(8,128)S(1)} collective-permute-done((f32[16,16,128]{2,1,0:T(8,128)}, f32[16,16,128]{2,1,0:T(8,128)S(1)}, u32[]{:S(2)}, u32[]{:S(2)}) %collective-permute-start) | collective-permute-done | bytes 131104 | tf_op jit(solution)/shard_map/while/body/ppermute | solution.py:137
  18.1 3.4 %collective-permute-done.1 = f32[16,16,128]{2,1,0:T(8,128)S(1)} collective-permute-done((f32[16,16,128]{2,1,0:T(8,128)S(1)}, f32[16,16,128]{2,1,0:T(8,128)S(1)}, u32[]{:S(2)}, u32[]{:S(2)}) %collective-permute-start.1) | collective-permute-done | bytes 131104 | tf_op jit(solution)/shard_map/while/body/ppermute | solution.py:137
  23.9 2.4 %collective-permute-start.4 = (f32[16,16,128]{2,1,0:T(8,128)S(1)}, f32[16,16,128]{2,1,0:T(8,128)S(1)}, u32[]{:S(2)}, u32[]{:S(2)}) collective-permute-start(f32[16,16,128]{2,1,0:T(8,128)S(1)} %slice_bitcast_fusion), channel_id=1, source_target_pairs={{0,8},{2,10},{4,12},{6,14},{8,16},{10,18},{12,20},{14,22},{16,24},... | collective-permute-start | bytes 393224 | tf_op jit(solution)/shard_map/ppermute | solution.py:132
  26.3 4.5 %collective-permute-done.4 = f32[16,16,128]{2,1,0:T(8,128)S(1)} collective-permute-done((f32[16,16,128]{2,1,0:T(8,128)S(1)}, f32[16,16,128]{2,1,0:T(8,128)S(1)}, u32[]{:S(2)}, u32[]{:S(2)}) %collective-permute-start.4) | collective-permute-done | bytes 131104 | tf_op jit(solution)/shard_map/ppermute | solution.py:132
  31.7 4.7 %collective-permute-start.5 = (f32[16,16,128]{2,1,0:T(8,128)S(1)}, f32[16,16,128]{2,1,0:T(8,128)S(1)}, u32[]{:S(2)}, u32[]{:S(2)}) collective-permute-start(f32[16,16,128]{2,1,0:T(8,128)S(1)} %multiply_add_fusion), channel_id=1, source_target_pairs={{0,16},{2,18},{4,20},{6,22},{8,24},{10,26},{12,28},{14,30},{1,17},... | collective-permute-start | bytes 393224 | tf_op jit(solution)/shard_map/ppermute | solution.py:132
  41.9 2.0 %collective-permute-start.10 = (bf16[256,768]{1,0:T(8,128)(2,1)}, bf16[256,768]{1,0:T(8,128)(2,1)S(1)}, u32[]{:S(2)}, u32[]{:S(2)}) collective-permute-start(bf16[256,768]{1,0:T(8,128)(2,1)} %copy-done.17), channel_id=1, source_target_pairs={{8,16},{10,18},{12,20},{14,22},{16,8},{18,10},{20,12},{22,14},{9,1... | collective-permute-start | bytes 1179656 | tf_op jit(solution)/shard_map/ppermute | solution.py:311
  45.2 8.4 %gated_conv.1.refs_0_ = bf16[2,256,1024]{2,1,0:T(8,128)(2,1)} custom-call(bf16[256,2048]{1,0:T(8,128)(2,1)} %q_ref.1, bf16[256,2048]{1,0:T(8,128)(2,1)S(1)} %get-tuple-element.375, bf16[256,2048]{1,0:T(8,128)(2,1)S(1)} %get-tuple-element.376, f32[16,2048]{1,0:T(8,128)S(1)} %get-tuple-element.385, f32[16,2048]{1,0:T(8,128)} %residue_ref.1, ...), custom_call_target="tpu_custom_call" | custom-call | flops 33554432 | bytes 4194304 | tf_op jit(solution)/shard_map/gated_conv/pallas_call | solution.py:115
  53.6 2.7 %collective-permute-done.7 = bf16[256,768]{1,0:T(8,128)(2,1)S(1)} collective-permute-done((bf16[256,768]{1,0:T(8,128)(2,1)}, bf16[256,768]{1,0:T(8,128)(2,1)S(1)}, u32[]{:S(2)}, u32[]{:S(2)}) %collective-permute-start.7) | collective-permute-done | bytes 393248 | tf_op jit(solution)/shard_map/ppermute | solution.py:137
  64.8 21.0 %collective-permute-done.13.refs_1_ = bf16[2,256,1024]{2,1,0:T(8,128)(2,1)} collective-permute-done((bf16[2,256,1024]{2,1,0:T(8,128)(2,1)S(1)}, bf16[2,256,1024]{2,1,0:T(8,128)(2,1)}, u32[]{:S(2)}, u32[]{:S(2)}) %collective-permute-start.13) | collective-permute-done | bytes 1048608 | tf_op jit(solution)/shard_map/ppermute | solution.py:137
  85.8 21.5 %collective-permute-done.14.refs_2_ = bf16[2,256,1024]{2,1,0:T(8,128)(2,1)} collective-permute-done((bf16[2,256,1024]{2,1,0:T(8,128)(2,1)S(1)}, bf16[2,256,1024]{2,1,0:T(8,128)(2,1)}, u32[]{:S(2)}, u32[]{:S(2)}) %collective-permute-start.14) | collective-permute-done | bytes 1048608 | tf_op jit(solution)/shard_map/ppermute | solution.py:137
  108.2 2.1 %collective-permute-done.12.refs_11_ = bf16[768,768]{1,0:T(8,128)(2,1)} collective-permute-done((bf16[768,768]{1,0:T(8,128)(2,1)S(1)}, bf16[768,768]{1,0:T(8,128)(2,1)}, u32[]{:S(2)}, u32[]{:S(2)}) %collective-permute-start.12) | collective-permute-done | bytes 1179680 | tf_op jit(solution)/shard_map/ppermute | solution.py:137
  112.3 3.1 %collective-permute-start.20 = (bf16[768,512]{1,0:T(8,128)(2,1)}, bf16[768,512]{1,0:T(8,128)(2,1)S(1)}, u32[]{:S(2)}, u32[]{:S(2)}) collective-permute-start(bf16[768,512]{1,0:T(8,128)(2,1)} %slice.22), channel_id=1, source_target_pairs={{8,0},{10,2},{12,4},{14,6},{16,24},{18,26},{20,28},{22,30},{9,1},{... | collective-permute-start | bytes 2359304 | tf_op jit(solution)/shard_map/ppermute | solution.py:314
  116.4 2.6 %collective-permute-start.21 = (bf16[768,512]{1,0:T(8,128)(2,1)}, bf16[768,512]{1,0:T(8,128)(2,1)S(1)}, u32[]{:S(2)}, u32[]{:S(2)}) collective-permute-start(bf16[768,512]{1,0:T(8,128)(2,1)} %slice.20), channel_id=1, source_target_pairs={{8,16},{10,18},{12,20},{14,22},{16,8},{18,10},{20,12},{22,14},{9,1... | collective-permute-start | bytes 2359304 | tf_op jit(solution)/shard_map/ppermute | solution.py:311
  120.4 11.8 %product.3 = (f32[256,512]{1,0:T(8,128)}, f32[256,512]{1,0:T(8,128)}, f32[256,512]{1,0:T(8,128)}, f32[256,512]{1,0:T(8,128)}, f32[256,256]{1,0:T(8,128)}, /*inde...) custom-call(s32[5]{0:T(128)} %stack.58.flag_ref, s32[4]{0:T(128)} %pad_add_fusion.place_ref, ...), custom_call_target="tpu_custom_call" | custom-call | flops 4831838208 | bytes 11010048 | tf_op jit(solution)/shard_map/product/pallas_call | solution.py:234
  132.6 5.0 %collective-permute-done.21.refs_11_ = bf16[768,512]{1,0:T(8,128)(2,1)S(1)} collective-permute-done((bf16[768,512]{1,0:T(8,128)(2,1)}, bf16[768,512]{1,0:T(8,128)(2,1)S(1)}, u32[]{:S(2)}, u32[]{:S(2)}) %collective-permute-start.21) | collective-permute-done | bytes 786464 | tf_op jit(solution)/shard_map/ppermute | solution.py:311
  140.3 2.7 %collective-permute-start.26 = (bf16[768,256]{1,0:T(8,128)(2,1)S(1)}, bf16[768,256]{1,0:T(8,128)(2,1)S(1)}, u32[]{:S(2)}, u32[]{:S(2)}) collective-permute-start(bf16[768,256]{1,0:T(8,128)(2,1)S(1)} %copy-done.16), channel_id=1, source_target_pairs={{8,16},{10,18},{12,20},{14,22},{16,8},{18,10},{20,12},{22,14},{9,1... | collective-permute-start | bytes 1179656 | tf_op jit(solution)/shard_map/ppermute | solution.py:311
  143.0 5.2 %product.4 = (bf16[256,512]{1,0:T(8,128)(2,1)}, bf16[256,512]{1,0:T(8,128)(2,1)}, bf16[256,512]{1,0:T(8,128)(2,1)}, bf16[256,512]{1,0:T(8,128)(2,1)}) custom-call(s32[5]{0:T(128)} %stack.58.flag_ref, s32[4]{0:T(128)} %pad_add_fusion.place_ref, bf16[2,256,1024]{2,1,0:T(8,128)(2,1)} %gated_conv.1.refs_0_, ...), custom_call_target="tpu_custom_call" | custom-call | flops 1073741824 | bytes 3145728 | tf_op jit(solution)/shard_map/product/pallas_call | solution.py:234
  153.3 4.1 %product.5 = (bf16[256,256]{1,0:T(8,128)(2,1)}, bf16[256,256]{1,0:T(8,128)(2,1)}, bf16[256,256]{1,0:T(8,128)(2,1)}, bf16[256,256]{1,0:T(8,128)(2,1)}) custom-call(s32[5]{0:T(128)} %stack.58.flag_ref, s32[4]{0:T(128)} %pad_add_fusion.place_ref, bf16[2,256,1024]{2,1,0:T(8,128)(2,1)} %gated_conv.1.refs_0_, ...), custom_call_target="tpu_custom_call" | custom-call | flops 536870912 | bytes 2621440 | tf_op jit(solution)/shard_map/product/pallas_call | solution.py:234
  161.0 2.3 %collective-permute-done.23.refs_2_ = bf16[256,512]{1,0:T(8,128)(2,1)S(1)} collective-permute-done((bf16[256,512]{1,0:T(8,128)(2,1)}, bf16[256,512]{1,0:T(8,128)(2,1)S(1)}, u32[]{:S(2)}, u32[]{:S(2)}) %collective-permute-start.23) | collective-permute-done | bytes 262176 | tf_op jit(solution)/shard_map/ppermute | solution.py:137
  165.2 2.6 %collective-permute-done.28.refs_6_ = bf16[256,256]{1,0:T(8,128)(2,1)S(1)} collective-permute-done((bf16[256,256]{1,0:T(8,128)(2,1)}, bf16[256,256]{1,0:T(8,128)(2,1)S(1)}, u32[]{:S(2)}, u32[]{:S(2)}) %collective-permute-start.28) | collective-permute-done | bytes 131104 | tf_op jit(solution)/shard_map/ppermute | solution.py:137
  (97 shorter events, 45.2 us)
Async XLA Ops:
  2.6 19.8 %collective-permute-start.2 = (bf16[256,768]{1,0:T(8,128)(2,1)S(1)}, bf16[256,768]{1,0:T(8,128)(2,1)S(1)}, u32[]{:S(2)}, u32[]{:S(2)}) collective-permute-start(bf16[256,768]{1,0:T(8,128)(2,1)S(1)} %get-tuple-element.195.refs_8_), channel_id=1, source_target_pairs={{0,16},{2,18},{4,20},{6,22},{8,24},{10,26},{12,28},{14,30},{16,0},... | collective-permute-start | bytes 1179656 | tf_op jit(solution)/shard_map/ppermute | solution.py:137
  5.2 17.9 %collective-permute-start.3 = (bf16[256,768]{1,0:T(8,128)(2,1)S(1)}, bf16[256,768]{1,0:T(8,128)(2,1)}, u32[]{:S(2)}, u32[]{:S(2)}) collective-permute-start(bf16[256,768]{1,0:T(8,128)(2,1)S(1)} %get-tuple-element.195.refs_8_), channel_id=1, source_target_pairs={{0,8},{2,10},{4,12},{6,14},{8,0},{10,2},{12,4},{14,6},{16,24},{18,... | collective-permute-start | bytes 1179656 | tf_op jit(solution)/shard_map/ppermute | solution.py:137
  31.7 8.6 %collective-permute-start.5 = (f32[16,16,128]{2,1,0:T(8,128)S(1)}, f32[16,16,128]{2,1,0:T(8,128)S(1)}, u32[]{:S(2)}, u32[]{:S(2)}) collective-permute-start(f32[16,16,128]{2,1,0:T(8,128)S(1)} %multiply_add_fusion), channel_id=1, source_target_pairs={{0,16},{2,18},{4,20},{6,22},{8,24},{10,26},{12,28},{14,30},{1,17},... | collective-permute-start | bytes 393224 | tf_op jit(solution)/shard_map/ppermute | solution.py:132
  36.5 17.1 %collective-permute-start.6 = (bf16[256,768]{1,0:T(8,128)(2,1)}, bf16[256,768]{1,0:T(8,128)(2,1)S(1)}, u32[]{:S(2)}, u32[]{:S(2)}) collective-permute-start(bf16[256,768]{1,0:T(8,128)(2,1)} %get-tuple-element.191), channel_id=1, source_target_pairs={{0,2},{2,0},{4,6},{6,4},{8,10},{10,8},{12,14},{14,12},{16,18},{18,... | collective-permute-start | bytes 1179656 | tf_op jit(solution)/shard_map/ppermute | solution.py:137
  38.0 18.3 %collective-permute-start.7 = (bf16[256,768]{1,0:T(8,128)(2,1)}, bf16[256,768]{1,0:T(8,128)(2,1)S(1)}, u32[]{:S(2)}, u32[]{:S(2)}) collective-permute-start(bf16[256,768]{1,0:T(8,128)(2,1)} %get-tuple-element.192), channel_id=1, source_target_pairs={{0,4},{2,6},{4,0},{6,2},{8,12},{10,14},{12,8},{14,10},{16,20},{18,... | collective-permute-start | bytes 1179656 | tf_op jit(solution)/shard_map/ppermute | solution.py:137
  39.5 16.8 %collective-permute-start.8 = (bf16[256,768]{1,0:T(8,128)(2,1)}, bf16[256,768]{1,0:T(8,128)(2,1)}, u32[]{:S(2)}, u32[]{:S(2)}) collective-permute-start(bf16[256,768]{1,0:T(8,128)(2,1)} %get-tuple-element.193), channel_id=1, source_target_pairs={{0,6},{2,4},{4,2},{6,0},{8,14},{10,12},{12,10},{14,8},{16,22},{18,... | collective-permute-start | bytes 1179656 | tf_op jit(solution)/shard_map/ppermute | solution.py:137
  41.9 15.5 %collective-permute-start.10 = (bf16[256,768]{1,0:T(8,128)(2,1)}, bf16[256,768]{1,0:T(8,128)(2,1)S(1)}, u32[]{:S(2)}, u32[]{:S(2)}) collective-permute-start(bf16[256,768]{1,0:T(8,128)(2,1)} %copy-done.17), channel_id=1, source_target_pairs={{8,16},{10,18},{12,20},{14,22},{16,8},{18,10},{20,12},{22,14},{9,1... | collective-permute-start | bytes 1179656 | tf_op jit(solution)/shard_map/ppermute | solution.py:311
  43.9 13.5 %collective-permute-start.9 = (bf16[256,768]{1,0:T(8,128)(2,1)}, bf16[256,768]{1,0:T(8,128)(2,1)S(1)}, u32[]{:S(2)}, u32[]{:S(2)}) collective-permute-start(bf16[256,768]{1,0:T(8,128)(2,1)} %copy-done.18), channel_id=1, source_target_pairs={{8,0},{10,2},{12,4},{14,6},{16,24},{18,26},{20,28},{22,30},{9,1},{... | collective-permute-start | bytes 1179656 | tf_op jit(solution)/shard_map/ppermute | solution.py:314
  57.4 50.8 %collective-permute-start.11 = (bf16[768,768]{1,0:T(8,128)(2,1)S(1)}, bf16[768,768]{1,0:T(8,128)(2,1)S(1)}, u32[]{:S(2)}, u32[]{:S(2)}) collective-permute-start(bf16[768,768]{1,0:T(8,128)(2,1)S(1)} %pad_maximum_fusion.1.refs_9_), channel_id=1, source_target_pairs={{0,16},{2,18},{4,20},{6,22},{8,24},{10,26},{12,28},{14,30},{16,0},... | collective-permute-start | bytes 3538952 | tf_op jit(solution)/shard_map/ppermute | solution.py:137
  58.8 51.5 %collective-permute-start.12 = (bf16[768,768]{1,0:T(8,128)(2,1)S(1)}, bf16[768,768]{1,0:T(8,128)(2,1)}, u32[]{:S(2)}, u32[]{:S(2)}) collective-permute-start(bf16[768,768]{1,0:T(8,128)(2,1)S(1)} %pad_maximum_fusion.1.refs_9_), channel_id=1, source_target_pairs={{0,8},{2,10},{4,12},{6,14},{8,0},{10,2},{12,4},{14,6},{16,24},{18,... | collective-permute-start | bytes 3538952 | tf_op jit(solution)/shard_map/ppermute | solution.py:137
  59.6 26.2 %collective-permute-start.13 = (bf16[2,256,1024]{2,1,0:T(8,128)(2,1)S(1)}, bf16[2,256,1024]{2,1,0:T(8,128)(2,1)}, u32[]{:S(2)}, u32[]{:S(2)}) collective-permute-start(bf16[2,256,1024]{2,1,0:T(8,128)(2,1)S(1)} %copy-done.5), channel_id=1, source_target_pairs={{0,2},{2,0},{4,6},{6,4},{8,10},{10,8},{12,14},{14,12},{16,18},{18,... | collective-permute-start | bytes 3145736 | tf_op jit(solution)/shard_map/ppermute | solution.py:137
  61.1 46.2 %collective-permute-start.14 = (bf16[2,256,1024]{2,1,0:T(8,128)(2,1)S(1)}, bf16[2,256,1024]{2,1,0:T(8,128)(2,1)}, u32[]{:S(2)}, u32[]{:S(2)}) collective-permute-start(bf16[2,256,1024]{2,1,0:T(8,128)(2,1)S(1)} %copy-done.5), channel_id=1, source_target_pairs={{0,4},{2,6},{4,0},{6,2},{8,12},{10,14},{12,8},{14,10},{16,20},{18,... | collective-permute-start | bytes 3145736 | tf_op jit(solution)/shard_map/ppermute | solution.py:137
  62.6 44.7 %collective-permute-start.15 = (bf16[2,256,1024]{2,1,0:T(8,128)(2,1)S(1)}, bf16[2,256,1024]{2,1,0:T(8,128)(2,1)}, u32[]{:S(2)}, u32[]{:S(2)}) collective-permute-start(bf16[2,256,1024]{2,1,0:T(8,128)(2,1)S(1)} %copy-done.5), channel_id=1, source_target_pairs={{0,6},{2,4},{4,2},{6,0},{8,14},{10,12},{12,10},{14,8},{16,22},{18,... | collective-permute-start | bytes 3145736 | tf_op jit(solution)/shard_map/ppermute | solution.py:137
  110.3 10.1 %collective-permute-start.17 = (bf16[2,256,1024]{2,1,0:T(8,128)(2,1)}, bf16[2,256,1024]{2,1,0:T(8,128)(2,1)}, u32[]{:S(2)}, u32[]{:S(2)}) collective-permute-start(bf16[2,256,1024]{2,1,0:T(8,128)(2,1)} %collective-permute-done.13.refs_1_), channel_id=1, source_target_pairs={{0,1},{1,0},{2,3},{3,2},{4,5},{5,4},{6,7},{7,6},{8,9},{9,8},{10,11... | collective-permute-start | bytes 3145736 | tf_op jit(solution)/shard_map/ppermute | solution.py:137
  110.8 9.6 %collective-permute-start.18 = (bf16[2,256,1024]{2,1,0:T(8,128)(2,1)}, bf16[2,256,1024]{2,1,0:T(8,128)(2,1)}, u32[]{:S(2)}, u32[]{:S(2)}) collective-permute-start(bf16[2,256,1024]{2,1,0:T(8,128)(2,1)} %collective-permute-done.14.refs_2_), channel_id=1, source_target_pairs={{0,1},{1,0},{2,3},{3,2},{4,5},{5,4},{6,7},{7,6},{8,9},{9,8},{10,11... | collective-permute-start | bytes 3145736 | tf_op jit(solution)/shard_map/ppermute | solution.py:137
  110.8 9.6 %collective-permute-start.19 = (bf16[2,256,1024]{2,1,0:T(8,128)(2,1)}, bf16[2,256,1024]{2,1,0:T(8,128)(2,1)}, u32[]{:S(2)}, u32[]{:S(2)}) collective-permute-start(bf16[2,256,1024]{2,1,0:T(8,128)(2,1)} %collective-permute-done.15.refs_3_), channel_id=1, source_target_pairs={{0,1},{1,0},{2,3},{3,2},{4,5},{5,4},{6,7},{7,6},{8,9},{9,8},{10,11... | collective-permute-start | bytes 3145736 | tf_op jit(solution)/shard_map/ppermute | solution.py:137
  112.3 20.3 %collective-permute-start.20 = (bf16[768,512]{1,0:T(8,128)(2,1)}, bf16[768,512]{1,0:T(8,128)(2,1)S(1)}, u32[]{:S(2)}, u32[]{:S(2)}) collective-permute-start(bf16[768,512]{1,0:T(8,128)(2,1)} %slice.22), channel_id=1, source_target_pairs={{8,0},{10,2},{12,4},{14,6},{16,24},{18,26},{20,28},{22,30},{9,1},{... | collective-permute-start | bytes 2359304 | tf_op jit(solution)/shard_map/ppermute | solution.py:314
  116.4 21.3 %collective-permute-start.21 = (bf16[768,512]{1,0:T(8,128)(2,1)}, bf16[768,512]{1,0:T(8,128)(2,1)S(1)}, u32[]{:S(2)}, u32[]{:S(2)}) collective-permute-start(bf16[768,512]{1,0:T(8,128)(2,1)} %slice.20), channel_id=1, source_target_pairs={{8,16},{10,18},{12,20},{14,22},{16,8},{18,10},{20,12},{22,14},{9,1... | collective-permute-start | bytes 2359304 | tf_op jit(solution)/shard_map/ppermute | solution.py:311
  138.9 12.9 %collective-permute-start.25 = (bf16[768,256]{1,0:T(8,128)(2,1)S(1)}, bf16[768,256]{1,0:T(8,128)(2,1)S(1)}, u32[]{:S(2)}, u32[]{:S(2)}) collective-permute-start(bf16[768,256]{1,0:T(8,128)(2,1)S(1)} %slice.23), channel_id=1, source_target_pairs={{8,0},{10,2},{12,4},{14,6},{16,24},{18,26},{20,28},{22,30},{9,1},{... | collective-permute-start | bytes 1179656 | tf_op jit(solution)/shard_map/ppermute | solution.py:314
  140.3 11.7 %collective-permute-start.26 = (bf16[768,256]{1,0:T(8,128)(2,1)S(1)}, bf16[768,256]{1,0:T(8,128)(2,1)S(1)}, u32[]{:S(2)}, u32[]{:S(2)}) collective-permute-start(bf16[768,256]{1,0:T(8,128)(2,1)S(1)} %copy-done.16), channel_id=1, source_target_pairs={{8,16},{10,18},{12,20},{14,22},{16,8},{18,10},{20,12},{22,14},{9,1... | collective-permute-start | bytes 1179656 | tf_op jit(solution)/shard_map/ppermute | solution.py:311
  148.2 12.2 %collective-permute-start.22 = (bf16[256,512]{1,0:T(8,128)(2,1)}, bf16[256,512]{1,0:T(8,128)(2,1)S(1)}, u32[]{:S(2)}, u32[]{:S(2)}) collective-permute-start(bf16[256,512]{1,0:T(8,128)(2,1)} %get-tuple-element.225), channel_id=1, source_target_pairs={{0,2},{2,0},{4,6},{6,4},{8,10},{10,8},{12,14},{14,12},{16,18},{18,... | collective-permute-start | bytes 786440 | tf_op jit(solution)/shard_map/ppermute | solution.py:137
  149.8 13.5 %collective-permute-start.23 = (bf16[256,512]{1,0:T(8,128)(2,1)}, bf16[256,512]{1,0:T(8,128)(2,1)S(1)}, u32[]{:S(2)}, u32[]{:S(2)}) collective-permute-start(bf16[256,512]{1,0:T(8,128)(2,1)} %get-tuple-element.226), channel_id=1, source_target_pairs={{0,4},{2,6},{4,0},{6,2},{8,12},{10,14},{12,8},{14,10},{16,20},{18,... | collective-permute-start | bytes 786440 | tf_op jit(solution)/shard_map/ppermute | solution.py:137
  151.3 13.1 %collective-permute-start.24 = (bf16[256,512]{1,0:T(8,128)(2,1)}, bf16[256,512]{1,0:T(8,128)(2,1)S(1)}, u32[]{:S(2)}, u32[]{:S(2)}) collective-permute-start(bf16[256,512]{1,0:T(8,128)(2,1)} %get-tuple-element.227), channel_id=1, source_target_pairs={{0,6},{2,4},{4,2},{6,0},{8,14},{10,12},{12,10},{14,8},{16,22},{18,... | collective-permute-start | bytes 786440 | tf_op jit(solution)/shard_map/ppermute | solution.py:137
  159.0 8.8 %collective-permute-start.28 = (bf16[256,256]{1,0:T(8,128)(2,1)}, bf16[256,256]{1,0:T(8,128)(2,1)S(1)}, u32[]{:S(2)}, u32[]{:S(2)}) collective-permute-start(bf16[256,256]{1,0:T(8,128)(2,1)} %get-tuple-element.236), channel_id=1, source_target_pairs={{0,4},{2,6},{4,0},{6,2},{8,12},{10,14},{12,8},{14,10},{16,20},{18,... | collective-permute-start | bytes 393224 | tf_op jit(solution)/shard_map/ppermute | solution.py:137
  (25 other events, 323.5 us)

commit v11 on v10

--- a/solution.py
+++ b/solution.py
@@ -27,7 +27,7 @@
         out_ref[pl.ds(g, modes, stride=groups), :] = ref[:, pl.ds(g * LANES, LANES)]
 
 
-def ends_kernel(k_ref, v_ref, rate_ref, end_ref, sig_ref, mode_ref):
+def ends_kernel(k_ref, v_ref, rate_ref, end_ref, speed_ref, sig_ref, mode_ref):
     rows, width = k_ref.shape
     modes, groups, _ = end_ref.shape
     spread_signal(k_ref, v_ref, sig_ref)
@@ -42,6 +42,7 @@
     state = lax.fori_loop(0, rows, step, (zero,) * modes, unroll=8)
     for m in range(modes):
         end_ref[m] = state[m]
+        speed_ref[m] = mode_ref[pl.ds(m * groups, groups), :]
 
 
 def conv_kernel(q_ref, k_ref, v_ref, rate_ref, residue_ref, skip_ref, enter_ref, out_ref, sig_ref, conv_ref, mode_ref, weight_ref):
@@ -91,8 +92,8 @@
         ends_kernel,
         grid=(chan // width,),
         in_specs=[wide, wide, moded],
-        out_specs=state,
-        out_shape=jax.ShapeDtypeStruct((modes, chan // LANES, LANES), jnp.float32),
+        out_specs=[state, state],
+        out_shape=[jax.ShapeDtypeStruct((modes, chan // LANES, LANES), jnp.float32)] * 2,
         scratch_shapes=[
             pltpu.VMEM((rows * width // LANES, LANES), jnp.float32),
             pltpu.VMEM((modes * width // LANES, LANES), jnp.float32),
@@ -223,11 +224,12 @@
                 for r in range(parts):
                     total = made[r * rows : (r + 1) * rows]
                     out_ref = out_refs[part * parts + r]
-                    if b:
-                        total = total + out_ref[:, inside]
-                    elif accs:
+                    if b or accs:
                         total = total + acc_buf[r, :, here]
-                    out_ref[:, inside] = total.astype(out_dtype)
+                    if b < count - 1:
+                        acc_buf[r, :, here] = total
+                    else:
+                        out_ref[:, inside] = total.astype(out_dtype)
 
     smem = pl.BlockSpec(memory_space=pltpu.SMEM)
     anywhere = pl.BlockSpec(memory_space=pl.ANY)
@@ -239,7 +241,7 @@
         scratch_shapes=[
             pltpu.VMEM((count, parts * rows, depth), jnp.bfloat16),
             pltpu.VMEM((count * depth, cols), jnp.bfloat16),
-            pltpu.VMEM((len(accs), *accs[0].shape) if accs else (8, LANES), jnp.float32),
+            pltpu.VMEM((parts, rows, cols), jnp.float32),
             pltpu.SemaphoreType.DMA((count,)),
             pltpu.SemaphoreType.DMA((count,)),
             pltpu.SemaphoreType.DMA,
@@ -289,7 +291,6 @@
 
 def split_block(q, k, v, residue, rate, skip, w_out):
     rows, chan = q.shape
-    modes = rate.shape[0]
     me = lax.axis_index("ctx")
     core = lax.axis_index("ch")
     spot, plane = me & (PLANE - 1), me // PLANE
@@ -297,7 +298,6 @@
     chunk, feats = w_out.shape
     cols = feats // PLANE
     wide = 2 * cols // 3
-    speed = rate.reshape(modes, chan // LANES, LANES)
 
     def far(x):
         return exchange(x, "ctx", 2 * PLANE)
@@ -316,35 +316,34 @@
     def group(x, r):
         return lax.dynamic_slice_in_dim(x, (spot ^ r) * cols, cols, axis=1)
 
-    def plane_scan(k, v, rate, speed):
-        def fade(span):
-            return jnp.exp(-speed * span)
-
-        ends = end_states(k, v, rate)
-        other = exchange(ends, "ctx", 1)
-        both = jnp.where(x_later, fade(float(rows)) * other + ends, fade(float(rows)) * ends + other)
-        before = jnp.where(x_later, other, 0.0)
-        other = exchange(both, "ctx", 2)
-        before = before + jnp.where(y_later, fade((spot & 1).astype(jnp.float32) * rows) * other, 0.0)
-        both = jnp.where(y_later, fade(2.0 * rows) * other + both, fade(2.0 * rows) * both + other)
-        return jnp.stack([both, before])
-
-    x_later, y_later = (spot & 1) != 0, (spot & 2) != 0
+    def plane_scan(k, v, rate):
+        ends, speed = end_states(k, v, rate)
+        found = [ends] + [exchange(ends, "ctx", r) for r in range(1, PLANE)]
+        total, before = jnp.zeros_like(ends), jnp.zeros_like(ends)
+        for r, state in enumerate(found):
+            place = spot ^ r
+            total = total + jnp.exp(-speed * ((PLANE - 1 - place) * rows).astype(jnp.float32)) * state
+            if r:
+                gap = jnp.maximum(spot - 1 - place, 0)
+                faded = jnp.exp(-speed * (gap * rows).astype(jnp.float32)) * state
+                before = before + jnp.where(place < spot, faded, 0.0)
+        return jnp.stack([total, before, speed])
+
     w0, w1, w2, w3 = tie(*[group(w_out, r) for r in range(PLANE)])
     f0, n0 = far(w0), near(w0)
-    scanned = box(plane_scan, k, v, rate, speed)
+    scanned = box(plane_scan, k, v, rate)
     f0, n0, w0, w1, w2, w3, scanned = tie(f0, n0, w0, w1, w2, w3, scanned)
 
     arrived = [exchange(w, "ctx", r + 1) for r, w in enumerate((w1, w2, w3))]
-    both, before = scanned[0], scanned[1]
+    both, before, speed = scanned[0], scanned[1], scanned[2]
     decay = jnp.exp(-speed * float(PLANE * rows))
     last = shift_ctx(both, PLANE)
     line = last + decay * shift_ctx(both + decay * last, 2 * PLANE)
     enter = before + jnp.exp(-speed * (spot * rows).astype(jnp.float32)) * line
-    f0, w0, enter = tie(f0, w0, enter)
+    rest = jnp.concatenate(arrived)
+    f0, w0, enter, rest = tie(f0, w0, enter, rest)
     out0, mid0 = outward(f0), across(w0)
     gated = gated_conv(q, k, v, rate, residue, skip, enter)
-    rest = jnp.concatenate(arrived)
     gated, rest, out0, mid0 = tie(gated, rest, out0, mid0)
 
     fr, nr = far(rest), near(rest)
@@ -366,18 +365,18 @@
         (1, None, [((n0,), 0), ((nr,), 0)]),
         (2, None, [((f0,), 0), ((fr,), 0)]),
     ]
-    accA, accB = product(flags, places, ours, theirs, blocks, None, [wide, cols - wide], jnp.float32)
-    outA, midA, fr, restB, *accs = tie(outA, midA, fr, restB, *accA, *accB)
-    accA, accB = accs[:PLANE], accs[PLANE:]
+    (accs,) = product(flags, places, ours, theirs, blocks, None, [wide], jnp.float32)
+    outA, midA, fr, restB, *accs = tie(outA, midA, fr, restB, *accs)
 
     outB, midB = outward(fr[:, wide:]), across(restB)
-
-    def finish(first, out1, mid1, accs):
-        blocks = [(3, 4, [((out0, mid0), first), ((out1, mid1), 0)])]
-        (made,) = product(flags, places, ours, theirs, blocks, accs, [accs[0].shape[1]], jnp.bfloat16)
-        return [made[0]] + [exchange(made[r], "ctx", r) for r in range(1, PLANE)]
-
-    return assemble(places, [finish(0, outA, midA, accA), finish(wide, outB, midB, accB)])
+    last = (3, 4, [((out0, mid0), 0), ((outA, midA), 0)])
+    (madeA,) = product(flags, places, ours, theirs, [last], accs, [wide], jnp.bfloat16)
+    backA = [madeA[0]] + [exchange(madeA[r], "ctx", r) for r in range(1, PLANE)]
+    blocks = [(flag, pick, [(arrays, wide) for arrays, _ in pieces]) for flag, pick, pieces in blocks]
+    blocks.append((3, 4, [((out0, mid0), wide), ((outB, midB), 0)]))
+    (madeB,) = product(flags, places, ours, theirs, blocks, None, [cols - wide], jnp.bfloat16)
+    backB = [madeB[0]] + [exchange(madeB[r], "ctx", r) for r in range(1, PLANE)]
+    return assemble(places, [backA, backB])
 
 
 def body(q, k, v, residue, rate, skip, w_out):
@@ -396,7 +395,7 @@
     skip = skip.reshape(groups, LANES)
     if split:
         return split_block(q, k, v, residue, rate, skip, w_out)
-    ends = end_states(k, v, rate)
+    ends, _ = end_states(k, v, rate)
     enter = entering_states(ends, rate.reshape(modes, groups, LANES), rows)
     gated = gated_conv(q, k, v, rate, residue, skip, enter)
     gated = gated.transpose(1, 0, 2).reshape(rows, chan)

time: 171 us -> 177 us (1.035)
  starting transfers between devices: 43.6 us -> 50.4 us
  waiting for transfers between devices: 73.2 us -> 71 us
  other arithmetic: 5.97 us -> 8.16 us
    ppermute x22 -> x23, waiting for transfers between devices: 62.8 us -> 57.7 us  [exchange(): return lax.ppermute(x, axis, [(i, i ^ flip) for i in range(count)])]
    ppermute x3, starting transfers between devices: 7.31 us -> 11.2 us  [across(): return lax.ppermute(x, 'ctx', [(i, i ^ 3 * PLANE) for i in middle])]
    ppermute x3, waiting for transfers between devices: 0.39 us -> 3.93 us  [outward(): return lax.ppermute(x, 'ctx', [(i, i ^ PLANE) for i in middle])]
    another operation x2, other arithmetic: 0.81 us -> 2.81 us  [plane_scan(): return jnp.stack([total, before, speed])]
    ppermute x22 -> x23, starting transfers between devices: 23.5 us -> 24.2 us  [exchange(): return lax.ppermute(x, axis, [(i, i ^ flip) for i in range(count)])]
  transfers between devices with their start and end apart: 30 -> 31, of which waited for: 17 -> 15; matrix products, arithmetic and copies ran while one was open for 5% -> 6% of each run, Pallas kernels for 20% -> 19%
where the time goes in v11:
time: 177 us
  waiting for transfers between devices  71 us (40%)
  starting transfers between devices  50.4 us (28%)
  Pallas kernels  35.6 us (20%)
  local copies, waits for them, and re-layouts  11.2 us (6%)
  other arithmetic  8.16 us (5%)
    ppermute x23, waiting for transfers between devices, exchange(): return lax.ppermute(x, axis, [(i, i ^ flip) for i in range(count)])  57.7 us
    ppermute x23, starting transfers between devices, exchange(): return lax.ppermute(x, axis, [(i, i ^ flip) for i in range(count)])  24.2 us
    pallas_call x3, Pallas kernels, product(): pl.pallas_call(kernel, in_specs=[smem, smem] + [anywhere] * (2 * parts +...  21.4 us
    ppermute x3, starting transfers between devices, across(): return lax.ppermute(x, 'ctx', [(i, i ^ 3 * PLANE) for i in middle])  11.2 us
    pallas_call x1, Pallas kernels, gated_conv(): pl.pallas_call(conv_kernel, grid=(chan // width,), in_specs=[wide, wide,...  8.37 us
    ppermute x2, starting transfers between devices, shift_ctx(): return lax.ppermute(x, 'ctx', [(i, i + by) for i in range(count - by)])  7.79 us
    ppermute x3, starting transfers between devices, outward(): return lax.ppermute(x, 'ctx', [(i, i ^ PLANE) for i in middle])  7.18 us
    ppermute x2, waiting for transfers between devices, shift_ctx(): return lax.ppermute(x, 'ctx', [(i, i + by) for i in range(count - by)])  4.84 us
  transfers between devices with their start and end apart: 31, of which 15 were waited for; matrix products, arithmetic and copies ran while one was open for 6% of the time, Pallas kernels for 19%

profile of v11, /device:TPU:8, one launch (start us, length us, event | category | flops | bytes accessed | tf_op | source)
XLA Modules:
  0.0 176.7 jit_solution(2416754095911525405)
XLA Ops:
  0.0 2.6 %constant_dynamic-slice_fusion = (bf16[256,768]{1,0:T(8,128)(2,1)}, bf16[256,768]{1,0:T(8,128)(2,1)}, bf16[256,768]{1,0:T(8,128)(2,1)S(1)}, bf16[256,768]{1,0:T(8,128)(2,1)}) fusion(bf16[256,3072]{1,0:T(8,128)(2,1)} %param.15, s32[]{:T(128)S(6)} %select_n.90, s32[]{:T(128)S(6)} %select_n.88, s32[]{:T(128)S(6)} %select_n.87, s32[]{:T(128)S(6)} %select_n.89), kind=kLoop, calls=%fused_computation.13 | loop fusion | bytes 3145744 | tf_op jit(solution)/shard_map/dynamic_slice | solution.py:317
  2.6 2.6 %collective-permute-start.3 = (bf16[256,768]{1,0:T(8,128)(2,1)S(1)}, bf16[256,768]{1,0:T(8,128)(2,1)}, u32[]{:S(2)}, u32[]{:S(2)}) collective-permute-start(bf16[256,768]{1,0:T(8,128)(2,1)S(1)} %get-tuple-element.222.refs_8_), channel_id=1, source_target_pairs={{0,16},{2,18},{4,20},{6,22},{8,24},{10,26},{12,28},{14,30},{16,0},... | collective-permute-start | bytes 1179656 | tf_op jit(solution)/shard_map/ppermute | solution.py:138
  6.4 15.5 %while.12 = (s32[]{:T(128)}, f32[3,16,16,128]{3,2,1,0:T(8,128)}, s32[]{:T(128)}, bf16[256,2048]{1,0:T(8,128)(2,1)S(1)}, bf16[256,2048]{1,0:T(8,128)(2,1)S(1)}, /...) while((s32[]{:T(128)}, f32[3,16,16,128]{3,2,1,0:T(8,128)}, ...), condition=%wide.region_1.2_spmd, body=%wide.region_0.1_spmd.sunk | while | flops 17727488 | bytes 5374260 | solution.py:168
  6.4 4.0 %end_states.3 = (f32[16,16,128]{2,1,0:T(8,128)}, f32[16,16,128]{2,1,0:T(8,128)}) custom-call(bf16[256,2048]{1,0:T(8,128)(2,1)S(1)} %get-tuple-element.398.k_ref, bf16[256,2048]{1,0:T(8,128)(2,1)S(1)} %get-tuple-element.399.v_ref, f32[16,2048]{1,0:T(8,128)S(1)} %get-tuple-element.400.rate_ref), custom_call_target="tpu_custom_call" | custom-call | flops 16777216 | bytes 2097152 | tf_op jit(solution)/shard_map/while/body/end_states/pallas_call | solution.py:91
  10.5 2.4 %collective-permute-start = (f32[16,16,128]{2,1,0:T(8,128)}, f32[16,16,128]{2,1,0:T(8,128)S(1)}, u32[]{:S(2)}, u32[]{:S(2)}) collective-permute-start(f32[16,16,128]{2,1,0:T(8,128)} %get-tuple-element.402), channel_id=1, source_target_pairs={{0,6},{2,4},{4,2},{6,0},{8,14},{10,12},{12,10},{14,8},{16,22},{18,... | collective-permute-start | bytes 393224 | tf_op jit(solution)/shard_map/while/body/ppermute | solution.py:138
  13.9 3.3 %collective-permute-done = f32[16,16,128]{2,1,0:T(8,128)S(1)} collective-permute-done((f32[16,16,128]{2,1,0:T(8,128)}, f32[16,16,128]{2,1,0:T(8,128)S(1)}, u32[]{:S(2)}, u32[]{:S(2)}) %collective-permute-start) | collective-permute-done | bytes 131104 | tf_op jit(solution)/shard_map/while/body/ppermute | solution.py:138
  32.5 5.4 %collective-permute-start.6 = (f32[16,16,128]{2,1,0:T(8,128)}, f32[16,16,128]{2,1,0:T(8,128)}, u32[]{:S(2)}, u32[]{:S(2)}) collective-permute-start(f32[16,16,128]{2,1,0:T(8,128)} %fusion), channel_id=1, source_target_pairs={{0,16},{2,18},{4,20},{6,22},{8,24},{10,26},{12,28},{14,30},{1,17},... | collective-permute-start | bytes 393224 | tf_op jit(solution)/shard_map/ppermute | solution.py:133
  37.9 3.9 %collective-permute-done.6 = f32[16,16,128]{2,1,0:T(8,128)} collective-permute-done((f32[16,16,128]{2,1,0:T(8,128)}, f32[16,16,128]{2,1,0:T(8,128)}, u32[]{:S(2)}, u32[]{:S(2)}) %collective-permute-start.6) | collective-permute-done | bytes 131104 | tf_op jit(solution)/shard_map/ppermute | solution.py:133
  43.6 2.4 %collective-permute-done.8 = bf16[256,768]{1,0:T(8,128)(2,1)S(1)} collective-permute-done((bf16[256,768]{1,0:T(8,128)(2,1)}, bf16[256,768]{1,0:T(8,128)(2,1)S(1)}, u32[]{:S(2)}, u32[]{:S(2)}) %collective-permute-start.8) | collective-permute-done | bytes 393248 | tf_op jit(solution)/shard_map/ppermute | solution.py:138
  48.1 3.5 %collective-permute-start.10 = (bf16[256,768]{1,0:T(8,128)(2,1)}, bf16[256,768]{1,0:T(8,128)(2,1)S(1)}, u32[]{:S(2)}, u32[]{:S(2)}) collective-permute-start(bf16[256,768]{1,0:T(8,128)(2,1)} %collective-permute-done.3.refs_12_), channel_id=1, source_target_pairs={{8,0},{10,2},{12,4},{14,6},{16,24},{18,26},{20,28},{22,30},{9,1},{... | collective-permute-start | bytes 1179656 | tf_op jit(solution)/shard_map/ppermute | solution.py:314
  51.5 3.6 %collective-permute-start.11 = (bf16[256,768]{1,0:T(8,128)(2,1)}, bf16[256,768]{1,0:T(8,128)(2,1)}, u32[]{:S(2)}, u32[]{:S(2)}) collective-permute-start(bf16[256,768]{1,0:T(8,128)(2,1)} %copy-done.11), channel_id=1, source_target_pairs={{8,16},{10,18},{12,20},{14,22},{16,8},{18,10},{20,12},{22,14},{9,1... | collective-permute-start | bytes 1179656 | tf_op jit(solution)/shard_map/ppermute | solution.py:311
  55.1 8.4 %gated_conv.1.refs_0_ = bf16[2,256,1024]{2,1,0:T(8,128)(2,1)} custom-call(bf16[256,2048]{1,0:T(8,128)(2,1)} %q_ref.1, bf16[256,2048]{1,0:T(8,128)(2,1)S(1)} %get-tuple-element.462, bf16[256,2048]{1,0:T(8,128)(2,1)S(1)} %get-tuple-element.463, f32[16,2048]{1,0:T(8,128)S(1)} %get-tuple-element.472, f32[16,2048]{1,0:T(8,128)} %residue_ref.1, ...), custom_call_target="tpu_custom_call" | custom-call | flops 33554432 | bytes 4194304 | tf_op jit(solution)/shard_map/gated_conv/pallas_call | solution.py:116
  63.6 2.4 %collective-permute-start.13 = (bf16[768,768]{1,0:T(8,128)(2,1)S(1)}, bf16[768,768]{1,0:T(8,128)(2,1)S(1)}, u32[]{:S(2)}, u32[]{:S(2)}) collective-permute-start(bf16[768,768]{1,0:T(8,128)(2,1)S(1)} %pad_maximum_fusion.1.refs_9_), channel_id=1, source_target_pairs={{0,8},{2,10},{4,12},{6,14},{8,0},{10,2},{12,4},{14,6},{16,24},{18,... | collective-permute-start | bytes 3538952 | tf_op jit(solution)/shard_map/ppermute | solution.py:138
  70.5 21.9 %collective-permute-done.14.refs_1_ = bf16[2,256,1024]{2,1,0:T(8,128)(2,1)} collective-permute-done((bf16[2,256,1024]{2,1,0:T(8,128)(2,1)}, bf16[2,256,1024]{2,1,0:T(8,128)(2,1)}, u32[]{:S(2)}, u32[]{:S(2)}) %collective-permute-start.14) | collective-permute-done | bytes 1048608 | tf_op jit(solution)/shard_map/ppermute | solution.py:138
  92.5 20.1 %collective-permute-done.15.refs_2_ = bf16[2,256,1024]{2,1,0:T(8,128)(2,1)} collective-permute-done((bf16[2,256,1024]{2,1,0:T(8,128)(2,1)}, bf16[2,256,1024]{2,1,0:T(8,128)(2,1)}, u32[]{:S(2)}, u32[]{:S(2)}) %collective-permute-start.15) | collective-permute-done | bytes 1048608 | tf_op jit(solution)/shard_map/ppermute | solution.py:138
  116.3 2.4 %collective-permute-start.21 = (bf16[768,512]{1,0:T(8,128)(2,1)}, bf16[768,512]{1,0:T(8,128)(2,1)S(1)}, u32[]{:S(2)}, u32[]{:S(2)}) collective-permute-start(bf16[768,512]{1,0:T(8,128)(2,1)} %slice.26), channel_id=1, source_target_pairs={{8,0},{10,2},{12,4},{14,6},{16,24},{18,26},{20,28},{22,30},{9,1},{... | collective-permute-start | bytes 2359304 | tf_op jit(solution)/shard_map/ppermute | solution.py:314
  118.7 4.0 %collective-permute-start.22 = (bf16[768,512]{1,0:T(8,128)(2,1)}, bf16[768,512]{1,0:T(8,128)(2,1)}, u32[]{:S(2)}, u32[]{:S(2)}) collective-permute-start(bf16[768,512]{1,0:T(8,128)(2,1)} %slice.24), channel_id=1, source_target_pairs={{8,16},{10,18},{12,20},{14,22},{16,8},{18,10},{20,12},{22,14},{9,1... | collective-permute-start | bytes 2359304 | tf_op jit(solution)/shard_map/ppermute | solution.py:311
  124.2 7.8 %product.3 = (f32[256,512]{1,0:T(8,128)}, f32[256,512]{1,0:T(8,128)}, f32[256,512]{1,0:T(8,128)}, f32[256,512]{1,0:T(8,128)}) custom-call(s32[5]{0:T(128)} %stack.63.flag_ref, s32[4]{0:T(128)} %pad_add_fusion.place_ref, bf16[2,256,1024]{2,1,0:T(8,128)(2,1)} %gated_conv.1.refs_0_, bf16[2,256,1024]{2,1,0:T(8,128)(2,1)} %collective-permute-done.14.refs_1_, ...), custom_call_target="tpu_custom_call" | custom-call | flops 3221225472 | bytes 9437184 | tf_op jit(solution)/shard_map/product/pallas_call | solution.py:236
  132.1 3.9 %collective-permute-done.21.refs_10_ = bf16[768,512]{1,0:T(8,128)(2,1)S(1)} collective-permute-done((bf16[768,512]{1,0:T(8,128)(2,1)}, bf16[768,512]{1,0:T(8,128)(2,1)S(1)}, u32[]{:S(2)}, u32[]{:S(2)}) %collective-permute-start.21) | collective-permute-done | bytes 786464 | tf_op jit(solution)/shard_map/ppermute | solution.py:314
  136.0 4.6 %collective-permute-done.22.refs_11_ = bf16[768,512]{1,0:T(8,128)(2,1)} collective-permute-done((bf16[768,512]{1,0:T(8,128)(2,1)}, bf16[768,512]{1,0:T(8,128)(2,1)}, u32[]{:S(2)}, u32[]{:S(2)}) %collective-permute-start.22) | collective-permute-done | bytes 786464 | tf_op jit(solution)/shard_map/ppermute | solution.py:311
  142.9 3.6 %collective-permute-start.27 = (bf16[768,256]{1,0:T(8,128)(2,1)S(1)}, bf16[768,256]{1,0:T(8,128)(2,1)S(1)}, u32[]{:S(2)}, u32[]{:S(2)}) collective-permute-start(bf16[768,256]{1,0:T(8,128)(2,1)S(1)} %slice.25), channel_id=1, source_target_pairs={{8,16},{10,18},{12,20},{14,22},{16,8},{18,10},{20,12},{22,14},{9,1... | collective-permute-start | bytes 1179656 | tf_op jit(solution)/shard_map/ppermute | solution.py:311
  146.6 5.2 %product.4 = (bf16[256,512]{1,0:T(8,128)(2,1)}, bf16[256,512]{1,0:T(8,128)(2,1)}, bf16[256,512]{1,0:T(8,128)(2,1)}, bf16[256,512]{1,0:T(8,128)(2,1)}) custom-call(s32[5]{0:T(128)} %stack.63.flag_ref, s32[4]{0:T(128)} %pad_add_fusion.place_ref, bf16[2,256,1024]{2,1,0:T(8,128)(2,1)} %gated_conv.1.refs_0_, ...), custom_call_target="tpu_custom_call" | custom-call | flops 1073741824 | bytes 3145728 | tf_op jit(solution)/shard_map/product/pallas_call | solution.py:236
  156.9 8.4 %product.5 = (bf16[256,256]{1,0:T(8,128)(2,1)}, bf16[256,256]{1,0:T(8,128)(2,1)}, bf16[256,256]{1,0:T(8,128)(2,1)}, bf16[256,256]{1,0:T(8,128)(2,1)}) custom-call(s32[5]{0:T(128)} %stack.63.flag_ref, s32[4]{0:T(128)} %pad_add_fusion.place_ref, bf16[2,256,1024]{2,1,0:T(8,128)(2,1)} %gated_conv.1.refs_0_, ...), custom_call_target="tpu_custom_call" | custom-call | flops 2147483648 | bytes 10485760 | tf_op jit(solution)/shard_map/product/pallas_call | solution.py:236
  171.7 2.4 %collective-permute-done.30.refs_7_ = bf16[256,256]{1,0:T(8,128)(2,1)S(1)} collective-permute-done((bf16[256,256]{1,0:T(8,128)(2,1)}, bf16[256,256]{1,0:T(8,128)(2,1)S(1)}, u32[]{:S(2)}, u32[]{:S(2)}) %collective-permute-start.30) | collective-permute-done | bytes 131104 | tf_op jit(solution)/shard_map/ppermute | solution.py:138
  (97 shorter events, 47.4 us)
Async XLA Ops:
  2.6 19.4 %collective-permute-start.3 = (bf16[256,768]{1,0:T(8,128)(2,1)S(1)}, bf16[256,768]{1,0:T(8,128)(2,1)}, u32[]{:S(2)}, u32[]{:S(2)}) collective-permute-start(bf16[256,768]{1,0:T(8,128)(2,1)S(1)} %get-tuple-element.222.refs_8_), channel_id=1, source_target_pairs={{0,16},{2,18},{4,20},{6,22},{8,24},{10,26},{12,28},{14,30},{16,0},... | collective-permute-start | bytes 1179656 | tf_op jit(solution)/shard_map/ppermute | solution.py:138
  5.2 17.7 %collective-permute-start.4 = (bf16[256,768]{1,0:T(8,128)(2,1)S(1)}, bf16[256,768]{1,0:T(8,128)(2,1)S(1)}, u32[]{:S(2)}, u32[]{:S(2)}) collective-permute-start(bf16[256,768]{1,0:T(8,128)(2,1)S(1)} %get-tuple-element.222.refs_8_), channel_id=1, source_target_pairs={{0,8},{2,10},{4,12},{6,14},{8,0},{10,2},{12,4},{14,6},{16,24},{18,... | collective-permute-start | bytes 1179656 | tf_op jit(solution)/shard_map/ppermute | solution.py:138
  24.0 6.9 %collective-permute-start.5 = (f32[16,16,128]{2,1,0:T(8,128)S(1)}, f32[16,16,128]{2,1,0:T(8,128)S(1)}, u32[]{:S(2)}, u32[]{:S(2)}) collective-permute-start(f32[16,16,128]{2,1,0:T(8,128)S(1)} %slice_bitcast_fusion), channel_id=1, source_target_pairs={{0,8},{2,10},{4,12},{6,14},{8,16},{10,18},{12,20},{14,22},{16,24},... | collective-permute-start | bytes 393224 | tf_op jit(solution)/shard_map/ppermute | solution.py:133
  26.3 17.2 %collective-permute-start.7 = (bf16[256,768]{1,0:T(8,128)(2,1)}, bf16[256,768]{1,0:T(8,128)(2,1)S(1)}, u32[]{:S(2)}, u32[]{:S(2)}) collective-permute-start(bf16[256,768]{1,0:T(8,128)(2,1)} %get-tuple-element.216), channel_id=1, source_target_pairs={{0,2},{2,0},{4,6},{6,4},{8,10},{10,8},{12,14},{14,12},{16,18},{18,... | collective-permute-start | bytes 1179656 | tf_op jit(solution)/shard_map/ppermute | solution.py:138
  27.9 18.1 %collective-permute-start.8 = (bf16[256,768]{1,0:T(8,128)(2,1)}, bf16[256,768]{1,0:T(8,128)(2,1)S(1)}, u32[]{:S(2)}, u32[]{:S(2)}) collective-permute-start(bf16[256,768]{1,0:T(8,128)(2,1)} %get-tuple-element.217), channel_id=1, source_target_pairs={{0,4},{2,6},{4,0},{6,2},{8,12},{10,14},{12,8},{14,10},{16,20},{18,... | collective-permute-start | bytes 1179656 | tf_op jit(solution)/shard_map/ppermute | solution.py:138
  29.4 17.3 %collective-permute-start.9 = (bf16[256,768]{1,0:T(8,128)(2,1)}, bf16[256,768]{1,0:T(8,128)(2,1)}, u32[]{:S(2)}, u32[]{:S(2)}) collective-permute-start(bf16[256,768]{1,0:T(8,128)(2,1)} %get-tuple-element.218), channel_id=1, source_target_pairs={{0,6},{2,4},{4,2},{6,0},{8,14},{10,12},{12,10},{14,8},{16,22},{18,... | collective-permute-start | bytes 1179656 | tf_op jit(solution)/shard_map/ppermute | solution.py:138
  32.5 9.3 %collective-permute-start.6 = (f32[16,16,128]{2,1,0:T(8,128)}, f32[16,16,128]{2,1,0:T(8,128)}, u32[]{:S(2)}, u32[]{:S(2)}) collective-permute-start(f32[16,16,128]{2,1,0:T(8,128)} %fusion), channel_id=1, source_target_pairs={{0,16},{2,18},{4,20},{6,22},{8,24},{10,26},{12,28},{14,30},{1,17},... | collective-permute-start | bytes 393224 | tf_op jit(solution)/shard_map/ppermute | solution.py:133
  48.1 15.4 %collective-permute-start.10 = (bf16[256,768]{1,0:T(8,128)(2,1)}, bf16[256,768]{1,0:T(8,128)(2,1)S(1)}, u32[]{:S(2)}, u32[]{:S(2)}) collective-permute-start(bf16[256,768]{1,0:T(8,128)(2,1)} %collective-permute-done.3.refs_12_), channel_id=1, source_target_pairs={{8,0},{10,2},{12,4},{14,6},{16,24},{18,26},{20,28},{22,30},{9,1},{... | collective-permute-start | bytes 1179656 | tf_op jit(solution)/shard_map/ppermute | solution.py:314
  51.5 12.0 %collective-permute-start.11 = (bf16[256,768]{1,0:T(8,128)(2,1)}, bf16[256,768]{1,0:T(8,128)(2,1)}, u32[]{:S(2)}, u32[]{:S(2)}) collective-permute-start(bf16[256,768]{1,0:T(8,128)(2,1)} %copy-done.11), channel_id=1, source_target_pairs={{8,16},{10,18},{12,20},{14,22},{16,8},{18,10},{20,12},{22,14},{9,1... | collective-permute-start | bytes 1179656 | tf_op jit(solution)/shard_map/ppermute | solution.py:311
  63.5 49.0 %collective-permute-start.12 = (bf16[768,768]{1,0:T(8,128)(2,1)S(1)}, bf16[768,768]{1,0:T(8,128)(2,1)S(1)}, u32[]{:S(2)}, u32[]{:S(2)}) collective-permute-start(bf16[768,768]{1,0:T(8,128)(2,1)S(1)} %pad_maximum_fusion.1.refs_9_), channel_id=1, source_target_pairs={{0,16},{2,18},{4,20},{6,22},{8,24},{10,26},{12,28},{14,30},{16,0},... | collective-permute-start | bytes 3538952 | tf_op jit(solution)/shard_map/ppermute | solution.py:138
  63.6 50.7 %collective-permute-start.13 = (bf16[768,768]{1,0:T(8,128)(2,1)S(1)}, bf16[768,768]{1,0:T(8,128)(2,1)S(1)}, u32[]{:S(2)}, u32[]{:S(2)}) collective-permute-start(bf16[768,768]{1,0:T(8,128)(2,1)S(1)} %pad_maximum_fusion.1.refs_9_), channel_id=1, source_target_pairs={{0,8},{2,10},{4,12},{6,14},{8,0},{10,2},{12,4},{14,6},{16,24},{18,... | collective-permute-start | bytes 3538952 | tf_op jit(solution)/shard_map/ppermute | solution.py:138
  66.0 26.4 %collective-permute-start.14 = (bf16[2,256,1024]{2,1,0:T(8,128)(2,1)}, bf16[2,256,1024]{2,1,0:T(8,128)(2,1)}, u32[]{:S(2)}, u32[]{:S(2)}) collective-permute-start(bf16[2,256,1024]{2,1,0:T(8,128)(2,1)} %gated_conv.1.refs_0_), channel_id=1, source_target_pairs={{0,2},{2,0},{4,6},{6,4},{8,10},{10,8},{12,14},{14,12},{16,18},{18,... | collective-permute-start | bytes 3145736 | tf_op jit(solution)/shard_map/ppermute | solution.py:138
  67.5 45.0 %collective-permute-start.15 = (bf16[2,256,1024]{2,1,0:T(8,128)(2,1)}, bf16[2,256,1024]{2,1,0:T(8,128)(2,1)}, u32[]{:S(2)}, u32[]{:S(2)}) collective-permute-start(bf16[2,256,1024]{2,1,0:T(8,128)(2,1)} %gated_conv.1.refs_0_), channel_id=1, source_target_pairs={{0,4},{2,6},{4,0},{6,2},{8,12},{10,14},{12,8},{14,10},{16,20},{18,... | collective-permute-start | bytes 3145736 | tf_op jit(solution)/shard_map/ppermute | solution.py:138
  69.1 43.5 %collective-permute-start.16 = (bf16[2,256,1024]{2,1,0:T(8,128)(2,1)}, bf16[2,256,1024]{2,1,0:T(8,128)(2,1)}, u32[]{:S(2)}, u32[]{:S(2)}) collective-permute-start(bf16[2,256,1024]{2,1,0:T(8,128)(2,1)} %gated_conv.1.refs_0_), channel_id=1, source_target_pairs={{0,6},{2,4},{4,2},{6,0},{8,14},{10,12},{12,10},{14,8},{16,22},{18,... | collective-permute-start | bytes 3145736 | tf_op jit(solution)/shard_map/ppermute | solution.py:138
  114.3 9.9 %collective-permute-start.18 = (bf16[2,256,1024]{2,1,0:T(8,128)(2,1)}, bf16[2,256,1024]{2,1,0:T(8,128)(2,1)}, u32[]{:S(2)}, u32[]{:S(2)}) collective-permute-start(bf16[2,256,1024]{2,1,0:T(8,128)(2,1)} %collective-permute-done.14.refs_1_), channel_id=1, source_target_pairs={{0,1},{1,0},{2,3},{3,2},{4,5},{5,4},{6,7},{7,6},{8,9},{9,8},{10,11... | collective-permute-start | bytes 3145736 | tf_op jit(solution)/shard_map/ppermute | solution.py:138
  114.8 9.4 %collective-permute-start.19 = (bf16[2,256,1024]{2,1,0:T(8,128)(2,1)}, bf16[2,256,1024]{2,1,0:T(8,128)(2,1)}, u32[]{:S(2)}, u32[]{:S(2)}) collective-permute-start(bf16[2,256,1024]{2,1,0:T(8,128)(2,1)} %collective-permute-done.15.refs_2_), channel_id=1, source_target_pairs={{0,1},{1,0},{2,3},{3,2},{4,5},{5,4},{6,7},{7,6},{8,9},{9,8},{10,11... | collective-permute-start | bytes 3145736 | tf_op jit(solution)/shard_map/ppermute | solution.py:138
  114.9 9.3 %collective-permute-start.20 = (bf16[2,256,1024]{2,1,0:T(8,128)(2,1)}, bf16[2,256,1024]{2,1,0:T(8,128)(2,1)}, u32[]{:S(2)}, u32[]{:S(2)}) collective-permute-start(bf16[2,256,1024]{2,1,0:T(8,128)(2,1)} %collective-permute-done.16.refs_3_), channel_id=1, source_target_pairs={{0,1},{1,0},{2,3},{3,2},{4,5},{5,4},{6,7},{7,6},{8,9},{9,8},{10,11... | collective-permute-start | bytes 3145736 | tf_op jit(solution)/shard_map/ppermute | solution.py:138
  116.3 19.7 %collective-permute-start.21 = (bf16[768,512]{1,0:T(8,128)(2,1)}, bf16[768,512]{1,0:T(8,128)(2,1)S(1)}, u32[]{:S(2)}, u32[]{:S(2)}) collective-permute-start(bf16[768,512]{1,0:T(8,128)(2,1)} %slice.26), channel_id=1, source_target_pairs={{8,0},{10,2},{12,4},{14,6},{16,24},{18,26},{20,28},{22,30},{9,1},{... | collective-permute-start | bytes 2359304 | tf_op jit(solution)/shard_map/ppermute | solution.py:314
  118.7 21.8 %collective-permute-start.22 = (bf16[768,512]{1,0:T(8,128)(2,1)}, bf16[768,512]{1,0:T(8,128)(2,1)}, u32[]{:S(2)}, u32[]{:S(2)}) collective-permute-start(bf16[768,512]{1,0:T(8,128)(2,1)} %slice.24), channel_id=1, source_target_pairs={{8,16},{10,18},{12,20},{14,22},{16,8},{18,10},{20,12},{22,14},{9,1... | collective-permute-start | bytes 2359304 | tf_op jit(solution)/shard_map/ppermute | solution.py:311
  141.6 13.8 %collective-permute-start.26 = (bf16[768,256]{1,0:T(8,128)(2,1)S(1)}, bf16[768,256]{1,0:T(8,128)(2,1)S(1)}, u32[]{:S(2)}, u32[]{:S(2)}) collective-permute-start(bf16[768,256]{1,0:T(8,128)(2,1)S(1)} %slice.27), channel_id=1, source_target_pairs={{8,0},{10,2},{12,4},{14,6},{16,24},{18,26},{20,28},{22,30},{9,1},{... | collective-permute-start | bytes 1179656 | tf_op jit(solution)/shard_map/ppermute | solution.py:314
  142.9 12.4 %collective-permute-start.27 = (bf16[768,256]{1,0:T(8,128)(2,1)S(1)}, bf16[768,256]{1,0:T(8,128)(2,1)S(1)}, u32[]{:S(2)}, u32[]{:S(2)}) collective-permute-start(bf16[768,256]{1,0:T(8,128)(2,1)S(1)} %slice.25), channel_id=1, source_target_pairs={{8,16},{10,18},{12,20},{14,22},{16,8},{18,10},{20,12},{22,14},{9,1... | collective-permute-start | bytes 1179656 | tf_op jit(solution)/shard_map/ppermute | solution.py:311
  151.8 16.2 %collective-permute-start.23 = (bf16[256,512]{1,0:T(8,128)(2,1)}, bf16[256,512]{1,0:T(8,128)(2,1)S(1)}, u32[]{:S(2)}, u32[]{:S(2)}) collective-permute-start(bf16[256,512]{1,0:T(8,128)(2,1)} %get-tuple-element.248), channel_id=1, source_target_pairs={{0,2},{2,0},{4,6},{6,4},{8,10},{10,8},{12,14},{14,12},{16,18},{18,... | collective-permute-start | bytes 786440 | tf_op jit(solution)/shard_map/ppermute | solution.py:138
  153.0 15.8 %collective-permute-start.24 = (bf16[256,512]{1,0:T(8,128)(2,1)}, bf16[256,512]{1,0:T(8,128)(2,1)S(1)}, u32[]{:S(2)}, u32[]{:S(2)}) collective-permute-start(bf16[256,512]{1,0:T(8,128)(2,1)} %get-tuple-element.249), channel_id=1, source_target_pairs={{0,4},{2,6},{4,0},{6,2},{8,12},{10,14},{12,8},{14,10},{16,20},{18,... | collective-permute-start | bytes 786440 | tf_op jit(solution)/shard_map/ppermute | solution.py:138
  154.5 14.3 %collective-permute-start.25 = (bf16[256,512]{1,0:T(8,128)(2,1)}, bf16[256,512]{1,0:T(8,128)(2,1)S(1)}, u32[]{:S(2)}, u32[]{:S(2)}) collective-permute-start(bf16[256,512]{1,0:T(8,128)(2,1)} %get-tuple-element.250), channel_id=1, source_target_pairs={{0,6},{2,4},{4,2},{6,0},{8,14},{10,12},{12,10},{14,8},{16,22},{18,... | collective-permute-start | bytes 786440 | tf_op jit(solution)/shard_map/ppermute | solution.py:138
  (26 other events, 283.2 us)

commit v12 on v10

--- a/solution.py
+++ b/solution.py
@@ -121,7 +121,7 @@
         scratch_shapes=[spread, spread, moded_spread, moded_spread],
         compiler_params=pltpu.CompilerParams(vmem_limit_bytes=VMEM_BYTES),
         cost_estimate=pl.CostEstimate(
-            flops=4 * modes * rows * chan, bytes_accessed=8 * rows * chan, transcendentals=2 * modes * chan
+            flops=4 * modes * rows, bytes_accessed=8 * rows, transcendentals=2 * modes
         ),
         name="gated_conv",
     )(q, k, v, rate, residue, skip, enter)
@@ -167,7 +167,7 @@
     return lax.fori_loop(0, once, run, empty)
 
 
-def product(flags, places, ours, theirs, blocks, accs, widths, out_dtype):
+def product(flags, places, ours, theirs, blocks, accs, widths, out_dtype, vmem_bytes):
     _, rows, depth = ours[0].shape
     chunk = depth // PLANE
     cols = sum(widths)
@@ -230,10 +230,10 @@
                     out_ref[:, inside] = total.astype(out_dtype)
 
     smem = pl.BlockSpec(memory_space=pltpu.SMEM)
-    anywhere = pl.BlockSpec(memory_space=pl.ANY)
+    anywhere, hbm = pl.BlockSpec(memory_space=pl.ANY), pl.BlockSpec(memory_space=pltpu.HBM)
     made = pl.pallas_call(
         kernel,
-        in_specs=[smem, smem] + [anywhere] * (2 * parts + len(weights) + len(accs)),
+        in_specs=[smem, smem] + [hbm] * (2 * parts) + [anywhere] * len(weights) + [hbm] * len(accs),
         out_specs=[pl.BlockSpec(memory_space=pltpu.VMEM)] * outs,
         out_shape=[jax.ShapeDtypeStruct((rows, width), out_dtype) for width in widths for _ in range(parts)],
         scratch_shapes=[
@@ -244,7 +244,7 @@
             pltpu.SemaphoreType.DMA((count,)),
             pltpu.SemaphoreType.DMA,
         ],
-        compiler_params=pltpu.CompilerParams(vmem_limit_bytes=VMEM_BYTES),
+        compiler_params=pltpu.CompilerParams(vmem_limit_bytes=vmem_bytes),
         cost_estimate=pl.CostEstimate(
             flops=2 * parts * rows * depth * count * cols,
             bytes_accessed=2 * count * depth * (parts * rows + cols),
@@ -331,26 +331,29 @@
 
     x_later, y_later = (spot & 1) != 0, (spot & 2) != 0
     w0, w1, w2, w3 = tie(*[group(w_out, r) for r in range(PLANE)])
-    f0, n0 = far(w0), near(w0)
+    f0 = far(w0)
+    arrived = [exchange(w, "ctx", r + 1) for r, w in enumerate((w1, w2, w3))]
     scanned = box(plane_scan, k, v, rate, speed)
-    f0, n0, w0, w1, w2, w3, scanned = tie(f0, n0, w0, w1, w2, w3, scanned)
-
-    arrived = [exchange(w, "ctx", r + 1) for r, w in enumerate((w1, w2, w3))]
+    f0, w0, scanned, *arrived = tie(f0, w0, scanned, *arrived)
+
     both, before = scanned[0], scanned[1]
     decay = jnp.exp(-speed * float(PLANE * rows))
     last = shift_ctx(both, PLANE)
     line = last + decay * shift_ctx(both + decay * last, 2 * PLANE)
     enter = before + jnp.exp(-speed * (spot * rows).astype(jnp.float32)) * line
     f0, w0, enter = tie(f0, w0, enter)
-    out0, mid0 = outward(f0), across(w0)
+    out0, mid0, n0 = outward(f0), across(w0), near(w0)
     gated = gated_conv(q, k, v, rate, residue, skip, enter)
     rest = jnp.concatenate(arrived)
-    gated, rest, out0, mid0 = tie(gated, rest, out0, mid0)
+    gated, rest, out0, mid0, n0 = tie(gated, rest, out0, mid0, n0)
 
     fr, nr = far(rest), near(rest)
     ours = [gated] + [exchange(gated, "ctx", r) for r in range(1, PLANE)]
     restA, restB = rest[:, :wide], rest[:, wide:]
-    fr, nr, rest, restA, restB, *ours = tie(fr, nr, rest, restA, restB, *ours)
+    ours = list(tie(*ours))
+    theirs = [exchange(x, "ch", 1) for x in ours[1:]]
+    fr, nr, rest, restA, restB, *held = tie(fr, nr, rest, restA, restB, *ours, *theirs)
+    ours, theirs = held[:PLANE], held[PLANE:]
 
     def source_of(b):
         return jnp.where(b // 2 == core, b & 1, 2 + (b & 1))
@@ -360,13 +363,13 @@
     places = jnp.stack([spot ^ r for r in range(PLANE)]).astype(jnp.int32)
 
     outA, midA = outward(fr[:, :wide]), across(restA)
-    theirs = [exchange(x, "ch", 1) for x in ours]
+    theirs = [exchange(ours[0], "ch", 1)] + theirs
     blocks = [
         (0, None, [((w0,), 0), ((rest,), 0)]),
         (1, None, [((n0,), 0), ((nr,), 0)]),
         (2, None, [((f0,), 0), ((fr,), 0)]),
     ]
-    accA, accB = product(flags, places, ours, theirs, blocks, None, [wide, cols - wide], jnp.float32)
+    accA, accB = product(flags, places, ours, theirs, blocks, None, [wide, cols - wide], jnp.float32, VMEM_BYTES)
     outA, midA, fr, restB, *accs = tie(outA, midA, fr, restB, *accA, *accB)
     accA, accB = accs[:PLANE], accs[PLANE:]
 
@@ -374,7 +377,7 @@
 
     def finish(first, out1, mid1, accs):
         blocks = [(3, 4, [((out0, mid0), first), ((out1, mid1), 0)])]
-        (made,) = product(flags, places, ours, theirs, blocks, accs, [accs[0].shape[1]], jnp.bfloat16)
+        (made,) = product(flags, places, ours, theirs, blocks, accs, [accs[0].shape[1]], jnp.bfloat16, 16 << 20)
         return [made[0]] + [exchange(made[r], "ctx", r) for r in range(1, PLANE)]
 
     return assemble(places, [finish(0, outA, midA, accA), finish(wide, outB, midB, accB)])

time: 171 us -> 185 us (1.082)
  local copies, waits for them, and re-layouts: 12.1 us -> 18.9 us
  waiting for transfers between devices: 73.2 us -> 78.2 us
  starting transfers between devices: 43.6 us -> 47.8 us
  Pallas kernels: 35.2 us -> 32.1 us
    unnamed x39 -> x59, local copies, waits for them, and re-layouts: 3.25 us -> 7.94 us
    ppermute x3, starting transfers between devices: 7.31 us -> 11.5 us  [across(): return lax.ppermute(x, 'ctx', [(i, i ^ 3 * PLANE) for i in middle])]
    ppermute x2, waiting for transfers between devices: 4.78 us -> 8.83 us  [shift_ctx(): return lax.ppermute(x, 'ctx', [(i, i + by) for i in range(count - by)])]
    pallas_call x3, Pallas kernels: 21.1 us -> 18 us  [product(): pl.pallas_call(kernel, in_specs=[smem, smem] + [hbm] * (2 * parts) + [any...]
    ppermute x2, starting transfers between devices: 7.06 us -> 4.17 us  [shift_ctx(): return lax.ppermute(x, 'ctx', [(i, i + by) for i in range(count - by)])]
    ppermute x3, starting transfers between devices: 5.71 us -> 8.38 us  [outward(): return lax.ppermute(x, 'ctx', [(i, i ^ PLANE) for i in middle])]
    slice x2, local copies, waits for them, and re-layouts: 1.73 us -> 3.9 us  [split_block(): restA, restB = (rest[:, :wide], rest[:, wide:])]
    ppermute x22, waiting for transfers between devices: 62.8 us -> 64.6 us  [exchange(): return lax.ppermute(x, axis, [(i, i ^ flip) for i in range(count)])]
  transfers between devices with their start and end apart: 30 -> 30, of which waited for: 17 -> 13; matrix products, arithmetic and copies ran while one was open for 5% -> 6% of each run, Pallas kernels for 20% -> 16%
where the time goes in v12:
time: 185 us; the launch traced here: 184 us
  waiting for transfers between devices  78.2 us (42%)
  starting transfers between devices  47.8 us (26%)
  Pallas kernels  32.1 us (17%)
  local copies, waits for them, and re-layouts  18.9 us (10%)
  other arithmetic  6.97 us (4%)
    ppermute x22, waiting for transfers between devices, exchange(): return lax.ppermute(x, axis, [(i, i ^ flip) for i in range(count)])  64.6 us
    ppermute x22, starting transfers between devices, exchange(): return lax.ppermute(x, axis, [(i, i ^ flip) for i in range(count)])  23.7 us
    pallas_call x3, Pallas kernels, product(): pl.pallas_call(kernel, in_specs=[smem, smem] + [hbm] * (2 * parts) + [any...  18 us
    ppermute x3, starting transfers between devices, across(): return lax.ppermute(x, 'ctx', [(i, i ^ 3 * PLANE) for i in middle])  11.5 us
    ppermute x2, waiting for transfers between devices, shift_ctx(): return lax.ppermute(x, 'ctx', [(i, i + by) for i in range(count - by)])  8.83 us
    ppermute x3, starting transfers between devices, outward(): return lax.ppermute(x, 'ctx', [(i, i ^ PLANE) for i in middle])  8.38 us
    pallas_call x1, Pallas kernels, gated_conv(): pl.pallas_call(conv_kernel, grid=(chan // width,), in_specs=[wide, wide,...  8.36 us
    unnamed x59, local copies, waits for them, and re-layouts  7.94 us
  transfers between devices with their start and end apart: 30, of which 13 were waited for; matrix products, arithmetic and copies ran while one was open for 6% of the time, Pallas kernels for 16%

profile of v12, /device:TPU:8, one launch (start us, length us, event | category | flops | bytes accessed | tf_op | source)
XLA Modules:
  0.0 184.5 jit_solution(9548715936339782787)
XLA Ops:
  0.0 2.7 %constant_dynamic-slice_fusion = (bf16[256,768]{1,0:T(8,128)(2,1)}, bf16[256,768]{1,0:T(8,128)(2,1)}, bf16[256,768]{1,0:T(8,128)(2,1)}, bf16[256,768]{1,0:T(8,128)(2,1)}) fusion(bf16[256,3072]{1,0:T(8,128)(2,1)} %param.15, s32[]{:T(128)S(6)} %select_n.94, s32[]{:T(128)S(6)} %select_n.92, s32[]{:T(128)S(6)} %select_n.91, s32[]{:T(128)S(6)} %select_n.93), kind=kLoop, calls=%fused_computation.9 | loop fusion | bytes 3145744 | tf_op jit(solution)/shard_map/dynamic_slice | solution.py:317
  2.7 2.6 %collective-permute-start.2 = (bf16[256,768]{1,0:T(8,128)(2,1)}, bf16[256,768]{1,0:T(8,128)(2,1)}, u32[]{:S(2)}, u32[]{:S(2)}) collective-permute-start(bf16[256,768]{1,0:T(8,128)(2,1)} %get-tuple-element.202.refs_8_), channel_id=1, source_target_pairs={{0,16},{2,18},{4,20},{6,22},{8,24},{10,26},{12,28},{14,30},{16,0},... | collective-permute-start | bytes 1179656 | tf_op jit(solution)/shard_map/ppermute | solution.py:137
  9.6 24.6 %while.12 = (s32[]{:T(128)}, f32[2,16,16,128]{3,2,1,0:T(8,128)}, s32[]{:T(128)}, pred[]{:T(512)}, bf16[256,2048]{1,0:T(8,128)(2,1)S(1)}, /*index=5*/bf16[256,204...) while((s32[]{:T(128)}, f32[2,16,16,128]{3,2,1,0:T(8,128)}, ...), condition=%wide.region_1.2_spmd, body=%wide.region_0.1_spmd.sunk | while | flops 17465344 | bytes 4980932 | solution.py:167
  9.6 3.9 %end_states.3 = f32[16,16,128]{2,1,0:T(8,128)} custom-call(bf16[256,2048]{1,0:T(8,128)(2,1)S(1)} %get-tuple-element.344.k_ref, bf16[256,2048]{1,0:T(8,128)(2,1)S(1)} %get-tuple-element.345.v_ref, f32[16,2048]{1,0:T(8,128)S(1)} %get-tuple-element.346.rate_ref), custom_call_target="tpu_custom_call" | custom-call | flops 16777216 | bytes 2097152 | tf_op jit(solution)/shard_map/while/body/end_states/pallas_call | solution.py:90
  15.0 12.4 %collective-permute-done = f32[16,16,128]{2,1,0:T(8,128)S(1)} collective-permute-done((f32[16,16,128]{2,1,0:T(8,128)}, f32[16,16,128]{2,1,0:T(8,128)S(1)}, u32[]{:S(2)}, u32[]{:S(2)}) %collective-permute-start) | collective-permute-done | bytes 131104 | tf_op jit(solution)/shard_map/while/body/ppermute | solution.py:137
  29.9 3.4 %collective-permute-done.1 = f32[16,16,128]{2,1,0:T(8,128)S(1)} collective-permute-done((f32[16,16,128]{2,1,0:T(8,128)S(1)}, f32[16,16,128]{2,1,0:T(8,128)S(1)}, u32[]{:S(2)}, u32[]{:S(2)}) %collective-permute-start.1) | collective-permute-done | bytes 131104 | tf_op jit(solution)/shard_map/while/body/ppermute | solution.py:137
  37.0 4.9 %collective-permute-done.6 = f32[16,16,128]{2,1,0:T(8,128)S(1)} collective-permute-done((f32[16,16,128]{2,1,0:T(8,128)S(1)}, f32[16,16,128]{2,1,0:T(8,128)S(1)}, u32[]{:S(2)}, u32[]{:S(2)}) %collective-permute-start.6) | collective-permute-done | bytes 131104 | tf_op jit(solution)/shard_map/ppermute | solution.py:132
  42.9 2.2 %collective-permute-start.7 = (f32[16,16,128]{2,1,0:T(8,128)S(1)}, f32[16,16,128]{2,1,0:T(8,128)S(1)}, u32[]{:S(2)}, u32[]{:S(2)}) collective-permute-start(f32[16,16,128]{2,1,0:T(8,128)S(1)} %multiply_add_fusion), channel_id=1, source_target_pairs={{0,16},{2,18},{4,20},{6,22},{8,24},{10,26},{12,28},{14,30},{1,17},... | collective-permute-start | bytes 393224 | tf_op jit(solution)/shard_map/ppermute | solution.py:132
  45.1 3.9 %collective-permute-done.7 = f32[16,16,128]{2,1,0:T(8,128)S(1)} collective-permute-done((f32[16,16,128]{2,1,0:T(8,128)S(1)}, f32[16,16,128]{2,1,0:T(8,128)S(1)}, u32[]{:S(2)}, u32[]{:S(2)}) %collective-permute-start.7) | collective-permute-done | bytes 131104 | tf_op jit(solution)/shard_map/ppermute | solution.py:132
  50.7 3.9 %collective-permute-start.8 = (bf16[256,768]{1,0:T(8,128)(2,1)}, bf16[256,768]{1,0:T(8,128)(2,1)S(1)}, u32[]{:S(2)}, u32[]{:S(2)}) collective-permute-start(bf16[256,768]{1,0:T(8,128)(2,1)} %collective-permute-done.2.refs_12_), channel_id=1, source_target_pairs={{8,0},{10,2},{12,4},{14,6},{16,24},{18,26},{20,28},{22,30},{9,1},{... | collective-permute-start | bytes 1179656 | tf_op jit(solution)/shard_map/ppermute | solution.py:314
  54.6 3.8 %collective-permute-start.9 = (bf16[256,768]{1,0:T(8,128)(2,1)}, bf16[256,768]{1,0:T(8,128)(2,1)S(1)}, u32[]{:S(2)}, u32[]{:S(2)}) collective-permute-start(bf16[256,768]{1,0:T(8,128)(2,1)} %get-tuple-element.202.refs_8_), channel_id=1, source_target_pairs={{8,16},{10,18},{12,20},{14,22},{16,8},{18,10},{20,12},{22,14},{9,1... | collective-permute-start | bytes 1179656 | tf_op jit(solution)/shard_map/ppermute | solution.py:311
  60.5 8.4 %gated_conv.1.refs_0_ = bf16[2,256,1024]{2,1,0:T(8,128)(2,1)} custom-call(bf16[256,2048]{1,0:T(8,128)(2,1)} %q_ref.1, bf16[256,2048]{1,0:T(8,128)(2,1)S(1)} %get-tuple-element.408, bf16[256,2048]{1,0:T(8,128)(2,1)S(1)} %get-tuple-element.409, f32[16,2048]{1,0:T(8,128)S(1)} %get-tuple-element.414, f32[16,2048]{1,0:T(8,128)} %residue_ref.1, ...), custom_call_target="tpu_custom_call" | custom-call | flops 16384 | bytes 2048 | tf_op jit(solution)/shard_map/gated_conv/pallas_call | solution.py:115
  74.0 21.2 %collective-permute-done.13.refs_1_ = bf16[2,256,1024]{2,1,0:T(8,128)(2,1)S(1)} collective-permute-done((bf16[2,256,1024]{2,1,0:T(8,128)(2,1)}, bf16[2,256,1024]{2,1,0:T(8,128)(2,1)S(1)}, u32[]{:S(2)}, u32[]{:S(2)}) %collective-permute-start.13) | collective-permute-done | bytes 1048608 | tf_op jit(solution)/shard_map/ppermute | solution.py:137
  95.3 17.4 %collective-permute-done.14.refs_2_ = bf16[2,256,1024]{2,1,0:T(8,128)(2,1)S(1)} collective-permute-done((bf16[2,256,1024]{2,1,0:T(8,128)(2,1)}, bf16[2,256,1024]{2,1,0:T(8,128)(2,1)S(1)}, u32[]{:S(2)}, u32[]{:S(2)}) %collective-permute-start.14) | collective-permute-done | bytes 1048608 | tf_op jit(solution)/shard_map/ppermute | solution.py:137
  120.7 3.1 %collective-permute-start.20 = (bf16[768,512]{1,0:T(8,128)(2,1)}, bf16[768,512]{1,0:T(8,128)(2,1)}, u32[]{:S(2)}, u32[]{:S(2)}) collective-permute-start(bf16[768,512]{1,0:T(8,128)(2,1)} %slice.22), channel_id=1, source_target_pairs={{8,0},{10,2},{12,4},{14,6},{16,24},{18,26},{20,28},{22,30},{9,1},{... | collective-permute-start | bytes 2359304 | tf_op jit(solution)/shard_map/ppermute | solution.py:314
  123.9 4.1 %collective-permute-start.21 = (bf16[768,512]{1,0:T(8,128)(2,1)}, bf16[768,512]{1,0:T(8,128)(2,1)}, u32[]{:S(2)}, u32[]{:S(2)}) collective-permute-start(bf16[768,512]{1,0:T(8,128)(2,1)} %slice.20), channel_id=1, source_target_pairs={{8,16},{10,18},{12,20},{14,22},{16,8},{18,10},{20,12},{22,14},{9,1... | collective-permute-start | bytes 2359304 | tf_op jit(solution)/shard_map/ppermute | solution.py:311
  129.3 12.0 %product.3 = (f32[256,512]{1,0:T(8,128)}, f32[256,512]{1,0:T(8,128)}, f32[256,512]{1,0:T(8,128)}, f32[256,512]{1,0:T(8,128)}, f32[256,256]{1,0:T(8,128)}, /*inde...) custom-call(s32[5]{0:T(128)} %stack.58.flag_ref, s32[4]{0:T(128)} %pad_add_fusion.place_ref, ...), custom_call_target="tpu_custom_call" | custom-call | flops 4831838208 | bytes 11010048 | tf_op jit(solution)/shard_map/product/pallas_call | solution.py:234
  141.3 4.7 %collective-permute-done.21.refs_11_ = bf16[768,512]{1,0:T(8,128)(2,1)} collective-permute-done((bf16[768,512]{1,0:T(8,128)(2,1)}, bf16[768,512]{1,0:T(8,128)(2,1)}, u32[]{:S(2)}, u32[]{:S(2)}) %collective-permute-start.21) | collective-permute-done | bytes 786464 | tf_op jit(solution)/shard_map/ppermute | solution.py:311
  148.4 3.6 %collective-permute-start.26 = (bf16[768,256]{1,0:T(8,128)(2,1)}, bf16[768,256]{1,0:T(8,128)(2,1)S(1)}, u32[]{:S(2)}, u32[]{:S(2)}) collective-permute-start(bf16[768,256]{1,0:T(8,128)(2,1)} %slice.21), channel_id=1, source_target_pairs={{8,16},{10,18},{12,20},{14,22},{16,8},{18,10},{20,12},{22,14},{9,1... | collective-permute-start | bytes 1179656 | tf_op jit(solution)/shard_map/ppermute | solution.py:311
  159.9 3.1 %product.4 = (bf16[256,512]{1,0:T(8,128)(2,1)S(1)}, bf16[256,512]{1,0:T(8,128)(2,1)S(1)}, bf16[256,512]{1,0:T(8,128)(2,1)S(1)}, bf16[256,512]{1,0:T(8,128)(2,1)S(1)}) custom-call(s32[5]{0:T(128)S(1)} %copy-done.23, s32[4]{0:T(128)S(1)} %copy-done.22, bf16[2,256,1024]{2,1,0:T(8,128)(2,1)} %gated_conv.1.refs_0_, bf16[2,256,1024]{2,1,0:T(8,128)(2,1)S(1)} %copy-done.1, ...), custom_call_target="tpu_custom_call" | custom-call | flops 1073741824 | bytes 3145728 | tf_op jit(solution)/shard_map/product/pallas_call | solution.py:234
  166.7 2.9 %product.5 = (bf16[256,256]{1,0:T(8,128)(2,1)S(1)}, bf16[256,256]{1,0:T(8,128)(2,1)S(1)}, bf16[256,256]{1,0:T(8,128)(2,1)S(1)}, bf16[256,256]{1,0:T(8,128)(2,1)S(1)}) custom-call(s32[5]{0:T(128)S(1)} %copy-done.23, s32[4]{0:T(128)S(1)} %copy-done.22, bf16[2,256,1024]{2,1,0:T(8,128)(2,1)} %gated_conv.1.refs_0_, bf16[2,256,1024]{2,1,0:T(8,128)(2,1)S(1)} %copy-done.1, ...), custom_call_target="tpu_custom_call" | custom-call | flops 536870912 | bytes 2621440 | tf_op jit(solution)/shard_map/product/pallas_call | solution.py:234
  172.7 2.2 %collective-permute-start.29 = (bf16[256,256]{1,0:T(8,128)(2,1)S(1)}, bf16[256,256]{1,0:T(8,128)(2,1)S(1)}, u32[]{:S(2)}, u32[]{:S(2)}) collective-permute-start(bf16[256,256]{1,0:T(8,128)(2,1)S(1)} %get-tuple-element.251), channel_id=1, source_target_pairs={{0,6},{2,4},{4,2},{6,0},{8,14},{10,12},{12,10},{14,8},{16,22},{18,... | collective-permute-start | bytes 393224 | tf_op jit(solution)/shard_map/ppermute | solution.py:137
  174.8 4.1 %collective-permute-done.23.refs_2_ = bf16[256,512]{1,0:T(8,128)(2,1)S(1)} collective-permute-done((bf16[256,512]{1,0:T(8,128)(2,1)S(1)}, bf16[256,512]{1,0:T(8,128)(2,1)S(1)}, u32[]{:S(2)}, u32[]{:S(2)}) %collective-permute-start.23) | collective-permute-done | bytes 262176 | tf_op jit(solution)/shard_map/ppermute | solution.py:137
  180.1 2.6 %collective-permute-done.28.refs_6_ = bf16[256,256]{1,0:T(8,128)(2,1)S(1)} collective-permute-done((bf16[256,256]{1,0:T(8,128)(2,1)S(1)}, bf16[256,256]{1,0:T(8,128)(2,1)S(1)}, u32[]{:S(2)}, u32[]{:S(2)}) %collective-permute-start.28) | collective-permute-done | bytes 131104 | tf_op jit(solution)/shard_map/ppermute | solution.py:137
  (117 shorter events, 50.7 us)
Async XLA Ops:
  2.7 31.4 %collective-permute-start.2 = (bf16[256,768]{1,0:T(8,128)(2,1)}, bf16[256,768]{1,0:T(8,128)(2,1)}, u32[]{:S(2)}, u32[]{:S(2)}) collective-permute-start(bf16[256,768]{1,0:T(8,128)(2,1)} %get-tuple-element.202.refs_8_), channel_id=1, source_target_pairs={{0,16},{2,18},{4,20},{6,22},{8,24},{10,26},{12,28},{14,30},{16,0},... | collective-permute-start | bytes 1179656 | tf_op jit(solution)/shard_map/ppermute | solution.py:137
  5.3 28.9 %collective-permute-start.3 = (bf16[256,768]{1,0:T(8,128)(2,1)}, bf16[256,768]{1,0:T(8,128)(2,1)S(1)}, u32[]{:S(2)}, u32[]{:S(2)}) collective-permute-start(bf16[256,768]{1,0:T(8,128)(2,1)} %get-tuple-element.191), channel_id=1, source_target_pairs={{0,2},{2,0},{4,6},{6,4},{8,10},{10,8},{12,14},{14,12},{16,18},{18,... | collective-permute-start | bytes 1179656 | tf_op jit(solution)/shard_map/ppermute | solution.py:137
  6.8 27.4 %collective-permute-start.4 = (bf16[256,768]{1,0:T(8,128)(2,1)}, bf16[256,768]{1,0:T(8,128)(2,1)S(1)}, u32[]{:S(2)}, u32[]{:S(2)}) collective-permute-start(bf16[256,768]{1,0:T(8,128)(2,1)} %get-tuple-element.192), channel_id=1, source_target_pairs={{0,4},{2,6},{4,0},{6,2},{8,12},{10,14},{12,8},{14,10},{16,20},{18,... | collective-permute-start | bytes 1179656 | tf_op jit(solution)/shard_map/ppermute | solution.py:137
  8.3 25.9 %collective-permute-start.5 = (bf16[256,768]{1,0:T(8,128)(2,1)}, bf16[256,768]{1,0:T(8,128)(2,1)}, u32[]{:S(2)}, u32[]{:S(2)}) collective-permute-start(bf16[256,768]{1,0:T(8,128)(2,1)} %get-tuple-element.193), channel_id=1, source_target_pairs={{0,6},{2,4},{4,2},{6,0},{8,14},{10,12},{12,10},{14,8},{16,22},{18,... | collective-permute-start | bytes 1179656 | tf_op jit(solution)/shard_map/ppermute | solution.py:137
  13.5 13.9 %collective-permute-start = (f32[16,16,128]{2,1,0:T(8,128)}, f32[16,16,128]{2,1,0:T(8,128)S(1)}, u32[]{:S(2)}, u32[]{:S(2)}) collective-permute-start(f32[16,16,128]{2,1,0:T(8,128)} %end_states.3), channel_id=1, source_target_pairs={{0,2},{2,0},{4,6},{6,4},{8,10},{10,8},{12,14},{14,12},{16,18},{18,... | collective-permute-start | bytes 393224 | tf_op jit(solution)/shard_map/while/body/ppermute | solution.py:137
  50.7 18.2 %collective-permute-start.10 = (bf16[256,768]{1,0:T(8,128)(2,1)}, bf16[256,768]{1,0:T(8,128)(2,1)}, u32[]{:S(2)}, u32[]{:S(2)}) collective-permute-start(bf16[256,768]{1,0:T(8,128)(2,1)} %get-tuple-element.202.refs_8_), channel_id=1, source_target_pairs={{0,8},{2,10},{4,12},{6,14},{8,0},{10,2},{12,4},{14,6},{16,24},{18,... | collective-permute-start | bytes 1179656 | tf_op jit(solution)/shard_map/ppermute | solution.py:137
  50.7 18.2 %collective-permute-start.8 = (bf16[256,768]{1,0:T(8,128)(2,1)}, bf16[256,768]{1,0:T(8,128)(2,1)S(1)}, u32[]{:S(2)}, u32[]{:S(2)}) collective-permute-start(bf16[256,768]{1,0:T(8,128)(2,1)} %collective-permute-done.2.refs_12_), channel_id=1, source_target_pairs={{8,0},{10,2},{12,4},{14,6},{16,24},{18,26},{20,28},{22,30},{9,1},{... | collective-permute-start | bytes 1179656 | tf_op jit(solution)/shard_map/ppermute | solution.py:314
  54.6 14.3 %collective-permute-start.9 = (bf16[256,768]{1,0:T(8,128)(2,1)}, bf16[256,768]{1,0:T(8,128)(2,1)S(1)}, u32[]{:S(2)}, u32[]{:S(2)}) collective-permute-start(bf16[256,768]{1,0:T(8,128)(2,1)} %get-tuple-element.202.refs_8_), channel_id=1, source_target_pairs={{8,16},{10,18},{12,20},{14,22},{16,8},{18,10},{20,12},{22,14},{9,1... | collective-permute-start | bytes 1179656 | tf_op jit(solution)/shard_map/ppermute | solution.py:311
  68.9 26.4 %collective-permute-start.13 = (bf16[2,256,1024]{2,1,0:T(8,128)(2,1)}, bf16[2,256,1024]{2,1,0:T(8,128)(2,1)S(1)}, u32[]{:S(2)}, u32[]{:S(2)}) collective-permute-start(bf16[2,256,1024]{2,1,0:T(8,128)(2,1)} %gated_conv.1.refs_0_), channel_id=1, source_target_pairs={{0,2},{2,0},{4,6},{6,4},{8,10},{10,8},{12,14},{14,12},{16,18},{18,... | collective-permute-start | bytes 3145736 | tf_op jit(solution)/shard_map/ppermute | solution.py:137
  70.5 42.2 %collective-permute-start.14 = (bf16[2,256,1024]{2,1,0:T(8,128)(2,1)}, bf16[2,256,1024]{2,1,0:T(8,128)(2,1)S(1)}, u32[]{:S(2)}, u32[]{:S(2)}) collective-permute-start(bf16[2,256,1024]{2,1,0:T(8,128)(2,1)} %gated_conv.1.refs_0_), channel_id=1, source_target_pairs={{0,4},{2,6},{4,0},{6,2},{8,12},{10,14},{12,8},{14,10},{16,20},{18,... | collective-permute-start | bytes 3145736 | tf_op jit(solution)/shard_map/ppermute | solution.py:137
  71.9 40.7 %collective-permute-start.15 = (bf16[2,256,1024]{2,1,0:T(8,128)(2,1)}, bf16[2,256,1024]{2,1,0:T(8,128)(2,1)S(1)}, u32[]{:S(2)}, u32[]{:S(2)}) collective-permute-start(bf16[2,256,1024]{2,1,0:T(8,128)(2,1)} %gated_conv.1.refs_0_), channel_id=1, source_target_pairs={{0,6},{2,4},{4,2},{6,0},{8,14},{10,12},{12,10},{14,8},{16,22},{18,... | collective-permute-start | bytes 3145736 | tf_op jit(solution)/shard_map/ppermute | solution.py:137
  72.5 45.2 %collective-permute-start.11 = (bf16[768,768]{1,0:T(8,128)(2,1)}, bf16[768,768]{1,0:T(8,128)(2,1)S(1)}, u32[]{:S(2)}, u32[]{:S(2)}) collective-permute-start(bf16[768,768]{1,0:T(8,128)(2,1)} %pad_maximum_fusion.1.refs_9_), channel_id=1, source_target_pairs={{0,16},{2,18},{4,20},{6,22},{8,24},{10,26},{12,28},{14,30},{16,0},... | collective-permute-start | bytes 3538952 | tf_op jit(solution)/shard_map/ppermute | solution.py:137
  72.7 46.7 %collective-permute-start.12 = (bf16[768,768]{1,0:T(8,128)(2,1)}, bf16[768,768]{1,0:T(8,128)(2,1)S(1)}, u32[]{:S(2)}, u32[]{:S(2)}) collective-permute-start(bf16[768,768]{1,0:T(8,128)(2,1)} %pad_maximum_fusion.1.refs_9_), channel_id=1, source_target_pairs={{0,8},{2,10},{4,12},{6,14},{8,0},{10,2},{12,4},{14,6},{16,24},{18,... | collective-permute-start | bytes 3538952 | tf_op jit(solution)/shard_map/ppermute | solution.py:137
  119.5 9.7 %collective-permute-start.19 = (bf16[2,256,1024]{2,1,0:T(8,128)(2,1)}, bf16[2,256,1024]{2,1,0:T(8,128)(2,1)}, u32[]{:S(2)}, u32[]{:S(2)}) collective-permute-start(bf16[2,256,1024]{2,1,0:T(8,128)(2,1)} %gated_conv.1.refs_0_), channel_id=1, source_target_pairs={{0,1},{1,0},{2,3},{3,2},{4,5},{5,4},{6,7},{7,6},{8,9},{9,8},{10,11... | collective-permute-start | bytes 3145736 | tf_op jit(solution)/shard_map/ppermute | solution.py:137
  120.7 20.6 %collective-permute-start.20 = (bf16[768,512]{1,0:T(8,128)(2,1)}, bf16[768,512]{1,0:T(8,128)(2,1)}, u32[]{:S(2)}, u32[]{:S(2)}) collective-permute-start(bf16[768,512]{1,0:T(8,128)(2,1)} %slice.22), channel_id=1, source_target_pairs={{8,0},{10,2},{12,4},{14,6},{16,24},{18,26},{20,28},{22,30},{9,1},{... | collective-permute-start | bytes 2359304 | tf_op jit(solution)/shard_map/ppermute | solution.py:314
  123.9 22.1 %collective-permute-start.21 = (bf16[768,512]{1,0:T(8,128)(2,1)}, bf16[768,512]{1,0:T(8,128)(2,1)}, u32[]{:S(2)}, u32[]{:S(2)}) collective-permute-start(bf16[768,512]{1,0:T(8,128)(2,1)} %slice.20), channel_id=1, source_target_pairs={{8,16},{10,18},{12,20},{14,22},{16,8},{18,10},{20,12},{22,14},{9,1... | collective-permute-start | bytes 2359304 | tf_op jit(solution)/shard_map/ppermute | solution.py:311
  147.1 19.6 %collective-permute-start.25 = (bf16[768,256]{1,0:T(8,128)(2,1)S(1)}, bf16[768,256]{1,0:T(8,128)(2,1)S(1)}, u32[]{:S(2)}, u32[]{:S(2)}) collective-permute-start(bf16[768,256]{1,0:T(8,128)(2,1)S(1)} %slice.23), channel_id=1, source_target_pairs={{8,0},{10,2},{12,4},{14,6},{16,24},{18,26},{20,28},{22,30},{9,1},{... | collective-permute-start | bytes 1179656 | tf_op jit(solution)/shard_map/ppermute | solution.py:314
  148.4 18.3 %collective-permute-start.26 = (bf16[768,256]{1,0:T(8,128)(2,1)}, bf16[768,256]{1,0:T(8,128)(2,1)S(1)}, u32[]{:S(2)}, u32[]{:S(2)}) collective-permute-start(bf16[768,256]{1,0:T(8,128)(2,1)} %slice.21), channel_id=1, source_target_pairs={{8,16},{10,18},{12,20},{14,22},{16,8},{18,10},{20,12},{22,14},{9,1... | collective-permute-start | bytes 1179656 | tf_op jit(solution)/shard_map/ppermute | solution.py:311
  163.1 9.6 %collective-permute-start.22 = (bf16[256,512]{1,0:T(8,128)(2,1)S(1)}, bf16[256,512]{1,0:T(8,128)(2,1)S(1)}, u32[]{:S(2)}, u32[]{:S(2)}) collective-permute-start(bf16[256,512]{1,0:T(8,128)(2,1)S(1)} %get-tuple-element.239), channel_id=1, source_target_pairs={{0,2},{2,0},{4,6},{6,4},{8,10},{10,8},{12,14},{14,12},{16,18},{18,... | collective-permute-start | bytes 786440 | tf_op jit(solution)/shard_map/ppermute | solution.py:137
  164.7 14.3 %collective-permute-start.23 = (bf16[256,512]{1,0:T(8,128)(2,1)S(1)}, bf16[256,512]{1,0:T(8,128)(2,1)S(1)}, u32[]{:S(2)}, u32[]{:S(2)}) collective-permute-start(bf16[256,512]{1,0:T(8,128)(2,1)S(1)} %get-tuple-element.240), channel_id=1, source_target_pairs={{0,4},{2,6},{4,0},{6,2},{8,12},{10,14},{12,8},{14,10},{16,20},{18,... | collective-permute-start | bytes 786440 | tf_op jit(solution)/shard_map/ppermute | solution.py:137
  166.1 12.9 %collective-permute-start.24 = (bf16[256,512]{1,0:T(8,128)(2,1)S(1)}, bf16[256,512]{1,0:T(8,128)(2,1)S(1)}, u32[]{:S(2)}, u32[]{:S(2)}) collective-permute-start(bf16[256,512]{1,0:T(8,128)(2,1)S(1)} %get-tuple-element.241), channel_id=1, source_target_pairs={{0,6},{2,4},{4,2},{6,0},{8,14},{10,12},{12,10},{14,8},{16,22},{18,... | collective-permute-start | bytes 786440 | tf_op jit(solution)/shard_map/ppermute | solution.py:137
  169.6 10.5 %collective-permute-start.27 = (bf16[256,256]{1,0:T(8,128)(2,1)S(1)}, bf16[256,256]{1,0:T(8,128)(2,1)S(1)}, u32[]{:S(2)}, u32[]{:S(2)}) collective-permute-start(bf16[256,256]{1,0:T(8,128)(2,1)S(1)} %get-tuple-element.249), channel_id=1, source_target_pairs={{0,2},{2,0},{4,6},{6,4},{8,10},{10,8},{12,14},{14,12},{16,18},{18,... | collective-permute-start | bytes 393224 | tf_op jit(solution)/shard_map/ppermute | solution.py:137
  171.2 11.5 %collective-permute-start.28 = (bf16[256,256]{1,0:T(8,128)(2,1)S(1)}, bf16[256,256]{1,0:T(8,128)(2,1)S(1)}, u32[]{:S(2)}, u32[]{:S(2)}) collective-permute-start(bf16[256,256]{1,0:T(8,128)(2,1)S(1)} %get-tuple-element.250), channel_id=1, source_target_pairs={{0,4},{2,6},{4,0},{6,2},{8,12},{10,14},{12,8},{14,10},{16,20},{18,... | collective-permute-start | bytes 393224 | tf_op jit(solution)/shard_map/ppermute | solution.py:137
  172.7 10.1 %collective-permute-start.29 = (bf16[256,256]{1,0:T(8,128)(2,1)S(1)}, bf16[256,256]{1,0:T(8,128)(2,1)S(1)}, u32[]{:S(2)}, u32[]{:S(2)}) collective-permute-start(bf16[256,256]{1,0:T(8,128)(2,1)S(1)} %get-tuple-element.251), channel_id=1, source_target_pairs={{0,6},{2,4},{4,2},{6,0},{8,14},{10,12},{12,10},{14,8},{16,22},{18,... | collective-permute-start | bytes 393224 | tf_op jit(solution)/shard_map/ppermute | solution.py:137
  (35 other events, 396.2 us)

commit v13 on v10

--- a/solution.py
+++ b/solution.py
@@ -44,7 +44,8 @@
         end_ref[m] = state[m]
 
 
-def conv_kernel(q_ref, k_ref, v_ref, rate_ref, residue_ref, skip_ref, enter_ref, out_ref, sig_ref, conv_ref, mode_ref, weight_ref):
+def conv_kernel(q_ref, k_ref, v_ref, rate_ref, residue_ref, skip_ref, enter_ref, *refs):
+    *plane_refs, out_ref, sig_ref, conv_ref, mode_ref, weight_ref = refs
     rows, width = k_ref.shape
     modes, groups, _ = enter_ref.shape
     spread_signal(k_ref, v_ref, sig_ref)
@@ -54,6 +55,13 @@
     decay = [jnp.exp(-rate) for rate in rates]
     weight = [weight_ref[pl.ds(m * groups, groups), :] * jnp.sqrt(2.0 * rate) for m, rate in enumerate(rates)]
     skip = skip_ref[...]
+    enter = [enter_ref[m] for m in range(modes)]
+    if plane_refs:
+        last_ref, earlier_ref, spot_ref = plane_refs
+        ahead = (spot_ref[0] * rows).astype(jnp.float32)
+        for m, rate in enumerate(rates):
+            line = last_ref[m] + jnp.exp(-rate * float(PLANE * rows)) * earlier_ref[m]
+            enter[m] = enter[m] + jnp.exp(-rate * ahead) * line
 
     def step(t, state):
         at = pl.ds(pl.multiple_of(t * groups, groups), groups)
@@ -65,7 +73,7 @@
         conv_ref[at, :] = terms[0]
         return state
 
-    lax.fori_loop(0, rows, step, tuple(enter_ref[m] for m in range(modes)), unroll=4)
+    lax.fori_loop(0, rows, step, tuple(enter), unroll=4)
     for g in range(groups):
         cols = pl.ds(g * LANES, LANES)
         conv = conv_ref[pl.ds(g, rows, stride=groups), :]
@@ -105,17 +113,22 @@
     )(k, v, rate)
 
 
-def gated_conv(q, k, v, rate, residue, skip, enter):
+def gated_conv(q, k, v, rate, residue, skip, enter, planes=None):
     rows, chan = k.shape
     modes = rate.shape[0]
     width = min(chan, 8 * LANES)
     wide, moded, state, single = block_specs(rows, modes, width)
     spread = pltpu.VMEM((rows * width // LANES, LANES), jnp.float32)
     moded_spread = pltpu.VMEM((modes * width // LANES, LANES), jnp.float32)
+    extra, extra_specs = [], []
+    if planes is not None:
+        last, earlier, spot = planes
+        extra = [last, earlier, spot.reshape(1).astype(jnp.int32)]
+        extra_specs = [state, state, pl.BlockSpec(memory_space=pltpu.SMEM)]
     return pl.pallas_call(
         conv_kernel,
         grid=(chan // width,),
-        in_specs=[wide, wide, wide, moded, moded, single, state],
+        in_specs=[wide, wide, wide, moded, moded, single, state] + extra_specs,
         out_specs=pl.BlockSpec((None, rows, width), lambda i: (i, 0, 0)),
         out_shape=jax.ShapeDtypeStruct((chan // width, rows, width), jnp.bfloat16),
         scratch_shapes=[spread, spread, moded_spread, moded_spread],
@@ -124,7 +137,7 @@
             flops=4 * modes * rows * chan, bytes_accessed=8 * rows * chan, transcendentals=2 * modes * chan
         ),
         name="gated_conv",
-    )(q, k, v, rate, residue, skip, enter)
+    )(q, k, v, rate, residue, skip, enter, *extra)
 
 
 def shift_ctx(x, by):
@@ -159,12 +172,17 @@
 def box(fn, *args):
     once = (lax.axis_index("ctx") >= 0).astype(jnp.int32)
     shapes = jax.eval_shape(fn, *args)
-    empty = jax.tree.map(lambda a: jnp.zeros(a.shape, a.dtype), shapes)
+    empty = pl.pallas_call(
+        lambda *refs: None,
+        out_specs=[pl.BlockSpec(memory_space=pl.ANY)] * len(shapes),
+        out_shape=list(shapes),
+        name="blank",
+    )()
 
     def run(step, _):
         return fn(*tie(step, *args)[1:])
 
-    return lax.fori_loop(0, once, run, empty)
+    return lax.fori_loop(0, once, run, tuple(empty))
 
 
 def product(flags, places, ours, theirs, blocks, accs, widths, out_dtype):
@@ -316,6 +334,13 @@
     def group(x, r):
         return lax.dynamic_slice_in_dim(x, (spot ^ r) * cols, cols, axis=1)
 
+    def source_of(b):
+        return jnp.where(b // 2 == core, b & 1, 2 + (b & 1))
+
+    is_middle = jnp.where((plane == 0) | (plane == 3), 0, 1)
+    flags = jnp.stack([source_of(plane ^ r) for r in range(4)] + [is_middle]).astype(jnp.int32)
+    places = jnp.stack([spot ^ r for r in range(PLANE)]).astype(jnp.int32)
+
     def plane_scan(k, v, rate, speed):
         def fade(span):
             return jnp.exp(-speed * span)
@@ -327,50 +352,45 @@
         other = exchange(both, "ctx", 2)
         before = before + jnp.where(y_later, fade((spot & 1).astype(jnp.float32) * rows) * other, 0.0)
         both = jnp.where(y_later, fade(2.0 * rows) * other + both, fade(2.0 * rows) * both + other)
-        return jnp.stack([both, before])
+        return both, before
 
     x_later, y_later = (spot & 1) != 0, (spot & 2) != 0
     w0, w1, w2, w3 = tie(*[group(w_out, r) for r in range(PLANE)])
     f0, n0 = far(w0), near(w0)
-    scanned = box(plane_scan, k, v, rate, speed)
-    f0, n0, w0, w1, w2, w3, scanned = tie(f0, n0, w0, w1, w2, w3, scanned)
+    both, before = box(plane_scan, k, v, rate, speed)
+    f0, n0, w0, w1, w2, w3, both, before = tie(f0, n0, w0, w1, w2, w3, both, before)
 
     arrived = [exchange(w, "ctx", r + 1) for r, w in enumerate((w1, w2, w3))]
-    both, before = scanned[0], scanned[1]
     decay = jnp.exp(-speed * float(PLANE * rows))
     last = shift_ctx(both, PLANE)
-    line = last + decay * shift_ctx(both + decay * last, 2 * PLANE)
-    enter = before + jnp.exp(-speed * (spot * rows).astype(jnp.float32)) * line
-    f0, w0, enter = tie(f0, w0, enter)
+    earlier = shift_ctx(both + decay * last, 2 * PLANE)
+    f0, w0, earlier = tie(f0, w0, earlier)
     out0, mid0 = outward(f0), across(w0)
-    gated = gated_conv(q, k, v, rate, residue, skip, enter)
+    gated = gated_conv(q, k, v, rate, residue, skip, before, (last, earlier, spot))
     rest = jnp.concatenate(arrived)
     gated, rest, out0, mid0 = tie(gated, rest, out0, mid0)
 
     fr, nr = far(rest), near(rest)
     ours = [gated] + [exchange(gated, "ctx", r) for r in range(1, PLANE)]
     restA, restB = rest[:, :wide], rest[:, wide:]
-    fr, nr, rest, restA, restB, *ours = tie(fr, nr, rest, restA, restB, *ours)
-
-    def source_of(b):
-        return jnp.where(b // 2 == core, b & 1, 2 + (b & 1))
-
-    is_middle = jnp.where((plane == 0) | (plane == 3), 0, 1)
-    flags = jnp.stack([source_of(plane ^ r) for r in range(4)] + [is_middle]).astype(jnp.int32)
-    places = jnp.stack([spot ^ r for r in range(PLANE)]).astype(jnp.int32)
+    ours = list(tie(*ours))
+    theirs = [exchange(x, "ch", 1) for x in ours[1:]]
+    fr, nr, rest, restA, restB, flags, places, *held = tie(fr, nr, rest, restA, restB, flags, places, *ours, *theirs)
+    ours, theirs = held[:PLANE], held[PLANE:]
 
     outA, midA = outward(fr[:, :wide]), across(restA)
-    theirs = [exchange(x, "ch", 1) for x in ours]
+    theirs = [exchange(ours[0], "ch", 1)] + theirs
     blocks = [
         (0, None, [((w0,), 0), ((rest,), 0)]),
         (1, None, [((n0,), 0), ((nr,), 0)]),
         (2, None, [((f0,), 0), ((fr,), 0)]),
     ]
     accA, accB = product(flags, places, ours, theirs, blocks, None, [wide, cols - wide], jnp.float32)
-    outA, midA, fr, restB, *accs = tie(outA, midA, fr, restB, *accA, *accB)
+    frB = fr[:, wide:]
+    outA, midA, frB, restB, *accs = tie(outA, midA, frB, restB, *accA, *accB)
     accA, accB = accs[:PLANE], accs[PLANE:]
 
-    outB, midB = outward(fr[:, wide:]), across(restB)
+    outB, midB = outward(frB), across(restB)
 
     def finish(first, out1, mid1, accs):
         blocks = [(3, 4, [((out0, mid0), first), ((out1, mid1), 0)])]

time: 171 us -> 172 us (level)
  starting transfers between devices: 43.6 us -> 45.7 us
    ppermute x22, starting transfers between devices: 23.5 us -> 25.2 us  [exchange(): return lax.ppermute(x, axis, [(i, i ^ flip) for i in range(count)])]
  transfers between devices with their start and end apart: 30 -> 30, of which waited for: 17 -> 17; matrix products, arithmetic and copies ran while one was open for 5% -> 6% of each run, Pallas kernels for 20% -> 20%
where the time goes in v13:
time: 172 us; the launch traced here: 171 us
  waiting for transfers between devices  74.4 us (43%)
  starting transfers between devices  45.7 us (27%)
  Pallas kernels  35.1 us (20%)
  local copies, waits for them, and re-layouts  11.1 us (6%)
  other arithmetic  4.54 us (3%)
    ppermute x22, waiting for transfers between devices, exchange(): return lax.ppermute(x, axis, [(i, i ^ flip) for i in range(count)])  61.8 us
    ppermute x22, starting transfers between devices, exchange(): return lax.ppermute(x, axis, [(i, i ^ flip) for i in range(count)])  25.2 us
    pallas_call x3, Pallas kernels, product(): pl.pallas_call(kernel, in_specs=[smem, smem] + [anywhere] * (2 * parts +...  20.9 us
    pallas_call x1, Pallas kernels, gated_conv(): pl.pallas_call(conv_kernel, grid=(chan // width,), in_specs=[wide, wide,...  8.5 us
    ppermute x2, starting transfers between devices, shift_ctx(): return lax.ppermute(x, 'ctx', [(i, i + by) for i in range(count - by)])  7.04 us
    ppermute x3, starting transfers between devices, outward(): return lax.ppermute(x, 'ctx', [(i, i ^ PLANE) for i in middle])  7.01 us
    ppermute x3, starting transfers between devices, across(): return lax.ppermute(x, 'ctx', [(i, i ^ 3 * PLANE) for i in middle])  6.45 us
    ppermute x3, waiting for transfers between devices, across(): return lax.ppermute(x, 'ctx', [(i, i ^ 3 * PLANE) for i in middle])  6.17 us
  transfers between devices with their start and end apart: 30, of which 17 were waited for; matrix products, arithmetic and copies ran while one was open for 6% of the time, Pallas kernels for 20%

profile of v13, /device:TPU:8, one launch (start us, length us, event | category | flops | bytes accessed | tf_op | source)
XLA Modules:
  0.0 171.2 jit_solution(17865225451625179500)
XLA Ops:
  0.0 2.7 %constant_dynamic-slice_fusion = (bf16[256,768]{1,0:T(8,128)(2,1)}, bf16[256,768]{1,0:T(8,128)(2,1)}, bf16[256,768]{1,0:T(8,128)(2,1)}, bf16[256,768]{1,0:T(8,128)(2,1)}) fusion(bf16[256,3072]{1,0:T(8,128)(2,1)} %param.15, s32[]{:T(128)S(6)} %select_n.84, s32[]{:T(128)S(6)} %select_n.82, s32[]{:T(128)S(6)} %select_n.81, s32[]{:T(128)S(6)} %select_n.83), kind=kLoop, calls=%fused_computation.5 | loop fusion | bytes 3145744 | tf_op jit(solution)/shard_map/dynamic_slice | solution.py:335
  2.7 2.6 %collective-permute-start.2 = (bf16[256,768]{1,0:T(8,128)(2,1)}, bf16[256,768]{1,0:T(8,128)(2,1)S(1)}, u32[]{:S(2)}, u32[]{:S(2)}) collective-permute-start(bf16[256,768]{1,0:T(8,128)(2,1)} %get-tuple-element.220.refs_8_), channel_id=1, source_target_pairs={{0,16},{2,18},{4,20},{6,22},{8,24},{10,26},{12,28},{14,30},{16,0},... | collective-permute-start | bytes 1179656 | tf_op jit(solution)/shard_map/ppermute | solution.py:150
  5.8 15.9 %while.14 = (s32[]{:T(128)}, f32[16,16,128]{2,1,0:T(8,128)}, f32[16,16,128]{2,1,0:T(8,128)}, s32[]{:T(128)}, pred[]{:T(512)}, /*index=5*/bf16[256,2048]{1,0:T(8,...) while((s32[]{:T(128)}, f32[16,16,128]{2,1,0:T(8,128)}, ...), condition=%wide.region_1.2_spmd, body=%wide.region_0.1_spmd.sunk | while | flops 17399808 | bytes 4456652 | solution.py:185
  5.8 4.0 %end_states.3 = f32[16,16,128]{2,1,0:T(8,128)} custom-call(bf16[256,2048]{1,0:T(8,128)(2,1)S(1)} %get-tuple-element.370.k_ref, bf16[256,2048]{1,0:T(8,128)(2,1)S(1)} %get-tuple-element.371.v_ref, f32[16,2048]{1,0:T(8,128)S(1)} %get-tuple-element.372.rate_ref), custom_call_target="tpu_custom_call" | custom-call | flops 16777216 | bytes 2097152 | tf_op jit(solution)/shard_map/while/body/end_states/pallas_call | solution.py:98
  11.3 3.7 %collective-permute-done = f32[16,16,128]{2,1,0:T(8,128)S(1)} collective-permute-done((f32[16,16,128]{2,1,0:T(8,128)}, f32[16,16,128]{2,1,0:T(8,128)S(1)}, u32[]{:S(2)}, u32[]{:S(2)}) %collective-permute-start) | collective-permute-done | bytes 131104 | tf_op jit(solution)/shard_map/while/body/ppermute | solution.py:150
  17.5 3.4 %collective-permute-done.1 = f32[16,16,128]{2,1,0:T(8,128)S(1)} collective-permute-done((f32[16,16,128]{2,1,0:T(8,128)S(1)}, f32[16,16,128]{2,1,0:T(8,128)S(1)}, u32[]{:S(2)}, u32[]{:S(2)}) %collective-permute-start.1) | collective-permute-done | bytes 131104 | tf_op jit(solution)/shard_map/while/body/ppermute | solution.py:150
  23.2 2.4 %collective-permute-start.4 = (f32[16,16,128]{2,1,0:T(8,128)}, f32[16,16,128]{2,1,0:T(8,128)S(1)}, u32[]{:S(2)}, u32[]{:S(2)}) collective-permute-start(f32[16,16,128]{2,1,0:T(8,128)} %get-tuple-element.212), channel_id=1, source_target_pairs={{0,8},{2,10},{4,12},{6,14},{8,16},{10,18},{12,20},{14,22},{16,24},... | collective-permute-start | bytes 393224 | tf_op jit(solution)/shard_map/ppermute | solution.py:145
  31.3 4.7 %collective-permute-start.5 = (f32[16,16,128]{2,1,0:T(8,128)S(1)}, f32[16,16,128]{2,1,0:T(8,128)S(1)}, u32[]{:S(2)}, u32[]{:S(2)}) collective-permute-start(f32[16,16,128]{2,1,0:T(8,128)S(1)} %multiply_add_fusion), channel_id=1, source_target_pairs={{0,16},{2,18},{4,20},{6,22},{8,24},{10,26},{12,28},{14,30},{1,17},... | collective-permute-start | bytes 393224 | tf_op jit(solution)/shard_map/ppermute | solution.py:145
  36.0 4.0 %collective-permute-done.5.refs_1_ = f32[16,16,128]{2,1,0:T(8,128)S(1)} collective-permute-done((f32[16,16,128]{2,1,0:T(8,128)S(1)}, f32[16,16,128]{2,1,0:T(8,128)S(1)}, u32[]{:S(2)}, u32[]{:S(2)}) %collective-permute-start.5) | collective-permute-done | bytes 131104 | tf_op jit(solution)/shard_map/ppermute | solution.py:145
  40.0 2.3 %collective-permute-start.10 = (bf16[256,768]{1,0:T(8,128)(2,1)}, bf16[256,768]{1,0:T(8,128)(2,1)S(1)}, u32[]{:S(2)}, u32[]{:S(2)}) collective-permute-start(bf16[256,768]{1,0:T(8,128)(2,1)} %get-tuple-element.220.refs_8_), channel_id=1, source_target_pairs={{8,16},{10,18},{12,20},{14,22},{16,8},{18,10},{20,12},{22,14},{9,1... | collective-permute-start | bytes 1179656 | tf_op jit(solution)/shard_map/ppermute | solution.py:329
  43.7 8.5 %gated_conv.1.refs_0_ = bf16[2,256,1024]{2,1,0:T(8,128)(2,1)} custom-call(bf16[256,2048]{1,0:T(8,128)(2,1)} %q_ref.1, bf16[256,2048]{1,0:T(8,128)(2,1)S(1)} %get-tuple-element.418, bf16[256,2048]{1,0:T(8,128)(2,1)S(1)} %get-tuple-element.419, f32[16,2048]{1,0:T(8,128)S(1)} %get-tuple-element.428, f32[16,2048]{1,0:T(8,128)} %residue_ref.1, ...), custom_call_target="tpu_custom_call" | custom-call | flops 33554432 | bytes 4194304 | tf_op jit(solution)/shard_map/gated_conv/pallas_call | solution.py:128
  57.1 2.9 %collective-permute-start.11 = (bf16[768,768]{1,0:T(8,128)(2,1)S(1)}, bf16[768,768]{1,0:T(8,128)(2,1)}, u32[]{:S(2)}, u32[]{:S(2)}) collective-permute-start(bf16[768,768]{1,0:T(8,128)(2,1)S(1)} %pad_maximum_fusion.refs_9_), channel_id=1, source_target_pairs={{0,16},{2,18},{4,20},{6,22},{8,24},{10,26},{12,28},{14,30},{16,0},... | collective-permute-start | bytes 3538952 | tf_op jit(solution)/shard_map/ppermute | solution.py:150
  61.5 18.4 %collective-permute-done.13.refs_1_ = bf16[2,256,1024]{2,1,0:T(8,128)(2,1)} collective-permute-done((bf16[2,256,1024]{2,1,0:T(8,128)(2,1)S(1)}, bf16[2,256,1024]{2,1,0:T(8,128)(2,1)}, u32[]{:S(2)}, u32[]{:S(2)}) %collective-permute-start.13) | collective-permute-done | bytes 1048608 | tf_op jit(solution)/shard_map/ppermute | solution.py:150
  79.9 21.5 %collective-permute-done.14.refs_2_ = bf16[2,256,1024]{2,1,0:T(8,128)(2,1)} collective-permute-done((bf16[2,256,1024]{2,1,0:T(8,128)(2,1)S(1)}, bf16[2,256,1024]{2,1,0:T(8,128)(2,1)}, u32[]{:S(2)}, u32[]{:S(2)}) %collective-permute-start.14) | collective-permute-done | bytes 1048608 | tf_op jit(solution)/shard_map/ppermute | solution.py:150
  104.9 3.6 %collective-permute-done.11.refs_13_ = bf16[768,768]{1,0:T(8,128)(2,1)} collective-permute-done((bf16[768,768]{1,0:T(8,128)(2,1)S(1)}, bf16[768,768]{1,0:T(8,128)(2,1)}, u32[]{:S(2)}, u32[]{:S(2)}) %collective-permute-start.11) | collective-permute-done | bytes 1179680 | tf_op jit(solution)/shard_map/ppermute | solution.py:150
  108.4 2.6 %collective-permute-done.12.refs_11_ = bf16[768,768]{1,0:T(8,128)(2,1)} collective-permute-done((bf16[768,768]{1,0:T(8,128)(2,1)S(1)}, bf16[768,768]{1,0:T(8,128)(2,1)}, u32[]{:S(2)}, u32[]{:S(2)}) %collective-permute-start.12) | collective-permute-done | bytes 1179680 | tf_op jit(solution)/shard_map/ppermute | solution.py:150
  113.2 4.4 %collective-permute-start.20 = (bf16[768,512]{1,0:T(8,128)(2,1)}, bf16[768,512]{1,0:T(8,128)(2,1)}, u32[]{:S(2)}, u32[]{:S(2)}) collective-permute-start(bf16[768,512]{1,0:T(8,128)(2,1)} %slice.14), channel_id=1, source_target_pairs={{8,0},{10,2},{12,4},{14,6},{16,24},{18,26},{20,28},{22,30},{9,1},{... | collective-permute-start | bytes 2359304 | tf_op jit(solution)/shard_map/ppermute | solution.py:332
  121.6 11.6 %product.3 = (f32[256,512]{1,0:T(8,128)}, f32[256,512]{1,0:T(8,128)}, f32[256,512]{1,0:T(8,128)}, f32[256,512]{1,0:T(8,128)}, f32[256,256]{1,0:T(8,128)}, /*inde...) custom-call(s32[5]{0:T(128)} %stack.36.flag_ref, s32[4]{0:T(128)} %pad_add_fusion.place_ref, ...), custom_call_target="tpu_custom_call" | custom-call | flops 4831838208 | bytes 11010048 | tf_op jit(solution)/shard_map/product/pallas_call | solution.py:252
  134.5 4.9 %collective-permute-done.21.refs_11_ = bf16[768,512]{1,0:T(8,128)(2,1)S(1)} collective-permute-done((bf16[768,512]{1,0:T(8,128)(2,1)}, bf16[768,512]{1,0:T(8,128)(2,1)S(1)}, u32[]{:S(2)}, u32[]{:S(2)}) %collective-permute-start.21) | collective-permute-done | bytes 786464 | tf_op jit(solution)/shard_map/ppermute | solution.py:329
  140.7 2.2 %collective-permute-start.26 = (bf16[768,256]{1,0:T(8,128)(2,1)S(1)}, bf16[768,256]{1,0:T(8,128)(2,1)S(1)}, u32[]{:S(2)}, u32[]{:S(2)}) collective-permute-start(bf16[768,256]{1,0:T(8,128)(2,1)S(1)} %copy-done.15), channel_id=1, source_target_pairs={{8,16},{10,18},{12,20},{14,22},{16,8},{18,10},{20,12},{22,14},{9,1... | collective-permute-start | bytes 1179656 | tf_op jit(solution)/shard_map/ppermute | solution.py:329
  142.9 5.2 %product.4 = (bf16[256,512]{1,0:T(8,128)(2,1)}, bf16[256,512]{1,0:T(8,128)(2,1)}, bf16[256,512]{1,0:T(8,128)(2,1)}, bf16[256,512]{1,0:T(8,128)(2,1)}) custom-call(s32[5]{0:T(128)} %stack.36.flag_ref, s32[4]{0:T(128)} %pad_add_fusion.place_ref, bf16[2,256,1024]{2,1,0:T(8,128)(2,1)} %gated_conv.1.refs_0_, ...), custom_call_target="tpu_custom_call" | custom-call | flops 1073741824 | bytes 3145728 | tf_op jit(solution)/shard_map/product/pallas_call | solution.py:252
  153.8 4.1 %product.5 = (bf16[256,256]{1,0:T(8,128)(2,1)}, bf16[256,256]{1,0:T(8,128)(2,1)}, bf16[256,256]{1,0:T(8,128)(2,1)}, bf16[256,256]{1,0:T(8,128)(2,1)}) custom-call(s32[5]{0:T(128)} %stack.36.flag_ref, s32[4]{0:T(128)} %pad_add_fusion.place_ref, bf16[2,256,1024]{2,1,0:T(8,128)(2,1)} %gated_conv.1.refs_0_, ...), custom_call_target="tpu_custom_call" | custom-call | flops 536870912 | bytes 2621440 | tf_op jit(solution)/shard_map/product/pallas_call | solution.py:252
  161.4 2.1 %collective-permute-done.23.refs_2_ = bf16[256,512]{1,0:T(8,128)(2,1)S(1)} collective-permute-done((bf16[256,512]{1,0:T(8,128)(2,1)}, bf16[256,512]{1,0:T(8,128)(2,1)S(1)}, u32[]{:S(2)}, u32[]{:S(2)}) %collective-permute-start.23) | collective-permute-done | bytes 262176 | tf_op jit(solution)/shard_map/ppermute | solution.py:150
  166.0 2.6 %collective-permute-done.28.refs_6_ = bf16[256,256]{1,0:T(8,128)(2,1)S(1)} collective-permute-done((bf16[256,256]{1,0:T(8,128)(2,1)}, bf16[256,256]{1,0:T(8,128)(2,1)S(1)}, u32[]{:S(2)}, u32[]{:S(2)}) %collective-permute-start.28) | collective-permute-done | bytes 131104 | tf_op jit(solution)/shard_map/ppermute | solution.py:150
  (94 shorter events, 46.6 us)
Async XLA Ops:
  2.7 19.6 %collective-permute-start.2 = (bf16[256,768]{1,0:T(8,128)(2,1)}, bf16[256,768]{1,0:T(8,128)(2,1)S(1)}, u32[]{:S(2)}, u32[]{:S(2)}) collective-permute-start(bf16[256,768]{1,0:T(8,128)(2,1)} %get-tuple-element.220.refs_8_), channel_id=1, source_target_pairs={{0,16},{2,18},{4,20},{6,22},{8,24},{10,26},{12,28},{14,30},{16,0},... | collective-permute-start | bytes 1179656 | tf_op jit(solution)/shard_map/ppermute | solution.py:150
  5.3 18.0 %collective-permute-start.3 = (bf16[256,768]{1,0:T(8,128)(2,1)}, bf16[256,768]{1,0:T(8,128)(2,1)S(1)}, u32[]{:S(2)}, u32[]{:S(2)}) collective-permute-start(bf16[256,768]{1,0:T(8,128)(2,1)} %get-tuple-element.220.refs_8_), channel_id=1, source_target_pairs={{0,8},{2,10},{4,12},{6,14},{8,0},{10,2},{12,4},{14,6},{16,24},{18,... | collective-permute-start | bytes 1179656 | tf_op jit(solution)/shard_map/ppermute | solution.py:150
  25.6 26.6 %collective-permute-start.6 = (bf16[256,768]{1,0:T(8,128)(2,1)}, bf16[256,768]{1,0:T(8,128)(2,1)S(1)}, u32[]{:S(2)}, u32[]{:S(2)}) collective-permute-start(bf16[256,768]{1,0:T(8,128)(2,1)} %get-tuple-element.216), channel_id=1, source_target_pairs={{0,2},{2,0},{4,6},{6,4},{8,10},{10,8},{12,14},{14,12},{16,18},{18,... | collective-permute-start | bytes 1179656 | tf_op jit(solution)/shard_map/ppermute | solution.py:150
  27.2 25.0 %collective-permute-start.7 = (bf16[256,768]{1,0:T(8,128)(2,1)}, bf16[256,768]{1,0:T(8,128)(2,1)}, u32[]{:S(2)}, u32[]{:S(2)}) collective-permute-start(bf16[256,768]{1,0:T(8,128)(2,1)} %get-tuple-element.217), channel_id=1, source_target_pairs={{0,4},{2,6},{4,0},{6,2},{8,12},{10,14},{12,8},{14,10},{16,20},{18,... | collective-permute-start | bytes 1179656 | tf_op jit(solution)/shard_map/ppermute | solution.py:150
  28.7 23.5 %collective-permute-start.8 = (bf16[256,768]{1,0:T(8,128)(2,1)}, bf16[256,768]{1,0:T(8,128)(2,1)}, u32[]{:S(2)}, u32[]{:S(2)}) collective-permute-start(bf16[256,768]{1,0:T(8,128)(2,1)} %get-tuple-element.218), channel_id=1, source_target_pairs={{0,6},{2,4},{4,2},{6,0},{8,14},{10,12},{12,10},{14,8},{16,22},{18,... | collective-permute-start | bytes 1179656 | tf_op jit(solution)/shard_map/ppermute | solution.py:150
  40.0 13.5 %collective-permute-start.10 = (bf16[256,768]{1,0:T(8,128)(2,1)}, bf16[256,768]{1,0:T(8,128)(2,1)S(1)}, u32[]{:S(2)}, u32[]{:S(2)}) collective-permute-start(bf16[256,768]{1,0:T(8,128)(2,1)} %get-tuple-element.220.refs_8_), channel_id=1, source_target_pairs={{8,16},{10,18},{12,20},{14,22},{16,8},{18,10},{20,12},{22,14},{9,1... | collective-permute-start | bytes 1179656 | tf_op jit(solution)/shard_map/ppermute | solution.py:329
  42.3 11.2 %collective-permute-start.9 = (bf16[256,768]{1,0:T(8,128)(2,1)}, bf16[256,768]{1,0:T(8,128)(2,1)S(1)}, u32[]{:S(2)}, u32[]{:S(2)}) collective-permute-start(bf16[256,768]{1,0:T(8,128)(2,1)} %copy-done.17), channel_id=1, source_target_pairs={{8,0},{10,2},{12,4},{14,6},{16,24},{18,26},{20,28},{22,30},{9,1},{... | collective-permute-start | bytes 1179656 | tf_op jit(solution)/shard_map/ppermute | solution.py:332
  53.6 26.2 %collective-permute-start.13 = (bf16[2,256,1024]{2,1,0:T(8,128)(2,1)S(1)}, bf16[2,256,1024]{2,1,0:T(8,128)(2,1)}, u32[]{:S(2)}, u32[]{:S(2)}) collective-permute-start(bf16[2,256,1024]{2,1,0:T(8,128)(2,1)S(1)} %copy-done.5), channel_id=1, source_target_pairs={{0,2},{2,0},{4,6},{6,4},{8,10},{10,8},{12,14},{14,12},{16,18},{18,... | collective-permute-start | bytes 3145736 | tf_op jit(solution)/shard_map/ppermute | solution.py:150
  55.1 46.2 %collective-permute-start.14 = (bf16[2,256,1024]{2,1,0:T(8,128)(2,1)S(1)}, bf16[2,256,1024]{2,1,0:T(8,128)(2,1)}, u32[]{:S(2)}, u32[]{:S(2)}) collective-permute-start(bf16[2,256,1024]{2,1,0:T(8,128)(2,1)S(1)} %copy-done.5), channel_id=1, source_target_pairs={{0,4},{2,6},{4,0},{6,2},{8,12},{10,14},{12,8},{14,10},{16,20},{18,... | collective-permute-start | bytes 3145736 | tf_op jit(solution)/shard_map/ppermute | solution.py:150
  56.7 44.7 %collective-permute-start.15 = (bf16[2,256,1024]{2,1,0:T(8,128)(2,1)S(1)}, bf16[2,256,1024]{2,1,0:T(8,128)(2,1)}, u32[]{:S(2)}, u32[]{:S(2)}) collective-permute-start(bf16[2,256,1024]{2,1,0:T(8,128)(2,1)S(1)} %copy-done.5), channel_id=1, source_target_pairs={{0,6},{2,4},{4,2},{6,0},{8,14},{10,12},{12,10},{14,8},{16,22},{18,... | collective-permute-start | bytes 3145736 | tf_op jit(solution)/shard_map/ppermute | solution.py:150
  57.1 51.3 %collective-permute-start.11 = (bf16[768,768]{1,0:T(8,128)(2,1)S(1)}, bf16[768,768]{1,0:T(8,128)(2,1)}, u32[]{:S(2)}, u32[]{:S(2)}) collective-permute-start(bf16[768,768]{1,0:T(8,128)(2,1)S(1)} %pad_maximum_fusion.refs_9_), channel_id=1, source_target_pairs={{0,16},{2,18},{4,20},{6,22},{8,24},{10,26},{12,28},{14,30},{16,0},... | collective-permute-start | bytes 3538952 | tf_op jit(solution)/shard_map/ppermute | solution.py:150
  60.1 51.0 %collective-permute-start.12 = (bf16[768,768]{1,0:T(8,128)(2,1)S(1)}, bf16[768,768]{1,0:T(8,128)(2,1)}, u32[]{:S(2)}, u32[]{:S(2)}) collective-permute-start(bf16[768,768]{1,0:T(8,128)(2,1)S(1)} %pad_maximum_fusion.refs_9_), channel_id=1, source_target_pairs={{0,8},{2,10},{4,12},{6,14},{8,0},{10,2},{12,4},{14,6},{16,24},{18,... | collective-permute-start | bytes 3538952 | tf_op jit(solution)/shard_map/ppermute | solution.py:150
  101.4 9.7 %collective-permute-start.16 = (bf16[2,256,1024]{2,1,0:T(8,128)(2,1)}, bf16[2,256,1024]{2,1,0:T(8,128)(2,1)}, u32[]{:S(2)}, u32[]{:S(2)}) collective-permute-start(bf16[2,256,1024]{2,1,0:T(8,128)(2,1)} %collective-permute-done.13.refs_1_), channel_id=1, source_target_pairs={{0,1},{1,0},{2,3},{3,2},{4,5},{5,4},{6,7},{7,6},{8,9},{9,8},{10,11... | collective-permute-start | bytes 3145736 | tf_op jit(solution)/shard_map/ppermute | solution.py:150
  101.4 9.7 %collective-permute-start.17 = (bf16[2,256,1024]{2,1,0:T(8,128)(2,1)}, bf16[2,256,1024]{2,1,0:T(8,128)(2,1)}, u32[]{:S(2)}, u32[]{:S(2)}) collective-permute-start(bf16[2,256,1024]{2,1,0:T(8,128)(2,1)} %collective-permute-done.14.refs_2_), channel_id=1, source_target_pairs={{0,1},{1,0},{2,3},{3,2},{4,5},{5,4},{6,7},{7,6},{8,9},{9,8},{10,11... | collective-permute-start | bytes 3145736 | tf_op jit(solution)/shard_map/ppermute | solution.py:150
  101.9 9.2 %collective-permute-start.18 = (bf16[2,256,1024]{2,1,0:T(8,128)(2,1)}, bf16[2,256,1024]{2,1,0:T(8,128)(2,1)}, u32[]{:S(2)}, u32[]{:S(2)}) collective-permute-start(bf16[2,256,1024]{2,1,0:T(8,128)(2,1)} %collective-permute-done.15.refs_3_), channel_id=1, source_target_pairs={{0,1},{1,0},{2,3},{3,2},{4,5},{5,4},{6,7},{7,6},{8,9},{9,8},{10,11... | collective-permute-start | bytes 3145736 | tf_op jit(solution)/shard_map/ppermute | solution.py:150
  111.1 9.5 %collective-permute-start.19 = (bf16[2,256,1024]{2,1,0:T(8,128)(2,1)S(1)}, bf16[2,256,1024]{2,1,0:T(8,128)(2,1)S(1)}, u32[]{:S(2)}, u32[]{:S(2)}) collective-permute-start(bf16[2,256,1024]{2,1,0:T(8,128)(2,1)S(1)} %copy-done.5), channel_id=1, source_target_pairs={{0,1},{1,0},{2,3},{3,2},{4,5},{5,4},{6,7},{7,6},{8,9},{9,8},{10,11... | collective-permute-start | bytes 3145736 | tf_op jit(solution)/shard_map/ppermute | solution.py:150
  113.2 21.3 %collective-permute-start.20 = (bf16[768,512]{1,0:T(8,128)(2,1)}, bf16[768,512]{1,0:T(8,128)(2,1)}, u32[]{:S(2)}, u32[]{:S(2)}) collective-permute-start(bf16[768,512]{1,0:T(8,128)(2,1)} %slice.14), channel_id=1, source_target_pairs={{8,0},{10,2},{12,4},{14,6},{16,24},{18,26},{20,28},{22,30},{9,1},{... | collective-permute-start | bytes 2359304 | tf_op jit(solution)/shard_map/ppermute | solution.py:332
  117.6 21.8 %collective-permute-start.21 = (bf16[768,512]{1,0:T(8,128)(2,1)}, bf16[768,512]{1,0:T(8,128)(2,1)S(1)}, u32[]{:S(2)}, u32[]{:S(2)}) collective-permute-start(bf16[768,512]{1,0:T(8,128)(2,1)} %slice.12), channel_id=1, source_target_pairs={{8,16},{10,18},{12,20},{14,22},{16,8},{18,10},{20,12},{22,14},{9,1... | collective-permute-start | bytes 2359304 | tf_op jit(solution)/shard_map/ppermute | solution.py:329
  139.4 12.3 %collective-permute-start.25 = (bf16[768,256]{1,0:T(8,128)(2,1)S(1)}, bf16[768,256]{1,0:T(8,128)(2,1)S(1)}, u32[]{:S(2)}, u32[]{:S(2)}) collective-permute-start(bf16[768,256]{1,0:T(8,128)(2,1)S(1)} %slice.15), channel_id=1, source_target_pairs={{8,0},{10,2},{12,4},{14,6},{16,24},{18,26},{20,28},{22,30},{9,1},{... | collective-permute-start | bytes 1179656 | tf_op jit(solution)/shard_map/ppermute | solution.py:332
  140.7 12.3 %collective-permute-start.26 = (bf16[768,256]{1,0:T(8,128)(2,1)S(1)}, bf16[768,256]{1,0:T(8,128)(2,1)S(1)}, u32[]{:S(2)}, u32[]{:S(2)}) collective-permute-start(bf16[768,256]{1,0:T(8,128)(2,1)S(1)} %copy-done.15), channel_id=1, source_target_pairs={{8,16},{10,18},{12,20},{14,22},{16,8},{18,10},{20,12},{22,14},{9,1... | collective-permute-start | bytes 1179656 | tf_op jit(solution)/shard_map/ppermute | solution.py:329
  148.2 12.8 %collective-permute-start.22 = (bf16[256,512]{1,0:T(8,128)(2,1)}, bf16[256,512]{1,0:T(8,128)(2,1)S(1)}, u32[]{:S(2)}, u32[]{:S(2)}) collective-permute-start(bf16[256,512]{1,0:T(8,128)(2,1)} %get-tuple-element.259), channel_id=1, source_target_pairs={{0,2},{2,0},{4,6},{6,4},{8,10},{10,8},{12,14},{14,12},{16,18},{18,... | collective-permute-start | bytes 786440 | tf_op jit(solution)/shard_map/ppermute | solution.py:150
  149.7 13.8 %collective-permute-start.23 = (bf16[256,512]{1,0:T(8,128)(2,1)}, bf16[256,512]{1,0:T(8,128)(2,1)S(1)}, u32[]{:S(2)}, u32[]{:S(2)}) collective-permute-start(bf16[256,512]{1,0:T(8,128)(2,1)} %get-tuple-element.260), channel_id=1, source_target_pairs={{0,4},{2,6},{4,0},{6,2},{8,12},{10,14},{12,8},{14,10},{16,20},{18,... | collective-permute-start | bytes 786440 | tf_op jit(solution)/shard_map/ppermute | solution.py:150
  151.2 13.1 %collective-permute-start.24 = (bf16[256,512]{1,0:T(8,128)(2,1)}, bf16[256,512]{1,0:T(8,128)(2,1)S(1)}, u32[]{:S(2)}, u32[]{:S(2)}) collective-permute-start(bf16[256,512]{1,0:T(8,128)(2,1)} %get-tuple-element.261), channel_id=1, source_target_pairs={{0,6},{2,4},{4,2},{6,0},{8,14},{10,12},{12,10},{14,8},{16,22},{18,... | collective-permute-start | bytes 786440 | tf_op jit(solution)/shard_map/ppermute | solution.py:150
  159.4 9.1 %collective-permute-start.28 = (bf16[256,256]{1,0:T(8,128)(2,1)}, bf16[256,256]{1,0:T(8,128)(2,1)S(1)}, u32[]{:S(2)}, u32[]{:S(2)}) collective-permute-start(bf16[256,256]{1,0:T(8,128)(2,1)} %get-tuple-element.270), channel_id=1, source_target_pairs={{0,4},{2,6},{4,0},{6,2},{8,12},{10,14},{12,8},{14,10},{16,20},{18,... | collective-permute-start | bytes 393224 | tf_op jit(solution)/shard_map/ppermute | solution.py:150
  (25 other events, 349.2 us)

commit v14 on v13

--- a/solution.py
+++ b/solution.py
@@ -57,11 +57,11 @@
     skip = skip_ref[...]
     enter = [enter_ref[m] for m in range(modes)]
     if plane_refs:
-        last_ref, earlier_ref, spot_ref = plane_refs
+        *earlier_refs, spot_ref = plane_refs
         ahead = (spot_ref[0] * rows).astype(jnp.float32)
         for m, rate in enumerate(rates):
-            line = last_ref[m] + jnp.exp(-rate * float(PLANE * rows)) * earlier_ref[m]
-            enter[m] = enter[m] + jnp.exp(-rate * ahead) * line
+            for n, earlier_ref in enumerate(earlier_refs):
+                enter[m] = enter[m] + jnp.exp(-rate * (ahead + float(n * PLANE * rows))) * earlier_ref[m]
 
     def step(t, state):
         at = pl.ds(pl.multiple_of(t * groups, groups), groups)
@@ -122,9 +122,9 @@
     moded_spread = pltpu.VMEM((modes * width // LANES, LANES), jnp.float32)
     extra, extra_specs = [], []
     if planes is not None:
-        last, earlier, spot = planes
-        extra = [last, earlier, spot.reshape(1).astype(jnp.int32)]
-        extra_specs = [state, state, pl.BlockSpec(memory_space=pltpu.SMEM)]
+        earlier, spot = planes
+        extra = [*earlier, spot.reshape(1).astype(jnp.int32)]
+        extra_specs = [state] * len(earlier) + [pl.BlockSpec(memory_space=pltpu.SMEM)]
     return pl.pallas_call(
         conv_kernel,
         grid=(chan // width,),
@@ -314,7 +314,6 @@
     count = lax.axis_size("ctx")
     chunk, feats = w_out.shape
     cols = feats // PLANE
-    wide = 2 * cols // 3
     speed = rate.reshape(modes, chan // LANES, LANES)
 
     def far(x):
@@ -361,43 +360,40 @@
     f0, n0, w0, w1, w2, w3, both, before = tie(f0, n0, w0, w1, w2, w3, both, before)
 
     arrived = [exchange(w, "ctx", r + 1) for r, w in enumerate((w1, w2, w3))]
-    decay = jnp.exp(-speed * float(PLANE * rows))
-    last = shift_ctx(both, PLANE)
-    earlier = shift_ctx(both + decay * last, 2 * PLANE)
-    f0, w0, earlier = tie(f0, w0, earlier)
+    earlier = [shift_ctx(both, PLANE * n) for n in range(1, 4)]
+    f0, w0, *earlier = tie(f0, w0, *earlier)
     out0, mid0 = outward(f0), across(w0)
-    gated = gated_conv(q, k, v, rate, residue, skip, before, (last, earlier, spot))
+    gated = gated_conv(q, k, v, rate, residue, skip, before, (earlier, spot))
     rest = jnp.concatenate(arrived)
     gated, rest, out0, mid0 = tie(gated, rest, out0, mid0)
 
     fr, nr = far(rest), near(rest)
     ours = [gated] + [exchange(gated, "ctx", r) for r in range(1, PLANE)]
-    restA, restB = rest[:, :wide], rest[:, wide:]
     ours = list(tie(*ours))
     theirs = [exchange(x, "ch", 1) for x in ours[1:]]
-    fr, nr, rest, restA, restB, flags, places, *held = tie(fr, nr, rest, restA, restB, flags, places, *ours, *theirs)
+    fr, nr, rest, flags, places, *held = tie(fr, nr, rest, flags, places, *ours, *theirs)
     ours, theirs = held[:PLANE], held[PLANE:]
 
-    outA, midA = outward(fr[:, :wide]), across(restA)
+    out1, mid1 = outward(fr), across(rest)
     theirs = [exchange(ours[0], "ch", 1)] + theirs
     blocks = [
         (0, None, [((w0,), 0), ((rest,), 0)]),
         (1, None, [((n0,), 0), ((nr,), 0)]),
         (2, None, [((f0,), 0), ((fr,), 0)]),
     ]
-    accA, accB = product(flags, places, ours, theirs, blocks, None, [wide, cols - wide], jnp.float32)
-    frB = fr[:, wide:]
-    outA, midA, frB, restB, *accs = tie(outA, midA, frB, restB, *accA, *accB)
-    accA, accB = accs[:PLANE], accs[PLANE:]
-
-    outB, midB = outward(frB), across(restB)
-
-    def finish(first, out1, mid1, accs):
-        blocks = [(3, 4, [((out0, mid0), first), ((out1, mid1), 0)])]
-        (made,) = product(flags, places, ours, theirs, blocks, accs, [accs[0].shape[1]], jnp.bfloat16)
-        return [made[0]] + [exchange(made[r], "ctx", r) for r in range(1, PLANE)]
-
-    return assemble(places, [finish(0, outA, midA, accA), finish(wide, outB, midB, accB)])
+    (accs,) = product(flags, places, ours, theirs, blocks, None, [cols], jnp.float32)
+    out1, mid1, *accs = tie(out1, mid1, *accs)
+
+    blocks = [(3, 4, [((out0, mid0), 0), ((out1, mid1), 0)])]
+
+    def finish(*spots):
+        chosen = [ours[r] for r in spots], [theirs[r] for r in spots]
+        return product(flags, places, *chosen, blocks, [accs[r] for r in spots], [cols], jnp.bfloat16)[0]
+
+    (made3,) = finish(3)
+    back3 = exchange(made3, "ctx", 3)
+    back3, made0, made1, made2 = tie(back3, *finish(0, 1, 2))
+    return assemble(places, [[made0, exchange(made1, "ctx", 1), exchange(made2, "ctx", 2), back3]])
 
 
 def body(q, k, v, residue, rate, skip, w_out):
@@ -411,7 +407,7 @@
         and cores == 2
         and chan == 8 * chunk
         and chunk % LANES == 0
-        and feats % (6 * PLANE * LANES) == 0
+        and feats % (2 * PLANE * LANES) == 0
     )
     skip = skip.reshape(groups, LANES)
     if split:

time: 172 us -> 173 us (level)
  waiting for transfers between devices: 74.4 us -> 82.6 us
  local copies, waits for them, and re-layouts: 11.1 us -> 6.78 us
  other arithmetic: 4.54 us -> 2.41 us
    ppermute x3 -> x2, waiting for transfers between devices: 1.3 us -> 11.8 us  [outward(): return lax.ppermute(x, 'ctx', [(i, i ^ PLANE) for i in middle])]
    slice x4 -> x0, local copies, waits for them, and re-layouts: 4.88 us -> none  [the longest x1 2.09 us: split_block(): outA, midA = (outward(fr[:, :wide]), across(restA))]
    ppermute x22 -> x19, starting transfers between devices: 25.2 us -> 20.7 us  [exchange(): return lax.ppermute(x, axis, [(i, i ^ flip) for i in range(count)])]
    ppermute x3 -> x2, starting transfers between devices: 6.45 us -> 9.58 us  [across(): return lax.ppermute(x, 'ctx', [(i, i ^ 3 * PLANE) for i in middle])]
    ppermute x3 -> x2, waiting for transfers between devices: 6.17 us -> 4.08 us  [across(): return lax.ppermute(x, 'ctx', [(i, i ^ 3 * PLANE) for i in middle])]
    unnamed x39 -> x31, local copies, waits for them, and re-layouts: 2.83 us -> 3.62 us
    ppermute x3 -> x2, starting transfers between devices: 7.01 us -> 6.33 us  [outward(): return lax.ppermute(x, 'ctx', [(i, i ^ PLANE) for i in middle])]
    ppermute x2 -> x3, starting transfers between devices: 7.04 us -> 7.69 us  [shift_ctx(): return lax.ppermute(x, 'ctx', [(i, i + by) for i in range(count - by)])]
  transfers between devices with their start and end apart: 30 -> 26, of which waited for: 17 -> 15; matrix products, arithmetic and copies ran while one was open for 6% -> 2% of each run, Pallas kernels for 20% -> 18%
where the time goes in v14:
time: 173 us; the launch traced here: 172 us
  waiting for transfers between devices  82.6 us (48%)
  starting transfers between devices  44.3 us (26%)
  Pallas kernels  35.9 us (21%)
  local copies, waits for them, and re-layouts  6.78 us (4%)
  other arithmetic  2.41 us (1%)
    ppermute x19, waiting for transfers between devices, exchange(): return lax.ppermute(x, axis, [(i, i ^ flip) for i in range(count)])  61.4 us
    pallas_call x3, Pallas kernels, product(): pl.pallas_call(kernel, in_specs=[smem, smem] + [anywhere] * (2 * parts +...  21.6 us
    ppermute x19, starting transfers between devices, exchange(): return lax.ppermute(x, axis, [(i, i ^ flip) for i in range(count)])  20.7 us
    ppermute x2, waiting for transfers between devices, outward(): return lax.ppermute(x, 'ctx', [(i, i ^ PLANE) for i in middle])  11.8 us
    ppermute x2, starting transfers between devices, across(): return lax.ppermute(x, 'ctx', [(i, i ^ 3 * PLANE) for i in middle])  9.58 us
    pallas_call x1, Pallas kernels, gated_conv(): pl.pallas_call(conv_kernel, grid=(chan // width,), in_specs=[wide, wide,...  8.55 us
    ppermute x3, starting transfers between devices, shift_ctx(): return lax.ppermute(x, 'ctx', [(i, i + by) for i in range(count - by)])  7.69 us
    ppermute x2, starting transfers between devices, outward(): return lax.ppermute(x, 'ctx', [(i, i ^ PLANE) for i in middle])  6.33 us
  transfers between devices with their start and end apart: 26, of which 15 were waited for; matrix products, arithmetic and copies ran while one was open for 2% of the time, Pallas kernels for 18%

profile of v14, /device:TPU:8, one launch (start us, length us, event | category | flops | bytes accessed | tf_op | source)
XLA Modules:
  0.0 172.3 jit_solution(16141654778596191035)
XLA Ops:
  0.0 2.6 %constant_dynamic-slice_fusion = (bf16[256,768]{1,0:T(8,128)(2,1)}, bf16[256,768]{1,0:T(8,128)(2,1)}, bf16[256,768]{1,0:T(8,128)(2,1)S(1)}, bf16[256,768]{1,0:T(8,128)(2,1)}) fusion(bf16[256,3072]{1,0:T(8,128)(2,1)} %param.15, s32[]{:T(128)S(6)} %select_n.84, s32[]{:T(128)S(6)} %select_n.82, s32[]{:T(128)S(6)} %select_n.81, s32[]{:T(128)S(6)} %select_n.83), kind=kLoop, calls=%fused_computation.4 | loop fusion | bytes 3145744 | tf_op jit(solution)/shard_map/dynamic_slice | solution.py:334
  2.6 3.0 %collective-permute-start.2 = (bf16[256,768]{1,0:T(8,128)(2,1)S(1)}, bf16[256,768]{1,0:T(8,128)(2,1)}, u32[]{:S(2)}, u32[]{:S(2)}) collective-permute-start(bf16[256,768]{1,0:T(8,128)(2,1)S(1)} %get-tuple-element.211.refs_8_), channel_id=1, source_target_pairs={{0,16},{2,18},{4,20},{6,22},{8,24},{10,26},{12,28},{14,30},{16,0},... | collective-permute-start | bytes 1179656 | tf_op jit(solution)/shard_map/ppermute | solution.py:150
  5.7 15.9 %while.14 = (s32[]{:T(128)}, f32[16,16,128]{2,1,0:T(8,128)}, f32[16,16,128]{2,1,0:T(8,128)}, s32[]{:T(128)}, pred[]{:T(512)}, /*index=5*/bf16[256,2048]{1,0:T(8,...) while((s32[]{:T(128)}, f32[16,16,128]{2,1,0:T(8,128)}, ...), condition=%wide.region_1.2_spmd, body=%wide.region_0.1_spmd.sunk | while | flops 17399808 | bytes 4456652 | solution.py:185
  5.7 4.0 %end_states.3 = f32[16,16,128]{2,1,0:T(8,128)} custom-call(bf16[256,2048]{1,0:T(8,128)(2,1)S(1)} %get-tuple-element.348.k_ref, bf16[256,2048]{1,0:T(8,128)(2,1)S(1)} %get-tuple-element.349.v_ref, f32[16,2048]{1,0:T(8,128)S(1)} %get-tuple-element.350.rate_ref), custom_call_target="tpu_custom_call" | custom-call | flops 16777216 | bytes 2097152 | tf_op jit(solution)/shard_map/while/body/end_states/pallas_call | solution.py:98
  11.1 3.7 %collective-permute-done = f32[16,16,128]{2,1,0:T(8,128)S(1)} collective-permute-done((f32[16,16,128]{2,1,0:T(8,128)}, f32[16,16,128]{2,1,0:T(8,128)S(1)}, u32[]{:S(2)}, u32[]{:S(2)}) %collective-permute-start) | collective-permute-done | bytes 131104 | tf_op jit(solution)/shard_map/while/body/ppermute | solution.py:150
  17.4 3.4 %collective-permute-done.1 = f32[16,16,128]{2,1,0:T(8,128)S(1)} collective-permute-done((f32[16,16,128]{2,1,0:T(8,128)S(1)}, f32[16,16,128]{2,1,0:T(8,128)S(1)}, u32[]{:S(2)}, u32[]{:S(2)}) %collective-permute-start.1) | collective-permute-done | bytes 131104 | tf_op jit(solution)/shard_map/while/body/ppermute | solution.py:150
  27.3 5.1 %collective-permute-start.5 = (f32[16,16,128]{2,1,0:T(8,128)}, f32[16,16,128]{2,1,0:T(8,128)S(1)}, u32[]{:S(2)}, u32[]{:S(2)}) collective-permute-start(f32[16,16,128]{2,1,0:T(8,128)} %get-tuple-element.203), channel_id=1, source_target_pairs={{0,16},{2,18},{4,20},{6,22},{8,24},{10,26},{12,28},{14,30},{1,17},... | collective-permute-start | bytes 393224 | tf_op jit(solution)/shard_map/ppermute | solution.py:145
  34.4 2.7 %collective-permute-done.5.refs_1_ = f32[16,16,128]{2,1,0:T(8,128)S(1)} collective-permute-done((f32[16,16,128]{2,1,0:T(8,128)}, f32[16,16,128]{2,1,0:T(8,128)S(1)}, u32[]{:S(2)}, u32[]{:S(2)}) %collective-permute-start.5) | collective-permute-done | bytes 131104 | tf_op jit(solution)/shard_map/ppermute | solution.py:145
  37.0 2.6 %collective-permute-done.4.refs_0_ = f32[16,16,128]{2,1,0:T(8,128)} collective-permute-done((f32[16,16,128]{2,1,0:T(8,128)}, f32[16,16,128]{2,1,0:T(8,128)}, u32[]{:S(2)}, u32[]{:S(2)}) %collective-permute-start.4) | collective-permute-done | bytes 131104 | tf_op jit(solution)/shard_map/ppermute | solution.py:145
  41.1 7.7 %collective-permute-start.11 = (bf16[256,768]{1,0:T(8,128)(2,1)}, bf16[256,768]{1,0:T(8,128)(2,1)}, u32[]{:S(2)}, u32[]{:S(2)}) collective-permute-start(bf16[256,768]{1,0:T(8,128)(2,1)} %copy-done.11), channel_id=1, source_target_pairs={{8,16},{10,18},{12,20},{14,22},{16,8},{18,10},{20,12},{22,14},{9,1... | collective-permute-start | bytes 1179656 | tf_op jit(solution)/shard_map/ppermute | solution.py:328
  48.8 8.6 %gated_conv.1.refs_0_ = bf16[2,256,1024]{2,1,0:T(8,128)(2,1)} custom-call(bf16[256,2048]{1,0:T(8,128)(2,1)} %q_ref.1, bf16[256,2048]{1,0:T(8,128)(2,1)S(1)} %get-tuple-element.393, bf16[256,2048]{1,0:T(8,128)(2,1)S(1)} %get-tuple-element.394, f32[16,2048]{1,0:T(8,128)S(1)} %get-tuple-element.398, f32[16,2048]{1,0:T(8,128)} %residue_ref.1, ...), custom_call_target="tpu_custom_call" | custom-call | flops 33554432 | bytes 4194304 | tf_op jit(solution)/shard_map/gated_conv/pallas_call | solution.py:128
  59.0 2.4 %collective-permute-start.16 = (bf16[2,256,1024]{2,1,0:T(8,128)(2,1)S(1)}, bf16[2,256,1024]{2,1,0:T(8,128)(2,1)}, u32[]{:S(2)}, u32[]{:S(2)}) collective-permute-start(bf16[2,256,1024]{2,1,0:T(8,128)(2,1)S(1)} %copy-done.7), channel_id=1, source_target_pairs={{0,6},{2,4},{4,2},{6,0},{8,14},{10,12},{12,10},{14,8},{16,22},{18,... | collective-permute-start | bytes 3145736 | tf_op jit(solution)/shard_map/ppermute | solution.py:150
  64.0 22.1 %collective-permute-done.16.refs_3_.refs_0_ = bf16[2,256,1024]{2,1,0:T(8,128)(2,1)} collective-permute-done((bf16[2,256,1024]{2,1,0:T(8,128)(2,1)S(1)}, bf16[2,256,1024]{2,1,0:T(8,128)(2,1)}, u32[]{:S(2)}, u32[]{:S(2)}) %collective-permute-start.16) | collective-permute-done | bytes 1048608 | tf_op jit(solution)/shard_map/ppermute | solution.py:150
  86.1 13.7 %collective-permute-done.15.refs_2_ = bf16[2,256,1024]{2,1,0:T(8,128)(2,1)S(1)} collective-permute-done((bf16[2,256,1024]{2,1,0:T(8,128)(2,1)S(1)}, bf16[2,256,1024]{2,1,0:T(8,128)(2,1)S(1)}, u32[]{:S(2)}, u32[]{:S(2)}) %collective-permute-start.15) | collective-permute-done | bytes 1048608 | tf_op jit(solution)/shard_map/ppermute | solution.py:150
  103.6 3.5 %collective-permute-done.12.refs_13_ = bf16[768,768]{1,0:T(8,128)(2,1)} collective-permute-done((bf16[768,768]{1,0:T(8,128)(2,1)S(1)}, bf16[768,768]{1,0:T(8,128)(2,1)}, u32[]{:S(2)}, u32[]{:S(2)}) %collective-permute-start.12) | collective-permute-done | bytes 1179680 | tf_op jit(solution)/shard_map/ppermute | solution.py:150
  107.3 4.8 %collective-permute-start.20 = (bf16[768,768]{1,0:T(8,128)(2,1)}, bf16[768,768]{1,0:T(8,128)(2,1)S(1)}, u32[]{:S(2)}, u32[]{:S(2)}) collective-permute-start(bf16[768,768]{1,0:T(8,128)(2,1)} %collective-permute-done.12.refs_13_), channel_id=1, source_target_pairs={{8,0},{10,2},{12,4},{14,6},{16,24},{18,26},{20,28},{22,30},{9,1},{... | collective-permute-start | bytes 3538952 | tf_op jit(solution)/shard_map/ppermute | solution.py:331
  114.0 12.3 %product.3 = (f32[256,768]{1,0:T(8,128)}, f32[256,768]{1,0:T(8,128)}, f32[256,768]{1,0:T(8,128)}, f32[256,768]{1,0:T(8,128)}) custom-call(s32[5]{0:T(128)} %stack.36.flag_ref, s32[4]{0:T(128)} %pad_add_fusion.place_ref, bf16[2,256,1024]{2,1,0:T(8,128)(2,1)} %gated_conv.1.refs_0_, bf16[2,256,1024]{2,1,0:T(8,128)(2,1)} %collective-permute-done.14.refs_1_, ...), custom_call_target="tpu_custom_call" | custom-call | flops 4831838208 | bytes 11010048 | tf_op jit(solution)/shard_map/product/pallas_call | solution.py:252
  126.4 11.8 %collective-permute-done.20.refs_4_.refs_8_ = bf16[768,768]{1,0:T(8,128)(2,1)S(1)} collective-permute-done((bf16[768,768]{1,0:T(8,128)(2,1)}, bf16[768,768]{1,0:T(8,128)(2,1)S(1)}, u32[]{:S(2)}, u32[]{:S(2)}) %collective-permute-start.20) | collective-permute-done | bytes 1179680 | tf_op jit(solution)/shard_map/ppermute | solution.py:331
  138.2 4.1 %collective-permute-done.21.refs_5_.refs_9_ = bf16[768,768]{1,0:T(8,128)(2,1)S(1)} collective-permute-done((bf16[768,768]{1,0:T(8,128)(2,1)}, bf16[768,768]{1,0:T(8,128)(2,1)S(1)}, u32[]{:S(2)}, u32[]{:S(2)}) %collective-permute-start.21) | collective-permute-done | bytes 1179680 | tf_op jit(solution)/shard_map/ppermute | solution.py:328
  143.3 3.8 %product.4 = bf16[256,768]{1,0:T(8,128)(2,1)} custom-call(s32[5]{0:T(128)} %stack.36.flag_ref, s32[4]{0:T(128)} %pad_add_fusion.place_ref, bf16[2,256,1024]{2,1,0:T(8,128)(2,1)} %collective-permute-done.16.refs_3_.refs_0_, bf16[2,256,1024]{2,1,0:T(8,128)(2,1)} %collective-permute-done.19.refs_7_.refs_1_, bf16[256,768]{1,0:T(8,128)(2,1)} %copy-done.8, ...), custom_call_target="tpu_custom_call" | custom-call | flops 402653184 | bytes 2097152 | tf_op jit(solution)/shard_map/product/pallas_call | solution.py:252
  147.1 2.5 %collective-permute-start.23 = (bf16[256,768]{1,0:T(8,128)(2,1)}, bf16[256,768]{1,0:T(8,128)(2,1)S(1)}, u32[]{:S(2)}, u32[]{:S(2)}) collective-permute-start(bf16[256,768]{1,0:T(8,128)(2,1)} %product.4), channel_id=1, source_target_pairs={{0,6},{2,4},{4,2},{6,0},{8,14},{10,12},{12,10},{14,8},{16,22},{18,... | collective-permute-start | bytes 1179656 | tf_op jit(solution)/shard_map/ppermute | solution.py:150
  149.6 5.5 %product.5 = (bf16[256,768]{1,0:T(8,128)(2,1)}, bf16[256,768]{1,0:T(8,128)(2,1)}, bf16[256,768]{1,0:T(8,128)(2,1)}) custom-call(s32[5]{0:T(128)} %stack.36.flag_ref, s32[4]{0:T(128)} %pad_add_fusion.place_ref, bf16[2,256,1024]{2,1,0:T(8,128)(2,1)} %gated_conv.1.refs_0_, bf16[2,256,1024]{2,1,0:T(8,128)(2,1)} %collective-permute-done.14.refs_1_, ...), custom_call_target="tpu_custom_call" | custom-call | flops 1207959552 | bytes 3145728 | tf_op jit(solution)/shard_map/product/pallas_call | solution.py:252
  155.2 3.5 %collective-permute-done.23.refs_3_ = bf16[256,768]{1,0:T(8,128)(2,1)S(1)} collective-permute-done((bf16[256,768]{1,0:T(8,128)(2,1)}, bf16[256,768]{1,0:T(8,128)(2,1)S(1)}, u32[]{:S(2)}, u32[]{:S(2)}) %collective-permute-start.23) | collective-permute-done | bytes 393248 | tf_op jit(solution)/shard_map/ppermute | solution.py:150
  161.7 6.7 %collective-permute-done.24.refs_1_ = bf16[256,768]{1,0:T(8,128)(2,1)S(1)} collective-permute-done((bf16[256,768]{1,0:T(8,128)(2,1)}, bf16[256,768]{1,0:T(8,128)(2,1)S(1)}, u32[]{:S(2)}, u32[]{:S(2)}) %collective-permute-start.24) | collective-permute-done | bytes 393248 | tf_op jit(solution)/shard_map/ppermute | solution.py:150
  (73 shorter events, 31.8 us)
Async XLA Ops:
  2.6 19.0 %collective-permute-start.3 = (bf16[256,768]{1,0:T(8,128)(2,1)S(1)}, bf16[256,768]{1,0:T(8,128)(2,1)S(1)}, u32[]{:S(2)}, u32[]{:S(2)}) collective-permute-start(bf16[256,768]{1,0:T(8,128)(2,1)S(1)} %get-tuple-element.211.refs_8_), channel_id=1, source_target_pairs={{0,8},{2,10},{4,12},{6,14},{8,0},{10,2},{12,4},{14,6},{16,24},{18,... | collective-permute-start | bytes 1179656 | tf_op jit(solution)/shard_map/ppermute | solution.py:150
  2.6 20.5 %collective-permute-start.2 = (bf16[256,768]{1,0:T(8,128)(2,1)S(1)}, bf16[256,768]{1,0:T(8,128)(2,1)}, u32[]{:S(2)}, u32[]{:S(2)}) collective-permute-start(bf16[256,768]{1,0:T(8,128)(2,1)S(1)} %get-tuple-element.211.refs_8_), channel_id=1, source_target_pairs={{0,16},{2,18},{4,20},{6,22},{8,24},{10,26},{12,28},{14,30},{16,0},... | collective-permute-start | bytes 1179656 | tf_op jit(solution)/shard_map/ppermute | solution.py:150
  23.1 9.3 %collective-permute-start.6 = (f32[16,16,128]{2,1,0:T(8,128)}, f32[16,16,128]{2,1,0:T(8,128)S(1)}, u32[]{:S(2)}, u32[]{:S(2)}) collective-permute-start(f32[16,16,128]{2,1,0:T(8,128)} %get-tuple-element.203), channel_id=1, source_target_pairs={{0,24},{2,26},{4,28},{6,30},{1,25},{3,27},{5,29},{7,31}} | collective-permute-start | bytes 393224 | tf_op jit(solution)/shard_map/ppermute | solution.py:145
  23.7 33.6 %collective-permute-start.7 = (bf16[256,768]{1,0:T(8,128)(2,1)}, bf16[256,768]{1,0:T(8,128)(2,1)S(1)}, u32[]{:S(2)}, u32[]{:S(2)}) collective-permute-start(bf16[256,768]{1,0:T(8,128)(2,1)} %get-tuple-element.207), channel_id=1, source_target_pairs={{0,2},{2,0},{4,6},{6,4},{8,10},{10,8},{12,14},{14,12},{16,18},{18,... | collective-permute-start | bytes 1179656 | tf_op jit(solution)/shard_map/ppermute | solution.py:150
  25.3 32.1 %collective-permute-start.8 = (bf16[256,768]{1,0:T(8,128)(2,1)}, bf16[256,768]{1,0:T(8,128)(2,1)S(1)}, u32[]{:S(2)}, u32[]{:S(2)}) collective-permute-start(bf16[256,768]{1,0:T(8,128)(2,1)} %get-tuple-element.208), channel_id=1, source_target_pairs={{0,4},{2,6},{4,0},{6,2},{8,12},{10,14},{12,8},{14,10},{16,20},{18,... | collective-permute-start | bytes 1179656 | tf_op jit(solution)/shard_map/ppermute | solution.py:150
  26.8 30.6 %collective-permute-start.9 = (bf16[256,768]{1,0:T(8,128)(2,1)}, bf16[256,768]{1,0:T(8,128)(2,1)S(1)}, u32[]{:S(2)}, u32[]{:S(2)}) collective-permute-start(bf16[256,768]{1,0:T(8,128)(2,1)} %get-tuple-element.209), channel_id=1, source_target_pairs={{0,6},{2,4},{4,2},{6,0},{8,14},{10,12},{12,10},{14,8},{16,22},{18,... | collective-permute-start | bytes 1179656 | tf_op jit(solution)/shard_map/ppermute | solution.py:150
  27.3 9.7 %collective-permute-start.5 = (f32[16,16,128]{2,1,0:T(8,128)}, f32[16,16,128]{2,1,0:T(8,128)S(1)}, u32[]{:S(2)}, u32[]{:S(2)}) collective-permute-start(f32[16,16,128]{2,1,0:T(8,128)} %get-tuple-element.203), channel_id=1, source_target_pairs={{0,16},{2,18},{4,20},{6,22},{8,24},{10,26},{12,28},{14,30},{1,17},... | collective-permute-start | bytes 393224 | tf_op jit(solution)/shard_map/ppermute | solution.py:145
  32.4 7.2 %collective-permute-start.4 = (f32[16,16,128]{2,1,0:T(8,128)}, f32[16,16,128]{2,1,0:T(8,128)}, u32[]{:S(2)}, u32[]{:S(2)}) collective-permute-start(f32[16,16,128]{2,1,0:T(8,128)} %get-tuple-element.203), channel_id=1, source_target_pairs={{0,8},{2,10},{4,12},{6,14},{8,16},{10,18},{12,20},{14,22},{16,24},... | collective-permute-start | bytes 393224 | tf_op jit(solution)/shard_map/ppermute | solution.py:145
  39.6 17.9 %collective-permute-start.10 = (bf16[256,768]{1,0:T(8,128)(2,1)}, bf16[256,768]{1,0:T(8,128)(2,1)S(1)}, u32[]{:S(2)}, u32[]{:S(2)}) collective-permute-start(bf16[256,768]{1,0:T(8,128)(2,1)} %collective-permute-done.2.refs_12_), channel_id=1, source_target_pairs={{8,0},{10,2},{12,4},{14,6},{16,24},{18,26},{20,28},{22,30},{9,1},{... | collective-permute-start | bytes 1179656 | tf_op jit(solution)/shard_map/ppermute | solution.py:331
  41.1 16.4 %collective-permute-start.11 = (bf16[256,768]{1,0:T(8,128)(2,1)}, bf16[256,768]{1,0:T(8,128)(2,1)}, u32[]{:S(2)}, u32[]{:S(2)}) collective-permute-start(bf16[256,768]{1,0:T(8,128)(2,1)} %copy-done.11), channel_id=1, source_target_pairs={{8,16},{10,18},{12,20},{14,22},{16,8},{18,10},{20,12},{22,14},{9,1... | collective-permute-start | bytes 1179656 | tf_op jit(solution)/shard_map/ppermute | solution.py:328
  59.0 27.1 %collective-permute-start.16 = (bf16[2,256,1024]{2,1,0:T(8,128)(2,1)S(1)}, bf16[2,256,1024]{2,1,0:T(8,128)(2,1)}, u32[]{:S(2)}, u32[]{:S(2)}) collective-permute-start(bf16[2,256,1024]{2,1,0:T(8,128)(2,1)S(1)} %copy-done.7), channel_id=1, source_target_pairs={{0,6},{2,4},{4,2},{6,0},{8,14},{10,12},{12,10},{14,8},{16,22},{18,... | collective-permute-start | bytes 3145736 | tf_op jit(solution)/shard_map/ppermute | solution.py:150
  61.5 38.4 %collective-permute-start.15 = (bf16[2,256,1024]{2,1,0:T(8,128)(2,1)S(1)}, bf16[2,256,1024]{2,1,0:T(8,128)(2,1)S(1)}, u32[]{:S(2)}, u32[]{:S(2)}) collective-permute-start(bf16[2,256,1024]{2,1,0:T(8,128)(2,1)S(1)} %copy-done.7), channel_id=1, source_target_pairs={{0,4},{2,6},{4,0},{6,2},{8,12},{10,14},{12,8},{14,10},{16,20},{18,... | collective-permute-start | bytes 3145736 | tf_op jit(solution)/shard_map/ppermute | solution.py:150
  62.0 38.0 %collective-permute-start.14 = (bf16[2,256,1024]{2,1,0:T(8,128)(2,1)S(1)}, bf16[2,256,1024]{2,1,0:T(8,128)(2,1)}, u32[]{:S(2)}, u32[]{:S(2)}) collective-permute-start(bf16[2,256,1024]{2,1,0:T(8,128)(2,1)S(1)} %copy-done.7), channel_id=1, source_target_pairs={{0,2},{2,0},{4,6},{6,4},{8,10},{10,8},{12,14},{14,12},{16,18},{18,... | collective-permute-start | bytes 3145736 | tf_op jit(solution)/shard_map/ppermute | solution.py:150
  62.5 41.1 %collective-permute-start.13 = (bf16[768,768]{1,0:T(8,128)(2,1)S(1)}, bf16[768,768]{1,0:T(8,128)(2,1)}, u32[]{:S(2)}, u32[]{:S(2)}) collective-permute-start(bf16[768,768]{1,0:T(8,128)(2,1)S(1)} %pad_maximum_fusion.refs_9_), channel_id=1, source_target_pairs={{0,8},{2,10},{4,12},{6,14},{8,0},{10,2},{12,4},{14,6},{16,24},{18,... | collective-permute-start | bytes 3538952 | tf_op jit(solution)/shard_map/ppermute | solution.py:150
  62.5 44.6 %collective-permute-start.12 = (bf16[768,768]{1,0:T(8,128)(2,1)S(1)}, bf16[768,768]{1,0:T(8,128)(2,1)}, u32[]{:S(2)}, u32[]{:S(2)}) collective-permute-start(bf16[768,768]{1,0:T(8,128)(2,1)S(1)} %pad_maximum_fusion.refs_9_), channel_id=1, source_target_pairs={{0,16},{2,18},{4,20},{6,22},{8,24},{10,26},{12,28},{14,30},{16,0},... | collective-permute-start | bytes 3538952 | tf_op jit(solution)/shard_map/ppermute | solution.py:150
  100.0 7.1 %collective-permute-start.17 = (bf16[2,256,1024]{2,1,0:T(8,128)(2,1)}, bf16[2,256,1024]{2,1,0:T(8,128)(2,1)}, u32[]{:S(2)}, u32[]{:S(2)}) collective-permute-start(bf16[2,256,1024]{2,1,0:T(8,128)(2,1)} %collective-permute-done.14.refs_1_), channel_id=1, source_target_pairs={{0,1},{1,0},{2,3},{3,2},{4,5},{5,4},{6,7},{7,6},{8,9},{9,8},{10,11... | collective-permute-start | bytes 3145736 | tf_op jit(solution)/shard_map/ppermute | solution.py:150
  100.0 7.1 %collective-permute-start.18 = (bf16[2,256,1024]{2,1,0:T(8,128)(2,1)S(1)}, bf16[2,256,1024]{2,1,0:T(8,128)(2,1)}, u32[]{:S(2)}, u32[]{:S(2)}) collective-permute-start(bf16[2,256,1024]{2,1,0:T(8,128)(2,1)S(1)} %collective-permute-done.15.refs_2_), channel_id=1, source_target_pairs={{0,1},{1,0},{2,3},{3,2},{4,5},{5,4},{6,7},{7,6},{8,9},{9,8},{10,11... | collective-permute-start | bytes 3145736 | tf_op jit(solution)/shard_map/ppermute | solution.py:150
  100.6 6.6 %collective-permute-start.19 = (bf16[2,256,1024]{2,1,0:T(8,128)(2,1)}, bf16[2,256,1024]{2,1,0:T(8,128)(2,1)}, u32[]{:S(2)}, u32[]{:S(2)}) collective-permute-start(bf16[2,256,1024]{2,1,0:T(8,128)(2,1)} %collective-permute-done.16.refs_3_.refs_0_), channel_id=1, source_target_pairs={{0,1},{1,0},{2,3},{3,2},{4,5},{5,4},{6,7},{7,6},{8,9},{9,8},{10,11... | collective-permute-start | bytes 3145736 | tf_op jit(solution)/shard_map/ppermute | solution.py:150
  107.2 6.9 %collective-permute-start.22 = (bf16[2,256,1024]{2,1,0:T(8,128)(2,1)S(1)}, bf16[2,256,1024]{2,1,0:T(8,128)(2,1)}, u32[]{:S(2)}, u32[]{:S(2)}) collective-permute-start(bf16[2,256,1024]{2,1,0:T(8,128)(2,1)S(1)} %copy-done.7), channel_id=1, source_target_pairs={{0,1},{1,0},{2,3},{3,2},{4,5},{5,4},{6,7},{7,6},{8,9},{9,8},{10,11... | collective-permute-start | bytes 3145736 | tf_op jit(solution)/shard_map/ppermute | solution.py:150
  107.3 30.9 %collective-permute-start.20 = (bf16[768,768]{1,0:T(8,128)(2,1)}, bf16[768,768]{1,0:T(8,128)(2,1)S(1)}, u32[]{:S(2)}, u32[]{:S(2)}) collective-permute-start(bf16[768,768]{1,0:T(8,128)(2,1)} %collective-permute-done.12.refs_13_), channel_id=1, source_target_pairs={{8,0},{10,2},{12,4},{14,6},{16,24},{18,26},{20,28},{22,30},{9,1},{... | collective-permute-start | bytes 3538952 | tf_op jit(solution)/shard_map/ppermute | solution.py:331
  112.1 30.2 %collective-permute-start.21 = (bf16[768,768]{1,0:T(8,128)(2,1)}, bf16[768,768]{1,0:T(8,128)(2,1)S(1)}, u32[]{:S(2)}, u32[]{:S(2)}) collective-permute-start(bf16[768,768]{1,0:T(8,128)(2,1)} %copy-done.9), channel_id=1, source_target_pairs={{8,16},{10,18},{12,20},{14,22},{16,8},{18,10},{20,12},{22,14},{9,1... | collective-permute-start | bytes 3538952 | tf_op jit(solution)/shard_map/ppermute | solution.py:328
  147.1 11.6 %collective-permute-start.23 = (bf16[256,768]{1,0:T(8,128)(2,1)}, bf16[256,768]{1,0:T(8,128)(2,1)S(1)}, u32[]{:S(2)}, u32[]{:S(2)}) collective-permute-start(bf16[256,768]{1,0:T(8,128)(2,1)} %product.4), channel_id=1, source_target_pairs={{0,6},{2,4},{4,2},{6,0},{8,14},{10,12},{12,10},{14,8},{16,22},{18,... | collective-permute-start | bytes 1179656 | tf_op jit(solution)/shard_map/ppermute | solution.py:150
  158.7 9.7 %collective-permute-start.24 = (bf16[256,768]{1,0:T(8,128)(2,1)}, bf16[256,768]{1,0:T(8,128)(2,1)S(1)}, u32[]{:S(2)}, u32[]{:S(2)}) collective-permute-start(bf16[256,768]{1,0:T(8,128)(2,1)} %get-tuple-element.247), channel_id=1, source_target_pairs={{0,2},{2,0},{4,6},{6,4},{8,10},{10,8},{12,14},{14,12},{16,18},{18,... | collective-permute-start | bytes 1179656 | tf_op jit(solution)/shard_map/ppermute | solution.py:150
  160.2 9.4 %collective-permute-start.25 = (bf16[256,768]{1,0:T(8,128)(2,1)}, bf16[256,768]{1,0:T(8,128)(2,1)S(1)}, u32[]{:S(2)}, u32[]{:S(2)}) collective-permute-start(bf16[256,768]{1,0:T(8,128)(2,1)} %get-tuple-element.248), channel_id=1, source_target_pairs={{0,4},{2,6},{4,0},{6,2},{8,12},{10,14},{12,8},{14,10},{16,20},{18,... | collective-permute-start | bytes 1179656 | tf_op jit(solution)/shard_map/ppermute | solution.py:150
  (17 other events, 192.0 us)

commit v15 on v14

--- a/solution.py
+++ b/solution.py
@@ -185,19 +185,17 @@
     return lax.fori_loop(0, once, run, tuple(empty))
 
 
-def product(flags, places, ours, theirs, blocks, accs, widths, out_dtype):
-    _, rows, depth = ours[0].shape
+def product(flags, places, ours, theirs, blocks, acc, out_dtype):
+    _, _, rows, depth = ours.shape
     chunk = depth // PLANE
-    cols = sum(widths)
-    count, parts = len(blocks), len(ours)
-    outs = parts * len(widths)
+    cols = blocks[0][2][0][0][0].shape[1]
+    count = len(blocks)
     weights = [array for _, _, pieces in blocks for choices, _ in pieces for array in choices]
-    accs = accs or []
-
-    def kernel(flag_ref, place_ref, *refs):
-        our_refs, their_refs, refs = refs[:parts], refs[parts : 2 * parts], refs[2 * parts :]
+    accs = [] if acc is None else [acc]
+
+    def kernel(flag_ref, place_ref, our_ref, their_ref, *refs):
         weight_refs, refs = list(refs[: len(weights)]), refs[len(weights) :]
-        acc_refs, out_refs = refs[: len(accs)], refs[len(accs) : len(accs) + outs]
+        acc_refs, out_ref = refs[: len(accs)], refs[len(accs)]
         gated_buf, weight_buf, acc_buf, gated_sems, weight_sems, acc_sem = refs[-6:]
 
         def target(b, at):
@@ -218,13 +216,11 @@
                             pl.when(flag_ref[pick] == c)(copy.start)
                 row += choices[0].shape[0]
             half = flag_ref[flag] & 1
-            for r in range(parts):
-                for c, refs_of in enumerate((our_refs, their_refs)):
-                    target_rows = gated_buf.at[b, pl.ds(r * rows, rows), :]
-                    copy = pltpu.make_async_copy(refs_of[r].at[half], target_rows, gated_sems.at[b])
-                    pl.when(flag_ref[flag] // 2 == c)(copy.start)
-        for r, acc_ref in enumerate(acc_refs):
-            pltpu.make_async_copy(acc_ref, acc_buf.at[r], acc_sem).start()
+            for c, ref in enumerate((our_ref, their_ref)):
+                copy = pltpu.make_async_copy(ref.at[:, half], gated_buf.at[b], gated_sems.at[b])
+                pl.when(flag_ref[flag] // 2 == c)(copy.start)
+        for acc_ref in acc_refs:
+            pltpu.make_async_copy(acc_ref, acc_buf, acc_sem).start()
         for b in range(count):
             block = weight_buf.at[pl.ds(b * depth, depth), :]
             pltpu.make_async_copy(block, block, weight_sems.at[b]).wait()
@@ -234,75 +230,56 @@
             for col in range(0, cols, 2 * LANES):
                 here = pl.ds(col, 2 * LANES)
                 made = jnp.dot(
-                    gated_buf[b], weight_buf[pl.ds(b * depth, depth), here], preferred_element_type=jnp.float32
-                )
-                part = 0 if col < widths[0] else 1
-                inside = pl.ds(col - part * widths[0], 2 * LANES)
-                for r in range(parts):
-                    total = made[r * rows : (r + 1) * rows]
-                    out_ref = out_refs[part * parts + r]
-                    if b:
-                        total = total + out_ref[:, inside]
-                    elif accs:
-                        total = total + acc_buf[r, :, here]
-                    out_ref[:, inside] = total.astype(out_dtype)
+                    gated_buf[b].reshape(PLANE * rows, depth),
+                    weight_buf[pl.ds(b * depth, depth), here],
+                    preferred_element_type=jnp.float32,
+                ).reshape(PLANE, rows, 2 * LANES)
+                if b or accs:
+                    made = made + acc_buf[:, :, here]
+                if b < count - 1:
+                    acc_buf[:, :, here] = made
+                else:
+                    out_ref[:, :, here] = made.astype(out_dtype)
 
     smem = pl.BlockSpec(memory_space=pltpu.SMEM)
     anywhere = pl.BlockSpec(memory_space=pl.ANY)
-    made = pl.pallas_call(
+    return pl.pallas_call(
         kernel,
-        in_specs=[smem, smem] + [anywhere] * (2 * parts + len(weights) + len(accs)),
-        out_specs=[pl.BlockSpec(memory_space=pltpu.VMEM)] * outs,
-        out_shape=[jax.ShapeDtypeStruct((rows, width), out_dtype) for width in widths for _ in range(parts)],
+        in_specs=[smem, smem] + [anywhere] * (2 + len(weights) + len(accs)),
+        out_specs=pl.BlockSpec(memory_space=pltpu.VMEM),
+        out_shape=jax.ShapeDtypeStruct((PLANE, rows, cols), out_dtype),
         scratch_shapes=[
-            pltpu.VMEM((count, parts * rows, depth), jnp.bfloat16),
+            pltpu.VMEM((count, PLANE, rows, depth), jnp.bfloat16),
             pltpu.VMEM((count * depth, cols), jnp.bfloat16),
-            pltpu.VMEM((len(accs), *accs[0].shape) if accs else (8, LANES), jnp.float32),
+            pltpu.VMEM((PLANE, rows, cols), jnp.float32),
             pltpu.SemaphoreType.DMA((count,)),
             pltpu.SemaphoreType.DMA((count,)),
             pltpu.SemaphoreType.DMA,
         ],
         compiler_params=pltpu.CompilerParams(vmem_limit_bytes=VMEM_BYTES),
         cost_estimate=pl.CostEstimate(
-            flops=2 * parts * rows * depth * count * cols,
-            bytes_accessed=2 * count * depth * (parts * rows + cols),
+            flops=2 * PLANE * rows * depth * count * cols,
+            bytes_accessed=2 * count * depth * (PLANE * rows + cols),
             transcendentals=0,
         ),
         name="product",
-    )(flags, places, *ours, *theirs, *weights, *accs)
-    return [list(made[at : at + parts]) for at in range(0, outs, parts)]
-
-
-def assemble(places, parts):
-    rows = parts[0][0].shape[0]
-    widths = [part[0].shape[1] for part in parts]
-    cols = sum(widths)
-    flat = [piece for part in parts for piece in part]
-
-    def kernel(place_ref, *refs):
-        *piece_refs, out_ref, sems = refs
-        copies = []
-        first = 0
-        for part, width in enumerate(widths):
-            for r in range(PLANE):
-                at = part * PLANE + r
-                start = pl.multiple_of(place_ref[r] * cols + first, LANES)
-                target = out_ref.at[:, pl.ds(start, width)]
-                copies.append(pltpu.make_async_copy(piece_refs[at], target, sems.at[at]))
-                copies[-1].start()
-            first += width
-        for copy in copies:
-            copy.wait()
+    )(flags, places, ours, theirs, *weights, *accs)
+
+
+def side_by_side(pieces):
+    count, rows, cols = pieces.shape
+
+    def kernel(pieces_ref, out_ref):
+        out_ref[...] = pieces_ref[...]
 
     return pl.pallas_call(
         kernel,
-        in_specs=[pl.BlockSpec(memory_space=pltpu.SMEM)] + [pl.BlockSpec(memory_space=pltpu.VMEM)] * len(flat),
-        out_specs=pl.BlockSpec(memory_space=pl.ANY),
-        out_shape=jax.ShapeDtypeStruct((rows, cols * PLANE), flat[0].dtype),
-        scratch_shapes=[pltpu.SemaphoreType.DMA((len(flat),))],
-        compiler_params=pltpu.CompilerParams(vmem_limit_bytes=16 << 20),
-        name="assemble",
-    )(places, *flat)
+        grid=(count,),
+        in_specs=[pl.BlockSpec((None, rows, cols), lambda i: (i, 0, 0))],
+        out_specs=pl.BlockSpec((rows, cols), lambda i: (0, i)),
+        out_shape=jax.ShapeDtypeStruct((rows, cols * count), pieces.dtype),
+        name="side_by_side",
+    )(pieces)
 
 
 def split_block(q, k, v, residue, rate, skip, w_out):
@@ -360,40 +337,34 @@
     f0, n0, w0, w1, w2, w3, both, before = tie(f0, n0, w0, w1, w2, w3, both, before)
 
     arrived = [exchange(w, "ctx", r + 1) for r, w in enumerate((w1, w2, w3))]
-    earlier = [shift_ctx(both, PLANE * n) for n in range(1, 4)]
-    f0, w0, *earlier = tie(f0, w0, *earlier)
+    decay = jnp.exp(-speed * float(PLANE * rows))
+    last = shift_ctx(both, PLANE)
+    earlier = shift_ctx(both + decay * last, 2 * PLANE)
+    f0, w0, earlier = tie(f0, w0, earlier)
     out0, mid0 = outward(f0), across(w0)
-    gated = gated_conv(q, k, v, rate, residue, skip, before, (earlier, spot))
+    gated = gated_conv(q, k, v, rate, residue, skip, before, ([last, earlier], spot))
     rest = jnp.concatenate(arrived)
     gated, rest, out0, mid0 = tie(gated, rest, out0, mid0)
 
     fr, nr = far(rest), near(rest)
-    ours = [gated] + [exchange(gated, "ctx", r) for r in range(1, PLANE)]
-    ours = list(tie(*ours))
-    theirs = [exchange(x, "ch", 1) for x in ours[1:]]
-    fr, nr, rest, flags, places, *held = tie(fr, nr, rest, flags, places, *ours, *theirs)
-    ours, theirs = held[:PLANE], held[PLANE:]
+    planes = [list(range(first, first + PLANE)) for first in range(0, count, PLANE)]
+    ours = lax.all_gather(gated, "ctx", axis_index_groups=planes)
+    fr, nr, rest, flags, places, ours = tie(fr, nr, rest, flags, places, ours)
 
     out1, mid1 = outward(fr), across(rest)
-    theirs = [exchange(ours[0], "ch", 1)] + theirs
+    theirs = exchange(ours, "ch", 1)
     blocks = [
         (0, None, [((w0,), 0), ((rest,), 0)]),
         (1, None, [((n0,), 0), ((nr,), 0)]),
         (2, None, [((f0,), 0), ((fr,), 0)]),
     ]
-    (accs,) = product(flags, places, ours, theirs, blocks, None, [cols], jnp.float32)
-    out1, mid1, *accs = tie(out1, mid1, *accs)
+    accs = product(flags, places, ours, theirs, blocks, None, jnp.float32)
+    out1, mid1, accs = tie(out1, mid1, accs)
 
     blocks = [(3, 4, [((out0, mid0), 0), ((out1, mid1), 0)])]
-
-    def finish(*spots):
-        chosen = [ours[r] for r in spots], [theirs[r] for r in spots]
-        return product(flags, places, *chosen, blocks, [accs[r] for r in spots], [cols], jnp.bfloat16)[0]
-
-    (made3,) = finish(3)
-    back3 = exchange(made3, "ctx", 3)
-    back3, made0, made1, made2 = tie(back3, *finish(0, 1, 2))
-    return assemble(places, [[made0, exchange(made1, "ctx", 1), exchange(made2, "ctx", 2), back3]])
+    made = product(flags, places, ours, theirs, blocks, accs, jnp.bfloat16)
+    back = lax.all_to_all(made, "ctx", 0, 0, axis_index_groups=planes)
+    return side_by_side(back)
 
 
 def body(q, k, v, residue, rate, skip, w_out):

time: 173 us -> 195 us (1.13)
  blocking collectives: 0 us -> 24 us
  between operations: 0.28 us -> 13.5 us
  starting transfers between devices: 44.3 us -> 32.4 us
  waiting for transfers between devices: 82.6 us -> 78.7 us
  other arithmetic: 2.41 us -> 4.49 us
    all_to_all x0 -> x1, blocking collectives: none -> 24 us  [split_block(): back = lax.all_to_all(made, 'ctx', 0, 0, axis_index_groups=planes)]
    ppermute x19 -> x10, starting transfers between devices: 20.7 us -> 14.8 us  [exchange(): return lax.ppermute(x, axis, [(i, i ^ flip) for i in range(count)])]
    ppermute x2, starting transfers between devices: 9.58 us -> 4.26 us  [across(): return lax.ppermute(x, 'ctx', [(i, i ^ 3 * PLANE) for i in middle])]
    ppermute x19 -> x10, waiting for transfers between devices: 61.4 us -> 59.6 us  [exchange(): return lax.ppermute(x, axis, [(i, i ^ flip) for i in range(count)])]
    pallas_call x4 -> x3, Pallas kernels: 23.4 us -> 22.4 us  [the longest x2 18.9 us: product(): pl.pallas_call(kernel, in_specs=[smem, smem] + [anywhere] * (2 + len(weig...]
    ppermute x3 -> x2, starting transfers between devices: 7.69 us -> 7.64 us  [shift_ctx(): return lax.ppermute(x, 'ctx', [(i, i + by) for i in range(count - by)])]
    ppermute x3 -> x2, waiting for transfers between devices: 5.25 us -> 5.2 us  [shift_ctx(): return lax.ppermute(x, 'ctx', [(i, i + by) for i in range(count - by)])]
  transfers between devices with their start and end apart: 26 -> 17, of which waited for: 15 -> 11; matrix products, arithmetic and copies ran while one was open for 2% -> 3% of each run, Pallas kernels for 18% -> 13%
where the time goes in v15:
time: 195 us; the launch traced here: 194 us
  waiting for transfers between devices  78.7 us (40%)
  Pallas kernels  34.9 us (18%)
  starting transfers between devices  32.4 us (17%)
  blocking collectives  24 us (12%)
  between operations  13.5 us (7%)
  local copies, waits for them, and re-layouts  6.02 us (3%)
  other arithmetic  4.49 us (2%)
    ppermute x10, waiting for transfers between devices, exchange(): return lax.ppermute(x, axis, [(i, i ^ flip) for i in range(count)])  59.6 us
    all_to_all x1, blocking collectives, split_block(): back = lax.all_to_all(made, 'ctx', 0, 0, axis_index_groups=planes)  24 us
    pallas_call x2, Pallas kernels, product(): pl.pallas_call(kernel, in_specs=[smem, smem] + [anywhere] * (2 + len(weig...  18.9 us
    ppermute x10, starting transfers between devices, exchange(): return lax.ppermute(x, axis, [(i, i ^ flip) for i in range(count)])  14.8 us
    ppermute x2, waiting for transfers between devices, outward(): return lax.ppermute(x, 'ctx', [(i, i ^ PLANE) for i in middle])  9.99 us
    pallas_call x1, Pallas kernels, gated_conv(): pl.pallas_call(conv_kernel, grid=(chan // width,), in_specs=[wide, wide,...  8.52 us
    ppermute x2, starting transfers between devices, shift_ctx(): return lax.ppermute(x, 'ctx', [(i, i + by) for i in range(count - by)])  7.64 us
    ppermute x2, starting transfers between devices, outward(): return lax.ppermute(x, 'ctx', [(i, i ^ PLANE) for i in middle])  5.64 us
  transfers between devices with their start and end apart: 17, of which 11 were waited for; matrix products, arithmetic and copies ran while one was open for 3% of the time, Pallas kernels for 13%

profile of v15, /device:TPU:8, one launch (start us, length us, event | category | flops | bytes accessed | tf_op | source)
XLA Modules:
  0.0 194.1 jit_solution(5363984267129407047)
XLA Ops:
  6.5 2.6 %constant_dynamic-slice_fusion = (bf16[256,768]{1,0:T(8,128)(2,1)}, bf16[256,768]{1,0:T(8,128)(2,1)}, bf16[256,768]{1,0:T(8,128)(2,1)S(1)}, bf16[256,768]{1,0:T(8,128)(2,1)}) fusion(bf16[256,3072]{1,0:T(8,128)(2,1)} %param.15, s32[]{:T(128)S(6)} %select_n.84, s32[]{:T(128)S(6)} %select_n.82, s32[]{:T(128)S(6)} %select_n.81, s32[]{:T(128)S(6)} %select_n.83), kind=kLoop, calls=%fused_computation.5 | loop fusion | bytes 3145744 | tf_op jit(solution)/shard_map/dynamic_slice | solution.py:311
  9.1 2.6 %collective-permute-start.2 = (bf16[256,768]{1,0:T(8,128)(2,1)S(1)}, bf16[256,768]{1,0:T(8,128)(2,1)S(1)}, u32[]{:S(2)}, u32[]{:S(2)}) collective-permute-start(bf16[256,768]{1,0:T(8,128)(2,1)S(1)} %get-tuple-element.183.refs_0_), channel_id=1, source_target_pairs={{0,16},{2,18},{4,20},{6,22},{8,24},{10,26},{12,28},{14,30},{16,0},... | collective-permute-start | bytes 1179656 | tf_op jit(solution)/shard_map/ppermute | solution.py:150
  12.2 15.9 %while.14 = (s32[]{:T(128)}, f32[16,16,128]{2,1,0:T(8,128)}, f32[16,16,128]{2,1,0:T(8,128)}, s32[]{:T(128)}, pred[]{:T(512)}, /*index=5*/bf16[256,2048]{1,0:T(8,...) while((s32[]{:T(128)}, f32[16,16,128]{2,1,0:T(8,128)}, ...), condition=%wide.region_1.2_spmd, body=%wide.region_0.1_spmd.sunk | while | flops 17399808 | bytes 4456652 | solution.py:185
  12.2 4.0 %end_states.3 = f32[16,16,128]{2,1,0:T(8,128)} custom-call(bf16[256,2048]{1,0:T(8,128)(2,1)S(1)} %get-tuple-element.296.k_ref, bf16[256,2048]{1,0:T(8,128)(2,1)S(1)} %get-tuple-element.297.v_ref, f32[16,2048]{1,0:T(8,128)S(1)} %get-tuple-element.298.rate_ref), custom_call_target="tpu_custom_call" | custom-call | flops 16777216 | bytes 2097152 | tf_op jit(solution)/shard_map/while/body/end_states/pallas_call | solution.py:98
  17.7 3.7 %collective-permute-done = f32[16,16,128]{2,1,0:T(8,128)S(1)} collective-permute-done((f32[16,16,128]{2,1,0:T(8,128)}, f32[16,16,128]{2,1,0:T(8,128)S(1)}, u32[]{:S(2)}, u32[]{:S(2)}) %collective-permute-start) | collective-permute-done | bytes 131104 | tf_op jit(solution)/shard_map/while/body/ppermute | solution.py:150
  23.9 3.4 %collective-permute-done.1 = f32[16,16,128]{2,1,0:T(8,128)S(1)} collective-permute-done((f32[16,16,128]{2,1,0:T(8,128)S(1)}, f32[16,16,128]{2,1,0:T(8,128)S(1)}, u32[]{:S(2)}, u32[]{:S(2)}) %collective-permute-start.1) | collective-permute-done | bytes 131104 | tf_op jit(solution)/shard_map/while/body/ppermute | solution.py:150
  29.5 2.4 %collective-permute-start.4 = (f32[16,16,128]{2,1,0:T(8,128)}, f32[16,16,128]{2,1,0:T(8,128)S(1)}, u32[]{:S(2)}, u32[]{:S(2)}) collective-permute-start(f32[16,16,128]{2,1,0:T(8,128)} %get-tuple-element.175), channel_id=1, source_target_pairs={{0,8},{2,10},{4,12},{6,14},{8,16},{10,18},{12,20},{14,22},{16,24},... | collective-permute-start | bytes 393224 | tf_op jit(solution)/shard_map/ppermute | solution.py:145
  37.6 5.3 %collective-permute-start.5 = (f32[16,16,128]{2,1,0:T(8,128)S(1)}, f32[16,16,128]{2,1,0:T(8,128)S(1)}, u32[]{:S(2)}, u32[]{:S(2)}) collective-permute-start(f32[16,16,128]{2,1,0:T(8,128)S(1)} %multiply_add_fusion), channel_id=1, source_target_pairs={{0,16},{2,18},{4,20},{6,22},{8,24},{10,26},{12,28},{14,30},{1,17},... | collective-permute-start | bytes 393224 | tf_op jit(solution)/shard_map/ppermute | solution.py:145
  42.9 4.0 %collective-permute-done.5.refs_1_ = f32[16,16,128]{2,1,0:T(8,128)S(1)} collective-permute-done((f32[16,16,128]{2,1,0:T(8,128)S(1)}, f32[16,16,128]{2,1,0:T(8,128)S(1)}, u32[]{:S(2)}, u32[]{:S(2)}) %collective-permute-start.5) | collective-permute-done | bytes 131104 | tf_op jit(solution)/shard_map/ppermute | solution.py:145
  47.0 2.3 %collective-permute-start.10 = (bf16[256,768]{1,0:T(8,128)(2,1)}, bf16[256,768]{1,0:T(8,128)(2,1)}, u32[]{:S(2)}, u32[]{:S(2)}) collective-permute-start(bf16[256,768]{1,0:T(8,128)(2,1)} %copy-done.8), channel_id=1, source_target_pairs={{8,16},{10,18},{12,20},{14,22},{16,8},{18,10},{20,12},{22,14},{9,1... | collective-permute-start | bytes 1179656 | tf_op jit(solution)/shard_map/ppermute | solution.py:305
  49.3 2.1 %collective-permute-start.9 = (bf16[256,768]{1,0:T(8,128)(2,1)}, bf16[256,768]{1,0:T(8,128)(2,1)}, u32[]{:S(2)}, u32[]{:S(2)}) collective-permute-start(bf16[256,768]{1,0:T(8,128)(2,1)} %copy-done.11), channel_id=1, source_target_pairs={{8,0},{10,2},{12,4},{14,6},{16,24},{18,26},{20,28},{22,30},{9,1},{... | collective-permute-start | bytes 1179656 | tf_op jit(solution)/shard_map/ppermute | solution.py:308
  51.4 8.5 %gated_conv.1 = bf16[2,256,1024]{2,1,0:T(8,128)(2,1)} custom-call(bf16[256,2048]{1,0:T(8,128)(2,1)} %q_ref.1, bf16[256,2048]{1,0:T(8,128)(2,1)S(1)} %get-tuple-element.339, bf16[256,2048]{1,0:T(8,128)(2,1)S(1)} %get-tuple-element.340, f32[16,2048]{1,0:T(8,128)S(1)} %get-tuple-element.345, f32[16,2048]{1,0:T(8,128)} %residue_ref.1, f32[16,128]{1,0:T(8,128)} %bitcast.20, ...), custom_call_target="tpu_custom_call" | custom-call | flops 33554432 | bytes 4194304 | tf_op jit(solution)/shard_map/gated_conv/pallas_call | solution.py:128
  61.9 2.6 %collective-permute-start.11 = (bf16[768,768]{1,0:T(8,128)(2,1)S(1)}, bf16[768,768]{1,0:T(8,128)(2,1)}, u32[]{:S(2)}, u32[]{:S(2)}) collective-permute-start(bf16[768,768]{1,0:T(8,128)(2,1)S(1)} %pad_maximum_fusion.refs_1_), channel_id=1, source_target_pairs={{0,16},{2,18},{4,20},{6,22},{8,24},{10,26},{12,28},{14,30},{16,0},... | collective-permute-start | bytes 3538952 | tf_op jit(solution)/shard_map/ppermute | solution.py:150
  64.5 2.6 %collective-permute-start.12 = (bf16[768,768]{1,0:T(8,128)(2,1)S(1)}, bf16[768,768]{1,0:T(8,128)(2,1)S(1)}, u32[]{:S(2)}, u32[]{:S(2)}) collective-permute-start(bf16[768,768]{1,0:T(8,128)(2,1)S(1)} %pad_maximum_fusion.refs_1_), channel_id=1, source_target_pairs={{0,8},{2,10},{4,12},{6,14},{8,0},{10,2},{12,4},{14,6},{16,24},{18,... | collective-permute-start | bytes 3538952 | tf_op jit(solution)/shard_map/ppermute | solution.py:150
  68.3 45.5 %collective-permute-done.11.refs_5_ = bf16[768,768]{1,0:T(8,128)(2,1)} collective-permute-done((bf16[768,768]{1,0:T(8,128)(2,1)S(1)}, bf16[768,768]{1,0:T(8,128)(2,1)}, u32[]{:S(2)}, u32[]{:S(2)}) %collective-permute-start.11) | collective-permute-done | bytes 1179680 | tf_op jit(solution)/shard_map/ppermute | solution.py:150
  113.8 3.6 %collective-permute-done.12.refs_3_ = bf16[768,768]{1,0:T(8,128)(2,1)S(1)} collective-permute-done((bf16[768,768]{1,0:T(8,128)(2,1)S(1)}, bf16[768,768]{1,0:T(8,128)(2,1)S(1)}, u32[]{:S(2)}, u32[]{:S(2)}) %collective-permute-start.12) | collective-permute-done | bytes 1179680 | tf_op jit(solution)/shard_map/ppermute | solution.py:150
  118.4 3.6 %collective-permute-start.14 = (bf16[768,768]{1,0:T(8,128)(2,1)}, bf16[768,768]{1,0:T(8,128)(2,1)S(1)}, u32[]{:S(2)}, u32[]{:S(2)}) collective-permute-start(bf16[768,768]{1,0:T(8,128)(2,1)} %collective-permute-done.11.refs_5_), channel_id=1, source_target_pairs={{8,0},{10,2},{12,4},{14,6},{16,24},{18,26},{20,28},{22,30},{9,1},{... | collective-permute-start | bytes 3538952 | tf_op jit(solution)/shard_map/ppermute | solution.py:308
  123.9 2.0 %collective-permute-done.13.their_ref = bf16[4,2,256,1024]{3,2,1,0:T(8,128)(2,1)} collective-permute-done((bf16[4,2,256,1024]{3,2,1,0:T(8,128)(2,1)}, bf16[4,2,256,1024]{3,2,1,0:T(8,128)(2,1)}, u32[]{:S(2)}, u32[]{:S(2)}) %collective-permute-start.13) | collective-permute-done | bytes 4194336 | tf_op jit(solution)/shard_map/ppermute | solution.py:150
  125.9 12.2 %product.2.refs_4_ = f32[4,256,768]{2,1,0:T(8,128)} custom-call(s32[5]{0:T(128)} %stack.36.flag_ref, s32[4]{0:T(128)} %pad_add_fusion.place_ref, bf16[4,2,256,1024]{3,2,1,0:T(8,128)(2,1)} %bitcast.18, bf16[4,2,256,1024]{3,2,1,0:T(8,128)(2,1)} %collective-permute-done.13.their_ref, bf16[256,768]{1,0:T(8,128)(2,1)} %copy-done.8, bf16[768,768]{1,0:T(8,128)(2,1)} %copy-done.5, ...), custom_call_target="tpu_custom_call" | custom-call | flops 4831838208 | bytes 11010048 | tf_op jit(solution)/shard_map/product/pallas_call | solution.py:246
  138.1 10.0 %collective-permute-done.14.refs_2_ = bf16[768,768]{1,0:T(8,128)(2,1)S(1)} collective-permute-done((bf16[768,768]{1,0:T(8,128)(2,1)}, bf16[768,768]{1,0:T(8,128)(2,1)S(1)}, u32[]{:S(2)}, u32[]{:S(2)}) %collective-permute-start.14) | collective-permute-done | bytes 1179680 | tf_op jit(solution)/shard_map/ppermute | solution.py:308
  148.1 3.9 %collective-permute-done.15.refs_3_ = bf16[768,768]{1,0:T(8,128)(2,1)S(1)} collective-permute-done((bf16[768,768]{1,0:T(8,128)(2,1)S(1)}, bf16[768,768]{1,0:T(8,128)(2,1)S(1)}, u32[]{:S(2)}, u32[]{:S(2)}) %collective-permute-start.15) | collective-permute-done | bytes 1179680 | tf_op jit(solution)/shard_map/ppermute | solution.py:305
  153.0 6.7 %product.3 = bf16[4,256,768]{2,1,0:T(8,128)(2,1)} custom-call(s32[5]{0:T(128)} %stack.36.flag_ref, s32[4]{0:T(128)} %pad_add_fusion.place_ref, bf16[4,2,256,1024]{3,2,1,0:T(8,128)(2,1)} %bitcast.19, bf16[4,2,256,1024]{3,2,1,0:T(8,128)(2,1)} %collective-permute-done.13.their_ref, bf16[256,768]{1,0:T(8,128)(2,1)} %collective-permute-done.9.refs_0_, ...), custom_call_target="tpu_custom_call" | custom-call | flops 1610612736 | bytes 3670016 | tf_op jit(solution)/shard_map/product/pallas_call | solution.py:246
  159.6 24.0 %all_to_all.5.pieces_ref = bf16[4,256,768]{2,1,0:T(8,128)(2,1)} all-to-all(bf16[4,256,768]{2,1,0:T(8,128)(2,1)} %product.3), channel_id=1, replica_groups={{0,2,4,6},{8,10,12,14},{16,18,20,22},{24,26,28,30},{1,3,5,7},{9,11,13,1..., dimensions={0} | all-to-all | bytes 3145728 | tf_op jit(solution)/shard_map/all_to_all | solution.py:366
  183.7 3.6 %side_by_side.1 = bf16[256,3072]{1,0:T(8,128)(2,1)} custom-call(bf16[4,256,768]{2,1,0:T(8,128)(2,1)} %all_to_all.5.pieces_ref), custom_call_target="tpu_custom_call" | custom-call | tf_op jit(solution)/shard_map/side_by_side/pallas_call | solution.py:275
  (51 shorter events, 19.6 us)
Async XLA Ops:
  6.5 110.8 %all-gather.3.cloned.1.call-start = ((), (), s32[]{:S(2)}) async-start(), calls=%async_computation.1 | async-start | bytes 5242880 | tf_op jit(solution)/shard_map/all_gather | solution.py:351
  6.5 5.6 %copy-start.2 = (f32[16,2048]{1,0:T(8,128)S(1)}, f32[16,2048]{1,0:T(8,128)}, u32[]{:S(2)}) copy-start(f32[16,2048]{1,0:T(8,128)} %rate_ref.1) | copy-start | bytes 393220
  6.5 5.6 %copy-start = (bf16[256,2048]{1,0:T(8,128)(2,1)S(1)}, bf16[256,2048]{1,0:T(8,128)(2,1)}, u32[]{:S(2)}) copy-start(bf16[256,2048]{1,0:T(8,128)(2,1)} %k_ref.1) | copy-start | bytes 3145732
  6.5 5.7 %copy-start.1 = (bf16[256,2048]{1,0:T(8,128)(2,1)S(1)}, bf16[256,2048]{1,0:T(8,128)(2,1)}, u32[]{:S(2)}) copy-start(bf16[256,2048]{1,0:T(8,128)(2,1)} %v_ref.1) | copy-start | bytes 3145732
  9.1 19.3 %collective-permute-start.2 = (bf16[256,768]{1,0:T(8,128)(2,1)S(1)}, bf16[256,768]{1,0:T(8,128)(2,1)S(1)}, u32[]{:S(2)}, u32[]{:S(2)}) collective-permute-start(bf16[256,768]{1,0:T(8,128)(2,1)S(1)} %get-tuple-element.183.refs_0_), channel_id=1, source_target_pairs={{0,16},{2,18},{4,20},{6,22},{8,24},{10,26},{12,28},{14,30},{16,0},... | collective-permute-start | bytes 1179656 | tf_op jit(solution)/shard_map/ppermute | solution.py:150
  11.7 17.9 %collective-permute-start.3 = (bf16[256,768]{1,0:T(8,128)(2,1)S(1)}, bf16[256,768]{1,0:T(8,128)(2,1)}, u32[]{:S(2)}, u32[]{:S(2)}) collective-permute-start(bf16[256,768]{1,0:T(8,128)(2,1)S(1)} %get-tuple-element.183.refs_0_), channel_id=1, source_target_pairs={{0,8},{2,10},{4,12},{6,14},{8,0},{10,2},{12,4},{14,6},{16,24},{18,... | collective-permute-start | bytes 1179656 | tf_op jit(solution)/shard_map/ppermute | solution.py:150
  16.2 5.2 %collective-permute-start = (f32[16,16,128]{2,1,0:T(8,128)}, f32[16,16,128]{2,1,0:T(8,128)S(1)}, u32[]{:S(2)}, u32[]{:S(2)}) collective-permute-start(f32[16,16,128]{2,1,0:T(8,128)} %end_states.3), channel_id=1, source_target_pairs={{0,2},{2,0},{4,6},{6,4},{8,10},{10,8},{12,14},{14,12},{16,18},{18,... | collective-permute-start | bytes 393224 | tf_op jit(solution)/shard_map/while/body/ppermute | solution.py:150
  22.3 5.0 %collective-permute-start.1 = (f32[16,16,128]{2,1,0:T(8,128)S(1)}, f32[16,16,128]{2,1,0:T(8,128)S(1)}, u32[]{:S(2)}, u32[]{:S(2)}) collective-permute-start(f32[16,16,128]{2,1,0:T(8,128)S(1)} %add_select_fusion.3), channel_id=1, source_target_pairs={{0,4},{2,6},{4,0},{6,2},{8,12},{10,14},{12,8},{14,10},{16,20},{18,... | collective-permute-start | bytes 393224 | tf_op jit(solution)/shard_map/while/body/ppermute | solution.py:150
  29.5 7.1 %collective-permute-start.4 = (f32[16,16,128]{2,1,0:T(8,128)}, f32[16,16,128]{2,1,0:T(8,128)S(1)}, u32[]{:S(2)}, u32[]{:S(2)}) collective-permute-start(f32[16,16,128]{2,1,0:T(8,128)} %get-tuple-element.175), channel_id=1, source_target_pairs={{0,8},{2,10},{4,12},{6,14},{8,16},{10,18},{12,20},{14,22},{16,24},... | collective-permute-start | bytes 393224 | tf_op jit(solution)/shard_map/ppermute | solution.py:145
  31.9 28.0 %collective-permute-start.6 = (bf16[256,768]{1,0:T(8,128)(2,1)}, bf16[256,768]{1,0:T(8,128)(2,1)S(1)}, u32[]{:S(2)}, u32[]{:S(2)}) collective-permute-start(bf16[256,768]{1,0:T(8,128)(2,1)} %get-tuple-element.179), channel_id=1, source_target_pairs={{0,2},{2,0},{4,6},{6,4},{8,10},{10,8},{12,14},{14,12},{16,18},{18,... | collective-permute-start | bytes 1179656 | tf_op jit(solution)/shard_map/ppermute | solution.py:150
  33.5 26.4 %collective-permute-start.7 = (bf16[256,768]{1,0:T(8,128)(2,1)}, bf16[256,768]{1,0:T(8,128)(2,1)S(1)}, u32[]{:S(2)}, u32[]{:S(2)}) collective-permute-start(bf16[256,768]{1,0:T(8,128)(2,1)} %get-tuple-element.180), channel_id=1, source_target_pairs={{0,4},{2,6},{4,0},{6,2},{8,12},{10,14},{12,8},{14,10},{16,20},{18,... | collective-permute-start | bytes 1179656 | tf_op jit(solution)/shard_map/ppermute | solution.py:150
  35.0 25.7 %collective-permute-start.8 = (bf16[256,768]{1,0:T(8,128)(2,1)}, bf16[256,768]{1,0:T(8,128)(2,1)}, u32[]{:S(2)}, u32[]{:S(2)}) collective-permute-start(bf16[256,768]{1,0:T(8,128)(2,1)} %get-tuple-element.181), channel_id=1, source_target_pairs={{0,6},{2,4},{4,2},{6,0},{8,14},{10,12},{12,10},{14,8},{16,22},{18,... | collective-permute-start | bytes 1179656 | tf_op jit(solution)/shard_map/ppermute | solution.py:150
  36.7 14.7 %copy-start.6 = (f32[16,16,128]{2,1,0:T(8,128)}, f32[16,16,128]{2,1,0:T(8,128)S(1)}, u32[]{:S(2)}) copy-start(f32[16,16,128]{2,1,0:T(8,128)S(1)} %collective-permute-done.4.refs_0_) | copy-start | bytes 393220
  37.6 9.3 %collective-permute-start.5 = (f32[16,16,128]{2,1,0:T(8,128)S(1)}, f32[16,16,128]{2,1,0:T(8,128)S(1)}, u32[]{:S(2)}, u32[]{:S(2)}) collective-permute-start(f32[16,16,128]{2,1,0:T(8,128)S(1)} %multiply_add_fusion), channel_id=1, source_target_pairs={{0,16},{2,18},{4,20},{6,22},{8,24},{10,26},{12,28},{14,30},{1,17},... | collective-permute-start | bytes 393224 | tf_op jit(solution)/shard_map/ppermute | solution.py:145
  47.0 4.4 %copy-start.9 = (f32[16,16,128]{2,1,0:T(8,128)}, f32[16,16,128]{2,1,0:T(8,128)S(1)}, u32[]{:S(2)}) copy-start(f32[16,16,128]{2,1,0:T(8,128)S(1)} %collective-permute-done.5.refs_1_) | copy-start | bytes 393220
  47.0 14.9 %collective-permute-start.10 = (bf16[256,768]{1,0:T(8,128)(2,1)}, bf16[256,768]{1,0:T(8,128)(2,1)}, u32[]{:S(2)}, u32[]{:S(2)}) collective-permute-start(bf16[256,768]{1,0:T(8,128)(2,1)} %copy-done.8), channel_id=1, source_target_pairs={{8,16},{10,18},{12,20},{14,22},{16,8},{18,10},{20,12},{22,14},{9,1... | collective-permute-start | bytes 1179656 | tf_op jit(solution)/shard_map/ppermute | solution.py:305
  49.3 12.6 %collective-permute-start.9 = (bf16[256,768]{1,0:T(8,128)(2,1)}, bf16[256,768]{1,0:T(8,128)(2,1)}, u32[]{:S(2)}, u32[]{:S(2)}) collective-permute-start(bf16[256,768]{1,0:T(8,128)(2,1)} %copy-done.11), channel_id=1, source_target_pairs={{8,0},{10,2},{12,4},{14,6},{16,24},{18,26},{20,28},{22,30},{9,1},{... | collective-permute-start | bytes 1179656 | tf_op jit(solution)/shard_map/ppermute | solution.py:308
  61.8 64.0 %copy-start.5 = (bf16[768,768]{1,0:T(8,128)(2,1)}, bf16[768,768]{1,0:T(8,128)(2,1)S(1)}, u32[]{:S(2)}) copy-start(bf16[768,768]{1,0:T(8,128)(2,1)S(1)} %pad_maximum_fusion.refs_1_) | copy-start | bytes 3538948
  61.9 51.9 %collective-permute-start.11 = (bf16[768,768]{1,0:T(8,128)(2,1)S(1)}, bf16[768,768]{1,0:T(8,128)(2,1)}, u32[]{:S(2)}, u32[]{:S(2)}) collective-permute-start(bf16[768,768]{1,0:T(8,128)(2,1)S(1)} %pad_maximum_fusion.refs_1_), channel_id=1, source_target_pairs={{0,16},{2,18},{4,20},{6,22},{8,24},{10,26},{12,28},{14,30},{16,0},... | collective-permute-start | bytes 3538952 | tf_op jit(solution)/shard_map/ppermute | solution.py:150
  64.5 52.9 %collective-permute-start.12 = (bf16[768,768]{1,0:T(8,128)(2,1)S(1)}, bf16[768,768]{1,0:T(8,128)(2,1)S(1)}, u32[]{:S(2)}, u32[]{:S(2)}) collective-permute-start(bf16[768,768]{1,0:T(8,128)(2,1)S(1)} %pad_maximum_fusion.refs_1_), channel_id=1, source_target_pairs={{0,8},{2,10},{4,12},{6,14},{8,0},{10,2},{12,4},{14,6},{16,24},{18,... | collective-permute-start | bytes 3538952 | tf_op jit(solution)/shard_map/ppermute | solution.py:150
  118.4 7.5 %collective-permute-start.13 = (bf16[4,2,256,1024]{3,2,1,0:T(8,128)(2,1)}, bf16[4,2,256,1024]{3,2,1,0:T(8,128)(2,1)}, u32[]{:S(2)}, u32[]{:S(2)}) collective-permute-start(bf16[4,2,256,1024]{3,2,1,0:T(8,128)(2,1)} %bitcast.17), channel_id=1, source_target_pairs={{0,1},{1,0},{2,3},{3,2},{4,5},{5,4},{6,7},{7,6},{8,9},{9,8},{10,11... | collective-permute-start | bytes 12582920 | tf_op jit(solution)/shard_map/ppermute | solution.py:150
  118.4 29.7 %collective-permute-start.14 = (bf16[768,768]{1,0:T(8,128)(2,1)}, bf16[768,768]{1,0:T(8,128)(2,1)S(1)}, u32[]{:S(2)}, u32[]{:S(2)}) collective-permute-start(bf16[768,768]{1,0:T(8,128)(2,1)} %collective-permute-done.11.refs_5_), channel_id=1, source_target_pairs={{8,0},{10,2},{12,4},{14,6},{16,24},{18,26},{20,28},{22,30},{9,1},{... | collective-permute-start | bytes 3538952 | tf_op jit(solution)/shard_map/ppermute | solution.py:308
  121.9 30.0 %collective-permute-start.15 = (bf16[768,768]{1,0:T(8,128)(2,1)S(1)}, bf16[768,768]{1,0:T(8,128)(2,1)S(1)}, u32[]{:S(2)}, u32[]{:S(2)}) collective-permute-start(bf16[768,768]{1,0:T(8,128)(2,1)S(1)} %pad_maximum_fusion.refs_1_), channel_id=1, source_target_pairs={{8,16},{10,18},{12,20},{14,22},{16,8},{18,10},{20,12},{22,14},{9,1... | collective-permute-start | bytes 3538952 | tf_op jit(solution)/shard_map/ppermute | solution.py:305
  148.1 3.9 %copy-start.3 = (bf16[768,768]{1,0:T(8,128)(2,1)}, bf16[768,768]{1,0:T(8,128)(2,1)S(1)}, u32[]{:S(2)}) copy-start(bf16[768,768]{1,0:T(8,128)(2,1)S(1)} %collective-permute-done.14.refs_2_) | copy-start | bytes 3538948
  (5 other events, 7.1 us)
Sparse Core Ops, SparseCore 0:
  62.0 54.8 all-gather.2

commit v16 on v14

--- a/solution.py
+++ b/solution.py
@@ -360,22 +360,22 @@
     f0, n0, w0, w1, w2, w3, both, before = tie(f0, n0, w0, w1, w2, w3, both, before)
 
     arrived = [exchange(w, "ctx", r + 1) for r, w in enumerate((w1, w2, w3))]
-    earlier = [shift_ctx(both, PLANE * n) for n in range(1, 4)]
-    f0, w0, *earlier = tie(f0, w0, *earlier)
+    decay = jnp.exp(-speed * float(PLANE * rows))
+    last = shift_ctx(both, PLANE)
+    earlier = shift_ctx(both + decay * last, 2 * PLANE)
+    f0, w0, earlier = tie(f0, w0, earlier)
     out0, mid0 = outward(f0), across(w0)
-    gated = gated_conv(q, k, v, rate, residue, skip, before, (earlier, spot))
+    gated = gated_conv(q, k, v, rate, residue, skip, before, ([last, earlier], spot))
     rest = jnp.concatenate(arrived)
     gated, rest, out0, mid0 = tie(gated, rest, out0, mid0)
 
-    fr, nr = far(rest), near(rest)
+    nr, fr = near(rest), far(rest)
     ours = [gated] + [exchange(gated, "ctx", r) for r in range(1, PLANE)]
-    ours = list(tie(*ours))
-    theirs = [exchange(x, "ch", 1) for x in ours[1:]]
-    fr, nr, rest, flags, places, *held = tie(fr, nr, rest, flags, places, *ours, *theirs)
-    ours, theirs = held[:PLANE], held[PLANE:]
+    theirs_x = exchange(ours[1], "ch", 1)
+    fr, nr, rest, flags, places, theirs_x, *ours = tie(fr, nr, rest, flags, places, theirs_x, *ours)
 
     out1, mid1 = outward(fr), across(rest)
-    theirs = [exchange(ours[0], "ch", 1)] + theirs
+    theirs = [theirs_x if r == 1 else exchange(x, "ch", 1) for r, x in enumerate(ours)]
     blocks = [
         (0, None, [((w0,), 0), ((rest,), 0)]),
         (1, None, [((n0,), 0), ((nr,), 0)]),

time: 173 us -> 171 us (0.988)
  starting transfers between devices: 44.3 us -> 40.2 us
  local copies, waits for them, and re-layouts: 6.78 us -> 8.98 us
    ppermute x19, starting transfers between devices: 20.7 us -> 18.8 us  [exchange(): return lax.ppermute(x, axis, [(i, i ^ flip) for i in range(count)])]
    unnamed x31 -> x35, local copies, waits for them, and re-layouts: 3.62 us -> 5.59 us
    ppermute x2, waiting for transfers between devices: 11.8 us -> 9.88 us  [outward(): return lax.ppermute(x, 'ctx', [(i, i ^ PLANE) for i in middle])]
    ppermute x3 -> x2, starting transfers between devices: 7.69 us -> 6.85 us  [shift_ctx(): return lax.ppermute(x, 'ctx', [(i, i + by) for i in range(count - by)])]
    ppermute x3 -> x2, waiting for transfers between devices: 5.25 us -> 4.88 us  [shift_ctx(): return lax.ppermute(x, 'ctx', [(i, i + by) for i in range(count - by)])]
  transfers between devices with their start and end apart: 26 -> 25, of which waited for: 15 -> 14; matrix products, arithmetic and copies ran while one was open for 2% -> 2% of each run, Pallas kernels for 18% -> 18%
where the time goes in v16:
time: 171 us; the launch traced here: 170 us
  waiting for transfers between devices  81.4 us (48%)
  starting transfers between devices  40.2 us (24%)
  Pallas kernels  35.8 us (21%)
  local copies, waits for them, and re-layouts  8.98 us (5%)
  other arithmetic  3.39 us (2%)
    ppermute x19, waiting for transfers between devices, exchange(): return lax.ppermute(x, axis, [(i, i ^ flip) for i in range(count)])  62.6 us
    pallas_call x3, Pallas kernels, product(): pl.pallas_call(kernel, in_specs=[smem, smem] + [anywhere] * (2 * parts +...  21.6 us
    ppermute x19, starting transfers between devices, exchange(): return lax.ppermute(x, axis, [(i, i ^ flip) for i in range(count)])  18.8 us
    ppermute x2, waiting for transfers between devices, outward(): return lax.ppermute(x, 'ctx', [(i, i ^ PLANE) for i in middle])  9.88 us
    pallas_call x1, Pallas kernels, gated_conv(): pl.pallas_call(conv_kernel, grid=(chan // width,), in_specs=[wide, wide,...  8.5 us
    ppermute x2, starting transfers between devices, across(): return lax.ppermute(x, 'ctx', [(i, i ^ 3 * PLANE) for i in middle])  8.48 us
    ppermute x2, starting transfers between devices, shift_ctx(): return lax.ppermute(x, 'ctx', [(i, i + by) for i in range(count - by)])  6.85 us
    ppermute x2, starting transfers between devices, outward(): return lax.ppermute(x, 'ctx', [(i, i ^ PLANE) for i in middle])  6.14 us
  transfers between devices with their start and end apart: 25, of which 14 were waited for; matrix products, arithmetic and copies ran while one was open for 2% of the time, Pallas kernels for 18%

profile of v16, /device:TPU:8, one launch (start us, length us, event | category | flops | bytes accessed | tf_op | source)
XLA Modules:
  0.0 170.2 jit_solution(2005750012356045027)
XLA Ops:
  0.0 2.6 %constant_dynamic-slice_fusion = (bf16[256,768]{1,0:T(8,128)(2,1)}, bf16[256,768]{1,0:T(8,128)(2,1)}, bf16[256,768]{1,0:T(8,128)(2,1)S(1)}, bf16[256,768]{1,0:T(8,128)(2,1)}) fusion(bf16[256,3072]{1,0:T(8,128)(2,1)} %param.15, s32[]{:T(128)S(6)} %select_n.84, s32[]{:T(128)S(6)} %select_n.82, s32[]{:T(128)S(6)} %select_n.81, s32[]{:T(128)S(6)} %select_n.83), kind=kLoop, calls=%fused_computation.5 | loop fusion | bytes 3145744 | tf_op jit(solution)/shard_map/dynamic_slice | solution.py:334
  2.6 3.0 %collective-permute-start.2 = (bf16[256,768]{1,0:T(8,128)(2,1)S(1)}, bf16[256,768]{1,0:T(8,128)(2,1)}, u32[]{:S(2)}, u32[]{:S(2)}) collective-permute-start(bf16[256,768]{1,0:T(8,128)(2,1)S(1)} %get-tuple-element.201.refs_8_), channel_id=1, source_target_pairs={{0,16},{2,18},{4,20},{6,22},{8,24},{10,26},{12,28},{14,30},{16,0},... | collective-permute-start | bytes 1179656 | tf_op jit(solution)/shard_map/ppermute | solution.py:150
  5.7 15.9 %while.14 = (s32[]{:T(128)}, f32[16,16,128]{2,1,0:T(8,128)}, f32[16,16,128]{2,1,0:T(8,128)}, s32[]{:T(128)}, pred[]{:T(512)}, /*index=5*/bf16[256,2048]{1,0:T(8,...) while((s32[]{:T(128)}, f32[16,16,128]{2,1,0:T(8,128)}, ...), condition=%wide.region_1.2_spmd, body=%wide.region_0.1_spmd.sunk | while | flops 17399808 | bytes 4456652 | solution.py:185
  5.7 4.0 %end_states.3 = f32[16,16,128]{2,1,0:T(8,128)} custom-call(bf16[256,2048]{1,0:T(8,128)(2,1)S(1)} %get-tuple-element.332.k_ref, bf16[256,2048]{1,0:T(8,128)(2,1)S(1)} %get-tuple-element.333.v_ref, f32[16,2048]{1,0:T(8,128)S(1)} %get-tuple-element.334.rate_ref), custom_call_target="tpu_custom_call" | custom-call | flops 16777216 | bytes 2097152 | tf_op jit(solution)/shard_map/while/body/end_states/pallas_call | solution.py:98
  11.2 3.7 %collective-permute-done = f32[16,16,128]{2,1,0:T(8,128)S(1)} collective-permute-done((f32[16,16,128]{2,1,0:T(8,128)}, f32[16,16,128]{2,1,0:T(8,128)S(1)}, u32[]{:S(2)}, u32[]{:S(2)}) %collective-permute-start) | collective-permute-done | bytes 131104 | tf_op jit(solution)/shard_map/while/body/ppermute | solution.py:150
  17.4 3.4 %collective-permute-done.1 = f32[16,16,128]{2,1,0:T(8,128)S(1)} collective-permute-done((f32[16,16,128]{2,1,0:T(8,128)S(1)}, f32[16,16,128]{2,1,0:T(8,128)S(1)}, u32[]{:S(2)}, u32[]{:S(2)}) %collective-permute-start.1) | collective-permute-done | bytes 131104 | tf_op jit(solution)/shard_map/while/body/ppermute | solution.py:150
  23.1 2.3 %collective-permute-start.4 = (f32[16,16,128]{2,1,0:T(8,128)}, f32[16,16,128]{2,1,0:T(8,128)S(1)}, u32[]{:S(2)}, u32[]{:S(2)}) collective-permute-start(f32[16,16,128]{2,1,0:T(8,128)} %get-tuple-element.193), channel_id=1, source_target_pairs={{0,8},{2,10},{4,12},{6,14},{8,16},{10,18},{12,20},{14,22},{16,24},... | collective-permute-start | bytes 393224 | tf_op jit(solution)/shard_map/ppermute | solution.py:145
  31.1 4.5 %collective-permute-start.5 = (f32[16,16,128]{2,1,0:T(8,128)S(1)}, f32[16,16,128]{2,1,0:T(8,128)S(1)}, u32[]{:S(2)}, u32[]{:S(2)}) collective-permute-start(f32[16,16,128]{2,1,0:T(8,128)S(1)} %multiply_add_fusion), channel_id=1, source_target_pairs={{0,16},{2,18},{4,20},{6,22},{8,24},{10,26},{12,28},{14,30},{1,17},... | collective-permute-start | bytes 393224 | tf_op jit(solution)/shard_map/ppermute | solution.py:145
  35.6 3.7 %collective-permute-done.5.refs_1_ = f32[16,16,128]{2,1,0:T(8,128)S(1)} collective-permute-done((f32[16,16,128]{2,1,0:T(8,128)S(1)}, f32[16,16,128]{2,1,0:T(8,128)S(1)}, u32[]{:S(2)}, u32[]{:S(2)}) %collective-permute-start.5) | collective-permute-done | bytes 131104 | tf_op jit(solution)/shard_map/ppermute | solution.py:145
  40.7 6.6 %collective-permute-start.10 = (bf16[256,768]{1,0:T(8,128)(2,1)}, bf16[256,768]{1,0:T(8,128)(2,1)}, u32[]{:S(2)}, u32[]{:S(2)}) collective-permute-start(bf16[256,768]{1,0:T(8,128)(2,1)} %copy-done.14), channel_id=1, source_target_pairs={{8,16},{10,18},{12,20},{14,22},{16,8},{18,10},{20,12},{22,14},{9,1... | collective-permute-start | bytes 1179656 | tf_op jit(solution)/shard_map/ppermute | solution.py:328
  47.3 8.5 %gated_conv.1.refs_0_ = bf16[2,256,1024]{2,1,0:T(8,128)(2,1)} custom-call(bf16[256,2048]{1,0:T(8,128)(2,1)} %q_ref.1, bf16[256,2048]{1,0:T(8,128)(2,1)S(1)} %get-tuple-element.377, bf16[256,2048]{1,0:T(8,128)(2,1)S(1)} %get-tuple-element.378, f32[16,2048]{1,0:T(8,128)S(1)} %get-tuple-element.383, f32[16,2048]{1,0:T(8,128)} %residue_ref.1, ...), custom_call_target="tpu_custom_call" | custom-call | flops 33554432 | bytes 4194304 | tf_op jit(solution)/shard_map/gated_conv/pallas_call | solution.py:128
  62.4 21.1 %collective-permute-done.13.refs_1_ = bf16[2,256,1024]{2,1,0:T(8,128)(2,1)S(1)} collective-permute-done((bf16[2,256,1024]{2,1,0:T(8,128)(2,1)S(1)}, bf16[2,256,1024]{2,1,0:T(8,128)(2,1)S(1)}, u32[]{:S(2)}, u32[]{:S(2)}) %collective-permute-start.13) | collective-permute-done | bytes 1048608 | tf_op jit(solution)/shard_map/ppermute | solution.py:150
  85.1 14.9 %collective-permute-done.16.refs_3_.refs_0_ = bf16[2,256,1024]{2,1,0:T(8,128)(2,1)} collective-permute-done((bf16[2,256,1024]{2,1,0:T(8,128)(2,1)S(1)}, bf16[2,256,1024]{2,1,0:T(8,128)(2,1)}, u32[]{:S(2)}, u32[]{:S(2)}) %collective-permute-start.16) | collective-permute-done | bytes 1048608 | tf_op jit(solution)/shard_map/ppermute | solution.py:150
  100.0 2.6 %collective-permute-done.15.refs_2_ = bf16[2,256,1024]{2,1,0:T(8,128)(2,1)} collective-permute-done((bf16[2,256,1024]{2,1,0:T(8,128)(2,1)S(1)}, bf16[2,256,1024]{2,1,0:T(8,128)(2,1)}, u32[]{:S(2)}, u32[]{:S(2)}) %collective-permute-start.15) | collective-permute-done | bytes 1048608 | tf_op jit(solution)/shard_map/ppermute | solution.py:150
  102.5 3.0 %collective-permute-done.11.refs_13_ = bf16[768,768]{1,0:T(8,128)(2,1)} collective-permute-done((bf16[768,768]{1,0:T(8,128)(2,1)S(1)}, bf16[768,768]{1,0:T(8,128)(2,1)}, u32[]{:S(2)}, u32[]{:S(2)}) %collective-permute-start.11) | collective-permute-done | bytes 1179680 | tf_op jit(solution)/shard_map/ppermute | solution.py:150
  106.1 4.8 %collective-permute-start.18 = (bf16[768,768]{1,0:T(8,128)(2,1)}, bf16[768,768]{1,0:T(8,128)(2,1)S(1)}, u32[]{:S(2)}, u32[]{:S(2)}) collective-permute-start(bf16[768,768]{1,0:T(8,128)(2,1)} %collective-permute-done.11.refs_13_), channel_id=1, source_target_pairs={{8,0},{10,2},{12,4},{14,6},{16,24},{18,26},{20,28},{22,30},{9,1},{... | collective-permute-start | bytes 3538952 | tf_op jit(solution)/shard_map/ppermute | solution.py:331
  110.9 1.9 %collective-permute-start.19 = (bf16[768,768]{1,0:T(8,128)(2,1)}, bf16[768,768]{1,0:T(8,128)(2,1)S(1)}, u32[]{:S(2)}, u32[]{:S(2)}) collective-permute-start(bf16[768,768]{1,0:T(8,128)(2,1)} %copy-done.9), channel_id=1, source_target_pairs={{8,16},{10,18},{12,20},{14,22},{16,8},{18,10},{20,12},{22,14},{9,1... | collective-permute-start | bytes 3538952 | tf_op jit(solution)/shard_map/ppermute | solution.py:328
  114.9 12.3 %product.3 = (f32[256,768]{1,0:T(8,128)}, f32[256,768]{1,0:T(8,128)}, f32[256,768]{1,0:T(8,128)}, f32[256,768]{1,0:T(8,128)}) custom-call(s32[5]{0:T(128)} %stack.36.flag_ref, s32[4]{0:T(128)} %pad_add_fusion.place_ref, bf16[2,256,1024]{2,1,0:T(8,128)(2,1)} %gated_conv.1.refs_0_, bf16[2,256,1024]{2,1,0:T(8,128)(2,1)} %copy-done.10, ...), custom_call_target="tpu_custom_call" | custom-call | flops 4831838208 | bytes 11010048 | tf_op jit(solution)/shard_map/product/pallas_call | solution.py:252
  127.2 9.9 %collective-permute-done.18.refs_4_.refs_8_ = bf16[768,768]{1,0:T(8,128)(2,1)S(1)} collective-permute-done((bf16[768,768]{1,0:T(8,128)(2,1)}, bf16[768,768]{1,0:T(8,128)(2,1)S(1)}, u32[]{:S(2)}, u32[]{:S(2)}) %collective-permute-start.18) | collective-permute-done | bytes 1179680 | tf_op jit(solution)/shard_map/ppermute | solution.py:331
  137.0 4.1 %collective-permute-done.19.refs_5_.refs_9_ = bf16[768,768]{1,0:T(8,128)(2,1)S(1)} collective-permute-done((bf16[768,768]{1,0:T(8,128)(2,1)}, bf16[768,768]{1,0:T(8,128)(2,1)S(1)}, u32[]{:S(2)}, u32[]{:S(2)}) %collective-permute-start.19) | collective-permute-done | bytes 1179680 | tf_op jit(solution)/shard_map/ppermute | solution.py:328
  142.2 3.8 %product.4 = bf16[256,768]{1,0:T(8,128)(2,1)} custom-call(s32[5]{0:T(128)} %stack.36.flag_ref, s32[4]{0:T(128)} %pad_add_fusion.place_ref, bf16[2,256,1024]{2,1,0:T(8,128)(2,1)} %collective-permute-done.16.refs_3_.refs_0_, bf16[2,256,1024]{2,1,0:T(8,128)(2,1)} %copy-done.12, bf16[256,768]{1,0:T(8,128)(2,1)} %copy-done.8, ...), custom_call_target="tpu_custom_call" | custom-call | flops 402653184 | bytes 2097152 | tf_op jit(solution)/shard_map/product/pallas_call | solution.py:252
  147.5 5.5 %product.5 = (bf16[256,768]{1,0:T(8,128)(2,1)}, bf16[256,768]{1,0:T(8,128)(2,1)}, bf16[256,768]{1,0:T(8,128)(2,1)}) custom-call(s32[5]{0:T(128)} %stack.36.flag_ref, s32[4]{0:T(128)} %pad_add_fusion.place_ref, bf16[2,256,1024]{2,1,0:T(8,128)(2,1)} %gated_conv.1.refs_0_, bf16[2,256,1024]{2,1,0:T(8,128)(2,1)} %copy-done.10, ...), custom_call_target="tpu_custom_call" | custom-call | flops 1207959552 | bytes 3145728 | tf_op jit(solution)/shard_map/product/pallas_call | solution.py:252
  153.1 4.5 %collective-permute-done.22.refs_3_ = bf16[256,768]{1,0:T(8,128)(2,1)S(1)} collective-permute-done((bf16[256,768]{1,0:T(8,128)(2,1)}, bf16[256,768]{1,0:T(8,128)(2,1)S(1)}, u32[]{:S(2)}, u32[]{:S(2)}) %collective-permute-start.22) | collective-permute-done | bytes 393248 | tf_op jit(solution)/shard_map/ppermute | solution.py:150
  159.6 7.7 %collective-permute-done.23.refs_1_ = bf16[256,768]{1,0:T(8,128)(2,1)S(1)} collective-permute-done((bf16[256,768]{1,0:T(8,128)(2,1)}, bf16[256,768]{1,0:T(8,128)(2,1)S(1)}, u32[]{:S(2)}, u32[]{:S(2)}) %collective-permute-start.23) | collective-permute-done | bytes 393248 | tf_op jit(solution)/shard_map/ppermute | solution.py:150
  (76 shorter events, 31.4 us)
Async XLA Ops:
  2.6 19.0 %collective-permute-start.3 = (bf16[256,768]{1,0:T(8,128)(2,1)S(1)}, bf16[256,768]{1,0:T(8,128)(2,1)S(1)}, u32[]{:S(2)}, u32[]{:S(2)}) collective-permute-start(bf16[256,768]{1,0:T(8,128)(2,1)S(1)} %get-tuple-element.201.refs_8_), channel_id=1, source_target_pairs={{0,8},{2,10},{4,12},{6,14},{8,0},{10,2},{12,4},{14,6},{16,24},{18,... | collective-permute-start | bytes 1179656 | tf_op jit(solution)/shard_map/ppermute | solution.py:150
  2.6 20.5 %collective-permute-start.2 = (bf16[256,768]{1,0:T(8,128)(2,1)S(1)}, bf16[256,768]{1,0:T(8,128)(2,1)}, u32[]{:S(2)}, u32[]{:S(2)}) collective-permute-start(bf16[256,768]{1,0:T(8,128)(2,1)S(1)} %get-tuple-element.201.refs_8_), channel_id=1, source_target_pairs={{0,16},{2,18},{4,20},{6,22},{8,24},{10,26},{12,28},{14,30},{16,0},... | collective-permute-start | bytes 1179656 | tf_op jit(solution)/shard_map/ppermute | solution.py:150
  9.7 5.2 %collective-permute-start = (f32[16,16,128]{2,1,0:T(8,128)}, f32[16,16,128]{2,1,0:T(8,128)S(1)}, u32[]{:S(2)}, u32[]{:S(2)}) collective-permute-start(f32[16,16,128]{2,1,0:T(8,128)} %end_states.3), channel_id=1, source_target_pairs={{0,2},{2,0},{4,6},{6,4},{8,10},{10,8},{12,14},{14,12},{16,18},{18,... | collective-permute-start | bytes 393224 | tf_op jit(solution)/shard_map/while/body/ppermute | solution.py:150
  23.1 7.1 %collective-permute-start.4 = (f32[16,16,128]{2,1,0:T(8,128)}, f32[16,16,128]{2,1,0:T(8,128)S(1)}, u32[]{:S(2)}, u32[]{:S(2)}) collective-permute-start(f32[16,16,128]{2,1,0:T(8,128)} %get-tuple-element.193), channel_id=1, source_target_pairs={{0,8},{2,10},{4,12},{6,14},{8,16},{10,18},{12,20},{14,22},{16,24},... | collective-permute-start | bytes 393224 | tf_op jit(solution)/shard_map/ppermute | solution.py:145
  25.4 30.3 %collective-permute-start.6 = (bf16[256,768]{1,0:T(8,128)(2,1)}, bf16[256,768]{1,0:T(8,128)(2,1)S(1)}, u32[]{:S(2)}, u32[]{:S(2)}) collective-permute-start(bf16[256,768]{1,0:T(8,128)(2,1)} %get-tuple-element.197), channel_id=1, source_target_pairs={{0,2},{2,0},{4,6},{6,4},{8,10},{10,8},{12,14},{14,12},{16,18},{18,... | collective-permute-start | bytes 1179656 | tf_op jit(solution)/shard_map/ppermute | solution.py:150
  27.0 28.8 %collective-permute-start.7 = (bf16[256,768]{1,0:T(8,128)(2,1)}, bf16[256,768]{1,0:T(8,128)(2,1)S(1)}, u32[]{:S(2)}, u32[]{:S(2)}) collective-permute-start(bf16[256,768]{1,0:T(8,128)(2,1)} %get-tuple-element.198), channel_id=1, source_target_pairs={{0,4},{2,6},{4,0},{6,2},{8,12},{10,14},{12,8},{14,10},{16,20},{18,... | collective-permute-start | bytes 1179656 | tf_op jit(solution)/shard_map/ppermute | solution.py:150
  28.5 27.3 %collective-permute-start.8 = (bf16[256,768]{1,0:T(8,128)(2,1)}, bf16[256,768]{1,0:T(8,128)(2,1)S(1)}, u32[]{:S(2)}, u32[]{:S(2)}) collective-permute-start(bf16[256,768]{1,0:T(8,128)(2,1)} %get-tuple-element.199), channel_id=1, source_target_pairs={{0,6},{2,4},{4,2},{6,0},{8,14},{10,12},{12,10},{14,8},{16,22},{18,... | collective-permute-start | bytes 1179656 | tf_op jit(solution)/shard_map/ppermute | solution.py:150
  31.1 8.2 %collective-permute-start.5 = (f32[16,16,128]{2,1,0:T(8,128)S(1)}, f32[16,16,128]{2,1,0:T(8,128)S(1)}, u32[]{:S(2)}, u32[]{:S(2)}) collective-permute-start(f32[16,16,128]{2,1,0:T(8,128)S(1)} %multiply_add_fusion), channel_id=1, source_target_pairs={{0,16},{2,18},{4,20},{6,22},{8,24},{10,26},{12,28},{14,30},{1,17},... | collective-permute-start | bytes 393224 | tf_op jit(solution)/shard_map/ppermute | solution.py:145
  39.4 16.5 %collective-permute-start.9 = (bf16[256,768]{1,0:T(8,128)(2,1)}, bf16[256,768]{1,0:T(8,128)(2,1)S(1)}, u32[]{:S(2)}, u32[]{:S(2)}) collective-permute-start(bf16[256,768]{1,0:T(8,128)(2,1)} %collective-permute-done.2.refs_12_), channel_id=1, source_target_pairs={{8,0},{10,2},{12,4},{14,6},{16,24},{18,26},{20,28},{22,30},{9,1},{... | collective-permute-start | bytes 1179656 | tf_op jit(solution)/shard_map/ppermute | solution.py:331
  40.7 15.2 %collective-permute-start.10 = (bf16[256,768]{1,0:T(8,128)(2,1)}, bf16[256,768]{1,0:T(8,128)(2,1)}, u32[]{:S(2)}, u32[]{:S(2)}) collective-permute-start(bf16[256,768]{1,0:T(8,128)(2,1)} %copy-done.14), channel_id=1, source_target_pairs={{8,16},{10,18},{12,20},{14,22},{16,8},{18,10},{20,12},{22,14},{9,1... | collective-permute-start | bytes 1179656 | tf_op jit(solution)/shard_map/ppermute | solution.py:328
  57.5 26.1 %collective-permute-start.13 = (bf16[2,256,1024]{2,1,0:T(8,128)(2,1)S(1)}, bf16[2,256,1024]{2,1,0:T(8,128)(2,1)S(1)}, u32[]{:S(2)}, u32[]{:S(2)}) collective-permute-start(bf16[2,256,1024]{2,1,0:T(8,128)(2,1)S(1)} %copy-done.7), channel_id=1, source_target_pairs={{0,2},{2,0},{4,6},{6,4},{8,10},{10,8},{12,14},{14,12},{16,18},{18,... | collective-permute-start | bytes 3145736 | tf_op jit(solution)/shard_map/ppermute | solution.py:150
  58.9 43.6 %collective-permute-start.12 = (bf16[768,768]{1,0:T(8,128)(2,1)S(1)}, bf16[768,768]{1,0:T(8,128)(2,1)}, u32[]{:S(2)}, u32[]{:S(2)}) collective-permute-start(bf16[768,768]{1,0:T(8,128)(2,1)S(1)} %pad_maximum_fusion.refs_9_), channel_id=1, source_target_pairs={{0,8},{2,10},{4,12},{6,14},{8,0},{10,2},{12,4},{14,6},{16,24},{18,... | collective-permute-start | bytes 3538952 | tf_op jit(solution)/shard_map/ppermute | solution.py:150
  59.0 46.6 %collective-permute-start.11 = (bf16[768,768]{1,0:T(8,128)(2,1)S(1)}, bf16[768,768]{1,0:T(8,128)(2,1)}, u32[]{:S(2)}, u32[]{:S(2)}) collective-permute-start(bf16[768,768]{1,0:T(8,128)(2,1)S(1)} %pad_maximum_fusion.refs_9_), channel_id=1, source_target_pairs={{0,16},{2,18},{4,20},{6,22},{8,24},{10,26},{12,28},{14,30},{16,0},... | collective-permute-start | bytes 3538952 | tf_op jit(solution)/shard_map/ppermute | solution.py:150
  60.4 39.5 %collective-permute-start.16 = (bf16[2,256,1024]{2,1,0:T(8,128)(2,1)S(1)}, bf16[2,256,1024]{2,1,0:T(8,128)(2,1)}, u32[]{:S(2)}, u32[]{:S(2)}) collective-permute-start(bf16[2,256,1024]{2,1,0:T(8,128)(2,1)S(1)} %copy-done.7), channel_id=1, source_target_pairs={{0,6},{2,4},{4,2},{6,0},{8,14},{10,12},{12,10},{14,8},{16,22},{18,... | collective-permute-start | bytes 3145736 | tf_op jit(solution)/shard_map/ppermute | solution.py:150
  61.9 40.6 %collective-permute-start.15 = (bf16[2,256,1024]{2,1,0:T(8,128)(2,1)S(1)}, bf16[2,256,1024]{2,1,0:T(8,128)(2,1)}, u32[]{:S(2)}, u32[]{:S(2)}) collective-permute-start(bf16[2,256,1024]{2,1,0:T(8,128)(2,1)S(1)} %copy-done.7), channel_id=1, source_target_pairs={{0,4},{2,6},{4,0},{6,2},{8,12},{10,14},{12,8},{14,10},{16,20},{18,... | collective-permute-start | bytes 3145736 | tf_op jit(solution)/shard_map/ppermute | solution.py:150
  83.6 22.0 %collective-permute-start.14 = (bf16[2,256,1024]{2,1,0:T(8,128)(2,1)S(1)}, bf16[2,256,1024]{2,1,0:T(8,128)(2,1)}, u32[]{:S(2)}, u32[]{:S(2)}) collective-permute-start(bf16[2,256,1024]{2,1,0:T(8,128)(2,1)S(1)} %collective-permute-done.13.refs_1_), channel_id=1, source_target_pairs={{0,1},{1,0},{2,3},{3,2},{4,5},{5,4},{6,7},{7,6},{8,9},{9,8},{10,11... | collective-permute-start | bytes 3145736 | tf_op jit(solution)/shard_map/ppermute | solution.py:150
  105.6 7.3 %collective-permute-start.17 = (bf16[2,256,1024]{2,1,0:T(8,128)(2,1)}, bf16[2,256,1024]{2,1,0:T(8,128)(2,1)S(1)}, u32[]{:S(2)}, u32[]{:S(2)}) collective-permute-start(bf16[2,256,1024]{2,1,0:T(8,128)(2,1)} %collective-permute-done.16.refs_3_.refs_0_), channel_id=1, source_target_pairs={{0,1},{1,0},{2,3},{3,2},{4,5},{5,4},{6,7},{7,6},{8,9},{9,8},{10,11... | collective-permute-start | bytes 3145736 | tf_op jit(solution)/shard_map/ppermute | solution.py:150
  105.6 7.3 %collective-permute-start.20 = (bf16[2,256,1024]{2,1,0:T(8,128)(2,1)S(1)}, bf16[2,256,1024]{2,1,0:T(8,128)(2,1)S(1)}, u32[]{:S(2)}, u32[]{:S(2)}) collective-permute-start(bf16[2,256,1024]{2,1,0:T(8,128)(2,1)S(1)} %copy-done.7), channel_id=1, source_target_pairs={{0,1},{1,0},{2,3},{3,2},{4,5},{5,4},{6,7},{7,6},{8,9},{9,8},{10,11... | collective-permute-start | bytes 3145736 | tf_op jit(solution)/shard_map/ppermute | solution.py:150
  106.1 8.8 %collective-permute-start.21 = (bf16[2,256,1024]{2,1,0:T(8,128)(2,1)}, bf16[2,256,1024]{2,1,0:T(8,128)(2,1)}, u32[]{:S(2)}, u32[]{:S(2)}) collective-permute-start(bf16[2,256,1024]{2,1,0:T(8,128)(2,1)} %collective-permute-done.15.refs_2_), channel_id=1, source_target_pairs={{0,1},{1,0},{2,3},{3,2},{4,5},{5,4},{6,7},{7,6},{8,9},{9,8},{10,11... | collective-permute-start | bytes 3145736 | tf_op jit(solution)/shard_map/ppermute | solution.py:150
  106.1 31.0 %collective-permute-start.18 = (bf16[768,768]{1,0:T(8,128)(2,1)}, bf16[768,768]{1,0:T(8,128)(2,1)S(1)}, u32[]{:S(2)}, u32[]{:S(2)}) collective-permute-start(bf16[768,768]{1,0:T(8,128)(2,1)} %collective-permute-done.11.refs_13_), channel_id=1, source_target_pairs={{8,0},{10,2},{12,4},{14,6},{16,24},{18,26},{20,28},{22,30},{9,1},{... | collective-permute-start | bytes 3538952 | tf_op jit(solution)/shard_map/ppermute | solution.py:331
  110.9 30.2 %collective-permute-start.19 = (bf16[768,768]{1,0:T(8,128)(2,1)}, bf16[768,768]{1,0:T(8,128)(2,1)S(1)}, u32[]{:S(2)}, u32[]{:S(2)}) collective-permute-start(bf16[768,768]{1,0:T(8,128)(2,1)} %copy-done.9), channel_id=1, source_target_pairs={{8,16},{10,18},{12,20},{14,22},{16,8},{18,10},{20,12},{22,14},{9,1... | collective-permute-start | bytes 3538952 | tf_op jit(solution)/shard_map/ppermute | solution.py:328
  146.0 11.6 %collective-permute-start.22 = (bf16[256,768]{1,0:T(8,128)(2,1)}, bf16[256,768]{1,0:T(8,128)(2,1)S(1)}, u32[]{:S(2)}, u32[]{:S(2)}) collective-permute-start(bf16[256,768]{1,0:T(8,128)(2,1)} %product.4), channel_id=1, source_target_pairs={{0,6},{2,4},{4,2},{6,0},{8,14},{10,12},{12,10},{14,8},{16,22},{18,... | collective-permute-start | bytes 1179656 | tf_op jit(solution)/shard_map/ppermute | solution.py:150
  157.6 9.7 %collective-permute-start.23 = (bf16[256,768]{1,0:T(8,128)(2,1)}, bf16[256,768]{1,0:T(8,128)(2,1)S(1)}, u32[]{:S(2)}, u32[]{:S(2)}) collective-permute-start(bf16[256,768]{1,0:T(8,128)(2,1)} %get-tuple-element.231), channel_id=1, source_target_pairs={{0,2},{2,0},{4,6},{6,4},{8,10},{10,8},{12,14},{14,12},{16,18},{18,... | collective-permute-start | bytes 1179656 | tf_op jit(solution)/shard_map/ppermute | solution.py:150
  158.1 9.4 %collective-permute-start.24 = (bf16[256,768]{1,0:T(8,128)(2,1)}, bf16[256,768]{1,0:T(8,128)(2,1)S(1)}, u32[]{:S(2)}, u32[]{:S(2)}) collective-permute-start(bf16[256,768]{1,0:T(8,128)(2,1)} %get-tuple-element.232), channel_id=1, source_target_pairs={{0,4},{2,6},{4,0},{6,2},{8,12},{10,14},{12,8},{14,10},{16,20},{18,... | collective-permute-start | bytes 1179656 | tf_op jit(solution)/shard_map/ppermute | solution.py:150
  (18 other events, 187.2 us)

commit v17 on v16

--- a/solution.py
+++ b/solution.py
@@ -185,7 +185,7 @@
     return lax.fori_loop(0, once, run, tuple(empty))
 
 
-def product(flags, places, ours, theirs, blocks, accs, widths, out_dtype):
+def product(flags, places, ours, theirs, blocks, accs, widths, out_dtype, spread=False):
     _, rows, depth = ours[0].shape
     chunk = depth // PLANE
     cols = sum(widths)
@@ -197,8 +197,11 @@
     def kernel(flag_ref, place_ref, *refs):
         our_refs, their_refs, refs = refs[:parts], refs[parts : 2 * parts], refs[2 * parts :]
         weight_refs, refs = list(refs[: len(weights)]), refs[len(weights) :]
-        acc_refs, out_refs = refs[: len(accs)], refs[len(accs) : len(accs) + outs]
-        gated_buf, weight_buf, acc_buf, gated_sems, weight_sems, acc_sem = refs[-6:]
+        acc_refs, out_refs = refs[: len(accs)], list(refs[len(accs) : len(accs) + outs])
+        gated_buf, weight_buf, acc_buf, own_buf, gated_sems, weight_sems, acc_sem = refs[-7:]
+        spread_ref = out_refs[0]
+        if spread:
+            out_refs[0] = own_buf
 
         def target(b, at):
             start = pl.multiple_of(b * depth + place_ref[at // chunk] * chunk, chunk)
@@ -247,17 +250,29 @@
                         total = total + acc_buf[r, :, here]
                     out_ref[:, inside] = total.astype(out_dtype)
 
+        if spread:
+            home = spread_ref.at[:, pl.ds(pl.multiple_of(place_ref[0] * cols, cols), cols)]
+            copy = pltpu.make_async_copy(own_buf, home, acc_sem)
+            copy.start()
+            copy.wait()
+
     smem = pl.BlockSpec(memory_space=pltpu.SMEM)
     anywhere = pl.BlockSpec(memory_space=pl.ANY)
+    out_specs = [pl.BlockSpec(memory_space=pltpu.VMEM)] * outs
+    out_shape = [jax.ShapeDtypeStruct((rows, width), out_dtype) for width in widths for _ in range(parts)]
+    if spread:
+        out_specs[0] = anywhere
+        out_shape[0] = jax.ShapeDtypeStruct((rows, PLANE * cols), out_dtype)
     made = pl.pallas_call(
         kernel,
         in_specs=[smem, smem] + [anywhere] * (2 * parts + len(weights) + len(accs)),
-        out_specs=[pl.BlockSpec(memory_space=pltpu.VMEM)] * outs,
-        out_shape=[jax.ShapeDtypeStruct((rows, width), out_dtype) for width in widths for _ in range(parts)],
+        out_specs=out_specs,
+        out_shape=out_shape,
         scratch_shapes=[
             pltpu.VMEM((count, parts * rows, depth), jnp.bfloat16),
             pltpu.VMEM((count * depth, cols), jnp.bfloat16),
             pltpu.VMEM((len(accs), *accs[0].shape) if accs else (8, LANES), jnp.float32),
+            pltpu.VMEM((rows, cols) if spread else (16, LANES), out_dtype),
             pltpu.SemaphoreType.DMA((count,)),
             pltpu.SemaphoreType.DMA((count,)),
             pltpu.SemaphoreType.DMA,
@@ -273,36 +288,31 @@
     return [list(made[at : at + parts]) for at in range(0, outs, parts)]
 
 
-def assemble(places, parts):
-    rows = parts[0][0].shape[0]
-    widths = [part[0].shape[1] for part in parts]
-    cols = sum(widths)
-    flat = [piece for part in parts for piece in part]
-
-    def kernel(place_ref, *refs):
+def assemble(places, held, pieces):
+    rows, cols = pieces[0].shape
+
+    def kernel(place_ref, _, *refs):
         *piece_refs, out_ref, sems = refs
         copies = []
-        first = 0
-        for part, width in enumerate(widths):
-            for r in range(PLANE):
-                at = part * PLANE + r
-                start = pl.multiple_of(place_ref[r] * cols + first, LANES)
-                target = out_ref.at[:, pl.ds(start, width)]
-                copies.append(pltpu.make_async_copy(piece_refs[at], target, sems.at[at]))
-                copies[-1].start()
-            first += width
+        for n, piece_ref in enumerate(piece_refs):
+            target = out_ref.at[:, pl.ds(pl.multiple_of(place_ref[n + 1] * cols, cols), cols)]
+            copies.append(pltpu.make_async_copy(piece_ref, target, sems.at[n]))
+            copies[-1].start()
         for copy in copies:
             copy.wait()
 
+    anywhere = pl.BlockSpec(memory_space=pl.ANY)
     return pl.pallas_call(
         kernel,
-        in_specs=[pl.BlockSpec(memory_space=pltpu.SMEM)] + [pl.BlockSpec(memory_space=pltpu.VMEM)] * len(flat),
-        out_specs=pl.BlockSpec(memory_space=pl.ANY),
-        out_shape=jax.ShapeDtypeStruct((rows, cols * PLANE), flat[0].dtype),
-        scratch_shapes=[pltpu.SemaphoreType.DMA((len(flat),))],
+        in_specs=[pl.BlockSpec(memory_space=pltpu.SMEM), anywhere]
+        + [pl.BlockSpec(memory_space=pltpu.VMEM)] * len(pieces),
+        out_specs=anywhere,
+        out_shape=jax.ShapeDtypeStruct(held.shape, held.dtype),
+        scratch_shapes=[pltpu.SemaphoreType.DMA((len(pieces),))],
+        input_output_aliases={1: 0},
         compiler_params=pltpu.CompilerParams(vmem_limit_bytes=16 << 20),
         name="assemble",
-    )(places, *flat)
+    )(places, held, *pieces)
 
 
 def split_block(q, k, v, residue, rate, skip, w_out):
@@ -355,24 +365,24 @@
 
     x_later, y_later = (spot & 1) != 0, (spot & 2) != 0
     w0, w1, w2, w3 = tie(*[group(w_out, r) for r in range(PLANE)])
-    f0, n0 = far(w0), near(w0)
+    n0, f0 = near(w0), far(w0)
     both, before = box(plane_scan, k, v, rate, speed)
-    f0, n0, w0, w1, w2, w3, both, before = tie(f0, n0, w0, w1, w2, w3, both, before)
+    n0, f0, w0, w1, w2, w3, both, before = tie(n0, f0, w0, w1, w2, w3, both, before)
 
     arrived = [exchange(w, "ctx", r + 1) for r, w in enumerate((w1, w2, w3))]
     decay = jnp.exp(-speed * float(PLANE * rows))
     last = shift_ctx(both, PLANE)
     earlier = shift_ctx(both + decay * last, 2 * PLANE)
     f0, w0, earlier = tie(f0, w0, earlier)
-    out0, mid0 = outward(f0), across(w0)
+    mid0, out0 = across(w0), outward(f0)
     gated = gated_conv(q, k, v, rate, residue, skip, before, ([last, earlier], spot))
     rest = jnp.concatenate(arrived)
-    gated, rest, out0, mid0 = tie(gated, rest, out0, mid0)
+    gated, rest, mid0, out0 = tie(gated, rest, mid0, out0)
 
     nr, fr = near(rest), far(rest)
     ours = [gated] + [exchange(gated, "ctx", r) for r in range(1, PLANE)]
     theirs_x = exchange(ours[1], "ch", 1)
-    fr, nr, rest, flags, places, theirs_x, *ours = tie(fr, nr, rest, flags, places, theirs_x, *ours)
+    nr, fr, rest, flags, places, theirs_x, *ours = tie(nr, fr, rest, flags, places, theirs_x, *ours)
 
     out1, mid1 = outward(fr), across(rest)
     theirs = [theirs_x if r == 1 else exchange(x, "ch", 1) for r, x in enumerate(ours)]
@@ -388,12 +398,12 @@
 
     def finish(*spots):
         chosen = [ours[r] for r in spots], [theirs[r] for r in spots]
-        return product(flags, places, *chosen, blocks, [accs[r] for r in spots], [cols], jnp.bfloat16)[0]
+        return product(flags, places, *chosen, blocks, [accs[r] for r in spots], [cols], jnp.bfloat16, 0 in spots)[0]
 
     (made3,) = finish(3)
     back3 = exchange(made3, "ctx", 3)
-    back3, made0, made1, made2 = tie(back3, *finish(0, 1, 2))
-    return assemble(places, [[made0, exchange(made1, "ctx", 1), exchange(made2, "ctx", 2), back3]])
+    back3, held, made1, made2 = tie(back3, *finish(0, 1, 2))
+    return assemble(places, held, [exchange(made1, "ctx", 1), exchange(made2, "ctx", 2), back3])
 
 
 def body(q, k, v, residue, rate, skip, w_out):

time: 171 us -> 173 us (1.012)
  waiting for transfers between devices: 81.4 us -> 85.9 us
    ppermute x2, starting transfers between devices: 8.48 us -> 4.26 us  [across(): return lax.ppermute(x, 'ctx', [(i, i ^ 3 * PLANE) for i in middle])]
    ppermute x19, waiting for transfers between devices: 62.6 us -> 66.8 us  [exchange(): return lax.ppermute(x, axis, [(i, i ^ flip) for i in range(count)])]
    ppermute x19, starting transfers between devices: 18.8 us -> 21.6 us  [exchange(): return lax.ppermute(x, axis, [(i, i ^ flip) for i in range(count)])]
    unnamed x35 -> x33, local copies, waits for them, and re-layouts: 5.59 us -> 4.56 us
  transfers between devices with their start and end apart: 25 -> 25, of which waited for: 14 -> 15; matrix products, arithmetic and copies ran while one was open for 2% -> 2% of each run, Pallas kernels for 18% -> 18%
where the time goes in v17:
time: 173 us; the launch traced here: 172 us
  waiting for transfers between devices  85.9 us (50%)
  starting transfers between devices  38.5 us (22%)
  Pallas kernels  36.4 us (21%)
  local copies, waits for them, and re-layouts  7.9 us (5%)
  other arithmetic  3.43 us (2%)
    ppermute x19, waiting for transfers between devices, exchange(): return lax.ppermute(x, axis, [(i, i ^ flip) for i in range(count)])  66.8 us
    pallas_call x3, Pallas kernels, product(): pl.pallas_call(kernel, in_specs=[smem, smem] + [anywhere] * (2 * parts +...  22.3 us
    ppermute x19, starting transfers between devices, exchange(): return lax.ppermute(x, axis, [(i, i ^ flip) for i in range(count)])  21.6 us
    ppermute x2, waiting for transfers between devices, outward(): return lax.ppermute(x, 'ctx', [(i, i ^ PLANE) for i in middle])  9.79 us
    pallas_call x1, Pallas kernels, gated_conv(): pl.pallas_call(conv_kernel, grid=(chan // width,), in_specs=[wide, wide,...  8.51 us
    ppermute x2, starting transfers between devices, shift_ctx(): return lax.ppermute(x, 'ctx', [(i, i + by) for i in range(count - by)])  6.93 us
    ppermute x2, starting transfers between devices, outward(): return lax.ppermute(x, 'ctx', [(i, i ^ PLANE) for i in middle])  5.64 us
    ppermute x2, waiting for transfers between devices, shift_ctx(): return lax.ppermute(x, 'ctx', [(i, i + by) for i in range(count - by)])  5.16 us
  transfers between devices with their start and end apart: 25, of which 15 were waited for; matrix products, arithmetic and copies ran while one was open for 2% of the time, Pallas kernels for 18%

profile of v17, /device:TPU:8, one launch (start us, length us, event | category | flops | bytes accessed | tf_op | source)
XLA Modules:
  0.0 172.4 jit_solution(1309301533211249476)
XLA Ops:
  0.0 2.6 %constant_dynamic-slice_fusion = (bf16[256,768]{1,0:T(8,128)(2,1)}, bf16[256,768]{1,0:T(8,128)(2,1)}, bf16[256,768]{1,0:T(8,128)(2,1)S(1)}, bf16[256,768]{1,0:T(8,128)(2,1)}) fusion(bf16[256,3072]{1,0:T(8,128)(2,1)} %param.15, s32[]{:T(128)S(6)} %select_n.84, s32[]{:T(128)S(6)} %select_n.82, s32[]{:T(128)S(6)} %select_n.81, s32[]{:T(128)S(6)} %select_n.83), kind=kLoop, calls=%fused_computation.5 | loop fusion | bytes 3145744 | tf_op jit(solution)/shard_map/dynamic_slice | solution.py:344
  2.6 2.6 %collective-permute-start.3 = (bf16[256,768]{1,0:T(8,128)(2,1)S(1)}, bf16[256,768]{1,0:T(8,128)(2,1)S(1)}, u32[]{:S(2)}, u32[]{:S(2)}) collective-permute-start(bf16[256,768]{1,0:T(8,128)(2,1)S(1)} %get-tuple-element.200.refs_8_), channel_id=1, source_target_pairs={{0,16},{2,18},{4,20},{6,22},{8,24},{10,26},{12,28},{14,30},{16,0},... | collective-permute-start | bytes 1179656 | tf_op jit(solution)/shard_map/ppermute | solution.py:150
  5.7 15.9 %while.14 = (s32[]{:T(128)}, f32[16,16,128]{2,1,0:T(8,128)}, f32[16,16,128]{2,1,0:T(8,128)}, s32[]{:T(128)}, pred[]{:T(512)}, /*index=5*/bf16[256,2048]{1,0:T(8,...) while((s32[]{:T(128)}, f32[16,16,128]{2,1,0:T(8,128)}, ...), condition=%wide.region_1.2_spmd, body=%wide.region_0.1_spmd.sunk | while | flops 17399808 | bytes 4456652 | solution.py:185
  5.7 4.0 %end_states.3 = f32[16,16,128]{2,1,0:T(8,128)} custom-call(bf16[256,2048]{1,0:T(8,128)(2,1)S(1)} %get-tuple-element.332.k_ref, bf16[256,2048]{1,0:T(8,128)(2,1)S(1)} %get-tuple-element.333.v_ref, f32[16,2048]{1,0:T(8,128)S(1)} %get-tuple-element.334.rate_ref), custom_call_target="tpu_custom_call" | custom-call | flops 16777216 | bytes 2097152 | tf_op jit(solution)/shard_map/while/body/end_states/pallas_call | solution.py:98
  11.1 3.7 %collective-permute-done = f32[16,16,128]{2,1,0:T(8,128)S(1)} collective-permute-done((f32[16,16,128]{2,1,0:T(8,128)}, f32[16,16,128]{2,1,0:T(8,128)S(1)}, u32[]{:S(2)}, u32[]{:S(2)}) %collective-permute-start) | collective-permute-done | bytes 131104 | tf_op jit(solution)/shard_map/while/body/ppermute | solution.py:150
  17.4 3.4 %collective-permute-done.1 = f32[16,16,128]{2,1,0:T(8,128)S(1)} collective-permute-done((f32[16,16,128]{2,1,0:T(8,128)S(1)}, f32[16,16,128]{2,1,0:T(8,128)S(1)}, u32[]{:S(2)}, u32[]{:S(2)}) %collective-permute-start.1) | collective-permute-done | bytes 131104 | tf_op jit(solution)/shard_map/while/body/ppermute | solution.py:150
  23.0 2.4 %collective-permute-start.4 = (f32[16,16,128]{2,1,0:T(8,128)}, f32[16,16,128]{2,1,0:T(8,128)S(1)}, u32[]{:S(2)}, u32[]{:S(2)}) collective-permute-start(f32[16,16,128]{2,1,0:T(8,128)} %get-tuple-element.193), channel_id=1, source_target_pairs={{0,8},{2,10},{4,12},{6,14},{8,16},{10,18},{12,20},{14,22},{16,24},... | collective-permute-start | bytes 393224 | tf_op jit(solution)/shard_map/ppermute | solution.py:145
  31.1 4.6 %collective-permute-start.5 = (f32[16,16,128]{2,1,0:T(8,128)S(1)}, f32[16,16,128]{2,1,0:T(8,128)S(1)}, u32[]{:S(2)}, u32[]{:S(2)}) collective-permute-start(f32[16,16,128]{2,1,0:T(8,128)S(1)} %multiply_add_fusion), channel_id=1, source_target_pairs={{0,16},{2,18},{4,20},{6,22},{8,24},{10,26},{12,28},{14,30},{1,17},... | collective-permute-start | bytes 393224 | tf_op jit(solution)/shard_map/ppermute | solution.py:145
  35.7 4.0 %collective-permute-done.5.refs_1_ = f32[16,16,128]{2,1,0:T(8,128)S(1)} collective-permute-done((f32[16,16,128]{2,1,0:T(8,128)S(1)}, f32[16,16,128]{2,1,0:T(8,128)S(1)}, u32[]{:S(2)}, u32[]{:S(2)}) %collective-permute-start.5) | collective-permute-done | bytes 131104 | tf_op jit(solution)/shard_map/ppermute | solution.py:145
  39.7 2.3 %collective-permute-start.9 = (bf16[256,768]{1,0:T(8,128)(2,1)}, bf16[256,768]{1,0:T(8,128)(2,1)S(1)}, u32[]{:S(2)}, u32[]{:S(2)}) collective-permute-start(bf16[256,768]{1,0:T(8,128)(2,1)} %copy-done.13), channel_id=1, source_target_pairs={{8,16},{10,18},{12,20},{14,22},{16,8},{18,10},{20,12},{22,14},{9,1... | collective-permute-start | bytes 1179656 | tf_op jit(solution)/shard_map/ppermute | solution.py:338
  44.1 8.5 %gated_conv.1.refs_0_ = bf16[2,256,1024]{2,1,0:T(8,128)(2,1)} custom-call(bf16[256,2048]{1,0:T(8,128)(2,1)} %q_ref.1, bf16[256,2048]{1,0:T(8,128)(2,1)S(1)} %get-tuple-element.377, bf16[256,2048]{1,0:T(8,128)(2,1)S(1)} %get-tuple-element.378, f32[16,2048]{1,0:T(8,128)S(1)} %get-tuple-element.383, f32[16,2048]{1,0:T(8,128)} %residue_ref.1, ...), custom_call_target="tpu_custom_call" | custom-call | flops 33554432 | bytes 4194304 | tf_op jit(solution)/shard_map/gated_conv/pallas_call | solution.py:128
  57.7 2.4 %collective-permute-start.11 = (bf16[768,768]{1,0:T(8,128)(2,1)S(1)}, bf16[768,768]{1,0:T(8,128)(2,1)}, u32[]{:S(2)}, u32[]{:S(2)}) collective-permute-start(bf16[768,768]{1,0:T(8,128)(2,1)S(1)} %pad_maximum_fusion.refs_9_), channel_id=1, source_target_pairs={{0,8},{2,10},{4,12},{6,14},{8,0},{10,2},{12,4},{14,6},{16,24},{18,... | collective-permute-start | bytes 3538952 | tf_op jit(solution)/shard_map/ppermute | solution.py:150
  62.1 18.2 %collective-permute-done.13.refs_1_ = bf16[2,256,1024]{2,1,0:T(8,128)(2,1)S(1)} collective-permute-done((bf16[2,256,1024]{2,1,0:T(8,128)(2,1)S(1)}, bf16[2,256,1024]{2,1,0:T(8,128)(2,1)S(1)}, u32[]{:S(2)}, u32[]{:S(2)}) %collective-permute-start.13) | collective-permute-done | bytes 1048608 | tf_op jit(solution)/shard_map/ppermute | solution.py:150
  81.9 19.9 %collective-permute-done.16.refs_3_.refs_0_ = bf16[2,256,1024]{2,1,0:T(8,128)(2,1)} collective-permute-done((bf16[2,256,1024]{2,1,0:T(8,128)(2,1)S(1)}, bf16[2,256,1024]{2,1,0:T(8,128)(2,1)}, u32[]{:S(2)}, u32[]{:S(2)}) %collective-permute-start.16) | collective-permute-done | bytes 1048608 | tf_op jit(solution)/shard_map/ppermute | solution.py:150
  101.8 5.3 %collective-permute-done.15.refs_2_ = bf16[2,256,1024]{2,1,0:T(8,128)(2,1)} collective-permute-done((bf16[2,256,1024]{2,1,0:T(8,128)(2,1)S(1)}, bf16[2,256,1024]{2,1,0:T(8,128)(2,1)}, u32[]{:S(2)}, u32[]{:S(2)}) %collective-permute-start.15) | collective-permute-done | bytes 1048608 | tf_op jit(solution)/shard_map/ppermute | solution.py:150
  107.1 3.0 %collective-permute-done.11.refs_11_ = bf16[768,768]{1,0:T(8,128)(2,1)} collective-permute-done((bf16[768,768]{1,0:T(8,128)(2,1)S(1)}, bf16[768,768]{1,0:T(8,128)(2,1)}, u32[]{:S(2)}, u32[]{:S(2)}) %collective-permute-start.11) | collective-permute-done | bytes 1179680 | tf_op jit(solution)/shard_map/ppermute | solution.py:150
  110.6 3.6 %collective-permute-start.18 = (bf16[768,768]{1,0:T(8,128)(2,1)}, bf16[768,768]{1,0:T(8,128)(2,1)S(1)}, u32[]{:S(2)}, u32[]{:S(2)}) collective-permute-start(bf16[768,768]{1,0:T(8,128)(2,1)} %collective-permute-done.12.refs_13_), channel_id=1, source_target_pairs={{8,0},{10,2},{12,4},{14,6},{16,24},{18,26},{20,28},{22,30},{9,1},{... | collective-permute-start | bytes 3538952 | tf_op jit(solution)/shard_map/ppermute | solution.py:341
  118.1 12.4 %product.3 = (f32[256,768]{1,0:T(8,128)}, f32[256,768]{1,0:T(8,128)}, f32[256,768]{1,0:T(8,128)}, f32[256,768]{1,0:T(8,128)}) custom-call(s32[5]{0:T(128)} %stack.36.flag_ref, s32[4]{0:T(128)} %pad_add_fusion.place_ref, bf16[2,256,1024]{2,1,0:T(8,128)(2,1)} %gated_conv.1.refs_0_, bf16[2,256,1024]{2,1,0:T(8,128)(2,1)} %copy-done.9, ...), custom_call_target="tpu_custom_call" | custom-call | flops 4831838208 | bytes 11010048 | tf_op jit(solution)/shard_map/product/pallas_call | solution.py:266
  130.6 9.8 %collective-permute-done.18.refs_4_.refs_8_ = bf16[768,768]{1,0:T(8,128)(2,1)S(1)} collective-permute-done((bf16[768,768]{1,0:T(8,128)(2,1)}, bf16[768,768]{1,0:T(8,128)(2,1)S(1)}, u32[]{:S(2)}, u32[]{:S(2)}) %collective-permute-start.18) | collective-permute-done | bytes 1179680 | tf_op jit(solution)/shard_map/ppermute | solution.py:341
  140.3 4.1 %collective-permute-done.19.refs_5_.refs_9_ = bf16[768,768]{1,0:T(8,128)(2,1)S(1)} collective-permute-done((bf16[768,768]{1,0:T(8,128)(2,1)}, bf16[768,768]{1,0:T(8,128)(2,1)S(1)}, u32[]{:S(2)}, u32[]{:S(2)}) %collective-permute-start.19) | collective-permute-done | bytes 1179680 | tf_op jit(solution)/shard_map/ppermute | solution.py:338
  145.5 3.8 %product.4 = bf16[256,768]{1,0:T(8,128)(2,1)} custom-call(s32[5]{0:T(128)} %stack.36.flag_ref, s32[4]{0:T(128)} %pad_add_fusion.place_ref, bf16[2,256,1024]{2,1,0:T(8,128)(2,1)} %collective-permute-done.16.refs_3_.refs_0_, bf16[2,256,1024]{2,1,0:T(8,128)(2,1)} %copy-done.11, bf16[256,768]{1,0:T(8,128)(2,1)} %collective-permute-done.10.refs_2_.refs_6_, ...), custom_call_target="tpu_custom_call" | custom-call | flops 402653184 | bytes 2097152 | tf_op jit(solution)/shard_map/product/pallas_call | solution.py:266
  150.8 6.1 %product.5 = (bf16[256,3072]{1,0:T(8,128)(2,1)}, bf16[256,768]{1,0:T(8,128)(2,1)}, bf16[256,768]{1,0:T(8,128)(2,1)}) custom-call(s32[5]{0:T(128)} %stack.36.flag_ref, s32[4]{0:T(128)} %pad_add_fusion.place_ref, bf16[2,256,1024]{2,1,0:T(8,128)(2,1)} %gated_conv.1.refs_0_, bf16[2,256,1024]{2,1,0:T(8,128)(2,1)} %copy-done.9, ...), custom_call_target="tpu_custom_call" | custom-call | flops 1207959552 | bytes 3145728 | tf_op jit(solution)/shard_map/product/pallas_call | solution.py:266
  157.0 3.9 %collective-permute-done.22.refs_2_ = bf16[256,768]{1,0:T(8,128)(2,1)S(1)} collective-permute-done((bf16[256,768]{1,0:T(8,128)(2,1)}, bf16[256,768]{1,0:T(8,128)(2,1)S(1)}, u32[]{:S(2)}, u32[]{:S(2)}) %collective-permute-start.22) | collective-permute-done | bytes 393248 | tf_op jit(solution)/shard_map/ppermute | solution.py:150
  162.9 7.6 %collective-permute-done.23.refs_0_ = bf16[256,768]{1,0:T(8,128)(2,1)S(1)} collective-permute-done((bf16[256,768]{1,0:T(8,128)(2,1)}, bf16[256,768]{1,0:T(8,128)(2,1)S(1)}, u32[]{:S(2)}, u32[]{:S(2)}) %collective-permute-start.23) | collective-permute-done | bytes 393248 | tf_op jit(solution)/shard_map/ppermute | solution.py:150
  (74 shorter events, 33.8 us)
Async XLA Ops:
  2.6 19.3 %collective-permute-start.3 = (bf16[256,768]{1,0:T(8,128)(2,1)S(1)}, bf16[256,768]{1,0:T(8,128)(2,1)S(1)}, u32[]{:S(2)}, u32[]{:S(2)}) collective-permute-start(bf16[256,768]{1,0:T(8,128)(2,1)S(1)} %get-tuple-element.200.refs_8_), channel_id=1, source_target_pairs={{0,16},{2,18},{4,20},{6,22},{8,24},{10,26},{12,28},{14,30},{16,0},... | collective-permute-start | bytes 1179656 | tf_op jit(solution)/shard_map/ppermute | solution.py:150
  5.2 17.9 %collective-permute-start.2 = (bf16[256,768]{1,0:T(8,128)(2,1)S(1)}, bf16[256,768]{1,0:T(8,128)(2,1)}, u32[]{:S(2)}, u32[]{:S(2)}) collective-permute-start(bf16[256,768]{1,0:T(8,128)(2,1)S(1)} %get-tuple-element.200.refs_8_), channel_id=1, source_target_pairs={{0,8},{2,10},{4,12},{6,14},{8,0},{10,2},{12,4},{14,6},{16,24},{18,... | collective-permute-start | bytes 1179656 | tf_op jit(solution)/shard_map/ppermute | solution.py:150
  9.7 5.2 %collective-permute-start = (f32[16,16,128]{2,1,0:T(8,128)}, f32[16,16,128]{2,1,0:T(8,128)S(1)}, u32[]{:S(2)}, u32[]{:S(2)}) collective-permute-start(f32[16,16,128]{2,1,0:T(8,128)} %end_states.3), channel_id=1, source_target_pairs={{0,2},{2,0},{4,6},{6,4},{8,10},{10,8},{12,14},{14,12},{16,18},{18,... | collective-permute-start | bytes 393224 | tf_op jit(solution)/shard_map/while/body/ppermute | solution.py:150
  23.0 7.1 %collective-permute-start.4 = (f32[16,16,128]{2,1,0:T(8,128)}, f32[16,16,128]{2,1,0:T(8,128)S(1)}, u32[]{:S(2)}, u32[]{:S(2)}) collective-permute-start(f32[16,16,128]{2,1,0:T(8,128)} %get-tuple-element.193), channel_id=1, source_target_pairs={{0,8},{2,10},{4,12},{6,14},{8,16},{10,18},{12,20},{14,22},{16,24},... | collective-permute-start | bytes 393224 | tf_op jit(solution)/shard_map/ppermute | solution.py:145
  25.4 27.2 %collective-permute-start.6 = (bf16[256,768]{1,0:T(8,128)(2,1)}, bf16[256,768]{1,0:T(8,128)(2,1)S(1)}, u32[]{:S(2)}, u32[]{:S(2)}) collective-permute-start(bf16[256,768]{1,0:T(8,128)(2,1)} %get-tuple-element.197), channel_id=1, source_target_pairs={{0,2},{2,0},{4,6},{6,4},{8,10},{10,8},{12,14},{14,12},{16,18},{18,... | collective-permute-start | bytes 1179656 | tf_op jit(solution)/shard_map/ppermute | solution.py:150
  26.9 25.7 %collective-permute-start.7 = (bf16[256,768]{1,0:T(8,128)(2,1)}, bf16[256,768]{1,0:T(8,128)(2,1)S(1)}, u32[]{:S(2)}, u32[]{:S(2)}) collective-permute-start(bf16[256,768]{1,0:T(8,128)(2,1)} %get-tuple-element.198), channel_id=1, source_target_pairs={{0,4},{2,6},{4,0},{6,2},{8,12},{10,14},{12,8},{14,10},{16,20},{18,... | collective-permute-start | bytes 1179656 | tf_op jit(solution)/shard_map/ppermute | solution.py:150
  28.5 24.2 %collective-permute-start.8 = (bf16[256,768]{1,0:T(8,128)(2,1)}, bf16[256,768]{1,0:T(8,128)(2,1)S(1)}, u32[]{:S(2)}, u32[]{:S(2)}) collective-permute-start(bf16[256,768]{1,0:T(8,128)(2,1)} %get-tuple-element.199), channel_id=1, source_target_pairs={{0,6},{2,4},{4,2},{6,0},{8,14},{10,12},{12,10},{14,8},{16,22},{18,... | collective-permute-start | bytes 1179656 | tf_op jit(solution)/shard_map/ppermute | solution.py:150
  31.1 8.6 %collective-permute-start.5 = (f32[16,16,128]{2,1,0:T(8,128)S(1)}, f32[16,16,128]{2,1,0:T(8,128)S(1)}, u32[]{:S(2)}, u32[]{:S(2)}) collective-permute-start(f32[16,16,128]{2,1,0:T(8,128)S(1)} %multiply_add_fusion), channel_id=1, source_target_pairs={{0,16},{2,18},{4,20},{6,22},{8,24},{10,26},{12,28},{14,30},{1,17},... | collective-permute-start | bytes 393224 | tf_op jit(solution)/shard_map/ppermute | solution.py:145
  39.7 13.1 %collective-permute-start.9 = (bf16[256,768]{1,0:T(8,128)(2,1)}, bf16[256,768]{1,0:T(8,128)(2,1)S(1)}, u32[]{:S(2)}, u32[]{:S(2)}) collective-permute-start(bf16[256,768]{1,0:T(8,128)(2,1)} %copy-done.13), channel_id=1, source_target_pairs={{8,16},{10,18},{12,20},{14,22},{16,8},{18,10},{20,12},{22,14},{9,1... | collective-permute-start | bytes 1179656 | tf_op jit(solution)/shard_map/ppermute | solution.py:338
  42.0 10.7 %collective-permute-start.10 = (bf16[256,768]{1,0:T(8,128)(2,1)}, bf16[256,768]{1,0:T(8,128)(2,1)}, u32[]{:S(2)}, u32[]{:S(2)}) collective-permute-start(bf16[256,768]{1,0:T(8,128)(2,1)} %copy-done.15), channel_id=1, source_target_pairs={{8,0},{10,2},{12,4},{14,6},{16,24},{18,26},{20,28},{22,30},{9,1},{... | collective-permute-start | bytes 1179656 | tf_op jit(solution)/shard_map/ppermute | solution.py:341
  54.3 26.1 %collective-permute-start.13 = (bf16[2,256,1024]{2,1,0:T(8,128)(2,1)S(1)}, bf16[2,256,1024]{2,1,0:T(8,128)(2,1)S(1)}, u32[]{:S(2)}, u32[]{:S(2)}) collective-permute-start(bf16[2,256,1024]{2,1,0:T(8,128)(2,1)S(1)} %copy-done.6), channel_id=1, source_target_pairs={{0,2},{2,0},{4,6},{6,4},{8,10},{10,8},{12,14},{14,12},{16,18},{18,... | collective-permute-start | bytes 3145736 | tf_op jit(solution)/shard_map/ppermute | solution.py:150
  55.8 51.4 %collective-permute-start.12 = (bf16[768,768]{1,0:T(8,128)(2,1)S(1)}, bf16[768,768]{1,0:T(8,128)(2,1)}, u32[]{:S(2)}, u32[]{:S(2)}) collective-permute-start(bf16[768,768]{1,0:T(8,128)(2,1)S(1)} %pad_maximum_fusion.refs_9_), channel_id=1, source_target_pairs={{0,16},{2,18},{4,20},{6,22},{8,24},{10,26},{12,28},{14,30},{16,0},... | collective-permute-start | bytes 3538952 | tf_op jit(solution)/shard_map/ppermute | solution.py:150
  57.7 52.4 %collective-permute-start.11 = (bf16[768,768]{1,0:T(8,128)(2,1)S(1)}, bf16[768,768]{1,0:T(8,128)(2,1)}, u32[]{:S(2)}, u32[]{:S(2)}) collective-permute-start(bf16[768,768]{1,0:T(8,128)(2,1)S(1)} %pad_maximum_fusion.refs_9_), channel_id=1, source_target_pairs={{0,8},{2,10},{4,12},{6,14},{8,0},{10,2},{12,4},{14,6},{16,24},{18,... | collective-permute-start | bytes 3538952 | tf_op jit(solution)/shard_map/ppermute | solution.py:150
  60.1 41.7 %collective-permute-start.16 = (bf16[2,256,1024]{2,1,0:T(8,128)(2,1)S(1)}, bf16[2,256,1024]{2,1,0:T(8,128)(2,1)}, u32[]{:S(2)}, u32[]{:S(2)}) collective-permute-start(bf16[2,256,1024]{2,1,0:T(8,128)(2,1)S(1)} %copy-done.6), channel_id=1, source_target_pairs={{0,6},{2,4},{4,2},{6,0},{8,14},{10,12},{12,10},{14,8},{16,22},{18,... | collective-permute-start | bytes 3145736 | tf_op jit(solution)/shard_map/ppermute | solution.py:150
  61.6 45.5 %collective-permute-start.15 = (bf16[2,256,1024]{2,1,0:T(8,128)(2,1)S(1)}, bf16[2,256,1024]{2,1,0:T(8,128)(2,1)}, u32[]{:S(2)}, u32[]{:S(2)}) collective-permute-start(bf16[2,256,1024]{2,1,0:T(8,128)(2,1)S(1)} %copy-done.6), channel_id=1, source_target_pairs={{0,4},{2,6},{4,0},{6,2},{8,12},{10,14},{12,8},{14,10},{16,20},{18,... | collective-permute-start | bytes 3145736 | tf_op jit(solution)/shard_map/ppermute | solution.py:150
  80.4 29.8 %collective-permute-start.14 = (bf16[2,256,1024]{2,1,0:T(8,128)(2,1)S(1)}, bf16[2,256,1024]{2,1,0:T(8,128)(2,1)}, u32[]{:S(2)}, u32[]{:S(2)}) collective-permute-start(bf16[2,256,1024]{2,1,0:T(8,128)(2,1)S(1)} %collective-permute-done.13.refs_1_), channel_id=1, source_target_pairs={{0,1},{1,0},{2,3},{3,2},{4,5},{5,4},{6,7},{7,6},{8,9},{9,8},{10,11... | collective-permute-start | bytes 3145736 | tf_op jit(solution)/shard_map/ppermute | solution.py:150
  110.1 6.0 %collective-permute-start.17 = (bf16[2,256,1024]{2,1,0:T(8,128)(2,1)}, bf16[2,256,1024]{2,1,0:T(8,128)(2,1)S(1)}, u32[]{:S(2)}, u32[]{:S(2)}) collective-permute-start(bf16[2,256,1024]{2,1,0:T(8,128)(2,1)} %collective-permute-done.16.refs_3_.refs_0_), channel_id=1, source_target_pairs={{0,1},{1,0},{2,3},{3,2},{4,5},{5,4},{6,7},{7,6},{8,9},{9,8},{10,11... | collective-permute-start | bytes 3145736 | tf_op jit(solution)/shard_map/ppermute | solution.py:150
  110.1 6.1 %collective-permute-start.20 = (bf16[2,256,1024]{2,1,0:T(8,128)(2,1)S(1)}, bf16[2,256,1024]{2,1,0:T(8,128)(2,1)S(1)}, u32[]{:S(2)}, u32[]{:S(2)}) collective-permute-start(bf16[2,256,1024]{2,1,0:T(8,128)(2,1)S(1)} %copy-done.6), channel_id=1, source_target_pairs={{0,1},{1,0},{2,3},{3,2},{4,5},{5,4},{6,7},{7,6},{8,9},{9,8},{10,11... | collective-permute-start | bytes 3145736 | tf_op jit(solution)/shard_map/ppermute | solution.py:150
  110.6 7.5 %collective-permute-start.21 = (bf16[2,256,1024]{2,1,0:T(8,128)(2,1)}, bf16[2,256,1024]{2,1,0:T(8,128)(2,1)}, u32[]{:S(2)}, u32[]{:S(2)}) collective-permute-start(bf16[2,256,1024]{2,1,0:T(8,128)(2,1)} %collective-permute-done.15.refs_2_), channel_id=1, source_target_pairs={{0,1},{1,0},{2,3},{3,2},{4,5},{5,4},{6,7},{7,6},{8,9},{9,8},{10,11... | collective-permute-start | bytes 3145736 | tf_op jit(solution)/shard_map/ppermute | solution.py:150
  110.6 29.7 %collective-permute-start.18 = (bf16[768,768]{1,0:T(8,128)(2,1)}, bf16[768,768]{1,0:T(8,128)(2,1)S(1)}, u32[]{:S(2)}, u32[]{:S(2)}) collective-permute-start(bf16[768,768]{1,0:T(8,128)(2,1)} %collective-permute-done.12.refs_13_), channel_id=1, source_target_pairs={{8,0},{10,2},{12,4},{14,6},{16,24},{18,26},{20,28},{22,30},{9,1},{... | collective-permute-start | bytes 3538952 | tf_op jit(solution)/shard_map/ppermute | solution.py:341
  114.2 30.2 %collective-permute-start.19 = (bf16[768,768]{1,0:T(8,128)(2,1)}, bf16[768,768]{1,0:T(8,128)(2,1)S(1)}, u32[]{:S(2)}, u32[]{:S(2)}) collective-permute-start(bf16[768,768]{1,0:T(8,128)(2,1)} %copy-done.8), channel_id=1, source_target_pairs={{8,16},{10,18},{12,20},{14,22},{16,8},{18,10},{20,12},{22,14},{9,1... | collective-permute-start | bytes 3538952 | tf_op jit(solution)/shard_map/ppermute | solution.py:338
  149.3 11.6 %collective-permute-start.22 = (bf16[256,768]{1,0:T(8,128)(2,1)}, bf16[256,768]{1,0:T(8,128)(2,1)S(1)}, u32[]{:S(2)}, u32[]{:S(2)}) collective-permute-start(bf16[256,768]{1,0:T(8,128)(2,1)} %product.4), channel_id=1, source_target_pairs={{0,6},{2,4},{4,2},{6,0},{8,14},{10,12},{12,10},{14,8},{16,22},{18,... | collective-permute-start | bytes 1179656 | tf_op jit(solution)/shard_map/ppermute | solution.py:150
  160.9 9.7 %collective-permute-start.23 = (bf16[256,768]{1,0:T(8,128)(2,1)}, bf16[256,768]{1,0:T(8,128)(2,1)S(1)}, u32[]{:S(2)}, u32[]{:S(2)}) collective-permute-start(bf16[256,768]{1,0:T(8,128)(2,1)} %get-tuple-element.231), channel_id=1, source_target_pairs={{0,2},{2,0},{4,6},{6,4},{8,10},{10,8},{12,14},{14,12},{16,18},{18,... | collective-permute-start | bytes 1179656 | tf_op jit(solution)/shard_map/ppermute | solution.py:150
  161.4 9.4 %collective-permute-start.24 = (bf16[256,768]{1,0:T(8,128)(2,1)}, bf16[256,768]{1,0:T(8,128)(2,1)S(1)}, u32[]{:S(2)}, u32[]{:S(2)}) collective-permute-start(bf16[256,768]{1,0:T(8,128)(2,1)} %get-tuple-element.232), channel_id=1, source_target_pairs={{0,4},{2,6},{4,0},{6,2},{8,12},{10,14},{12,8},{14,10},{16,20},{18,... | collective-permute-start | bytes 1179656 | tf_op jit(solution)/shard_map/ppermute | solution.py:150
  (17 other events, 194.7 us)

commit v18 on v16

--- a/solution.py
+++ b/solution.py
@@ -185,19 +185,17 @@
     return lax.fori_loop(0, once, run, tuple(empty))
 
 
-def product(flags, places, ours, theirs, blocks, accs, widths, out_dtype):
+def product(flags, places, ours, theirs, blocks, accs, first_col, cols, out_dtype):
     _, rows, depth = ours[0].shape
     chunk = depth // PLANE
-    cols = sum(widths)
     count, parts = len(blocks), len(ours)
-    outs = parts * len(widths)
     weights = [array for _, _, pieces in blocks for choices, _ in pieces for array in choices]
     accs = accs or []
 
     def kernel(flag_ref, place_ref, *refs):
         our_refs, their_refs, refs = refs[:parts], refs[parts : 2 * parts], refs[2 * parts :]
         weight_refs, refs = list(refs[: len(weights)]), refs[len(weights) :]
-        acc_refs, out_refs = refs[: len(accs)], refs[len(accs) : len(accs) + outs]
+        acc_refs, out_refs = refs[: len(accs)], refs[len(accs) : len(accs) + parts]
         gated_buf, weight_buf, acc_buf, gated_sems, weight_sems, acc_sem = refs[-6:]
 
         def target(b, at):
@@ -224,7 +222,7 @@
                     copy = pltpu.make_async_copy(refs_of[r].at[half], target_rows, gated_sems.at[b])
                     pl.when(flag_ref[flag] // 2 == c)(copy.start)
         for r, acc_ref in enumerate(acc_refs):
-            pltpu.make_async_copy(acc_ref, acc_buf.at[r], acc_sem).start()
+            pltpu.make_async_copy(acc_ref.at[:, pl.ds(first_col, cols)], acc_buf.at[r], acc_sem).start()
         for b in range(count):
             block = weight_buf.at[pl.ds(b * depth, depth), :]
             pltpu.make_async_copy(block, block, weight_sems.at[b]).wait()
@@ -232,32 +230,29 @@
             if accs and not b:
                 pltpu.make_async_copy(acc_buf, acc_buf, acc_sem).wait()
             for col in range(0, cols, 2 * LANES):
-                here = pl.ds(col, 2 * LANES)
+                here = pl.ds(col, min(2 * LANES, cols - col))
                 made = jnp.dot(
                     gated_buf[b], weight_buf[pl.ds(b * depth, depth), here], preferred_element_type=jnp.float32
                 )
-                part = 0 if col < widths[0] else 1
-                inside = pl.ds(col - part * widths[0], 2 * LANES)
                 for r in range(parts):
                     total = made[r * rows : (r + 1) * rows]
-                    out_ref = out_refs[part * parts + r]
                     if b:
-                        total = total + out_ref[:, inside]
+                        total = total + out_refs[r][:, here]
                     elif accs:
                         total = total + acc_buf[r, :, here]
-                    out_ref[:, inside] = total.astype(out_dtype)
+                    out_refs[r][:, here] = total.astype(out_dtype)
 
     smem = pl.BlockSpec(memory_space=pltpu.SMEM)
     anywhere = pl.BlockSpec(memory_space=pl.ANY)
     made = pl.pallas_call(
         kernel,
         in_specs=[smem, smem] + [anywhere] * (2 * parts + len(weights) + len(accs)),
-        out_specs=[pl.BlockSpec(memory_space=pltpu.VMEM)] * outs,
-        out_shape=[jax.ShapeDtypeStruct((rows, width), out_dtype) for width in widths for _ in range(parts)],
+        out_specs=[pl.BlockSpec(memory_space=pltpu.VMEM)] * parts,
+        out_shape=[jax.ShapeDtypeStruct((rows, cols), out_dtype)] * parts,
         scratch_shapes=[
             pltpu.VMEM((count, parts * rows, depth), jnp.bfloat16),
             pltpu.VMEM((count * depth, cols), jnp.bfloat16),
-            pltpu.VMEM((len(accs), *accs[0].shape) if accs else (8, LANES), jnp.float32),
+            pltpu.VMEM((parts, rows, cols) if accs else (8, LANES), jnp.float32),
             pltpu.SemaphoreType.DMA((count,)),
             pltpu.SemaphoreType.DMA((count,)),
             pltpu.SemaphoreType.DMA,
@@ -270,7 +265,7 @@
         ),
         name="product",
     )(flags, places, *ours, *theirs, *weights, *accs)
-    return [list(made[at : at + parts]) for at in range(0, outs, parts)]
+    return [list(made)]
 
 
 def assemble(places, parts):
@@ -372,28 +367,31 @@
     nr, fr = near(rest), far(rest)
     ours = [gated] + [exchange(gated, "ctx", r) for r in range(1, PLANE)]
     theirs_x = exchange(ours[1], "ch", 1)
-    fr, nr, rest, flags, places, theirs_x, *ours = tie(fr, nr, rest, flags, places, theirs_x, *ours)
-
-    out1, mid1 = outward(fr), across(rest)
+    half = cols // 2
+    restA, restB = rest[:, :half], rest[:, half:]
+    fr, nr, rest, restA, restB, flags, places, theirs_x, *ours = tie(
+        fr, nr, rest, restA, restB, flags, places, theirs_x, *ours
+    )
+
+    outA, midA = outward(fr[:, :half]), across(restA)
     theirs = [theirs_x if r == 1 else exchange(x, "ch", 1) for r, x in enumerate(ours)]
     blocks = [
         (0, None, [((w0,), 0), ((rest,), 0)]),
         (1, None, [((n0,), 0), ((nr,), 0)]),
         (2, None, [((f0,), 0), ((fr,), 0)]),
     ]
-    (accs,) = product(flags, places, ours, theirs, blocks, None, [cols], jnp.float32)
-    out1, mid1, *accs = tie(out1, mid1, *accs)
-
-    blocks = [(3, 4, [((out0, mid0), 0), ((out1, mid1), 0)])]
-
-    def finish(*spots):
-        chosen = [ours[r] for r in spots], [theirs[r] for r in spots]
-        return product(flags, places, *chosen, blocks, [accs[r] for r in spots], [cols], jnp.bfloat16)[0]
-
-    (made3,) = finish(3)
-    back3 = exchange(made3, "ctx", 3)
-    back3, made0, made1, made2 = tie(back3, *finish(0, 1, 2))
-    return assemble(places, [[made0, exchange(made1, "ctx", 1), exchange(made2, "ctx", 2), back3]])
+    (accs,) = product(flags, places, ours, theirs, blocks, None, 0, cols, jnp.float32)
+    frB = fr[:, half:]
+    outA, midA, frB, restB, *accs = tie(outA, midA, frB, restB, *accs)
+
+    outB, midB = outward(frB), across(restB)
+
+    def finish(first, out1, mid1):
+        blocks = [(3, 4, [((out0, mid0), first), ((out1, mid1), 0)])]
+        (made,) = product(flags, places, ours, theirs, blocks, accs, first, half, jnp.bfloat16)
+        return [made[0]] + [exchange(made[r], "ctx", r) for r in range(1, PLANE)]
+
+    return assemble(places, [finish(0, outA, midA), finish(half, outB, midB)])
 
 
 def body(q, k, v, residue, rate, skip, w_out):

time: 171 us -> 170 us (level)
  waiting for transfers between devices: 81.4 us -> 67.4 us
  starting transfers between devices: 40.2 us -> 49.6 us
  local copies, waits for them, and re-layouts: 8.98 us -> 11.5 us
    ppermute x2 -> x3, waiting for transfers between devices: 9.88 us -> 2.11 us  [outward(): return lax.ppermute(x, 'ctx', [(i, i ^ PLANE) for i in middle])]
    ppermute x19 -> x22, waiting for transfers between devices: 62.6 us -> 56.4 us  [exchange(): return lax.ppermute(x, axis, [(i, i ^ flip) for i in range(count)])]
    ppermute x2 -> x3, starting transfers between devices: 8.48 us -> 12.2 us  [across(): return lax.ppermute(x, 'ctx', [(i, i ^ 3 * PLANE) for i in middle])]
    slice x0 -> x2, local copies, waits for them, and re-layouts: none -> 3.53 us  [the longest x1 2.38 us: split_block(): frB = fr[:, half:]]
    ppermute x19 -> x22, starting transfers between devices: 18.8 us -> 22.3 us  [exchange(): return lax.ppermute(x, axis, [(i, i ^ flip) for i in range(count)])]
    ppermute x2 -> x3, starting transfers between devices: 6.14 us -> 8.21 us  [outward(): return lax.ppermute(x, 'ctx', [(i, i ^ PLANE) for i in middle])]
    unnamed x35 -> x37, local copies, waits for them, and re-layouts: 5.59 us -> 4.66 us
    ppermute x2 -> x3, waiting for transfers between devices: 4.08 us -> 4.05 us  [across(): return lax.ppermute(x, 'ctx', [(i, i ^ 3 * PLANE) for i in middle])]
  transfers between devices with their start and end apart: 25 -> 30, of which waited for: 14 -> 14; matrix products, arithmetic and copies ran while one was open for 2% -> 5% of each run, Pallas kernels for 18% -> 21%
where the time goes in v18:
time: 170 us; the launch traced here: 169 us
  waiting for transfers between devices  67.4 us (40%)
  starting transfers between devices  49.6 us (29%)
  Pallas kernels  36.5 us (21%)
  local copies, waits for them, and re-layouts  11.5 us (7%)
  other arithmetic  3.39 us (2%)
    ppermute x22, waiting for transfers between devices, exchange(): return lax.ppermute(x, axis, [(i, i ^ flip) for i in range(count)])  56.4 us
    pallas_call x3, Pallas kernels, product(): pl.pallas_call(kernel, in_specs=[smem, smem] + [anywhere] * (2 * parts +...  22.3 us
    ppermute x22, starting transfers between devices, exchange(): return lax.ppermute(x, axis, [(i, i ^ flip) for i in range(count)])  22.3 us
    ppermute x3, starting transfers between devices, across(): return lax.ppermute(x, 'ctx', [(i, i ^ 3 * PLANE) for i in middle])  12.2 us
    pallas_call x1, Pallas kernels, gated_conv(): pl.pallas_call(conv_kernel, grid=(chan // width,), in_specs=[wide, wide,...  8.5 us
    ppermute x3, starting transfers between devices, outward(): return lax.ppermute(x, 'ctx', [(i, i ^ PLANE) for i in middle])  8.21 us
    ppermute x2, starting transfers between devices, shift_ctx(): return lax.ppermute(x, 'ctx', [(i, i + by) for i in range(count - by)])  6.85 us
    ppermute x2, waiting for transfers between devices, shift_ctx(): return lax.ppermute(x, 'ctx', [(i, i + by) for i in range(count - by)])  4.88 us
  transfers between devices with their start and end apart: 30, of which 14 were waited for; matrix products, arithmetic and copies ran while one was open for 5% of the time, Pallas kernels for 21%

profile of v18, /device:TPU:8, one launch (start us, length us, event | category | flops | bytes accessed | tf_op | source)
XLA Modules:
  0.0 168.9 jit_solution(17446442676631779049)
XLA Ops:
  0.0 2.6 %constant_dynamic-slice_fusion = (bf16[256,768]{1,0:T(8,128)(2,1)}, bf16[256,768]{1,0:T(8,128)(2,1)}, bf16[256,768]{1,0:T(8,128)(2,1)S(1)}, bf16[256,768]{1,0:T(8,128)(2,1)}) fusion(bf16[256,3072]{1,0:T(8,128)(2,1)} %param.15, s32[]{:T(128)S(6)} %select_n.84, s32[]{:T(128)S(6)} %select_n.82, s32[]{:T(128)S(6)} %select_n.81, s32[]{:T(128)S(6)} %select_n.83), kind=kLoop, calls=%fused_computation.5 | loop fusion | bytes 3145744 | tf_op jit(solution)/shard_map/dynamic_slice | solution.py:329
  2.6 3.0 %collective-permute-start.2 = (bf16[256,768]{1,0:T(8,128)(2,1)S(1)}, bf16[256,768]{1,0:T(8,128)(2,1)}, u32[]{:S(2)}, u32[]{:S(2)}) collective-permute-start(bf16[256,768]{1,0:T(8,128)(2,1)S(1)} %get-tuple-element.206.refs_8_), channel_id=1, source_target_pairs={{0,16},{2,18},{4,20},{6,22},{8,24},{10,26},{12,28},{14,30},{16,0},... | collective-permute-start | bytes 1179656 | tf_op jit(solution)/shard_map/ppermute | solution.py:150
  5.7 15.9 %while.14 = (s32[]{:T(128)}, f32[16,16,128]{2,1,0:T(8,128)}, f32[16,16,128]{2,1,0:T(8,128)}, s32[]{:T(128)}, pred[]{:T(512)}, /*index=5*/bf16[256,2048]{1,0:T(8,...) while((s32[]{:T(128)}, f32[16,16,128]{2,1,0:T(8,128)}, ...), condition=%wide.region_1.2_spmd, body=%wide.region_0.1_spmd.sunk | while | flops 17399808 | bytes 4456652 | solution.py:185
  5.7 4.0 %end_states.3 = f32[16,16,128]{2,1,0:T(8,128)} custom-call(bf16[256,2048]{1,0:T(8,128)(2,1)S(1)} %get-tuple-element.346.k_ref, bf16[256,2048]{1,0:T(8,128)(2,1)S(1)} %get-tuple-element.347.v_ref, f32[16,2048]{1,0:T(8,128)S(1)} %get-tuple-element.348.rate_ref), custom_call_target="tpu_custom_call" | custom-call | flops 16777216 | bytes 2097152 | tf_op jit(solution)/shard_map/while/body/end_states/pallas_call | solution.py:98
  11.2 3.7 %collective-permute-done = f32[16,16,128]{2,1,0:T(8,128)S(1)} collective-permute-done((f32[16,16,128]{2,1,0:T(8,128)}, f32[16,16,128]{2,1,0:T(8,128)S(1)}, u32[]{:S(2)}, u32[]{:S(2)}) %collective-permute-start) | collective-permute-done | bytes 131104 | tf_op jit(solution)/shard_map/while/body/ppermute | solution.py:150
  17.4 3.4 %collective-permute-done.1 = f32[16,16,128]{2,1,0:T(8,128)S(1)} collective-permute-done((f32[16,16,128]{2,1,0:T(8,128)S(1)}, f32[16,16,128]{2,1,0:T(8,128)S(1)}, u32[]{:S(2)}, u32[]{:S(2)}) %collective-permute-start.1) | collective-permute-done | bytes 131104 | tf_op jit(solution)/shard_map/while/body/ppermute | solution.py:150
  23.1 2.3 %collective-permute-start.4 = (f32[16,16,128]{2,1,0:T(8,128)}, f32[16,16,128]{2,1,0:T(8,128)S(1)}, u32[]{:S(2)}, u32[]{:S(2)}) collective-permute-start(f32[16,16,128]{2,1,0:T(8,128)} %get-tuple-element.198), channel_id=1, source_target_pairs={{0,8},{2,10},{4,12},{6,14},{8,16},{10,18},{12,20},{14,22},{16,24},... | collective-permute-start | bytes 393224 | tf_op jit(solution)/shard_map/ppermute | solution.py:145
  31.1 4.5 %collective-permute-start.5 = (f32[16,16,128]{2,1,0:T(8,128)S(1)}, f32[16,16,128]{2,1,0:T(8,128)S(1)}, u32[]{:S(2)}, u32[]{:S(2)}) collective-permute-start(f32[16,16,128]{2,1,0:T(8,128)S(1)} %multiply_add_fusion), channel_id=1, source_target_pairs={{0,16},{2,18},{4,20},{6,22},{8,24},{10,26},{12,28},{14,30},{1,17},... | collective-permute-start | bytes 393224 | tf_op jit(solution)/shard_map/ppermute | solution.py:145
  35.6 3.7 %collective-permute-done.5.refs_1_ = f32[16,16,128]{2,1,0:T(8,128)S(1)} collective-permute-done((f32[16,16,128]{2,1,0:T(8,128)S(1)}, f32[16,16,128]{2,1,0:T(8,128)S(1)}, u32[]{:S(2)}, u32[]{:S(2)}) %collective-permute-start.5) | collective-permute-done | bytes 131104 | tf_op jit(solution)/shard_map/ppermute | solution.py:145
  40.7 6.6 %collective-permute-start.10 = (bf16[256,768]{1,0:T(8,128)(2,1)}, bf16[256,768]{1,0:T(8,128)(2,1)}, u32[]{:S(2)}, u32[]{:S(2)}) collective-permute-start(bf16[256,768]{1,0:T(8,128)(2,1)} %copy-done.15), channel_id=1, source_target_pairs={{8,16},{10,18},{12,20},{14,22},{16,8},{18,10},{20,12},{22,14},{9,1... | collective-permute-start | bytes 1179656 | tf_op jit(solution)/shard_map/ppermute | solution.py:323
  47.3 8.5 %gated_conv.1.refs_0_ = bf16[2,256,1024]{2,1,0:T(8,128)(2,1)} custom-call(bf16[256,2048]{1,0:T(8,128)(2,1)} %q_ref.1, bf16[256,2048]{1,0:T(8,128)(2,1)S(1)} %get-tuple-element.394, bf16[256,2048]{1,0:T(8,128)(2,1)S(1)} %get-tuple-element.395, f32[16,2048]{1,0:T(8,128)S(1)} %get-tuple-element.404, f32[16,2048]{1,0:T(8,128)} %residue_ref.1, ...), custom_call_target="tpu_custom_call" | custom-call | flops 33554432 | bytes 4194304 | tf_op jit(solution)/shard_map/gated_conv/pallas_call | solution.py:128
  62.4 21.1 %collective-permute-done.13.refs_1_ = bf16[2,256,1024]{2,1,0:T(8,128)(2,1)S(1)} collective-permute-done((bf16[2,256,1024]{2,1,0:T(8,128)(2,1)S(1)}, bf16[2,256,1024]{2,1,0:T(8,128)(2,1)S(1)}, u32[]{:S(2)}, u32[]{:S(2)}) %collective-permute-start.13) | collective-permute-done | bytes 1048608 | tf_op jit(solution)/shard_map/ppermute | solution.py:150
  86.1 13.8 %collective-permute-done.16.refs_3_ = bf16[2,256,1024]{2,1,0:T(8,128)(2,1)} collective-permute-done((bf16[2,256,1024]{2,1,0:T(8,128)(2,1)S(1)}, bf16[2,256,1024]{2,1,0:T(8,128)(2,1)}, u32[]{:S(2)}, u32[]{:S(2)}) %collective-permute-start.16) | collective-permute-done | bytes 1048608 | tf_op jit(solution)/shard_map/ppermute | solution.py:150
  99.9 2.6 %collective-permute-done.15.refs_2_ = bf16[2,256,1024]{2,1,0:T(8,128)(2,1)} collective-permute-done((bf16[2,256,1024]{2,1,0:T(8,128)(2,1)S(1)}, bf16[2,256,1024]{2,1,0:T(8,128)(2,1)}, u32[]{:S(2)}, u32[]{:S(2)}) %collective-permute-start.15) | collective-permute-done | bytes 1048608 | tf_op jit(solution)/shard_map/ppermute | solution.py:150
  102.5 3.0 %collective-permute-done.11.refs_13_ = bf16[768,768]{1,0:T(8,128)(2,1)} collective-permute-done((bf16[768,768]{1,0:T(8,128)(2,1)S(1)}, bf16[768,768]{1,0:T(8,128)(2,1)}, u32[]{:S(2)}, u32[]{:S(2)}) %collective-permute-start.11) | collective-permute-done | bytes 1179680 | tf_op jit(solution)/shard_map/ppermute | solution.py:150
  106.1 3.6 %collective-permute-start.21 = (bf16[768,384]{1,0:T(8,128)(2,1)}, bf16[768,384]{1,0:T(8,128)(2,1)}, u32[]{:S(2)}, u32[]{:S(2)}) collective-permute-start(bf16[768,384]{1,0:T(8,128)(2,1)} %get-tuple-element.219), channel_id=1, source_target_pairs={{8,16},{10,18},{12,20},{14,22},{16,8},{18,10},{20,12},{22,14},{9,1... | collective-permute-start | bytes 1769480 | tf_op jit(solution)/shard_map/ppermute | solution.py:323
  109.7 2.4 %fusion = (bf16[768,384]{1,0:T(8,128)(2,1)}, bf16[768,384]{1,0:T(8,128)(2,1)}) fusion(bf16[768,768]{1,0:T(8,128)(2,1)} %collective-permute-done.11.refs_13_), kind=kLoop, calls=%fused_computation.10 | loop fusion | bytes 2359296 | tf_op jit(solution)/shard_map/slice | solution.py:384
  112.0 3.5 %collective-permute-start.20 = (bf16[768,384]{1,0:T(8,128)(2,1)}, bf16[768,384]{1,0:T(8,128)(2,1)}, u32[]{:S(2)}, u32[]{:S(2)}) collective-permute-start(bf16[768,384]{1,0:T(8,128)(2,1)} %get-tuple-element.273), channel_id=1, source_target_pairs={{8,0},{10,2},{12,4},{14,6},{16,24},{18,26},{20,28},{22,30},{9,1},{... | collective-permute-start | bytes 1769480 | tf_op jit(solution)/shard_map/ppermute | solution.py:326
  116.8 12.4 %product.3 = (f32[256,768]{1,0:T(8,128)}, f32[256,768]{1,0:T(8,128)}, f32[256,768]{1,0:T(8,128)}, f32[256,768]{1,0:T(8,128)}) custom-call(s32[5]{0:T(128)} %stack.36.flag_ref, s32[4]{0:T(128)} %pad_add_fusion.place_ref, bf16[2,256,1024]{2,1,0:T(8,128)(2,1)} %gated_conv.1.refs_0_, bf16[2,256,1024]{2,1,0:T(8,128)(2,1)} %copy-done.8, ...), custom_call_target="tpu_custom_call" | custom-call | flops 4831838208 | bytes 11010048 | tf_op jit(solution)/shard_map/product/pallas_call | solution.py:247
  129.2 3.4 %collective-permute-start.25 = (bf16[768,384]{1,0:T(8,128)(2,1)}, bf16[768,384]{1,0:T(8,128)(2,1)S(1)}, u32[]{:S(2)}, u32[]{:S(2)}) collective-permute-start(bf16[768,384]{1,0:T(8,128)(2,1)} %get-tuple-element.238), channel_id=1, source_target_pairs={{8,0},{10,2},{12,4},{14,6},{16,24},{18,26},{20,28},{22,30},{9,1},{... | collective-permute-start | bytes 1769480 | tf_op jit(solution)/shard_map/ppermute | solution.py:326
  134.8 5.0 %product.4 = (bf16[256,384]{1,0:T(8,128)(2,1)}, bf16[256,384]{1,0:T(8,128)(2,1)}, bf16[256,384]{1,0:T(8,128)(2,1)}, bf16[256,384]{1,0:T(8,128)(2,1)}) custom-call(s32[5]{0:T(128)} %stack.36.flag_ref, s32[4]{0:T(128)} %pad_add_fusion.place_ref, bf16[2,256,1024]{2,1,0:T(8,128)(2,1)} %gated_conv.1.refs_0_, bf16[2,256,1024]{2,1,0:T(8,128)(2,1)} %copy-done.8, ...), custom_call_target="tpu_custom_call" | custom-call | flops 805306368 | bytes 2883584 | tf_op jit(solution)/shard_map/product/pallas_call | solution.py:247
  145.4 4.0 %collective-permute-done.26.refs_11_ = bf16[768,384]{1,0:T(8,128)(2,1)S(1)} collective-permute-done((bf16[768,384]{1,0:T(8,128)(2,1)}, bf16[768,384]{1,0:T(8,128)(2,1)S(1)}, u32[]{:S(2)}, u32[]{:S(2)}) %collective-permute-start.26) | collective-permute-done | bytes 589856 | tf_op jit(solution)/shard_map/ppermute | solution.py:323
  150.3 4.9 %product.5 = (bf16[256,384]{1,0:T(8,128)(2,1)}, bf16[256,384]{1,0:T(8,128)(2,1)}, bf16[256,384]{1,0:T(8,128)(2,1)}, bf16[256,384]{1,0:T(8,128)(2,1)}) custom-call(s32[5]{0:T(128)} %stack.36.flag_ref, s32[4]{0:T(128)} %pad_add_fusion.place_ref, bf16[2,256,1024]{2,1,0:T(8,128)(2,1)} %gated_conv.1.refs_0_, bf16[2,256,1024]{2,1,0:T(8,128)(2,1)} %copy-done.8, ...), custom_call_target="tpu_custom_call" | custom-call | flops 805306368 | bytes 2883584 | tf_op jit(solution)/shard_map/product/pallas_call | solution.py:247
  158.8 4.2 %collective-permute-done.27.refs_5_ = bf16[256,384]{1,0:T(8,128)(2,1)S(1)} collective-permute-done((bf16[256,384]{1,0:T(8,128)(2,1)}, bf16[256,384]{1,0:T(8,128)(2,1)S(1)}, u32[]{:S(2)}, u32[]{:S(2)}) %collective-permute-start.27) | collective-permute-done | bytes 196640 | tf_op jit(solution)/shard_map/ppermute | solution.py:150
  (90 shorter events, 42.1 us)
Async XLA Ops:
  2.6 19.1 %collective-permute-start.3 = (bf16[256,768]{1,0:T(8,128)(2,1)S(1)}, bf16[256,768]{1,0:T(8,128)(2,1)S(1)}, u32[]{:S(2)}, u32[]{:S(2)}) collective-permute-start(bf16[256,768]{1,0:T(8,128)(2,1)S(1)} %get-tuple-element.206.refs_8_), channel_id=1, source_target_pairs={{0,8},{2,10},{4,12},{6,14},{8,0},{10,2},{12,4},{14,6},{16,24},{18,... | collective-permute-start | bytes 1179656 | tf_op jit(solution)/shard_map/ppermute | solution.py:150
  2.6 20.5 %collective-permute-start.2 = (bf16[256,768]{1,0:T(8,128)(2,1)S(1)}, bf16[256,768]{1,0:T(8,128)(2,1)}, u32[]{:S(2)}, u32[]{:S(2)}) collective-permute-start(bf16[256,768]{1,0:T(8,128)(2,1)S(1)} %get-tuple-element.206.refs_8_), channel_id=1, source_target_pairs={{0,16},{2,18},{4,20},{6,22},{8,24},{10,26},{12,28},{14,30},{16,0},... | collective-permute-start | bytes 1179656 | tf_op jit(solution)/shard_map/ppermute | solution.py:150
  25.4 30.3 %collective-permute-start.6 = (bf16[256,768]{1,0:T(8,128)(2,1)}, bf16[256,768]{1,0:T(8,128)(2,1)S(1)}, u32[]{:S(2)}, u32[]{:S(2)}) collective-permute-start(bf16[256,768]{1,0:T(8,128)(2,1)} %get-tuple-element.202), channel_id=1, source_target_pairs={{0,2},{2,0},{4,6},{6,4},{8,10},{10,8},{12,14},{14,12},{16,18},{18,... | collective-permute-start | bytes 1179656 | tf_op jit(solution)/shard_map/ppermute | solution.py:150
  27.0 28.8 %collective-permute-start.7 = (bf16[256,768]{1,0:T(8,128)(2,1)}, bf16[256,768]{1,0:T(8,128)(2,1)S(1)}, u32[]{:S(2)}, u32[]{:S(2)}) collective-permute-start(bf16[256,768]{1,0:T(8,128)(2,1)} %get-tuple-element.203), channel_id=1, source_target_pairs={{0,4},{2,6},{4,0},{6,2},{8,12},{10,14},{12,8},{14,10},{16,20},{18,... | collective-permute-start | bytes 1179656 | tf_op jit(solution)/shard_map/ppermute | solution.py:150
  28.5 27.3 %collective-permute-start.8 = (bf16[256,768]{1,0:T(8,128)(2,1)}, bf16[256,768]{1,0:T(8,128)(2,1)S(1)}, u32[]{:S(2)}, u32[]{:S(2)}) collective-permute-start(bf16[256,768]{1,0:T(8,128)(2,1)} %get-tuple-element.204), channel_id=1, source_target_pairs={{0,6},{2,4},{4,2},{6,0},{8,14},{10,12},{12,10},{14,8},{16,22},{18,... | collective-permute-start | bytes 1179656 | tf_op jit(solution)/shard_map/ppermute | solution.py:150
  39.4 16.5 %collective-permute-start.9 = (bf16[256,768]{1,0:T(8,128)(2,1)}, bf16[256,768]{1,0:T(8,128)(2,1)S(1)}, u32[]{:S(2)}, u32[]{:S(2)}) collective-permute-start(bf16[256,768]{1,0:T(8,128)(2,1)} %collective-permute-done.2.refs_12_), channel_id=1, source_target_pairs={{8,0},{10,2},{12,4},{14,6},{16,24},{18,26},{20,28},{22,30},{9,1},{... | collective-permute-start | bytes 1179656 | tf_op jit(solution)/shard_map/ppermute | solution.py:326
  40.7 15.2 %collective-permute-start.10 = (bf16[256,768]{1,0:T(8,128)(2,1)}, bf16[256,768]{1,0:T(8,128)(2,1)}, u32[]{:S(2)}, u32[]{:S(2)}) collective-permute-start(bf16[256,768]{1,0:T(8,128)(2,1)} %copy-done.15), channel_id=1, source_target_pairs={{8,16},{10,18},{12,20},{14,22},{16,8},{18,10},{20,12},{22,14},{9,1... | collective-permute-start | bytes 1179656 | tf_op jit(solution)/shard_map/ppermute | solution.py:323
  57.4 26.1 %collective-permute-start.13 = (bf16[2,256,1024]{2,1,0:T(8,128)(2,1)S(1)}, bf16[2,256,1024]{2,1,0:T(8,128)(2,1)S(1)}, u32[]{:S(2)}, u32[]{:S(2)}) collective-permute-start(bf16[2,256,1024]{2,1,0:T(8,128)(2,1)S(1)} %copy-done.5), channel_id=1, source_target_pairs={{0,2},{2,0},{4,6},{6,4},{8,10},{10,8},{12,14},{14,12},{16,18},{18,... | collective-permute-start | bytes 3145736 | tf_op jit(solution)/shard_map/ppermute | solution.py:150
  58.9 43.6 %collective-permute-start.12 = (bf16[768,768]{1,0:T(8,128)(2,1)S(1)}, bf16[768,768]{1,0:T(8,128)(2,1)}, u32[]{:S(2)}, u32[]{:S(2)}) collective-permute-start(bf16[768,768]{1,0:T(8,128)(2,1)S(1)} %pad_maximum_fusion.refs_9_), channel_id=1, source_target_pairs={{0,8},{2,10},{4,12},{6,14},{8,0},{10,2},{12,4},{14,6},{16,24},{18,... | collective-permute-start | bytes 3538952 | tf_op jit(solution)/shard_map/ppermute | solution.py:150
  58.9 46.6 %collective-permute-start.11 = (bf16[768,768]{1,0:T(8,128)(2,1)S(1)}, bf16[768,768]{1,0:T(8,128)(2,1)}, u32[]{:S(2)}, u32[]{:S(2)}) collective-permute-start(bf16[768,768]{1,0:T(8,128)(2,1)S(1)} %pad_maximum_fusion.refs_9_), channel_id=1, source_target_pairs={{0,16},{2,18},{4,20},{6,22},{8,24},{10,26},{12,28},{14,30},{16,0},... | collective-permute-start | bytes 3538952 | tf_op jit(solution)/shard_map/ppermute | solution.py:150
  60.4 39.5 %collective-permute-start.16 = (bf16[2,256,1024]{2,1,0:T(8,128)(2,1)S(1)}, bf16[2,256,1024]{2,1,0:T(8,128)(2,1)}, u32[]{:S(2)}, u32[]{:S(2)}) collective-permute-start(bf16[2,256,1024]{2,1,0:T(8,128)(2,1)S(1)} %copy-done.5), channel_id=1, source_target_pairs={{0,6},{2,4},{4,2},{6,0},{8,14},{10,12},{12,10},{14,8},{16,22},{18,... | collective-permute-start | bytes 3145736 | tf_op jit(solution)/shard_map/ppermute | solution.py:150
  61.9 40.6 %collective-permute-start.15 = (bf16[2,256,1024]{2,1,0:T(8,128)(2,1)S(1)}, bf16[2,256,1024]{2,1,0:T(8,128)(2,1)}, u32[]{:S(2)}, u32[]{:S(2)}) collective-permute-start(bf16[2,256,1024]{2,1,0:T(8,128)(2,1)S(1)} %copy-done.5), channel_id=1, source_target_pairs={{0,4},{2,6},{4,0},{6,2},{8,12},{10,14},{12,8},{14,10},{16,20},{18,... | collective-permute-start | bytes 3145736 | tf_op jit(solution)/shard_map/ppermute | solution.py:150
  83.5 22.0 %collective-permute-start.14 = (bf16[2,256,1024]{2,1,0:T(8,128)(2,1)S(1)}, bf16[2,256,1024]{2,1,0:T(8,128)(2,1)}, u32[]{:S(2)}, u32[]{:S(2)}) collective-permute-start(bf16[2,256,1024]{2,1,0:T(8,128)(2,1)S(1)} %collective-permute-done.13.refs_1_), channel_id=1, source_target_pairs={{0,1},{1,0},{2,3},{3,2},{4,5},{5,4},{6,7},{7,6},{8,9},{9,8},{10,11... | collective-permute-start | bytes 3145736 | tf_op jit(solution)/shard_map/ppermute | solution.py:150
  105.5 10.0 %collective-permute-start.17 = (bf16[2,256,1024]{2,1,0:T(8,128)(2,1)S(1)}, bf16[2,256,1024]{2,1,0:T(8,128)(2,1)S(1)}, u32[]{:S(2)}, u32[]{:S(2)}) collective-permute-start(bf16[2,256,1024]{2,1,0:T(8,128)(2,1)S(1)} %copy-done.5), channel_id=1, source_target_pairs={{0,1},{1,0},{2,3},{3,2},{4,5},{5,4},{6,7},{7,6},{8,9},{9,8},{10,11... | collective-permute-start | bytes 3145736 | tf_op jit(solution)/shard_map/ppermute | solution.py:150
  105.6 10.0 %collective-permute-start.18 = (bf16[2,256,1024]{2,1,0:T(8,128)(2,1)}, bf16[2,256,1024]{2,1,0:T(8,128)(2,1)S(1)}, u32[]{:S(2)}, u32[]{:S(2)}) collective-permute-start(bf16[2,256,1024]{2,1,0:T(8,128)(2,1)} %collective-permute-done.15.refs_2_), channel_id=1, source_target_pairs={{0,1},{1,0},{2,3},{3,2},{4,5},{5,4},{6,7},{7,6},{8,9},{9,8},{10,11... | collective-permute-start | bytes 3145736 | tf_op jit(solution)/shard_map/ppermute | solution.py:150
  106.1 9.5 %collective-permute-start.19 = (bf16[2,256,1024]{2,1,0:T(8,128)(2,1)}, bf16[2,256,1024]{2,1,0:T(8,128)(2,1)}, u32[]{:S(2)}, u32[]{:S(2)}) collective-permute-start(bf16[2,256,1024]{2,1,0:T(8,128)(2,1)} %collective-permute-done.16.refs_3_), channel_id=1, source_target_pairs={{0,1},{1,0},{2,3},{3,2},{4,5},{5,4},{6,7},{7,6},{8,9},{9,8},{10,11... | collective-permute-start | bytes 3145736 | tf_op jit(solution)/shard_map/ppermute | solution.py:150
  106.1 23.2 %collective-permute-start.21 = (bf16[768,384]{1,0:T(8,128)(2,1)}, bf16[768,384]{1,0:T(8,128)(2,1)}, u32[]{:S(2)}, u32[]{:S(2)}) collective-permute-start(bf16[768,384]{1,0:T(8,128)(2,1)} %get-tuple-element.219), channel_id=1, source_target_pairs={{8,16},{10,18},{12,20},{14,22},{16,8},{18,10},{20,12},{22,14},{9,1... | collective-permute-start | bytes 1769480 | tf_op jit(solution)/shard_map/ppermute | solution.py:323
  112.0 17.2 %collective-permute-start.20 = (bf16[768,384]{1,0:T(8,128)(2,1)}, bf16[768,384]{1,0:T(8,128)(2,1)}, u32[]{:S(2)}, u32[]{:S(2)}) collective-permute-start(bf16[768,384]{1,0:T(8,128)(2,1)} %get-tuple-element.273), channel_id=1, source_target_pairs={{8,0},{10,2},{12,4},{14,6},{16,24},{18,26},{20,28},{22,30},{9,1},{... | collective-permute-start | bytes 1769480 | tf_op jit(solution)/shard_map/ppermute | solution.py:326
  129.2 16.2 %collective-permute-start.25 = (bf16[768,384]{1,0:T(8,128)(2,1)}, bf16[768,384]{1,0:T(8,128)(2,1)S(1)}, u32[]{:S(2)}, u32[]{:S(2)}) collective-permute-start(bf16[768,384]{1,0:T(8,128)(2,1)} %get-tuple-element.238), channel_id=1, source_target_pairs={{8,0},{10,2},{12,4},{14,6},{16,24},{18,26},{20,28},{22,30},{9,1},{... | collective-permute-start | bytes 1769480 | tf_op jit(solution)/shard_map/ppermute | solution.py:326
  132.7 16.8 %collective-permute-start.26 = (bf16[768,384]{1,0:T(8,128)(2,1)}, bf16[768,384]{1,0:T(8,128)(2,1)S(1)}, u32[]{:S(2)}, u32[]{:S(2)}) collective-permute-start(bf16[768,384]{1,0:T(8,128)(2,1)} %get-tuple-element.239), channel_id=1, source_target_pairs={{8,16},{10,18},{12,20},{14,22},{16,8},{18,10},{20,12},{22,14},{9,1... | collective-permute-start | bytes 1769480 | tf_op jit(solution)/shard_map/ppermute | solution.py:323
  139.7 17.6 %collective-permute-start.22 = (bf16[256,384]{1,0:T(8,128)(2,1)}, bf16[256,384]{1,0:T(8,128)(2,1)S(1)}, u32[]{:S(2)}, u32[]{:S(2)}) collective-permute-start(bf16[256,384]{1,0:T(8,128)(2,1)} %get-tuple-element.235), channel_id=1, source_target_pairs={{0,2},{2,0},{4,6},{6,4},{8,10},{10,8},{12,14},{14,12},{16,18},{18,... | collective-permute-start | bytes 589832 | tf_op jit(solution)/shard_map/ppermute | solution.py:150
  140.3 18.5 %collective-permute-start.23 = (bf16[256,384]{1,0:T(8,128)(2,1)}, bf16[256,384]{1,0:T(8,128)(2,1)S(1)}, u32[]{:S(2)}, u32[]{:S(2)}) collective-permute-start(bf16[256,384]{1,0:T(8,128)(2,1)} %get-tuple-element.236), channel_id=1, source_target_pairs={{0,4},{2,6},{4,0},{6,2},{8,12},{10,14},{12,8},{14,10},{16,20},{18,... | collective-permute-start | bytes 589832 | tf_op jit(solution)/shard_map/ppermute | solution.py:150
  141.9 16.9 %collective-permute-start.24 = (bf16[256,384]{1,0:T(8,128)(2,1)}, bf16[256,384]{1,0:T(8,128)(2,1)S(1)}, u32[]{:S(2)}, u32[]{:S(2)}) collective-permute-start(bf16[256,384]{1,0:T(8,128)(2,1)} %get-tuple-element.237), channel_id=1, source_target_pairs={{0,6},{2,4},{4,2},{6,0},{8,14},{10,12},{12,10},{14,8},{16,22},{18,... | collective-permute-start | bytes 589832 | tf_op jit(solution)/shard_map/ppermute | solution.py:150
  157.4 8.7 %collective-permute-start.29 = (bf16[256,384]{1,0:T(8,128)(2,1)}, bf16[256,384]{1,0:T(8,128)(2,1)S(1)}, u32[]{:S(2)}, u32[]{:S(2)}) collective-permute-start(bf16[256,384]{1,0:T(8,128)(2,1)} %get-tuple-element.243), channel_id=1, source_target_pairs={{0,6},{2,4},{4,2},{6,0},{8,14},{10,12},{12,10},{14,8},{16,22},{18,... | collective-permute-start | bytes 589832 | tf_op jit(solution)/shard_map/ppermute | solution.py:150
  (24 other events, 210.9 us)

commit v19 on v18

--- a/solution.py
+++ b/solution.py
@@ -352,7 +352,7 @@
     w0, w1, w2, w3 = tie(*[group(w_out, r) for r in range(PLANE)])
     f0, n0 = far(w0), near(w0)
     both, before = box(plane_scan, k, v, rate, speed)
-    f0, n0, w0, w1, w2, w3, both, before = tie(f0, n0, w0, w1, w2, w3, both, before)
+    n0, f0, w0, w1, w2, w3, both, before = tie(n0, f0, w0, w1, w2, w3, both, before)
 
     arrived = [exchange(w, "ctx", r + 1) for r, w in enumerate((w1, w2, w3))]
     decay = jnp.exp(-speed * float(PLANE * rows))
@@ -362,36 +362,37 @@
     out0, mid0 = outward(f0), across(w0)
     gated = gated_conv(q, k, v, rate, residue, skip, before, ([last, earlier], spot))
     rest = jnp.concatenate(arrived)
-    gated, rest, out0, mid0 = tie(gated, rest, out0, mid0)
+    gated, rest, mid0, out0 = tie(gated, rest, mid0, out0)
 
     nr, fr = near(rest), far(rest)
     ours = [gated] + [exchange(gated, "ctx", r) for r in range(1, PLANE)]
     theirs_x = exchange(ours[1], "ch", 1)
-    half = cols // 2
-    restA, restB = rest[:, :half], rest[:, half:]
+    wide = 2 * cols // 3
+    restA, restB = rest[:, :wide], rest[:, wide:]
     fr, nr, rest, restA, restB, flags, places, theirs_x, *ours = tie(
         fr, nr, rest, restA, restB, flags, places, theirs_x, *ours
     )
 
-    outA, midA = outward(fr[:, :half]), across(restA)
+    outA, midA = outward(fr[:, :wide]), across(restA)
     theirs = [theirs_x if r == 1 else exchange(x, "ch", 1) for r, x in enumerate(ours)]
     blocks = [
         (0, None, [((w0,), 0), ((rest,), 0)]),
         (1, None, [((n0,), 0), ((nr,), 0)]),
         (2, None, [((f0,), 0), ((fr,), 0)]),
     ]
+    late, theirs[0] = tie(fr, theirs[0])
+    frB = late[:, wide:]
     (accs,) = product(flags, places, ours, theirs, blocks, None, 0, cols, jnp.float32)
-    frB = fr[:, half:]
     outA, midA, frB, restB, *accs = tie(outA, midA, frB, restB, *accs)
 
     outB, midB = outward(frB), across(restB)
 
-    def finish(first, out1, mid1):
+    def finish(first, width, out1, mid1):
         blocks = [(3, 4, [((out0, mid0), first), ((out1, mid1), 0)])]
-        (made,) = product(flags, places, ours, theirs, blocks, accs, first, half, jnp.bfloat16)
+        (made,) = product(flags, places, ours, theirs, blocks, accs, first, width, jnp.bfloat16)
         return [made[0]] + [exchange(made[r], "ctx", r) for r in range(1, PLANE)]
 
-    return assemble(places, [finish(0, outA, midA), finish(half, outB, midB)])
+    return assemble(places, [finish(0, wide, outA, midA), finish(wide, cols - wide, outB, midB)])
 
 
 def body(q, k, v, residue, rate, skip, w_out):
@@ -405,7 +406,7 @@
         and cores == 2
         and chan == 8 * chunk
         and chunk % LANES == 0
-        and feats % (2 * PLANE * LANES) == 0
+        and feats % (6 * PLANE * LANES) == 0
     )
     skip = skip.reshape(groups, LANES)
     if split:

time: 170 us -> 166 us (0.976)
  waiting for transfers between devices: 67.4 us -> 54.1 us
  starting transfers between devices: 49.6 us -> 60 us
    ppermute x22, waiting for transfers between devices: 56.4 us -> 44.8 us  [exchange(): return lax.ppermute(x, axis, [(i, i ^ flip) for i in range(count)])]
    ppermute x22, starting transfers between devices: 22.3 us -> 33.4 us  [exchange(): return lax.ppermute(x, axis, [(i, i ^ flip) for i in range(count)])]
    ppermute x3, waiting for transfers between devices: 2.11 us -> 0.01 us  [outward(): return lax.ppermute(x, 'ctx', [(i, i ^ PLANE) for i in middle])]
    unnamed x37 -> x39, local copies, waits for them, and re-layouts: 4.66 us -> 2.58 us
    ppermute x3, starting transfers between devices: 8.21 us -> 6.29 us  [outward(): return lax.ppermute(x, 'ctx', [(i, i ^ PLANE) for i in middle])]
    slice x2 -> x4, local copies, waits for them, and re-layouts: 3.53 us -> 5.08 us  [the longest x1 2.06 us: split_block(): outA, midA = (outward(fr[:, :wide]), across(restA))]
  transfers between devices with their start and end apart: 30 -> 30, of which waited for: 14 -> 14; matrix products, arithmetic and copies ran while one was open for 5% -> 6% of each run, Pallas kernels for 21% -> 21%
where the time goes in v19:
time: 166 us
  starting transfers between devices  60 us (36%)
  waiting for transfers between devices  54.1 us (33%)
  Pallas kernels  36 us (22%)
  local copies, waits for them, and re-layouts  10.9 us (7%)
  other arithmetic  4.54 us (3%)
    ppermute x22, waiting for transfers between devices, exchange(): return lax.ppermute(x, axis, [(i, i ^ flip) for i in range(count)])  44.8 us
    ppermute x22, starting transfers between devices, exchange(): return lax.ppermute(x, axis, [(i, i ^ flip) for i in range(count)])  33.4 us
    pallas_call x3, Pallas kernels, product(): pl.pallas_call(kernel, in_specs=[smem, smem] + [anywhere] * (2 * parts +...  21.8 us
    ppermute x3, starting transfers between devices, across(): return lax.ppermute(x, 'ctx', [(i, i ^ 3 * PLANE) for i in middle])  13.5 us
    pallas_call x1, Pallas kernels, gated_conv(): pl.pallas_call(conv_kernel, grid=(chan // width,), in_specs=[wide, wide,...  8.49 us
    ppermute x2, starting transfers between devices, shift_ctx(): return lax.ppermute(x, 'ctx', [(i, i + by) for i in range(count - by)])  6.85 us
    ppermute x3, starting transfers between devices, outward(): return lax.ppermute(x, 'ctx', [(i, i ^ PLANE) for i in middle])  6.29 us
    ppermute x2, waiting for transfers between devices, shift_ctx(): return lax.ppermute(x, 'ctx', [(i, i + by) for i in range(count - by)])  4.88 us
  transfers between devices with their start and end apart: 30, of which 14 were waited for; matrix products, arithmetic and copies ran while one was open for 6% of the time, Pallas kernels for 21%

profile of v19, /device:TPU:8, one launch (start us, length us, event | category | flops | bytes accessed | tf_op | source)
XLA Modules:
  0.0 165.9 jit_solution(16205020391881434140)
XLA Ops:
  0.0 2.6 %constant_dynamic-slice_fusion = (bf16[256,768]{1,0:T(8,128)(2,1)}, bf16[256,768]{1,0:T(8,128)(2,1)}, bf16[256,768]{1,0:T(8,128)(2,1)S(1)}, bf16[256,768]{1,0:T(8,128)(2,1)}) fusion(bf16[256,3072]{1,0:T(8,128)(2,1)} %param.15, s32[]{:T(128)S(6)} %select_n.84, s32[]{:T(128)S(6)} %select_n.82, s32[]{:T(128)S(6)} %select_n.81, s32[]{:T(128)S(6)} %select_n.83), kind=kLoop, calls=%fused_computation.5 | loop fusion | bytes 3145744 | tf_op jit(solution)/shard_map/dynamic_slice | solution.py:329
  2.6 3.0 %collective-permute-start.3 = (bf16[256,768]{1,0:T(8,128)(2,1)S(1)}, bf16[256,768]{1,0:T(8,128)(2,1)}, u32[]{:S(2)}, u32[]{:S(2)}) collective-permute-start(bf16[256,768]{1,0:T(8,128)(2,1)S(1)} %get-tuple-element.207.refs_8_), channel_id=1, source_target_pairs={{0,16},{2,18},{4,20},{6,22},{8,24},{10,26},{12,28},{14,30},{16,0},... | collective-permute-start | bytes 1179656 | tf_op jit(solution)/shard_map/ppermute | solution.py:150
  5.7 15.9 %while.14 = (s32[]{:T(128)}, f32[16,16,128]{2,1,0:T(8,128)}, f32[16,16,128]{2,1,0:T(8,128)}, s32[]{:T(128)}, pred[]{:T(512)}, /*index=5*/bf16[256,2048]{1,0:T(8,...) while((s32[]{:T(128)}, f32[16,16,128]{2,1,0:T(8,128)}, ...), condition=%wide.region_1.2_spmd, body=%wide.region_0.1_spmd.sunk | while | flops 17399808 | bytes 4456652 | solution.py:185
  5.7 4.0 %end_states.3 = f32[16,16,128]{2,1,0:T(8,128)} custom-call(bf16[256,2048]{1,0:T(8,128)(2,1)S(1)} %get-tuple-element.346.k_ref, bf16[256,2048]{1,0:T(8,128)(2,1)S(1)} %get-tuple-element.347.v_ref, f32[16,2048]{1,0:T(8,128)S(1)} %get-tuple-element.348.rate_ref), custom_call_target="tpu_custom_call" | custom-call | flops 16777216 | bytes 2097152 | tf_op jit(solution)/shard_map/while/body/end_states/pallas_call | solution.py:98
  11.2 3.7 %collective-permute-done = f32[16,16,128]{2,1,0:T(8,128)S(1)} collective-permute-done((f32[16,16,128]{2,1,0:T(8,128)}, f32[16,16,128]{2,1,0:T(8,128)S(1)}, u32[]{:S(2)}, u32[]{:S(2)}) %collective-permute-start) | collective-permute-done | bytes 131104 | tf_op jit(solution)/shard_map/while/body/ppermute | solution.py:150
  17.4 3.4 %collective-permute-done.1 = f32[16,16,128]{2,1,0:T(8,128)S(1)} collective-permute-done((f32[16,16,128]{2,1,0:T(8,128)S(1)}, f32[16,16,128]{2,1,0:T(8,128)S(1)}, u32[]{:S(2)}, u32[]{:S(2)}) %collective-permute-start.1) | collective-permute-done | bytes 131104 | tf_op jit(solution)/shard_map/while/body/ppermute | solution.py:150
  23.1 2.3 %collective-permute-start.4 = (f32[16,16,128]{2,1,0:T(8,128)}, f32[16,16,128]{2,1,0:T(8,128)S(1)}, u32[]{:S(2)}, u32[]{:S(2)}) collective-permute-start(f32[16,16,128]{2,1,0:T(8,128)} %get-tuple-element.200), channel_id=1, source_target_pairs={{0,8},{2,10},{4,12},{6,14},{8,16},{10,18},{12,20},{14,22},{16,24},... | collective-permute-start | bytes 393224 | tf_op jit(solution)/shard_map/ppermute | solution.py:145
  31.1 4.5 %collective-permute-start.5 = (f32[16,16,128]{2,1,0:T(8,128)S(1)}, f32[16,16,128]{2,1,0:T(8,128)S(1)}, u32[]{:S(2)}, u32[]{:S(2)}) collective-permute-start(f32[16,16,128]{2,1,0:T(8,128)S(1)} %multiply_add_fusion), channel_id=1, source_target_pairs={{0,16},{2,18},{4,20},{6,22},{8,24},{10,26},{12,28},{14,30},{1,17},... | collective-permute-start | bytes 393224 | tf_op jit(solution)/shard_map/ppermute | solution.py:145
  35.6 3.7 %collective-permute-done.5.refs_1_ = f32[16,16,128]{2,1,0:T(8,128)S(1)} collective-permute-done((f32[16,16,128]{2,1,0:T(8,128)S(1)}, f32[16,16,128]{2,1,0:T(8,128)S(1)}, u32[]{:S(2)}, u32[]{:S(2)}) %collective-permute-start.5) | collective-permute-done | bytes 131104 | tf_op jit(solution)/shard_map/ppermute | solution.py:145
  40.7 6.6 %collective-permute-start.9 = (bf16[256,768]{1,0:T(8,128)(2,1)}, bf16[256,768]{1,0:T(8,128)(2,1)S(1)}, u32[]{:S(2)}, u32[]{:S(2)}) collective-permute-start(bf16[256,768]{1,0:T(8,128)(2,1)} %copy-done.14), channel_id=1, source_target_pairs={{8,16},{10,18},{12,20},{14,22},{16,8},{18,10},{20,12},{22,14},{9,1... | collective-permute-start | bytes 1179656 | tf_op jit(solution)/shard_map/ppermute | solution.py:323
  47.3 8.5 %gated_conv.1.refs_0_ = bf16[2,256,1024]{2,1,0:T(8,128)(2,1)} custom-call(bf16[256,2048]{1,0:T(8,128)(2,1)} %q_ref.1, bf16[256,2048]{1,0:T(8,128)(2,1)S(1)} %get-tuple-element.394, bf16[256,2048]{1,0:T(8,128)(2,1)S(1)} %get-tuple-element.395, f32[16,2048]{1,0:T(8,128)S(1)} %get-tuple-element.404, f32[16,2048]{1,0:T(8,128)} %residue_ref.1, ...), custom_call_target="tpu_custom_call" | custom-call | flops 33554432 | bytes 4194304 | tf_op jit(solution)/shard_map/gated_conv/pallas_call | solution.py:128
  57.2 10.7 %collective-permute-start.13 = (bf16[2,256,1024]{2,1,0:T(8,128)(2,1)S(1)}, bf16[2,256,1024]{2,1,0:T(8,128)(2,1)}, u32[]{:S(2)}, u32[]{:S(2)}) collective-permute-start(bf16[2,256,1024]{2,1,0:T(8,128)(2,1)S(1)} %copy-done.5), channel_id=1, source_target_pairs={{0,2},{2,0},{4,6},{6,4},{8,10},{10,8},{12,14},{14,12},{16,18},{18,... | collective-permute-start | bytes 3145736 | tf_op jit(solution)/shard_map/ppermute | solution.py:150
  67.9 3.8 %collective-permute-start.12 = (bf16[768,768]{1,0:T(8,128)(2,1)S(1)}, bf16[768,768]{1,0:T(8,128)(2,1)}, u32[]{:S(2)}, u32[]{:S(2)}) collective-permute-start(bf16[768,768]{1,0:T(8,128)(2,1)S(1)} %pad_maximum_fusion.refs_9_), channel_id=1, source_target_pairs={{0,8},{2,10},{4,12},{6,14},{8,0},{10,2},{12,4},{14,6},{16,24},{18,... | collective-permute-start | bytes 3538952 | tf_op jit(solution)/shard_map/ppermute | solution.py:150
  73.3 14.2 %collective-permute-done.13.refs_1_ = bf16[2,256,1024]{2,1,0:T(8,128)(2,1)} collective-permute-done((bf16[2,256,1024]{2,1,0:T(8,128)(2,1)S(1)}, bf16[2,256,1024]{2,1,0:T(8,128)(2,1)}, u32[]{:S(2)}, u32[]{:S(2)}) %collective-permute-start.13) | collective-permute-done | bytes 1048608 | tf_op jit(solution)/shard_map/ppermute | solution.py:150
  90.4 11.7 %collective-permute-done.15.refs_2_ = bf16[2,256,1024]{2,1,0:T(8,128)(2,1)} collective-permute-done((bf16[2,256,1024]{2,1,0:T(8,128)(2,1)S(1)}, bf16[2,256,1024]{2,1,0:T(8,128)(2,1)}, u32[]{:S(2)}, u32[]{:S(2)}) %collective-permute-start.15) | collective-permute-done | bytes 1048608 | tf_op jit(solution)/shard_map/ppermute | solution.py:150
  105.8 2.1 %slice.14 = bf16[768,512]{1,0:T(8,128)(2,1)} slice(bf16[768,768]{1,0:T(8,128)(2,1)} %collective-permute-done.11.refs_13_), slice={[0:768], [0:512]} | slice | bytes 1572864 | tf_op jit(solution)/shard_map/slice | solution.py:376
  107.9 3.7 %collective-permute-start.20 = (bf16[768,512]{1,0:T(8,128)(2,1)}, bf16[768,512]{1,0:T(8,128)(2,1)}, u32[]{:S(2)}, u32[]{:S(2)}) collective-permute-start(bf16[768,512]{1,0:T(8,128)(2,1)} %slice.14), channel_id=1, source_target_pairs={{8,0},{10,2},{12,4},{14,6},{16,24},{18,26},{20,28},{22,30},{9,1},{... | collective-permute-start | bytes 2359304 | tf_op jit(solution)/shard_map/ppermute | solution.py:326
  111.6 3.5 %collective-permute-start.21 = (bf16[768,512]{1,0:T(8,128)(2,1)}, bf16[768,512]{1,0:T(8,128)(2,1)S(1)}, u32[]{:S(2)}, u32[]{:S(2)}) collective-permute-start(bf16[768,512]{1,0:T(8,128)(2,1)} %slice.12), channel_id=1, source_target_pairs={{8,16},{10,18},{12,20},{14,22},{16,8},{18,10},{20,12},{22,14},{9,1... | collective-permute-start | bytes 2359304 | tf_op jit(solution)/shard_map/ppermute | solution.py:323
  116.4 12.5 %product.3 = (f32[256,768]{1,0:T(8,128)}, f32[256,768]{1,0:T(8,128)}, f32[256,768]{1,0:T(8,128)}, f32[256,768]{1,0:T(8,128)}) custom-call(s32[5]{0:T(128)} %stack.36.flag_ref, s32[4]{0:T(128)} %pad_add_fusion.place_ref, bf16[2,256,1024]{2,1,0:T(8,128)(2,1)} %gated_conv.1.refs_0_, bf16[2,256,1024]{2,1,0:T(8,128)(2,1)} %collective-permute-done.13.refs_1_, ...), custom_call_target="tpu_custom_call" | custom-call | flops 4831838208 | bytes 11010048 | tf_op jit(solution)/shard_map/product/pallas_call | solution.py:247
  129.0 4.4 %collective-permute-done.21.refs_11_ = bf16[768,512]{1,0:T(8,128)(2,1)S(1)} collective-permute-done((bf16[768,512]{1,0:T(8,128)(2,1)}, bf16[768,512]{1,0:T(8,128)(2,1)S(1)}, u32[]{:S(2)}, u32[]{:S(2)}) %collective-permute-start.21) | collective-permute-done | bytes 786464 | tf_op jit(solution)/shard_map/ppermute | solution.py:323
  134.7 3.5 %collective-permute-start.26 = (bf16[768,256]{1,0:T(8,128)(2,1)S(1)}, bf16[768,256]{1,0:T(8,128)(2,1)S(1)}, u32[]{:S(2)}, u32[]{:S(2)}) collective-permute-start(bf16[768,256]{1,0:T(8,128)(2,1)S(1)} %copy-done.13), channel_id=1, source_target_pairs={{8,16},{10,18},{12,20},{14,22},{16,8},{18,10},{20,12},{22,14},{9,1... | collective-permute-start | bytes 1179656 | tf_op jit(solution)/shard_map/ppermute | solution.py:323
  138.2 5.2 %product.4 = (bf16[256,512]{1,0:T(8,128)(2,1)}, bf16[256,512]{1,0:T(8,128)(2,1)}, bf16[256,512]{1,0:T(8,128)(2,1)}, bf16[256,512]{1,0:T(8,128)(2,1)}) custom-call(s32[5]{0:T(128)} %stack.36.flag_ref, s32[4]{0:T(128)} %pad_add_fusion.place_ref, bf16[2,256,1024]{2,1,0:T(8,128)(2,1)} %gated_conv.1.refs_0_, ...), custom_call_target="tpu_custom_call" | custom-call | flops 1073741824 | bytes 3145728 | tf_op jit(solution)/shard_map/product/pallas_call | solution.py:247
  148.5 4.1 %product.5 = (bf16[256,256]{1,0:T(8,128)(2,1)}, bf16[256,256]{1,0:T(8,128)(2,1)}, bf16[256,256]{1,0:T(8,128)(2,1)}, bf16[256,256]{1,0:T(8,128)(2,1)}) custom-call(s32[5]{0:T(128)} %stack.36.flag_ref, s32[4]{0:T(128)} %pad_add_fusion.place_ref, bf16[2,256,1024]{2,1,0:T(8,128)(2,1)} %gated_conv.1.refs_0_, ...), custom_call_target="tpu_custom_call" | custom-call | flops 536870912 | bytes 2621440 | tf_op jit(solution)/shard_map/product/pallas_call | solution.py:247
  156.1 3.4 %collective-permute-done.24.refs_3_ = bf16[256,512]{1,0:T(8,128)(2,1)S(1)} collective-permute-done((bf16[256,512]{1,0:T(8,128)(2,1)}, bf16[256,512]{1,0:T(8,128)(2,1)S(1)}, u32[]{:S(2)}, u32[]{:S(2)}) %collective-permute-start.24) | collective-permute-done | bytes 262176 | tf_op jit(solution)/shard_map/ppermute | solution.py:150
  (94 shorter events, 40.5 us)
Async XLA Ops:
  2.6 19.0 %collective-permute-start.2 = (bf16[256,768]{1,0:T(8,128)(2,1)S(1)}, bf16[256,768]{1,0:T(8,128)(2,1)S(1)}, u32[]{:S(2)}, u32[]{:S(2)}) collective-permute-start(bf16[256,768]{1,0:T(8,128)(2,1)S(1)} %get-tuple-element.207.refs_8_), channel_id=1, source_target_pairs={{0,8},{2,10},{4,12},{6,14},{8,0},{10,2},{12,4},{14,6},{16,24},{18,... | collective-permute-start | bytes 1179656 | tf_op jit(solution)/shard_map/ppermute | solution.py:150
  2.6 20.5 %collective-permute-start.3 = (bf16[256,768]{1,0:T(8,128)(2,1)S(1)}, bf16[256,768]{1,0:T(8,128)(2,1)}, u32[]{:S(2)}, u32[]{:S(2)}) collective-permute-start(bf16[256,768]{1,0:T(8,128)(2,1)S(1)} %get-tuple-element.207.refs_8_), channel_id=1, source_target_pairs={{0,16},{2,18},{4,20},{6,22},{8,24},{10,26},{12,28},{14,30},{16,0},... | collective-permute-start | bytes 1179656 | tf_op jit(solution)/shard_map/ppermute | solution.py:150
  25.4 30.3 %collective-permute-start.6 = (bf16[256,768]{1,0:T(8,128)(2,1)}, bf16[256,768]{1,0:T(8,128)(2,1)S(1)}, u32[]{:S(2)}, u32[]{:S(2)}) collective-permute-start(bf16[256,768]{1,0:T(8,128)(2,1)} %get-tuple-element.204), channel_id=1, source_target_pairs={{0,2},{2,0},{4,6},{6,4},{8,10},{10,8},{12,14},{14,12},{16,18},{18,... | collective-permute-start | bytes 1179656 | tf_op jit(solution)/shard_map/ppermute | solution.py:150
  27.0 28.8 %collective-permute-start.7 = (bf16[256,768]{1,0:T(8,128)(2,1)}, bf16[256,768]{1,0:T(8,128)(2,1)}, u32[]{:S(2)}, u32[]{:S(2)}) collective-permute-start(bf16[256,768]{1,0:T(8,128)(2,1)} %get-tuple-element.205), channel_id=1, source_target_pairs={{0,4},{2,6},{4,0},{6,2},{8,12},{10,14},{12,8},{14,10},{16,20},{18,... | collective-permute-start | bytes 1179656 | tf_op jit(solution)/shard_map/ppermute | solution.py:150
  28.5 27.3 %collective-permute-start.8 = (bf16[256,768]{1,0:T(8,128)(2,1)}, bf16[256,768]{1,0:T(8,128)(2,1)}, u32[]{:S(2)}, u32[]{:S(2)}) collective-permute-start(bf16[256,768]{1,0:T(8,128)(2,1)} %get-tuple-element.206), channel_id=1, source_target_pairs={{0,6},{2,4},{4,2},{6,0},{8,14},{10,12},{12,10},{14,8},{16,22},{18,... | collective-permute-start | bytes 1179656 | tf_op jit(solution)/shard_map/ppermute | solution.py:150
  39.4 17.7 %collective-permute-start.10 = (bf16[256,768]{1,0:T(8,128)(2,1)}, bf16[256,768]{1,0:T(8,128)(2,1)S(1)}, u32[]{:S(2)}, u32[]{:S(2)}) collective-permute-start(bf16[256,768]{1,0:T(8,128)(2,1)} %collective-permute-done.3.refs_12_), channel_id=1, source_target_pairs={{8,0},{10,2},{12,4},{14,6},{16,24},{18,26},{20,28},{22,30},{9,1},{... | collective-permute-start | bytes 1179656 | tf_op jit(solution)/shard_map/ppermute | solution.py:326
  40.7 16.4 %collective-permute-start.9 = (bf16[256,768]{1,0:T(8,128)(2,1)}, bf16[256,768]{1,0:T(8,128)(2,1)S(1)}, u32[]{:S(2)}, u32[]{:S(2)}) collective-permute-start(bf16[256,768]{1,0:T(8,128)(2,1)} %copy-done.14), channel_id=1, source_target_pairs={{8,16},{10,18},{12,20},{14,22},{16,8},{18,10},{20,12},{22,14},{9,1... | collective-permute-start | bytes 1179656 | tf_op jit(solution)/shard_map/ppermute | solution.py:323
  57.2 30.3 %collective-permute-start.13 = (bf16[2,256,1024]{2,1,0:T(8,128)(2,1)S(1)}, bf16[2,256,1024]{2,1,0:T(8,128)(2,1)}, u32[]{:S(2)}, u32[]{:S(2)}) collective-permute-start(bf16[2,256,1024]{2,1,0:T(8,128)(2,1)S(1)} %copy-done.5), channel_id=1, source_target_pairs={{0,2},{2,0},{4,6},{6,4},{8,10},{10,8},{12,14},{14,12},{16,18},{18,... | collective-permute-start | bytes 3145736 | tf_op jit(solution)/shard_map/ppermute | solution.py:150
  67.9 35.4 %collective-permute-start.11 = (bf16[768,768]{1,0:T(8,128)(2,1)S(1)}, bf16[768,768]{1,0:T(8,128)(2,1)}, u32[]{:S(2)}, u32[]{:S(2)}) collective-permute-start(bf16[768,768]{1,0:T(8,128)(2,1)S(1)} %pad_maximum_fusion.refs_9_), channel_id=1, source_target_pairs={{0,16},{2,18},{4,20},{6,22},{8,24},{10,26},{12,28},{14,30},{16,0},... | collective-permute-start | bytes 3538952 | tf_op jit(solution)/shard_map/ppermute | solution.py:150
  67.9 37.4 %collective-permute-start.12 = (bf16[768,768]{1,0:T(8,128)(2,1)S(1)}, bf16[768,768]{1,0:T(8,128)(2,1)}, u32[]{:S(2)}, u32[]{:S(2)}) collective-permute-start(bf16[768,768]{1,0:T(8,128)(2,1)S(1)} %pad_maximum_fusion.refs_9_), channel_id=1, source_target_pairs={{0,8},{2,10},{4,12},{6,14},{8,0},{10,2},{12,4},{14,6},{16,24},{18,... | collective-permute-start | bytes 3538952 | tf_op jit(solution)/shard_map/ppermute | solution.py:150
  71.8 30.3 %collective-permute-start.15 = (bf16[2,256,1024]{2,1,0:T(8,128)(2,1)S(1)}, bf16[2,256,1024]{2,1,0:T(8,128)(2,1)}, u32[]{:S(2)}, u32[]{:S(2)}) collective-permute-start(bf16[2,256,1024]{2,1,0:T(8,128)(2,1)S(1)} %copy-done.5), channel_id=1, source_target_pairs={{0,4},{2,6},{4,0},{6,2},{8,12},{10,14},{12,8},{14,10},{16,20},{18,... | collective-permute-start | bytes 3145736 | tf_op jit(solution)/shard_map/ppermute | solution.py:150
  73.3 28.8 %collective-permute-start.16 = (bf16[2,256,1024]{2,1,0:T(8,128)(2,1)S(1)}, bf16[2,256,1024]{2,1,0:T(8,128)(2,1)}, u32[]{:S(2)}, u32[]{:S(2)}) collective-permute-start(bf16[2,256,1024]{2,1,0:T(8,128)(2,1)S(1)} %copy-done.5), channel_id=1, source_target_pairs={{0,6},{2,4},{4,2},{6,0},{8,14},{10,12},{12,10},{14,8},{16,22},{18,... | collective-permute-start | bytes 3145736 | tf_op jit(solution)/shard_map/ppermute | solution.py:150
  87.5 17.8 %collective-permute-start.14 = (bf16[2,256,1024]{2,1,0:T(8,128)(2,1)}, bf16[2,256,1024]{2,1,0:T(8,128)(2,1)}, u32[]{:S(2)}, u32[]{:S(2)}) collective-permute-start(bf16[2,256,1024]{2,1,0:T(8,128)(2,1)} %collective-permute-done.13.refs_1_), channel_id=1, source_target_pairs={{0,1},{1,0},{2,3},{3,2},{4,5},{5,4},{6,7},{7,6},{8,9},{9,8},{10,11... | collective-permute-start | bytes 3145736 | tf_op jit(solution)/shard_map/ppermute | solution.py:150
  105.3 9.7 %collective-permute-start.17 = (bf16[2,256,1024]{2,1,0:T(8,128)(2,1)S(1)}, bf16[2,256,1024]{2,1,0:T(8,128)(2,1)S(1)}, u32[]{:S(2)}, u32[]{:S(2)}) collective-permute-start(bf16[2,256,1024]{2,1,0:T(8,128)(2,1)S(1)} %copy-done.5), channel_id=1, source_target_pairs={{0,1},{1,0},{2,3},{3,2},{4,5},{5,4},{6,7},{7,6},{8,9},{9,8},{10,11... | collective-permute-start | bytes 3145736 | tf_op jit(solution)/shard_map/ppermute | solution.py:150
  105.3 11.1 %collective-permute-start.18 = (bf16[2,256,1024]{2,1,0:T(8,128)(2,1)}, bf16[2,256,1024]{2,1,0:T(8,128)(2,1)}, u32[]{:S(2)}, u32[]{:S(2)}) collective-permute-start(bf16[2,256,1024]{2,1,0:T(8,128)(2,1)} %collective-permute-done.15.refs_2_), channel_id=1, source_target_pairs={{0,1},{1,0},{2,3},{3,2},{4,5},{5,4},{6,7},{7,6},{8,9},{9,8},{10,11... | collective-permute-start | bytes 3145736 | tf_op jit(solution)/shard_map/ppermute | solution.py:150
  105.8 10.6 %collective-permute-start.19 = (bf16[2,256,1024]{2,1,0:T(8,128)(2,1)}, bf16[2,256,1024]{2,1,0:T(8,128)(2,1)}, u32[]{:S(2)}, u32[]{:S(2)}) collective-permute-start(bf16[2,256,1024]{2,1,0:T(8,128)(2,1)} %collective-permute-done.16.refs_3_), channel_id=1, source_target_pairs={{0,1},{1,0},{2,3},{3,2},{4,5},{5,4},{6,7},{7,6},{8,9},{9,8},{10,11... | collective-permute-start | bytes 3145736 | tf_op jit(solution)/shard_map/ppermute | solution.py:150
  107.9 21.1 %collective-permute-start.20 = (bf16[768,512]{1,0:T(8,128)(2,1)}, bf16[768,512]{1,0:T(8,128)(2,1)}, u32[]{:S(2)}, u32[]{:S(2)}) collective-permute-start(bf16[768,512]{1,0:T(8,128)(2,1)} %slice.14), channel_id=1, source_target_pairs={{8,0},{10,2},{12,4},{14,6},{16,24},{18,26},{20,28},{22,30},{9,1},{... | collective-permute-start | bytes 2359304 | tf_op jit(solution)/shard_map/ppermute | solution.py:326
  111.6 21.8 %collective-permute-start.21 = (bf16[768,512]{1,0:T(8,128)(2,1)}, bf16[768,512]{1,0:T(8,128)(2,1)S(1)}, u32[]{:S(2)}, u32[]{:S(2)}) collective-permute-start(bf16[768,512]{1,0:T(8,128)(2,1)} %slice.12), channel_id=1, source_target_pairs={{8,16},{10,18},{12,20},{14,22},{16,8},{18,10},{20,12},{22,14},{9,1... | collective-permute-start | bytes 2359304 | tf_op jit(solution)/shard_map/ppermute | solution.py:323
  133.4 13.6 %collective-permute-start.25 = (bf16[768,256]{1,0:T(8,128)(2,1)S(1)}, bf16[768,256]{1,0:T(8,128)(2,1)S(1)}, u32[]{:S(2)}, u32[]{:S(2)}) collective-permute-start(bf16[768,256]{1,0:T(8,128)(2,1)S(1)} %slice.15), channel_id=1, source_target_pairs={{8,0},{10,2},{12,4},{14,6},{16,24},{18,26},{20,28},{22,30},{9,1},{... | collective-permute-start | bytes 1179656 | tf_op jit(solution)/shard_map/ppermute | solution.py:326
  134.7 12.3 %collective-permute-start.26 = (bf16[768,256]{1,0:T(8,128)(2,1)S(1)}, bf16[768,256]{1,0:T(8,128)(2,1)S(1)}, u32[]{:S(2)}, u32[]{:S(2)}) collective-permute-start(bf16[768,256]{1,0:T(8,128)(2,1)S(1)} %copy-done.13), channel_id=1, source_target_pairs={{8,16},{10,18},{12,20},{14,22},{16,8},{18,10},{20,12},{22,14},{9,1... | collective-permute-start | bytes 1179656 | tf_op jit(solution)/shard_map/ppermute | solution.py:323
  143.4 11.8 %collective-permute-start.22 = (bf16[256,512]{1,0:T(8,128)(2,1)}, bf16[256,512]{1,0:T(8,128)(2,1)S(1)}, u32[]{:S(2)}, u32[]{:S(2)}) collective-permute-start(bf16[256,512]{1,0:T(8,128)(2,1)} %get-tuple-element.239), channel_id=1, source_target_pairs={{0,2},{2,0},{4,6},{6,4},{8,10},{10,8},{12,14},{14,12},{16,18},{18,... | collective-permute-start | bytes 786440 | tf_op jit(solution)/shard_map/ppermute | solution.py:150
  144.5 11.6 %collective-permute-start.23 = (bf16[256,512]{1,0:T(8,128)(2,1)}, bf16[256,512]{1,0:T(8,128)(2,1)S(1)}, u32[]{:S(2)}, u32[]{:S(2)}) collective-permute-start(bf16[256,512]{1,0:T(8,128)(2,1)} %get-tuple-element.240), channel_id=1, source_target_pairs={{0,4},{2,6},{4,0},{6,2},{8,12},{10,14},{12,8},{14,10},{16,20},{18,... | collective-permute-start | bytes 786440 | tf_op jit(solution)/shard_map/ppermute | solution.py:150
  146.0 13.5 %collective-permute-start.24 = (bf16[256,512]{1,0:T(8,128)(2,1)}, bf16[256,512]{1,0:T(8,128)(2,1)S(1)}, u32[]{:S(2)}, u32[]{:S(2)}) collective-permute-start(bf16[256,512]{1,0:T(8,128)(2,1)} %get-tuple-element.241), channel_id=1, source_target_pairs={{0,6},{2,4},{4,2},{6,0},{8,14},{10,12},{12,10},{14,8},{16,22},{18,... | collective-permute-start | bytes 786440 | tf_op jit(solution)/shard_map/ppermute | solution.py:150
  153.7 8.4 %collective-permute-start.28 = (bf16[256,256]{1,0:T(8,128)(2,1)}, bf16[256,256]{1,0:T(8,128)(2,1)S(1)}, u32[]{:S(2)}, u32[]{:S(2)}) collective-permute-start(bf16[256,256]{1,0:T(8,128)(2,1)} %get-tuple-element.246), channel_id=1, source_target_pairs={{0,4},{2,6},{4,0},{6,2},{8,12},{10,14},{12,8},{14,10},{16,20},{18,... | collective-permute-start | bytes 393224 | tf_op jit(solution)/shard_map/ppermute | solution.py:150
  (25 other events, 319.6 us)

commit v20 on v19

--- a/solution.py
+++ b/solution.py
@@ -362,19 +362,17 @@
     out0, mid0 = outward(f0), across(w0)
     gated = gated_conv(q, k, v, rate, residue, skip, before, ([last, earlier], spot))
     rest = jnp.concatenate(arrived)
-    gated, rest, mid0, out0 = tie(gated, rest, mid0, out0)
 
     nr, fr = near(rest), far(rest)
     ours = [gated] + [exchange(gated, "ctx", r) for r in range(1, PLANE)]
-    theirs_x = exchange(ours[1], "ch", 1)
     wide = 2 * cols // 3
     restA, restB = rest[:, :wide], rest[:, wide:]
-    fr, nr, rest, restA, restB, flags, places, theirs_x, *ours = tie(
-        fr, nr, rest, restA, restB, flags, places, theirs_x, *ours
+    fr, nr, rest, restA, restB, mid0, out0, flags, places, *ours = tie(
+        fr, nr, rest, restA, restB, mid0, out0, flags, places, *ours
     )
 
     outA, midA = outward(fr[:, :wide]), across(restA)
-    theirs = [theirs_x if r == 1 else exchange(x, "ch", 1) for r, x in enumerate(ours)]
+    theirs = [exchange(x, "ch", 1) for x in ours]
     blocks = [
         (0, None, [((w0,), 0), ((rest,), 0)]),
         (1, None, [((n0,), 0), ((nr,), 0)]),

time: 166 us -> 171 us (1.030)
  starting transfers between devices: 60 us -> 48 us
  waiting for transfers between devices: 54.1 us -> 65.9 us
  local copies, waits for them, and re-layouts: 10.9 us -> 16.9 us
    ppermute x3, waiting for transfers between devices: 4.4 us -> 20 us  [across(): return lax.ppermute(x, 'ctx', [(i, i ^ 3 * PLANE) for i in middle])]
    ppermute x22, starting transfers between devices: 33.4 us -> 27.1 us  [exchange(): return lax.ppermute(x, axis, [(i, i ^ flip) for i in range(count)])]
    ppermute x22, waiting for transfers between devices: 44.8 us -> 39.7 us  [exchange(): return lax.ppermute(x, axis, [(i, i ^ flip) for i in range(count)])]
    ppermute x3, starting transfers between devices: 13.5 us -> 9.95 us  [across(): return lax.ppermute(x, 'ctx', [(i, i ^ 3 * PLANE) for i in middle])]
    unnamed x39 -> x43, local copies, waits for them, and re-layouts: 2.58 us -> 5.96 us
    ppermute x3, starting transfers between devices: 6.29 us -> 3.94 us  [outward(): return lax.ppermute(x, 'ctx', [(i, i ^ PLANE) for i in middle])]
  transfers between devices with their start and end apart: 30 -> 30, of which waited for: 14 -> 14; matrix products, arithmetic and copies ran while one was open for 6% -> 8% of each run, Pallas kernels for 21% -> 20%
where the time goes in v20:
time: 171 us; the launch traced here: 170 us
  waiting for transfers between devices  65.9 us (39%)
  starting transfers between devices  48 us (28%)
  Pallas kernels  35.8 us (21%)
  local copies, waits for them, and re-layouts  16.9 us (10%)
  other arithmetic  3.36 us (2%)
    ppermute x22, waiting for transfers between devices, exchange(): return lax.ppermute(x, axis, [(i, i ^ flip) for i in range(count)])  39.7 us
    ppermute x22, starting transfers between devices, exchange(): return lax.ppermute(x, axis, [(i, i ^ flip) for i in range(count)])  27.1 us
    pallas_call x3, Pallas kernels, product(): pl.pallas_call(kernel, in_specs=[smem, smem] + [anywhere] * (2 * parts +...  21.7 us
    ppermute x3, waiting for transfers between devices, across(): return lax.ppermute(x, 'ctx', [(i, i ^ 3 * PLANE) for i in middle])  20 us
    ppermute x3, starting transfers between devices, across(): return lax.ppermute(x, 'ctx', [(i, i ^ 3 * PLANE) for i in middle])  9.95 us
    pallas_call x1, Pallas kernels, gated_conv(): pl.pallas_call(conv_kernel, grid=(chan // width,), in_specs=[wide, wide,...  8.45 us
    ppermute x2, starting transfers between devices, shift_ctx(): return lax.ppermute(x, 'ctx', [(i, i + by) for i in range(count - by)])  6.98 us
    ppermute x2, waiting for transfers between devices, shift_ctx(): return lax.ppermute(x, 'ctx', [(i, i + by) for i in range(count - by)])  6.19 us
  transfers between devices with their start and end apart: 30, of which 14 were waited for; matrix products, arithmetic and copies ran while one was open for 8% of the time, Pallas kernels for 20%

profile of v20, /device:TPU:8, one launch (start us, length us, event | category | flops | bytes accessed | tf_op | source)
XLA Modules:
  0.0 170.3 jit_solution(10222544517787523092)
XLA Ops:
  0.0 2.6 %constant_dynamic-slice_fusion = (bf16[256,768]{1,0:T(8,128)(2,1)}, bf16[256,768]{1,0:T(8,128)(2,1)}, bf16[256,768]{1,0:T(8,128)(2,1)S(1)}, bf16[256,768]{1,0:T(8,128)(2,1)}) fusion(bf16[256,3072]{1,0:T(8,128)(2,1)} %param.15, s32[]{:T(128)S(6)} %select_n.84, s32[]{:T(128)S(6)} %select_n.82, s32[]{:T(128)S(6)} %select_n.81, s32[]{:T(128)S(6)} %select_n.83), kind=kLoop, calls=%fused_computation.7 | loop fusion | bytes 3145744 | tf_op jit(solution)/shard_map/dynamic_slice | solution.py:329
  2.6 3.0 %collective-permute-start.3 = (bf16[256,768]{1,0:T(8,128)(2,1)S(1)}, bf16[256,768]{1,0:T(8,128)(2,1)}, u32[]{:S(2)}, u32[]{:S(2)}) collective-permute-start(bf16[256,768]{1,0:T(8,128)(2,1)S(1)} %get-tuple-element.202.refs_8_), channel_id=1, source_target_pairs={{0,16},{2,18},{4,20},{6,22},{8,24},{10,26},{12,28},{14,30},{16,0},... | collective-permute-start | bytes 1179656 | tf_op jit(solution)/shard_map/ppermute | solution.py:150
  5.7 15.9 %while.14 = (s32[]{:T(128)}, f32[16,16,128]{2,1,0:T(8,128)}, f32[16,16,128]{2,1,0:T(8,128)}, s32[]{:T(128)}, pred[]{:T(512)}, /*index=5*/bf16[256,2048]{1,0:T(8,...) while((s32[]{:T(128)}, f32[16,16,128]{2,1,0:T(8,128)}, ...), condition=%wide.region_1.2_spmd, body=%wide.region_0.1_spmd.sunk | while | flops 17399808 | bytes 4456652 | solution.py:185
  5.7 4.0 %end_states.3 = f32[16,16,128]{2,1,0:T(8,128)} custom-call(bf16[256,2048]{1,0:T(8,128)(2,1)S(1)} %get-tuple-element.340.k_ref, bf16[256,2048]{1,0:T(8,128)(2,1)S(1)} %get-tuple-element.341.v_ref, f32[16,2048]{1,0:T(8,128)S(1)} %get-tuple-element.342.rate_ref), custom_call_target="tpu_custom_call" | custom-call | flops 16777216 | bytes 2097152 | tf_op jit(solution)/shard_map/while/body/end_states/pallas_call | solution.py:98
  11.1 3.7 %collective-permute-done = f32[16,16,128]{2,1,0:T(8,128)S(1)} collective-permute-done((f32[16,16,128]{2,1,0:T(8,128)}, f32[16,16,128]{2,1,0:T(8,128)S(1)}, u32[]{:S(2)}, u32[]{:S(2)}) %collective-permute-start) | collective-permute-done | bytes 131104 | tf_op jit(solution)/shard_map/while/body/ppermute | solution.py:150
  17.4 3.4 %collective-permute-done.1 = f32[16,16,128]{2,1,0:T(8,128)S(1)} collective-permute-done((f32[16,16,128]{2,1,0:T(8,128)S(1)}, f32[16,16,128]{2,1,0:T(8,128)S(1)}, u32[]{:S(2)}, u32[]{:S(2)}) %collective-permute-start.1) | collective-permute-done | bytes 131104 | tf_op jit(solution)/shard_map/while/body/ppermute | solution.py:150
  23.1 2.3 %collective-permute-start.9 = (f32[16,16,128]{2,1,0:T(8,128)}, f32[16,16,128]{2,1,0:T(8,128)S(1)}, u32[]{:S(2)}, u32[]{:S(2)}) collective-permute-start(f32[16,16,128]{2,1,0:T(8,128)} %get-tuple-element.201), channel_id=1, source_target_pairs={{0,8},{2,10},{4,12},{6,14},{8,16},{10,18},{12,20},{14,22},{16,24},... | collective-permute-start | bytes 393224 | tf_op jit(solution)/shard_map/ppermute | solution.py:145
  31.1 4.6 %collective-permute-start.10 = (f32[16,16,128]{2,1,0:T(8,128)S(1)}, f32[16,16,128]{2,1,0:T(8,128)S(1)}, u32[]{:S(2)}, u32[]{:S(2)}) collective-permute-start(f32[16,16,128]{2,1,0:T(8,128)S(1)} %multiply_add_fusion), channel_id=1, source_target_pairs={{0,16},{2,18},{4,20},{6,22},{8,24},{10,26},{12,28},{14,30},{1,17},... | collective-permute-start | bytes 393224 | tf_op jit(solution)/shard_map/ppermute | solution.py:145
  35.8 5.0 %collective-permute-done.10.refs_1_ = f32[16,16,128]{2,1,0:T(8,128)S(1)} collective-permute-done((f32[16,16,128]{2,1,0:T(8,128)S(1)}, f32[16,16,128]{2,1,0:T(8,128)S(1)}, u32[]{:S(2)}, u32[]{:S(2)}) %collective-permute-start.10) | collective-permute-done | bytes 131104 | tf_op jit(solution)/shard_map/ppermute | solution.py:145
  48.5 2.7 %collective-permute-start.8 = (bf16[768,768]{1,0:T(8,128)(2,1)}, bf16[768,768]{1,0:T(8,128)(2,1)}, u32[]{:S(2)}, u32[]{:S(2)}) collective-permute-start(bf16[768,768]{1,0:T(8,128)(2,1)} %constant_dynamic-update-slice_fusion.refs_9_), channel_id=1, source_target_pairs={{0,8},{2,10},{4,12},{6,14},{8,0},{10,2},{12,4},{14,6},{16,24},{18,... | collective-permute-start | bytes 3538952 | tf_op jit(solution)/shard_map/ppermute | solution.py:150
  51.2 8.5 %gated_conv.1.refs_0_ = bf16[2,256,1024]{2,1,0:T(8,128)(2,1)} custom-call(bf16[256,2048]{1,0:T(8,128)(2,1)} %q_ref.1, bf16[256,2048]{1,0:T(8,128)(2,1)S(1)} %get-tuple-element.388, bf16[256,2048]{1,0:T(8,128)(2,1)S(1)} %get-tuple-element.389, f32[16,2048]{1,0:T(8,128)S(1)} %get-tuple-element.398, f32[16,2048]{1,0:T(8,128)} %residue_ref.1, ...), custom_call_target="tpu_custom_call" | custom-call | flops 33554432 | bytes 4194304 | tf_op jit(solution)/shard_map/gated_conv/pallas_call | solution.py:128
  61.1 18.1 %collective-permute-done.11.refs_9_ = bf16[256,768]{1,0:T(8,128)(2,1)S(1)} collective-permute-done((bf16[256,768]{1,0:T(8,128)(2,1)S(1)}, bf16[256,768]{1,0:T(8,128)(2,1)S(1)}, u32[]{:S(2)}, u32[]{:S(2)}) %collective-permute-start.11) | collective-permute-done | bytes 393248 | tf_op jit(solution)/shard_map/ppermute | solution.py:323
  83.5 2.2 %slice.16 = bf16[768,512]{1,0:T(8,128)(2,1)} slice(bf16[768,768]{1,0:T(8,128)(2,1)} %constant_dynamic-update-slice_fusion.refs_9_), slice={[0:768], [0:512]} | slice | bytes 1572864 | tf_op jit(solution)/shard_map/slice | solution.py:369
  86.7 23.5 %collective-permute-done.14.refs_2_ = bf16[2,256,1024]{2,1,0:T(8,128)(2,1)} collective-permute-done((bf16[2,256,1024]{2,1,0:T(8,128)(2,1)}, bf16[2,256,1024]{2,1,0:T(8,128)(2,1)}, u32[]{:S(2)}, u32[]{:S(2)}) %collective-permute-start.14) | collective-permute-done | bytes 1048608 | tf_op jit(solution)/shard_map/ppermute | solution.py:150
  111.3 2.1 %slice.14 = bf16[768,512]{1,0:T(8,128)(2,1)} slice(bf16[768,768]{1,0:T(8,128)(2,1)} %collective-permute-done.7.refs_13_), slice={[0:768], [0:512]} | slice | bytes 1572864 | tf_op jit(solution)/shard_map/slice | solution.py:374
  114.7 4.4 %collective-permute-start.21 = (bf16[768,512]{1,0:T(8,128)(2,1)}, bf16[768,512]{1,0:T(8,128)(2,1)}, u32[]{:S(2)}, u32[]{:S(2)}) collective-permute-start(bf16[768,512]{1,0:T(8,128)(2,1)} %slice.16), channel_id=1, source_target_pairs={{8,16},{10,18},{12,20},{14,22},{16,8},{18,10},{20,12},{22,14},{9,1... | collective-permute-start | bytes 2359304 | tf_op jit(solution)/shard_map/ppermute | solution.py:323
  122.8 12.4 %product.3 = (f32[256,768]{1,0:T(8,128)}, f32[256,768]{1,0:T(8,128)}, f32[256,768]{1,0:T(8,128)}, f32[256,768]{1,0:T(8,128)}) custom-call(s32[5]{0:T(128)} %stack.38.flag_ref, s32[4]{0:T(128)} %pad_add_fusion.place_ref, bf16[2,256,1024]{2,1,0:T(8,128)(2,1)} %gated_conv.1.refs_0_, bf16[2,256,1024]{2,1,0:T(8,128)(2,1)} %copy-done.7, ...), custom_call_target="tpu_custom_call" | custom-call | flops 4831838208 | bytes 11010048 | tf_op jit(solution)/shard_map/product/pallas_call | solution.py:247
  138.5 3.6 %collective-permute-start.26 = (bf16[768,256]{1,0:T(8,128)(2,1)S(1)}, bf16[768,256]{1,0:T(8,128)(2,1)S(1)}, u32[]{:S(2)}, u32[]{:S(2)}) collective-permute-start(bf16[768,256]{1,0:T(8,128)(2,1)S(1)} %slice.17), channel_id=1, source_target_pairs={{8,16},{10,18},{12,20},{14,22},{16,8},{18,10},{20,12},{22,14},{9,1... | collective-permute-start | bytes 1179656 | tf_op jit(solution)/shard_map/ppermute | solution.py:323
  142.1 5.2 %product.4 = (bf16[256,512]{1,0:T(8,128)(2,1)}, bf16[256,512]{1,0:T(8,128)(2,1)}, bf16[256,512]{1,0:T(8,128)(2,1)}, bf16[256,512]{1,0:T(8,128)(2,1)}) custom-call(s32[5]{0:T(128)} %stack.38.flag_ref, s32[4]{0:T(128)} %pad_add_fusion.place_ref, bf16[2,256,1024]{2,1,0:T(8,128)(2,1)} %gated_conv.1.refs_0_, bf16[2,256,1024]{2,1,0:T(8,128)(2,1)} %copy-done.7, ...), custom_call_target="tpu_custom_call" | custom-call | flops 1073741824 | bytes 3145728 | tf_op jit(solution)/shard_map/product/pallas_call | solution.py:247
  149.0 2.0 %collective-permute-start.23 = (bf16[256,512]{1,0:T(8,128)(2,1)}, bf16[256,512]{1,0:T(8,128)(2,1)S(1)}, u32[]{:S(2)}, u32[]{:S(2)}) collective-permute-start(bf16[256,512]{1,0:T(8,128)(2,1)} %get-tuple-element.234), channel_id=1, source_target_pairs={{0,4},{2,6},{4,0},{6,2},{8,12},{10,14},{12,8},{14,10},{16,20},{18,... | collective-permute-start | bytes 786440 | tf_op jit(solution)/shard_map/ppermute | solution.py:150
  152.6 4.1 %product.5 = (bf16[256,256]{1,0:T(8,128)(2,1)}, bf16[256,256]{1,0:T(8,128)(2,1)}, bf16[256,256]{1,0:T(8,128)(2,1)}, bf16[256,256]{1,0:T(8,128)(2,1)}) custom-call(s32[5]{0:T(128)} %stack.38.flag_ref, s32[4]{0:T(128)} %pad_add_fusion.place_ref, bf16[2,256,1024]{2,1,0:T(8,128)(2,1)} %gated_conv.1.refs_0_, bf16[2,256,1024]{2,1,0:T(8,128)(2,1)} %copy-done.7, ...), custom_call_target="tpu_custom_call" | custom-call | flops 536870912 | bytes 2621440 | tf_op jit(solution)/shard_map/product/pallas_call | solution.py:247
  158.2 2.0 %collective-permute-start.28 = (bf16[256,256]{1,0:T(8,128)(2,1)}, bf16[256,256]{1,0:T(8,128)(2,1)S(1)}, u32[]{:S(2)}, u32[]{:S(2)}) collective-permute-start(bf16[256,256]{1,0:T(8,128)(2,1)} %get-tuple-element.240), channel_id=1, source_target_pairs={{0,4},{2,6},{4,0},{6,2},{8,12},{10,14},{12,8},{14,10},{16,20},{18,... | collective-permute-start | bytes 393224 | tf_op jit(solution)/shard_map/ppermute | solution.py:150
  160.2 3.7 %collective-permute-done.23.refs_2_ = bf16[256,512]{1,0:T(8,128)(2,1)S(1)} collective-permute-done((bf16[256,512]{1,0:T(8,128)(2,1)}, bf16[256,512]{1,0:T(8,128)(2,1)S(1)}, u32[]{:S(2)}, u32[]{:S(2)}) %collective-permute-start.23) | collective-permute-done | bytes 262176 | tf_op jit(solution)/shard_map/ppermute | solution.py:150
  164.7 2.3 %collective-permute-done.28.refs_6_ = bf16[256,256]{1,0:T(8,128)(2,1)S(1)} collective-permute-done((bf16[256,256]{1,0:T(8,128)(2,1)}, bf16[256,256]{1,0:T(8,128)(2,1)S(1)}, u32[]{:S(2)}, u32[]{:S(2)}) %collective-permute-start.28) | collective-permute-done | bytes 131104 | tf_op jit(solution)/shard_map/ppermute | solution.py:150
  (98 shorter events, 44.6 us)
Async XLA Ops:
  2.6 19.0 %collective-permute-start.2 = (bf16[256,768]{1,0:T(8,128)(2,1)S(1)}, bf16[256,768]{1,0:T(8,128)(2,1)}, u32[]{:S(2)}, u32[]{:S(2)}) collective-permute-start(bf16[256,768]{1,0:T(8,128)(2,1)S(1)} %get-tuple-element.202.refs_8_), channel_id=1, source_target_pairs={{0,8},{2,10},{4,12},{6,14},{8,0},{10,2},{12,4},{14,6},{16,24},{18,... | collective-permute-start | bytes 1179656 | tf_op jit(solution)/shard_map/ppermute | solution.py:150
  2.6 20.5 %collective-permute-start.3 = (bf16[256,768]{1,0:T(8,128)(2,1)S(1)}, bf16[256,768]{1,0:T(8,128)(2,1)}, u32[]{:S(2)}, u32[]{:S(2)}) collective-permute-start(bf16[256,768]{1,0:T(8,128)(2,1)S(1)} %get-tuple-element.202.refs_8_), channel_id=1, source_target_pairs={{0,16},{2,18},{4,20},{6,22},{8,24},{10,26},{12,28},{14,30},{16,0},... | collective-permute-start | bytes 1179656 | tf_op jit(solution)/shard_map/ppermute | solution.py:150
  25.4 18.6 %collective-permute-start.4 = (bf16[256,768]{1,0:T(8,128)(2,1)}, bf16[256,768]{1,0:T(8,128)(2,1)S(1)}, u32[]{:S(2)}, u32[]{:S(2)}) collective-permute-start(bf16[256,768]{1,0:T(8,128)(2,1)} %get-tuple-element.196), channel_id=1, source_target_pairs={{0,2},{2,0},{4,6},{6,4},{8,10},{10,8},{12,14},{14,12},{16,18},{18,... | collective-permute-start | bytes 1179656 | tf_op jit(solution)/shard_map/ppermute | solution.py:150
  27.0 18.0 %collective-permute-start.5 = (bf16[256,768]{1,0:T(8,128)(2,1)}, bf16[256,768]{1,0:T(8,128)(2,1)S(1)}, u32[]{:S(2)}, u32[]{:S(2)}) collective-permute-start(bf16[256,768]{1,0:T(8,128)(2,1)} %get-tuple-element.197), channel_id=1, source_target_pairs={{0,4},{2,6},{4,0},{6,2},{8,12},{10,14},{12,8},{14,10},{16,20},{18,... | collective-permute-start | bytes 1179656 | tf_op jit(solution)/shard_map/ppermute | solution.py:150
  28.5 17.3 %collective-permute-start.6 = (bf16[256,768]{1,0:T(8,128)(2,1)}, bf16[256,768]{1,0:T(8,128)(2,1)S(1)}, u32[]{:S(2)}, u32[]{:S(2)}) collective-permute-start(bf16[256,768]{1,0:T(8,128)(2,1)} %get-tuple-element.198), channel_id=1, source_target_pairs={{0,6},{2,4},{4,2},{6,0},{8,14},{10,12},{12,10},{14,8},{16,22},{18,... | collective-permute-start | bytes 1179656 | tf_op jit(solution)/shard_map/ppermute | solution.py:150
  31.1 9.7 %collective-permute-start.10 = (f32[16,16,128]{2,1,0:T(8,128)S(1)}, f32[16,16,128]{2,1,0:T(8,128)S(1)}, u32[]{:S(2)}, u32[]{:S(2)}) collective-permute-start(f32[16,16,128]{2,1,0:T(8,128)S(1)} %multiply_add_fusion), channel_id=1, source_target_pairs={{0,16},{2,18},{4,20},{6,22},{8,24},{10,26},{12,28},{14,30},{1,17},... | collective-permute-start | bytes 393224 | tf_op jit(solution)/shard_map/ppermute | solution.py:145
  40.8 38.4 %collective-permute-start.11 = (bf16[256,768]{1,0:T(8,128)(2,1)S(1)}, bf16[256,768]{1,0:T(8,128)(2,1)S(1)}, u32[]{:S(2)}, u32[]{:S(2)}) collective-permute-start(bf16[256,768]{1,0:T(8,128)(2,1)S(1)} %get-tuple-element.202.refs_8_), channel_id=1, source_target_pairs={{8,16},{10,18},{12,20},{14,22},{16,8},{18,10},{20,12},{22,14},{9,1... | collective-permute-start | bytes 1179656 | tf_op jit(solution)/shard_map/ppermute | solution.py:323
  42.7 38.5 %collective-permute-start.12 = (bf16[256,768]{1,0:T(8,128)(2,1)}, bf16[256,768]{1,0:T(8,128)(2,1)S(1)}, u32[]{:S(2)}, u32[]{:S(2)}) collective-permute-start(bf16[256,768]{1,0:T(8,128)(2,1)} %collective-permute-done.3.refs_12_), channel_id=1, source_target_pairs={{8,0},{10,2},{12,4},{14,6},{16,24},{18,26},{20,28},{22,30},{9,1},{... | collective-permute-start | bytes 1179656 | tf_op jit(solution)/shard_map/ppermute | solution.py:326
  46.5 63.6 %collective-permute-start.7 = (bf16[768,768]{1,0:T(8,128)(2,1)}, bf16[768,768]{1,0:T(8,128)(2,1)}, u32[]{:S(2)}, u32[]{:S(2)}) collective-permute-start(bf16[768,768]{1,0:T(8,128)(2,1)} %constant_dynamic-update-slice_fusion.refs_9_), channel_id=1, source_target_pairs={{0,16},{2,18},{4,20},{6,22},{8,24},{10,26},{12,28},{14,30},{16,0},... | collective-permute-start | bytes 3538952 | tf_op jit(solution)/shard_map/ppermute | solution.py:150
  48.5 61.6 %collective-permute-start.8 = (bf16[768,768]{1,0:T(8,128)(2,1)}, bf16[768,768]{1,0:T(8,128)(2,1)}, u32[]{:S(2)}, u32[]{:S(2)}) collective-permute-start(bf16[768,768]{1,0:T(8,128)(2,1)} %constant_dynamic-update-slice_fusion.refs_9_), channel_id=1, source_target_pairs={{0,8},{2,10},{4,12},{6,14},{8,0},{10,2},{12,4},{14,6},{16,24},{18,... | collective-permute-start | bytes 3538952 | tf_op jit(solution)/shard_map/ppermute | solution.py:150
  59.6 27.0 %collective-permute-start.13 = (bf16[2,256,1024]{2,1,0:T(8,128)(2,1)}, bf16[2,256,1024]{2,1,0:T(8,128)(2,1)S(1)}, u32[]{:S(2)}, u32[]{:S(2)}) collective-permute-start(bf16[2,256,1024]{2,1,0:T(8,128)(2,1)} %gated_conv.1.refs_0_), channel_id=1, source_target_pairs={{0,2},{2,0},{4,6},{6,4},{8,10},{10,8},{12,14},{14,12},{16,18},{18,... | collective-permute-start | bytes 3145736 | tf_op jit(solution)/shard_map/ppermute | solution.py:150
  79.2 31.0 %collective-permute-start.14 = (bf16[2,256,1024]{2,1,0:T(8,128)(2,1)}, bf16[2,256,1024]{2,1,0:T(8,128)(2,1)}, u32[]{:S(2)}, u32[]{:S(2)}) collective-permute-start(bf16[2,256,1024]{2,1,0:T(8,128)(2,1)} %gated_conv.1.refs_0_), channel_id=1, source_target_pairs={{0,4},{2,6},{4,0},{6,2},{8,12},{10,14},{12,8},{14,10},{16,20},{18,... | collective-permute-start | bytes 3145736 | tf_op jit(solution)/shard_map/ppermute | solution.py:150
  81.2 28.9 %collective-permute-start.15 = (bf16[2,256,1024]{2,1,0:T(8,128)(2,1)}, bf16[2,256,1024]{2,1,0:T(8,128)(2,1)}, u32[]{:S(2)}, u32[]{:S(2)}) collective-permute-start(bf16[2,256,1024]{2,1,0:T(8,128)(2,1)} %gated_conv.1.refs_0_), channel_id=1, source_target_pairs={{0,6},{2,4},{4,2},{6,0},{8,14},{10,12},{12,10},{14,8},{16,22},{18,... | collective-permute-start | bytes 3145736 | tf_op jit(solution)/shard_map/ppermute | solution.py:150
  110.2 10.6 %collective-permute-start.17 = (bf16[2,256,1024]{2,1,0:T(8,128)(2,1)S(1)}, bf16[2,256,1024]{2,1,0:T(8,128)(2,1)S(1)}, u32[]{:S(2)}, u32[]{:S(2)}) collective-permute-start(bf16[2,256,1024]{2,1,0:T(8,128)(2,1)S(1)} %collective-permute-done.13.refs_1_), channel_id=1, source_target_pairs={{0,1},{1,0},{2,3},{3,2},{4,5},{5,4},{6,7},{7,6},{8,9},{9,8},{10,11... | collective-permute-start | bytes 3145736 | tf_op jit(solution)/shard_map/ppermute | solution.py:150
  110.7 11.1 %collective-permute-start.18 = (bf16[2,256,1024]{2,1,0:T(8,128)(2,1)}, bf16[2,256,1024]{2,1,0:T(8,128)(2,1)S(1)}, u32[]{:S(2)}, u32[]{:S(2)}) collective-permute-start(bf16[2,256,1024]{2,1,0:T(8,128)(2,1)} %collective-permute-done.14.refs_2_), channel_id=1, source_target_pairs={{0,1},{1,0},{2,3},{3,2},{4,5},{5,4},{6,7},{7,6},{8,9},{9,8},{10,11... | collective-permute-start | bytes 3145736 | tf_op jit(solution)/shard_map/ppermute | solution.py:150
  110.8 12.0 %collective-permute-start.19 = (bf16[2,256,1024]{2,1,0:T(8,128)(2,1)}, bf16[2,256,1024]{2,1,0:T(8,128)(2,1)}, u32[]{:S(2)}, u32[]{:S(2)}) collective-permute-start(bf16[2,256,1024]{2,1,0:T(8,128)(2,1)} %collective-permute-done.15.refs_3_), channel_id=1, source_target_pairs={{0,1},{1,0},{2,3},{3,2},{4,5},{5,4},{6,7},{7,6},{8,9},{9,8},{10,11... | collective-permute-start | bytes 3145736 | tf_op jit(solution)/shard_map/ppermute | solution.py:150
  113.3 21.9 %collective-permute-start.20 = (bf16[768,512]{1,0:T(8,128)(2,1)}, bf16[768,512]{1,0:T(8,128)(2,1)S(1)}, u32[]{:S(2)}, u32[]{:S(2)}) collective-permute-start(bf16[768,512]{1,0:T(8,128)(2,1)} %slice.14), channel_id=1, source_target_pairs={{8,0},{10,2},{12,4},{14,6},{16,24},{18,26},{20,28},{22,30},{9,1},{... | collective-permute-start | bytes 2359304 | tf_op jit(solution)/shard_map/ppermute | solution.py:326
  114.7 22.5 %collective-permute-start.21 = (bf16[768,512]{1,0:T(8,128)(2,1)}, bf16[768,512]{1,0:T(8,128)(2,1)}, u32[]{:S(2)}, u32[]{:S(2)}) collective-permute-start(bf16[768,512]{1,0:T(8,128)(2,1)} %slice.16), channel_id=1, source_target_pairs={{8,16},{10,18},{12,20},{14,22},{16,8},{18,10},{20,12},{22,14},{9,1... | collective-permute-start | bytes 2359304 | tf_op jit(solution)/shard_map/ppermute | solution.py:323
  137.2 13.9 %collective-permute-start.25 = (bf16[768,256]{1,0:T(8,128)(2,1)}, bf16[768,256]{1,0:T(8,128)(2,1)S(1)}, u32[]{:S(2)}, u32[]{:S(2)}) collective-permute-start(bf16[768,256]{1,0:T(8,128)(2,1)} %slice.15), channel_id=1, source_target_pairs={{8,0},{10,2},{12,4},{14,6},{16,24},{18,26},{20,28},{22,30},{9,1},{... | collective-permute-start | bytes 1179656 | tf_op jit(solution)/shard_map/ppermute | solution.py:326
  138.5 12.6 %collective-permute-start.26 = (bf16[768,256]{1,0:T(8,128)(2,1)S(1)}, bf16[768,256]{1,0:T(8,128)(2,1)S(1)}, u32[]{:S(2)}, u32[]{:S(2)}) collective-permute-start(bf16[768,256]{1,0:T(8,128)(2,1)S(1)} %slice.17), channel_id=1, source_target_pairs={{8,16},{10,18},{12,20},{14,22},{16,8},{18,10},{20,12},{22,14},{9,1... | collective-permute-start | bytes 1179656 | tf_op jit(solution)/shard_map/ppermute | solution.py:323
  147.4 12.9 %collective-permute-start.22 = (bf16[256,512]{1,0:T(8,128)(2,1)}, bf16[256,512]{1,0:T(8,128)(2,1)S(1)}, u32[]{:S(2)}, u32[]{:S(2)}) collective-permute-start(bf16[256,512]{1,0:T(8,128)(2,1)} %get-tuple-element.233), channel_id=1, source_target_pairs={{0,2},{2,0},{4,6},{6,4},{8,10},{10,8},{12,14},{14,12},{16,18},{18,... | collective-permute-start | bytes 786440 | tf_op jit(solution)/shard_map/ppermute | solution.py:150
  149.0 14.9 %collective-permute-start.23 = (bf16[256,512]{1,0:T(8,128)(2,1)}, bf16[256,512]{1,0:T(8,128)(2,1)S(1)}, u32[]{:S(2)}, u32[]{:S(2)}) collective-permute-start(bf16[256,512]{1,0:T(8,128)(2,1)} %get-tuple-element.234), channel_id=1, source_target_pairs={{0,4},{2,6},{4,0},{6,2},{8,12},{10,14},{12,8},{14,10},{16,20},{18,... | collective-permute-start | bytes 786440 | tf_op jit(solution)/shard_map/ppermute | solution.py:150
  151.1 13.0 %collective-permute-start.24 = (bf16[256,512]{1,0:T(8,128)(2,1)}, bf16[256,512]{1,0:T(8,128)(2,1)S(1)}, u32[]{:S(2)}, u32[]{:S(2)}) collective-permute-start(bf16[256,512]{1,0:T(8,128)(2,1)} %get-tuple-element.235), channel_id=1, source_target_pairs={{0,6},{2,4},{4,2},{6,0},{8,14},{10,12},{12,10},{14,8},{16,22},{18,... | collective-permute-start | bytes 786440 | tf_op jit(solution)/shard_map/ppermute | solution.py:150
  158.2 8.8 %collective-permute-start.28 = (bf16[256,256]{1,0:T(8,128)(2,1)}, bf16[256,256]{1,0:T(8,128)(2,1)S(1)}, u32[]{:S(2)}, u32[]{:S(2)}) collective-permute-start(bf16[256,256]{1,0:T(8,128)(2,1)} %get-tuple-element.240), channel_id=1, source_target_pairs={{0,4},{2,6},{4,0},{6,2},{8,12},{10,14},{12,8},{14,10},{16,20},{18,... | collective-permute-start | bytes 393224 | tf_op jit(solution)/shard_map/ppermute | solution.py:150
  (26 other events, 261.0 us)

commit v21 on v19

--- a/solution.py
+++ b/solution.py
@@ -362,7 +362,7 @@
     out0, mid0 = outward(f0), across(w0)
     gated = gated_conv(q, k, v, rate, residue, skip, before, ([last, earlier], spot))
     rest = jnp.concatenate(arrived)
-    gated, rest, mid0, out0 = tie(gated, rest, mid0, out0)
+    gated, rest, out0, mid0 = tie(gated, rest, out0, mid0)
 
     nr, fr = near(rest), far(rest)
     ours = [gated] + [exchange(gated, "ctx", r) for r in range(1, PLANE)]

time: 166 us -> 165 us (level)
  starting transfers between devices: 60 us -> 46.5 us
  waiting for transfers between devices: 54.1 us -> 66 us
    ppermute x22, waiting for transfers between devices: 44.8 us -> 55.3 us  [exchange(): return lax.ppermute(x, axis, [(i, i ^ flip) for i in range(count)])]
    ppermute x22, starting transfers between devices: 33.4 us -> 25.5 us  [exchange(): return lax.ppermute(x, axis, [(i, i ^ flip) for i in range(count)])]
    ppermute x3, starting transfers between devices: 13.5 us -> 8.41 us  [across(): return lax.ppermute(x, 'ctx', [(i, i ^ 3 * PLANE) for i in middle])]
  transfers between devices with their start and end apart: 30 -> 30, of which waited for: 14 -> 15; matrix products, arithmetic and copies ran while one was open for 6% -> 6% of each run, Pallas kernels for 21% -> 21%
where the time goes in v21:
time: 165 us; the launch traced here: 164 us
  waiting for transfers between devices  66 us (40%)
  starting transfers between devices  46.5 us (28%)
  Pallas kernels  36.1 us (22%)
  local copies, waits for them, and re-layouts  10.8 us (7%)
  other arithmetic  4.64 us (3%)
    ppermute x22, waiting for transfers between devices, exchange(): return lax.ppermute(x, axis, [(i, i ^ flip) for i in range(count)])  55.3 us
    ppermute x22, starting transfers between devices, exchange(): return lax.ppermute(x, axis, [(i, i ^ flip) for i in range(count)])  25.5 us
    pallas_call x3, Pallas kernels, product(): pl.pallas_call(kernel, in_specs=[smem, smem] + [anywhere] * (2 * parts +...  21.9 us
    pallas_call x1, Pallas kernels, gated_conv(): pl.pallas_call(conv_kernel, grid=(chan // width,), in_specs=[wide, wide,...  8.5 us
    ppermute x3, starting transfers between devices, across(): return lax.ppermute(x, 'ctx', [(i, i ^ 3 * PLANE) for i in middle])  8.41 us
    ppermute x2, starting transfers between devices, shift_ctx(): return lax.ppermute(x, 'ctx', [(i, i + by) for i in range(count - by)])  6.85 us
    ppermute x2, waiting for transfers between devices, shift_ctx(): return lax.ppermute(x, 'ctx', [(i, i + by) for i in range(count - by)])  5.98 us
    ppermute x3, starting transfers between devices, outward(): return lax.ppermute(x, 'ctx', [(i, i ^ PLANE) for i in middle])  5.72 us
  transfers between devices with their start and end apart: 30, of which 15 were waited for; matrix products, arithmetic and copies ran while one was open for 6% of the time, Pallas kernels for 21%

profile of v21, /device:TPU:8, one launch (start us, length us, event | category | flops | bytes accessed | tf_op | source)
XLA Modules:
  0.0 164.3 jit_solution(8164619897526128449)
XLA Ops:
  0.0 2.7 %constant_dynamic-slice_fusion = (bf16[256,768]{1,0:T(8,128)(2,1)}, bf16[256,768]{1,0:T(8,128)(2,1)}, bf16[256,768]{1,0:T(8,128)(2,1)}, bf16[256,768]{1,0:T(8,128)(2,1)}) fusion(bf16[256,3072]{1,0:T(8,128)(2,1)} %param.15, s32[]{:T(128)S(6)} %select_n.84, s32[]{:T(128)S(6)} %select_n.82, s32[]{:T(128)S(6)} %select_n.81, s32[]{:T(128)S(6)} %select_n.83), kind=kLoop, calls=%fused_computation.5 | loop fusion | bytes 3145744 | tf_op jit(solution)/shard_map/dynamic_slice | solution.py:329
  2.7 3.0 %collective-permute-start.3 = (bf16[256,768]{1,0:T(8,128)(2,1)}, bf16[256,768]{1,0:T(8,128)(2,1)}, u32[]{:S(2)}, u32[]{:S(2)}) collective-permute-start(bf16[256,768]{1,0:T(8,128)(2,1)} %get-tuple-element.208.refs_8_), channel_id=1, source_target_pairs={{0,16},{2,18},{4,20},{6,22},{8,24},{10,26},{12,28},{14,30},{16,0},... | collective-permute-start | bytes 1179656 | tf_op jit(solution)/shard_map/ppermute | solution.py:150
  5.8 15.9 %while.14 = (s32[]{:T(128)}, f32[16,16,128]{2,1,0:T(8,128)}, f32[16,16,128]{2,1,0:T(8,128)}, s32[]{:T(128)}, pred[]{:T(512)}, /*index=5*/bf16[256,2048]{1,0:T(8,...) while((s32[]{:T(128)}, f32[16,16,128]{2,1,0:T(8,128)}, ...), condition=%wide.region_1.2_spmd, body=%wide.region_0.1_spmd.sunk | while | flops 17399808 | bytes 4456652 | solution.py:185
  5.8 4.0 %end_states.3 = f32[16,16,128]{2,1,0:T(8,128)} custom-call(bf16[256,2048]{1,0:T(8,128)(2,1)S(1)} %get-tuple-element.346.k_ref, bf16[256,2048]{1,0:T(8,128)(2,1)S(1)} %get-tuple-element.347.v_ref, f32[16,2048]{1,0:T(8,128)S(1)} %get-tuple-element.348.rate_ref), custom_call_target="tpu_custom_call" | custom-call | flops 16777216 | bytes 2097152 | tf_op jit(solution)/shard_map/while/body/end_states/pallas_call | solution.py:98
  11.3 3.7 %collective-permute-done = f32[16,16,128]{2,1,0:T(8,128)S(1)} collective-permute-done((f32[16,16,128]{2,1,0:T(8,128)}, f32[16,16,128]{2,1,0:T(8,128)S(1)}, u32[]{:S(2)}, u32[]{:S(2)}) %collective-permute-start) | collective-permute-done | bytes 131104 | tf_op jit(solution)/shard_map/while/body/ppermute | solution.py:150
  17.5 3.4 %collective-permute-done.1 = f32[16,16,128]{2,1,0:T(8,128)S(1)} collective-permute-done((f32[16,16,128]{2,1,0:T(8,128)S(1)}, f32[16,16,128]{2,1,0:T(8,128)S(1)}, u32[]{:S(2)}, u32[]{:S(2)}) %collective-permute-start.1) | collective-permute-done | bytes 131104 | tf_op jit(solution)/shard_map/while/body/ppermute | solution.py:150
  23.4 2.3 %collective-permute-start.4 = (f32[16,16,128]{2,1,0:T(8,128)}, f32[16,16,128]{2,1,0:T(8,128)S(1)}, u32[]{:S(2)}, u32[]{:S(2)}) collective-permute-start(f32[16,16,128]{2,1,0:T(8,128)} %get-tuple-element.200), channel_id=1, source_target_pairs={{0,8},{2,10},{4,12},{6,14},{8,16},{10,18},{12,20},{14,22},{16,24},... | collective-permute-start | bytes 393224 | tf_op jit(solution)/shard_map/ppermute | solution.py:145
  31.5 4.5 %collective-permute-start.5 = (f32[16,16,128]{2,1,0:T(8,128)S(1)}, f32[16,16,128]{2,1,0:T(8,128)S(1)}, u32[]{:S(2)}, u32[]{:S(2)}) collective-permute-start(f32[16,16,128]{2,1,0:T(8,128)S(1)} %multiply_add_fusion), channel_id=1, source_target_pairs={{0,16},{2,18},{4,20},{6,22},{8,24},{10,26},{12,28},{14,30},{1,17},... | collective-permute-start | bytes 393224 | tf_op jit(solution)/shard_map/ppermute | solution.py:145
  36.0 4.8 %collective-permute-done.5.refs_1_ = f32[16,16,128]{2,1,0:T(8,128)S(1)} collective-permute-done((f32[16,16,128]{2,1,0:T(8,128)S(1)}, f32[16,16,128]{2,1,0:T(8,128)S(1)}, u32[]{:S(2)}, u32[]{:S(2)}) %collective-permute-start.5) | collective-permute-done | bytes 131104 | tf_op jit(solution)/shard_map/ppermute | solution.py:145
  44.1 8.5 %gated_conv.1.refs_0_ = bf16[2,256,1024]{2,1,0:T(8,128)(2,1)} custom-call(bf16[256,2048]{1,0:T(8,128)(2,1)} %q_ref.1, bf16[256,2048]{1,0:T(8,128)(2,1)S(1)} %get-tuple-element.394, bf16[256,2048]{1,0:T(8,128)(2,1)S(1)} %get-tuple-element.395, f32[16,2048]{1,0:T(8,128)S(1)} %get-tuple-element.404, f32[16,2048]{1,0:T(8,128)} %residue_ref.1, ...), custom_call_target="tpu_custom_call" | custom-call | flops 33554432 | bytes 4194304 | tf_op jit(solution)/shard_map/gated_conv/pallas_call | solution.py:128
  55.6 3.7 %collective-permute-start.11 = (bf16[768,768]{1,0:T(8,128)(2,1)S(1)}, bf16[768,768]{1,0:T(8,128)(2,1)}, u32[]{:S(2)}, u32[]{:S(2)}) collective-permute-start(bf16[768,768]{1,0:T(8,128)(2,1)S(1)} %pad_maximum_fusion.refs_9_), channel_id=1, source_target_pairs={{0,16},{2,18},{4,20},{6,22},{8,24},{10,26},{12,28},{14,30},{16,0},... | collective-permute-start | bytes 3538952 | tf_op jit(solution)/shard_map/ppermute | solution.py:150
  62.3 18.0 %collective-permute-done.13.refs_1_ = bf16[2,256,1024]{2,1,0:T(8,128)(2,1)} collective-permute-done((bf16[2,256,1024]{2,1,0:T(8,128)(2,1)S(1)}, bf16[2,256,1024]{2,1,0:T(8,128)(2,1)}, u32[]{:S(2)}, u32[]{:S(2)}) %collective-permute-start.13) | collective-permute-done | bytes 1048608 | tf_op jit(solution)/shard_map/ppermute | solution.py:150
  83.2 16.9 %collective-permute-done.15.refs_2_ = bf16[2,256,1024]{2,1,0:T(8,128)(2,1)} collective-permute-done((bf16[2,256,1024]{2,1,0:T(8,128)(2,1)S(1)}, bf16[2,256,1024]{2,1,0:T(8,128)(2,1)}, u32[]{:S(2)}, u32[]{:S(2)}) %collective-permute-start.15) | collective-permute-done | bytes 1048608 | tf_op jit(solution)/shard_map/ppermute | solution.py:150
  101.6 2.8 %collective-permute-done.12.refs_11_ = bf16[768,768]{1,0:T(8,128)(2,1)} collective-permute-done((bf16[768,768]{1,0:T(8,128)(2,1)S(1)}, bf16[768,768]{1,0:T(8,128)(2,1)}, u32[]{:S(2)}, u32[]{:S(2)}) %collective-permute-start.12) | collective-permute-done | bytes 1179680 | tf_op jit(solution)/shard_map/ppermute | solution.py:150
  104.9 2.1 %slice.14 = bf16[768,512]{1,0:T(8,128)(2,1)} slice(bf16[768,768]{1,0:T(8,128)(2,1)} %collective-permute-done.11.refs_13_), slice={[0:768], [0:512]} | slice | bytes 1572864 | tf_op jit(solution)/shard_map/slice | solution.py:376
  107.0 3.1 %collective-permute-start.20 = (bf16[768,512]{1,0:T(8,128)(2,1)}, bf16[768,512]{1,0:T(8,128)(2,1)}, u32[]{:S(2)}, u32[]{:S(2)}) collective-permute-start(bf16[768,512]{1,0:T(8,128)(2,1)} %slice.14), channel_id=1, source_target_pairs={{8,0},{10,2},{12,4},{14,6},{16,24},{18,26},{20,28},{22,30},{9,1},{... | collective-permute-start | bytes 2359304 | tf_op jit(solution)/shard_map/ppermute | solution.py:326
  110.1 3.2 %collective-permute-start.21 = (bf16[768,512]{1,0:T(8,128)(2,1)}, bf16[768,512]{1,0:T(8,128)(2,1)S(1)}, u32[]{:S(2)}, u32[]{:S(2)}) collective-permute-start(bf16[768,512]{1,0:T(8,128)(2,1)} %slice.12), channel_id=1, source_target_pairs={{8,16},{10,18},{12,20},{14,22},{16,8},{18,10},{20,12},{22,14},{9,1... | collective-permute-start | bytes 2359304 | tf_op jit(solution)/shard_map/ppermute | solution.py:323
  114.6 12.5 %product.3 = (f32[256,768]{1,0:T(8,128)}, f32[256,768]{1,0:T(8,128)}, f32[256,768]{1,0:T(8,128)}, f32[256,768]{1,0:T(8,128)}) custom-call(s32[5]{0:T(128)} %stack.36.flag_ref, s32[4]{0:T(128)} %pad_add_fusion.place_ref, bf16[2,256,1024]{2,1,0:T(8,128)(2,1)} %gated_conv.1.refs_0_, bf16[2,256,1024]{2,1,0:T(8,128)(2,1)} %collective-permute-done.13.refs_1_, ...), custom_call_target="tpu_custom_call" | custom-call | flops 4831838208 | bytes 11010048 | tf_op jit(solution)/shard_map/product/pallas_call | solution.py:247
  127.2 4.6 %collective-permute-done.21.refs_11_ = bf16[768,512]{1,0:T(8,128)(2,1)S(1)} collective-permute-done((bf16[768,512]{1,0:T(8,128)(2,1)}, bf16[768,512]{1,0:T(8,128)(2,1)S(1)}, u32[]{:S(2)}, u32[]{:S(2)}) %collective-permute-start.21) | collective-permute-done | bytes 786464 | tf_op jit(solution)/shard_map/ppermute | solution.py:323
  133.1 3.3 %collective-permute-start.26 = (bf16[768,256]{1,0:T(8,128)(2,1)S(1)}, bf16[768,256]{1,0:T(8,128)(2,1)S(1)}, u32[]{:S(2)}, u32[]{:S(2)}) collective-permute-start(bf16[768,256]{1,0:T(8,128)(2,1)S(1)} %copy-done.13), channel_id=1, source_target_pairs={{8,16},{10,18},{12,20},{14,22},{16,8},{18,10},{20,12},{22,14},{9,1... | collective-permute-start | bytes 1179656 | tf_op jit(solution)/shard_map/ppermute | solution.py:323
  136.4 5.2 %product.4 = (bf16[256,512]{1,0:T(8,128)(2,1)}, bf16[256,512]{1,0:T(8,128)(2,1)}, bf16[256,512]{1,0:T(8,128)(2,1)}, bf16[256,512]{1,0:T(8,128)(2,1)}) custom-call(s32[5]{0:T(128)} %stack.36.flag_ref, s32[4]{0:T(128)} %pad_add_fusion.place_ref, bf16[2,256,1024]{2,1,0:T(8,128)(2,1)} %gated_conv.1.refs_0_, ...), custom_call_target="tpu_custom_call" | custom-call | flops 1073741824 | bytes 3145728 | tf_op jit(solution)/shard_map/product/pallas_call | solution.py:247
  146.7 4.1 %product.5 = (bf16[256,256]{1,0:T(8,128)(2,1)}, bf16[256,256]{1,0:T(8,128)(2,1)}, bf16[256,256]{1,0:T(8,128)(2,1)}, bf16[256,256]{1,0:T(8,128)(2,1)}) custom-call(s32[5]{0:T(128)} %stack.36.flag_ref, s32[4]{0:T(128)} %pad_add_fusion.place_ref, bf16[2,256,1024]{2,1,0:T(8,128)(2,1)} %gated_conv.1.refs_0_, ...), custom_call_target="tpu_custom_call" | custom-call | flops 536870912 | bytes 2621440 | tf_op jit(solution)/shard_map/product/pallas_call | solution.py:247
  154.4 2.8 %collective-permute-done.23.refs_2_ = bf16[256,512]{1,0:T(8,128)(2,1)S(1)} collective-permute-done((bf16[256,512]{1,0:T(8,128)(2,1)}, bf16[256,512]{1,0:T(8,128)(2,1)S(1)}, u32[]{:S(2)}, u32[]{:S(2)}) %collective-permute-start.23) | collective-permute-done | bytes 262176 | tf_op jit(solution)/shard_map/ppermute | solution.py:150
  159.1 2.6 %collective-permute-done.28.refs_6_ = bf16[256,256]{1,0:T(8,128)(2,1)S(1)} collective-permute-done((bf16[256,256]{1,0:T(8,128)(2,1)}, bf16[256,256]{1,0:T(8,128)(2,1)S(1)}, u32[]{:S(2)}, u32[]{:S(2)}) %collective-permute-start.28) | collective-permute-done | bytes 131104 | tf_op jit(solution)/shard_map/ppermute | solution.py:150
  (92 shorter events, 42.2 us)
Async XLA Ops:
  2.7 19.0 %collective-permute-start.2 = (bf16[256,768]{1,0:T(8,128)(2,1)}, bf16[256,768]{1,0:T(8,128)(2,1)S(1)}, u32[]{:S(2)}, u32[]{:S(2)}) collective-permute-start(bf16[256,768]{1,0:T(8,128)(2,1)} %get-tuple-element.208.refs_8_), channel_id=1, source_target_pairs={{0,8},{2,10},{4,12},{6,14},{8,0},{10,2},{12,4},{14,6},{16,24},{18,... | collective-permute-start | bytes 1179656 | tf_op jit(solution)/shard_map/ppermute | solution.py:150
  2.7 20.7 %collective-permute-start.3 = (bf16[256,768]{1,0:T(8,128)(2,1)}, bf16[256,768]{1,0:T(8,128)(2,1)}, u32[]{:S(2)}, u32[]{:S(2)}) collective-permute-start(bf16[256,768]{1,0:T(8,128)(2,1)} %get-tuple-element.208.refs_8_), channel_id=1, source_target_pairs={{0,16},{2,18},{4,20},{6,22},{8,24},{10,26},{12,28},{14,30},{16,0},... | collective-permute-start | bytes 1179656 | tf_op jit(solution)/shard_map/ppermute | solution.py:150
  25.8 26.9 %collective-permute-start.6 = (bf16[256,768]{1,0:T(8,128)(2,1)}, bf16[256,768]{1,0:T(8,128)(2,1)S(1)}, u32[]{:S(2)}, u32[]{:S(2)}) collective-permute-start(bf16[256,768]{1,0:T(8,128)(2,1)} %get-tuple-element.204), channel_id=1, source_target_pairs={{0,2},{2,0},{4,6},{6,4},{8,10},{10,8},{12,14},{14,12},{16,18},{18,... | collective-permute-start | bytes 1179656 | tf_op jit(solution)/shard_map/ppermute | solution.py:150
  27.3 25.3 %collective-permute-start.7 = (bf16[256,768]{1,0:T(8,128)(2,1)}, bf16[256,768]{1,0:T(8,128)(2,1)}, u32[]{:S(2)}, u32[]{:S(2)}) collective-permute-start(bf16[256,768]{1,0:T(8,128)(2,1)} %get-tuple-element.205), channel_id=1, source_target_pairs={{0,4},{2,6},{4,0},{6,2},{8,12},{10,14},{12,8},{14,10},{16,20},{18,... | collective-permute-start | bytes 1179656 | tf_op jit(solution)/shard_map/ppermute | solution.py:150
  28.8 23.8 %collective-permute-start.8 = (bf16[256,768]{1,0:T(8,128)(2,1)}, bf16[256,768]{1,0:T(8,128)(2,1)}, u32[]{:S(2)}, u32[]{:S(2)}) collective-permute-start(bf16[256,768]{1,0:T(8,128)(2,1)} %get-tuple-element.206), channel_id=1, source_target_pairs={{0,6},{2,4},{4,2},{6,0},{8,14},{10,12},{12,10},{14,8},{16,22},{18,... | collective-permute-start | bytes 1179656 | tf_op jit(solution)/shard_map/ppermute | solution.py:150
  31.5 9.3 %collective-permute-start.5 = (f32[16,16,128]{2,1,0:T(8,128)S(1)}, f32[16,16,128]{2,1,0:T(8,128)S(1)}, u32[]{:S(2)}, u32[]{:S(2)}) collective-permute-start(f32[16,16,128]{2,1,0:T(8,128)S(1)} %multiply_add_fusion), channel_id=1, source_target_pairs={{0,16},{2,18},{4,20},{6,22},{8,24},{10,26},{12,28},{14,30},{1,17},... | collective-permute-start | bytes 393224 | tf_op jit(solution)/shard_map/ppermute | solution.py:145
  40.8 13.1 %collective-permute-start.10 = (bf16[256,768]{1,0:T(8,128)(2,1)}, bf16[256,768]{1,0:T(8,128)(2,1)S(1)}, u32[]{:S(2)}, u32[]{:S(2)}) collective-permute-start(bf16[256,768]{1,0:T(8,128)(2,1)} %get-tuple-element.208.refs_8_), channel_id=1, source_target_pairs={{8,16},{10,18},{12,20},{14,22},{16,8},{18,10},{20,12},{22,14},{9,1... | collective-permute-start | bytes 1179656 | tf_op jit(solution)/shard_map/ppermute | solution.py:323
  42.8 11.2 %collective-permute-start.9 = (bf16[256,768]{1,0:T(8,128)(2,1)}, bf16[256,768]{1,0:T(8,128)(2,1)S(1)}, u32[]{:S(2)}, u32[]{:S(2)}) collective-permute-start(bf16[256,768]{1,0:T(8,128)(2,1)} %collective-permute-done.3.refs_12_), channel_id=1, source_target_pairs={{8,0},{10,2},{12,4},{14,6},{16,24},{18,26},{20,28},{22,30},{9,1},{... | collective-permute-start | bytes 1179656 | tf_op jit(solution)/shard_map/ppermute | solution.py:326
  54.1 26.2 %collective-permute-start.13 = (bf16[2,256,1024]{2,1,0:T(8,128)(2,1)S(1)}, bf16[2,256,1024]{2,1,0:T(8,128)(2,1)}, u32[]{:S(2)}, u32[]{:S(2)}) collective-permute-start(bf16[2,256,1024]{2,1,0:T(8,128)(2,1)S(1)} %copy-done.5), channel_id=1, source_target_pairs={{0,2},{2,0},{4,6},{6,4},{8,10},{10,8},{12,14},{14,12},{16,18},{18,... | collective-permute-start | bytes 3145736 | tf_op jit(solution)/shard_map/ppermute | solution.py:150
  55.6 46.0 %collective-permute-start.11 = (bf16[768,768]{1,0:T(8,128)(2,1)S(1)}, bf16[768,768]{1,0:T(8,128)(2,1)}, u32[]{:S(2)}, u32[]{:S(2)}) collective-permute-start(bf16[768,768]{1,0:T(8,128)(2,1)S(1)} %pad_maximum_fusion.refs_9_), channel_id=1, source_target_pairs={{0,16},{2,18},{4,20},{6,22},{8,24},{10,26},{12,28},{14,30},{16,0},... | collective-permute-start | bytes 3538952 | tf_op jit(solution)/shard_map/ppermute | solution.py:150
  59.3 45.1 %collective-permute-start.12 = (bf16[768,768]{1,0:T(8,128)(2,1)S(1)}, bf16[768,768]{1,0:T(8,128)(2,1)}, u32[]{:S(2)}, u32[]{:S(2)}) collective-permute-start(bf16[768,768]{1,0:T(8,128)(2,1)S(1)} %pad_maximum_fusion.refs_9_), channel_id=1, source_target_pairs={{0,8},{2,10},{4,12},{6,14},{8,0},{10,2},{12,4},{14,6},{16,24},{18,... | collective-permute-start | bytes 3538952 | tf_op jit(solution)/shard_map/ppermute | solution.py:150
  60.3 39.9 %collective-permute-start.15 = (bf16[2,256,1024]{2,1,0:T(8,128)(2,1)S(1)}, bf16[2,256,1024]{2,1,0:T(8,128)(2,1)}, u32[]{:S(2)}, u32[]{:S(2)}) collective-permute-start(bf16[2,256,1024]{2,1,0:T(8,128)(2,1)S(1)} %copy-done.5), channel_id=1, source_target_pairs={{0,4},{2,6},{4,0},{6,2},{8,12},{10,14},{12,8},{14,10},{16,20},{18,... | collective-permute-start | bytes 3145736 | tf_op jit(solution)/shard_map/ppermute | solution.py:150
  61.8 38.4 %collective-permute-start.16 = (bf16[2,256,1024]{2,1,0:T(8,128)(2,1)S(1)}, bf16[2,256,1024]{2,1,0:T(8,128)(2,1)}, u32[]{:S(2)}, u32[]{:S(2)}) collective-permute-start(bf16[2,256,1024]{2,1,0:T(8,128)(2,1)S(1)} %copy-done.5), channel_id=1, source_target_pairs={{0,6},{2,4},{4,2},{6,0},{8,14},{10,12},{12,10},{14,8},{16,22},{18,... | collective-permute-start | bytes 3145736 | tf_op jit(solution)/shard_map/ppermute | solution.py:150
  80.3 24.1 %collective-permute-start.14 = (bf16[2,256,1024]{2,1,0:T(8,128)(2,1)}, bf16[2,256,1024]{2,1,0:T(8,128)(2,1)}, u32[]{:S(2)}, u32[]{:S(2)}) collective-permute-start(bf16[2,256,1024]{2,1,0:T(8,128)(2,1)} %collective-permute-done.13.refs_1_), channel_id=1, source_target_pairs={{0,1},{1,0},{2,3},{3,2},{4,5},{5,4},{6,7},{7,6},{8,9},{9,8},{10,11... | collective-permute-start | bytes 3145736 | tf_op jit(solution)/shard_map/ppermute | solution.py:150
  104.4 10.2 %collective-permute-start.18 = (bf16[2,256,1024]{2,1,0:T(8,128)(2,1)}, bf16[2,256,1024]{2,1,0:T(8,128)(2,1)}, u32[]{:S(2)}, u32[]{:S(2)}) collective-permute-start(bf16[2,256,1024]{2,1,0:T(8,128)(2,1)} %collective-permute-done.15.refs_2_), channel_id=1, source_target_pairs={{0,1},{1,0},{2,3},{3,2},{4,5},{5,4},{6,7},{7,6},{8,9},{9,8},{10,11... | collective-permute-start | bytes 3145736 | tf_op jit(solution)/shard_map/ppermute | solution.py:150
  104.9 9.7 %collective-permute-start.19 = (bf16[2,256,1024]{2,1,0:T(8,128)(2,1)}, bf16[2,256,1024]{2,1,0:T(8,128)(2,1)}, u32[]{:S(2)}, u32[]{:S(2)}) collective-permute-start(bf16[2,256,1024]{2,1,0:T(8,128)(2,1)} %collective-permute-done.16.refs_3_), channel_id=1, source_target_pairs={{0,1},{1,0},{2,3},{3,2},{4,5},{5,4},{6,7},{7,6},{8,9},{9,8},{10,11... | collective-permute-start | bytes 3145736 | tf_op jit(solution)/shard_map/ppermute | solution.py:150
  107.0 20.2 %collective-permute-start.20 = (bf16[768,512]{1,0:T(8,128)(2,1)}, bf16[768,512]{1,0:T(8,128)(2,1)}, u32[]{:S(2)}, u32[]{:S(2)}) collective-permute-start(bf16[768,512]{1,0:T(8,128)(2,1)} %slice.14), channel_id=1, source_target_pairs={{8,0},{10,2},{12,4},{14,6},{16,24},{18,26},{20,28},{22,30},{9,1},{... | collective-permute-start | bytes 2359304 | tf_op jit(solution)/shard_map/ppermute | solution.py:326
  110.1 21.7 %collective-permute-start.21 = (bf16[768,512]{1,0:T(8,128)(2,1)}, bf16[768,512]{1,0:T(8,128)(2,1)S(1)}, u32[]{:S(2)}, u32[]{:S(2)}) collective-permute-start(bf16[768,512]{1,0:T(8,128)(2,1)} %slice.12), channel_id=1, source_target_pairs={{8,16},{10,18},{12,20},{14,22},{16,8},{18,10},{20,12},{22,14},{9,1... | collective-permute-start | bytes 2359304 | tf_op jit(solution)/shard_map/ppermute | solution.py:323
  131.8 13.4 %collective-permute-start.25 = (bf16[768,256]{1,0:T(8,128)(2,1)S(1)}, bf16[768,256]{1,0:T(8,128)(2,1)S(1)}, u32[]{:S(2)}, u32[]{:S(2)}) collective-permute-start(bf16[768,256]{1,0:T(8,128)(2,1)S(1)} %slice.15), channel_id=1, source_target_pairs={{8,0},{10,2},{12,4},{14,6},{16,24},{18,26},{20,28},{22,30},{9,1},{... | collective-permute-start | bytes 1179656 | tf_op jit(solution)/shard_map/ppermute | solution.py:326
  133.1 12.2 %collective-permute-start.26 = (bf16[768,256]{1,0:T(8,128)(2,1)S(1)}, bf16[768,256]{1,0:T(8,128)(2,1)S(1)}, u32[]{:S(2)}, u32[]{:S(2)}) collective-permute-start(bf16[768,256]{1,0:T(8,128)(2,1)S(1)} %copy-done.13), channel_id=1, source_target_pairs={{8,16},{10,18},{12,20},{14,22},{16,8},{18,10},{20,12},{22,14},{9,1... | collective-permute-start | bytes 1179656 | tf_op jit(solution)/shard_map/ppermute | solution.py:323
  141.6 12.3 %collective-permute-start.22 = (bf16[256,512]{1,0:T(8,128)(2,1)}, bf16[256,512]{1,0:T(8,128)(2,1)S(1)}, u32[]{:S(2)}, u32[]{:S(2)}) collective-permute-start(bf16[256,512]{1,0:T(8,128)(2,1)} %get-tuple-element.239), channel_id=1, source_target_pairs={{0,2},{2,0},{4,6},{6,4},{8,10},{10,8},{12,14},{14,12},{16,18},{18,... | collective-permute-start | bytes 786440 | tf_op jit(solution)/shard_map/ppermute | solution.py:150
  143.2 13.9 %collective-permute-start.23 = (bf16[256,512]{1,0:T(8,128)(2,1)}, bf16[256,512]{1,0:T(8,128)(2,1)S(1)}, u32[]{:S(2)}, u32[]{:S(2)}) collective-permute-start(bf16[256,512]{1,0:T(8,128)(2,1)} %get-tuple-element.240), channel_id=1, source_target_pairs={{0,4},{2,6},{4,0},{6,2},{8,12},{10,14},{12,8},{14,10},{16,20},{18,... | collective-permute-start | bytes 786440 | tf_op jit(solution)/shard_map/ppermute | solution.py:150
  144.7 13.1 %collective-permute-start.24 = (bf16[256,512]{1,0:T(8,128)(2,1)}, bf16[256,512]{1,0:T(8,128)(2,1)S(1)}, u32[]{:S(2)}, u32[]{:S(2)}) collective-permute-start(bf16[256,512]{1,0:T(8,128)(2,1)} %get-tuple-element.241), channel_id=1, source_target_pairs={{0,6},{2,4},{4,2},{6,0},{8,14},{10,12},{12,10},{14,8},{16,22},{18,... | collective-permute-start | bytes 786440 | tf_op jit(solution)/shard_map/ppermute | solution.py:150
  152.4 9.3 %collective-permute-start.28 = (bf16[256,256]{1,0:T(8,128)(2,1)}, bf16[256,256]{1,0:T(8,128)(2,1)S(1)}, u32[]{:S(2)}, u32[]{:S(2)}) collective-permute-start(bf16[256,256]{1,0:T(8,128)(2,1)} %get-tuple-element.246), channel_id=1, source_target_pairs={{0,4},{2,6},{4,0},{6,2},{8,12},{10,14},{12,8},{14,10},{16,20},{18,... | collective-permute-start | bytes 393224 | tf_op jit(solution)/shard_map/ppermute | solution.py:150
  (24 other events, 312.0 us)

commit v22 on v21

--- a/solution.py
+++ b/solution.py
@@ -39,7 +39,7 @@
         return tuple(d * h + s for d, h in zip(decay, state))
 
     zero = jnp.zeros((groups, LANES), jnp.float32)
-    state = lax.fori_loop(0, rows, step, (zero,) * modes, unroll=8)
+    state = lax.fori_loop(0, rows, step, (zero,) * modes, unroll=16)
     for m in range(modes):
         end_ref[m] = state[m]
 
@@ -73,7 +73,7 @@
         conv_ref[at, :] = terms[0]
         return state
 
-    lax.fori_loop(0, rows, step, tuple(enter), unroll=4)
+    lax.fori_loop(0, rows, step, tuple(enter), unroll=8)
     for g in range(groups):
         cols = pl.ds(g * LANES, LANES)
         conv = conv_ref[pl.ds(g, rows, stride=groups), :]
@@ -227,13 +227,13 @@
             block = weight_buf.at[pl.ds(b * depth, depth), :]
             pltpu.make_async_copy(block, block, weight_sems.at[b]).wait()
             pltpu.make_async_copy(gated_buf.at[b], gated_buf.at[b], gated_sems.at[b]).wait()
-            if accs and not b:
-                pltpu.make_async_copy(acc_buf, acc_buf, acc_sem).wait()
             for col in range(0, cols, 2 * LANES):
                 here = pl.ds(col, min(2 * LANES, cols - col))
                 made = jnp.dot(
                     gated_buf[b], weight_buf[pl.ds(b * depth, depth), here], preferred_element_type=jnp.float32
                 )
+                if accs and not b and not col:
+                    pltpu.make_async_copy(acc_buf, acc_buf, acc_sem).wait()
                 for r in range(parts):
                     total = made[r * rows : (r + 1) * rows]
                     if b:

time: 165 us -> 166 us (level)
  transfers between devices with their start and end apart: 30 -> 30, of which waited for: 15 -> 14; matrix products, arithmetic and copies ran while one was open for 6% -> 6% of each run, Pallas kernels for 21% -> 21%
where the time goes in v22:
time: 166 us
  waiting for transfers between devices  65.5 us (39%)
  starting transfers between devices  47.2 us (28%)
  Pallas kernels  36.9 us (22%)
  local copies, waits for them, and re-layouts  10.9 us (7%)
  other arithmetic  4.64 us (3%)
    ppermute x22, waiting for transfers between devices, exchange(): return lax.ppermute(x, axis, [(i, i ^ flip) for i in range(count)])  55.3 us
    ppermute x22, starting transfers between devices, exchange(): return lax.ppermute(x, axis, [(i, i ^ flip) for i in range(count)])  25.5 us
    pallas_call x3, Pallas kernels, product(): pl.pallas_call(kernel, in_specs=[smem, smem] + [anywhere] * (2 * parts +...  23.2 us
    ppermute x3, starting transfers between devices, across(): return lax.ppermute(x, 'ctx', [(i, i ^ 3 * PLANE) for i in middle])  9.08 us
    pallas_call x1, Pallas kernels, gated_conv(): pl.pallas_call(conv_kernel, grid=(chan // width,), in_specs=[wide, wide,...  8.16 us
    ppermute x2, starting transfers between devices, shift_ctx(): return lax.ppermute(x, 'ctx', [(i, i + by) for i in range(count - by)])  6.85 us
    ppermute x2, waiting for transfers between devices, shift_ctx(): return lax.ppermute(x, 'ctx', [(i, i + by) for i in range(count - by)])  5.98 us
    ppermute x3, starting transfers between devices, outward(): return lax.ppermute(x, 'ctx', [(i, i ^ PLANE) for i in middle])  5.72 us
  transfers between devices with their start and end apart: 30, of which 14 were waited for; matrix products, arithmetic and copies ran while one was open for 6% of the time, Pallas kernels for 21%

profile of v22, /device:TPU:8, one launch (start us, length us, event | category | flops | bytes accessed | tf_op | source)
XLA Modules:
  0.0 165.5 jit_solution(9273442914848026404)
XLA Ops:
  0.0 2.7 %constant_dynamic-slice_fusion = (bf16[256,768]{1,0:T(8,128)(2,1)}, bf16[256,768]{1,0:T(8,128)(2,1)}, bf16[256,768]{1,0:T(8,128)(2,1)}, bf16[256,768]{1,0:T(8,128)(2,1)}) fusion(bf16[256,3072]{1,0:T(8,128)(2,1)} %param.15, s32[]{:T(128)S(6)} %select_n.84, s32[]{:T(128)S(6)} %select_n.82, s32[]{:T(128)S(6)} %select_n.81, s32[]{:T(128)S(6)} %select_n.83), kind=kLoop, calls=%fused_computation.5 | loop fusion | bytes 3145744 | tf_op jit(solution)/shard_map/dynamic_slice | solution.py:329
  2.7 3.0 %collective-permute-start.3 = (bf16[256,768]{1,0:T(8,128)(2,1)}, bf16[256,768]{1,0:T(8,128)(2,1)}, u32[]{:S(2)}, u32[]{:S(2)}) collective-permute-start(bf16[256,768]{1,0:T(8,128)(2,1)} %get-tuple-element.208.refs_8_), channel_id=1, source_target_pairs={{0,16},{2,18},{4,20},{6,22},{8,24},{10,26},{12,28},{14,30},{16,0},... | collective-permute-start | bytes 1179656 | tf_op jit(solution)/shard_map/ppermute | solution.py:150
  5.8 15.8 %while.14 = (s32[]{:T(128)}, f32[16,16,128]{2,1,0:T(8,128)}, f32[16,16,128]{2,1,0:T(8,128)}, s32[]{:T(128)}, pred[]{:T(512)}, /*index=5*/bf16[256,2048]{1,0:T(8,...) while((s32[]{:T(128)}, f32[16,16,128]{2,1,0:T(8,128)}, ...), condition=%wide.region_1.2_spmd, body=%wide.region_0.1_spmd.sunk | while | flops 17399808 | bytes 4456652 | solution.py:185
  5.8 3.9 %end_states.3 = f32[16,16,128]{2,1,0:T(8,128)} custom-call(bf16[256,2048]{1,0:T(8,128)(2,1)S(1)} %get-tuple-element.346.k_ref, bf16[256,2048]{1,0:T(8,128)(2,1)S(1)} %get-tuple-element.347.v_ref, f32[16,2048]{1,0:T(8,128)S(1)} %get-tuple-element.348.rate_ref), custom_call_target="tpu_custom_call" | custom-call | flops 16777216 | bytes 2097152 | tf_op jit(solution)/shard_map/while/body/end_states/pallas_call | solution.py:98
  11.2 3.7 %collective-permute-done = f32[16,16,128]{2,1,0:T(8,128)S(1)} collective-permute-done((f32[16,16,128]{2,1,0:T(8,128)}, f32[16,16,128]{2,1,0:T(8,128)S(1)}, u32[]{:S(2)}, u32[]{:S(2)}) %collective-permute-start) | collective-permute-done | bytes 131104 | tf_op jit(solution)/shard_map/while/body/ppermute | solution.py:150
  17.4 3.4 %collective-permute-done.1 = f32[16,16,128]{2,1,0:T(8,128)S(1)} collective-permute-done((f32[16,16,128]{2,1,0:T(8,128)S(1)}, f32[16,16,128]{2,1,0:T(8,128)S(1)}, u32[]{:S(2)}, u32[]{:S(2)}) %collective-permute-start.1) | collective-permute-done | bytes 131104 | tf_op jit(solution)/shard_map/while/body/ppermute | solution.py:150
  23.4 2.3 %collective-permute-start.4 = (f32[16,16,128]{2,1,0:T(8,128)}, f32[16,16,128]{2,1,0:T(8,128)S(1)}, u32[]{:S(2)}, u32[]{:S(2)}) collective-permute-start(f32[16,16,128]{2,1,0:T(8,128)} %get-tuple-element.200), channel_id=1, source_target_pairs={{0,8},{2,10},{4,12},{6,14},{8,16},{10,18},{12,20},{14,22},{16,24},... | collective-permute-start | bytes 393224 | tf_op jit(solution)/shard_map/ppermute | solution.py:145
  31.5 4.5 %collective-permute-start.5 = (f32[16,16,128]{2,1,0:T(8,128)S(1)}, f32[16,16,128]{2,1,0:T(8,128)S(1)}, u32[]{:S(2)}, u32[]{:S(2)}) collective-permute-start(f32[16,16,128]{2,1,0:T(8,128)S(1)} %multiply_add_fusion), channel_id=1, source_target_pairs={{0,16},{2,18},{4,20},{6,22},{8,24},{10,26},{12,28},{14,30},{1,17},... | collective-permute-start | bytes 393224 | tf_op jit(solution)/shard_map/ppermute | solution.py:145
  36.0 4.8 %collective-permute-done.5.refs_1_ = f32[16,16,128]{2,1,0:T(8,128)S(1)} collective-permute-done((f32[16,16,128]{2,1,0:T(8,128)S(1)}, f32[16,16,128]{2,1,0:T(8,128)S(1)}, u32[]{:S(2)}, u32[]{:S(2)}) %collective-permute-start.5) | collective-permute-done | bytes 131104 | tf_op jit(solution)/shard_map/ppermute | solution.py:145
  44.1 8.2 %gated_conv.1.refs_0_ = bf16[2,256,1024]{2,1,0:T(8,128)(2,1)} custom-call(bf16[256,2048]{1,0:T(8,128)(2,1)} %q_ref.1, bf16[256,2048]{1,0:T(8,128)(2,1)S(1)} %get-tuple-element.394, bf16[256,2048]{1,0:T(8,128)(2,1)S(1)} %get-tuple-element.395, f32[16,2048]{1,0:T(8,128)S(1)} %get-tuple-element.404, f32[16,2048]{1,0:T(8,128)} %residue_ref.1, ...), custom_call_target="tpu_custom_call" | custom-call | flops 33554432 | bytes 4194304 | tf_op jit(solution)/shard_map/gated_conv/pallas_call | solution.py:128
  55.2 4.4 %collective-permute-start.11 = (bf16[768,768]{1,0:T(8,128)(2,1)S(1)}, bf16[768,768]{1,0:T(8,128)(2,1)}, u32[]{:S(2)}, u32[]{:S(2)}) collective-permute-start(bf16[768,768]{1,0:T(8,128)(2,1)S(1)} %pad_maximum_fusion.refs_9_), channel_id=1, source_target_pairs={{0,16},{2,18},{4,20},{6,22},{8,24},{10,26},{12,28},{14,30},{16,0},... | collective-permute-start | bytes 3538952 | tf_op jit(solution)/shard_map/ppermute | solution.py:150
  62.0 18.0 %collective-permute-done.13.refs_1_ = bf16[2,256,1024]{2,1,0:T(8,128)(2,1)} collective-permute-done((bf16[2,256,1024]{2,1,0:T(8,128)(2,1)S(1)}, bf16[2,256,1024]{2,1,0:T(8,128)(2,1)}, u32[]{:S(2)}, u32[]{:S(2)}) %collective-permute-start.13) | collective-permute-done | bytes 1048608 | tf_op jit(solution)/shard_map/ppermute | solution.py:150
  82.9 16.9 %collective-permute-done.15.refs_2_ = bf16[2,256,1024]{2,1,0:T(8,128)(2,1)} collective-permute-done((bf16[2,256,1024]{2,1,0:T(8,128)(2,1)S(1)}, bf16[2,256,1024]{2,1,0:T(8,128)(2,1)}, u32[]{:S(2)}, u32[]{:S(2)}) %collective-permute-start.15) | collective-permute-done | bytes 1048608 | tf_op jit(solution)/shard_map/ppermute | solution.py:150
  101.2 2.8 %collective-permute-done.12.refs_11_ = bf16[768,768]{1,0:T(8,128)(2,1)} collective-permute-done((bf16[768,768]{1,0:T(8,128)(2,1)S(1)}, bf16[768,768]{1,0:T(8,128)(2,1)}, u32[]{:S(2)}, u32[]{:S(2)}) %collective-permute-start.12) | collective-permute-done | bytes 1179680 | tf_op jit(solution)/shard_map/ppermute | solution.py:150
  104.6 2.1 %slice.14 = bf16[768,512]{1,0:T(8,128)(2,1)} slice(bf16[768,768]{1,0:T(8,128)(2,1)} %collective-permute-done.11.refs_13_), slice={[0:768], [0:512]} | slice | bytes 1572864 | tf_op jit(solution)/shard_map/slice | solution.py:376
  106.6 3.1 %collective-permute-start.20 = (bf16[768,512]{1,0:T(8,128)(2,1)}, bf16[768,512]{1,0:T(8,128)(2,1)}, u32[]{:S(2)}, u32[]{:S(2)}) collective-permute-start(bf16[768,512]{1,0:T(8,128)(2,1)} %slice.14), channel_id=1, source_target_pairs={{8,0},{10,2},{12,4},{14,6},{16,24},{18,26},{20,28},{22,30},{9,1},{... | collective-permute-start | bytes 2359304 | tf_op jit(solution)/shard_map/ppermute | solution.py:326
  109.7 3.5 %collective-permute-start.21 = (bf16[768,512]{1,0:T(8,128)(2,1)}, bf16[768,512]{1,0:T(8,128)(2,1)S(1)}, u32[]{:S(2)}, u32[]{:S(2)}) collective-permute-start(bf16[768,512]{1,0:T(8,128)(2,1)} %slice.12), channel_id=1, source_target_pairs={{8,16},{10,18},{12,20},{14,22},{16,8},{18,10},{20,12},{22,14},{9,1... | collective-permute-start | bytes 2359304 | tf_op jit(solution)/shard_map/ppermute | solution.py:323
  114.6 12.5 %product.3 = (f32[256,768]{1,0:T(8,128)}, f32[256,768]{1,0:T(8,128)}, f32[256,768]{1,0:T(8,128)}, f32[256,768]{1,0:T(8,128)}) custom-call(s32[5]{0:T(128)} %stack.36.flag_ref, s32[4]{0:T(128)} %pad_add_fusion.place_ref, bf16[2,256,1024]{2,1,0:T(8,128)(2,1)} %gated_conv.1.refs_0_, bf16[2,256,1024]{2,1,0:T(8,128)(2,1)} %collective-permute-done.13.refs_1_, ...), custom_call_target="tpu_custom_call" | custom-call | flops 4831838208 | bytes 11010048 | tf_op jit(solution)/shard_map/product/pallas_call | solution.py:247
  127.2 4.2 %collective-permute-done.21.refs_11_ = bf16[768,512]{1,0:T(8,128)(2,1)S(1)} collective-permute-done((bf16[768,512]{1,0:T(8,128)(2,1)}, bf16[768,512]{1,0:T(8,128)(2,1)S(1)}, u32[]{:S(2)}, u32[]{:S(2)}) %collective-permute-start.21) | collective-permute-done | bytes 786464 | tf_op jit(solution)/shard_map/ppermute | solution.py:323
  132.8 3.6 %collective-permute-start.26 = (bf16[768,256]{1,0:T(8,128)(2,1)S(1)}, bf16[768,256]{1,0:T(8,128)(2,1)S(1)}, u32[]{:S(2)}, u32[]{:S(2)}) collective-permute-start(bf16[768,256]{1,0:T(8,128)(2,1)S(1)} %copy-done.13), channel_id=1, source_target_pairs={{8,16},{10,18},{12,20},{14,22},{16,8},{18,10},{20,12},{22,14},{9,1... | collective-permute-start | bytes 1179656 | tf_op jit(solution)/shard_map/ppermute | solution.py:323
  136.4 6.4 %product.4 = (bf16[256,512]{1,0:T(8,128)(2,1)}, bf16[256,512]{1,0:T(8,128)(2,1)}, bf16[256,512]{1,0:T(8,128)(2,1)}, bf16[256,512]{1,0:T(8,128)(2,1)}) custom-call(s32[5]{0:T(128)} %stack.36.flag_ref, s32[4]{0:T(128)} %pad_add_fusion.place_ref, bf16[2,256,1024]{2,1,0:T(8,128)(2,1)} %gated_conv.1.refs_0_, ...), custom_call_target="tpu_custom_call" | custom-call | flops 1073741824 | bytes 3145728 | tf_op jit(solution)/shard_map/product/pallas_call | solution.py:247
  147.9 4.2 %product.5 = (bf16[256,256]{1,0:T(8,128)(2,1)}, bf16[256,256]{1,0:T(8,128)(2,1)}, bf16[256,256]{1,0:T(8,128)(2,1)}, bf16[256,256]{1,0:T(8,128)(2,1)}) custom-call(s32[5]{0:T(128)} %stack.36.flag_ref, s32[4]{0:T(128)} %pad_add_fusion.place_ref, bf16[2,256,1024]{2,1,0:T(8,128)(2,1)} %gated_conv.1.refs_0_, ...), custom_call_target="tpu_custom_call" | custom-call | flops 536870912 | bytes 2621440 | tf_op jit(solution)/shard_map/product/pallas_call | solution.py:247
  155.6 2.7 %collective-permute-done.23.refs_2_ = bf16[256,512]{1,0:T(8,128)(2,1)S(1)} collective-permute-done((bf16[256,512]{1,0:T(8,128)(2,1)}, bf16[256,512]{1,0:T(8,128)(2,1)S(1)}, u32[]{:S(2)}, u32[]{:S(2)}) %collective-permute-start.23) | collective-permute-done | bytes 262176 | tf_op jit(solution)/shard_map/ppermute | solution.py:150
  160.3 2.6 %collective-permute-done.28.refs_6_ = bf16[256,256]{1,0:T(8,128)(2,1)S(1)} collective-permute-done((bf16[256,256]{1,0:T(8,128)(2,1)}, bf16[256,256]{1,0:T(8,128)(2,1)S(1)}, u32[]{:S(2)}, u32[]{:S(2)}) %collective-permute-start.28) | collective-permute-done | bytes 131104 | tf_op jit(solution)/shard_map/ppermute | solution.py:150
  (92 shorter events, 41.6 us)
Async XLA Ops:
  2.7 18.9 %collective-permute-start.2 = (bf16[256,768]{1,0:T(8,128)(2,1)}, bf16[256,768]{1,0:T(8,128)(2,1)S(1)}, u32[]{:S(2)}, u32[]{:S(2)}) collective-permute-start(bf16[256,768]{1,0:T(8,128)(2,1)} %get-tuple-element.208.refs_8_), channel_id=1, source_target_pairs={{0,8},{2,10},{4,12},{6,14},{8,0},{10,2},{12,4},{14,6},{16,24},{18,... | collective-permute-start | bytes 1179656 | tf_op jit(solution)/shard_map/ppermute | solution.py:150
  2.7 20.7 %collective-permute-start.3 = (bf16[256,768]{1,0:T(8,128)(2,1)}, bf16[256,768]{1,0:T(8,128)(2,1)}, u32[]{:S(2)}, u32[]{:S(2)}) collective-permute-start(bf16[256,768]{1,0:T(8,128)(2,1)} %get-tuple-element.208.refs_8_), channel_id=1, source_target_pairs={{0,16},{2,18},{4,20},{6,22},{8,24},{10,26},{12,28},{14,30},{16,0},... | collective-permute-start | bytes 1179656 | tf_op jit(solution)/shard_map/ppermute | solution.py:150
  25.8 26.5 %collective-permute-start.6 = (bf16[256,768]{1,0:T(8,128)(2,1)}, bf16[256,768]{1,0:T(8,128)(2,1)S(1)}, u32[]{:S(2)}, u32[]{:S(2)}) collective-permute-start(bf16[256,768]{1,0:T(8,128)(2,1)} %get-tuple-element.204), channel_id=1, source_target_pairs={{0,2},{2,0},{4,6},{6,4},{8,10},{10,8},{12,14},{14,12},{16,18},{18,... | collective-permute-start | bytes 1179656 | tf_op jit(solution)/shard_map/ppermute | solution.py:150
  27.3 25.0 %collective-permute-start.7 = (bf16[256,768]{1,0:T(8,128)(2,1)}, bf16[256,768]{1,0:T(8,128)(2,1)}, u32[]{:S(2)}, u32[]{:S(2)}) collective-permute-start(bf16[256,768]{1,0:T(8,128)(2,1)} %get-tuple-element.205), channel_id=1, source_target_pairs={{0,4},{2,6},{4,0},{6,2},{8,12},{10,14},{12,8},{14,10},{16,20},{18,... | collective-permute-start | bytes 1179656 | tf_op jit(solution)/shard_map/ppermute | solution.py:150
  28.8 23.5 %collective-permute-start.8 = (bf16[256,768]{1,0:T(8,128)(2,1)}, bf16[256,768]{1,0:T(8,128)(2,1)}, u32[]{:S(2)}, u32[]{:S(2)}) collective-permute-start(bf16[256,768]{1,0:T(8,128)(2,1)} %get-tuple-element.206), channel_id=1, source_target_pairs={{0,6},{2,4},{4,2},{6,0},{8,14},{10,12},{12,10},{14,8},{16,22},{18,... | collective-permute-start | bytes 1179656 | tf_op jit(solution)/shard_map/ppermute | solution.py:150
  31.5 9.3 %collective-permute-start.5 = (f32[16,16,128]{2,1,0:T(8,128)S(1)}, f32[16,16,128]{2,1,0:T(8,128)S(1)}, u32[]{:S(2)}, u32[]{:S(2)}) collective-permute-start(f32[16,16,128]{2,1,0:T(8,128)S(1)} %multiply_add_fusion), channel_id=1, source_target_pairs={{0,16},{2,18},{4,20},{6,22},{8,24},{10,26},{12,28},{14,30},{1,17},... | collective-permute-start | bytes 393224 | tf_op jit(solution)/shard_map/ppermute | solution.py:145
  40.8 12.8 %collective-permute-start.10 = (bf16[256,768]{1,0:T(8,128)(2,1)}, bf16[256,768]{1,0:T(8,128)(2,1)S(1)}, u32[]{:S(2)}, u32[]{:S(2)}) collective-permute-start(bf16[256,768]{1,0:T(8,128)(2,1)} %get-tuple-element.208.refs_8_), channel_id=1, source_target_pairs={{8,16},{10,18},{12,20},{14,22},{16,8},{18,10},{20,12},{22,14},{9,1... | collective-permute-start | bytes 1179656 | tf_op jit(solution)/shard_map/ppermute | solution.py:323
  42.8 10.9 %collective-permute-start.9 = (bf16[256,768]{1,0:T(8,128)(2,1)}, bf16[256,768]{1,0:T(8,128)(2,1)S(1)}, u32[]{:S(2)}, u32[]{:S(2)}) collective-permute-start(bf16[256,768]{1,0:T(8,128)(2,1)} %collective-permute-done.3.refs_12_), channel_id=1, source_target_pairs={{8,0},{10,2},{12,4},{14,6},{16,24},{18,26},{20,28},{22,30},{9,1},{... | collective-permute-start | bytes 1179656 | tf_op jit(solution)/shard_map/ppermute | solution.py:326
  53.7 26.2 %collective-permute-start.13 = (bf16[2,256,1024]{2,1,0:T(8,128)(2,1)S(1)}, bf16[2,256,1024]{2,1,0:T(8,128)(2,1)}, u32[]{:S(2)}, u32[]{:S(2)}) collective-permute-start(bf16[2,256,1024]{2,1,0:T(8,128)(2,1)S(1)} %copy-done.5), channel_id=1, source_target_pairs={{0,2},{2,0},{4,6},{6,4},{8,10},{10,8},{12,14},{14,12},{16,18},{18,... | collective-permute-start | bytes 3145736 | tf_op jit(solution)/shard_map/ppermute | solution.py:150
  55.2 46.0 %collective-permute-start.11 = (bf16[768,768]{1,0:T(8,128)(2,1)S(1)}, bf16[768,768]{1,0:T(8,128)(2,1)}, u32[]{:S(2)}, u32[]{:S(2)}) collective-permute-start(bf16[768,768]{1,0:T(8,128)(2,1)S(1)} %pad_maximum_fusion.refs_9_), channel_id=1, source_target_pairs={{0,16},{2,18},{4,20},{6,22},{8,24},{10,26},{12,28},{14,30},{16,0},... | collective-permute-start | bytes 3538952 | tf_op jit(solution)/shard_map/ppermute | solution.py:150
  59.6 44.4 %collective-permute-start.12 = (bf16[768,768]{1,0:T(8,128)(2,1)S(1)}, bf16[768,768]{1,0:T(8,128)(2,1)}, u32[]{:S(2)}, u32[]{:S(2)}) collective-permute-start(bf16[768,768]{1,0:T(8,128)(2,1)S(1)} %pad_maximum_fusion.refs_9_), channel_id=1, source_target_pairs={{0,8},{2,10},{4,12},{6,14},{8,0},{10,2},{12,4},{14,6},{16,24},{18,... | collective-permute-start | bytes 3538952 | tf_op jit(solution)/shard_map/ppermute | solution.py:150
  60.0 39.9 %collective-permute-start.15 = (bf16[2,256,1024]{2,1,0:T(8,128)(2,1)S(1)}, bf16[2,256,1024]{2,1,0:T(8,128)(2,1)}, u32[]{:S(2)}, u32[]{:S(2)}) collective-permute-start(bf16[2,256,1024]{2,1,0:T(8,128)(2,1)S(1)} %copy-done.5), channel_id=1, source_target_pairs={{0,4},{2,6},{4,0},{6,2},{8,12},{10,14},{12,8},{14,10},{16,20},{18,... | collective-permute-start | bytes 3145736 | tf_op jit(solution)/shard_map/ppermute | solution.py:150
  61.5 38.4 %collective-permute-start.16 = (bf16[2,256,1024]{2,1,0:T(8,128)(2,1)S(1)}, bf16[2,256,1024]{2,1,0:T(8,128)(2,1)}, u32[]{:S(2)}, u32[]{:S(2)}) collective-permute-start(bf16[2,256,1024]{2,1,0:T(8,128)(2,1)S(1)} %copy-done.5), channel_id=1, source_target_pairs={{0,6},{2,4},{4,2},{6,0},{8,14},{10,12},{12,10},{14,8},{16,22},{18,... | collective-permute-start | bytes 3145736 | tf_op jit(solution)/shard_map/ppermute | solution.py:150
  79.9 24.1 %collective-permute-start.14 = (bf16[2,256,1024]{2,1,0:T(8,128)(2,1)}, bf16[2,256,1024]{2,1,0:T(8,128)(2,1)}, u32[]{:S(2)}, u32[]{:S(2)}) collective-permute-start(bf16[2,256,1024]{2,1,0:T(8,128)(2,1)} %collective-permute-done.13.refs_1_), channel_id=1, source_target_pairs={{0,1},{1,0},{2,3},{3,2},{4,5},{5,4},{6,7},{7,6},{8,9},{9,8},{10,11... | collective-permute-start | bytes 3145736 | tf_op jit(solution)/shard_map/ppermute | solution.py:150
  104.0 9.2 %collective-permute-start.17 = (bf16[2,256,1024]{2,1,0:T(8,128)(2,1)S(1)}, bf16[2,256,1024]{2,1,0:T(8,128)(2,1)S(1)}, u32[]{:S(2)}, u32[]{:S(2)}) collective-permute-start(bf16[2,256,1024]{2,1,0:T(8,128)(2,1)S(1)} %copy-done.5), channel_id=1, source_target_pairs={{0,1},{1,0},{2,3},{3,2},{4,5},{5,4},{6,7},{7,6},{8,9},{9,8},{10,11... | collective-permute-start | bytes 3145736 | tf_op jit(solution)/shard_map/ppermute | solution.py:150
  104.0 10.6 %collective-permute-start.18 = (bf16[2,256,1024]{2,1,0:T(8,128)(2,1)}, bf16[2,256,1024]{2,1,0:T(8,128)(2,1)}, u32[]{:S(2)}, u32[]{:S(2)}) collective-permute-start(bf16[2,256,1024]{2,1,0:T(8,128)(2,1)} %collective-permute-done.15.refs_2_), channel_id=1, source_target_pairs={{0,1},{1,0},{2,3},{3,2},{4,5},{5,4},{6,7},{7,6},{8,9},{9,8},{10,11... | collective-permute-start | bytes 3145736 | tf_op jit(solution)/shard_map/ppermute | solution.py:150
  104.6 10.1 %collective-permute-start.19 = (bf16[2,256,1024]{2,1,0:T(8,128)(2,1)}, bf16[2,256,1024]{2,1,0:T(8,128)(2,1)}, u32[]{:S(2)}, u32[]{:S(2)}) collective-permute-start(bf16[2,256,1024]{2,1,0:T(8,128)(2,1)} %collective-permute-done.16.refs_3_), channel_id=1, source_target_pairs={{0,1},{1,0},{2,3},{3,2},{4,5},{5,4},{6,7},{7,6},{8,9},{9,8},{10,11... | collective-permute-start | bytes 3145736 | tf_op jit(solution)/shard_map/ppermute | solution.py:150
  106.6 20.5 %collective-permute-start.20 = (bf16[768,512]{1,0:T(8,128)(2,1)}, bf16[768,512]{1,0:T(8,128)(2,1)}, u32[]{:S(2)}, u32[]{:S(2)}) collective-permute-start(bf16[768,512]{1,0:T(8,128)(2,1)} %slice.14), channel_id=1, source_target_pairs={{8,0},{10,2},{12,4},{14,6},{16,24},{18,26},{20,28},{22,30},{9,1},{... | collective-permute-start | bytes 2359304 | tf_op jit(solution)/shard_map/ppermute | solution.py:326
  109.7 21.7 %collective-permute-start.21 = (bf16[768,512]{1,0:T(8,128)(2,1)}, bf16[768,512]{1,0:T(8,128)(2,1)S(1)}, u32[]{:S(2)}, u32[]{:S(2)}) collective-permute-start(bf16[768,512]{1,0:T(8,128)(2,1)} %slice.12), channel_id=1, source_target_pairs={{8,16},{10,18},{12,20},{14,22},{16,8},{18,10},{20,12},{22,14},{9,1... | collective-permute-start | bytes 2359304 | tf_op jit(solution)/shard_map/ppermute | solution.py:323
  131.4 14.9 %collective-permute-start.25 = (bf16[768,256]{1,0:T(8,128)(2,1)S(1)}, bf16[768,256]{1,0:T(8,128)(2,1)S(1)}, u32[]{:S(2)}, u32[]{:S(2)}) collective-permute-start(bf16[768,256]{1,0:T(8,128)(2,1)S(1)} %slice.15), channel_id=1, source_target_pairs={{8,0},{10,2},{12,4},{14,6},{16,24},{18,26},{20,28},{22,30},{9,1},{... | collective-permute-start | bytes 1179656 | tf_op jit(solution)/shard_map/ppermute | solution.py:326
  132.8 13.6 %collective-permute-start.26 = (bf16[768,256]{1,0:T(8,128)(2,1)S(1)}, bf16[768,256]{1,0:T(8,128)(2,1)S(1)}, u32[]{:S(2)}, u32[]{:S(2)}) collective-permute-start(bf16[768,256]{1,0:T(8,128)(2,1)S(1)} %copy-done.13), channel_id=1, source_target_pairs={{8,16},{10,18},{12,20},{14,22},{16,8},{18,10},{20,12},{22,14},{9,1... | collective-permute-start | bytes 1179656 | tf_op jit(solution)/shard_map/ppermute | solution.py:323
  142.8 12.3 %collective-permute-start.22 = (bf16[256,512]{1,0:T(8,128)(2,1)}, bf16[256,512]{1,0:T(8,128)(2,1)S(1)}, u32[]{:S(2)}, u32[]{:S(2)}) collective-permute-start(bf16[256,512]{1,0:T(8,128)(2,1)} %get-tuple-element.239), channel_id=1, source_target_pairs={{0,2},{2,0},{4,6},{6,4},{8,10},{10,8},{12,14},{14,12},{16,18},{18,... | collective-permute-start | bytes 786440 | tf_op jit(solution)/shard_map/ppermute | solution.py:150
  144.4 13.9 %collective-permute-start.23 = (bf16[256,512]{1,0:T(8,128)(2,1)}, bf16[256,512]{1,0:T(8,128)(2,1)S(1)}, u32[]{:S(2)}, u32[]{:S(2)}) collective-permute-start(bf16[256,512]{1,0:T(8,128)(2,1)} %get-tuple-element.240), channel_id=1, source_target_pairs={{0,4},{2,6},{4,0},{6,2},{8,12},{10,14},{12,8},{14,10},{16,20},{18,... | collective-permute-start | bytes 786440 | tf_op jit(solution)/shard_map/ppermute | solution.py:150
  145.9 13.1 %collective-permute-start.24 = (bf16[256,512]{1,0:T(8,128)(2,1)}, bf16[256,512]{1,0:T(8,128)(2,1)S(1)}, u32[]{:S(2)}, u32[]{:S(2)}) collective-permute-start(bf16[256,512]{1,0:T(8,128)(2,1)} %get-tuple-element.241), channel_id=1, source_target_pairs={{0,6},{2,4},{4,2},{6,0},{8,14},{10,12},{12,10},{14,8},{16,22},{18,... | collective-permute-start | bytes 786440 | tf_op jit(solution)/shard_map/ppermute | solution.py:150
  (24 other events, 312.2 us)

commit v23 on v22

--- a/solution.py
+++ b/solution.py
@@ -227,13 +227,13 @@
             block = weight_buf.at[pl.ds(b * depth, depth), :]
             pltpu.make_async_copy(block, block, weight_sems.at[b]).wait()
             pltpu.make_async_copy(gated_buf.at[b], gated_buf.at[b], gated_sems.at[b]).wait()
+            if accs and not b:
+                pltpu.make_async_copy(acc_buf, acc_buf, acc_sem).wait()
             for col in range(0, cols, 2 * LANES):
                 here = pl.ds(col, min(2 * LANES, cols - col))
                 made = jnp.dot(
                     gated_buf[b], weight_buf[pl.ds(b * depth, depth), here], preferred_element_type=jnp.float32
                 )
-                if accs and not b and not col:
-                    pltpu.make_async_copy(acc_buf, acc_buf, acc_sem).wait()
                 for r in range(parts):
                     total = made[r * rows : (r + 1) * rows]
                     if b:

time: 166 us -> 165 us (level)
  no operation moved by 1% of the time
where the time goes in v23:
time: 165 us; the launch traced here: 164 us
  waiting for transfers between devices  65.6 us (40%)
  starting transfers between devices  47.2 us (29%)
  Pallas kernels  35.6 us (22%)
  local copies, waits for them, and re-layouts  10.9 us (7%)
  other arithmetic  4.64 us (3%)
    ppermute x22, waiting for transfers between devices, exchange(): return lax.ppermute(x, axis, [(i, i ^ flip) for i in range(count)])  55.4 us
    ppermute x22, starting transfers between devices, exchange(): return lax.ppermute(x, axis, [(i, i ^ flip) for i in range(count)])  25.5 us
    pallas_call x3, Pallas kernels, product(): pl.pallas_call(kernel, in_specs=[smem, smem] + [anywhere] * (2 * parts +...  21.9 us
    ppermute x3, starting transfers between devices, across(): return lax.ppermute(x, 'ctx', [(i, i ^ 3 * PLANE) for i in middle])  9.08 us
    pallas_call x1, Pallas kernels, gated_conv(): pl.pallas_call(conv_kernel, grid=(chan // width,), in_specs=[wide, wide,...  8.16 us
    ppermute x2, starting transfers between devices, shift_ctx(): return lax.ppermute(x, 'ctx', [(i, i + by) for i in range(count - by)])  6.85 us
    ppermute x2, waiting for transfers between devices, shift_ctx(): return lax.ppermute(x, 'ctx', [(i, i + by) for i in range(count - by)])  5.98 us
    ppermute x3, starting transfers between devices, outward(): return lax.ppermute(x, 'ctx', [(i, i ^ PLANE) for i in middle])  5.72 us
  transfers between devices with their start and end apart: 30, of which 14 were waited for; matrix products, arithmetic and copies ran while one was open for 6% of the time, Pallas kernels for 21%

profile of v23, /device:TPU:8, one launch (start us, length us, event | category | flops | bytes accessed | tf_op | source)
XLA Modules:
  0.0 164.3 jit_solution(2908230348610023081)
XLA Ops:
  0.0 2.7 %constant_dynamic-slice_fusion = (bf16[256,768]{1,0:T(8,128)(2,1)}, bf16[256,768]{1,0:T(8,128)(2,1)}, bf16[256,768]{1,0:T(8,128)(2,1)}, bf16[256,768]{1,0:T(8,128)(2,1)}) fusion(bf16[256,3072]{1,0:T(8,128)(2,1)} %param.15, s32[]{:T(128)S(6)} %select_n.84, s32[]{:T(128)S(6)} %select_n.82, s32[]{:T(128)S(6)} %select_n.81, s32[]{:T(128)S(6)} %select_n.83), kind=kLoop, calls=%fused_computation.5 | loop fusion | bytes 3145744 | tf_op jit(solution)/shard_map/dynamic_slice | solution.py:329
  2.7 3.0 %collective-permute-start.3 = (bf16[256,768]{1,0:T(8,128)(2,1)}, bf16[256,768]{1,0:T(8,128)(2,1)}, u32[]{:S(2)}, u32[]{:S(2)}) collective-permute-start(bf16[256,768]{1,0:T(8,128)(2,1)} %get-tuple-element.208.refs_8_), channel_id=1, source_target_pairs={{0,16},{2,18},{4,20},{6,22},{8,24},{10,26},{12,28},{14,30},{16,0},... | collective-permute-start | bytes 1179656 | tf_op jit(solution)/shard_map/ppermute | solution.py:150
  5.8 15.8 %while.14 = (s32[]{:T(128)}, f32[16,16,128]{2,1,0:T(8,128)}, f32[16,16,128]{2,1,0:T(8,128)}, s32[]{:T(128)}, pred[]{:T(512)}, /*index=5*/bf16[256,2048]{1,0:T(8,...) while((s32[]{:T(128)}, f32[16,16,128]{2,1,0:T(8,128)}, ...), condition=%wide.region_1.2_spmd, body=%wide.region_0.1_spmd.sunk | while | flops 17399808 | bytes 4456652 | solution.py:185
  5.8 3.9 %end_states.3 = f32[16,16,128]{2,1,0:T(8,128)} custom-call(bf16[256,2048]{1,0:T(8,128)(2,1)S(1)} %get-tuple-element.346.k_ref, bf16[256,2048]{1,0:T(8,128)(2,1)S(1)} %get-tuple-element.347.v_ref, f32[16,2048]{1,0:T(8,128)S(1)} %get-tuple-element.348.rate_ref), custom_call_target="tpu_custom_call" | custom-call | flops 16777216 | bytes 2097152 | tf_op jit(solution)/shard_map/while/body/end_states/pallas_call | solution.py:98
  11.2 3.7 %collective-permute-done = f32[16,16,128]{2,1,0:T(8,128)S(1)} collective-permute-done((f32[16,16,128]{2,1,0:T(8,128)}, f32[16,16,128]{2,1,0:T(8,128)S(1)}, u32[]{:S(2)}, u32[]{:S(2)}) %collective-permute-start) | collective-permute-done | bytes 131104 | tf_op jit(solution)/shard_map/while/body/ppermute | solution.py:150
  17.4 3.4 %collective-permute-done.1 = f32[16,16,128]{2,1,0:T(8,128)S(1)} collective-permute-done((f32[16,16,128]{2,1,0:T(8,128)S(1)}, f32[16,16,128]{2,1,0:T(8,128)S(1)}, u32[]{:S(2)}, u32[]{:S(2)}) %collective-permute-start.1) | collective-permute-done | bytes 131104 | tf_op jit(solution)/shard_map/while/body/ppermute | solution.py:150
  23.4 2.3 %collective-permute-start.4 = (f32[16,16,128]{2,1,0:T(8,128)}, f32[16,16,128]{2,1,0:T(8,128)S(1)}, u32[]{:S(2)}, u32[]{:S(2)}) collective-permute-start(f32[16,16,128]{2,1,0:T(8,128)} %get-tuple-element.200), channel_id=1, source_target_pairs={{0,8},{2,10},{4,12},{6,14},{8,16},{10,18},{12,20},{14,22},{16,24},... | collective-permute-start | bytes 393224 | tf_op jit(solution)/shard_map/ppermute | solution.py:145
  31.5 4.5 %collective-permute-start.5 = (f32[16,16,128]{2,1,0:T(8,128)S(1)}, f32[16,16,128]{2,1,0:T(8,128)S(1)}, u32[]{:S(2)}, u32[]{:S(2)}) collective-permute-start(f32[16,16,128]{2,1,0:T(8,128)S(1)} %multiply_add_fusion), channel_id=1, source_target_pairs={{0,16},{2,18},{4,20},{6,22},{8,24},{10,26},{12,28},{14,30},{1,17},... | collective-permute-start | bytes 393224 | tf_op jit(solution)/shard_map/ppermute | solution.py:145
  36.0 4.8 %collective-permute-done.5.refs_1_ = f32[16,16,128]{2,1,0:T(8,128)S(1)} collective-permute-done((f32[16,16,128]{2,1,0:T(8,128)S(1)}, f32[16,16,128]{2,1,0:T(8,128)S(1)}, u32[]{:S(2)}, u32[]{:S(2)}) %collective-permute-start.5) | collective-permute-done | bytes 131104 | tf_op jit(solution)/shard_map/ppermute | solution.py:145
  44.1 8.2 %gated_conv.1.refs_0_ = bf16[2,256,1024]{2,1,0:T(8,128)(2,1)} custom-call(bf16[256,2048]{1,0:T(8,128)(2,1)} %q_ref.1, bf16[256,2048]{1,0:T(8,128)(2,1)S(1)} %get-tuple-element.394, bf16[256,2048]{1,0:T(8,128)(2,1)S(1)} %get-tuple-element.395, f32[16,2048]{1,0:T(8,128)S(1)} %get-tuple-element.404, f32[16,2048]{1,0:T(8,128)} %residue_ref.1, ...), custom_call_target="tpu_custom_call" | custom-call | flops 33554432 | bytes 4194304 | tf_op jit(solution)/shard_map/gated_conv/pallas_call | solution.py:128
  55.2 4.4 %collective-permute-start.11 = (bf16[768,768]{1,0:T(8,128)(2,1)S(1)}, bf16[768,768]{1,0:T(8,128)(2,1)}, u32[]{:S(2)}, u32[]{:S(2)}) collective-permute-start(bf16[768,768]{1,0:T(8,128)(2,1)S(1)} %pad_maximum_fusion.refs_9_), channel_id=1, source_target_pairs={{0,16},{2,18},{4,20},{6,22},{8,24},{10,26},{12,28},{14,30},{16,0},... | collective-permute-start | bytes 3538952 | tf_op jit(solution)/shard_map/ppermute | solution.py:150
  62.0 18.0 %collective-permute-done.13.refs_1_ = bf16[2,256,1024]{2,1,0:T(8,128)(2,1)} collective-permute-done((bf16[2,256,1024]{2,1,0:T(8,128)(2,1)S(1)}, bf16[2,256,1024]{2,1,0:T(8,128)(2,1)}, u32[]{:S(2)}, u32[]{:S(2)}) %collective-permute-start.13) | collective-permute-done | bytes 1048608 | tf_op jit(solution)/shard_map/ppermute | solution.py:150
  82.9 16.9 %collective-permute-done.15.refs_2_ = bf16[2,256,1024]{2,1,0:T(8,128)(2,1)} collective-permute-done((bf16[2,256,1024]{2,1,0:T(8,128)(2,1)S(1)}, bf16[2,256,1024]{2,1,0:T(8,128)(2,1)}, u32[]{:S(2)}, u32[]{:S(2)}) %collective-permute-start.15) | collective-permute-done | bytes 1048608 | tf_op jit(solution)/shard_map/ppermute | solution.py:150
  101.2 2.8 %collective-permute-done.12.refs_11_ = bf16[768,768]{1,0:T(8,128)(2,1)} collective-permute-done((bf16[768,768]{1,0:T(8,128)(2,1)S(1)}, bf16[768,768]{1,0:T(8,128)(2,1)}, u32[]{:S(2)}, u32[]{:S(2)}) %collective-permute-start.12) | collective-permute-done | bytes 1179680 | tf_op jit(solution)/shard_map/ppermute | solution.py:150
  104.6 2.1 %slice.14 = bf16[768,512]{1,0:T(8,128)(2,1)} slice(bf16[768,768]{1,0:T(8,128)(2,1)} %collective-permute-done.11.refs_13_), slice={[0:768], [0:512]} | slice | bytes 1572864 | tf_op jit(solution)/shard_map/slice | solution.py:376
  106.6 3.1 %collective-permute-start.20 = (bf16[768,512]{1,0:T(8,128)(2,1)}, bf16[768,512]{1,0:T(8,128)(2,1)}, u32[]{:S(2)}, u32[]{:S(2)}) collective-permute-start(bf16[768,512]{1,0:T(8,128)(2,1)} %slice.14), channel_id=1, source_target_pairs={{8,0},{10,2},{12,4},{14,6},{16,24},{18,26},{20,28},{22,30},{9,1},{... | collective-permute-start | bytes 2359304 | tf_op jit(solution)/shard_map/ppermute | solution.py:326
  109.7 3.5 %collective-permute-start.21 = (bf16[768,512]{1,0:T(8,128)(2,1)}, bf16[768,512]{1,0:T(8,128)(2,1)S(1)}, u32[]{:S(2)}, u32[]{:S(2)}) collective-permute-start(bf16[768,512]{1,0:T(8,128)(2,1)} %slice.12), channel_id=1, source_target_pairs={{8,16},{10,18},{12,20},{14,22},{16,8},{18,10},{20,12},{22,14},{9,1... | collective-permute-start | bytes 2359304 | tf_op jit(solution)/shard_map/ppermute | solution.py:323
  114.6 12.5 %product.3 = (f32[256,768]{1,0:T(8,128)}, f32[256,768]{1,0:T(8,128)}, f32[256,768]{1,0:T(8,128)}, f32[256,768]{1,0:T(8,128)}) custom-call(s32[5]{0:T(128)} %stack.36.flag_ref, s32[4]{0:T(128)} %pad_add_fusion.place_ref, bf16[2,256,1024]{2,1,0:T(8,128)(2,1)} %gated_conv.1.refs_0_, bf16[2,256,1024]{2,1,0:T(8,128)(2,1)} %collective-permute-done.13.refs_1_, ...), custom_call_target="tpu_custom_call" | custom-call | flops 4831838208 | bytes 11010048 | tf_op jit(solution)/shard_map/product/pallas_call | solution.py:247
  127.2 4.2 %collective-permute-done.21.refs_11_ = bf16[768,512]{1,0:T(8,128)(2,1)S(1)} collective-permute-done((bf16[768,512]{1,0:T(8,128)(2,1)}, bf16[768,512]{1,0:T(8,128)(2,1)S(1)}, u32[]{:S(2)}, u32[]{:S(2)}) %collective-permute-start.21) | collective-permute-done | bytes 786464 | tf_op jit(solution)/shard_map/ppermute | solution.py:323
  132.8 3.6 %collective-permute-start.26 = (bf16[768,256]{1,0:T(8,128)(2,1)S(1)}, bf16[768,256]{1,0:T(8,128)(2,1)S(1)}, u32[]{:S(2)}, u32[]{:S(2)}) collective-permute-start(bf16[768,256]{1,0:T(8,128)(2,1)S(1)} %copy-done.13), channel_id=1, source_target_pairs={{8,16},{10,18},{12,20},{14,22},{16,8},{18,10},{20,12},{22,14},{9,1... | collective-permute-start | bytes 1179656 | tf_op jit(solution)/shard_map/ppermute | solution.py:323
  136.4 5.2 %product.4 = (bf16[256,512]{1,0:T(8,128)(2,1)}, bf16[256,512]{1,0:T(8,128)(2,1)}, bf16[256,512]{1,0:T(8,128)(2,1)}, bf16[256,512]{1,0:T(8,128)(2,1)}) custom-call(s32[5]{0:T(128)} %stack.36.flag_ref, s32[4]{0:T(128)} %pad_add_fusion.place_ref, bf16[2,256,1024]{2,1,0:T(8,128)(2,1)} %gated_conv.1.refs_0_, ...), custom_call_target="tpu_custom_call" | custom-call | flops 1073741824 | bytes 3145728 | tf_op jit(solution)/shard_map/product/pallas_call | solution.py:247
  146.7 4.1 %product.5 = (bf16[256,256]{1,0:T(8,128)(2,1)}, bf16[256,256]{1,0:T(8,128)(2,1)}, bf16[256,256]{1,0:T(8,128)(2,1)}, bf16[256,256]{1,0:T(8,128)(2,1)}) custom-call(s32[5]{0:T(128)} %stack.36.flag_ref, s32[4]{0:T(128)} %pad_add_fusion.place_ref, bf16[2,256,1024]{2,1,0:T(8,128)(2,1)} %gated_conv.1.refs_0_, ...), custom_call_target="tpu_custom_call" | custom-call | flops 536870912 | bytes 2621440 | tf_op jit(solution)/shard_map/product/pallas_call | solution.py:247
  154.4 2.8 %collective-permute-done.23.refs_2_ = bf16[256,512]{1,0:T(8,128)(2,1)S(1)} collective-permute-done((bf16[256,512]{1,0:T(8,128)(2,1)}, bf16[256,512]{1,0:T(8,128)(2,1)S(1)}, u32[]{:S(2)}, u32[]{:S(2)}) %collective-permute-start.23) | collective-permute-done | bytes 262176 | tf_op jit(solution)/shard_map/ppermute | solution.py:150
  159.1 2.6 %collective-permute-done.28.refs_6_ = bf16[256,256]{1,0:T(8,128)(2,1)S(1)} collective-permute-done((bf16[256,256]{1,0:T(8,128)(2,1)}, bf16[256,256]{1,0:T(8,128)(2,1)S(1)}, u32[]{:S(2)}, u32[]{:S(2)}) %collective-permute-start.28) | collective-permute-done | bytes 131104 | tf_op jit(solution)/shard_map/ppermute | solution.py:150
  (92 shorter events, 41.6 us)
Async XLA Ops:
  2.7 18.9 %collective-permute-start.2 = (bf16[256,768]{1,0:T(8,128)(2,1)}, bf16[256,768]{1,0:T(8,128)(2,1)S(1)}, u32[]{:S(2)}, u32[]{:S(2)}) collective-permute-start(bf16[256,768]{1,0:T(8,128)(2,1)} %get-tuple-element.208.refs_8_), channel_id=1, source_target_pairs={{0,8},{2,10},{4,12},{6,14},{8,0},{10,2},{12,4},{14,6},{16,24},{18,... | collective-permute-start | bytes 1179656 | tf_op jit(solution)/shard_map/ppermute | solution.py:150
  2.7 20.7 %collective-permute-start.3 = (bf16[256,768]{1,0:T(8,128)(2,1)}, bf16[256,768]{1,0:T(8,128)(2,1)}, u32[]{:S(2)}, u32[]{:S(2)}) collective-permute-start(bf16[256,768]{1,0:T(8,128)(2,1)} %get-tuple-element.208.refs_8_), channel_id=1, source_target_pairs={{0,16},{2,18},{4,20},{6,22},{8,24},{10,26},{12,28},{14,30},{16,0},... | collective-permute-start | bytes 1179656 | tf_op jit(solution)/shard_map/ppermute | solution.py:150
  25.8 26.5 %collective-permute-start.6 = (bf16[256,768]{1,0:T(8,128)(2,1)}, bf16[256,768]{1,0:T(8,128)(2,1)S(1)}, u32[]{:S(2)}, u32[]{:S(2)}) collective-permute-start(bf16[256,768]{1,0:T(8,128)(2,1)} %get-tuple-element.204), channel_id=1, source_target_pairs={{0,2},{2,0},{4,6},{6,4},{8,10},{10,8},{12,14},{14,12},{16,18},{18,... | collective-permute-start | bytes 1179656 | tf_op jit(solution)/shard_map/ppermute | solution.py:150
  27.3 25.0 %collective-permute-start.7 = (bf16[256,768]{1,0:T(8,128)(2,1)}, bf16[256,768]{1,0:T(8,128)(2,1)}, u32[]{:S(2)}, u32[]{:S(2)}) collective-permute-start(bf16[256,768]{1,0:T(8,128)(2,1)} %get-tuple-element.205), channel_id=1, source_target_pairs={{0,4},{2,6},{4,0},{6,2},{8,12},{10,14},{12,8},{14,10},{16,20},{18,... | collective-permute-start | bytes 1179656 | tf_op jit(solution)/shard_map/ppermute | solution.py:150
  28.8 23.5 %collective-permute-start.8 = (bf16[256,768]{1,0:T(8,128)(2,1)}, bf16[256,768]{1,0:T(8,128)(2,1)}, u32[]{:S(2)}, u32[]{:S(2)}) collective-permute-start(bf16[256,768]{1,0:T(8,128)(2,1)} %get-tuple-element.206), channel_id=1, source_target_pairs={{0,6},{2,4},{4,2},{6,0},{8,14},{10,12},{12,10},{14,8},{16,22},{18,... | collective-permute-start | bytes 1179656 | tf_op jit(solution)/shard_map/ppermute | solution.py:150
  31.5 9.3 %collective-permute-start.5 = (f32[16,16,128]{2,1,0:T(8,128)S(1)}, f32[16,16,128]{2,1,0:T(8,128)S(1)}, u32[]{:S(2)}, u32[]{:S(2)}) collective-permute-start(f32[16,16,128]{2,1,0:T(8,128)S(1)} %multiply_add_fusion), channel_id=1, source_target_pairs={{0,16},{2,18},{4,20},{6,22},{8,24},{10,26},{12,28},{14,30},{1,17},... | collective-permute-start | bytes 393224 | tf_op jit(solution)/shard_map/ppermute | solution.py:145
  40.8 12.8 %collective-permute-start.10 = (bf16[256,768]{1,0:T(8,128)(2,1)}, bf16[256,768]{1,0:T(8,128)(2,1)S(1)}, u32[]{:S(2)}, u32[]{:S(2)}) collective-permute-start(bf16[256,768]{1,0:T(8,128)(2,1)} %get-tuple-element.208.refs_8_), channel_id=1, source_target_pairs={{8,16},{10,18},{12,20},{14,22},{16,8},{18,10},{20,12},{22,14},{9,1... | collective-permute-start | bytes 1179656 | tf_op jit(solution)/shard_map/ppermute | solution.py:323
  42.8 10.9 %collective-permute-start.9 = (bf16[256,768]{1,0:T(8,128)(2,1)}, bf16[256,768]{1,0:T(8,128)(2,1)S(1)}, u32[]{:S(2)}, u32[]{:S(2)}) collective-permute-start(bf16[256,768]{1,0:T(8,128)(2,1)} %collective-permute-done.3.refs_12_), channel_id=1, source_target_pairs={{8,0},{10,2},{12,4},{14,6},{16,24},{18,26},{20,28},{22,30},{9,1},{... | collective-permute-start | bytes 1179656 | tf_op jit(solution)/shard_map/ppermute | solution.py:326
  53.7 26.2 %collective-permute-start.13 = (bf16[2,256,1024]{2,1,0:T(8,128)(2,1)S(1)}, bf16[2,256,1024]{2,1,0:T(8,128)(2,1)}, u32[]{:S(2)}, u32[]{:S(2)}) collective-permute-start(bf16[2,256,1024]{2,1,0:T(8,128)(2,1)S(1)} %copy-done.5), channel_id=1, source_target_pairs={{0,2},{2,0},{4,6},{6,4},{8,10},{10,8},{12,14},{14,12},{16,18},{18,... | collective-permute-start | bytes 3145736 | tf_op jit(solution)/shard_map/ppermute | solution.py:150
  55.2 46.0 %collective-permute-start.11 = (bf16[768,768]{1,0:T(8,128)(2,1)S(1)}, bf16[768,768]{1,0:T(8,128)(2,1)}, u32[]{:S(2)}, u32[]{:S(2)}) collective-permute-start(bf16[768,768]{1,0:T(8,128)(2,1)S(1)} %pad_maximum_fusion.refs_9_), channel_id=1, source_target_pairs={{0,16},{2,18},{4,20},{6,22},{8,24},{10,26},{12,28},{14,30},{16,0},... | collective-permute-start | bytes 3538952 | tf_op jit(solution)/shard_map/ppermute | solution.py:150
  59.6 44.4 %collective-permute-start.12 = (bf16[768,768]{1,0:T(8,128)(2,1)S(1)}, bf16[768,768]{1,0:T(8,128)(2,1)}, u32[]{:S(2)}, u32[]{:S(2)}) collective-permute-start(bf16[768,768]{1,0:T(8,128)(2,1)S(1)} %pad_maximum_fusion.refs_9_), channel_id=1, source_target_pairs={{0,8},{2,10},{4,12},{6,14},{8,0},{10,2},{12,4},{14,6},{16,24},{18,... | collective-permute-start | bytes 3538952 | tf_op jit(solution)/shard_map/ppermute | solution.py:150
  60.0 39.9 %collective-permute-start.15 = (bf16[2,256,1024]{2,1,0:T(8,128)(2,1)S(1)}, bf16[2,256,1024]{2,1,0:T(8,128)(2,1)}, u32[]{:S(2)}, u32[]{:S(2)}) collective-permute-start(bf16[2,256,1024]{2,1,0:T(8,128)(2,1)S(1)} %copy-done.5), channel_id=1, source_target_pairs={{0,4},{2,6},{4,0},{6,2},{8,12},{10,14},{12,8},{14,10},{16,20},{18,... | collective-permute-start | bytes 3145736 | tf_op jit(solution)/shard_map/ppermute | solution.py:150
  61.5 38.4 %collective-permute-start.16 = (bf16[2,256,1024]{2,1,0:T(8,128)(2,1)S(1)}, bf16[2,256,1024]{2,1,0:T(8,128)(2,1)}, u32[]{:S(2)}, u32[]{:S(2)}) collective-permute-start(bf16[2,256,1024]{2,1,0:T(8,128)(2,1)S(1)} %copy-done.5), channel_id=1, source_target_pairs={{0,6},{2,4},{4,2},{6,0},{8,14},{10,12},{12,10},{14,8},{16,22},{18,... | collective-permute-start | bytes 3145736 | tf_op jit(solution)/shard_map/ppermute | solution.py:150
  79.9 24.1 %collective-permute-start.14 = (bf16[2,256,1024]{2,1,0:T(8,128)(2,1)}, bf16[2,256,1024]{2,1,0:T(8,128)(2,1)}, u32[]{:S(2)}, u32[]{:S(2)}) collective-permute-start(bf16[2,256,1024]{2,1,0:T(8,128)(2,1)} %collective-permute-done.13.refs_1_), channel_id=1, source_target_pairs={{0,1},{1,0},{2,3},{3,2},{4,5},{5,4},{6,7},{7,6},{8,9},{9,8},{10,11... | collective-permute-start | bytes 3145736 | tf_op jit(solution)/shard_map/ppermute | solution.py:150
  104.0 10.6 %collective-permute-start.18 = (bf16[2,256,1024]{2,1,0:T(8,128)(2,1)}, bf16[2,256,1024]{2,1,0:T(8,128)(2,1)}, u32[]{:S(2)}, u32[]{:S(2)}) collective-permute-start(bf16[2,256,1024]{2,1,0:T(8,128)(2,1)} %collective-permute-done.15.refs_2_), channel_id=1, source_target_pairs={{0,1},{1,0},{2,3},{3,2},{4,5},{5,4},{6,7},{7,6},{8,9},{9,8},{10,11... | collective-permute-start | bytes 3145736 | tf_op jit(solution)/shard_map/ppermute | solution.py:150
  104.6 10.1 %collective-permute-start.19 = (bf16[2,256,1024]{2,1,0:T(8,128)(2,1)}, bf16[2,256,1024]{2,1,0:T(8,128)(2,1)}, u32[]{:S(2)}, u32[]{:S(2)}) collective-permute-start(bf16[2,256,1024]{2,1,0:T(8,128)(2,1)} %collective-permute-done.16.refs_3_), channel_id=1, source_target_pairs={{0,1},{1,0},{2,3},{3,2},{4,5},{5,4},{6,7},{7,6},{8,9},{9,8},{10,11... | collective-permute-start | bytes 3145736 | tf_op jit(solution)/shard_map/ppermute | solution.py:150
  106.6 20.5 %collective-permute-start.20 = (bf16[768,512]{1,0:T(8,128)(2,1)}, bf16[768,512]{1,0:T(8,128)(2,1)}, u32[]{:S(2)}, u32[]{:S(2)}) collective-permute-start(bf16[768,512]{1,0:T(8,128)(2,1)} %slice.14), channel_id=1, source_target_pairs={{8,0},{10,2},{12,4},{14,6},{16,24},{18,26},{20,28},{22,30},{9,1},{... | collective-permute-start | bytes 2359304 | tf_op jit(solution)/shard_map/ppermute | solution.py:326
  109.7 21.7 %collective-permute-start.21 = (bf16[768,512]{1,0:T(8,128)(2,1)}, bf16[768,512]{1,0:T(8,128)(2,1)S(1)}, u32[]{:S(2)}, u32[]{:S(2)}) collective-permute-start(bf16[768,512]{1,0:T(8,128)(2,1)} %slice.12), channel_id=1, source_target_pairs={{8,16},{10,18},{12,20},{14,22},{16,8},{18,10},{20,12},{22,14},{9,1... | collective-permute-start | bytes 2359304 | tf_op jit(solution)/shard_map/ppermute | solution.py:323
  131.4 13.7 %collective-permute-start.25 = (bf16[768,256]{1,0:T(8,128)(2,1)S(1)}, bf16[768,256]{1,0:T(8,128)(2,1)S(1)}, u32[]{:S(2)}, u32[]{:S(2)}) collective-permute-start(bf16[768,256]{1,0:T(8,128)(2,1)S(1)} %slice.15), channel_id=1, source_target_pairs={{8,0},{10,2},{12,4},{14,6},{16,24},{18,26},{20,28},{22,30},{9,1},{... | collective-permute-start | bytes 1179656 | tf_op jit(solution)/shard_map/ppermute | solution.py:326
  132.8 12.4 %collective-permute-start.26 = (bf16[768,256]{1,0:T(8,128)(2,1)S(1)}, bf16[768,256]{1,0:T(8,128)(2,1)S(1)}, u32[]{:S(2)}, u32[]{:S(2)}) collective-permute-start(bf16[768,256]{1,0:T(8,128)(2,1)S(1)} %copy-done.13), channel_id=1, source_target_pairs={{8,16},{10,18},{12,20},{14,22},{16,8},{18,10},{20,12},{22,14},{9,1... | collective-permute-start | bytes 1179656 | tf_op jit(solution)/shard_map/ppermute | solution.py:323
  141.6 12.3 %collective-permute-start.22 = (bf16[256,512]{1,0:T(8,128)(2,1)}, bf16[256,512]{1,0:T(8,128)(2,1)S(1)}, u32[]{:S(2)}, u32[]{:S(2)}) collective-permute-start(bf16[256,512]{1,0:T(8,128)(2,1)} %get-tuple-element.239), channel_id=1, source_target_pairs={{0,2},{2,0},{4,6},{6,4},{8,10},{10,8},{12,14},{14,12},{16,18},{18,... | collective-permute-start | bytes 786440 | tf_op jit(solution)/shard_map/ppermute | solution.py:150
  143.2 13.9 %collective-permute-start.23 = (bf16[256,512]{1,0:T(8,128)(2,1)}, bf16[256,512]{1,0:T(8,128)(2,1)S(1)}, u32[]{:S(2)}, u32[]{:S(2)}) collective-permute-start(bf16[256,512]{1,0:T(8,128)(2,1)} %get-tuple-element.240), channel_id=1, source_target_pairs={{0,4},{2,6},{4,0},{6,2},{8,12},{10,14},{12,8},{14,10},{16,20},{18,... | collective-permute-start | bytes 786440 | tf_op jit(solution)/shard_map/ppermute | solution.py:150
  144.7 13.1 %collective-permute-start.24 = (bf16[256,512]{1,0:T(8,128)(2,1)}, bf16[256,512]{1,0:T(8,128)(2,1)S(1)}, u32[]{:S(2)}, u32[]{:S(2)}) collective-permute-start(bf16[256,512]{1,0:T(8,128)(2,1)} %get-tuple-element.241), channel_id=1, source_target_pairs={{0,6},{2,4},{4,2},{6,0},{8,14},{10,12},{12,10},{14,8},{16,22},{18,... | collective-permute-start | bytes 786440 | tf_op jit(solution)/shard_map/ppermute | solution.py:150
  152.4 9.3 %collective-permute-start.28 = (bf16[256,256]{1,0:T(8,128)(2,1)}, bf16[256,256]{1,0:T(8,128)(2,1)S(1)}, u32[]{:S(2)}, u32[]{:S(2)}) collective-permute-start(bf16[256,256]{1,0:T(8,128)(2,1)} %get-tuple-element.246), channel_id=1, source_target_pairs={{0,4},{2,6},{4,0},{6,2},{8,12},{10,14},{12,8},{14,10},{16,20},{18,... | collective-permute-start | bytes 393224 | tf_op jit(solution)/shard_map/ppermute | solution.py:150
  (24 other events, 312.4 us)
